TPU v7x, 32 devices: a whole 2x2x4 slice. The times are simulated.
32 devices in a mesh: leaf: 2 (over y), node: 8 (over z, x), tensor: 2 (over core).
Axes of the slice: x: 2, y: 2, z: 4, core: 2. Of those that a mesh axis runs over, the one named last changes fastest.
Arguments:
- queries: bfloat16 [2048, 64, 128], P(('leaf', 'node'), 'tensor'), parts along dimension 0, may hold values from -6 to 6
- keys: bfloat16 [2048, 8, 128], P(('leaf', 'node'), 'tensor'), parts along dimension 0, may hold values from -6 to 6
- values: bfloat16 [2048, 8, 128], P(('leaf', 'node'), 'tensor'), parts along dimension 0, may hold values from -6 to 6
- grad_out: bfloat16 [2048, 64, 128], P(('leaf', 'node'), 'tensor'), parts along dimension 0, may hold values from -6 to 6
- parents: int32 [128], P('leaf'), parts along dimension 0, may hold values from -1 to 62, as said below
- lengths: int32 [128], P('leaf'), parts along dimension 0, may hold values from 8 to 16, as said below
Outputs:
- grad_queries: bfloat16 [2048, 64, 128], P(('leaf', 'node'), 'tensor'), parts along dimension 0
- grad_keys: float32 [2048, 8, 128], P(('leaf', 'node'), 'tensor'), parts along dimension 0
- grad_values: float32 [2048, 8, 128], P(('leaf', 'node'), 'tensor'), parts along dimension 0
There are 2 independent parts, one for each index of `leaf`. A program takes and returns all parts, laid end to end along the dimension named above; each array names one. Nothing has to cross between parts.
Inputs may be any that keep to these rules, and one draw needn't show every extreme that they name: `parents`: node t has parent t - 1 unless t is the first of the 8 nodes of a device. The first node of device 0 is the root. The first node of any other device has as parent either node 7 or one of the first 2 nodes of a lower device; every ancestor of a node outside device 0 lies on device 0 or on one of the 7 devices below its own, and every such node descends from node 7. `lengths`: the nodes of device 0 are full.
All inputs are finite; a program needn't handle non-finite values.
Results may differ from a plain program's by a relative error of at most 0.0097.
Values may be sent and summed in bfloat16 or wider, within the bound.
No kernel may reach another device: no remote copies, remote signals or barrier semaphores. Data moves between devices by JAX's collectives and lax.ppermute only.
A program may use at most 64 MiB of HBM per device.

v0:
```python
import jax
import jax.numpy as jnp
from jax import lax
from jax.sharding import PartitionSpec as P

TILE = 16
TD = 8
CAP = 2
W = 7


def broadcast(array, axis, root):
    mine = lax.axis_index(axis) == root
    return lax.psum(jnp.where(mine, array, jnp.zeros_like(array)), axis)


def from_behind(block, axis, distance):
    devices = range(lax.axis_size(axis))
    route = [(i - distance, i) for i in devices if i - distance in devices]
    return lax.ppermute(block, axis, route)


def per_device(queries, keys, values, grad_out, parents, lengths):
    tokens_per_device = queries.shape[0]
    heads_q = queries.shape[1]
    heads_kv = keys.shape[1]
    head_size = queries.shape[2]
    heads_per_group = heads_q // heads_kv
    front_rows = CAP * TILE
    score_scale = head_size ** (-0.5)
    device_here = lax.axis_index("node")
    token_pos = jnp.arange(tokens_per_device) % TILE
    token_tile = jnp.arange(tokens_per_device) // TILE
    own_lengths = lax.dynamic_slice_in_dim(lengths, device_here * TD, TD)
    live_here = token_pos < jnp.repeat(own_lengths, TILE, total_repeat_length=tokens_per_device)
    gradient_live = jnp.where(live_here[:, None, None], grad_out, jnp.zeros_like(grad_out))
    cursor = parents[device_here * TD]
    depth_need = jnp.zeros((W + 1,), jnp.int32)
    slot_index = jnp.arange(W + 1)
    for repeat_index in range(W):
        owner_dev = jnp.floor_divide(cursor, TD)
        distance = device_here - owner_dev
        active = (owner_dev >= 1) & (distance >= 1) & (distance <= W)
        depth_need = jnp.where(active & (slot_index == distance), cursor % TD + 1, depth_need)
        cursor = jnp.where(active, parents[jnp.maximum(owner_dev, 0) * TD], cursor)
    root_near = (device_here >= 1) & (device_here <= W)
    depth_need = jnp.where(root_near & (slot_index == device_here), CAP, depth_need)
    prompt_keys, prompt_values = (broadcast(keys, "node", 0), broadcast(values, "node", 0))
    head_keys = keys[:front_rows]
    head_values = values[:front_rows]
    window_k = []
    window_v = []
    for distance_step in range(1, W + 1):
        moved_k, moved_v = from_behind((head_keys, head_values), "node", distance_step)
        window_k.append(moved_k)
        window_v.append(moved_v)
    window_keys = jnp.stack(window_k)
    window_values = jnp.stack(window_v)
    front_pos = jnp.arange(front_rows) % TILE
    front_tile = jnp.arange(front_rows) // TILE
    window_index = (
        jnp.maximum(device_here - jnp.arange(1, W + 1), 0)[:, None] * TD + jnp.arange(CAP)[None, :]
    )
    window_lengths = lengths[window_index]
    window_live = front_pos[None, :] < window_lengths[:, front_tile]
    window_seen = window_live & (front_tile[None, :] < depth_need[1:, None])
    prompt_seen = (device_here >= 1) & (
        token_pos < jnp.repeat(lengths[:TD], TILE, total_repeat_length=tokens_per_device)
    )
    prompt_seen = prompt_seen & (
        (jnp.arange(tokens_per_device) >= front_rows) | jnp.logical_not(root_near)
    )
    local_seen = (
        (token_tile[None, :] < token_tile[:, None])
        | (token_tile[None, :] == token_tile[:, None]) & (token_pos[None, :] <= token_pos[:, None])
    ) & live_here[None, :]
    window_count = W * front_rows
    visible = jnp.concatenate(
        [
            jnp.broadcast_to(prompt_seen[None, :], (tokens_per_device, tokens_per_device)),
            jnp.broadcast_to(
                window_seen.reshape(1, window_count), (tokens_per_device, window_count)
            ),
            local_seen,
        ],
        axis=1,
    )
    all_keys = jnp.concatenate(
        [prompt_keys, window_keys.reshape(window_count, heads_kv, head_size), keys], axis=0
    )
    all_values = jnp.concatenate(
        [prompt_values, window_values.reshape(window_count, heads_kv, head_size), values], axis=0
    )
    grad_q_parts = []
    grad_k_parts = []
    grad_v_parts = []
    for group_index in range(heads_kv):
        query_group = queries[
            :, group_index * heads_per_group : (group_index + 1) * heads_per_group, :
        ]
        grad_group = gradient_live[
            :, group_index * heads_per_group : (group_index + 1) * heads_per_group, :
        ]
        key_group = all_keys[:, group_index, :]
        value_group = all_values[:, group_index, :]
        scores = (
            jnp.einsum("trd,kd->rtk", query_group, key_group, preferred_element_type=jnp.float32)
            * score_scale
        )
        scores = jnp.where(visible[None], scores, -jnp.inf)
        row_top = jnp.max(scores, axis=-1, keepdims=True)
        probs = jnp.exp(scores - row_top)
        probs = probs / jnp.sum(probs, axis=-1, keepdims=True)
        probs_low = probs.astype(jnp.bfloat16)
        grad_probs = jnp.einsum(
            "trd,kd->rtk", grad_group, value_group, preferred_element_type=jnp.float32
        )
        row_delta = jnp.sum(probs * grad_probs, axis=-1, keepdims=True)
        grad_scores = (probs * (grad_probs - row_delta) * score_scale).astype(jnp.bfloat16)
        grad_q_parts.append(
            jnp.einsum("rtk,kd->trd", grad_scores, key_group, preferred_element_type=jnp.float32)
        )
        grad_k_parts.append(
            jnp.einsum("rtk,trd->kd", grad_scores, query_group, preferred_element_type=jnp.float32)
        )
        grad_v_parts.append(
            jnp.einsum("rtk,trd->kd", probs_low, grad_group, preferred_element_type=jnp.float32)
        )
    grad_queries = jnp.concatenate(grad_q_parts, axis=1).astype(jnp.bfloat16)
    grad_k_all = jnp.stack(grad_k_parts, axis=1)
    grad_v_all = jnp.stack(grad_v_parts, axis=1)
    prompt_grad_k = grad_k_all[:tokens_per_device]
    prompt_grad_v = grad_v_all[:tokens_per_device]
    window_grad_k = grad_k_all[tokens_per_device : tokens_per_device + window_count].reshape(
        W, front_rows, heads_kv, head_size
    )
    window_grad_v = grad_v_all[tokens_per_device : tokens_per_device + window_count].reshape(
        W, front_rows, heads_kv, head_size
    )
    local_grad_k = grad_k_all[tokens_per_device + window_count :]
    local_grad_v = grad_v_all[tokens_per_device + window_count :]
    received_k = jnp.zeros((front_rows, heads_kv, head_size), jnp.float32)
    received_v = jnp.zeros((front_rows, heads_kv, head_size), jnp.float32)
    for distance_step in range(1, W + 1):
        back_k, back_v = (
            from_behind(
                window_grad_k[distance_step - 1].astype(jnp.bfloat16), "node", -distance_step
            ).astype(jnp.float32),
            from_behind(
                window_grad_v[distance_step - 1].astype(jnp.bfloat16), "node", -distance_step
            ).astype(jnp.float32),
        )
        received_k = received_k + back_k
        received_v = received_v + back_v
    total_k, total_v = lax.psum((prompt_grad_k, prompt_grad_v), "node")
    at_root = device_here == 0
    grad_keys = local_grad_k + jnp.where(at_root, total_k, jnp.zeros_like(total_k))
    grad_values = local_grad_v + jnp.where(at_root, total_v, jnp.zeros_like(total_v))
    grad_keys = grad_keys.at[:front_rows].add(received_k)
    grad_values = grad_values.at[:front_rows].add(received_v)
    return (grad_queries, grad_keys, grad_values)


def solution(mesh):
    placed = (
        P(("leaf", "node"), "tensor", None),
        P(("leaf", "node"), "tensor", None),
        P(("leaf", "node"), "tensor", None),
        P(("leaf", "node"), "tensor", None),
        P("leaf"),
        P("leaf"),
    )
    return jax.shard_map(
        per_device,
        mesh=mesh,
        in_specs=placed,
        out_specs=(
            P(("leaf", "node"), "tensor", None),
            P(("leaf", "node"), "tensor", None),
            P(("leaf", "node"), "tensor", None),
        ),
        check_vma=False,
    )
```

profile of v0, /device:TPU:0, one launch (start us, length us, event | category | flops | bytes accessed | tf_op | source)
XLA Modules:
  0.0 290.3 jit_solution(4059501013791025350)
XLA Ops:
  8.0 7.9 %collective-permute-start.13 = (bf16[32,4,128]{2,1,0:T(4,128)(2,1)S(1)}, bf16[32,4,128]{2,1,0:T(4,128)(2,1)S(1)}, u32[]{:S(2)}, u32[]{:S(2)}) collective-permute-start(bf16[32,4,128]{2,1,0:T(4,128)(2,1)S(1)} %slice.231), channel_id=1, source_target_pairs={{0,14},{1,15},{16,30},{17,31}} | collective-permute-start | bytes 98312 | tf_op jit(solution)/shard_map/ppermute | solution.py:20
  20.6 2.5 collective-permute-start
  23.0 1.6 fusion.128
  24.6 1.6 broadcast_select_fusion
  43.2 1.6 fusion.129
  48.7 5.0 %or_and_fusion.1 = pred[128]{0:T(512)(128)(4,1)S(1)} fusion(pred[]{:T(512)S(6)} %not.3, pred[]{:T(512)S(6)} %ge.55, pred[128]{0:T(512)(128)(4,1)S(1)} %copy-done.22, pred[128]{0:T(512)(128)(4,1)S(1)} %copy-done.21, pred[128]{0:T(512)(128)(4,1)S(1)} %copy-done.20, pred[128]{0:T(512)(128)(4,1)S(1)} %copy-done.19, pred[128]{0:T(512)(128)(4,1)S(1)} %copy-done.18, ...), kind=kLoop, calls=%fused_computation.162 | loop fusion | flops 2304 | bytes 1058 | tf_op jit(solution)/shard_map/and | solution.py:70
  53.8 4.9 %select_compare_fusion = pred[128]{0:T(512)(128)(4,1)S(1)} fusion(pred[128]{0:T(512)(128)(4,1)S(1)} %copy-done.22, pred[128]{0:T(512)(128)(4,1)S(1)} %copy-done.21, pred[128]{0:T(512)(128)(4,1)S(1)} %copy-done.20, pred[128]{0:T(512)(128)(4,1)S(1)} %copy-done.19, pred[128]{0:T(512)(128)(4,1)S(1)} %copy-done.18, pred[128]{0:T(512)(128)(4,1)S(1)} %copy-done.17, ...), kind=kLoop, calls=%fused_computation.184 | loop fusion | flops 1792 | bytes 1056 | tf_op jit(solution)/shard_map/lt | solution.py:35
  60.0 3.4 %collective-permute-start.7 = (bf16[32,4,128]{2,1,0:T(4,128)(2,1)S(1)}, bf16[32,4,128]{2,1,0:T(4,128)(2,1)S(1)}, u32[]{:S(2)}, u32[]{:S(2)}) collective-permute-start(bf16[32,4,128]{2,1,0:T(4,128)(2,1)S(1)} %slice.231), channel_id=1, source_target_pairs={{0,2},{2,4},{4,6},{6,8},{8,10},{10,12},{12,14},{1,3},{3,5},{5,7},{... | collective-permute-start | bytes 98312 | tf_op jit(solution)/shard_map/ppermute | solution.py:20
  63.4 1.6 collective-permute-done.7
  65.0 4.2 %collective-permute-start.1 = (bf16[32,4,128]{2,1,0:T(4,128)(2,1)S(1)}, bf16[32,4,128]{2,1,0:T(4,128)(2,1)S(1)}, u32[]{:S(2)}, u32[]{:S(2)}) collective-permute-start(bf16[32,4,128]{2,1,0:T(4,128)(2,1)S(1)} %slice.226), channel_id=1, source_target_pairs={{0,4},{2,6},{4,8},{6,10},{8,12},{10,14},{1,5},{3,7},{5,9},{7,11},{... | collective-permute-start | bytes 98312 | tf_op jit(solution)/shard_map/ppermute | solution.py:20
  69.2 1.6 collective-permute-done.1
  70.8 3.1 %collective-permute-start.2 = (bf16[32,4,128]{2,1,0:T(4,128)(2,1)S(1)}, bf16[32,4,128]{2,1,0:T(4,128)(2,1)S(1)}, u32[]{:S(2)}, u32[]{:S(2)}) collective-permute-start(bf16[32,4,128]{2,1,0:T(4,128)(2,1)S(1)} %slice.226), channel_id=1, source_target_pairs={{0,6},{2,8},{4,10},{6,12},{8,14},{1,7},{3,9},{5,11},{7,13},{9,15},... | collective-permute-start | bytes 98312 | tf_op jit(solution)/shard_map/ppermute | solution.py:20
  73.9 1.6 collective-permute-done.2
  75.4 6.6 %collective-permute-start.3 = (bf16[32,4,128]{2,1,0:T(4,128)(2,1)S(1)}, bf16[32,4,128]{2,1,0:T(4,128)(2,1)S(1)}, u32[]{:S(2)}, u32[]{:S(2)}) collective-permute-start(bf16[32,4,128]{2,1,0:T(4,128)(2,1)S(1)} %slice.226), channel_id=1, source_target_pairs={{0,8},{2,10},{4,12},{6,14},{1,9},{3,11},{5,13},{7,15},{16,24},{18,... | collective-permute-start | bytes 98312 | tf_op jit(solution)/shard_map/ppermute | solution.py:20
  82.1 1.8 collective-permute-done.3
  83.9 3.4 %collective-permute-start.4 = (bf16[32,4,128]{2,1,0:T(4,128)(2,1)S(1)}, bf16[32,4,128]{2,1,0:T(4,128)(2,1)S(1)}, u32[]{:S(2)}, u32[]{:S(2)}) collective-permute-start(bf16[32,4,128]{2,1,0:T(4,128)(2,1)S(1)} %slice.226), channel_id=1, source_target_pairs={{0,10},{2,12},{4,14},{1,11},{3,13},{5,15},{16,26},{18,28},{20,30},... | collective-permute-start | bytes 98312 | tf_op jit(solution)/shard_map/ppermute | solution.py:20
  87.3 1.6 collective-permute-done.4
  88.9 7.9 %collective-permute-start.5 = (bf16[32,4,128]{2,1,0:T(4,128)(2,1)S(1)}, bf16[32,4,128]{2,1,0:T(4,128)(2,1)S(1)}, u32[]{:S(2)}, u32[]{:S(2)}) collective-permute-start(bf16[32,4,128]{2,1,0:T(4,128)(2,1)S(1)} %slice.226), channel_id=1, source_target_pairs={{0,12},{2,14},{1,13},{3,15},{16,28},{18,30},{17,29},{19,31}} | collective-permute-start | bytes 98312 | tf_op jit(solution)/shard_map/ppermute | solution.py:20
  96.8 1.6 collective-permute-done.5
  98.3 4.4 %collective-permute-start.6 = (bf16[32,4,128]{2,1,0:T(4,128)(2,1)S(1)}, bf16[32,4,128]{2,1,0:T(4,128)(2,1)S(1)}, u32[]{:S(2)}, u32[]{:S(2)}) collective-permute-start(bf16[32,4,128]{2,1,0:T(4,128)(2,1)S(1)} %slice.226), channel_id=1, source_target_pairs={{0,14},{1,15},{16,30},{17,31}} | collective-permute-start | bytes 98312 | tf_op jit(solution)/shard_map/ppermute | solution.py:20
  102.8 1.6 collective-permute-done.6
  105.7 1.6 collective-permute-done.8
  107.2 1.5 collective-permute-start.9
  111.8 1.7 fusion.52
  113.5 1.7 fusion.55
  115.2 1.7 fusion.58
  116.9 2.9 %fusion.140 = (f32[8,128]{1,0:T(8,128)S(1)}, f32[8,128,480]{1,2,0:T(8,128)}) fusion(pred[128,480]{0,1:T(8,128)(4,1)} %pad_add_fusion, bf16[128,8,128]{2,1,0:T(8,128)(2,1)} %get-tuple-element.61, bf16[480,4,128]{2,0,1:T(8,128)(2,1)S(1)} %get-tuple-element.111), kind=kOutput, calls=%fused_computation.211 | convolution fusion | flops 127795680 | bytes 2416640 | tf_op jit(solution)/shard_map/sub | solution.py:112
  119.9 4.8 %convolution_bitcast_fusion.7 = f32[480,1,128]{2,0,1:T(8,128)} fusion(f32[480,128,8]{1,0,2:T(8,128)} %fusion.58, bf16[128,8,128]{2,1,0:T(8,128)(2,1)} %get-tuple-element.61, f32[8,128,480]{1,2,0:T(8,128)} %get-tuple-element.106, f32[8,128]{1,0:T(8,128)S(1)} %get-tuple-element.105), kind=kOutput, calls=%fused_computation.57 | convolution fusion | flops 129271264 | bytes 4444160 | tf_op jit(solution)/shard_map/rtk,trd->kd/dot_general | solution.py:124
  124.6 4.7 %fusion.24 = bf16[128,8,128]{0,2,1:T(8,128)(2,1)} fusion(f32[480,128,8]{1,0,2:T(8,128)} %fusion.58, bf16[480,4,128]{2,0,1:T(8,128)(2,1)S(1)} %get-tuple-element.111, f32[8,128,480]{1,2,0:T(8,128)} %get-tuple-element.106, f32[8,128]{1,0:T(8,128)S(1)} %get-tuple-element.105), kind=kOutput, calls=%fused_computation.46 | convolution fusion | flops 129402336 | bytes 8257536 | tf_op jit(solution)/shard_map/rtk,kd->trd/dot_general | solution.py:121
  129.4 2.0 convolution_bitcast_fusion.3
  131.4 2.9 %fusion.134 = (f32[8,128]{1,0:T(8,128)S(1)}, f32[8,128,480]{1,2,0:T(8,128)}) fusion(pred[128,480]{0,1:T(8,128)(4,1)} %pad_add_fusion, bf16[128,8,128]{2,1,0:T(8,128)(2,1)S(1)} %copy-done.10, bf16[480,4,128]{2,0,1:T(8,128)(2,1)} %copy-done.9), kind=kOutput, calls=%fused_computation.209 | convolution fusion | flops 127795680 | bytes 2416640 | tf_op jit(solution)/shard_map/sub | solution.py:112
  134.3 4.7 %convolution_bitcast_fusion.5 = f32[480,1,128]{2,0,1:T(8,128)} fusion(f32[480,128,8]{1,0,2:T(8,128)} %fusion.52, bf16[128,8,128]{2,1,0:T(8,128)(2,1)S(1)} %copy-done.10, f32[8,128,480]{1,2,0:T(8,128)} %get-tuple-element.102, f32[8,128]{1,0:T(8,128)S(1)} %get-tuple-element.101), kind=kOutput, calls=%fused_computation.55 | convolution fusion | flops 129271264 | bytes 4444160 | tf_op jit(solution)/shard_map/rtk,trd->kd/dot_general | solution.py:124
  139.0 4.8 %fusion.26 = bf16[128,8,128]{0,2,1:T(8,128)(2,1)} fusion(f32[480,128,8]{1,0,2:T(8,128)} %fusion.52, bf16[480,4,128]{2,0,1:T(8,128)(2,1)} %copy-done.9, f32[8,128,480]{1,2,0:T(8,128)} %get-tuple-element.102, f32[8,128]{1,0:T(8,128)S(1)} %get-tuple-element.101), kind=kOutput, calls=%fused_computation.48 | convolution fusion | flops 129402336 | bytes 8257536 | tf_op jit(solution)/shard_map/rtk,kd->trd/dot_general | solution.py:121
  143.8 2.0 convolution_bitcast_fusion.1
  145.7 2.9 %fusion.137 = (f32[8,128]{1,0:T(8,128)S(1)}, f32[8,128,480]{1,2,0:T(8,128)}) fusion(pred[128,480]{0,1:T(8,128)(4,1)} %pad_add_fusion, bf16[128,8,128]{2,1,0:T(8,128)(2,1)} %get-tuple-element.63, bf16[480,4,128]{2,0,1:T(8,128)(2,1)} %copy-done.9), kind=kOutput, calls=%fused_computation.210 | convolution fusion | flops 127795680 | bytes 2416640 | tf_op jit(solution)/shard_map/sub | solution.py:112
  148.7 4.7 %convolution_bitcast_fusion.6 = f32[480,1,128]{2,0,1:T(8,128)} fusion(f32[480,128,8]{1,0,2:T(8,128)} %fusion.55, bf16[128,8,128]{2,1,0:T(8,128)(2,1)} %get-tuple-element.63, f32[8,128,480]{1,2,0:T(8,128)} %get-tuple-element.104, f32[8,128]{1,0:T(8,128)S(1)} %get-tuple-element.103), kind=kOutput, calls=%fused_computation.56 | convolution fusion | flops 129271264 | bytes 4444160 | tf_op jit(solution)/shard_map/rtk,trd->kd/dot_general | solution.py:124
  153.4 4.8 %fusion.25 = bf16[128,8,128]{0,2,1:T(8,128)(2,1)} fusion(f32[480,128,8]{1,0,2:T(8,128)} %fusion.55, bf16[480,4,128]{2,0,1:T(8,128)(2,1)} %copy-done.9, f32[8,128,480]{1,2,0:T(8,128)} %get-tuple-element.104, f32[8,128]{1,0:T(8,128)S(1)} %get-tuple-element.103), kind=kOutput, calls=%fused_computation.47 | convolution fusion | flops 129402336 | bytes 8257536 | tf_op jit(solution)/shard_map/rtk,kd->trd/dot_general | solution.py:121
  158.2 2.7 convolution_bitcast_fusion.2
  160.9 3.0 %fusion.131 = (f32[8,128]{1,0:T(8,128)S(1)}, f32[8,128,480]{1,2,0:T(8,128)}) fusion(pred[128,480]{0,1:T(8,128)(4,1)} %pad_add_fusion, bf16[128,8,128]{2,1,0:T(8,128)(2,1)} %get-tuple-element.64, bf16[480,4,128]{2,0,1:T(8,128)(2,1)} %copy-done.9), kind=kOutput, calls=%fused_computation.208 | convolution fusion | flops 127795680 | bytes 2416640 | tf_op jit(solution)/shard_map/sub | solution.py:112
  163.9 2.7 convolution_bitcast_fusion
  166.5 3.7 %fusion.27 = bf16[128,8,128]{0,2,1:T(8,128)(2,1)} fusion(f32[480,128,8]{1,0,2:T(8,128)S(1)} %fusion.49, bf16[480,4,128]{2,0,1:T(8,128)(2,1)} %copy-done.9, f32[8,128,480]{1,2,0:T(8,128)} %get-tuple-element.100, f32[8,128]{1,0:T(8,128)S(1)} %get-tuple-element.99), kind=kOutput, calls=%fused_computation.49 | convolution fusion | flops 129402336 | bytes 8257536 | tf_op jit(solution)/shard_map/rtk,kd->trd/dot_general | solution.py:121
  170.2 3.0 %convolution_bitcast_fusion.4 = f32[480,1,128]{2,0,1:T(8,128)S(1)} fusion(f32[480,128,8]{1,0,2:T(8,128)S(1)} %fusion.49, bf16[128,8,128]{2,1,0:T(8,128)(2,1)} %get-tuple-element.64, f32[8,128,480]{1,2,0:T(8,128)} %get-tuple-element.100, f32[8,128]{1,0:T(8,128)S(1)} %get-tuple-element.99), kind=kOutput, calls=%fused_computation.54 | convolution fusion | flops 129271264 | bytes 4444160 | tf_op jit(solution)/shard_map/rtk,trd->kd/dot_general | solution.py:124
  174.0 1.4 pad_maximum_fusion.1
  175.7 1.7 copy.53
  179.6 1.4 collective-permute-start.14
  186.3 75.2 %all-reduce.5.cloned.1.call-done = (f32[128,4,128]{2,0,1:T(8,128)}, f32[128,4,128]{2,0,1:T(8,128)}) async-done(((f32[128,4,128]{2,0,1:T(8,128)}, f32[128,4,128]{2,0,1:T(8,128)}), (f32[128,4,128]{2,0,1:T(8,128)}, f32[128,4,128]{2,0,1:T(8,128)})) %all-reduce.5.cloned.1.call-update) | async-done | bytes 524304 | tf_op jit(solution)/shard_map/psum | solution.py:155
  274.1 2.7 collective-permute-done.27
  280.2 2.4 collective-permute-done.22
  (151 shorter events, 49.7 us)
Async XLA Ops:
  7.2 38.0 %copy-start = (s32[64]{0:T(128)S(1)}, s32[64]{0:T(128)}, u32[]{:S(2)}) copy-start(s32[64]{0:T(128)} %param.21) | copy-start | bytes 772
  7.2 103.2 %all-reduce.7.cloned.1.call-start = ((), (), s32[]{:S(2)}) async-start(), calls=%async_computation.1 | async-start | bytes 524288 | tf_op jit(solution)/shard_map/psum | solution.py:14
  8.0 102.3 %collective-permute-start.13 = (bf16[32,4,128]{2,1,0:T(4,128)(2,1)S(1)}, bf16[32,4,128]{2,1,0:T(4,128)(2,1)S(1)}, u32[]{:S(2)}, u32[]{:S(2)}) collective-permute-start(bf16[32,4,128]{2,1,0:T(4,128)(2,1)S(1)} %slice.231), channel_id=1, source_target_pairs={{0,14},{1,15},{16,30},{17,31}} | collective-permute-start | bytes 98312 | tf_op jit(solution)/shard_map/ppermute | solution.py:20
  15.9 94.3 %collective-permute-start.12 = (bf16[32,4,128]{2,1,0:T(4,128)(2,1)S(1)}, bf16[32,4,128]{2,1,0:T(4,128)(2,1)S(1)}, u32[]{:S(2)}, u32[]{:S(2)}) collective-permute-start(bf16[32,4,128]{2,1,0:T(4,128)(2,1)S(1)} %slice.231), channel_id=1, source_target_pairs={{0,12},{2,14},{1,13},{3,15},{16,28},{18,30},{17,29},{19,31}} | collective-permute-start | bytes 98312 | tf_op jit(solution)/shard_map/ppermute | solution.py:20
  17.2 92.9 %collective-permute-start.11 = (bf16[32,4,128]{2,1,0:T(4,128)(2,1)S(1)}, bf16[32,4,128]{2,1,0:T(4,128)(2,1)S(1)}, u32[]{:S(2)}, u32[]{:S(2)}) collective-permute-start(bf16[32,4,128]{2,1,0:T(4,128)(2,1)S(1)} %slice.231), channel_id=1, source_target_pairs={{0,10},{2,12},{4,14},{1,11},{3,13},{5,15},{16,26},{18,28},{20,30},... | collective-permute-start | bytes 98312 | tf_op jit(solution)/shard_map/ppermute | solution.py:20
  18.5 91.6 %collective-permute-start.10 = (bf16[32,4,128]{2,1,0:T(4,128)(2,1)S(1)}, bf16[32,4,128]{2,1,0:T(4,128)(2,1)S(1)}, u32[]{:S(2)}, u32[]{:S(2)}) collective-permute-start(bf16[32,4,128]{2,1,0:T(4,128)(2,1)S(1)} %slice.231), channel_id=1, source_target_pairs={{0,8},{2,10},{4,12},{6,14},{1,9},{3,11},{5,13},{7,15},{16,24},{18,... | collective-permute-start | bytes 98312 | tf_op jit(solution)/shard_map/ppermute | solution.py:20
  20.6 39.5 %collective-permute-start = (bf16[32,4,128]{2,1,0:T(4,128)(2,1)S(1)}, bf16[32,4,128]{2,1,0:T(4,128)(2,1)S(1)}, u32[]{:S(2)}, u32[]{:S(2)}) collective-permute-start(bf16[32,4,128]{2,1,0:T(4,128)(2,1)S(1)} %slice.226), channel_id=1, source_target_pairs={{0,2},{2,4},{4,6},{6,8},{8,10},{10,12},{12,14},{1,3},{3,5},{5,7},{... | collective-permute-start | bytes 98312 | tf_op jit(solution)/shard_map/ppermute | solution.py:20
  26.2 235.3 %all-reduce.5.cloned.1.call-start = ((), (), s32[]{:S(2)}) async-start(), calls=%async_computation | async-start | bytes 1048576 | tf_op jit(solution)/shard_map/psum | solution.py:155
  45.2 2.4 copy-start.2
  45.8 2.9 copy-start.16
  45.8 2.9 copy-start.17
  45.8 2.9 copy-start.18
  45.9 2.9 copy-start.19
  45.9 2.9 copy-start.20
  45.9 2.8 copy-start.21
  45.9 2.8 copy-start.22
  45.9 12.8 %copy-start.1 = (bf16[128,32,128]{2,1,0:T(8,128)(2,1)S(1)}, bf16[128,32,128]{2,1,0:T(8,128)(2,1)}, u32[]{:S(2)}) copy-start(bf16[128,32,128]{2,1,0:T(8,128)(2,1)} %param.19) | copy-start | bytes 3145732
  60.0 4.9 %collective-permute-start.7 = (bf16[32,4,128]{2,1,0:T(4,128)(2,1)S(1)}, bf16[32,4,128]{2,1,0:T(4,128)(2,1)S(1)}, u32[]{:S(2)}, u32[]{:S(2)}) collective-permute-start(bf16[32,4,128]{2,1,0:T(4,128)(2,1)S(1)} %slice.231), channel_id=1, source_target_pairs={{0,2},{2,4},{4,6},{6,8},{8,10},{10,12},{12,14},{1,3},{3,5},{5,7},{... | collective-permute-start | bytes 98312 | tf_op jit(solution)/shard_map/ppermute | solution.py:20
  65.0 5.8 %collective-permute-start.1 = (bf16[32,4,128]{2,1,0:T(4,128)(2,1)S(1)}, bf16[32,4,128]{2,1,0:T(4,128)(2,1)S(1)}, u32[]{:S(2)}, u32[]{:S(2)}) collective-permute-start(bf16[32,4,128]{2,1,0:T(4,128)(2,1)S(1)} %slice.226), channel_id=1, source_target_pairs={{0,4},{2,6},{4,8},{6,10},{8,12},{10,14},{1,5},{3,7},{5,9},{7,11},{... | collective-permute-start | bytes 98312 | tf_op jit(solution)/shard_map/ppermute | solution.py:20
  70.8 4.7 %collective-permute-start.2 = (bf16[32,4,128]{2,1,0:T(4,128)(2,1)S(1)}, bf16[32,4,128]{2,1,0:T(4,128)(2,1)S(1)}, u32[]{:S(2)}, u32[]{:S(2)}) collective-permute-start(bf16[32,4,128]{2,1,0:T(4,128)(2,1)S(1)} %slice.226), channel_id=1, source_target_pairs={{0,6},{2,8},{4,10},{6,12},{8,14},{1,7},{3,9},{5,11},{7,13},{9,15},... | collective-permute-start | bytes 98312 | tf_op jit(solution)/shard_map/ppermute | solution.py:20
  75.4 8.4 %collective-permute-start.3 = (bf16[32,4,128]{2,1,0:T(4,128)(2,1)S(1)}, bf16[32,4,128]{2,1,0:T(4,128)(2,1)S(1)}, u32[]{:S(2)}, u32[]{:S(2)}) collective-permute-start(bf16[32,4,128]{2,1,0:T(4,128)(2,1)S(1)} %slice.226), channel_id=1, source_target_pairs={{0,8},{2,10},{4,12},{6,14},{1,9},{3,11},{5,13},{7,15},{16,24},{18,... | collective-permute-start | bytes 98312 | tf_op jit(solution)/shard_map/ppermute | solution.py:20
  83.9 5.0 %collective-permute-start.4 = (bf16[32,4,128]{2,1,0:T(4,128)(2,1)S(1)}, bf16[32,4,128]{2,1,0:T(4,128)(2,1)S(1)}, u32[]{:S(2)}, u32[]{:S(2)}) collective-permute-start(bf16[32,4,128]{2,1,0:T(4,128)(2,1)S(1)} %slice.226), channel_id=1, source_target_pairs={{0,10},{2,12},{4,14},{1,11},{3,13},{5,15},{16,26},{18,28},{20,30},... | collective-permute-start | bytes 98312 | tf_op jit(solution)/shard_map/ppermute | solution.py:20
  88.9 9.5 %collective-permute-start.5 = (bf16[32,4,128]{2,1,0:T(4,128)(2,1)S(1)}, bf16[32,4,128]{2,1,0:T(4,128)(2,1)S(1)}, u32[]{:S(2)}, u32[]{:S(2)}) collective-permute-start(bf16[32,4,128]{2,1,0:T(4,128)(2,1)S(1)} %slice.226), channel_id=1, source_target_pairs={{0,12},{2,14},{1,13},{3,15},{16,28},{18,30},{17,29},{19,31}} | collective-permute-start | bytes 98312 | tf_op jit(solution)/shard_map/ppermute | solution.py:20
  98.3 6.0 %collective-permute-start.6 = (bf16[32,4,128]{2,1,0:T(4,128)(2,1)S(1)}, bf16[32,4,128]{2,1,0:T(4,128)(2,1)S(1)}, u32[]{:S(2)}, u32[]{:S(2)}) collective-permute-start(bf16[32,4,128]{2,1,0:T(4,128)(2,1)S(1)} %slice.226), channel_id=1, source_target_pairs={{0,14},{1,15},{16,30},{17,31}} | collective-permute-start | bytes 98312 | tf_op jit(solution)/shard_map/ppermute | solution.py:20
  104.3 2.9 collective-permute-start.8
  107.2 2.9 collective-permute-start.9
  111.4 13.2 %copy-start.9 = (bf16[480,4,128]{2,0,1:T(8,128)(2,1)}, bf16[480,4,128]{2,0,1:T(8,128)(2,1)S(1)}, u32[]{:S(2)}) copy-start(bf16[480,4,128]{2,0,1:T(8,128)(2,1)S(1)} %get-tuple-element.111) | copy-start | bytes 1474564
  129.4 2.0 copy-start.10
  170.2 3.7 %copy-start.5 = (f32[480,1,128]{2,0,1:T(8,128)S(1)}, f32[480,1,128]{2,0,1:T(8,128)}, u32[]{:S(2)}) copy-start(f32[480,1,128]{2,0,1:T(8,128)} %convolution_bitcast_fusion.7) | copy-start | bytes 737284
  170.2 3.7 %copy-start.6 = (f32[480,1,128]{2,0,1:T(8,128)S(1)}, f32[480,1,128]{2,0,1:T(8,128)}, u32[]{:S(2)}) copy-start(f32[480,1,128]{2,0,1:T(8,128)} %convolution_bitcast_fusion.5) | copy-start | bytes 737284
  170.2 3.7 %copy-start.7 = (f32[480,1,128]{2,0,1:T(8,128)S(1)}, f32[480,1,128]{2,0,1:T(8,128)}, u32[]{:S(2)}) copy-start(f32[480,1,128]{2,0,1:T(8,128)} %convolution_bitcast_fusion.6) | copy-start | bytes 737284
  175.5 2.5 copy-start.3
  175.5 2.5 copy-start.4
  179.6 83.0 %copy-start.15 = (bf16[32,4,128]{2,0,1:T(8,128)(2,1)S(1)}, bf16[32,4,128]{2,0,1:T(8,128)(2,1)}, u32[]{:S(2)}) copy-start(bf16[32,4,128]{2,0,1:T(8,128)(2,1)} %get-tuple-element.77) | copy-start | bytes 98308
  179.6 83.0 %collective-permute-start.14 = (bf16[32,4,128]{2,0,1:T(8,128)(2,1)}, bf16[32,4,128]{2,0,1:T(8,128)(2,1)S(1)}, u32[]{:S(2)}, u32[]{:S(2)}) collective-permute-start(bf16[32,4,128]{2,0,1:T(8,128)(2,1)} %get-tuple-element.72), channel_id=1, source_target_pairs={{2,0},{4,2},{6,4},{8,6},{10,8},{12,10},{14,12},{3,1},{5,3},{7,5},{... | collective-permute-start | bytes 98312 | tf_op jit(solution)/shard_map/ppermute | solution.py:20
  181.0 82.9 %collective-permute-start.20 = (bf16[32,4,128]{2,0,1:T(8,128)(2,1)}, bf16[32,4,128]{2,0,1:T(8,128)(2,1)S(1)}, u32[]{:S(2)}, u32[]{:S(2)}) collective-permute-start(bf16[32,4,128]{2,0,1:T(8,128)(2,1)} %get-tuple-element.73), channel_id=1, source_target_pairs={{14,0},{15,1},{30,16},{31,17}} | collective-permute-start | bytes 98312 | tf_op jit(solution)/shard_map/ppermute | solution.py:20
  182.3 82.9 %collective-permute-start.19 = (bf16[32,4,128]{2,0,1:T(8,128)(2,1)}, bf16[32,4,128]{2,0,1:T(8,128)(2,1)S(1)}, u32[]{:S(2)}, u32[]{:S(2)}) collective-permute-start(bf16[32,4,128]{2,0,1:T(8,128)(2,1)} %get-tuple-element.74), channel_id=1, source_target_pairs={{12,0},{14,2},{13,1},{15,3},{28,16},{30,18},{29,17},{31,19}} | collective-permute-start | bytes 98312 | tf_op jit(solution)/shard_map/ppermute | solution.py:20
  183.6 82.9 %collective-permute-start.18 = (bf16[32,4,128]{2,0,1:T(8,128)(2,1)}, bf16[32,4,128]{2,0,1:T(8,128)(2,1)S(1)}, u32[]{:S(2)}, u32[]{:S(2)}) collective-permute-start(bf16[32,4,128]{2,0,1:T(8,128)(2,1)} %get-tuple-element.75), channel_id=1, source_target_pairs={{10,0},{12,2},{14,4},{11,1},{13,3},{15,5},{26,16},{28,18},{30,20},... | collective-permute-start | bytes 98312 | tf_op jit(solution)/shard_map/ppermute | solution.py:20
  184.9 83.9 %collective-permute-start.17 = (bf16[32,4,128]{2,0,1:T(8,128)(2,1)}, bf16[32,4,128]{2,0,1:T(8,128)(2,1)S(1)}, u32[]{:S(2)}, u32[]{:S(2)}) collective-permute-start(bf16[32,4,128]{2,0,1:T(8,128)(2,1)} %get-tuple-element.76), channel_id=1, source_target_pairs={{8,0},{10,2},{12,4},{14,6},{9,1},{11,3},{13,5},{15,7},{24,16},{26,... | collective-permute-start | bytes 98312 | tf_op jit(solution)/shard_map/ppermute | solution.py:20
  262.6 7.6 %collective-permute-start.16 = (bf16[32,4,128]{2,0,1:T(8,128)(2,1)S(1)}, bf16[32,4,128]{2,0,1:T(8,128)(2,1)S(1)}, u32[]{:S(2)}, u32[]{:S(2)}) collective-permute-start(bf16[32,4,128]{2,0,1:T(8,128)(2,1)S(1)} %copy-done.15), channel_id=1, source_target_pairs={{6,0},{8,2},{10,4},{12,6},{14,8},{7,1},{9,3},{11,5},{13,7},{15,9},... | collective-permute-start | bytes 98312 | tf_op jit(solution)/shard_map/ppermute | solution.py:20
  263.9 7.6 %collective-permute-start.15 = (bf16[32,4,128]{2,0,1:T(8,128)(2,1)S(1)}, bf16[32,4,128]{2,0,1:T(8,128)(2,1)S(1)}, u32[]{:S(2)}, u32[]{:S(2)}) collective-permute-start(bf16[32,4,128]{2,0,1:T(8,128)(2,1)S(1)} %get-tuple-element.78), channel_id=1, source_target_pairs={{4,0},{6,2},{8,4},{10,6},{12,8},{14,10},{5,1},{7,3},{9,5},{11,7},{... | collective-permute-start | bytes 98312 | tf_op jit(solution)/shard_map/ppermute | solution.py:20
  265.2 7.6 %collective-permute-start.21 = (bf16[32,4,128]{2,0,1:T(8,128)(2,1)S(1)}, bf16[32,4,128]{2,0,1:T(8,128)(2,1)S(1)}, u32[]{:S(2)}, u32[]{:S(2)}) collective-permute-start(bf16[32,4,128]{2,0,1:T(8,128)(2,1)S(1)} %get-tuple-element.65), channel_id=1, source_target_pairs={{2,0},{4,2},{6,4},{8,6},{10,8},{12,10},{14,12},{3,1},{5,3},{7,5},{... | collective-permute-start | bytes 98312 | tf_op jit(solution)/shard_map/ppermute | solution.py:20
  266.5 10.3 %collective-permute-start.27 = (bf16[32,4,128]{2,0,1:T(8,128)(2,1)S(1)}, bf16[32,4,128]{2,0,1:T(8,128)(2,1)S(1)}, u32[]{:S(2)}, u32[]{:S(2)}) collective-permute-start(bf16[32,4,128]{2,0,1:T(8,128)(2,1)S(1)} %get-tuple-element.66), channel_id=1, source_target_pairs={{14,0},{15,1},{30,16},{31,17}} | collective-permute-start | bytes 98312 | tf_op jit(solution)/shard_map/ppermute | solution.py:20
  268.8 10.2 %collective-permute-start.26 = (bf16[32,4,128]{2,0,1:T(8,128)(2,1)S(1)}, bf16[32,4,128]{2,0,1:T(8,128)(2,1)S(1)}, u32[]{:S(2)}, u32[]{:S(2)}) collective-permute-start(bf16[32,4,128]{2,0,1:T(8,128)(2,1)S(1)} %get-tuple-element.67), channel_id=1, source_target_pairs={{12,0},{14,2},{13,1},{15,3},{28,16},{30,18},{29,17},{31,19}} | collective-permute-start | bytes 98312 | tf_op jit(solution)/shard_map/ppermute | solution.py:20
  270.1 8.9 %collective-permute-start.25 = (bf16[32,4,128]{2,0,1:T(8,128)(2,1)S(1)}, bf16[32,4,128]{2,0,1:T(8,128)(2,1)S(1)}, u32[]{:S(2)}, u32[]{:S(2)}) collective-permute-start(bf16[32,4,128]{2,0,1:T(8,128)(2,1)S(1)} %get-tuple-element.68), channel_id=1, source_target_pairs={{10,0},{12,2},{14,4},{11,1},{13,3},{15,5},{26,16},{28,18},{30,20},... | collective-permute-start | bytes 98312 | tf_op jit(solution)/shard_map/ppermute | solution.py:20
  271.4 7.6 %collective-permute-start.24 = (bf16[32,4,128]{2,0,1:T(8,128)(2,1)S(1)}, bf16[32,4,128]{2,0,1:T(8,128)(2,1)S(1)}, u32[]{:S(2)}, u32[]{:S(2)}) collective-permute-start(bf16[32,4,128]{2,0,1:T(8,128)(2,1)S(1)} %get-tuple-element.69), channel_id=1, source_target_pairs={{8,0},{10,2},{12,4},{14,6},{9,1},{11,3},{13,5},{15,7},{24,16},{26,... | collective-permute-start | bytes 98312 | tf_op jit(solution)/shard_map/ppermute | solution.py:20
  272.8 7.5 %collective-permute-start.23 = (bf16[32,4,128]{2,0,1:T(8,128)(2,1)S(1)}, bf16[32,4,128]{2,0,1:T(8,128)(2,1)S(1)}, u32[]{:S(2)}, u32[]{:S(2)}) collective-permute-start(bf16[32,4,128]{2,0,1:T(8,128)(2,1)S(1)} %get-tuple-element.70), channel_id=1, source_target_pairs={{6,0},{8,2},{10,4},{12,6},{14,8},{7,1},{9,3},{11,5},{13,7},{15,9},... | collective-permute-start | bytes 98312 | tf_op jit(solution)/shard_map/ppermute | solution.py:20
  276.8 5.8 %collective-permute-start.22 = (bf16[32,4,128]{2,0,1:T(8,128)(2,1)S(1)}, bf16[32,4,128]{2,0,1:T(8,128)(2,1)S(1)}, u32[]{:S(2)}, u32[]{:S(2)}) collective-permute-start(bf16[32,4,128]{2,0,1:T(8,128)(2,1)S(1)} %get-tuple-element.71), channel_id=1, source_target_pairs={{4,0},{6,2},{8,4},{10,6},{12,8},{14,10},{5,1},{7,3},{9,5},{11,7},{... | collective-permute-start | bytes 98312 | tf_op jit(solution)/shard_map/ppermute | solution.py:20
  (5 other events, 7.0 us)
Sparse Core Ops, SparseCore 0:
  26.4 69.0 all-reduce.6
  179.0 82.4 all-reduce.4
where the time goes:
time: 292 us; the launch traced here: 290 us
  waiting for transfers between devices  95.6 us (33%)
  starting transfers between devices  68.2 us (23%)
  matrix products  61.8 us (21%)
  local copies, waits for them, and re-layouts  22.9 us (8%)
  between operations  22.3 us (8%)
  other arithmetic  19.5 us (7%)
    psum x1, waiting for transfers between devices, per_device(): total_k, total_v = lax.psum((prompt_grad_k, prompt_grad_v), 'node')  75.2 us
    ppermute x28, starting transfers between devices, from_behind(): return lax.ppermute(block, axis, route)  68.2 us
    ppermute x28, waiting for transfers between devices, from_behind(): return lax.ppermute(block, axis, route)  20.3 us
    dot_general x4, matrix products, per_device(): jnp.einsum('rtk,kd->trd', grad_scores, key_group, preferred_element_type=...  18 us
    dot_general x4, matrix products, per_device(): jnp.einsum('rtk,trd->kd', grad_scores, query_group, preferred_element_typ...  17.2 us
    sub x4, matrix products, per_device(): probs = jnp.exp(scores - row_top)  11.8 us
    dot_general x4, matrix products, per_device(): jnp.einsum('rtk,trd->kd', probs_low, grad_group, preferred_element_type=j...  9.3 us
    dynamic_slice x6, local copies, waits for them, and re-layouts, per_device(): cursor = jnp.where(active, parents[jnp.maximum(owner_dev, 0) * TD], cursor)  7.45 us
  transfers between devices with their start and end apart: 30, of which 13 were waited for; matrix products, arithmetic and copies ran while one was open for 12% of the time, Pallas kernels for 0%

commit v1 on v0

v1 whole, which is shorter than its diff:
```python
import functools
import math

import jax
import jax.numpy as jnp
from jax import lax
from jax.experimental import pallas as pl
from jax.experimental.pallas import tpu as pltpu
from jax.sharding import PartitionSpec as P

TILE = 16
TD = 8
CAP = 2
W = 7
GROUPS_PER_STEP = 2
CHUNK = 32
MASKED = -1e30
BF16 = jnp.bfloat16
F32 = jnp.float32


def shifted(block, distance, size):
    route = [(i - distance, i) for i in range(size) if 0 <= i - distance < size]
    return lax.ppermute(block, "node", route)


def tree_strides(size):
    strides = []
    stride = 1
    while stride < size:
        strides.append(stride)
        stride *= 2
    return strides


def column_limits(device, window, parents, lengths):
    cursor = parents[device * TD]
    need = [jnp.int32(0)] * (window + 1)
    for _ in range(W):
        owner = jnp.where(cursor < 0, -1, lax.div(jnp.maximum(cursor, 0), TD))
        distance = device - owner
        active = (owner >= 1) & (distance >= 1) & (distance <= W)
        depth = lax.rem(jnp.maximum(cursor, 0), TD) + 1
        for k in range(1, window + 1):
            need[k] = jnp.where(active & (distance == k), depth, need[k])
        cursor = jnp.where(active, parents[jnp.maximum(owner, 0) * TD], cursor)
    limits = [jnp.where(device >= 1, lengths[t], 0) for t in range(TD)]
    for k in range(1, window + 1):
        owner = device - k
        for c in range(CAP):
            seen = (owner >= 1) & (c < need[k])
            limits.append(jnp.where(seen, lengths[jnp.maximum(owner, 0) * TD + c], 0))
    limits += [lengths[device * TD + t] for t in range(TD)]
    return limits


def attention_kernel(rounds, window, heads_kv, scale, *refs):
    parents, lengths = refs[:2]
    prompt = refs[2 : 2 + rounds]
    behind = refs[2 + rounds : 2 + rounds + window]
    keys, values, q_ref, g_ref = refs[2 + rounds + window : 6 + rounds + window]
    dq_ref, dprompt_ref, dbehind_ref, dk_ref, dv_ref = refs[6 + rounds + window : 11 + rounds + window]
    kh, vh, bias, acc_k, acc_v, wide = refs[11 + rounds + window :]
    tokens = TD * TILE
    front = CAP * TILE
    before = tokens + window * front
    step = pl.program_id(0)
    device = lax.axis_index("node")

    @pl.when(step == 0)
    def _():
        def split(block, heads_ref, start, count):
            wide[: count * heads_kv] = block
            for h in range(heads_kv):
                heads_ref[h, start : start + count] = wide[pl.ds(h, count, stride=heads_kv), :].astype(BF16)

        for side, heads_ref, own in ((0, kh, keys), (1, vh, values)):
            block = prompt[0][side].astype(F32)
            for r in range(1, rounds):
                block = block + prompt[r][side].astype(F32)
            split(block, heads_ref, 0, tokens)
            for k in range(window):
                split(behind[k][side].astype(F32), heads_ref, tokens + k * front, front)
            split(own[...].astype(F32), heads_ref, before, tokens)
        place = lax.broadcasted_iota(jnp.int32, (TILE, 128), 0)
        for t, limit in enumerate(column_limits(device, window, parents, lengths)):
            bias[t * TILE : (t + 1) * TILE] = jnp.where(place < limit, 0.0, MASKED)

    columns = CHUNK * 8
    column_token = lax.broadcasted_iota(jnp.int32, (CHUNK, columns), 1) // 8
    causal = jnp.where(lax.broadcasted_iota(jnp.int32, (CHUNK, columns), 0) <= column_token, 0.0, MASKED)
    lane_place = lax.broadcasted_iota(jnp.int32, (1, 128), 1) // 8

    for c in reversed(range(tokens // CHUNK)):
        rows = before + (c + 1) * CHUNK
        live = jnp.concatenate(
            [
                jnp.where(lane_place < lengths[device * TD + c * (CHUNK // TILE) + t], 1.0, 0.0)
                for t in range(CHUNK // TILE)
            ],
            axis=1,
        )
        q_all = q_ref[c * CHUNK : (c + 1) * CHUNK].astype(F32)
        g_all = g_ref[c * CHUNK : (c + 1) * CHUNK].astype(F32)
        dq_parts = []
        for part in range(GROUPS_PER_STEP):
            head = step * GROUPS_PER_STEP + part
            q = q_all[:, part * 8 : (part + 1) * 8].reshape(columns, 128).astype(BF16)
            g = g_all[:, part * 8 : (part + 1) * 8].reshape(columns, 128).astype(BF16)
            k = kh[head, :rows]
            v = vh[head, :rows]
            s = lax.dot_general(k, q, (((1,), (1,)), ((), ())), preferred_element_type=F32)
            column_bias = bias[:rows]
            s = s + jnp.concatenate([column_bias] * (columns // 128), axis=1)
            s = jnp.concatenate([s[: rows - CHUNK], s[rows - CHUNK :] + causal], axis=0)
            top = jnp.max(s, axis=0, keepdims=True)
            e = jnp.exp2((s - top) * (scale * math.log2(math.e)))
            total = jnp.sum(e, axis=0, keepdims=True)
            dp = lax.dot_general(v, g, (((1,), (1,)), ((), ())), preferred_element_type=F32)
            weight = live / total
            p = e * weight
            delta = jnp.sum(p * dp, axis=0, keepdims=True)
            ds = (p * (dp - delta) * scale).astype(BF16)
            p = p.astype(BF16)
            dk = jnp.dot(ds, q, preferred_element_type=F32)
            dv = jnp.dot(p, g, preferred_element_type=F32)
            if c == tokens // CHUNK - 1:
                acc_k[head, :rows] = dk
                acc_v[head, :rows] = dv
            else:
                acc_k[head, :rows] += dk
                acc_v[head, :rows] += dv
            dq = lax.dot_general(k, ds, (((0,), (0,)), ((), ())), preferred_element_type=F32)
            dq_parts.append(dq.T.reshape(CHUNK, 8, 128))
        dq_ref[c * CHUNK : (c + 1) * CHUNK] = jnp.concatenate(dq_parts, axis=1).astype(BF16)

    @pl.when(step == pl.num_programs(0) - 1)
    def _():
        def join(acc, start, count):
            for h in range(heads_kv):
                wide[pl.ds(h, count, stride=heads_kv), :] = acc[h, start : start + count]
            return wide[: count * heads_kv]

        for side, acc, own in ((0, acc_k, dk_ref), (1, acc_v, dv_ref)):
            dprompt_ref[side] = join(acc, 0, tokens).astype(BF16)
            for k in range(window):
                dbehind_ref[k, side] = join(acc, tokens + k * front, front).astype(BF16)
            own[...] = join(acc, before, tokens)


def attention(prompt, behind, keys, values, queries, grad_out, parents, lengths, heads_kv):
    tokens, heads_q, head_size = queries.shape
    window = len(behind)
    rounds = len(prompt)
    front = CAP * TILE
    all_rows = 2 * tokens + window * front
    step_heads = 8 * GROUPS_PER_STEP
    smem = pl.BlockSpec(memory_space=pltpu.SMEM)

    def whole(shape):
        return pl.BlockSpec(shape, lambda i: (0,) * len(shape))

    by_heads = pl.BlockSpec((tokens, step_heads, head_size), lambda i: (0, i, 0))
    products = 5 * 2 * tokens * heads_q * head_size * all_rows
    return pl.pallas_call(
        functools.partial(attention_kernel, rounds, window, heads_kv, head_size**-0.5),
        grid=(heads_q // step_heads,),
        in_specs=[smem, smem]
        + [whole(a.shape) for a in (*prompt, *behind, keys, values)]
        + [by_heads, by_heads],
        out_specs=[
            by_heads,
            whole((2, tokens * heads_kv, head_size)),
            whole((window, 2, front * heads_kv, head_size)),
            whole((tokens * heads_kv, head_size)),
            whole((tokens * heads_kv, head_size)),
        ],
        out_shape=[
            jax.ShapeDtypeStruct(queries.shape, BF16),
            jax.ShapeDtypeStruct((2, tokens * heads_kv, head_size), BF16),
            jax.ShapeDtypeStruct((window, 2, front * heads_kv, head_size), BF16),
            jax.ShapeDtypeStruct((tokens * heads_kv, head_size), F32),
            jax.ShapeDtypeStruct((tokens * heads_kv, head_size), F32),
        ],
        scratch_shapes=[
            pltpu.VMEM((heads_kv, all_rows, head_size), BF16),
            pltpu.VMEM((heads_kv, all_rows, head_size), BF16),
            pltpu.VMEM((all_rows, 128), F32),
            pltpu.VMEM((heads_kv, all_rows, head_size), F32),
            pltpu.VMEM((heads_kv, all_rows, head_size), F32),
            pltpu.VMEM((tokens * heads_kv, head_size), F32),
        ],
        compiler_params=pltpu.CompilerParams(vmem_limit_bytes=40 * 1024 * 1024),
        cost_estimate=pl.CostEstimate(
            flops=products, bytes_accessed=4 * 1024 * 1024, transcendentals=tokens * heads_q * all_rows
        ),
        name="tree_attention_backward",
    )(parents, lengths, *prompt, *behind, keys, values, queries, grad_out)


def per_device(size, queries, keys, values, grad_out, parents, lengths):
    tokens, heads_kv, head_size = keys.shape
    rows = tokens * heads_kv
    front = CAP * TILE * heads_kv
    window = max(1, min(W, size - 2))
    device = lax.axis_index("node")
    keys = keys.reshape(rows, head_size)
    values = values.reshape(rows, head_size)
    pair = jnp.stack([keys, values])
    strides = tree_strides(size)

    prompt = []
    held = pair
    for stride in reversed(strides):
        route = [(i, i + stride) for i in range(0, size, 2 * stride) if i + stride < size]
        arrived = lax.ppermute(held, "node", route)
        prompt.append(arrived)
        if stride > 1:
            held = jnp.where(lax.rem(device, 2 * stride) == 0, held, arrived)
    head = pair[:, :front]
    behind = [shifted(head, k, size) for k in range(1, window + 1)]

    grad_queries, dprompt, dbehind, dk, dv = attention(
        prompt, behind, keys, values, queries, grad_out, parents, lengths, heads_kv
    )

    total = dprompt
    for stride in strides:
        route = [(i + stride, i) for i in range(0, size, 2 * stride) if i + stride < size]
        arrived = lax.ppermute(total, "node", route)
        total = (total.astype(F32) + arrived.astype(F32)).astype(BF16 if stride < strides[-1] else F32)
    back = sum(shifted(dbehind[k - 1], -k, size).astype(F32) for k in range(1, window + 1))
    total = jnp.where(device == 0, total, 0.0)
    own = []
    for side, local in ((0, dk), (1, dv)):
        whole = local + total[side]
        own.append(whole.at[:front].add(back[side]).reshape(tokens, heads_kv, head_size))
    return grad_queries, own[0], own[1]


def solution(mesh):
    by_token = P(("leaf", "node"), "tensor", None)
    return jax.shard_map(
        functools.partial(per_device, mesh.shape["node"]),
        mesh=mesh,
        in_specs=(by_token, by_token, by_token, by_token, P("leaf"), P("leaf")),
        out_specs=(by_token, by_token, by_token),
        check_vma=False,
    )
```

time: 292 us -> 86.7 us (0.30)
  matrix products: 61.8 us -> 0 us
  waiting for transfers between devices: 95.6 us -> 34.9 us
  starting transfers between devices: 68.2 us -> 37.1 us
  local copies, waits for them, and re-layouts: 22.9 us -> 1.48 us
  between operations: 22.3 us -> 0.97 us
  other arithmetic: 19.5 us -> 1.48 us
  Pallas kernels: 0 us -> 10.3 us
    psum x2 -> x0, waiting for transfers between devices: 75.3 us -> none  [the longest x1 75.2 us: per_device(): total_k, total_v = lax.psum((prompt_grad_k, prompt_grad_v), 'node')]
    dot_general x16 -> x0, matrix products: 50 us -> none  [the longest x4 18 us: per_device(): jnp.einsum('rtk,kd->trd', grad_scores, key_group, preferred_element_type=...]
    ppermute x28 -> x18, starting transfers between devices: 68.2 us -> 37.1 us  [the longest x12 24.7 us: shifted(): return lax.ppermute(block, 'node', route)]
    ppermute x28 -> x18, waiting for transfers between devices: 20.3 us -> 34.9 us  [the longest x3 16.4 us: per_device(): arrived = lax.ppermute(total, 'node', route)]
    sub x4 -> x0, matrix products: 11.8 us -> none  [per_device(): probs = jnp.exp(scores - row_top)]
    pallas_call x0 -> x1, Pallas kernels: none -> 10.3 us  [attention(): pl.pallas_call(functools.partial(attention_kernel, rounds, window, heads_...]
    dynamic_slice x8 -> x0, local copies, waits for them, and re-layouts: 9.43 us -> none  [the longest x6 7.45 us: per_device(): cursor = jnp.where(active, parents[jnp.maximum(owner_dev, 0) * TD], cursor)]
    and x3 -> x0, other arithmetic: 5.18 us -> none  [the longest x1 4.99 us: per_device(): prompt_seen & ((jnp.arange(tokens_per_device) >= front_rows) | jnp.logica...]
  transfers between devices with their start and end apart: 30 -> 18, of which waited for: 13 -> 10; matrix products, arithmetic and copies ran while one was open for 12% -> 0% of each run, Pallas kernels for 0% -> 0%
where the time goes in v1:
time: 86.7 us; the launch traced here: 86.2 us
  starting transfers between devices  37.1 us (43%)
  waiting for transfers between devices  34.9 us (40%)
  Pallas kernels  10.3 us (12%)
  local copies, waits for them, and re-layouts  1.48 us (2%)
  other arithmetic  1.48 us (2%)
  between operations  0.97 us (1%)
    ppermute x12, starting transfers between devices, shifted(): return lax.ppermute(block, 'node', route)  24.7 us
    ppermute x3, waiting for transfers between devices, per_device(): arrived = lax.ppermute(total, 'node', route)  16.4 us
    ppermute x3, waiting for transfers between devices, per_device(): arrived = lax.ppermute(held, 'node', route)  10.4 us
    pallas_call x1, Pallas kernels, attention(): pl.pallas_call(functools.partial(attention_kernel, rounds, window, heads_...  10.3 us
    ppermute x3, starting transfers between devices, per_device(): arrived = lax.ppermute(held, 'node', route)  8.57 us
    ppermute x12, waiting for transfers between devices, shifted(): return lax.ppermute(block, 'node', route)  8.01 us
    ppermute x3, starting transfers between devices, per_device(): arrived = lax.ppermute(total, 'node', route)  3.85 us
  transfers between devices with their start and end apart: 18, of which 10 were waited for; matrix products, arithmetic and copies ran while one was open for 0% of the time, Pallas kernels for 0%

profile of v1, /device:TPU:0, one launch (start us, length us, event | category | flops | bytes accessed | tf_op | source)
XLA Modules:
  0.0 86.2 jit_solution(17415532558822817096)
XLA Ops:
  0.7 1.0 %pad_maximum_fusion = bf16[2,512,128]{2,1,0:T(8,128)(2,1)S(1)} fusion(bf16[1,512,128]{2,1,0:T(8,128)(2,1)} %bitcast.38, bf16[1,512,128]{2,1,0:T(8,128)(2,1)} %bitcast.43), kind=kLoop, calls=%fused_computation.4 | loop fusion | flops 131072 | bytes 524288 | tf_op jit(solution)/shard_map/stack | solution.py:209
  1.7 6.0 %collective-permute-start = (bf16[2,512,128]{2,1,0:T(8,128)(2,1)S(1)}, bf16[2,512,128]{2,1,0:T(8,128)(2,1)S(1)}, u32[]{:S(2)}, u32[]{:S(2)}) collective-permute-start(bf16[2,512,128]{2,1,0:T(8,128)(2,1)S(1)} %pad_maximum_fusion), channel_id=1, source_target_pairs={{0,8},{1,9},{16,24},{17,25}} | collective-permute-start | bytes 786440 | tf_op jit(solution)/shard_map/ppermute | solution.py:216
  7.7 0.0 copy-start.2
  7.7 0.0 copy-start.3
  7.7 5.5 %collective-permute-done.refs_2_ = bf16[2,512,128]{2,1,0:T(8,128)(2,1)S(1)} collective-permute-done((bf16[2,512,128]{2,1,0:T(8,128)(2,1)S(1)}, bf16[2,512,128]{2,1,0:T(8,128)(2,1)S(1)}, u32[]{:S(2)}, u32[]{:S(2)}) %collective-permute-start) | collective-permute-done | bytes 262176 | tf_op jit(solution)/shard_map/ppermute | solution.py:216
  13.2 1.3 %collective-permute-start.1 = (bf16[2,512,128]{2,1,0:T(8,128)(2,1)S(1)}, bf16[2,512,128]{2,1,0:T(8,128)(2,1)S(1)}, u32[]{:S(2)}, u32[]{:S(2)}) collective-permute-start(bf16[2,512,128]{2,1,0:T(8,128)(2,1)S(1)} %broadcast_select_fusion.1), channel_id=1, source_target_pairs={{0,4},{8,12},{1,5},{9,13},{16,20},{24,28},{17,21},{25,29}} | collective-permute-start | bytes 786440 | tf_op jit(solution)/shard_map/ppermute | solution.py:216
  14.5 4.9 %collective-permute-done.1.refs_3_ = bf16[2,512,128]{2,1,0:T(8,128)(2,1)S(1)} collective-permute-done((bf16[2,512,128]{2,1,0:T(8,128)(2,1)S(1)}, bf16[2,512,128]{2,1,0:T(8,128)(2,1)S(1)}, u32[]{:S(2)}, u32[]{:S(2)}) %collective-permute-start.1) | collective-permute-done | bytes 262176 | tf_op jit(solution)/shard_map/ppermute | solution.py:216
  19.5 1.3 %collective-permute-start.2 = (bf16[2,512,128]{2,1,0:T(8,128)(2,1)S(1)}, bf16[2,512,128]{2,1,0:T(8,128)(2,1)S(1)}, u32[]{:S(2)}, u32[]{:S(2)}) collective-permute-start(bf16[2,512,128]{2,1,0:T(8,128)(2,1)S(1)} %broadcast_select_fusion), channel_id=1, source_target_pairs={{0,2},{4,6},{8,10},{12,14},{1,3},{5,7},{9,11},{13,15},{16,18},{20,... | collective-permute-start | bytes 786440 | tf_op jit(solution)/shard_map/ppermute | solution.py:216
  20.9 7.2 %collective-permute-start.8 = (bf16[2,128,128]{2,1,0:T(8,128)(2,1)S(1)}, bf16[2,128,128]{2,1,0:T(8,128)(2,1)S(1)}, u32[]{:S(2)}, u32[]{:S(2)}) collective-permute-start(bf16[2,128,128]{2,1,0:T(8,128)(2,1)S(1)} %fusion.2), channel_id=1, source_target_pairs={{0,12},{2,14},{1,13},{3,15},{16,28},{18,30},{17,29},{19,31}} | collective-permute-start | bytes 196616 | tf_op jit(solution)/shard_map/ppermute | solution.py:24
  28.1 1.3 %collective-permute-start.7 = (bf16[2,128,128]{2,1,0:T(8,128)(2,1)S(1)}, bf16[2,128,128]{2,1,0:T(8,128)(2,1)S(1)}, u32[]{:S(2)}, u32[]{:S(2)}) collective-permute-start(bf16[2,128,128]{2,1,0:T(8,128)(2,1)S(1)} %fusion.2), channel_id=1, source_target_pairs={{0,10},{2,12},{4,14},{1,11},{3,13},{5,15},{16,26},{18,28},{20,30},... | collective-permute-start | bytes 196616 | tf_op jit(solution)/shard_map/ppermute | solution.py:24
  29.4 1.3 %collective-permute-start.6 = (bf16[2,128,128]{2,1,0:T(8,128)(2,1)S(1)}, bf16[2,128,128]{2,1,0:T(8,128)(2,1)S(1)}, u32[]{:S(2)}, u32[]{:S(2)}) collective-permute-start(bf16[2,128,128]{2,1,0:T(8,128)(2,1)S(1)} %fusion.2), channel_id=1, source_target_pairs={{0,8},{2,10},{4,12},{6,14},{1,9},{3,11},{5,13},{7,15},{16,24},{18,... | collective-permute-start | bytes 196616 | tf_op jit(solution)/shard_map/ppermute | solution.py:24
  30.7 1.3 %collective-permute-start.5 = (bf16[2,128,128]{2,1,0:T(8,128)(2,1)S(1)}, bf16[2,128,128]{2,1,0:T(8,128)(2,1)S(1)}, u32[]{:S(2)}, u32[]{:S(2)}) collective-permute-start(bf16[2,128,128]{2,1,0:T(8,128)(2,1)S(1)} %fusion.2), channel_id=1, source_target_pairs={{0,6},{2,8},{4,10},{6,12},{8,14},{1,7},{3,9},{5,11},{7,13},{9,15},... | collective-permute-start | bytes 196616 | tf_op jit(solution)/shard_map/ppermute | solution.py:24
  32.0 0.0 collective-permute-done.8.refs_10_
  32.0 2.5 %collective-permute-start.4 = (bf16[2,128,128]{2,1,0:T(8,128)(2,1)S(1)}, bf16[2,128,128]{2,1,0:T(8,128)(2,1)S(1)}, u32[]{:S(2)}, u32[]{:S(2)}) collective-permute-start(bf16[2,128,128]{2,1,0:T(8,128)(2,1)S(1)} %fusion.2), channel_id=1, source_target_pairs={{0,4},{2,6},{4,8},{6,10},{8,12},{10,14},{1,5},{3,7},{5,9},{7,11},{... | collective-permute-start | bytes 196616 | tf_op jit(solution)/shard_map/ppermute | solution.py:24
  34.5 3.4 %collective-permute-start.3 = (bf16[2,128,128]{2,1,0:T(8,128)(2,1)S(1)}, bf16[2,128,128]{2,1,0:T(8,128)(2,1)S(1)}, u32[]{:S(2)}, u32[]{:S(2)}) collective-permute-start(bf16[2,128,128]{2,1,0:T(8,128)(2,1)S(1)} %fusion.2), channel_id=1, source_target_pairs={{0,2},{2,4},{4,6},{6,8},{8,10},{10,12},{12,14},{1,3},{3,5},{5,7},{... | collective-permute-start | bytes 196616 | tf_op jit(solution)/shard_map/ppermute | solution.py:24
  37.9 0.0 collective-permute-done.5.refs_7_
  37.9 0.0 collective-permute-done.4.refs_6_
  37.9 1.9 %collective-permute-done.3.refs_5_ = bf16[2,128,128]{2,1,0:T(8,128)(2,1)S(1)} collective-permute-done((bf16[2,128,128]{2,1,0:T(8,128)(2,1)S(1)}, bf16[2,128,128]{2,1,0:T(8,128)(2,1)S(1)}, u32[]{:S(2)}, u32[]{:S(2)}) %collective-permute-start.3) | collective-permute-done | bytes 65568 | tf_op jit(solution)/shard_map/ppermute | solution.py:24
  39.7 0.0 collective-permute-done.2.refs_4_
  39.8 0.6 copy-done.4
  40.4 0.0 copy-done.5
  40.4 10.3 %tree_attention_backward.1 = (bf16[128,32,128]{2,1,0:T(8,128)(2,1)}, bf16[2,512,128]{2,1,0:T(8,128)(2,1)S(1)}, bf16[6,2,128,128]{3,2,1,0:T(8,128)(2,1)S(1)}, f32[512,128]{1,0:T(8,128)S(1)}, f32[512,128]{1,0:T(8,128)S(1)}) custom-call(s32[64]{0:T(128)S(1)} %copy-done.4, s32[64]{0:T(128)S(1)} %copy-done.5, ...), custom_call_target="tpu_custom_call" | custom-call | flops 2348810240 | bytes 4194304 | tf_op jit(solution)/shard_map/tree_attention_backward/pallas_call | solution.py:165
  50.7 1.3 %collective-permute-start.9 = (bf16[2,512,128]{2,1,0:T(8,128)(2,1)S(1)}, bf16[2,512,128]{2,1,0:T(8,128)(2,1)S(1)}, u32[]{:S(2)}, u32[]{:S(2)}) collective-permute-start(bf16[2,512,128]{2,1,0:T(8,128)(2,1)S(1)} %get-tuple-element.34), channel_id=1, source_target_pairs={{2,0},{6,4},{10,8},{14,12},{3,1},{7,5},{11,9},{15,13},{18,16},{22,... | collective-permute-start | bytes 786440 | tf_op jit(solution)/shard_map/ppermute | solution.py:230
  52.0 7.0 %collective-permute-done.9 = bf16[2,512,128]{2,1,0:T(8,128)(2,1)S(1)} collective-permute-done((bf16[2,512,128]{2,1,0:T(8,128)(2,1)S(1)}, bf16[2,512,128]{2,1,0:T(8,128)(2,1)S(1)}, u32[]{:S(2)}, u32[]{:S(2)}) %collective-permute-start.9) | collective-permute-done | bytes 262176 | tf_op jit(solution)/shard_map/ppermute | solution.py:230
  59.0 0.1 add_convert_fusion.1
  59.0 1.3 %collective-permute-start.10 = (bf16[2,512,128]{2,1,0:T(8,128)(2,1)S(1)}, bf16[2,512,128]{2,1,0:T(8,128)(2,1)S(1)}, u32[]{:S(2)}, u32[]{:S(2)}) collective-permute-start(bf16[2,512,128]{2,1,0:T(8,128)(2,1)S(1)} %add_convert_fusion.1), channel_id=1, source_target_pairs={{4,0},{12,8},{5,1},{13,9},{20,16},{28,24},{21,17},{29,25}} | collective-permute-start | bytes 786440 | tf_op jit(solution)/shard_map/ppermute | solution.py:230
  60.4 1.3 %collective-permute-start.12 = (bf16[2,128,128]{2,1,0:T(8,128)(2,1)S(1)}, bf16[2,128,128]{2,1,0:T(8,128)(2,1)S(1)}, u32[]{:S(2)}, u32[]{:S(2)}) collective-permute-start(bf16[2,128,128]{2,1,0:T(8,128)(2,1)S(1)} %get-tuple-element.39), channel_id=1, source_target_pairs={{2,0},{4,2},{6,4},{8,6},{10,8},{12,10},{14,12},{3,1},{5,3},{7,5},{... | collective-permute-start | bytes 196616 | tf_op jit(solution)/shard_map/ppermute | solution.py:24
  61.7 1.3 %collective-permute-start.17 = (bf16[2,128,128]{2,1,0:T(8,128)(2,1)S(1)}, bf16[2,128,128]{2,1,0:T(8,128)(2,1)S(1)}, u32[]{:S(2)}, u32[]{:S(2)}) collective-permute-start(bf16[2,128,128]{2,1,0:T(8,128)(2,1)S(1)} %get-tuple-element.40), channel_id=1, source_target_pairs={{12,0},{14,2},{13,1},{15,3},{28,16},{30,18},{29,17},{31,19}} | collective-permute-start | bytes 196616 | tf_op jit(solution)/shard_map/ppermute | solution.py:24
  63.0 1.3 %collective-permute-start.16 = (bf16[2,128,128]{2,1,0:T(8,128)(2,1)S(1)}, bf16[2,128,128]{2,1,0:T(8,128)(2,1)S(1)}, u32[]{:S(2)}, u32[]{:S(2)}) collective-permute-start(bf16[2,128,128]{2,1,0:T(8,128)(2,1)S(1)} %get-tuple-element.41), channel_id=1, source_target_pairs={{10,0},{12,2},{14,4},{11,1},{13,3},{15,5},{26,16},{28,18},{30,20},... | collective-permute-start | bytes 196616 | tf_op jit(solution)/shard_map/ppermute | solution.py:24
  64.3 1.3 %collective-permute-start.15 = (bf16[2,128,128]{2,1,0:T(8,128)(2,1)S(1)}, bf16[2,128,128]{2,1,0:T(8,128)(2,1)S(1)}, u32[]{:S(2)}, u32[]{:S(2)}) collective-permute-start(bf16[2,128,128]{2,1,0:T(8,128)(2,1)S(1)} %get-tuple-element.42), channel_id=1, source_target_pairs={{8,0},{10,2},{12,4},{14,6},{9,1},{11,3},{13,5},{15,7},{24,16},{26,... | collective-permute-start | bytes 196616 | tf_op jit(solution)/shard_map/ppermute | solution.py:24
  65.6 1.4 %collective-permute-done.12 = bf16[2,128,128]{2,1,0:T(8,128)(2,1)S(1)} collective-permute-done((bf16[2,128,128]{2,1,0:T(8,128)(2,1)S(1)}, bf16[2,128,128]{2,1,0:T(8,128)(2,1)S(1)}, u32[]{:S(2)}, u32[]{:S(2)}) %collective-permute-start.12) | collective-permute-done | bytes 65568 | tf_op jit(solution)/shard_map/ppermute | solution.py:24
  67.0 1.3 %collective-permute-start.14 = (bf16[2,128,128]{2,1,0:T(8,128)(2,1)S(1)}, bf16[2,128,128]{2,1,0:T(8,128)(2,1)S(1)}, u32[]{:S(2)}, u32[]{:S(2)}) collective-permute-start(bf16[2,128,128]{2,1,0:T(8,128)(2,1)S(1)} %get-tuple-element.43), channel_id=1, source_target_pairs={{6,0},{8,2},{10,4},{12,6},{14,8},{7,1},{9,3},{11,5},{13,7},{15,9},... | collective-permute-start | bytes 196616 | tf_op jit(solution)/shard_map/ppermute | solution.py:24
  68.3 2.3 %collective-permute-done.10 = bf16[2,512,128]{2,1,0:T(8,128)(2,1)S(1)} collective-permute-done((bf16[2,512,128]{2,1,0:T(8,128)(2,1)S(1)}, bf16[2,512,128]{2,1,0:T(8,128)(2,1)S(1)}, u32[]{:S(2)}, u32[]{:S(2)}) %collective-permute-start.10) | collective-permute-done | bytes 262176 | tf_op jit(solution)/shard_map/ppermute | solution.py:230
  70.6 1.3 %collective-permute-start.13 = (bf16[2,128,128]{2,1,0:T(8,128)(2,1)S(1)}, bf16[2,128,128]{2,1,0:T(8,128)(2,1)S(1)}, u32[]{:S(2)}, u32[]{:S(2)}) collective-permute-start(bf16[2,128,128]{2,1,0:T(8,128)(2,1)S(1)} %get-tuple-element.44), channel_id=1, source_target_pairs={{4,0},{6,2},{8,4},{10,6},{12,8},{14,10},{5,1},{7,3},{9,5},{11,7},{... | collective-permute-start | bytes 196616 | tf_op jit(solution)/shard_map/ppermute | solution.py:24
  71.9 0.1 add_convert_fusion
  72.0 2.6 %collective-permute-done.17 = bf16[2,128,128]{2,1,0:T(8,128)(2,1)S(1)} collective-permute-done((bf16[2,128,128]{2,1,0:T(8,128)(2,1)S(1)}, bf16[2,128,128]{2,1,0:T(8,128)(2,1)S(1)}, u32[]{:S(2)}, u32[]{:S(2)}) %collective-permute-start.17) | collective-permute-done | bytes 65568 | tf_op jit(solution)/shard_map/ppermute | solution.py:24
  74.6 1.3 %collective-permute-start.11 = (bf16[2,512,128]{2,1,0:T(8,128)(2,1)S(1)}, bf16[2,512,128]{2,1,0:T(8,128)(2,1)S(1)}, u32[]{:S(2)}, u32[]{:S(2)}) collective-permute-start(bf16[2,512,128]{2,1,0:T(8,128)(2,1)S(1)} %add_convert_fusion), channel_id=1, source_target_pairs={{8,0},{9,1},{24,16},{25,17}} | collective-permute-start | bytes 786440 | tf_op jit(solution)/shard_map/ppermute | solution.py:230
  75.9 0.0 collective-permute-done.16
  75.9 0.4 collective-permute-done.14
  76.3 1.7 %collective-permute-done.13 = bf16[2,128,128]{2,1,0:T(8,128)(2,1)S(1)} collective-permute-done((bf16[2,128,128]{2,1,0:T(8,128)(2,1)S(1)}, bf16[2,128,128]{2,1,0:T(8,128)(2,1)S(1)}, u32[]{:S(2)}, u32[]{:S(2)}) %collective-permute-start.13) | collective-permute-done | bytes 65568 | tf_op jit(solution)/shard_map/ppermute | solution.py:24
  78.0 0.1 convert_add_fusion
  78.1 7.2 %collective-permute-done.11 = bf16[2,512,128]{2,1,0:T(8,128)(2,1)S(1)} collective-permute-done((bf16[2,512,128]{2,1,0:T(8,128)(2,1)S(1)}, bf16[2,512,128]{2,1,0:T(8,128)(2,1)S(1)}, u32[]{:S(2)}, u32[]{:S(2)}) %collective-permute-start.11) | collective-permute-done | bytes 262176 | tf_op jit(solution)/shard_map/ppermute | solution.py:230
  85.2 0.1 add_select_fusion
  85.3 0.1 fusion
  85.4 0.0 copy-start.6
  85.4 0.0 copy-start.7
  85.4 0.7 copy-done.6
  86.1 0.1 copy-done.7
  (16 shorter events, 0.2 us)
Async XLA Ops:
  0.6 12.6 %copy-start = (bf16[128,4,128]{2,1,0:T(4,128)(2,1)S(1)}, bf16[128,4,128]{2,1,0:T(4,128)(2,1)}, u32[]{:S(2)}) copy-start(bf16[128,4,128]{2,1,0:T(4,128)(2,1)} %param.12) | copy-start | bytes 393220
  0.6 12.5 %copy-start.1 = (bf16[128,4,128]{2,1,0:T(4,128)(2,1)S(1)}, bf16[128,4,128]{2,1,0:T(4,128)(2,1)}, u32[]{:S(2)}) copy-start(bf16[128,4,128]{2,1,0:T(4,128)(2,1)} %param.11) | copy-start | bytes 393220
  1.7 11.5 %collective-permute-start = (bf16[2,512,128]{2,1,0:T(8,128)(2,1)S(1)}, bf16[2,512,128]{2,1,0:T(8,128)(2,1)S(1)}, u32[]{:S(2)}, u32[]{:S(2)}) collective-permute-start(bf16[2,512,128]{2,1,0:T(8,128)(2,1)S(1)} %pad_maximum_fusion), channel_id=1, source_target_pairs={{0,8},{1,9},{16,24},{17,25}} | collective-permute-start | bytes 786440 | tf_op jit(solution)/shard_map/ppermute | solution.py:216
  7.7 32.1 %copy-start.2 = (bf16[128,32,128]{2,1,0:T(8,128)(2,1)S(1)}, bf16[128,32,128]{2,1,0:T(8,128)(2,1)}, u32[]{:S(2)}) copy-start(bf16[128,32,128]{2,1,0:T(8,128)(2,1)} %refs_13_.1) | copy-start | bytes 3145732
  7.7 32.1 %copy-start.3 = (bf16[128,32,128]{2,1,0:T(8,128)(2,1)S(1)}, bf16[128,32,128]{2,1,0:T(8,128)(2,1)}, u32[]{:S(2)}) copy-start(bf16[128,32,128]{2,1,0:T(8,128)(2,1)} %refs_14_.1) | copy-start | bytes 3145732
  13.2 6.3 %collective-permute-start.1 = (bf16[2,512,128]{2,1,0:T(8,128)(2,1)S(1)}, bf16[2,512,128]{2,1,0:T(8,128)(2,1)S(1)}, u32[]{:S(2)}, u32[]{:S(2)}) collective-permute-start(bf16[2,512,128]{2,1,0:T(8,128)(2,1)S(1)} %broadcast_select_fusion.1), channel_id=1, source_target_pairs={{0,4},{8,12},{1,5},{9,13},{16,20},{24,28},{17,21},{25,29}} | collective-permute-start | bytes 786440 | tf_op jit(solution)/shard_map/ppermute | solution.py:216
  19.5 20.2 %collective-permute-start.2 = (bf16[2,512,128]{2,1,0:T(8,128)(2,1)S(1)}, bf16[2,512,128]{2,1,0:T(8,128)(2,1)S(1)}, u32[]{:S(2)}, u32[]{:S(2)}) collective-permute-start(bf16[2,512,128]{2,1,0:T(8,128)(2,1)S(1)} %broadcast_select_fusion), channel_id=1, source_target_pairs={{0,2},{4,6},{8,10},{12,14},{1,3},{5,7},{9,11},{13,15},{16,18},{20,... | collective-permute-start | bytes 786440 | tf_op jit(solution)/shard_map/ppermute | solution.py:216
  20.9 11.1 %collective-permute-start.8 = (bf16[2,128,128]{2,1,0:T(8,128)(2,1)S(1)}, bf16[2,128,128]{2,1,0:T(8,128)(2,1)S(1)}, u32[]{:S(2)}, u32[]{:S(2)}) collective-permute-start(bf16[2,128,128]{2,1,0:T(8,128)(2,1)S(1)} %fusion.2), channel_id=1, source_target_pairs={{0,12},{2,14},{1,13},{3,15},{16,28},{18,30},{17,29},{19,31}} | collective-permute-start | bytes 196616 | tf_op jit(solution)/shard_map/ppermute | solution.py:24
  28.1 6.4 %collective-permute-start.7 = (bf16[2,128,128]{2,1,0:T(8,128)(2,1)S(1)}, bf16[2,128,128]{2,1,0:T(8,128)(2,1)S(1)}, u32[]{:S(2)}, u32[]{:S(2)}) collective-permute-start(bf16[2,128,128]{2,1,0:T(8,128)(2,1)S(1)} %fusion.2), channel_id=1, source_target_pairs={{0,10},{2,12},{4,14},{1,11},{3,13},{5,15},{16,26},{18,28},{20,30},... | collective-permute-start | bytes 196616 | tf_op jit(solution)/shard_map/ppermute | solution.py:24
  29.4 8.5 %collective-permute-start.6 = (bf16[2,128,128]{2,1,0:T(8,128)(2,1)S(1)}, bf16[2,128,128]{2,1,0:T(8,128)(2,1)S(1)}, u32[]{:S(2)}, u32[]{:S(2)}) collective-permute-start(bf16[2,128,128]{2,1,0:T(8,128)(2,1)S(1)} %fusion.2), channel_id=1, source_target_pairs={{0,8},{2,10},{4,12},{6,14},{1,9},{3,11},{5,13},{7,15},{16,24},{18,... | collective-permute-start | bytes 196616 | tf_op jit(solution)/shard_map/ppermute | solution.py:24
  30.7 7.2 %collective-permute-start.5 = (bf16[2,128,128]{2,1,0:T(8,128)(2,1)S(1)}, bf16[2,128,128]{2,1,0:T(8,128)(2,1)S(1)}, u32[]{:S(2)}, u32[]{:S(2)}) collective-permute-start(bf16[2,128,128]{2,1,0:T(8,128)(2,1)S(1)} %fusion.2), channel_id=1, source_target_pairs={{0,6},{2,8},{4,10},{6,12},{8,14},{1,7},{3,9},{5,11},{7,13},{9,15},... | collective-permute-start | bytes 196616 | tf_op jit(solution)/shard_map/ppermute | solution.py:24
  32.0 5.9 %collective-permute-start.4 = (bf16[2,128,128]{2,1,0:T(8,128)(2,1)S(1)}, bf16[2,128,128]{2,1,0:T(8,128)(2,1)S(1)}, u32[]{:S(2)}, u32[]{:S(2)}) collective-permute-start(bf16[2,128,128]{2,1,0:T(8,128)(2,1)S(1)} %fusion.2), channel_id=1, source_target_pairs={{0,4},{2,6},{4,8},{6,10},{8,12},{10,14},{1,5},{3,7},{5,9},{7,11},{... | collective-permute-start | bytes 196616 | tf_op jit(solution)/shard_map/ppermute | solution.py:24
  34.5 5.3 %collective-permute-start.3 = (bf16[2,128,128]{2,1,0:T(8,128)(2,1)S(1)}, bf16[2,128,128]{2,1,0:T(8,128)(2,1)S(1)}, u32[]{:S(2)}, u32[]{:S(2)}) collective-permute-start(bf16[2,128,128]{2,1,0:T(8,128)(2,1)S(1)} %fusion.2), channel_id=1, source_target_pairs={{0,2},{2,4},{4,6},{6,8},{8,10},{10,12},{12,14},{1,3},{3,5},{5,7},{... | collective-permute-start | bytes 196616 | tf_op jit(solution)/shard_map/ppermute | solution.py:24
  39.7 0.7 copy-start.4
  39.7 0.7 copy-start.5
  50.7 8.3 %collective-permute-start.9 = (bf16[2,512,128]{2,1,0:T(8,128)(2,1)S(1)}, bf16[2,512,128]{2,1,0:T(8,128)(2,1)S(1)}, u32[]{:S(2)}, u32[]{:S(2)}) collective-permute-start(bf16[2,512,128]{2,1,0:T(8,128)(2,1)S(1)} %get-tuple-element.34), channel_id=1, source_target_pairs={{2,0},{6,4},{10,8},{14,12},{3,1},{7,5},{11,9},{15,13},{18,16},{22,... | collective-permute-start | bytes 786440 | tf_op jit(solution)/shard_map/ppermute | solution.py:230
  59.0 11.6 %collective-permute-start.10 = (bf16[2,512,128]{2,1,0:T(8,128)(2,1)S(1)}, bf16[2,512,128]{2,1,0:T(8,128)(2,1)S(1)}, u32[]{:S(2)}, u32[]{:S(2)}) collective-permute-start(bf16[2,512,128]{2,1,0:T(8,128)(2,1)S(1)} %add_convert_fusion.1), channel_id=1, source_target_pairs={{4,0},{12,8},{5,1},{13,9},{20,16},{28,24},{21,17},{29,25}} | collective-permute-start | bytes 786440 | tf_op jit(solution)/shard_map/ppermute | solution.py:230
  60.4 6.6 %collective-permute-start.12 = (bf16[2,128,128]{2,1,0:T(8,128)(2,1)S(1)}, bf16[2,128,128]{2,1,0:T(8,128)(2,1)S(1)}, u32[]{:S(2)}, u32[]{:S(2)}) collective-permute-start(bf16[2,128,128]{2,1,0:T(8,128)(2,1)S(1)} %get-tuple-element.39), channel_id=1, source_target_pairs={{2,0},{4,2},{6,4},{8,6},{10,8},{12,10},{14,12},{3,1},{5,3},{7,5},{... | collective-permute-start | bytes 196616 | tf_op jit(solution)/shard_map/ppermute | solution.py:24
  61.7 12.9 %collective-permute-start.17 = (bf16[2,128,128]{2,1,0:T(8,128)(2,1)S(1)}, bf16[2,128,128]{2,1,0:T(8,128)(2,1)S(1)}, u32[]{:S(2)}, u32[]{:S(2)}) collective-permute-start(bf16[2,128,128]{2,1,0:T(8,128)(2,1)S(1)} %get-tuple-element.40), channel_id=1, source_target_pairs={{12,0},{14,2},{13,1},{15,3},{28,16},{30,18},{29,17},{31,19}} | collective-permute-start | bytes 196616 | tf_op jit(solution)/shard_map/ppermute | solution.py:24
  63.0 12.9 %collective-permute-start.16 = (bf16[2,128,128]{2,1,0:T(8,128)(2,1)S(1)}, bf16[2,128,128]{2,1,0:T(8,128)(2,1)S(1)}, u32[]{:S(2)}, u32[]{:S(2)}) collective-permute-start(bf16[2,128,128]{2,1,0:T(8,128)(2,1)S(1)} %get-tuple-element.41), channel_id=1, source_target_pairs={{10,0},{12,2},{14,4},{11,1},{13,3},{15,5},{26,16},{28,18},{30,20},... | collective-permute-start | bytes 196616 | tf_op jit(solution)/shard_map/ppermute | solution.py:24
  64.3 11.6 %collective-permute-start.15 = (bf16[2,128,128]{2,1,0:T(8,128)(2,1)S(1)}, bf16[2,128,128]{2,1,0:T(8,128)(2,1)S(1)}, u32[]{:S(2)}, u32[]{:S(2)}) collective-permute-start(bf16[2,128,128]{2,1,0:T(8,128)(2,1)S(1)} %get-tuple-element.42), channel_id=1, source_target_pairs={{8,0},{10,2},{12,4},{14,6},{9,1},{11,3},{13,5},{15,7},{24,16},{26,... | collective-permute-start | bytes 196616 | tf_op jit(solution)/shard_map/ppermute | solution.py:24
  67.0 9.3 %collective-permute-start.14 = (bf16[2,128,128]{2,1,0:T(8,128)(2,1)S(1)}, bf16[2,128,128]{2,1,0:T(8,128)(2,1)S(1)}, u32[]{:S(2)}, u32[]{:S(2)}) collective-permute-start(bf16[2,128,128]{2,1,0:T(8,128)(2,1)S(1)} %get-tuple-element.43), channel_id=1, source_target_pairs={{6,0},{8,2},{10,4},{12,6},{14,8},{7,1},{9,3},{11,5},{13,7},{15,9},... | collective-permute-start | bytes 196616 | tf_op jit(solution)/shard_map/ppermute | solution.py:24
  70.6 7.4 %collective-permute-start.13 = (bf16[2,128,128]{2,1,0:T(8,128)(2,1)S(1)}, bf16[2,128,128]{2,1,0:T(8,128)(2,1)S(1)}, u32[]{:S(2)}, u32[]{:S(2)}) collective-permute-start(bf16[2,128,128]{2,1,0:T(8,128)(2,1)S(1)} %get-tuple-element.44), channel_id=1, source_target_pairs={{4,0},{6,2},{8,4},{10,6},{12,8},{14,10},{5,1},{7,3},{9,5},{11,7},{... | collective-permute-start | bytes 196616 | tf_op jit(solution)/shard_map/ppermute | solution.py:24
  74.6 10.6 %collective-permute-start.11 = (bf16[2,512,128]{2,1,0:T(8,128)(2,1)S(1)}, bf16[2,512,128]{2,1,0:T(8,128)(2,1)S(1)}, u32[]{:S(2)}, u32[]{:S(2)}) collective-permute-start(bf16[2,512,128]{2,1,0:T(8,128)(2,1)S(1)} %add_convert_fusion), channel_id=1, source_target_pairs={{8,0},{9,1},{24,16},{25,17}} | collective-permute-start | bytes 786440 | tf_op jit(solution)/shard_map/ppermute | solution.py:230
  85.4 0.7 copy-start.6
  85.4 0.8 copy-start.7

commit v2 on v1

--- a/solution.py
+++ b/solution.py
@@ -24,13 +24,12 @@
     return lax.ppermute(block, "node", route)
 
 
-def tree_strides(size):
-    strides = []
-    stride = 1
-    while stride < size:
-        strides.append(stride)
-        stride *= 2
-    return strides
+def permuted(block, route):
+    return lax.ppermute(block, "node", route)
+
+
+def after(arrays, *earlier):
+    return lax.optimization_barrier((*arrays, *earlier))[: len(arrays)]
 
 
 def column_limits(device, window, parents, lengths):
@@ -207,34 +206,74 @@
     keys = keys.reshape(rows, head_size)
     values = values.reshape(rows, head_size)
     pair = jnp.stack([keys, values])
-    strides = tree_strides(size)
-
-    prompt = []
-    held = pair
+    half = size // 2
+    strides = []
+    stride = half // 2
+    while stride > 1:
+        strides.append(stride)
+        stride //= 2
+    head = pair[:, :front]
+    behind = {}
+
+    def fetch(count):
+        for k in range(len(behind) + 1, min(len(behind) + count, window) + 1):
+            behind[k] = shifted(head, k, size)
+        return list(behind.values())
+
+    keys_1 = permuted(keys, [(0, half)])
+    values_1 = permuted(values, [(0, 1)])
+    keys_1, values_1 = after((keys_1, values_1), *fetch(2))
+    keys_2 = permuted(jnp.where(device == 0, keys, keys_1), [(0, 1), (half, half + 1)])
+    values_2 = permuted(jnp.where(device == 0, values, values_1), [(0, half), (1, half + 1)])
+    keys_2, values_2 = after((keys_2, values_2), *fetch(2))
+    held = jnp.stack(
+        [
+            jnp.where(device == 0, keys, jnp.where(device == half, keys_1, keys_2)),
+            jnp.where(device == 0, values, jnp.where(device == 1, values_1, values_2)),
+        ]
+    )
+    prompt = [held]
+    for stride in strides:
+        route = [(i + j, i + j + stride) for i in range(0, size, 2 * stride) for j in (0, 1)]
+        arrived = permuted(held, route)
+        prompt.append(arrived)
+        if stride > 2:
+            held = held + arrived
+    fetch(window)
+
+    grad_queries, dprompt, dbehind, dk, dv = attention(
+        prompt, list(behind.values()), keys, values, queries, grad_out, parents, lengths, heads_kv
+    )
+
+    back = {}
+
+    def send_back(count):
+        for k in range(len(back) + 1, min(len(back) + count, window) + 1):
+            back[k] = shifted(dbehind[k - 1], -k, size)
+        return list(back.values())
+
+    def added(total, arrived):
+        return (total.astype(F32) + arrived.astype(F32)).astype(BF16)
+
+    total = dprompt
     for stride in reversed(strides):
-        route = [(i, i + stride) for i in range(0, size, 2 * stride) if i + stride < size]
-        arrived = lax.ppermute(held, "node", route)
-        prompt.append(arrived)
-        if stride > 1:
-            held = jnp.where(lax.rem(device, 2 * stride) == 0, held, arrived)
-    head = pair[:, :front]
-    behind = [shifted(head, k, size) for k in range(1, window + 1)]
-
-    grad_queries, dprompt, dbehind, dk, dv = attention(
-        prompt, behind, keys, values, queries, grad_out, parents, lengths, heads_kv
-    )
-
-    total = dprompt
-    for stride in strides:
-        route = [(i + stride, i) for i in range(0, size, 2 * stride) if i + stride < size]
-        arrived = lax.ppermute(total, "node", route)
-        total = (total.astype(F32) + arrived.astype(F32)).astype(BF16 if stride < strides[-1] else F32)
-    back = sum(shifted(dbehind[k - 1], -k, size).astype(F32) for k in range(1, window + 1))
-    total = jnp.where(device == 0, total, 0.0)
+        route = [(i + j + stride, i + j) for i in range(0, size, 2 * stride) for j in (0, 1)]
+        total = added(total, permuted(total, route))
+    total, = after((total,), *send_back(2))
+    total_k, total_v = total[0], total[1]
+    moved_k = permuted(total_k, [(1, 0), (half + 1, half)])
+    moved_v = permuted(total_v, [(half, 0), (half + 1, 1)])
+    moved_k, moved_v = after((moved_k, moved_v), *send_back(2))
+    total_k = added(total_k, moved_k)
+    total_v = added(total_v, moved_v)
+    last_k = permuted(total_k, [(half, 0)])
+    last_v = permuted(total_v, [(1, 0)])
+    send_back(window)
     own = []
-    for side, local in ((0, dk), (1, dv)):
-        whole = local + total[side]
-        own.append(whole.at[:front].add(back[side]).reshape(tokens, heads_kv, head_size))
+    for side, local, total, last in ((0, dk, total_k, last_k), (1, dv, total_v, last_v)):
+        whole = local + jnp.where(device == 0, total.astype(F32) + last.astype(F32), 0.0)
+        received = sum(block[side].astype(F32) for block in back.values())
+        own.append(whole.at[:front].add(received).reshape(tokens, heads_kv, head_size))
     return grad_queries, own[0], own[1]
 
 

time: 86.7 us -> 84.6 us (0.976)
  waiting for transfers between devices: 34.9 us -> 26.7 us
  starting transfers between devices: 37.1 us -> 44 us
    ppermute x6 -> x10, waiting for transfers between devices: 26.9 us -> 12.1 us  [permuted(): return lax.ppermute(block, 'node', route)]
    ppermute x6 -> x10, starting transfers between devices: 12.4 us -> 24.8 us  [permuted(): return lax.ppermute(block, 'node', route)]
    ppermute x12, waiting for transfers between devices: 8.01 us -> 14.5 us  [shifted(): return lax.ppermute(block, 'node', route)]
    ppermute x12, starting transfers between devices: 24.7 us -> 19.2 us  [shifted(): return lax.ppermute(block, 'node', route)]
  transfers between devices with their start and end apart: 18 -> 22, of which waited for: 10 -> 13; matrix products, arithmetic and copies ran while one was open for 0% -> 1% of each run, Pallas kernels for 0% -> 0%
where the time goes in v2:
time: 84.6 us; the launch traced here: 84 us
  starting transfers between devices  44 us (52%)
  waiting for transfers between devices  26.7 us (32%)
  Pallas kernels  10.3 us (12%)
  other arithmetic  1.24 us (1%)
  between operations  0.98 us (1%)
  local copies, waits for them, and re-layouts  0.86 us (1%)
    ppermute x10, starting transfers between devices, permuted(): return lax.ppermute(block, 'node', route)  24.8 us
    ppermute x12, starting transfers between devices, shifted(): return lax.ppermute(block, 'node', route)  19.2 us
    ppermute x12, waiting for transfers between devices, shifted(): return lax.ppermute(block, 'node', route)  14.5 us
    ppermute x10, waiting for transfers between devices, permuted(): return lax.ppermute(block, 'node', route)  12.1 us
    pallas_call x1, Pallas kernels, attention(): pl.pallas_call(functools.partial(attention_kernel, rounds, window, heads_...  10.3 us
  transfers between devices with their start and end apart: 22, of which 13 were waited for; matrix products, arithmetic and copies ran while one was open for 1% of the time, Pallas kernels for 0%

profile of v2, /device:TPU:0, one launch (start us, length us, event | category | flops | bytes accessed | tf_op | source)
XLA Modules:
  0.0 84.0 jit_solution(15497490827278313032)
XLA Ops:
  0.6 5.9 %collective-permute-start = (bf16[512,128]{1,0:T(8,128)(2,1)}, bf16[512,128]{1,0:T(8,128)(2,1)S(1)}, u32[]{:S(2)}, u32[]{:S(2)}) collective-permute-start(bf16[512,128]{1,0:T(8,128)(2,1)} %bitcast.39), channel_id=1, source_target_pairs={{0,8},{1,9},{16,24},{17,25}} | collective-permute-start | bytes 393224 | tf_op jit(solution)/shard_map/ppermute | solution.py:28
  6.6 1.3 %collective-permute-start.1 = (bf16[512,128]{1,0:T(8,128)(2,1)}, bf16[512,128]{1,0:T(8,128)(2,1)S(1)}, u32[]{:S(2)}, u32[]{:S(2)}) collective-permute-start(bf16[512,128]{1,0:T(8,128)(2,1)} %bitcast.34), channel_id=1, source_target_pairs={{0,2},{1,3},{16,18},{17,19}} | collective-permute-start | bytes 393224 | tf_op jit(solution)/shard_map/ppermute | solution.py:28
  7.9 0.8 pad_maximum_fusion.1
  8.7 1.3 %collective-permute-start.3 = (bf16[2,128,128]{2,1,0:T(8,128)(2,1)S(1)}, bf16[2,128,128]{2,1,0:T(8,128)(2,1)S(1)}, u32[]{:S(2)}, u32[]{:S(2)}) collective-permute-start(bf16[2,128,128]{2,1,0:T(8,128)(2,1)S(1)} %pad_maximum_fusion.1), channel_id=1, source_target_pairs={{0,4},{2,6},{4,8},{6,10},{8,12},{10,14},{1,5},{3,7},{5,9},{7,11},{... | collective-permute-start | bytes 196616 | tf_op jit(solution)/shard_map/ppermute | solution.py:24
  10.0 1.3 %collective-permute-start.2 = (bf16[2,128,128]{2,1,0:T(8,128)(2,1)S(1)}, bf16[2,128,128]{2,1,0:T(8,128)(2,1)S(1)}, u32[]{:S(2)}, u32[]{:S(2)}) collective-permute-start(bf16[2,128,128]{2,1,0:T(8,128)(2,1)S(1)} %pad_maximum_fusion.1), channel_id=1, source_target_pairs={{0,2},{2,4},{4,6},{6,8},{8,10},{10,12},{12,14},{1,3},{3,5},{5,7},{... | collective-permute-start | bytes 196616 | tf_op jit(solution)/shard_map/ppermute | solution.py:24
  11.3 0.0 copy-start
  11.3 0.6 collective-permute-done.3.refs_5_
  11.9 1.3 %collective-permute-done.2.refs_4_ = bf16[2,128,128]{2,1,0:T(8,128)(2,1)S(1)} collective-permute-done((bf16[2,128,128]{2,1,0:T(8,128)(2,1)S(1)}, bf16[2,128,128]{2,1,0:T(8,128)(2,1)S(1)}, u32[]{:S(2)}, u32[]{:S(2)}) %collective-permute-start.2) | collective-permute-done | bytes 65568 | tf_op jit(solution)/shard_map/ppermute | solution.py:24
  13.2 0.0 copy-start.3
  13.3 0.0 copy-start.2
  13.3 6.2 %collective-permute-start.5 = (bf16[512,128]{1,0:T(8,128)(2,1)S(1)}, bf16[512,128]{1,0:T(8,128)(2,1)S(1)}, u32[]{:S(2)}, u32[]{:S(2)}) collective-permute-start(bf16[512,128]{1,0:T(8,128)(2,1)S(1)} %broadcast_select_fusion), channel_id=1, source_target_pairs={{0,8},{2,10},{1,9},{3,11},{16,24},{18,26},{17,25},{19,27}} | collective-permute-start | bytes 393224 | tf_op jit(solution)/shard_map/ppermute | solution.py:28
  19.5 2.5 %collective-permute-start.4 = (bf16[512,128]{1,0:T(8,128)(2,1)S(1)}, bf16[512,128]{1,0:T(8,128)(2,1)S(1)}, u32[]{:S(2)}, u32[]{:S(2)}) collective-permute-start(bf16[512,128]{1,0:T(8,128)(2,1)S(1)} %broadcast_select_fusion.1), channel_id=1, source_target_pairs={{0,2},{8,10},{1,3},{9,11},{16,18},{24,26},{17,19},{25,27}} | collective-permute-start | bytes 393224 | tf_op jit(solution)/shard_map/ppermute | solution.py:28
  22.1 1.3 %collective-permute-start.7 = (bf16[2,128,128]{2,1,0:T(8,128)(2,1)S(1)}, bf16[2,128,128]{2,1,0:T(8,128)(2,1)S(1)}, u32[]{:S(2)}, u32[]{:S(2)}) collective-permute-start(bf16[2,128,128]{2,1,0:T(8,128)(2,1)S(1)} %pad_maximum_fusion.1), channel_id=1, source_target_pairs={{0,8},{2,10},{4,12},{6,14},{1,9},{3,11},{5,13},{7,15},{16,24},{18,... | collective-permute-start | bytes 196616 | tf_op jit(solution)/shard_map/ppermute | solution.py:24
  23.4 1.3 %collective-permute-start.6 = (bf16[2,128,128]{2,1,0:T(8,128)(2,1)S(1)}, bf16[2,128,128]{2,1,0:T(8,128)(2,1)S(1)}, u32[]{:S(2)}, u32[]{:S(2)}) collective-permute-start(bf16[2,128,128]{2,1,0:T(8,128)(2,1)S(1)} %pad_maximum_fusion.1), channel_id=1, source_target_pairs={{0,6},{2,8},{4,10},{6,12},{8,14},{1,7},{3,9},{5,11},{7,13},{9,15},... | collective-permute-start | bytes 196616 | tf_op jit(solution)/shard_map/ppermute | solution.py:24
  24.7 0.6 collective-permute-done.7.refs_7_
  25.2 1.3 %collective-permute-done.6.refs_6_ = bf16[2,128,128]{2,1,0:T(8,128)(2,1)S(1)} collective-permute-done((bf16[2,128,128]{2,1,0:T(8,128)(2,1)S(1)}, bf16[2,128,128]{2,1,0:T(8,128)(2,1)S(1)}, u32[]{:S(2)}, u32[]{:S(2)}) %collective-permute-start.6) | collective-permute-done | bytes 65568 | tf_op jit(solution)/shard_map/ppermute | solution.py:24
  26.6 0.0 copy-start.4
  26.6 0.0 copy-start.5
  26.7 2.3 %collective-permute-start.8 = (bf16[2,512,128]{2,1,0:T(8,128)(2,1)S(1)}, bf16[2,512,128]{2,1,0:T(8,128)(2,1)S(1)}, u32[]{:S(2)}, u32[]{:S(2)}) collective-permute-start(bf16[2,512,128]{2,1,0:T(8,128)(2,1)S(1)} %pad_maximum_fusion.refs_2_), channel_id=1, source_target_pairs={{0,4},{2,6},{8,12},{10,14},{1,5},{3,7},{9,13},{11,15},{16,20},{18,... | collective-permute-start | bytes 786440 | tf_op jit(solution)/shard_map/ppermute | solution.py:28
  29.0 5.0 %collective-permute-start.9 = (bf16[2,128,128]{2,1,0:T(8,128)(2,1)S(1)}, bf16[2,128,128]{2,1,0:T(8,128)(2,1)S(1)}, u32[]{:S(2)}, u32[]{:S(2)}) collective-permute-start(bf16[2,128,128]{2,1,0:T(8,128)(2,1)S(1)} %pad_maximum_fusion.1), channel_id=1, source_target_pairs={{0,10},{2,12},{4,14},{1,11},{3,13},{5,15},{16,26},{18,28},{20,30},... | collective-permute-start | bytes 196616 | tf_op jit(solution)/shard_map/ppermute | solution.py:24
  34.0 1.3 %collective-permute-start.10 = (bf16[2,128,128]{2,1,0:T(8,128)(2,1)S(1)}, bf16[2,128,128]{2,1,0:T(8,128)(2,1)S(1)}, u32[]{:S(2)}, u32[]{:S(2)}) collective-permute-start(bf16[2,128,128]{2,1,0:T(8,128)(2,1)S(1)} %pad_maximum_fusion.1), channel_id=1, source_target_pairs={{0,12},{2,14},{1,13},{3,15},{16,28},{18,30},{17,29},{19,31}} | collective-permute-start | bytes 196616 | tf_op jit(solution)/shard_map/ppermute | solution.py:24
  35.3 0.6 collective-permute-done.9.refs_8_
  35.9 1.3 %collective-permute-done.10.refs_9_ = bf16[2,128,128]{2,1,0:T(8,128)(2,1)S(1)} collective-permute-done((bf16[2,128,128]{2,1,0:T(8,128)(2,1)S(1)}, bf16[2,128,128]{2,1,0:T(8,128)(2,1)S(1)}, u32[]{:S(2)}, u32[]{:S(2)}) %collective-permute-start.10) | collective-permute-done | bytes 65568 | tf_op jit(solution)/shard_map/ppermute | solution.py:24
  37.2 10.3 %tree_attention_backward.1 = (bf16[128,32,128]{2,1,0:T(8,128)(2,1)}, bf16[2,512,128]{2,1,0:T(8,128)(2,1)S(1)}, bf16[6,2,128,128]{3,2,1,0:T(8,128)(2,1)S(1)}, f32[512,128]{1,0:T(8,128)S(1)}, f32[512,128]{1,0:T(8,128)S(1)}) custom-call(s32[64]{0:T(128)S(1)} %copy-done.4, s32[64]{0:T(128)S(1)} %copy-done.5, bf16[2,512,128]{2,1,0:T(8,128)(2,1)S(1)} %pad_maximum_fusion.refs_2_, ...), custom_call_target="tpu_custom_call" | custom-call | flops 2348810240 | bytes 4194304 | tf_op jit(solution)/shard_map/tree_attention_backward/pallas_call | solution.py:164
  47.5 1.3 %collective-permute-start.11 = (bf16[2,512,128]{2,1,0:T(8,128)(2,1)S(1)}, bf16[2,512,128]{2,1,0:T(8,128)(2,1)S(1)}, u32[]{:S(2)}, u32[]{:S(2)}) collective-permute-start(bf16[2,512,128]{2,1,0:T(8,128)(2,1)S(1)} %get-tuple-element.45), channel_id=1, source_target_pairs={{4,0},{6,2},{12,8},{14,10},{5,1},{7,3},{13,9},{15,11},{20,16},{22,... | collective-permute-start | bytes 786440 | tf_op jit(solution)/shard_map/ppermute | solution.py:28
  48.9 1.3 %collective-permute-start.13 = (bf16[2,128,128]{2,1,0:T(8,128)(2,1)S(1)}, bf16[2,128,128]{2,1,0:T(8,128)(2,1)S(1)}, u32[]{:S(2)}, u32[]{:S(2)}) collective-permute-start(bf16[2,128,128]{2,1,0:T(8,128)(2,1)S(1)} %get-tuple-element.57), channel_id=1, source_target_pairs={{4,0},{6,2},{8,4},{10,6},{12,8},{14,10},{5,1},{7,3},{9,5},{11,7},{... | collective-permute-start | bytes 196616 | tf_op jit(solution)/shard_map/ppermute | solution.py:24
  50.2 1.3 %collective-permute-start.12 = (bf16[2,128,128]{2,1,0:T(8,128)(2,1)S(1)}, bf16[2,128,128]{2,1,0:T(8,128)(2,1)S(1)}, u32[]{:S(2)}, u32[]{:S(2)}) collective-permute-start(bf16[2,128,128]{2,1,0:T(8,128)(2,1)S(1)} %get-tuple-element.58), channel_id=1, source_target_pairs={{2,0},{4,2},{6,4},{8,6},{10,8},{12,10},{14,12},{3,1},{5,3},{7,5},{... | collective-permute-start | bytes 196616 | tf_op jit(solution)/shard_map/ppermute | solution.py:24
  51.5 5.7 %collective-permute-done.11 = bf16[2,512,128]{2,1,0:T(8,128)(2,1)S(1)} collective-permute-done((bf16[2,512,128]{2,1,0:T(8,128)(2,1)S(1)}, bf16[2,512,128]{2,1,0:T(8,128)(2,1)S(1)}, u32[]{:S(2)}, u32[]{:S(2)}) %collective-permute-start.11) | collective-permute-done | bytes 262176 | tf_op jit(solution)/shard_map/ppermute | solution.py:28
  57.2 0.1 add_convert_fusion
  57.2 0.6 collective-permute-done.13
  57.9 1.3 %collective-permute-start.15 = (bf16[512,128]{1,0:T(8,128)(2,1)S(1)}, bf16[512,128]{1,0:T(8,128)(2,1)S(1)}, u32[]{:S(2)}, u32[]{:S(2)}) collective-permute-start(bf16[512,128]{1,0:T(8,128)(2,1)S(1)} %get-tuple-element.61), channel_id=1, source_target_pairs={{8,0},{10,2},{9,1},{11,3},{24,16},{26,18},{25,17},{27,19}} | collective-permute-start | bytes 393224 | tf_op jit(solution)/shard_map/ppermute | solution.py:28
  59.2 1.3 %collective-permute-start.14 = (bf16[512,128]{1,0:T(8,128)(2,1)S(1)}, bf16[512,128]{1,0:T(8,128)(2,1)S(1)}, u32[]{:S(2)}, u32[]{:S(2)}) collective-permute-start(bf16[512,128]{1,0:T(8,128)(2,1)S(1)} %get-tuple-element.62), channel_id=1, source_target_pairs={{2,0},{10,8},{3,1},{11,9},{18,16},{26,24},{19,17},{27,25}} | collective-permute-start | bytes 393224 | tf_op jit(solution)/shard_map/ppermute | solution.py:28
  60.5 1.3 %collective-permute-start.17 = (bf16[2,128,128]{2,1,0:T(8,128)(2,1)S(1)}, bf16[2,128,128]{2,1,0:T(8,128)(2,1)S(1)}, u32[]{:S(2)}, u32[]{:S(2)}) collective-permute-start(bf16[2,128,128]{2,1,0:T(8,128)(2,1)S(1)} %get-tuple-element.55), channel_id=1, source_target_pairs={{8,0},{10,2},{12,4},{14,6},{9,1},{11,3},{13,5},{15,7},{24,16},{26,... | collective-permute-start | bytes 196616 | tf_op jit(solution)/shard_map/ppermute | solution.py:24
  61.8 1.3 %collective-permute-start.16 = (bf16[2,128,128]{2,1,0:T(8,128)(2,1)S(1)}, bf16[2,128,128]{2,1,0:T(8,128)(2,1)S(1)}, u32[]{:S(2)}, u32[]{:S(2)}) collective-permute-start(bf16[2,128,128]{2,1,0:T(8,128)(2,1)S(1)} %get-tuple-element.56), channel_id=1, source_target_pairs={{6,0},{8,2},{10,4},{12,6},{14,8},{7,1},{9,3},{11,5},{13,7},{15,9},... | collective-permute-start | bytes 196616 | tf_op jit(solution)/shard_map/ppermute | solution.py:24
  63.1 5.6 %collective-permute-done.17 = bf16[2,128,128]{2,1,0:T(8,128)(2,1)S(1)} collective-permute-done((bf16[2,128,128]{2,1,0:T(8,128)(2,1)S(1)}, bf16[2,128,128]{2,1,0:T(8,128)(2,1)S(1)}, u32[]{:S(2)}, u32[]{:S(2)}) %collective-permute-start.17) | collective-permute-done | bytes 65568 | tf_op jit(solution)/shard_map/ppermute | solution.py:24
  68.7 0.7 collective-permute-done.16
  69.4 0.1 add_convert_fusion.1
  69.4 1.3 %collective-permute-start.21 = (bf16[512,128]{1,0:T(8,128)(2,1)S(1)}, bf16[512,128]{1,0:T(8,128)(2,1)S(1)}, u32[]{:S(2)}, u32[]{:S(2)}) collective-permute-start(bf16[512,128]{1,0:T(8,128)(2,1)S(1)} %get-tuple-element.59), channel_id=1, source_target_pairs={{2,0},{3,1},{18,16},{19,17}} | collective-permute-start | bytes 393224 | tf_op jit(solution)/shard_map/ppermute | solution.py:28
  70.7 1.3 %collective-permute-start.19 = (bf16[2,128,128]{2,1,0:T(8,128)(2,1)S(1)}, bf16[2,128,128]{2,1,0:T(8,128)(2,1)S(1)}, u32[]{:S(2)}, u32[]{:S(2)}) collective-permute-start(bf16[2,128,128]{2,1,0:T(8,128)(2,1)S(1)} %get-tuple-element.53), channel_id=1, source_target_pairs={{10,0},{12,2},{14,4},{11,1},{13,3},{15,5},{26,16},{28,18},{30,20},... | collective-permute-start | bytes 196616 | tf_op jit(solution)/shard_map/ppermute | solution.py:24
  72.0 1.3 %collective-permute-start.20 = (bf16[2,128,128]{2,1,0:T(8,128)(2,1)S(1)}, bf16[2,128,128]{2,1,0:T(8,128)(2,1)S(1)}, u32[]{:S(2)}, u32[]{:S(2)}) collective-permute-start(bf16[2,128,128]{2,1,0:T(8,128)(2,1)S(1)} %get-tuple-element.54), channel_id=1, source_target_pairs={{12,0},{14,2},{13,1},{15,3},{28,16},{30,18},{29,17},{31,19}} | collective-permute-start | bytes 196616 | tf_op jit(solution)/shard_map/ppermute | solution.py:24
  73.3 1.3 %collective-permute-start.18 = (bf16[512,128]{1,0:T(8,128)(2,1)S(1)}, bf16[512,128]{1,0:T(8,128)(2,1)S(1)}, u32[]{:S(2)}, u32[]{:S(2)}) collective-permute-start(bf16[512,128]{1,0:T(8,128)(2,1)S(1)} %get-tuple-element.60), channel_id=1, source_target_pairs={{8,0},{9,1},{24,16},{25,17}} | collective-permute-start | bytes 393224 | tf_op jit(solution)/shard_map/ppermute | solution.py:28
  74.6 2.8 %collective-permute-done.21 = bf16[512,128]{1,0:T(8,128)(2,1)S(1)} collective-permute-done((bf16[512,128]{1,0:T(8,128)(2,1)S(1)}, bf16[512,128]{1,0:T(8,128)(2,1)S(1)}, u32[]{:S(2)}, u32[]{:S(2)}) %collective-permute-start.21) | collective-permute-done | bytes 131104 | tf_op jit(solution)/shard_map/ppermute | solution.py:28
  77.5 3.6 %collective-permute-done.18 = bf16[512,128]{1,0:T(8,128)(2,1)S(1)} collective-permute-done((bf16[512,128]{1,0:T(8,128)(2,1)S(1)}, bf16[512,128]{1,0:T(8,128)(2,1)S(1)}, u32[]{:S(2)}, u32[]{:S(2)}) %collective-permute-start.18) | collective-permute-done | bytes 131104 | tf_op jit(solution)/shard_map/ppermute | solution.py:28
  81.2 2.0 %collective-permute-done.20 = bf16[2,128,128]{2,1,0:T(8,128)(2,1)S(1)} collective-permute-done((bf16[2,128,128]{2,1,0:T(8,128)(2,1)S(1)}, bf16[2,128,128]{2,1,0:T(8,128)(2,1)S(1)}, u32[]{:S(2)}, u32[]{:S(2)}) %collective-permute-start.20) | collective-permute-done | bytes 65568 | tf_op jit(solution)/shard_map/ppermute | solution.py:24
  83.2 0.1 fusion
  83.3 0.0 copy-start.7
  83.3 0.7 copy-done.6
  84.0 0.1 copy-done.7
  (25 shorter events, 0.3 us)
Async XLA Ops:
  0.6 12.6 %collective-permute-start = (bf16[512,128]{1,0:T(8,128)(2,1)}, bf16[512,128]{1,0:T(8,128)(2,1)S(1)}, u32[]{:S(2)}, u32[]{:S(2)}) collective-permute-start(bf16[512,128]{1,0:T(8,128)(2,1)} %bitcast.39), channel_id=1, source_target_pairs={{0,8},{1,9},{16,24},{17,25}} | collective-permute-start | bytes 393224 | tf_op jit(solution)/shard_map/ppermute | solution.py:28
  6.6 6.6 %collective-permute-start.1 = (bf16[512,128]{1,0:T(8,128)(2,1)}, bf16[512,128]{1,0:T(8,128)(2,1)S(1)}, u32[]{:S(2)}, u32[]{:S(2)}) collective-permute-start(bf16[512,128]{1,0:T(8,128)(2,1)} %bitcast.34), channel_id=1, source_target_pairs={{0,2},{1,3},{16,18},{17,19}} | collective-permute-start | bytes 393224 | tf_op jit(solution)/shard_map/ppermute | solution.py:28
  7.9 5.3 %copy-start.1 = (bf16[128,4,128]{2,1,0:T(4,128)(2,1)S(1)}, bf16[128,4,128]{2,1,0:T(4,128)(2,1)}, u32[]{:S(2)}) copy-start(bf16[128,4,128]{2,1,0:T(4,128)(2,1)} %param.11) | copy-start | bytes 393220
  8.7 3.2 %collective-permute-start.3 = (bf16[2,128,128]{2,1,0:T(8,128)(2,1)S(1)}, bf16[2,128,128]{2,1,0:T(8,128)(2,1)S(1)}, u32[]{:S(2)}, u32[]{:S(2)}) collective-permute-start(bf16[2,128,128]{2,1,0:T(8,128)(2,1)S(1)} %pad_maximum_fusion.1), channel_id=1, source_target_pairs={{0,4},{2,6},{4,8},{6,10},{8,12},{10,14},{1,5},{3,7},{5,9},{7,11},{... | collective-permute-start | bytes 196616 | tf_op jit(solution)/shard_map/ppermute | solution.py:24
  10.0 3.2 %collective-permute-start.2 = (bf16[2,128,128]{2,1,0:T(8,128)(2,1)S(1)}, bf16[2,128,128]{2,1,0:T(8,128)(2,1)S(1)}, u32[]{:S(2)}, u32[]{:S(2)}) collective-permute-start(bf16[2,128,128]{2,1,0:T(8,128)(2,1)S(1)} %pad_maximum_fusion.1), channel_id=1, source_target_pairs={{0,2},{2,4},{4,6},{6,8},{8,10},{10,12},{12,14},{1,3},{3,5},{5,7},{... | collective-permute-start | bytes 196616 | tf_op jit(solution)/shard_map/ppermute | solution.py:24
  11.3 1.9 %copy-start = (bf16[128,4,128]{2,1,0:T(4,128)(2,1)S(1)}, bf16[128,4,128]{2,1,0:T(4,128)(2,1)}, u32[]{:S(2)}) copy-start(bf16[128,4,128]{2,1,0:T(4,128)(2,1)} %param.12) | copy-start | bytes 393220
  13.2 24.0 %copy-start.3 = (bf16[128,32,128]{2,1,0:T(8,128)(2,1)S(1)}, bf16[128,32,128]{2,1,0:T(8,128)(2,1)}, u32[]{:S(2)}) copy-start(bf16[128,32,128]{2,1,0:T(8,128)(2,1)} %refs_13_.1) | copy-start | bytes 3145732
  13.3 23.9 %copy-start.2 = (bf16[128,32,128]{2,1,0:T(8,128)(2,1)S(1)}, bf16[128,32,128]{2,1,0:T(8,128)(2,1)}, u32[]{:S(2)}) copy-start(bf16[128,32,128]{2,1,0:T(8,128)(2,1)} %refs_12_.1) | copy-start | bytes 3145732
  13.3 13.2 %collective-permute-start.5 = (bf16[512,128]{1,0:T(8,128)(2,1)S(1)}, bf16[512,128]{1,0:T(8,128)(2,1)S(1)}, u32[]{:S(2)}, u32[]{:S(2)}) collective-permute-start(bf16[512,128]{1,0:T(8,128)(2,1)S(1)} %broadcast_select_fusion), channel_id=1, source_target_pairs={{0,8},{2,10},{1,9},{3,11},{16,24},{18,26},{17,25},{19,27}} | collective-permute-start | bytes 393224 | tf_op jit(solution)/shard_map/ppermute | solution.py:28
  19.5 7.0 %collective-permute-start.4 = (bf16[512,128]{1,0:T(8,128)(2,1)S(1)}, bf16[512,128]{1,0:T(8,128)(2,1)S(1)}, u32[]{:S(2)}, u32[]{:S(2)}) collective-permute-start(bf16[512,128]{1,0:T(8,128)(2,1)S(1)} %broadcast_select_fusion.1), channel_id=1, source_target_pairs={{0,2},{8,10},{1,3},{9,11},{16,18},{24,26},{17,19},{25,27}} | collective-permute-start | bytes 393224 | tf_op jit(solution)/shard_map/ppermute | solution.py:28
  22.1 3.2 %collective-permute-start.7 = (bf16[2,128,128]{2,1,0:T(8,128)(2,1)S(1)}, bf16[2,128,128]{2,1,0:T(8,128)(2,1)S(1)}, u32[]{:S(2)}, u32[]{:S(2)}) collective-permute-start(bf16[2,128,128]{2,1,0:T(8,128)(2,1)S(1)} %pad_maximum_fusion.1), channel_id=1, source_target_pairs={{0,8},{2,10},{4,12},{6,14},{1,9},{3,11},{5,13},{7,15},{16,24},{18,... | collective-permute-start | bytes 196616 | tf_op jit(solution)/shard_map/ppermute | solution.py:24
  23.4 3.2 %collective-permute-start.6 = (bf16[2,128,128]{2,1,0:T(8,128)(2,1)S(1)}, bf16[2,128,128]{2,1,0:T(8,128)(2,1)S(1)}, u32[]{:S(2)}, u32[]{:S(2)}) collective-permute-start(bf16[2,128,128]{2,1,0:T(8,128)(2,1)S(1)} %pad_maximum_fusion.1), channel_id=1, source_target_pairs={{0,6},{2,8},{4,10},{6,12},{8,14},{1,7},{3,9},{5,11},{7,13},{9,15},... | collective-permute-start | bytes 196616 | tf_op jit(solution)/shard_map/ppermute | solution.py:24
  26.6 10.6 %copy-start.4 = (s32[64]{0:T(128)S(1)}, s32[64]{0:T(128)}, u32[]{:S(2)}) copy-start(s32[64]{0:T(128)} %refs_0_.1) | copy-start | bytes 772
  26.6 10.6 %copy-start.5 = (s32[64]{0:T(128)S(1)}, s32[64]{0:T(128)}, u32[]{:S(2)}) copy-start(s32[64]{0:T(128)} %refs_1_.1) | copy-start | bytes 772
  26.7 10.6 %collective-permute-start.8 = (bf16[2,512,128]{2,1,0:T(8,128)(2,1)S(1)}, bf16[2,512,128]{2,1,0:T(8,128)(2,1)S(1)}, u32[]{:S(2)}, u32[]{:S(2)}) collective-permute-start(bf16[2,512,128]{2,1,0:T(8,128)(2,1)S(1)} %pad_maximum_fusion.refs_2_), channel_id=1, source_target_pairs={{0,4},{2,6},{8,12},{10,14},{1,5},{3,7},{9,13},{11,15},{16,20},{18,... | collective-permute-start | bytes 786440 | tf_op jit(solution)/shard_map/ppermute | solution.py:28
  29.0 6.9 %collective-permute-start.9 = (bf16[2,128,128]{2,1,0:T(8,128)(2,1)S(1)}, bf16[2,128,128]{2,1,0:T(8,128)(2,1)S(1)}, u32[]{:S(2)}, u32[]{:S(2)}) collective-permute-start(bf16[2,128,128]{2,1,0:T(8,128)(2,1)S(1)} %pad_maximum_fusion.1), channel_id=1, source_target_pairs={{0,10},{2,12},{4,14},{1,11},{3,13},{5,15},{16,26},{18,28},{20,30},... | collective-permute-start | bytes 196616 | tf_op jit(solution)/shard_map/ppermute | solution.py:24
  34.0 3.2 %collective-permute-start.10 = (bf16[2,128,128]{2,1,0:T(8,128)(2,1)S(1)}, bf16[2,128,128]{2,1,0:T(8,128)(2,1)S(1)}, u32[]{:S(2)}, u32[]{:S(2)}) collective-permute-start(bf16[2,128,128]{2,1,0:T(8,128)(2,1)S(1)} %pad_maximum_fusion.1), channel_id=1, source_target_pairs={{0,12},{2,14},{1,13},{3,15},{16,28},{18,30},{17,29},{19,31}} | collective-permute-start | bytes 196616 | tf_op jit(solution)/shard_map/ppermute | solution.py:24
  47.5 9.6 %collective-permute-start.11 = (bf16[2,512,128]{2,1,0:T(8,128)(2,1)S(1)}, bf16[2,512,128]{2,1,0:T(8,128)(2,1)S(1)}, u32[]{:S(2)}, u32[]{:S(2)}) collective-permute-start(bf16[2,512,128]{2,1,0:T(8,128)(2,1)S(1)} %get-tuple-element.45), channel_id=1, source_target_pairs={{4,0},{6,2},{12,8},{14,10},{5,1},{7,3},{13,9},{15,11},{20,16},{22,... | collective-permute-start | bytes 786440 | tf_op jit(solution)/shard_map/ppermute | solution.py:28
  48.9 9.0 %collective-permute-start.13 = (bf16[2,128,128]{2,1,0:T(8,128)(2,1)S(1)}, bf16[2,128,128]{2,1,0:T(8,128)(2,1)S(1)}, u32[]{:S(2)}, u32[]{:S(2)}) collective-permute-start(bf16[2,128,128]{2,1,0:T(8,128)(2,1)S(1)} %get-tuple-element.57), channel_id=1, source_target_pairs={{4,0},{6,2},{8,4},{10,6},{12,8},{14,10},{5,1},{7,3},{9,5},{11,7},{... | collective-permute-start | bytes 196616 | tf_op jit(solution)/shard_map/ppermute | solution.py:24
  50.2 7.7 %collective-permute-start.12 = (bf16[2,128,128]{2,1,0:T(8,128)(2,1)S(1)}, bf16[2,128,128]{2,1,0:T(8,128)(2,1)S(1)}, u32[]{:S(2)}, u32[]{:S(2)}) collective-permute-start(bf16[2,128,128]{2,1,0:T(8,128)(2,1)S(1)} %get-tuple-element.58), channel_id=1, source_target_pairs={{2,0},{4,2},{6,4},{8,6},{10,8},{12,10},{14,12},{3,1},{5,3},{7,5},{... | collective-permute-start | bytes 196616 | tf_op jit(solution)/shard_map/ppermute | solution.py:24
  57.9 11.5 %collective-permute-start.15 = (bf16[512,128]{1,0:T(8,128)(2,1)S(1)}, bf16[512,128]{1,0:T(8,128)(2,1)S(1)}, u32[]{:S(2)}, u32[]{:S(2)}) collective-permute-start(bf16[512,128]{1,0:T(8,128)(2,1)S(1)} %get-tuple-element.61), channel_id=1, source_target_pairs={{8,0},{10,2},{9,1},{11,3},{24,16},{26,18},{25,17},{27,19}} | collective-permute-start | bytes 393224 | tf_op jit(solution)/shard_map/ppermute | solution.py:28
  59.2 10.2 %collective-permute-start.14 = (bf16[512,128]{1,0:T(8,128)(2,1)S(1)}, bf16[512,128]{1,0:T(8,128)(2,1)S(1)}, u32[]{:S(2)}, u32[]{:S(2)}) collective-permute-start(bf16[512,128]{1,0:T(8,128)(2,1)S(1)} %get-tuple-element.62), channel_id=1, source_target_pairs={{2,0},{10,8},{3,1},{11,9},{18,16},{26,24},{19,17},{27,25}} | collective-permute-start | bytes 393224 | tf_op jit(solution)/shard_map/ppermute | solution.py:28
  60.5 8.2 %collective-permute-start.17 = (bf16[2,128,128]{2,1,0:T(8,128)(2,1)S(1)}, bf16[2,128,128]{2,1,0:T(8,128)(2,1)S(1)}, u32[]{:S(2)}, u32[]{:S(2)}) collective-permute-start(bf16[2,128,128]{2,1,0:T(8,128)(2,1)S(1)} %get-tuple-element.55), channel_id=1, source_target_pairs={{8,0},{10,2},{12,4},{14,6},{9,1},{11,3},{13,5},{15,7},{24,16},{26,... | collective-permute-start | bytes 196616 | tf_op jit(solution)/shard_map/ppermute | solution.py:24
  61.8 7.6 %collective-permute-start.16 = (bf16[2,128,128]{2,1,0:T(8,128)(2,1)S(1)}, bf16[2,128,128]{2,1,0:T(8,128)(2,1)S(1)}, u32[]{:S(2)}, u32[]{:S(2)}) collective-permute-start(bf16[2,128,128]{2,1,0:T(8,128)(2,1)S(1)} %get-tuple-element.56), channel_id=1, source_target_pairs={{6,0},{8,2},{10,4},{12,6},{14,8},{7,1},{9,3},{11,5},{13,7},{15,9},... | collective-permute-start | bytes 196616 | tf_op jit(solution)/shard_map/ppermute | solution.py:24
  69.4 8.0 %collective-permute-start.21 = (bf16[512,128]{1,0:T(8,128)(2,1)S(1)}, bf16[512,128]{1,0:T(8,128)(2,1)S(1)}, u32[]{:S(2)}, u32[]{:S(2)}) collective-permute-start(bf16[512,128]{1,0:T(8,128)(2,1)S(1)} %get-tuple-element.59), channel_id=1, source_target_pairs={{2,0},{3,1},{18,16},{19,17}} | collective-permute-start | bytes 393224 | tf_op jit(solution)/shard_map/ppermute | solution.py:28
  70.7 10.4 %collective-permute-start.19 = (bf16[2,128,128]{2,1,0:T(8,128)(2,1)S(1)}, bf16[2,128,128]{2,1,0:T(8,128)(2,1)S(1)}, u32[]{:S(2)}, u32[]{:S(2)}) collective-permute-start(bf16[2,128,128]{2,1,0:T(8,128)(2,1)S(1)} %get-tuple-element.53), channel_id=1, source_target_pairs={{10,0},{12,2},{14,4},{11,1},{13,3},{15,5},{26,16},{28,18},{30,20},... | collective-permute-start | bytes 196616 | tf_op jit(solution)/shard_map/ppermute | solution.py:24
  72.0 11.1 %collective-permute-start.20 = (bf16[2,128,128]{2,1,0:T(8,128)(2,1)S(1)}, bf16[2,128,128]{2,1,0:T(8,128)(2,1)S(1)}, u32[]{:S(2)}, u32[]{:S(2)}) collective-permute-start(bf16[2,128,128]{2,1,0:T(8,128)(2,1)S(1)} %get-tuple-element.54), channel_id=1, source_target_pairs={{12,0},{14,2},{13,1},{15,3},{28,16},{30,18},{29,17},{31,19}} | collective-permute-start | bytes 196616 | tf_op jit(solution)/shard_map/ppermute | solution.py:24
  73.3 7.8 %collective-permute-start.18 = (bf16[512,128]{1,0:T(8,128)(2,1)S(1)}, bf16[512,128]{1,0:T(8,128)(2,1)S(1)}, u32[]{:S(2)}, u32[]{:S(2)}) collective-permute-start(bf16[512,128]{1,0:T(8,128)(2,1)S(1)} %get-tuple-element.60), channel_id=1, source_target_pairs={{8,0},{9,1},{24,16},{25,17}} | collective-permute-start | bytes 393224 | tf_op jit(solution)/shard_map/ppermute | solution.py:28
  83.3 0.7 copy-start.6
  83.3 0.8 copy-start.7

commit v3 on v1

--- a/solution.py
+++ b/solution.py
@@ -19,18 +19,8 @@
 F32 = jnp.float32
 
 
-def shifted(block, distance, size):
-    route = [(i - distance, i) for i in range(size) if 0 <= i - distance < size]
+def permuted(block, route):
     return lax.ppermute(block, "node", route)
-
-
-def tree_strides(size):
-    strides = []
-    stride = 1
-    while stride < size:
-        strides.append(stride)
-        stride *= 2
-    return strides
 
 
 def column_limits(device, window, parents, lengths):
@@ -54,13 +44,12 @@
     return limits
 
 
-def attention_kernel(rounds, window, heads_kv, scale, *refs):
-    parents, lengths = refs[:2]
-    prompt = refs[2 : 2 + rounds]
-    behind = refs[2 + rounds : 2 + rounds + window]
-    keys, values, q_ref, g_ref = refs[2 + rounds + window : 6 + rounds + window]
-    dq_ref, dprompt_ref, dbehind_ref, dk_ref, dv_ref = refs[6 + rounds + window : 11 + rounds + window]
-    kh, vh, bias, acc_k, acc_v, wide = refs[11 + rounds + window :]
+def attention_kernel(slots, heads_kv, scale, *refs):
+    parents, lengths, prompt_k, prompt_v, keys, values, q_ref, g_ref = refs[:8]
+    blocks = refs[8 : 8 + 1 + max(source for source, _ in slots)]
+    dq_ref, send_ref, keep_ref, dk_ref, dv_ref = refs[8 + len(blocks) : 13 + len(blocks)]
+    kh, vh, bias, acc_k, acc_v, wide = refs[13 + len(blocks) :]
+    window = len(slots)
     tokens = TD * TILE
     front = CAP * TILE
     before = tokens + window * front
@@ -74,13 +63,12 @@
             for h in range(heads_kv):
                 heads_ref[h, start : start + count] = wide[pl.ds(h, count, stride=heads_kv), :].astype(BF16)
 
-        for side, heads_ref, own in ((0, kh, keys), (1, vh, values)):
-            block = prompt[0][side].astype(F32)
-            for r in range(1, rounds):
-                block = block + prompt[r][side].astype(F32)
-            split(block, heads_ref, 0, tokens)
-            for k in range(window):
-                split(behind[k][side].astype(F32), heads_ref, tokens + k * front, front)
+        for side, heads_ref, prompt, own in ((0, kh, prompt_k, keys), (1, vh, prompt_v, values)):
+            split(prompt[...].astype(F32), heads_ref, 0, tokens)
+            for k, (source, start) in enumerate(slots):
+                start += side * front * heads_kv
+                block = blocks[source][start : start + front * heads_kv]
+                split(block.astype(F32), heads_ref, tokens + k * front, front)
             split(own[...].astype(F32), heads_ref, before, tokens)
         place = lax.broadcasted_iota(jnp.int32, (TILE, 128), 0)
         for t, limit in enumerate(column_limits(device, window, parents, lengths)):
@@ -141,21 +129,39 @@
                 wide[pl.ds(h, count, stride=heads_kv), :] = acc[h, start : start + count]
             return wide[: count * heads_kv]
 
+        rows = tokens * heads_kv
+        rows_front = front * heads_kv
+        even = lax.rem(device, 2) == 0
         for side, acc, own in ((0, acc_k, dk_ref), (1, acc_v, dv_ref)):
-            dprompt_ref[side] = join(acc, 0, tokens).astype(BF16)
+            dprompt = join(acc, 0, tokens).astype(BF16)
+            kept = even if side == 0 else jnp.logical_not(even)
+
+            @pl.when(kept)
+            def _():
+                keep_ref[:rows] = dprompt
+
+            @pl.when(jnp.logical_not(kept))
+            def _():
+                send_ref[:rows] = dprompt
+
             for k in range(window):
-                dbehind_ref[k, side] = join(acc, tokens + k * front, front).astype(BF16)
+                block = join(acc, tokens + k * front, front).astype(BF16)
+                start = rows + (k // 2 * 2 + side) * rows_front
+                (send_ref, keep_ref)[k % 2][start : start + rows_front] = block
             own[...] = join(acc, before, tokens)
 
 
-def attention(prompt, behind, keys, values, queries, grad_out, parents, lengths, heads_kv):
+def attention(prompt_k, prompt_v, slots, blocks, keys, values, queries, grad_out, parents, lengths):
     tokens, heads_q, head_size = queries.shape
-    window = len(behind)
-    rounds = len(prompt)
+    window = len(slots)
+    rows = keys.shape[0]
+    heads_kv = rows // tokens
     front = CAP * TILE
     all_rows = 2 * tokens + window * front
     step_heads = 8 * GROUPS_PER_STEP
     smem = pl.BlockSpec(memory_space=pltpu.SMEM)
+    sent = rows + (window + 1) // 2 * 2 * front * heads_kv
+    kept = rows + window // 2 * 2 * front * heads_kv
 
     def whole(shape):
         return pl.BlockSpec(shape, lambda i: (0,) * len(shape))
@@ -163,24 +169,25 @@
     by_heads = pl.BlockSpec((tokens, step_heads, head_size), lambda i: (0, i, 0))
     products = 5 * 2 * tokens * heads_q * head_size * all_rows
     return pl.pallas_call(
-        functools.partial(attention_kernel, rounds, window, heads_kv, head_size**-0.5),
+        functools.partial(attention_kernel, slots, heads_kv, head_size**-0.5),
         grid=(heads_q // step_heads,),
         in_specs=[smem, smem]
-        + [whole(a.shape) for a in (*prompt, *behind, keys, values)]
-        + [by_heads, by_heads],
+        + [whole(a.shape) for a in (prompt_k, prompt_v, keys, values)]
+        + [by_heads, by_heads]
+        + [whole(a.shape) for a in blocks],
         out_specs=[
             by_heads,
-            whole((2, tokens * heads_kv, head_size)),
-            whole((window, 2, front * heads_kv, head_size)),
-            whole((tokens * heads_kv, head_size)),
-            whole((tokens * heads_kv, head_size)),
+            whole((sent, head_size)),
+            whole((kept, head_size)),
+            whole((rows, head_size)),
+            whole((rows, head_size)),
         ],
         out_shape=[
             jax.ShapeDtypeStruct(queries.shape, BF16),
-            jax.ShapeDtypeStruct((2, tokens * heads_kv, head_size), BF16),
-            jax.ShapeDtypeStruct((window, 2, front * heads_kv, head_size), BF16),
-            jax.ShapeDtypeStruct((tokens * heads_kv, head_size), F32),
-            jax.ShapeDtypeStruct((tokens * heads_kv, head_size), F32),
+            jax.ShapeDtypeStruct((sent, head_size), BF16),
+            jax.ShapeDtypeStruct((kept, head_size), BF16),
+            jax.ShapeDtypeStruct((rows, head_size), F32),
+            jax.ShapeDtypeStruct((rows, head_size), F32),
         ],
         scratch_shapes=[
             pltpu.VMEM((heads_kv, all_rows, head_size), BF16),
@@ -188,53 +195,104 @@
             pltpu.VMEM((all_rows, 128), F32),
             pltpu.VMEM((heads_kv, all_rows, head_size), F32),
             pltpu.VMEM((heads_kv, all_rows, head_size), F32),
-            pltpu.VMEM((tokens * heads_kv, head_size), F32),
+            pltpu.VMEM((rows, head_size), F32),
         ],
         compiler_params=pltpu.CompilerParams(vmem_limit_bytes=40 * 1024 * 1024),
         cost_estimate=pl.CostEstimate(
             flops=products, bytes_accessed=4 * 1024 * 1024, transcendentals=tokens * heads_q * all_rows
         ),
         name="tree_attention_backward",
-    )(parents, lengths, *prompt, *behind, keys, values, queries, grad_out)
+    )(parents, lengths, prompt_k, prompt_v, keys, values, queries, grad_out, *blocks)
+
+
+def shift_route(distance, size):
+    return [(i, i + distance) for i in range(size - distance)]
+
+
+def back(route):
+    return [(j, i) for i, j in route]
+
+
+def added(*blocks):
+    total = blocks[0].astype(F32)
+    for block in blocks[1:]:
+        total = total + block.astype(F32)
+    return total
 
 
 def per_device(size, queries, keys, values, grad_out, parents, lengths):
     tokens, heads_kv, head_size = keys.shape
     rows = tokens * heads_kv
-    front = CAP * TILE * heads_kv
-    window = max(1, min(W, size - 2))
+    unit = 2 * CAP * TILE * heads_kv
+    one = CAP * TILE * heads_kv
+    near = size <= W + 1
+    window = min(W, size - 2) if near else W
     device = lax.axis_index("node")
+    even = lax.rem(device, 2) == 0
     keys = keys.reshape(rows, head_size)
     values = values.reshape(rows, head_size)
-    pair = jnp.stack([keys, values])
-    strides = tree_strides(size)
-
-    prompt = []
-    held = pair
+    strides = [2**i for i in range(2, size.bit_length()) if 2**i < size]
+    neighbours = [(i, i ^ 1) for i in range(size)]
+    far_route = shift_route(4, size)[1:]
+    near_route = shift_route(2, size)
+
+    def prompt_route(stride):
+        return [(i + j, i + j + stride) for i in range(0, size, 2 * stride) for j in (0, 1)]
+
+    head = jnp.concatenate([keys[:one], values[:one]])
+    held = jnp.where(device == 0, keys, permuted(values, [(0, 1)]))
+    far = permuted(head, far_route)
     for stride in reversed(strides):
-        route = [(i, i + stride) for i in range(0, size, 2 * stride) if i + stride < size]
-        arrived = lax.ppermute(held, "node", route)
-        prompt.append(arrived)
-        if stride > 1:
-            held = jnp.where(lax.rem(device, 2 * stride) == 0, held, arrived)
-    head = pair[:, :front]
-    behind = [shifted(head, k, size) for k in range(1, window + 1)]
-
-    grad_queries, dprompt, dbehind, dk, dv = attention(
-        prompt, behind, keys, values, queries, grad_out, parents, lengths, heads_kv
+        held = added(held, permuted(held, prompt_route(stride))).astype(BF16)
+    second = permuted(jnp.concatenate([held, head, far]), near_route)
+    held = jnp.where(lax.rem(device, 4) < 2, held, second[:rows])
+    two, four, six = second[rows : rows + unit], far, second[rows + unit :]
+    if near:
+        even_slots = jnp.where(even, jnp.concatenate([head, two, four]), jnp.concatenate([two, four, six]))
+        third = permuted(jnp.concatenate([held, even_slots]), neighbours)
+        other, start = third[:rows], rows
+    else:
+        third = permuted(jnp.concatenate([head, two, four, six]), shift_route(1, size))
+        other, start = permuted(held, neighbours), 0
+    slots = [(0, start), (1, rows), (0, start + unit), (2, 0), (0, start + 2 * unit), (1, rows + unit), (0, start + 3 * unit)]
+    slots = slots[:window]
+
+    grad_queries, send, keep, dk, dv = attention(
+        jnp.where(even, held, other), jnp.where(even, other, held), slots, (third, second, far),
+        keys, values, queries, grad_out, parents, lengths,
     )
 
-    total = dprompt
+    def slot(array, index):
+        return array[rows + index * unit : rows + (index + 1) * unit]
+
+    if near:
+        third = permuted(send, neighbours)
+        total = added(keep[:rows], third[:rows])
+        from_third = [slot(third, i) for i in range(3)]
+        none = jnp.zeros_like(from_third[0])
+        mine = jnp.where(even, from_third[0], none)
+        two = added(slot(keep, 0), jnp.where(even, from_third[1], from_third[0]))
+        four = added(slot(keep, 1), jnp.where(even, from_third[2], from_third[1]))
+        six = added(slot(keep, 2), jnp.where(even, none, from_third[2]))
+    else:
+        third = permuted(send[rows:], back(shift_route(1, size)))
+        total = added(keep[:rows], permuted(send[:rows], neighbours))
+        mine = third[:unit]
+        two = added(slot(keep, 0), third[unit : 2 * unit])
+        four = added(slot(keep, 1), third[2 * unit : 3 * unit])
+        six = added(slot(keep, 2), third[3 * unit :])
+    second = permuted(jnp.concatenate([total.astype(BF16), two.astype(BF16), six.astype(BF16)]), back(near_route))
+    total = added(total.astype(BF16), jnp.where(lax.rem(device, 4) < 2, second[:rows], 0)).astype(BF16)
+    mine = added(mine, slot(second, 0))
+    four = added(four, slot(second, 1)).astype(BF16)
     for stride in strides:
-        route = [(i + stride, i) for i in range(0, size, 2 * stride) if i + stride < size]
-        arrived = lax.ppermute(total, "node", route)
-        total = (total.astype(F32) + arrived.astype(F32)).astype(BF16 if stride < strides[-1] else F32)
-    back = sum(shifted(dbehind[k - 1], -k, size).astype(F32) for k in range(1, window + 1))
-    total = jnp.where(device == 0, total, 0.0)
+        total = added(total, permuted(total, back(prompt_route(stride)))).astype(BF16)
+    mine = added(mine, permuted(four, back(far_route)))
+    last = permuted(total, [(1, 0)])
     own = []
-    for side, local in ((0, dk), (1, dv)):
-        whole = local + total[side]
-        own.append(whole.at[:front].add(back[side]).reshape(tokens, heads_kv, head_size))
+    for side, local, prompt in ((0, dk, total), (1, dv, last)):
+        whole = local + jnp.where(device == 0, prompt.astype(F32), 0.0)
+        own.append(whole.at[:one].add(mine[side * one : (side + 1) * one]).reshape(tokens, heads_kv, head_size))
     return grad_queries, own[0], own[1]
 
 

time: 86.7 us -> 72.5 us (0.84)
  starting transfers between devices: 37.1 us -> 16.9 us
  waiting for transfers between devices: 34.9 us -> 41.1 us
    ppermute x18 -> x10, starting transfers between devices: 37.1 us -> 16.9 us  [permuted(): return lax.ppermute(block, 'node', route)]
    ppermute x18 -> x10, waiting for transfers between devices: 34.9 us -> 41.1 us  [permuted(): return lax.ppermute(block, 'node', route)]
    another operation x2 -> x0, other arithmetic: 1.04 us -> none  [per_device(): pair = jnp.stack([keys, values])]
    select_n x3 -> x4, other arithmetic: 0.14 us -> 1.08 us  [the longest x1 0.99 us: per_device(): held = jnp.where(device == 0, keys, permuted(values, [(0, 1)]))]
  transfers between devices with their start and end apart: 18 -> 10, of which waited for: 10 -> 8; matrix products, arithmetic and copies ran while one was open for 0% -> 0% of each run, Pallas kernels for 0% -> 0%
where the time goes in v3:
time: 72.5 us; the launch traced here: 72.2 us
  waiting for transfers between devices  41.1 us (57%)
  starting transfers between devices  16.9 us (23%)
  Pallas kernels  10.3 us (14%)
  other arithmetic  1.51 us (2%)
  local copies, waits for them, and re-layouts  1.47 us (2%)
  between operations  0.92 us (1%)
    ppermute x10, waiting for transfers between devices, permuted(): return lax.ppermute(block, 'node', route)  41.1 us
    ppermute x10, starting transfers between devices, permuted(): return lax.ppermute(block, 'node', route)  16.9 us
    pallas_call x1, Pallas kernels, attention(): pl.pallas_call(functools.partial(attention_kernel, slots, heads_kv, head_...  10.3 us
  transfers between devices with their start and end apart: 10, of which 8 were waited for; matrix products, arithmetic and copies ran while one was open for 0% of the time, Pallas kernels for 0%

profile of v3, /device:TPU:0, one launch (start us, length us, event | category | flops | bytes accessed | tf_op | source)
XLA Modules:
  0.0 72.2 jit_solution(3380556912868361911)
XLA Ops:
  0.6 4.8 %collective-permute-start = (bf16[512,128]{1,0:T(8,128)(2,1)}, bf16[512,128]{1,0:T(8,128)(2,1)S(1)}, u32[]{:S(2)}, u32[]{:S(2)}) collective-permute-start(bf16[512,128]{1,0:T(8,128)(2,1)} %bitcast.8), channel_id=1, source_target_pairs={{0,2},{1,3},{16,18},{17,19}} | collective-permute-start | bytes 393224 | tf_op jit(solution)/shard_map/ppermute | solution.py:23
  5.5 3.0 %collective-permute-done = bf16[512,128]{1,0:T(8,128)(2,1)S(1)} collective-permute-done((bf16[512,128]{1,0:T(8,128)(2,1)}, bf16[512,128]{1,0:T(8,128)(2,1)S(1)}, u32[]{:S(2)}, u32[]{:S(2)}) %collective-permute-start) | collective-permute-done | bytes 131104 | tf_op jit(solution)/shard_map/ppermute | solution.py:23
  8.5 0.0 copy-start
  8.5 0.0 copy-start.1
  8.5 1.0 %broadcast_select_fusion = bf16[512,128]{1,0:T(8,128)(2,1)S(1)} fusion(bf16[512,128]{1,0:T(8,128)(2,1)} %bitcast.6, bf16[512,128]{1,0:T(8,128)(2,1)S(1)} %collective-permute-done, pred[]{:T(512)S(6)} %eq.9), kind=kLoop, calls=%fused_computation.16 | loop fusion | flops 65536 | bytes 393217 | tf_op jit(solution)/shard_map/jit(_where)/select_n | solution.py:243
  9.5 1.3 %collective-permute-start.1 = (bf16[512,128]{1,0:T(8,128)(2,1)S(1)}, bf16[512,128]{1,0:T(8,128)(2,1)S(1)}, u32[]{:S(2)}, u32[]{:S(2)}) collective-permute-start(bf16[512,128]{1,0:T(8,128)(2,1)S(1)} %broadcast_select_fusion), channel_id=1, source_target_pairs={{0,8},{2,10},{1,9},{3,11},{16,24},{18,26},{17,25},{19,27}} | collective-permute-start | bytes 393224 | tf_op jit(solution)/shard_map/ppermute | solution.py:23
  10.8 0.0 copy-done
  10.9 0.0 copy-done.1
  10.9 0.7 collective-permute-start.2
  11.6 1.7 %collective-permute-done.1 = bf16[512,128]{1,0:T(8,128)(2,1)S(1)} collective-permute-done((bf16[512,128]{1,0:T(8,128)(2,1)S(1)}, bf16[512,128]{1,0:T(8,128)(2,1)S(1)}, u32[]{:S(2)}, u32[]{:S(2)}) %collective-permute-start.1) | collective-permute-done | bytes 131104 | tf_op jit(solution)/shard_map/ppermute | solution.py:23
  13.4 0.0 collective-permute-done.2.refs_10_
  13.4 1.3 %collective-permute-start.3 = (bf16[1024,128]{1,0:T(8,128)(2,1)S(1)}, bf16[1024,128]{1,0:T(8,128)(2,1)S(1)}, u32[]{:S(2)}, u32[]{:S(2)}) collective-permute-start(bf16[1024,128]{1,0:T(8,128)(2,1)S(1)} %pad_maximum_fusion.1), channel_id=1, source_target_pairs={{0,4},{2,6},{4,8},{6,10},{8,12},{10,14},{1,5},{3,7},{5,9},{7,11},{... | collective-permute-start | bytes 786440 | tf_op jit(solution)/shard_map/ppermute | solution.py:23
  14.7 4.4 %collective-permute-done.3.refs_9_ = bf16[1024,128]{1,0:T(8,128)(2,1)S(1)} collective-permute-done((bf16[1024,128]{1,0:T(8,128)(2,1)S(1)}, bf16[1024,128]{1,0:T(8,128)(2,1)S(1)}, u32[]{:S(2)}, u32[]{:S(2)}) %collective-permute-start.3) | collective-permute-done | bytes 262176 | tf_op jit(solution)/shard_map/ppermute | solution.py:23
  19.1 0.0 copy-start.3
  19.1 0.0 copy-start.2
  19.2 2.5 %collective-permute-start.4 = (bf16[1280,128]{1,0:T(8,128)(2,1)S(1)}, bf16[1280,128]{1,0:T(8,128)(2,1)S(1)}, u32[]{:S(2)}, u32[]{:S(2)}) collective-permute-start(bf16[1280,128]{1,0:T(8,128)(2,1)S(1)} %pad_maximum_fusion), channel_id=1, source_target_pairs={{0,2},{2,0},{4,6},{6,4},{8,10},{10,8},{12,14},{14,12},{1,3},{3,1},... | collective-permute-start | bytes 983048 | tf_op jit(solution)/shard_map/ppermute | solution.py:23
  21.8 5.6 %collective-permute-done.4.refs_8_ = bf16[1280,128]{1,0:T(8,128)(2,1)S(1)} collective-permute-done((bf16[1280,128]{1,0:T(8,128)(2,1)S(1)}, bf16[1280,128]{1,0:T(8,128)(2,1)S(1)}, u32[]{:S(2)}, u32[]{:S(2)}) %collective-permute-start.4) | collective-permute-done | bytes 327712 | tf_op jit(solution)/shard_map/ppermute | solution.py:23
  27.3 0.0 copy-start.4
  27.3 0.0 copy-start.5
  27.4 0.0 copy-done.3
  27.4 0.0 copy-done.2
  27.4 0.6 copy-done.4
  28.0 0.0 copy-done.5
  28.0 10.3 %tree_attention_backward.1 = (bf16[128,32,128]{2,1,0:T(8,128)(2,1)}, bf16[1280,128]{1,0:T(8,128)(2,1)S(1)}, bf16[1280,128]{1,0:T(8,128)(2,1)S(1)}, f32[512,128]{1,0:T(8,128)S(1)}, f32[512,128]{1,0:T(8,128)S(1)}) custom-call(s32[64]{0:T(128)S(1)} %copy-done.4, s32[64]{0:T(128)S(1)} %copy-done.5, bf16[512,128]{1,0:T(8,128)(2,1)S(1)} %get-tuple-element.42.refs_2_, ...), custom_call_target="tpu_custom_call" | custom-call | flops 2348810240 | bytes 4194304 | tf_op jit(solution)/shard_map/tree_attention_backward/pallas_call | solution.py:171
  38.3 1.7 %collective-permute-start.5 = (bf16[1280,128]{1,0:T(8,128)(2,1)S(1)}, bf16[1280,128]{1,0:T(8,128)(2,1)S(1)}, u32[]{:S(2)}, u32[]{:S(2)}) collective-permute-start(bf16[1280,128]{1,0:T(8,128)(2,1)S(1)} %get-tuple-element.35), channel_id=1, source_target_pairs={{0,2},{2,0},{4,6},{6,4},{8,10},{10,8},{12,14},{14,12},{1,3},{3,1},... | collective-permute-start | bytes 983048 | tf_op jit(solution)/shard_map/ppermute | solution.py:23
  40.0 5.3 %collective-permute-done.5 = bf16[1280,128]{1,0:T(8,128)(2,1)S(1)} collective-permute-done((bf16[1280,128]{1,0:T(8,128)(2,1)S(1)}, bf16[1280,128]{1,0:T(8,128)(2,1)S(1)}, u32[]{:S(2)}, u32[]{:S(2)}) %collective-permute-start.5) | collective-permute-done | bytes 327712 | tf_op jit(solution)/shard_map/ppermute | solution.py:23
  45.4 0.1 add_convert_fusion.6
  45.5 1.3 %collective-permute-start.6 = (bf16[1024,128]{1,0:T(8,128)(2,1)S(1)}, bf16[1024,128]{1,0:T(8,128)(2,1)S(1)}, u32[]{:S(2)}, u32[]{:S(2)}) collective-permute-start(bf16[1024,128]{1,0:T(8,128)(2,1)S(1)} %pad_maximum_fusion.2), channel_id=1, source_target_pairs={{4,0},{6,2},{8,4},{10,6},{12,8},{14,10},{5,1},{7,3},{9,5},{11,7},{... | collective-permute-start | bytes 786440 | tf_op jit(solution)/shard_map/ppermute | solution.py:23
  46.8 8.9 %collective-permute-done.6 = bf16[1024,128]{1,0:T(8,128)(2,1)S(1)} collective-permute-done((bf16[1024,128]{1,0:T(8,128)(2,1)S(1)}, bf16[1024,128]{1,0:T(8,128)(2,1)S(1)}, u32[]{:S(2)}, u32[]{:S(2)}) %collective-permute-start.6) | collective-permute-done | bytes 262176 | tf_op jit(solution)/shard_map/ppermute | solution.py:23
  55.7 1.3 %collective-permute-start.7 = (bf16[512,128]{1,0:T(8,128)(2,1)S(1)}, bf16[512,128]{1,0:T(8,128)(2,1)S(1)}, u32[]{:S(2)}, u32[]{:S(2)}) collective-permute-start(bf16[512,128]{1,0:T(8,128)(2,1)S(1)} %add_convert_fusion.1), channel_id=1, source_target_pairs={{8,0},{10,2},{9,1},{11,3},{24,16},{26,18},{25,17},{27,19}} | collective-permute-start | bytes 393224 | tf_op jit(solution)/shard_map/ppermute | solution.py:23
  57.1 0.7 collective-permute-start.8
  57.7 6.7 %collective-permute-done.7 = bf16[512,128]{1,0:T(8,128)(2,1)S(1)} collective-permute-done((bf16[512,128]{1,0:T(8,128)(2,1)S(1)}, bf16[512,128]{1,0:T(8,128)(2,1)S(1)}, u32[]{:S(2)}, u32[]{:S(2)}) %collective-permute-start.7) | collective-permute-done | bytes 131104 | tf_op jit(solution)/shard_map/ppermute | solution.py:23
  64.5 0.1 select_add_fusion.1
  64.5 1.3 %collective-permute-start.9 = (bf16[512,128]{1,0:T(8,128)(2,1)S(1)}, bf16[512,128]{1,0:T(8,128)(2,1)S(1)}, u32[]{:S(2)}, u32[]{:S(2)}) collective-permute-start(bf16[512,128]{1,0:T(8,128)(2,1)S(1)} %get-tuple-element.38), channel_id=1, source_target_pairs={{2,0},{3,1},{18,16},{19,17}} | collective-permute-start | bytes 393224 | tf_op jit(solution)/shard_map/ppermute | solution.py:23
  65.8 0.0 collective-permute-done.8
  65.9 5.5 %collective-permute-done.9 = bf16[512,128]{1,0:T(8,128)(2,1)S(1)} collective-permute-done((bf16[512,128]{1,0:T(8,128)(2,1)S(1)}, bf16[512,128]{1,0:T(8,128)(2,1)S(1)}, u32[]{:S(2)}, u32[]{:S(2)}) %collective-permute-start.9) | collective-permute-done | bytes 131104 | tf_op jit(solution)/shard_map/ppermute | solution.py:23
  71.4 0.0 copy-start.6
  71.5 0.0 copy-start.7
  71.5 0.7 copy-done.6
  72.2 0.1 copy-done.7
  (17 shorter events, 0.4 us)
Async XLA Ops:
  0.6 7.9 %collective-permute-start = (bf16[512,128]{1,0:T(8,128)(2,1)}, bf16[512,128]{1,0:T(8,128)(2,1)S(1)}, u32[]{:S(2)}, u32[]{:S(2)}) collective-permute-start(bf16[512,128]{1,0:T(8,128)(2,1)} %bitcast.8), channel_id=1, source_target_pairs={{0,2},{1,3},{16,18},{17,19}} | collective-permute-start | bytes 393224 | tf_op jit(solution)/shard_map/ppermute | solution.py:23
  8.5 2.3 %copy-start = (bf16[128,4,128]{2,1,0:T(4,128)(2,1)S(1)}, bf16[128,4,128]{2,1,0:T(4,128)(2,1)}, u32[]{:S(2)}) copy-start(bf16[128,4,128]{2,1,0:T(4,128)(2,1)} %param.11) | copy-start | bytes 393220
  8.5 2.3 %copy-start.1 = (bf16[128,4,128]{2,1,0:T(4,128)(2,1)S(1)}, bf16[128,4,128]{2,1,0:T(4,128)(2,1)}, u32[]{:S(2)}) copy-start(bf16[128,4,128]{2,1,0:T(4,128)(2,1)} %param.12) | copy-start | bytes 393220
  9.5 3.8 %collective-permute-start.1 = (bf16[512,128]{1,0:T(8,128)(2,1)S(1)}, bf16[512,128]{1,0:T(8,128)(2,1)S(1)}, u32[]{:S(2)}, u32[]{:S(2)}) collective-permute-start(bf16[512,128]{1,0:T(8,128)(2,1)S(1)} %broadcast_select_fusion), channel_id=1, source_target_pairs={{0,8},{2,10},{1,9},{3,11},{16,24},{18,26},{17,25},{19,27}} | collective-permute-start | bytes 393224 | tf_op jit(solution)/shard_map/ppermute | solution.py:23
  10.9 2.5 %collective-permute-start.2 = (bf16[256,128]{1,0:T(8,128)(2,1)S(1)}, bf16[256,128]{1,0:T(8,128)(2,1)S(1)}, u32[]{:S(2)}, u32[]{:S(2)}) collective-permute-start(bf16[256,128]{1,0:T(8,128)(2,1)S(1)} %pad_maximum_fusion.3), channel_id=1, source_target_pairs={{2,10},{4,12},{6,14},{3,11},{5,13},{7,15},{18,26},{20,28},{22,30},... | collective-permute-start | bytes 196616 | tf_op jit(solution)/shard_map/ppermute | solution.py:23
  13.4 5.7 %collective-permute-start.3 = (bf16[1024,128]{1,0:T(8,128)(2,1)S(1)}, bf16[1024,128]{1,0:T(8,128)(2,1)S(1)}, u32[]{:S(2)}, u32[]{:S(2)}) collective-permute-start(bf16[1024,128]{1,0:T(8,128)(2,1)S(1)} %pad_maximum_fusion.1), channel_id=1, source_target_pairs={{0,4},{2,6},{4,8},{6,10},{8,12},{10,14},{1,5},{3,7},{5,9},{7,11},{... | collective-permute-start | bytes 786440 | tf_op jit(solution)/shard_map/ppermute | solution.py:23
  19.1 8.3 %copy-start.3 = (bf16[128,32,128]{2,1,0:T(8,128)(2,1)S(1)}, bf16[128,32,128]{2,1,0:T(8,128)(2,1)}, u32[]{:S(2)}) copy-start(bf16[128,32,128]{2,1,0:T(8,128)(2,1)} %refs_7_.1) | copy-start | bytes 3145732
  19.1 8.3 %copy-start.2 = (bf16[128,32,128]{2,1,0:T(8,128)(2,1)S(1)}, bf16[128,32,128]{2,1,0:T(8,128)(2,1)}, u32[]{:S(2)}) copy-start(bf16[128,32,128]{2,1,0:T(8,128)(2,1)} %refs_6_.1) | copy-start | bytes 3145732
  19.2 8.1 %collective-permute-start.4 = (bf16[1280,128]{1,0:T(8,128)(2,1)S(1)}, bf16[1280,128]{1,0:T(8,128)(2,1)S(1)}, u32[]{:S(2)}, u32[]{:S(2)}) collective-permute-start(bf16[1280,128]{1,0:T(8,128)(2,1)S(1)} %pad_maximum_fusion), channel_id=1, source_target_pairs={{0,2},{2,0},{4,6},{6,4},{8,10},{10,8},{12,14},{14,12},{1,3},{3,1},... | collective-permute-start | bytes 983048 | tf_op jit(solution)/shard_map/ppermute | solution.py:23
  27.3 0.7 copy-start.4
  27.3 0.7 copy-start.5
  38.3 7.1 %collective-permute-start.5 = (bf16[1280,128]{1,0:T(8,128)(2,1)S(1)}, bf16[1280,128]{1,0:T(8,128)(2,1)S(1)}, u32[]{:S(2)}, u32[]{:S(2)}) collective-permute-start(bf16[1280,128]{1,0:T(8,128)(2,1)S(1)} %get-tuple-element.35), channel_id=1, source_target_pairs={{0,2},{2,0},{4,6},{6,4},{8,10},{10,8},{12,14},{14,12},{1,3},{3,1},... | collective-permute-start | bytes 983048 | tf_op jit(solution)/shard_map/ppermute | solution.py:23
  45.5 10.2 %collective-permute-start.6 = (bf16[1024,128]{1,0:T(8,128)(2,1)S(1)}, bf16[1024,128]{1,0:T(8,128)(2,1)S(1)}, u32[]{:S(2)}, u32[]{:S(2)}) collective-permute-start(bf16[1024,128]{1,0:T(8,128)(2,1)S(1)} %pad_maximum_fusion.2), channel_id=1, source_target_pairs={{4,0},{6,2},{8,4},{10,6},{12,8},{14,10},{5,1},{7,3},{9,5},{11,7},{... | collective-permute-start | bytes 786440 | tf_op jit(solution)/shard_map/ppermute | solution.py:23
  55.7 8.7 %collective-permute-start.7 = (bf16[512,128]{1,0:T(8,128)(2,1)S(1)}, bf16[512,128]{1,0:T(8,128)(2,1)S(1)}, u32[]{:S(2)}, u32[]{:S(2)}) collective-permute-start(bf16[512,128]{1,0:T(8,128)(2,1)S(1)} %add_convert_fusion.1), channel_id=1, source_target_pairs={{8,0},{10,2},{9,1},{11,3},{24,16},{26,18},{25,17},{27,19}} | collective-permute-start | bytes 393224 | tf_op jit(solution)/shard_map/ppermute | solution.py:23
  57.1 8.7 %collective-permute-start.8 = (bf16[256,128]{1,0:T(8,128)(2,1)S(1)}, bf16[256,128]{1,0:T(8,128)(2,1)S(1)}, u32[]{:S(2)}, u32[]{:S(2)}) collective-permute-start(bf16[256,128]{1,0:T(8,128)(2,1)S(1)} %add_convert_fusion.4), channel_id=1, source_target_pairs={{10,2},{12,4},{14,6},{11,3},{13,5},{15,7},{26,18},{28,20},{30,22},... | collective-permute-start | bytes 196616 | tf_op jit(solution)/shard_map/ppermute | solution.py:23
  64.5 6.9 %collective-permute-start.9 = (bf16[512,128]{1,0:T(8,128)(2,1)S(1)}, bf16[512,128]{1,0:T(8,128)(2,1)S(1)}, u32[]{:S(2)}, u32[]{:S(2)}) collective-permute-start(bf16[512,128]{1,0:T(8,128)(2,1)S(1)} %get-tuple-element.38), channel_id=1, source_target_pairs={{2,0},{3,1},{18,16},{19,17}} | collective-permute-start | bytes 393224 | tf_op jit(solution)/shard_map/ppermute | solution.py:23
  71.4 0.7 copy-start.6
  71.5 0.8 %copy-start.7 = (f32[512,128]{1,0:T(8,128)}, f32[512,128]{1,0:T(8,128)S(1)}, u32[]{:S(2)}) copy-start(f32[512,128]{1,0:T(8,128)S(1)} %get-tuple-element.45) | copy-start | bytes 786436

commit v4 on v3

v4 whole, which is shorter than its diff:
```python
import functools
import math

import jax
import jax.numpy as jnp
from jax import lax
from jax.experimental import pallas as pl
from jax.experimental.pallas import tpu as pltpu
from jax.sharding import PartitionSpec as P

TILE = 16
TD = 8
CAP = 2
W = 7
CHUNK = 32
MASKED = -1e30
BF16 = jnp.bfloat16
F32 = jnp.float32


def permuted(block, route):
    return lax.ppermute(block, "node", route)


def column_limits(device, window, parents, lengths):
    cursor = parents[device * TD]
    need = [jnp.int32(0)] * (window + 1)
    for _ in range(W):
        owner = jnp.where(cursor < 0, -1, lax.div(jnp.maximum(cursor, 0), TD))
        distance = device - owner
        active = (owner >= 1) & (distance >= 1) & (distance <= W)
        depth = lax.rem(jnp.maximum(cursor, 0), TD) + 1
        for k in range(1, window + 1):
            need[k] = jnp.where(active & (distance == k), depth, need[k])
        cursor = jnp.where(active, parents[jnp.maximum(owner, 0) * TD], cursor)
    limits = [jnp.where(device >= 1, lengths[t], 0) for t in range(TD)]
    for k in range(1, window + 1):
        owner = device - k
        for c in range(CAP):
            seen = (owner >= 1) & (c < need[k])
            limits.append(jnp.where(seen, lengths[jnp.maximum(owner, 0) * TD + c], 0))
    limits += [lengths[device * TD + t] for t in range(TD)]
    return limits


def split_heads(block, heads_ref, start, count, heads_kv, wide):
    wide[: count * heads_kv] = block.astype(F32)
    for h in range(heads_kv):
        heads_ref[h, start : start + count] = wide[pl.ds(h, count, stride=heads_kv), :].astype(BF16)


def join_heads(blocks, count, heads_kv, wide):
    for h in range(heads_kv):
        wide[pl.ds(h, count, stride=heads_kv), :] = blocks[h]
    return wide[: count * heads_kv]


def prepare_kernel(window, heads_kv, *refs):
    parents, lengths, keys, values, q_ref, g_ref, qh, gh, own_k, own_v, bias, weight, wide = refs
    tokens = TD * TILE
    device = lax.axis_index("node")
    for pair in range(heads_kv // 2):
        for ref, out in ((q_ref, qh), (g_ref, gh)):
            both = ref[:, pair * 16 : (pair + 1) * 16].astype(F32)
            for part in range(2):
                out[2 * pair + part] = both[:, part * 8 : (part + 1) * 8].reshape(tokens * 8, 128).astype(BF16)
    split_heads(keys[...], own_k, 0, tokens, heads_kv, wide)
    split_heads(values[...], own_v, 0, tokens, heads_kv, wide)
    place = lax.broadcasted_iota(jnp.int32, (TILE, 128), 0)
    for t, limit in enumerate(column_limits(device, window, parents, lengths)):
        bias[t * TILE : (t + 1) * TILE] = jnp.where(place < limit, 0.0, MASKED)
    lane_place = lax.broadcasted_iota(jnp.int32, (8, 128), 1) // 8
    for t in range(TD):
        weight[:, t * 128 : (t + 1) * 128] = jnp.where(lane_place < lengths[device * TD + t], 1.0, 0.0)


def probs_kernel(slots, heads_kv, scale, *refs):
    prompt_k, prompt_v, own_k, own_v, qh, gh, bias, weight_ref = refs[:8]
    blocks = refs[8 : 8 + 1 + max(source for source, _ in slots)]
    send_ref, keep_ref, kh, ds_ref, p_own = refs[8 + len(blocks) : 13 + len(blocks)]
    vh, p_ref, grads, wide = refs[13 + len(blocks) :]
    window = len(slots)
    tokens = TD * TILE
    front = CAP * TILE
    before = tokens + window * front
    columns = CHUNK * 8
    device = lax.axis_index("node")

    for side, heads_ref, prompt, own in ((0, kh, prompt_k, own_k), (1, vh, prompt_v, own_v)):
        split_heads(prompt[...], heads_ref, 0, tokens, heads_kv, wide)
        for k, (source, start) in enumerate(slots):
            start += side * front * heads_kv
            block = blocks[source][start : start + front * heads_kv]
            split_heads(block, heads_ref, tokens + k * front, front, heads_kv, wide)
        heads_ref[:, before:] = own[...]

    column_token = lax.broadcasted_iota(jnp.int32, (CHUNK, columns), 1) // 8
    causal = jnp.where(lax.broadcasted_iota(jnp.int32, (CHUNK, columns), 0) <= column_token, 0.0, MASKED)
    for head in range(heads_kv):
        for c in range(tokens // CHUNK):
            rows = before + (c + 1) * CHUNK
            span = slice(c * columns, (c + 1) * columns)
            q = qh[head, span]
            g = gh[head, span]
            s = lax.dot_general(kh[head, :rows], q, (((1,), (1,)), ((), ())), preferred_element_type=F32)
            dp = lax.dot_general(vh[head, :rows], g, (((1,), (1,)), ((), ())), preferred_element_type=F32)
            s = s + jnp.concatenate([bias[:rows]] * (columns // 128), axis=1)
            s = jnp.concatenate([s[: rows - CHUNK], s[rows - CHUNK :] + causal], axis=0)
            top = jnp.max(s, axis=0, keepdims=True)
            e = jnp.exp2((s - top) * (scale * math.log2(math.e)))
            total = jnp.sum(e, axis=0, keepdims=True)
            p = e * (weight_ref[:1, span] / total)
            delta = jnp.sum(p * dp, axis=0, keepdims=True)
            ds_ref[head, :rows, span] = (p * (dp - delta) * scale).astype(BF16)
            p_ref[:, span] = p[:before].astype(BF16)
            p_own[head, : rows - before, span] = p[before:].astype(BF16)
        grads[0, head] = jnp.dot(ds_ref[head, :before], qh[head], preferred_element_type=F32)
        grads[1, head] = jnp.dot(p_ref[...], gh[head], preferred_element_type=F32)

    rows = tokens * heads_kv
    rows_front = front * heads_kv
    even = lax.rem(device, 2) == 0
    for side in range(2):
        dprompt = join_heads([grads[side, h, :tokens] for h in range(heads_kv)], tokens, heads_kv, wide).astype(BF16)
        kept = even if side == 0 else jnp.logical_not(even)

        @pl.when(kept)
        def _():
            keep_ref[:rows] = dprompt

        @pl.when(jnp.logical_not(kept))
        def _():
            send_ref[:rows] = dprompt

        for k in range(window):
            span = slice(tokens + k * front, tokens + (k + 1) * front)
            block = join_heads([grads[side, h, span] for h in range(heads_kv)], front, heads_kv, wide).astype(BF16)
            start = rows + (k // 2 * 2 + side) * rows_front
            (send_ref, keep_ref)[k % 2][start : start + rows_front] = block


def grads_kernel(heads_kv, *refs):
    qh, gh, kh, ds_ref, p_own, dq_ref, dk_ref, dv_ref, wide = refs
    tokens = TD * TILE
    before = kh.shape[1] - tokens
    columns = CHUNK * 8
    dk = []
    dv = []
    for pair in range(heads_kv // 2):
        for c in range(tokens // CHUNK):
            rows = before + (c + 1) * CHUNK
            span = slice(c * columns, (c + 1) * columns)
            parts = []
            for head in (2 * pair, 2 * pair + 1):
                dq = lax.dot_general(
                    kh[head, :rows], ds_ref[head, :rows, span], (((0,), (0,)), ((), ())), preferred_element_type=F32
                )
                parts.append(dq.T.reshape(CHUNK, 8, 128))
            dq_ref[c * CHUNK : (c + 1) * CHUNK, pair * 16 : (pair + 1) * 16] = jnp.concatenate(parts, axis=1).astype(BF16)
        for head in (2 * pair, 2 * pair + 1):
            for source, factor, out in ((ds_ref.at[head, before:], qh, dk), (p_own.at[head], gh, dv)):
                pieces = []
                for c in range(tokens // CHUNK):
                    start = c * columns
                    pieces.append(
                        jnp.dot(
                            source[c * CHUNK : (c + 1) * CHUNK, start:], factor[head, start:], preferred_element_type=F32
                        )
                    )
                out.append(jnp.concatenate(pieces, axis=0))
    dk_ref[...] = join_heads(dk, tokens, heads_kv, wide)
    dv_ref[...] = join_heads(dv, tokens, heads_kv, wide)


VMEM = pl.BlockSpec(memory_space=pltpu.VMEM)
SMEM = pl.BlockSpec(memory_space=pltpu.SMEM)


def call(kernel, name, operands, outputs, scratch, flops, transcendentals=0, scalars=0):
    sizes = [a.size * a.dtype.itemsize for a in (*operands, *outputs)]
    return pl.pallas_call(
        kernel,
        in_specs=[SMEM] * scalars + [VMEM] * (len(operands) - scalars),
        out_specs=[VMEM] * len(outputs),
        out_shape=outputs,
        scratch_shapes=scratch,
        compiler_params=pltpu.CompilerParams(vmem_limit_bytes=28 * 1024 * 1024),
        cost_estimate=pl.CostEstimate(flops=flops, bytes_accessed=sum(sizes), transcendentals=transcendentals),
        name=name,
    )(*operands)


def prepare(window, queries, grad_out, keys, values, parents, lengths):
    tokens, heads_q, head_size = queries.shape
    rows = keys.shape[0]
    heads_kv = rows // tokens
    array = jax.ShapeDtypeStruct
    return call(
        functools.partial(prepare_kernel, window, heads_kv),
        "prepare",
        (parents, lengths, keys, values, queries, grad_out),
        [array((heads_kv, tokens * 8, head_size), BF16)] * 2
        + [array((heads_kv, tokens, head_size), BF16)] * 2
        + [array((2 * tokens + window * CAP * TILE, 128), F32), array((8, tokens * 8), F32)],
        [pltpu.VMEM((rows, head_size), F32)],
        flops=1 << 20,
        scalars=2,
    )


def probs(slots, prompt_k, prompt_v, prepared, blocks):
    qh, gh, own_k, own_v, bias, weight = prepared
    heads_kv, tokens, head_size = own_k.shape
    window = len(slots)
    rows = tokens * heads_kv
    front = CAP * TILE
    before = tokens + window * front
    sent = rows + (window + 1) // 2 * 2 * front * heads_kv
    kept = rows + window // 2 * 2 * front * heads_kv
    array = jax.ShapeDtypeStruct
    work = heads_kv * tokens * 8 * (before + tokens)
    return call(
        functools.partial(probs_kernel, slots, heads_kv, head_size**-0.5),
        "probs",
        (prompt_k, prompt_v, own_k, own_v, qh, gh, bias, weight, *blocks),
        [
            array((sent, head_size), BF16),
            array((kept, head_size), BF16),
            array((heads_kv, before + tokens, head_size), BF16),
            array((heads_kv, before + tokens, tokens * 8), BF16),
            array((heads_kv, tokens, tokens * 8), BF16),
        ],
        [
            pltpu.VMEM((heads_kv, before + tokens, head_size), BF16),
            pltpu.VMEM((before, tokens * 8), BF16),
            pltpu.VMEM((2, heads_kv, before, head_size), F32),
            pltpu.VMEM((rows, head_size), F32),
        ],
        flops=8 * work * head_size,
        transcendentals=work,
    )


def grads(qh, gh, kh, ds, p_own):
    heads_kv, tokens, _ = p_own.shape
    head_size = kh.shape[2]
    array = jax.ShapeDtypeStruct
    return call(
        functools.partial(grads_kernel, heads_kv),
        "grads",
        (qh, gh, kh, ds, p_own),
        [
            array((tokens, heads_kv * 8, head_size), BF16),
            array((tokens * heads_kv, head_size), F32),
            array((tokens * heads_kv, head_size), F32),
        ],
        [pltpu.VMEM((tokens * heads_kv, head_size), F32)],
        flops=4 * heads_kv * tokens * 8 * kh.shape[1] * head_size,
    )


def shift_route(distance, size):
    return [(i, i + distance) for i in range(size - distance)]


def back(route):
    return [(j, i) for i, j in route]


def added(*blocks):
    total = blocks[0].astype(F32)
    for block in blocks[1:]:
        total = total + block.astype(F32)
    return total


def per_device(size, queries, keys, values, grad_out, parents, lengths):
    tokens, heads_kv, head_size = keys.shape
    rows = tokens * heads_kv
    unit = 2 * CAP * TILE * heads_kv
    one = CAP * TILE * heads_kv
    near = size <= W + 1
    window = min(W, size - 2) if near else W
    device = lax.axis_index("node")
    even = lax.rem(device, 2) == 0
    keys = keys.reshape(rows, head_size)
    values = values.reshape(rows, head_size)
    strides = [2**i for i in range(2, size.bit_length()) if 2**i < size]
    neighbours = [(i, i ^ 1) for i in range(size)]
    far_route = shift_route(4, size)[1:]
    near_route = shift_route(2, size)

    def prompt_route(stride):
        return [(i + j, i + j + stride) for i in range(0, size, 2 * stride) for j in (0, 1)]

    top = strides[-1]
    prepared = prepare(window, queries, grad_out, keys, values, parents, lengths)
    values_far = permuted(values, [(0, top + 1)])
    keys_far = permuted(keys, [(0, top)])
    values_next = permuted(values, [(0, 1)])
    head = jnp.concatenate([keys[:one], values[:one]])
    far = permuted(head, far_route)
    held = jnp.where(device == 0, keys, added(values_far, keys_far, values_next).astype(BF16))
    for stride in reversed(strides[:-1]):
        held = added(held, permuted(held, prompt_route(stride))).astype(BF16)
    second = permuted(jnp.concatenate([held, head, far]), near_route)
    held = jnp.where(lax.rem(device, 4) < 2, held, second[:rows])
    two, four, six = second[rows : rows + unit], far, second[rows + unit :]
    if near:
        even_slots = jnp.where(even, jnp.concatenate([head, two, four]), jnp.concatenate([two, four, six]))
        third = permuted(jnp.concatenate([held, even_slots]), neighbours)
        other, start = third[:rows], rows
    else:
        third = permuted(jnp.concatenate([head, two, four, six]), shift_route(1, size))
        other, start = permuted(held, neighbours), 0
    slots = [(0, start), (1, rows), (0, start + unit), (2, 0), (0, start + 2 * unit), (1, rows + unit), (0, start + 3 * unit)]
    slots = slots[:window]

    send, keep, kh, ds, p_own = probs(
        slots, jnp.where(even, held, other), jnp.where(even, other, held), prepared, (third, second, far)
    )
    grad_queries, dk, dv = grads(*prepared[:2], kh, ds, p_own)

    def slot(array, index):
        return array[rows + index * unit : rows + (index + 1) * unit]

    if near:
        third = permuted(send, neighbours)
        total = added(keep[:rows], third[:rows])
        from_third = [slot(third, i) for i in range(3)]
        none = jnp.zeros_like(from_third[0])
        mine = jnp.where(even, from_third[0], none)
        two = added(slot(keep, 0), jnp.where(even, from_third[1], from_third[0]))
        four = added(slot(keep, 1), jnp.where(even, from_third[2], from_third[1]))
        six = added(slot(keep, 2), jnp.where(even, none, from_third[2]))
    else:
        third = permuted(send[rows:], back(shift_route(1, size)))
        total = added(keep[:rows], permuted(send[:rows], neighbours))
        mine = third[:unit]
        two = added(slot(keep, 0), third[unit : 2 * unit])
        four = added(slot(keep, 1), third[2 * unit : 3 * unit])
        six = added(slot(keep, 2), third[3 * unit :])
    second = permuted(jnp.concatenate([total.astype(BF16), two.astype(BF16), six.astype(BF16)]), back(near_route))
    total = added(total.astype(BF16), jnp.where(lax.rem(device, 4) < 2, second[:rows], 0)).astype(BF16)
    mine = added(mine, slot(second, 0))
    four = added(four, slot(second, 1)).astype(BF16)
    for stride in strides[:-1]:
        total = added(total, permuted(total, back(prompt_route(stride)))).astype(BF16)
    values_far = permuted(total, [(top + 1, 0)])
    keys_far = permuted(total, [(top, 0)])
    values_next = permuted(total, [(1, 0)])
    mine = added(mine, permuted(four, back(far_route)))
    own = []
    for side, local, prompt in ((0, dk, added(total, keys_far)), (1, dv, added(values_far, values_next))):
        whole = local + jnp.where(device == 0, prompt, 0.0)
        own.append(whole.at[:one].add(mine[side * one : (side + 1) * one]).reshape(tokens, heads_kv, head_size))
    return grad_queries, own[0], own[1]


def solution(mesh):
    by_token = P(("leaf", "node"), "tensor", None)
    return jax.shard_map(
        functools.partial(per_device, mesh.shape["node"]),
        mesh=mesh,
        in_specs=(by_token, by_token, by_token, by_token, P("leaf"), P("leaf")),
        out_specs=(by_token, by_token, by_token),
        check_vma=False,
    )
```

time: 72.5 us -> 67.6 us (0.932)
  waiting for transfers between devices: 41.1 us -> 30.3 us
  local copies, waits for them, and re-layouts: 1.47 us -> 5.45 us
  starting transfers between devices: 16.9 us -> 19.2 us
    ppermute x10 -> x12, waiting for transfers between devices: 41.1 us -> 30.3 us  [permuted(): return lax.ppermute(block, 'node', route)]
    unnamed x16, local copies, waits for them, and re-layouts: 1.43 us -> 3.9 us
    ppermute x10 -> x12, starting transfers between devices: 16.9 us -> 19.2 us  [permuted(): return lax.ppermute(block, 'node', route)]
    slice x2, local copies, waits for them, and re-layouts: 0.03 us -> 1.55 us  [per_device(): head = jnp.concatenate([keys[:one], values[:one]])]
    pallas_call x1 -> x3, Pallas kernels: 10.3 us -> 9.71 us  [call(): pl.pallas_call(kernel, in_specs=[SMEM] * scalars + [VMEM] * (len(operands...]
  transfers between devices with their start and end apart: 10 -> 12, of which waited for: 8 -> 6; matrix products, arithmetic and copies ran while one was open for 0% -> 4% of each run, Pallas kernels for 0% -> 5%
where the time goes in v4:
time: 67.6 us; the launch traced here: 67.1 us
  waiting for transfers between devices  30.3 us (45%)
  starting transfers between devices  19.2 us (28%)
  Pallas kernels  9.71 us (14%)
  local copies, waits for them, and re-layouts  5.45 us (8%)
  other arithmetic  1.48 us (2%)
  between operations  0.96 us (1%)
    ppermute x12, waiting for transfers between devices, permuted(): return lax.ppermute(block, 'node', route)  30.3 us
    ppermute x12, starting transfers between devices, permuted(): return lax.ppermute(block, 'node', route)  19.2 us
    pallas_call x3, Pallas kernels, call(): pl.pallas_call(kernel, in_specs=[SMEM] * scalars + [VMEM] * (len(operands...  9.71 us
    unnamed x16, local copies, waits for them, and re-layouts  3.9 us
    slice x2, local copies, waits for them, and re-layouts, per_device(): head = jnp.concatenate([keys[:one], values[:one]])  1.55 us
  transfers between devices with their start and end apart: 12, of which 6 were waited for; matrix products, arithmetic and copies ran while one was open for 4% of the time, Pallas kernels for 5%

profile of v4, /device:TPU:0, one launch (start us, length us, event | category | flops | bytes accessed | tf_op | source)
XLA Modules:
  0.0 67.1 jit_solution(7752457207629883853)
XLA Ops:
  0.6 0.0 copy-start.1
  0.6 0.0 copy-start
  0.6 6.1 %collective-permute-start.1 = (bf16[512,128]{1,0:T(8,128)(2,1)}, bf16[512,128]{1,0:T(8,128)(2,1)S(1)}, u32[]{:S(2)}, u32[]{:S(2)}) collective-permute-start(bf16[512,128]{1,0:T(8,128)(2,1)} %bitcast.6), channel_id=1, source_target_pairs={{0,8},{1,9},{16,24},{17,25}} | collective-permute-start | bytes 393224 | tf_op jit(solution)/shard_map/ppermute | solution.py:22
  6.7 1.3 %collective-permute-start.2 = (bf16[512,128]{1,0:T(8,128)(2,1)}, bf16[512,128]{1,0:T(8,128)(2,1)S(1)}, u32[]{:S(2)}, u32[]{:S(2)}) collective-permute-start(bf16[512,128]{1,0:T(8,128)(2,1)} %bitcast.9), channel_id=1, source_target_pairs={{0,2},{1,3},{16,18},{17,19}} | collective-permute-start | bytes 393224 | tf_op jit(solution)/shard_map/ppermute | solution.py:22
  8.0 1.3 %collective-permute-start = (bf16[512,128]{1,0:T(8,128)(2,1)}, bf16[512,128]{1,0:T(8,128)(2,1)S(1)}, u32[]{:S(2)}, u32[]{:S(2)}) collective-permute-start(bf16[512,128]{1,0:T(8,128)(2,1)} %bitcast.10), channel_id=1, source_target_pairs={{0,10},{1,11},{16,26},{17,27}} | collective-permute-start | bytes 393224 | tf_op jit(solution)/shard_map/ppermute | solution.py:22
  9.4 0.8 %slice.101 = bf16[32,4,128]{2,1,0:T(4,128)(2,1)S(1)} slice(bf16[128,4,128]{2,1,0:T(4,128)(2,1)} %param.11), slice={[0:32], [0:4], [0:128]} | slice | bytes 65536 | tf_op jit(solution)/shard_map/slice | solution.py:301
  10.1 0.8 %slice.103 = bf16[32,4,128]{2,1,0:T(4,128)(2,1)S(1)} slice(bf16[128,4,128]{2,1,0:T(4,128)(2,1)} %param.12), slice={[0:32], [0:4], [0:128]} | slice | bytes 65536 | tf_op jit(solution)/shard_map/slice | solution.py:301
  10.9 0.7 collective-permute-start.3
  11.6 0.0 collective-permute-done.1
  11.6 0.0 collective-permute-done.2
  11.6 1.0 %collective-permute-done = bf16[512,128]{1,0:T(8,128)(2,1)S(1)} collective-permute-done((bf16[512,128]{1,0:T(8,128)(2,1)}, bf16[512,128]{1,0:T(8,128)(2,1)S(1)}, u32[]{:S(2)}, u32[]{:S(2)}) %collective-permute-start) | collective-permute-done | bytes 131104 | tf_op jit(solution)/shard_map/ppermute | solution.py:22
  12.6 1.0 %fusion = bf16[512,128]{1,0:T(8,128)(2,1)S(1)} fusion(bf16[512,128]{1,0:T(8,128)(2,1)} %bitcast.7, bf16[512,128]{1,0:T(8,128)(2,1)S(1)} %collective-permute-done.2, bf16[512,128]{1,0:T(8,128)(2,1)S(1)} %collective-permute-done.1, bf16[512,128]{1,0:T(8,128)(2,1)S(1)} %collective-permute-done, pred[]{:T(512)S(6)} %eq.9), kind=kLoop, calls=%fused_computation.9 | loop fusion | flops 458752 | bytes 655361 | tf_op jit(solution)/shard_map/jit(_where)/select_n | solution.py:303
  13.6 0.0 collective-permute-done.3.refs_10_
  13.7 3.6 %collective-permute-start.4 = (bf16[1024,128]{1,0:T(8,128)(2,1)S(1)}, bf16[1024,128]{1,0:T(8,128)(2,1)S(1)}, u32[]{:S(2)}, u32[]{:S(2)}) collective-permute-start(bf16[1024,128]{1,0:T(8,128)(2,1)S(1)} %pad_maximum_fusion.1), channel_id=1, source_target_pairs={{0,4},{2,6},{4,8},{6,10},{8,12},{10,14},{1,5},{3,7},{5,9},{7,11},{... | collective-permute-start | bytes 786440 | tf_op jit(solution)/shard_map/ppermute | solution.py:22
  17.3 5.7 %collective-permute-done.4.refs_9_ = bf16[1024,128]{1,0:T(8,128)(2,1)S(1)} collective-permute-done((bf16[1024,128]{1,0:T(8,128)(2,1)S(1)}, bf16[1024,128]{1,0:T(8,128)(2,1)S(1)}, u32[]{:S(2)}, u32[]{:S(2)}) %collective-permute-start.4) | collective-permute-done | bytes 262176 | tf_op jit(solution)/shard_map/ppermute | solution.py:22
  23.1 0.1 collective-permute-start.5
  23.2 0.0 copy-done.1
  23.2 0.0 copy-done
  23.2 0.0 copy-start.2
  23.3 0.9 %copy-done.2 = bf16[128,4,128]{2,1,0:T(4,128)(2,1)S(1)} copy-done((bf16[128,4,128]{2,1,0:T(4,128)(2,1)S(1)}, bf16[128,4,128]{2,1,0:T(4,128)(2,1)}, u32[]{:S(2)}) %copy-start.2) | copy-done | bytes 131096
  24.2 0.0 copy-start.3
  24.2 0.9 %copy-done.3 = bf16[128,4,128]{2,1,0:T(4,128)(2,1)S(1)} copy-done((bf16[128,4,128]{2,1,0:T(4,128)(2,1)S(1)}, bf16[128,4,128]{2,1,0:T(4,128)(2,1)}, u32[]{:S(2)}) %copy-start.3) | copy-done | bytes 131096
  25.1 0.0 copy-start.4
  25.1 0.7 copy-done.4
  25.7 0.7 copy-done.5
  26.4 1.1 %prepare.1 = (bf16[4,1024,128]{2,1,0:T(8,128)(2,1)S(1)}, bf16[4,1024,128]{2,1,0:T(8,128)(2,1)S(1)}, bf16[4,128,128]{2,1,0:T(8,128)(2,1)S(1)}, bf16[4,128,128]{2,...) custom-call(s32[64]{0:T(128)S(1)} %copy-done.4, s32[64]{0:T(128)S(1)} %copy-done.5, ...), custom_call_target="tpu_custom_call" | custom-call | flops 1048576 | bytes 4981248 | tf_op jit(solution)/shard_map/prepare/pallas_call | solution.py:181
  27.5 4.5 %collective-permute-done.5.refs_8_ = bf16[1280,128]{1,0:T(8,128)(2,1)S(1)} collective-permute-done((bf16[1280,128]{1,0:T(8,128)(2,1)S(1)}, bf16[1280,128]{1,0:T(8,128)(2,1)S(1)}, u32[]{:S(2)}, u32[]{:S(2)}) %collective-permute-start.5) | collective-permute-done | bytes 327712 | tf_op jit(solution)/shard_map/ppermute | solution.py:22
  32.0 6.2 %probs.1 = (bf16[1280,128]{1,0:T(8,128)(2,1)S(1)}, bf16[1280,128]{1,0:T(8,128)(2,1)S(1)}, bf16[4,448,128]{2,1,0:T(8,128)(2,1)S(1)}, bf16[4,448,1024]{2,1,0:T(8,128)(2,1)S(1)}, bf16[4,128,1024]{2,1,0:T(8,128)(2,1)S(1)}) custom-call(bf16[512,128]{1,0:T(8,128)(2,1)S(1)} %get-tuple-element.58.refs_0_, bf16[512,128]{1,0:T(8,128)(2,1)S(1)} %get-tuple-element.57.refs_1_, ...), custom_call_target="tpu_custom_call" | custom-call | flops 1879048192 | bytes 9371648 | tf_op jit(solution)/shard_map/probs/pallas_call | solution.py:181
  38.2 0.4 collective-permute-start.6
  38.6 7.6 %collective-permute-done.6 = bf16[1280,128]{1,0:T(8,128)(2,1)S(1)} collective-permute-done((bf16[1280,128]{1,0:T(8,128)(2,1)S(1)}, bf16[1280,128]{1,0:T(8,128)(2,1)S(1)}, u32[]{:S(2)}, u32[]{:S(2)}) %collective-permute-start.6) | collective-permute-done | bytes 327712 | tf_op jit(solution)/shard_map/ppermute | solution.py:22
  46.2 0.1 add_convert_fusion.5
  46.3 1.3 %collective-permute-start.7 = (bf16[1024,128]{1,0:T(8,128)(2,1)S(1)}, bf16[1024,128]{1,0:T(8,128)(2,1)S(1)}, u32[]{:S(2)}, u32[]{:S(2)}) collective-permute-start(bf16[1024,128]{1,0:T(8,128)(2,1)S(1)} %pad_maximum_fusion.2), channel_id=1, source_target_pairs={{4,0},{6,2},{8,4},{10,6},{12,8},{14,10},{5,1},{7,3},{9,5},{11,7},{... | collective-permute-start | bytes 786440 | tf_op jit(solution)/shard_map/ppermute | solution.py:22
  47.6 2.4 %grads.1 = (bf16[128,32,128]{2,1,0:T(8,128)(2,1)}, f32[512,128]{1,0:T(8,128)S(1)}, f32[512,128]{1,0:T(8,128)S(1)}) custom-call(bf16[4,1024,128]{2,1,0:T(8,128)(2,1)S(1)} %get-tuple-element.41.refs_4_.refs_0_, bf16[4,1024,128]{2,1,0:T(8,128)(2,1)S(1)} %get-tuple-element.42.refs_5_.refs_1_, bf16[4,448,128]{2,1,0:T(8,128)(2,1)S(1)} %get-tuple-element.47.refs_2_, ...), custom_call_target="tpu_custom_call" | custom-call | flops 939524096 | bytes 8847360 | tf_op jit(solution)/shard_map/grads/pallas_call | solution.py:181
  50.0 5.0 %collective-permute-done.7 = bf16[1024,128]{1,0:T(8,128)(2,1)S(1)} collective-permute-done((bf16[1024,128]{1,0:T(8,128)(2,1)S(1)}, bf16[1024,128]{1,0:T(8,128)(2,1)S(1)}, u32[]{:S(2)}, u32[]{:S(2)}) %collective-permute-start.7) | collective-permute-done | bytes 262176 | tf_op jit(solution)/shard_map/ppermute | solution.py:22
  55.1 0.7 collective-permute-start.9
  55.8 1.3 %collective-permute-start.11 = (bf16[512,128]{1,0:T(8,128)(2,1)S(1)}, bf16[512,128]{1,0:T(8,128)(2,1)S(1)}, u32[]{:S(2)}, u32[]{:S(2)}) collective-permute-start(bf16[512,128]{1,0:T(8,128)(2,1)S(1)} %add_convert_fusion), channel_id=1, source_target_pairs={{2,0},{3,1},{18,16},{19,17}} | collective-permute-start | bytes 393224 | tf_op jit(solution)/shard_map/ppermute | solution.py:22
  57.1 1.3 %collective-permute-start.10 = (bf16[512,128]{1,0:T(8,128)(2,1)S(1)}, bf16[512,128]{1,0:T(8,128)(2,1)S(1)}, u32[]{:S(2)}, u32[]{:S(2)}) collective-permute-start(bf16[512,128]{1,0:T(8,128)(2,1)S(1)} %add_convert_fusion), channel_id=1, source_target_pairs={{10,0},{11,1},{26,16},{27,17}} | collective-permute-start | bytes 393224 | tf_op jit(solution)/shard_map/ppermute | solution.py:22
  58.4 1.3 %collective-permute-start.8 = (bf16[512,128]{1,0:T(8,128)(2,1)S(1)}, bf16[512,128]{1,0:T(8,128)(2,1)S(1)}, u32[]{:S(2)}, u32[]{:S(2)}) collective-permute-start(bf16[512,128]{1,0:T(8,128)(2,1)S(1)} %add_convert_fusion), channel_id=1, source_target_pairs={{8,0},{9,1},{24,16},{25,17}} | collective-permute-start | bytes 393224 | tf_op jit(solution)/shard_map/ppermute | solution.py:22
  59.7 0.0 collective-permute-done.9
  59.7 6.4 %collective-permute-done.8 = bf16[512,128]{1,0:T(8,128)(2,1)S(1)} collective-permute-done((bf16[512,128]{1,0:T(8,128)(2,1)S(1)}, bf16[512,128]{1,0:T(8,128)(2,1)S(1)}, u32[]{:S(2)}, u32[]{:S(2)}) %collective-permute-start.8) | collective-permute-done | bytes 131104 | tf_op jit(solution)/shard_map/ppermute | solution.py:22
  66.1 0.1 select_add_fusion.1
  66.2 0.0 collective-permute-done.11
  66.2 0.0 collective-permute-done.10
  66.2 0.1 select_add_fusion
  66.3 0.0 copy-start.6
  66.3 0.0 copy-start.7
  66.3 0.7 %copy-done.6 = f32[512,128]{1,0:T(8,128)} copy-done((f32[512,128]{1,0:T(8,128)}, f32[512,128]{1,0:T(8,128)S(1)}, u32[]{:S(2)}) %copy-start.6) | copy-done | bytes 262168
  67.0 0.1 copy-done.7
  (14 shorter events, 0.4 us)
Async XLA Ops:
  0.6 22.6 %copy-start.1 = (bf16[128,32,128]{2,1,0:T(8,128)(2,1)S(1)}, bf16[128,32,128]{2,1,0:T(8,128)(2,1)}, u32[]{:S(2)}) copy-start(bf16[128,32,128]{2,1,0:T(8,128)(2,1)} %refs_5_.1) | copy-start | bytes 3145732
  0.6 22.6 %copy-start = (bf16[128,32,128]{2,1,0:T(8,128)(2,1)S(1)}, bf16[128,32,128]{2,1,0:T(8,128)(2,1)}, u32[]{:S(2)}) copy-start(bf16[128,32,128]{2,1,0:T(8,128)(2,1)} %refs_4_.1) | copy-start | bytes 3145732
  0.6 11.0 %collective-permute-start.1 = (bf16[512,128]{1,0:T(8,128)(2,1)}, bf16[512,128]{1,0:T(8,128)(2,1)S(1)}, u32[]{:S(2)}, u32[]{:S(2)}) collective-permute-start(bf16[512,128]{1,0:T(8,128)(2,1)} %bitcast.6), channel_id=1, source_target_pairs={{0,8},{1,9},{16,24},{17,25}} | collective-permute-start | bytes 393224 | tf_op jit(solution)/shard_map/ppermute | solution.py:22
  6.7 4.9 %collective-permute-start.2 = (bf16[512,128]{1,0:T(8,128)(2,1)}, bf16[512,128]{1,0:T(8,128)(2,1)S(1)}, u32[]{:S(2)}, u32[]{:S(2)}) collective-permute-start(bf16[512,128]{1,0:T(8,128)(2,1)} %bitcast.9), channel_id=1, source_target_pairs={{0,2},{1,3},{16,18},{17,19}} | collective-permute-start | bytes 393224 | tf_op jit(solution)/shard_map/ppermute | solution.py:22
  8.0 4.6 %collective-permute-start = (bf16[512,128]{1,0:T(8,128)(2,1)}, bf16[512,128]{1,0:T(8,128)(2,1)S(1)}, u32[]{:S(2)}, u32[]{:S(2)}) collective-permute-start(bf16[512,128]{1,0:T(8,128)(2,1)} %bitcast.10), channel_id=1, source_target_pairs={{0,10},{1,11},{16,26},{17,27}} | collective-permute-start | bytes 393224 | tf_op jit(solution)/shard_map/ppermute | solution.py:22
  10.9 2.7 %collective-permute-start.3 = (bf16[256,128]{1,0:T(8,128)(2,1)S(1)}, bf16[256,128]{1,0:T(8,128)(2,1)S(1)}, u32[]{:S(2)}, u32[]{:S(2)}) collective-permute-start(bf16[256,128]{1,0:T(8,128)(2,1)S(1)} %pad_maximum_fusion.3), channel_id=1, source_target_pairs={{2,10},{4,12},{6,14},{3,11},{5,13},{7,15},{18,26},{20,28},{22,30},... | collective-permute-start | bytes 196616 | tf_op jit(solution)/shard_map/ppermute | solution.py:22
  13.7 9.4 %collective-permute-start.4 = (bf16[1024,128]{1,0:T(8,128)(2,1)S(1)}, bf16[1024,128]{1,0:T(8,128)(2,1)S(1)}, u32[]{:S(2)}, u32[]{:S(2)}) collective-permute-start(bf16[1024,128]{1,0:T(8,128)(2,1)S(1)} %pad_maximum_fusion.1), channel_id=1, source_target_pairs={{0,4},{2,6},{4,8},{6,10},{8,12},{10,14},{1,5},{3,7},{5,9},{7,11},{... | collective-permute-start | bytes 786440 | tf_op jit(solution)/shard_map/ppermute | solution.py:22
  23.1 8.9 %collective-permute-start.5 = (bf16[1280,128]{1,0:T(8,128)(2,1)S(1)}, bf16[1280,128]{1,0:T(8,128)(2,1)S(1)}, u32[]{:S(2)}, u32[]{:S(2)}) collective-permute-start(bf16[1280,128]{1,0:T(8,128)(2,1)S(1)} %pad_maximum_fusion), channel_id=1, source_target_pairs={{0,2},{2,0},{4,6},{6,4},{8,10},{10,8},{12,14},{14,12},{1,3},{3,1},... | collective-permute-start | bytes 983048 | tf_op jit(solution)/shard_map/ppermute | solution.py:22
  23.2 0.9 %copy-start.2 = (bf16[128,4,128]{2,1,0:T(4,128)(2,1)S(1)}, bf16[128,4,128]{2,1,0:T(4,128)(2,1)}, u32[]{:S(2)}) copy-start(bf16[128,4,128]{2,1,0:T(4,128)(2,1)} %param.11) | copy-start | bytes 393220
  24.2 0.9 %copy-start.3 = (bf16[128,4,128]{2,1,0:T(4,128)(2,1)S(1)}, bf16[128,4,128]{2,1,0:T(4,128)(2,1)}, u32[]{:S(2)}) copy-start(bf16[128,4,128]{2,1,0:T(4,128)(2,1)} %param.12) | copy-start | bytes 393220
  25.1 0.7 copy-start.4
  25.7 0.7 copy-start.5
  38.2 7.9 %collective-permute-start.6 = (bf16[1280,128]{1,0:T(8,128)(2,1)S(1)}, bf16[1280,128]{1,0:T(8,128)(2,1)S(1)}, u32[]{:S(2)}, u32[]{:S(2)}) collective-permute-start(bf16[1280,128]{1,0:T(8,128)(2,1)S(1)} %get-tuple-element.53), channel_id=1, source_target_pairs={{0,2},{2,0},{4,6},{6,4},{8,10},{10,8},{12,14},{14,12},{1,3},{3,1},... | collective-permute-start | bytes 983048 | tf_op jit(solution)/shard_map/ppermute | solution.py:22
  46.3 8.7 %collective-permute-start.7 = (bf16[1024,128]{1,0:T(8,128)(2,1)S(1)}, bf16[1024,128]{1,0:T(8,128)(2,1)S(1)}, u32[]{:S(2)}, u32[]{:S(2)}) collective-permute-start(bf16[1024,128]{1,0:T(8,128)(2,1)S(1)} %pad_maximum_fusion.2), channel_id=1, source_target_pairs={{4,0},{6,2},{8,4},{10,6},{12,8},{14,10},{5,1},{7,3},{9,5},{11,7},{... | collective-permute-start | bytes 786440 | tf_op jit(solution)/shard_map/ppermute | solution.py:22
  55.1 4.6 %collective-permute-start.9 = (bf16[256,128]{1,0:T(8,128)(2,1)S(1)}, bf16[256,128]{1,0:T(8,128)(2,1)S(1)}, u32[]{:S(2)}, u32[]{:S(2)}) collective-permute-start(bf16[256,128]{1,0:T(8,128)(2,1)S(1)} %add_convert_fusion.3), channel_id=1, source_target_pairs={{10,2},{12,4},{14,6},{11,3},{13,5},{15,7},{26,18},{28,20},{30,22},... | collective-permute-start | bytes 196616 | tf_op jit(solution)/shard_map/ppermute | solution.py:22
  55.8 10.4 %collective-permute-start.11 = (bf16[512,128]{1,0:T(8,128)(2,1)S(1)}, bf16[512,128]{1,0:T(8,128)(2,1)S(1)}, u32[]{:S(2)}, u32[]{:S(2)}) collective-permute-start(bf16[512,128]{1,0:T(8,128)(2,1)S(1)} %add_convert_fusion), channel_id=1, source_target_pairs={{2,0},{3,1},{18,16},{19,17}} | collective-permute-start | bytes 393224 | tf_op jit(solution)/shard_map/ppermute | solution.py:22
  57.1 9.1 %collective-permute-start.10 = (bf16[512,128]{1,0:T(8,128)(2,1)S(1)}, bf16[512,128]{1,0:T(8,128)(2,1)S(1)}, u32[]{:S(2)}, u32[]{:S(2)}) collective-permute-start(bf16[512,128]{1,0:T(8,128)(2,1)S(1)} %add_convert_fusion), channel_id=1, source_target_pairs={{10,0},{11,1},{26,16},{27,17}} | collective-permute-start | bytes 393224 | tf_op jit(solution)/shard_map/ppermute | solution.py:22
  58.4 7.8 %collective-permute-start.8 = (bf16[512,128]{1,0:T(8,128)(2,1)S(1)}, bf16[512,128]{1,0:T(8,128)(2,1)S(1)}, u32[]{:S(2)}, u32[]{:S(2)}) collective-permute-start(bf16[512,128]{1,0:T(8,128)(2,1)S(1)} %add_convert_fusion), channel_id=1, source_target_pairs={{8,0},{9,1},{24,16},{25,17}} | collective-permute-start | bytes 393224 | tf_op jit(solution)/shard_map/ppermute | solution.py:22
  66.3 0.7 %copy-start.6 = (f32[512,128]{1,0:T(8,128)}, f32[512,128]{1,0:T(8,128)S(1)}, u32[]{:S(2)}) copy-start(f32[512,128]{1,0:T(8,128)S(1)} %get-tuple-element.62) | copy-start | bytes 786436
  66.3 0.8 %copy-start.7 = (f32[512,128]{1,0:T(8,128)}, f32[512,128]{1,0:T(8,128)S(1)}, u32[]{:S(2)}) copy-start(f32[512,128]{1,0:T(8,128)S(1)} %get-tuple-element.61) | copy-start | bytes 786436

commit v5 on v4

--- a/solution.py
+++ b/solution.py
@@ -33,14 +33,13 @@
         for k in range(1, window + 1):
             need[k] = jnp.where(active & (distance == k), depth, need[k])
         cursor = jnp.where(active, parents[jnp.maximum(owner, 0) * TD], cursor)
-    limits = [jnp.where(device >= 1, lengths[t], 0) for t in range(TD)]
+    prompt = [jnp.where(device >= 1, lengths[t], 0) for t in range(TD)]
+    behind = []
     for k in range(1, window + 1):
         owner = device - k
-        for c in range(CAP):
-            seen = (owner >= 1) & (c < need[k])
-            limits.append(jnp.where(seen, lengths[jnp.maximum(owner, 0) * TD + c], 0))
-    limits += [lengths[device * TD + t] for t in range(TD)]
-    return limits
+        seen = [(owner >= 1) & (c < need[k]) for c in range(CAP)]
+        behind.append([jnp.where(seen[c], lengths[jnp.maximum(owner, 0) * TD + c], 0) for c in range(CAP)])
+    return prompt, behind, [lengths[device * TD + t] for t in range(TD)]
 
 
 def split_heads(block, heads_ref, start, count, heads_kv, wide):
@@ -55,7 +54,7 @@
     return wide[: count * heads_kv]
 
 
-def prepare_kernel(window, heads_kv, *refs):
+def prepare_kernel(order, heads_kv, *refs):
     parents, lengths, keys, values, q_ref, g_ref, qh, gh, own_k, own_v, bias, weight, wide = refs
     tokens = TD * TILE
     device = lax.axis_index("node")
@@ -67,19 +66,26 @@
     split_heads(keys[...], own_k, 0, tokens, heads_kv, wide)
     split_heads(values[...], own_v, 0, tokens, heads_kv, wide)
     place = lax.broadcasted_iota(jnp.int32, (TILE, 128), 0)
-    for t, limit in enumerate(column_limits(device, window, parents, lengths)):
+    prompt, behind, own = column_limits(device, len(order), parents, lengths)
+    even = lax.rem(device, 2) == 0
+    limits = prompt
+    for on_even, on_odd in order:
+        limits = limits + [jnp.where(even, x, y) for x, y in zip(behind[on_even - 1], behind[on_odd - 1])]
+    for t, limit in enumerate(limits + own):
         bias[t * TILE : (t + 1) * TILE] = jnp.where(place < limit, 0.0, MASKED)
     lane_place = lax.broadcasted_iota(jnp.int32, (8, 128), 1) // 8
     for t in range(TD):
         weight[:, t * 128 : (t + 1) * 128] = jnp.where(lane_place < lengths[device * TD + t], 1.0, 0.0)
 
 
-def probs_kernel(slots, heads_kv, scale, *refs):
+def probs_kernel(sources, targets, heads_kv, scale, *refs):
     prompt_k, prompt_v, own_k, own_v, qh, gh, bias, weight_ref = refs[:8]
-    blocks = refs[8 : 8 + 1 + max(source for source, _ in slots)]
-    send_ref, keep_ref, kh, ds_ref, p_own = refs[8 + len(blocks) : 13 + len(blocks)]
-    vh, p_ref, grads, wide = refs[13 + len(blocks) :]
-    window = len(slots)
+    n_in = 1 + max(source for source, _ in sources)
+    n_out = 1 + max(target for target, _ in targets)
+    blocks = refs[8 : 8 + n_in]
+    outs = refs[8 + n_in : 8 + n_in + n_out]
+    kh, ds_ref, p_own, vh, p_ref, grads, wide = refs[8 + n_in + n_out :]
+    window = len(sources)
     tokens = TD * TILE
     front = CAP * TILE
     before = tokens + window * front
@@ -88,7 +94,7 @@
 
     for side, heads_ref, prompt, own in ((0, kh, prompt_k, own_k), (1, vh, prompt_v, own_v)):
         split_heads(prompt[...], heads_ref, 0, tokens, heads_kv, wide)
-        for k, (source, start) in enumerate(slots):
+        for k, (source, start) in enumerate(sources):
             start += side * front * heads_kv
             block = blocks[source][start : start + front * heads_kv]
             split_heads(block, heads_ref, tokens + k * front, front, heads_kv, wide)
@@ -126,17 +132,17 @@
 
         @pl.when(kept)
         def _():
-            keep_ref[:rows] = dprompt
+            outs[1][:rows] = dprompt
 
         @pl.when(jnp.logical_not(kept))
         def _():
-            send_ref[:rows] = dprompt
-
-        for k in range(window):
+            outs[0][:rows] = dprompt
+
+        for k, (target, start) in enumerate(targets):
             span = slice(tokens + k * front, tokens + (k + 1) * front)
             block = join_heads([grads[side, h, span] for h in range(heads_kv)], front, heads_kv, wide).astype(BF16)
-            start = rows + (k // 2 * 2 + side) * rows_front
-            (send_ref, keep_ref)[k % 2][start : start + rows_front] = block
+            start += side * rows_front
+            outs[target][start : start + rows_front] = block
 
 
 def grads_kernel(heads_kv, *refs):
@@ -190,42 +196,40 @@
     )(*operands)
 
 
-def prepare(window, queries, grad_out, keys, values, parents, lengths):
+def prepare(order, queries, grad_out, keys, values, parents, lengths):
     tokens, heads_q, head_size = queries.shape
     rows = keys.shape[0]
     heads_kv = rows // tokens
     array = jax.ShapeDtypeStruct
     return call(
-        functools.partial(prepare_kernel, window, heads_kv),
+        functools.partial(prepare_kernel, order, heads_kv),
         "prepare",
         (parents, lengths, keys, values, queries, grad_out),
         [array((heads_kv, tokens * 8, head_size), BF16)] * 2
         + [array((heads_kv, tokens, head_size), BF16)] * 2
-        + [array((2 * tokens + window * CAP * TILE, 128), F32), array((8, tokens * 8), F32)],
+        + [array((2 * tokens + len(order) * CAP * TILE, 128), F32), array((8, tokens * 8), F32)],
         [pltpu.VMEM((rows, head_size), F32)],
         flops=1 << 20,
         scalars=2,
     )
 
 
-def probs(slots, prompt_k, prompt_v, prepared, blocks):
+def probs(sources, targets, prompt_k, prompt_v, prepared, blocks):
     qh, gh, own_k, own_v, bias, weight = prepared
     heads_kv, tokens, head_size = own_k.shape
-    window = len(slots)
     rows = tokens * heads_kv
     front = CAP * TILE
-    before = tokens + window * front
-    sent = rows + (window + 1) // 2 * 2 * front * heads_kv
-    kept = rows + window // 2 * 2 * front * heads_kv
+    unit = 2 * front * heads_kv
+    before = tokens + len(sources) * front
+    sizes = [max(start for target, start in targets if target == t) + unit for t in range(1 + max(targets)[0])]
     array = jax.ShapeDtypeStruct
     work = heads_kv * tokens * 8 * (before + tokens)
     return call(
-        functools.partial(probs_kernel, slots, heads_kv, head_size**-0.5),
+        functools.partial(probs_kernel, sources, targets, heads_kv, head_size**-0.5),
         "probs",
         (prompt_k, prompt_v, own_k, own_v, qh, gh, bias, weight, *blocks),
-        [
-            array((sent, head_size), BF16),
-            array((kept, head_size), BF16),
+        [array((size, head_size), BF16) for size in sizes]
+        + [
             array((heads_kv, before + tokens, head_size), BF16),
             array((heads_kv, before + tokens, tokens * 8), BF16),
             array((heads_kv, tokens, tokens * 8), BF16),
@@ -274,82 +278,105 @@
     return total
 
 
+def after(array, *earlier):
+    return lax.optimization_barrier((array, *earlier))[0]
+
+
 def per_device(size, queries, keys, values, grad_out, parents, lengths):
     tokens, heads_kv, head_size = keys.shape
     rows = tokens * heads_kv
-    unit = 2 * CAP * TILE * heads_kv
     one = CAP * TILE * heads_kv
-    near = size <= W + 1
-    window = min(W, size - 2) if near else W
+    unit = 2 * one
     device = lax.axis_index("node")
     even = lax.rem(device, 2) == 0
+    lower = lax.rem(device, 4) < 2
     keys = keys.reshape(rows, head_size)
     values = values.reshape(rows, head_size)
     strides = [2**i for i in range(2, size.bit_length()) if 2**i < size]
+    top = strides[-1]
     neighbours = [(i, i ^ 1) for i in range(size)]
     far_route = shift_route(4, size)[1:]
     near_route = shift_route(2, size)
+    six_route = [(1, 7)]
+    small = size == W + 1
+    if small:
+        order = [(1, 3), (2, 2), (3, 1), (4, 4), (5, 5), (6, 6)]
+        sources = [(0, rows), (1, rows), (2, 0), (3, 0), (2, unit), (4, 0)]
+        targets = [(0, rows), (1, rows), (2, 0), (1, rows + unit), (2, unit), (1, rows + 2 * unit)]
+    else:
+        order = [(k, k) for k in range(1, W + 1)]
+        sources = [(0, 0), (1, rows), (0, unit), (2, 0), (0, 2 * unit), (1, rows + unit), (0, 3 * unit)]
+        targets = [(1 - k % 2, rows + (k - 1) // 2 * unit) for k in range(1, W + 1)]
 
     def prompt_route(stride):
         return [(i + j, i + j + stride) for i in range(0, size, 2 * stride) for j in (0, 1)]
 
-    top = strides[-1]
-    prepared = prepare(window, queries, grad_out, keys, values, parents, lengths)
+    def units(array, start, count):
+        return [array[start + i * unit : start + (i + 1) * unit] for i in range(count)]
+
+    prepared = prepare(order, queries, grad_out, keys, values, parents, lengths)
+    held = lax.optimization_barrier(jnp.where(device == 0, keys, jnp.zeros_like(keys)))
+    keys_far = permuted(keys, [(0, top)])
     values_far = permuted(values, [(0, top + 1)])
-    keys_far = permuted(keys, [(0, top)])
     values_next = permuted(values, [(0, 1)])
-    head = jnp.concatenate([keys[:one], values[:one]])
+    head = after(jnp.concatenate([keys[:one], values[:one]]), keys_far)
     far = permuted(head, far_route)
-    held = jnp.where(device == 0, keys, added(values_far, keys_far, values_next).astype(BF16))
+    held = added(held, values_next, values_far, keys_far).astype(BF16)
     for stride in reversed(strides[:-1]):
         held = added(held, permuted(held, prompt_route(stride))).astype(BF16)
-    second = permuted(jnp.concatenate([held, head, far]), near_route)
-    held = jnp.where(lax.rem(device, 4) < 2, held, second[:rows])
-    two, four, six = second[rows : rows + unit], far, second[rows + unit :]
-    if near:
-        even_slots = jnp.where(even, jnp.concatenate([head, two, four]), jnp.concatenate([two, four, six]))
-        third = permuted(jnp.concatenate([held, even_slots]), neighbours)
-        other, start = third[:rows], rows
+    if small:
+        six = permuted(head, six_route)
+        held = after(held, far, six)
+        second = permuted(jnp.concatenate([held, head]), near_route)
+        crossed = jnp.where(even, jnp.concatenate([head, far]), jnp.concatenate([far, six]))
+        crossed = permuted(crossed, neighbours)
+        held = jnp.where(lower, held, second[:rows])
+        third = permuted(after(jnp.concatenate([held, second[rows:]]), crossed), neighbours)
+        other = third[:rows]
+        blocks = (third, second, crossed, far, six)
     else:
-        third = permuted(jnp.concatenate([head, two, four, six]), shift_route(1, size))
-        other, start = permuted(held, neighbours), 0
-    slots = [(0, start), (1, rows), (0, start + unit), (2, 0), (0, start + 2 * unit), (1, rows + unit), (0, start + 3 * unit)]
-    slots = slots[:window]
-
-    send, keep, kh, ds, p_own = probs(
-        slots, jnp.where(even, held, other), jnp.where(even, other, held), prepared, (third, second, far)
+        second = permuted(jnp.concatenate([held, head, far]), near_route)
+        held = jnp.where(lower, held, second[:rows])
+        third = permuted(jnp.concatenate([head, second[rows : rows + unit], far, second[rows + unit :]]), shift_route(1, size))
+        other = permuted(held, neighbours)
+        blocks = (third, second, far)
+
+    *sent, kh, ds, p_own = probs(
+        sources, targets, jnp.where(even, held, other), jnp.where(even, other, held), prepared, blocks
     )
     grad_queries, dk, dv = grads(*prepared[:2], kh, ds, p_own)
 
-    def slot(array, index):
-        return array[rows + index * unit : rows + (index + 1) * unit]
-
-    if near:
+    send, keep = sent[:2]
+    two, four, six = units(keep, rows, 3)
+    if small:
         third = permuted(send, neighbours)
-        total = added(keep[:rows], third[:rows])
-        from_third = [slot(third, i) for i in range(3)]
-        none = jnp.zeros_like(from_third[0])
-        mine = jnp.where(even, from_third[0], none)
-        two = added(slot(keep, 0), jnp.where(even, from_third[1], from_third[0]))
-        four = added(slot(keep, 1), jnp.where(even, from_third[2], from_third[1]))
-        six = added(slot(keep, 2), jnp.where(even, none, from_third[2]))
+        total = added(keep[:rows], third[:rows]).astype(BF16)
+        two = added(two, third[rows:])
+        total = after(total, dk)
+        second = permuted(after(jnp.concatenate([total, two.astype(BF16)])), back(near_route))
+        first, last = units(permuted(after(sent[2], third), neighbours), 0, 2)
+        four, six, first, last, second = lax.optimization_barrier((four, six, first, last, second))
+        none = jnp.zeros_like(first)
+        mine = added(jnp.where(even, first, none), second[rows:])
+        four = added(four, jnp.where(even, last, first))
+        six = added(six, jnp.where(even, none, last)).astype(BF16)
     else:
-        third = permuted(send[rows:], back(shift_route(1, size)))
-        total = added(keep[:rows], permuted(send[:rows], neighbours))
-        mine = third[:unit]
-        two = added(slot(keep, 0), third[unit : 2 * unit])
-        four = added(slot(keep, 1), third[2 * unit : 3 * unit])
-        six = added(slot(keep, 2), third[3 * unit :])
-    second = permuted(jnp.concatenate([total.astype(BF16), two.astype(BF16), six.astype(BF16)]), back(near_route))
-    total = added(total.astype(BF16), jnp.where(lax.rem(device, 4) < 2, second[:rows], 0)).astype(BF16)
-    mine = added(mine, slot(second, 0))
-    four = added(four, slot(second, 1)).astype(BF16)
+        zero, *third = units(permuted(send[rows:], back(shift_route(1, size))), 0, 4)
+        total = added(keep[:rows], permuted(send[:rows], neighbours)).astype(BF16)
+        two, four, six = (added(x, y).astype(BF16) for x, y in zip((two, four, six), third))
+        second = permuted(jnp.concatenate([total, two, six]), back(near_route))
+        mine = added(zero, second[rows : rows + unit])
+        four = added(four, second[rows + unit :])
+    total = added(total, jnp.where(lower, second[:rows], jnp.zeros_like(total))).astype(BF16)
     for stride in strides[:-1]:
         total = added(total, permuted(total, back(prompt_route(stride)))).astype(BF16)
+    keys_far = permuted(total, [(top, 0)])
     values_far = permuted(total, [(top + 1, 0)])
-    keys_far = permuted(total, [(top, 0)])
     values_next = permuted(total, [(1, 0)])
+    four = after(four.astype(BF16), values_next)
     mine = added(mine, permuted(four, back(far_route)))
+    if small:
+        mine = added(mine, permuted(after(six, values_next), back(six_route)))
     own = []
     for side, local, prompt in ((0, dk, added(total, keys_far)), (1, dv, added(values_far, values_next))):
         whole = local + jnp.where(device == 0, prompt, 0.0)

time: 67.6 us -> 69.4 us (1.027)
  the two profiles are of different devices: /device:TPU:0 before, /device:TPU:6 now
where the time goes in v5:
time: 69.4 us; the launch traced here: 68.8 us
  starting transfers between devices  25.5 us (37%)
  waiting for transfers between devices  24.2 us (35%)
  Pallas kernels  9.74 us (14%)
  local copies, waits for them, and re-layouts  7.91 us (11%)
  between operations  0.95 us (1%)
    ppermute x16, starting transfers between devices, permuted(): return lax.ppermute(block, 'node', route)  25.5 us
    ppermute x16, waiting for transfers between devices, permuted(): return lax.ppermute(block, 'node', route)  24.2 us
    pallas_call x3, Pallas kernels, call(): pl.pallas_call(kernel, in_specs=[SMEM] * scalars + [VMEM] * (len(operands...  9.74 us
    unnamed x16, local copies, waits for them, and re-layouts  6.34 us
    slice x2, local copies, waits for them, and re-layouts, per_device(): head = after(jnp.concatenate([keys[:one], values[:one]]), keys_far)  1.55 us
  transfers between devices with their start and end apart: 16, of which 11 were waited for; matrix products, arithmetic and copies ran while one was open for 3% of the time, Pallas kernels for 5%

profile of v5, /device:TPU:6, one launch (start us, length us, event | category | flops | bytes accessed | tf_op | source)
XLA Modules:
  0.0 68.8 jit_solution(6250910757048640245)
XLA Ops:
  0.6 0.7 collective-permute-start.1
  1.3 1.3 %collective-permute-start = (bf16[512,128]{1,0:T(8,128)(2,1)}, bf16[512,128]{1,0:T(8,128)(2,1)S(1)}, u32[]{:S(2)}, u32[]{:S(2)}) collective-permute-start(bf16[512,128]{1,0:T(8,128)(2,1)} %bitcast.10), channel_id=1, source_target_pairs={{0,2},{1,3},{16,18},{17,19}} | collective-permute-start | bytes 393224 | tf_op jit(solution)/shard_map/ppermute | solution.py:22
  2.6 0.7 collective-permute-start.2
  3.3 0.8 %slice.95 = bf16[32,4,128]{2,1,0:T(4,128)(2,1)S(1)} slice(bf16[128,4,128]{2,1,0:T(4,128)(2,1)} %param.11), slice={[0:32], [0:4], [0:128]} | slice | bytes 65536 | tf_op jit(solution)/shard_map/slice | solution.py:322
  4.1 0.8 %slice.97 = bf16[32,4,128]{2,1,0:T(4,128)(2,1)S(1)} slice(bf16[128,4,128]{2,1,0:T(4,128)(2,1)} %param.12), slice={[0:32], [0:4], [0:128]} | slice | bytes 65536 | tf_op jit(solution)/shard_map/slice | solution.py:322
  4.9 0.0 collective-permute-done.2
  4.9 4.9 %collective-permute-start.4 = (bf16[256,128]{1,0:T(8,128)(2,1)S(1)}, bf16[256,128]{1,0:T(8,128)(2,1)S(1)}, u32[]{:S(2)}, u32[]{:S(2)}) collective-permute-start(bf16[256,128]{1,0:T(8,128)(2,1)S(1)} %pad_maximum_fusion.3), channel_id=1, source_target_pairs={{2,14},{3,15},{18,30},{19,31}} | collective-permute-start | bytes 196616 | tf_op jit(solution)/shard_map/ppermute | solution.py:22
  9.8 1.3 %collective-permute-start.3 = (bf16[256,128]{1,0:T(8,128)(2,1)S(1)}, bf16[256,128]{1,0:T(8,128)(2,1)S(1)}, u32[]{:S(2)}, u32[]{:S(2)}) collective-permute-start(bf16[256,128]{1,0:T(8,128)(2,1)S(1)} %pad_maximum_fusion.3), channel_id=1, source_target_pairs={{2,10},{4,12},{6,14},{3,11},{5,13},{7,15},{18,26},{20,28},{22,30},... | collective-permute-start | bytes 196616 | tf_op jit(solution)/shard_map/ppermute | solution.py:22
  11.1 0.0 collective-permute-done.1
  11.1 0.2 collective-permute-done
  11.3 0.1 add_convert_fusion.2
  11.4 0.7 %collective-permute-done.4.refs_12_ = bf16[256,128]{1,0:T(8,128)(2,1)S(1)} collective-permute-done((bf16[256,128]{1,0:T(8,128)(2,1)S(1)}, bf16[256,128]{1,0:T(8,128)(2,1)S(1)}, u32[]{:S(2)}, u32[]{:S(2)}) %collective-permute-start.4) | collective-permute-done | bytes 65568 | tf_op jit(solution)/shard_map/ppermute | solution.py:22
  12.1 0.9 %collective-permute-done.3.refs_11_ = bf16[256,128]{1,0:T(8,128)(2,1)S(1)} collective-permute-done((bf16[256,128]{1,0:T(8,128)(2,1)S(1)}, bf16[256,128]{1,0:T(8,128)(2,1)S(1)}, u32[]{:S(2)}, u32[]{:S(2)}) %collective-permute-start.3) | collective-permute-done | bytes 65568 | tf_op jit(solution)/shard_map/ppermute | solution.py:22
  13.0 4.3 %collective-permute-start.5 = (bf16[768,128]{1,0:T(8,128)(2,1)S(1)}, bf16[768,128]{1,0:T(8,128)(2,1)S(1)}, u32[]{:S(2)}, u32[]{:S(2)}) collective-permute-start(bf16[768,128]{1,0:T(8,128)(2,1)S(1)} %pad_maximum_fusion), channel_id=1, source_target_pairs={{0,4},{2,6},{4,8},{6,10},{8,12},{10,14},{1,5},{3,7},{5,9},{7,11},{... | collective-permute-start | bytes 589832 | tf_op jit(solution)/shard_map/ppermute | solution.py:22
  17.4 0.1 collective-permute-start.6
  17.5 3.7 %collective-permute-done.5.refs_9_ = bf16[768,128]{1,0:T(8,128)(2,1)S(1)} collective-permute-done((bf16[768,128]{1,0:T(8,128)(2,1)S(1)}, bf16[768,128]{1,0:T(8,128)(2,1)S(1)}, u32[]{:S(2)}, u32[]{:S(2)}) %collective-permute-start.5) | collective-permute-done | bytes 196640 | tf_op jit(solution)/shard_map/ppermute | solution.py:22
  21.2 1.2 %collective-permute-done.6.refs_10_ = bf16[512,128]{1,0:T(8,128)(2,1)S(1)} collective-permute-done((bf16[512,128]{1,0:T(8,128)(2,1)S(1)}, bf16[512,128]{1,0:T(8,128)(2,1)S(1)}, u32[]{:S(2)}, u32[]{:S(2)}) %collective-permute-start.6) | collective-permute-done | bytes 131104 | tf_op jit(solution)/shard_map/ppermute | solution.py:22
  22.4 0.0 collective-permute-start.7
  22.4 1.2 %copy-done = bf16[128,32,128]{2,1,0:T(8,128)(2,1)S(1)} copy-done((bf16[128,32,128]{2,1,0:T(8,128)(2,1)S(1)}, bf16[128,32,128]{2,1,0:T(8,128)(2,1)}, u32[]{:S(2)}) %copy-start) | copy-done | bytes 1048600
  23.7 1.2 %copy-done.1 = bf16[128,32,128]{2,1,0:T(8,128)(2,1)S(1)} copy-done((bf16[128,32,128]{2,1,0:T(8,128)(2,1)S(1)}, bf16[128,32,128]{2,1,0:T(8,128)(2,1)}, u32[]{:S(2)}) %copy-start.1) | copy-done | bytes 1048600
  24.9 0.9 %copy-done.2 = bf16[128,4,128]{2,1,0:T(4,128)(2,1)S(1)} copy-done((bf16[128,4,128]{2,1,0:T(4,128)(2,1)S(1)}, bf16[128,4,128]{2,1,0:T(4,128)(2,1)}, u32[]{:S(2)}) %copy-start.2) | copy-done | bytes 131096
  25.8 0.9 %copy-done.3 = bf16[128,4,128]{2,1,0:T(4,128)(2,1)S(1)} copy-done((bf16[128,4,128]{2,1,0:T(4,128)(2,1)S(1)}, bf16[128,4,128]{2,1,0:T(4,128)(2,1)}, u32[]{:S(2)}) %copy-start.3) | copy-done | bytes 131096
  26.7 0.7 copy-done.4
  27.3 0.7 copy-done.5
  28.0 1.1 %prepare.1 = (bf16[4,1024,128]{2,1,0:T(8,128)(2,1)S(1)}, bf16[4,1024,128]{2,1,0:T(8,128)(2,1)S(1)}, bf16[4,128,128]{2,1,0:T(8,128)(2,1)S(1)}, bf16[4,128,128]{2,...) custom-call(s32[64]{0:T(128)S(1)} %copy-done.4, s32[64]{0:T(128)S(1)} %copy-done.5, ...), custom_call_target="tpu_custom_call" | custom-call | flops 1048576 | bytes 4981248 | tf_op jit(solution)/shard_map/prepare/pallas_call | solution.py:187
  29.1 0.0 collective-permute-done.7.refs_8_
  29.1 6.2 %probs.1 = (bf16[768,128]{1,0:T(8,128)(2,1)S(1)}, bf16[1280,128]{1,0:T(8,128)(2,1)S(1)}, bf16[512,128]{1,0:T(8,128)(2,1)S(1)}, bf16[4,448,128]{2,1,0:T(8,128)(2,...) custom-call(bf16[512,128]{1,0:T(8,128)(2,1)S(1)} %get-tuple-element.84.refs_0_, ...), custom_call_target="tpu_custom_call" | custom-call | flops 1879048192 | bytes 9371648 | tf_op jit(solution)/shard_map/probs/pallas_call | solution.py:187
  35.4 2.1 %collective-permute-start.8 = (bf16[768,128]{1,0:T(8,128)(2,1)S(1)}, bf16[768,128]{1,0:T(8,128)(2,1)S(1)}, u32[]{:S(2)}, u32[]{:S(2)}) collective-permute-start(bf16[768,128]{1,0:T(8,128)(2,1)S(1)} %get-tuple-element.69), channel_id=1, source_target_pairs={{0,2},{2,0},{4,6},{6,4},{8,10},{10,8},{12,14},{14,12},{1,3},{3,1},... | collective-permute-start | bytes 589832 | tf_op jit(solution)/shard_map/ppermute | solution.py:22
  37.4 2.4 %grads.1 = (bf16[128,32,128]{2,1,0:T(8,128)(2,1)}, f32[512,128]{1,0:T(8,128)S(1)}, f32[512,128]{1,0:T(8,128)S(1)}) custom-call(bf16[4,1024,128]{2,1,0:T(8,128)(2,1)S(1)} %get-tuple-element.54.refs_4_.refs_0_, bf16[4,1024,128]{2,1,0:T(8,128)(2,1)S(1)} %get-tuple-element.55.refs_5_.refs_1_, bf16[4,448,128]{2,1,0:T(8,128)(2,1)S(1)} %get-tuple-element.63.refs_2_, ...), custom_call_target="tpu_custom_call" | custom-call | flops 939524096 | bytes 8847360 | tf_op jit(solution)/shard_map/grads/pallas_call | solution.py:187
  39.9 1.6 %collective-permute-done.8 = bf16[768,128]{1,0:T(8,128)(2,1)S(1)} collective-permute-done((bf16[768,128]{1,0:T(8,128)(2,1)S(1)}, bf16[768,128]{1,0:T(8,128)(2,1)S(1)}, u32[]{:S(2)}, u32[]{:S(2)}) %collective-permute-start.8) | collective-permute-done | bytes 196640 | tf_op jit(solution)/shard_map/ppermute | solution.py:22
  41.5 2.3 %collective-permute-start.9 = (bf16[512,128]{1,0:T(8,128)(2,1)S(1)}, bf16[512,128]{1,0:T(8,128)(2,1)S(1)}, u32[]{:S(2)}, u32[]{:S(2)}) collective-permute-start(bf16[512,128]{1,0:T(8,128)(2,1)S(1)} %get-tuple-element.72), channel_id=1, source_target_pairs={{0,2},{2,0},{4,6},{6,4},{8,10},{10,8},{12,14},{14,12},{1,3},{3,1},... | collective-permute-start | bytes 393224 | tf_op jit(solution)/shard_map/ppermute | solution.py:22
  43.9 1.3 %collective-permute-start.10 = (bf16[768,128]{1,0:T(8,128)(2,1)S(1)}, bf16[768,128]{1,0:T(8,128)(2,1)S(1)}, u32[]{:S(2)}, u32[]{:S(2)}) collective-permute-start(bf16[768,128]{1,0:T(8,128)(2,1)S(1)} %pad_maximum_fusion.2), channel_id=1, source_target_pairs={{4,0},{6,2},{8,4},{10,6},{12,8},{14,10},{5,1},{7,3},{9,5},{11,7},{... | collective-permute-start | bytes 589832 | tf_op jit(solution)/shard_map/ppermute | solution.py:22
  45.2 1.6 %collective-permute-done.9 = bf16[512,128]{1,0:T(8,128)(2,1)S(1)} collective-permute-done((bf16[512,128]{1,0:T(8,128)(2,1)S(1)}, bf16[512,128]{1,0:T(8,128)(2,1)S(1)}, u32[]{:S(2)}, u32[]{:S(2)}) %collective-permute-start.9) | collective-permute-done | bytes 131104 | tf_op jit(solution)/shard_map/ppermute | solution.py:22
  46.8 4.7 %collective-permute-done.10 = bf16[768,128]{1,0:T(8,128)(2,1)S(1)} collective-permute-done((bf16[768,128]{1,0:T(8,128)(2,1)S(1)}, bf16[768,128]{1,0:T(8,128)(2,1)S(1)}, u32[]{:S(2)}, u32[]{:S(2)}) %collective-permute-start.10) | collective-permute-done | bytes 196640 | tf_op jit(solution)/shard_map/ppermute | solution.py:22
  51.5 0.7 collective-permute-start.15
  52.2 2.7 %collective-permute-start.12 = (bf16[512,128]{1,0:T(8,128)(2,1)S(1)}, bf16[512,128]{1,0:T(8,128)(2,1)S(1)}, u32[]{:S(2)}, u32[]{:S(2)}) collective-permute-start(bf16[512,128]{1,0:T(8,128)(2,1)S(1)} %add_convert_fusion), channel_id=1, source_target_pairs={{2,0},{3,1},{18,16},{19,17}} | collective-permute-start | bytes 393224 | tf_op jit(solution)/shard_map/ppermute | solution.py:22
  54.9 0.7 collective-permute-start.11
  55.6 3.1 %collective-permute-done.12 = bf16[512,128]{1,0:T(8,128)(2,1)S(1)} collective-permute-done((bf16[512,128]{1,0:T(8,128)(2,1)S(1)}, bf16[512,128]{1,0:T(8,128)(2,1)S(1)}, u32[]{:S(2)}, u32[]{:S(2)}) %collective-permute-start.12) | collective-permute-done | bytes 131104 | tf_op jit(solution)/shard_map/ppermute | solution.py:22
  58.7 1.3 %collective-permute-start.13 = (bf16[256,128]{1,0:T(8,128)(2,1)S(1)}, bf16[256,128]{1,0:T(8,128)(2,1)S(1)}, u32[]{:S(2)}, u32[]{:S(2)}) collective-permute-start(bf16[256,128]{1,0:T(8,128)(2,1)S(1)} %get-tuple-element.77), channel_id=1, source_target_pairs={{10,2},{12,4},{14,6},{11,3},{13,5},{15,7},{26,18},{28,20},{30,22},... | collective-permute-start | bytes 196616 | tf_op jit(solution)/shard_map/ppermute | solution.py:22
  60.0 1.3 %collective-permute-start.14 = (bf16[256,128]{1,0:T(8,128)(2,1)S(1)}, bf16[256,128]{1,0:T(8,128)(2,1)S(1)}, u32[]{:S(2)}, u32[]{:S(2)}) collective-permute-start(bf16[256,128]{1,0:T(8,128)(2,1)S(1)} %get-tuple-element.79), channel_id=1, source_target_pairs={{14,2},{15,3},{30,18},{31,19}} | collective-permute-start | bytes 196616 | tf_op jit(solution)/shard_map/ppermute | solution.py:22
  61.3 0.0 collective-permute-done.11
  61.3 0.1 select_add_fusion.1
  61.5 4.3 %collective-permute-done.13 = bf16[256,128]{1,0:T(8,128)(2,1)S(1)} collective-permute-done((bf16[256,128]{1,0:T(8,128)(2,1)S(1)}, bf16[256,128]{1,0:T(8,128)(2,1)S(1)}, u32[]{:S(2)}, u32[]{:S(2)}) %collective-permute-start.13) | collective-permute-done | bytes 65568 | tf_op jit(solution)/shard_map/ppermute | solution.py:22
  65.8 2.2 %collective-permute-done.14 = bf16[256,128]{1,0:T(8,128)(2,1)S(1)} collective-permute-done((bf16[256,128]{1,0:T(8,128)(2,1)S(1)}, bf16[256,128]{1,0:T(8,128)(2,1)S(1)}, u32[]{:S(2)}, u32[]{:S(2)}) %collective-permute-start.14) | collective-permute-done | bytes 65568 | tf_op jit(solution)/shard_map/ppermute | solution.py:22
  68.1 0.0 copy-start.6
  68.1 0.0 copy-start.7
  68.1 0.7 copy-done.6
  68.8 0.1 copy-done.7
  (25 shorter events, 0.5 us)
Async XLA Ops:
  0.6 10.5 %collective-permute-start.1 = (bf16[512,128]{1,0:T(8,128)(2,1)}, bf16[512,128]{1,0:T(8,128)(2,1)S(1)}, u32[]{:S(2)}, u32[]{:S(2)}) collective-permute-start(bf16[512,128]{1,0:T(8,128)(2,1)} %bitcast.9), channel_id=1, source_target_pairs={{0,10},{1,11},{16,26},{17,27}} | collective-permute-start | bytes 393224 | tf_op jit(solution)/shard_map/ppermute | solution.py:22
  1.3 10.0 %collective-permute-start = (bf16[512,128]{1,0:T(8,128)(2,1)}, bf16[512,128]{1,0:T(8,128)(2,1)S(1)}, u32[]{:S(2)}, u32[]{:S(2)}) collective-permute-start(bf16[512,128]{1,0:T(8,128)(2,1)} %bitcast.10), channel_id=1, source_target_pairs={{0,2},{1,3},{16,18},{17,19}} | collective-permute-start | bytes 393224 | tf_op jit(solution)/shard_map/ppermute | solution.py:22
  2.6 2.3 %collective-permute-start.2 = (bf16[512,128]{1,0:T(8,128)(2,1)}, bf16[512,128]{1,0:T(8,128)(2,1)S(1)}, u32[]{:S(2)}, u32[]{:S(2)}) collective-permute-start(bf16[512,128]{1,0:T(8,128)(2,1)} %bitcast.6), channel_id=1, source_target_pairs={{0,8},{1,9},{16,24},{17,25}} | collective-permute-start | bytes 393224 | tf_op jit(solution)/shard_map/ppermute | solution.py:22
  4.9 7.2 %collective-permute-start.4 = (bf16[256,128]{1,0:T(8,128)(2,1)S(1)}, bf16[256,128]{1,0:T(8,128)(2,1)S(1)}, u32[]{:S(2)}, u32[]{:S(2)}) collective-permute-start(bf16[256,128]{1,0:T(8,128)(2,1)S(1)} %pad_maximum_fusion.3), channel_id=1, source_target_pairs={{2,14},{3,15},{18,30},{19,31}} | collective-permute-start | bytes 196616 | tf_op jit(solution)/shard_map/ppermute | solution.py:22
  9.8 3.2 %collective-permute-start.3 = (bf16[256,128]{1,0:T(8,128)(2,1)S(1)}, bf16[256,128]{1,0:T(8,128)(2,1)S(1)}, u32[]{:S(2)}, u32[]{:S(2)}) collective-permute-start(bf16[256,128]{1,0:T(8,128)(2,1)S(1)} %pad_maximum_fusion.3), channel_id=1, source_target_pairs={{2,10},{4,12},{6,14},{3,11},{5,13},{7,15},{18,26},{20,28},{22,30},... | collective-permute-start | bytes 196616 | tf_op jit(solution)/shard_map/ppermute | solution.py:22
  13.0 8.2 %collective-permute-start.5 = (bf16[768,128]{1,0:T(8,128)(2,1)S(1)}, bf16[768,128]{1,0:T(8,128)(2,1)S(1)}, u32[]{:S(2)}, u32[]{:S(2)}) collective-permute-start(bf16[768,128]{1,0:T(8,128)(2,1)S(1)} %pad_maximum_fusion), channel_id=1, source_target_pairs={{0,4},{2,6},{4,8},{6,10},{8,12},{10,14},{1,5},{3,7},{5,9},{7,11},{... | collective-permute-start | bytes 589832 | tf_op jit(solution)/shard_map/ppermute | solution.py:22
  17.4 5.0 %collective-permute-start.6 = (bf16[512,128]{1,0:T(8,128)(2,1)S(1)}, bf16[512,128]{1,0:T(8,128)(2,1)S(1)}, u32[]{:S(2)}, u32[]{:S(2)}) collective-permute-start(bf16[512,128]{1,0:T(8,128)(2,1)S(1)} %maximum_select_fusion), channel_id=1, source_target_pairs={{0,2},{2,0},{4,6},{6,4},{8,10},{10,8},{12,14},{14,12},{1,3},{3,1},... | collective-permute-start | bytes 393224 | tf_op jit(solution)/shard_map/ppermute | solution.py:22
  22.4 6.7 %collective-permute-start.7 = (bf16[768,128]{1,0:T(8,128)(2,1)S(1)}, bf16[768,128]{1,0:T(8,128)(2,1)S(1)}, u32[]{:S(2)}, u32[]{:S(2)}) collective-permute-start(bf16[768,128]{1,0:T(8,128)(2,1)S(1)} %pad_maximum_fusion.1), channel_id=1, source_target_pairs={{0,2},{2,0},{4,6},{6,4},{8,10},{10,8},{12,14},{14,12},{1,3},{3,1},... | collective-permute-start | bytes 589832 | tf_op jit(solution)/shard_map/ppermute | solution.py:22
  22.4 1.2 %copy-start = (bf16[128,32,128]{2,1,0:T(8,128)(2,1)S(1)}, bf16[128,32,128]{2,1,0:T(8,128)(2,1)}, u32[]{:S(2)}) copy-start(bf16[128,32,128]{2,1,0:T(8,128)(2,1)} %refs_4_.1) | copy-start | bytes 3145732
  23.6 1.2 %copy-start.1 = (bf16[128,32,128]{2,1,0:T(8,128)(2,1)S(1)}, bf16[128,32,128]{2,1,0:T(8,128)(2,1)}, u32[]{:S(2)}) copy-start(bf16[128,32,128]{2,1,0:T(8,128)(2,1)} %refs_5_.1) | copy-start | bytes 3145732
  24.9 0.9 %copy-start.2 = (bf16[128,4,128]{2,1,0:T(4,128)(2,1)S(1)}, bf16[128,4,128]{2,1,0:T(4,128)(2,1)}, u32[]{:S(2)}) copy-start(bf16[128,4,128]{2,1,0:T(4,128)(2,1)} %param.11) | copy-start | bytes 393220
  25.8 0.9 %copy-start.3 = (bf16[128,4,128]{2,1,0:T(4,128)(2,1)S(1)}, bf16[128,4,128]{2,1,0:T(4,128)(2,1)}, u32[]{:S(2)}) copy-start(bf16[128,4,128]{2,1,0:T(4,128)(2,1)} %param.12) | copy-start | bytes 393220
  26.7 0.7 copy-start.4
  27.3 0.7 copy-start.5
  35.4 6.1 %collective-permute-start.8 = (bf16[768,128]{1,0:T(8,128)(2,1)S(1)}, bf16[768,128]{1,0:T(8,128)(2,1)S(1)}, u32[]{:S(2)}, u32[]{:S(2)}) collective-permute-start(bf16[768,128]{1,0:T(8,128)(2,1)S(1)} %get-tuple-element.69), channel_id=1, source_target_pairs={{0,2},{2,0},{4,6},{6,4},{8,10},{10,8},{12,14},{14,12},{1,3},{3,1},... | collective-permute-start | bytes 589832 | tf_op jit(solution)/shard_map/ppermute | solution.py:22
  41.5 5.3 %collective-permute-start.9 = (bf16[512,128]{1,0:T(8,128)(2,1)S(1)}, bf16[512,128]{1,0:T(8,128)(2,1)S(1)}, u32[]{:S(2)}, u32[]{:S(2)}) collective-permute-start(bf16[512,128]{1,0:T(8,128)(2,1)S(1)} %get-tuple-element.72), channel_id=1, source_target_pairs={{0,2},{2,0},{4,6},{6,4},{8,10},{10,8},{12,14},{14,12},{1,3},{3,1},... | collective-permute-start | bytes 393224 | tf_op jit(solution)/shard_map/ppermute | solution.py:22
  43.9 7.6 %collective-permute-start.10 = (bf16[768,128]{1,0:T(8,128)(2,1)S(1)}, bf16[768,128]{1,0:T(8,128)(2,1)S(1)}, u32[]{:S(2)}, u32[]{:S(2)}) collective-permute-start(bf16[768,128]{1,0:T(8,128)(2,1)S(1)} %pad_maximum_fusion.2), channel_id=1, source_target_pairs={{4,0},{6,2},{8,4},{10,6},{12,8},{14,10},{5,1},{7,3},{9,5},{11,7},{... | collective-permute-start | bytes 589832 | tf_op jit(solution)/shard_map/ppermute | solution.py:22
  51.5 9.9 %collective-permute-start.15 = (bf16[512,128]{1,0:T(8,128)(2,1)S(1)}, bf16[512,128]{1,0:T(8,128)(2,1)S(1)}, u32[]{:S(2)}, u32[]{:S(2)}) collective-permute-start(bf16[512,128]{1,0:T(8,128)(2,1)S(1)} %add_convert_fusion), channel_id=1, source_target_pairs={{10,0},{11,1},{26,16},{27,17}} | collective-permute-start | bytes 393224 | tf_op jit(solution)/shard_map/ppermute | solution.py:22
  52.2 6.5 %collective-permute-start.12 = (bf16[512,128]{1,0:T(8,128)(2,1)S(1)}, bf16[512,128]{1,0:T(8,128)(2,1)S(1)}, u32[]{:S(2)}, u32[]{:S(2)}) collective-permute-start(bf16[512,128]{1,0:T(8,128)(2,1)S(1)} %add_convert_fusion), channel_id=1, source_target_pairs={{2,0},{3,1},{18,16},{19,17}} | collective-permute-start | bytes 393224 | tf_op jit(solution)/shard_map/ppermute | solution.py:22
  54.9 6.5 %collective-permute-start.11 = (bf16[512,128]{1,0:T(8,128)(2,1)S(1)}, bf16[512,128]{1,0:T(8,128)(2,1)S(1)}, u32[]{:S(2)}, u32[]{:S(2)}) collective-permute-start(bf16[512,128]{1,0:T(8,128)(2,1)S(1)} %add_convert_fusion), channel_id=1, source_target_pairs={{8,0},{9,1},{24,16},{25,17}} | collective-permute-start | bytes 393224 | tf_op jit(solution)/shard_map/ppermute | solution.py:22
  58.7 7.0 %collective-permute-start.13 = (bf16[256,128]{1,0:T(8,128)(2,1)S(1)}, bf16[256,128]{1,0:T(8,128)(2,1)S(1)}, u32[]{:S(2)}, u32[]{:S(2)}) collective-permute-start(bf16[256,128]{1,0:T(8,128)(2,1)S(1)} %get-tuple-element.77), channel_id=1, source_target_pairs={{10,2},{12,4},{14,6},{11,3},{13,5},{15,7},{26,18},{28,20},{30,22},... | collective-permute-start | bytes 196616 | tf_op jit(solution)/shard_map/ppermute | solution.py:22
  60.0 8.0 %collective-permute-start.14 = (bf16[256,128]{1,0:T(8,128)(2,1)S(1)}, bf16[256,128]{1,0:T(8,128)(2,1)S(1)}, u32[]{:S(2)}, u32[]{:S(2)}) collective-permute-start(bf16[256,128]{1,0:T(8,128)(2,1)S(1)} %get-tuple-element.79), channel_id=1, source_target_pairs={{14,2},{15,3},{30,18},{31,19}} | collective-permute-start | bytes 196616 | tf_op jit(solution)/shard_map/ppermute | solution.py:22
  68.1 0.7 %copy-start.6 = (f32[512,128]{1,0:T(8,128)}, f32[512,128]{1,0:T(8,128)S(1)}, u32[]{:S(2)}) copy-start(f32[512,128]{1,0:T(8,128)S(1)} %get-tuple-element.86) | copy-start | bytes 786436
  68.1 0.8 %copy-start.7 = (f32[512,128]{1,0:T(8,128)}, f32[512,128]{1,0:T(8,128)S(1)}, u32[]{:S(2)}) copy-start(f32[512,128]{1,0:T(8,128)S(1)} %get-tuple-element.85) | copy-start | bytes 786436

commit v6 on v5

--- a/solution.py
+++ b/solution.py
@@ -54,15 +54,21 @@
     return wide[: count * heads_kv]
 
 
-def prepare_kernel(order, heads_kv, *refs):
-    parents, lengths, keys, values, q_ref, g_ref, qh, gh, own_k, own_v, bias, weight, wide = refs
+def load_kernel(order, heads_kv, *refs):
+    sources, outs, scratch = refs[:4], refs[4:10], refs[10:]
+    head, held, own_k, own_v, bias, weight = outs
+    parents, lengths, keys, values, wide, arrived = scratch
+    copies = [pltpu.make_async_copy(a, b, arrived.at[i]) for i, (a, b) in enumerate(zip(sources, scratch))]
+    for copy in copies:
+        copy.start()
     tokens = TD * TILE
+    front = CAP * TILE * heads_kv
     device = lax.axis_index("node")
-    for pair in range(heads_kv // 2):
-        for ref, out in ((q_ref, qh), (g_ref, gh)):
-            both = ref[:, pair * 16 : (pair + 1) * 16].astype(F32)
-            for part in range(2):
-                out[2 * pair + part] = both[:, part * 8 : (part + 1) * 8].reshape(tokens * 8, 128).astype(BF16)
+    for copy in copies:
+        copy.wait()
+    head[:front] = keys[:front]
+    head[front:] = values[:front]
+    held[...] = jnp.where(device == 0, keys[...], jnp.zeros_like(keys))
     split_heads(keys[...], own_k, 0, tokens, heads_kv, wide)
     split_heads(values[...], own_v, 0, tokens, heads_kv, wide)
     place = lax.broadcasted_iota(jnp.int32, (TILE, 128), 0)
@@ -76,6 +82,22 @@
     lane_place = lax.broadcasted_iota(jnp.int32, (8, 128), 1) // 8
     for t in range(TD):
         weight[:, t * 128 : (t + 1) * 128] = jnp.where(lane_place < lengths[device * TD + t], 1.0, 0.0)
+
+
+def pack_kernel(heads_kv, q_ref, g_ref, qh, gh, blocks, arrived):
+    tokens = TD * TILE
+    copies = []
+    for pair in range(heads_kv // 2):
+        for ref, out in ((q_ref, qh), (g_ref, gh)):
+            i = len(copies)
+            copy = pltpu.make_async_copy(ref.at[:, pair * 16 : (pair + 1) * 16], blocks.at[i], arrived.at[i])
+            copy.start()
+            copies.append((copy, out, pair))
+    for i, (copy, out, pair) in enumerate(copies):
+        copy.wait()
+        both = blocks[i].astype(F32)
+        for part in range(2):
+            out[2 * pair + part] = both[:, part * 8 : (part + 1) * 8].reshape(tokens * 8, 128).astype(BF16)
 
 
 def probs_kernel(sources, targets, heads_kv, scale, *refs):
@@ -179,14 +201,18 @@
 
 
 VMEM = pl.BlockSpec(memory_space=pltpu.VMEM)
-SMEM = pl.BlockSpec(memory_space=pltpu.SMEM)
-
-
-def call(kernel, name, operands, outputs, scratch, flops, transcendentals=0, scalars=0):
+
+
+HBM = pl.BlockSpec(memory_space=pltpu.HBM)
+
+
+def call(kernel, name, operands, outputs, scratch, flops, transcendentals=0, place=VMEM):
     sizes = [a.size * a.dtype.itemsize for a in (*operands, *outputs)]
+    if place is HBM:
+        operands = [pltpu.with_memory_space_constraint(a, pltpu.HBM) for a in operands]
     return pl.pallas_call(
         kernel,
-        in_specs=[SMEM] * scalars + [VMEM] * (len(operands) - scalars),
+        in_specs=[place] * len(operands),
         out_specs=[VMEM] * len(outputs),
         out_shape=outputs,
         scratch_shapes=scratch,
@@ -196,26 +222,41 @@
     )(*operands)
 
 
-def prepare(order, queries, grad_out, keys, values, parents, lengths):
-    tokens, heads_q, head_size = queries.shape
-    rows = keys.shape[0]
+def load(order, keys, values, parents, lengths, tokens):
+    rows, head_size = keys.shape
     heads_kv = rows // tokens
     array = jax.ShapeDtypeStruct
     return call(
-        functools.partial(prepare_kernel, order, heads_kv),
-        "prepare",
-        (parents, lengths, keys, values, queries, grad_out),
-        [array((heads_kv, tokens * 8, head_size), BF16)] * 2
+        functools.partial(load_kernel, order, heads_kv),
+        "load",
+        (parents, lengths, keys, values),
+        [array((2 * CAP * TILE * heads_kv, head_size), BF16), array((rows, head_size), BF16)]
         + [array((heads_kv, tokens, head_size), BF16)] * 2
         + [array((2 * tokens + len(order) * CAP * TILE, 128), F32), array((8, tokens * 8), F32)],
-        [pltpu.VMEM((rows, head_size), F32)],
+        [pltpu.SMEM(parents.shape, jnp.int32), pltpu.SMEM(lengths.shape, jnp.int32)]
+        + [pltpu.VMEM((rows, head_size), BF16)] * 2
+        + [pltpu.VMEM((rows, head_size), F32), pltpu.SemaphoreType.DMA((4,))],
         flops=1 << 20,
-        scalars=2,
-    )
-
-
-def probs(sources, targets, prompt_k, prompt_v, prepared, blocks):
-    qh, gh, own_k, own_v, bias, weight = prepared
+        place=HBM,
+    )
+
+
+def pack(queries, grad_out, heads_kv):
+    tokens, heads_q, head_size = queries.shape
+    array = jax.ShapeDtypeStruct
+    return call(
+        functools.partial(pack_kernel, heads_kv),
+        "pack",
+        (queries, grad_out),
+        [array((heads_kv, tokens * 8, head_size), BF16)] * 2,
+        [pltpu.VMEM((heads_kv, tokens, 16, head_size), BF16), pltpu.SemaphoreType.DMA((heads_kv,))],
+        flops=1 << 20,
+        place=HBM,
+    )
+
+
+def probs(sources, targets, prompt_k, prompt_v, qh, gh, own, blocks):
+    own_k, own_v, bias, weight = own
     heads_kv, tokens, head_size = own_k.shape
     rows = tokens * heads_kv
     front = CAP * TILE
@@ -302,7 +343,7 @@
     if small:
         order = [(1, 3), (2, 2), (3, 1), (4, 4), (5, 5), (6, 6)]
         sources = [(0, rows), (1, rows), (2, 0), (3, 0), (2, unit), (4, 0)]
-        targets = [(0, rows), (1, rows), (2, 0), (1, rows + unit), (2, unit), (1, rows + 2 * unit)]
+        targets = [(k % 2, rows + k // 2 * unit) for k in range(6)]
     else:
         order = [(k, k) for k in range(1, W + 1)]
         sources = [(0, 0), (1, rows), (0, unit), (2, 0), (0, 2 * unit), (1, rows + unit), (0, 3 * unit)]
@@ -314,19 +355,19 @@
     def units(array, start, count):
         return [array[start + i * unit : start + (i + 1) * unit] for i in range(count)]
 
-    prepared = prepare(order, queries, grad_out, keys, values, parents, lengths)
-    held = lax.optimization_barrier(jnp.where(device == 0, keys, jnp.zeros_like(keys)))
+    head, held, *own = load(order, keys, values, parents, lengths, tokens)
+    qh, gh = pack(queries, grad_out, heads_kv)
     keys_far = permuted(keys, [(0, top)])
     values_far = permuted(values, [(0, top + 1)])
     values_next = permuted(values, [(0, 1)])
-    head = after(jnp.concatenate([keys[:one], values[:one]]), keys_far)
+    head = after(head, keys_far)
     far = permuted(head, far_route)
     held = added(held, values_next, values_far, keys_far).astype(BF16)
     for stride in reversed(strides[:-1]):
         held = added(held, permuted(held, prompt_route(stride))).astype(BF16)
     if small:
         six = permuted(head, six_route)
-        held = after(held, far, six)
+        held = after(held, far, six, qh)
         second = permuted(jnp.concatenate([held, head]), near_route)
         crossed = jnp.where(even, jnp.concatenate([head, far]), jnp.concatenate([far, six]))
         crossed = permuted(crossed, neighbours)
@@ -342,24 +383,21 @@
         blocks = (third, second, far)
 
     *sent, kh, ds, p_own = probs(
-        sources, targets, jnp.where(even, held, other), jnp.where(even, other, held), prepared, blocks
-    )
-    grad_queries, dk, dv = grads(*prepared[:2], kh, ds, p_own)
+        sources, targets, jnp.where(even, held, other), jnp.where(even, other, held), qh, gh, own, blocks
+    )
+    grad_queries, dk, dv = grads(qh, gh, kh, ds, p_own)
 
     send, keep = sent[:2]
     two, four, six = units(keep, rows, 3)
     if small:
         third = permuted(send, neighbours)
-        total = added(keep[:rows], third[:rows]).astype(BF16)
-        two = added(two, third[rows:])
-        total = after(total, dk)
-        second = permuted(after(jnp.concatenate([total, two.astype(BF16)])), back(near_route))
-        first, last = units(permuted(after(sent[2], third), neighbours), 0, 2)
-        four, six, first, last, second = lax.optimization_barrier((four, six, first, last, second))
+        total = after(added(keep[:rows], third[:rows]).astype(BF16), dk)
+        near, first, last = units(third, rows, 3)
         none = jnp.zeros_like(first)
-        mine = added(jnp.where(even, first, none), second[rows:])
+        second = permuted(jnp.concatenate([total, added(two, near).astype(BF16)]), back(near_route))
         four = added(four, jnp.where(even, last, first))
-        six = added(six, jnp.where(even, none, last)).astype(BF16)
+        six = permuted(added(six, jnp.where(even, none, last)).astype(BF16), back(six_route))
+        mine = added(jnp.where(even, first, none), second[rows:], six)
     else:
         zero, *third = units(permuted(send[rows:], back(shift_route(1, size))), 0, 4)
         total = added(keep[:rows], permuted(send[:rows], neighbours)).astype(BF16)
@@ -367,16 +405,16 @@
         second = permuted(jnp.concatenate([total, two, six]), back(near_route))
         mine = added(zero, second[rows : rows + unit])
         four = added(four, second[rows + unit :])
+    four = permuted(four.astype(BF16), back(far_route))
+    mine = added(mine, four)
     total = added(total, jnp.where(lower, second[:rows], jnp.zeros_like(total))).astype(BF16)
+    if small:
+        total = after(total, four, six)
     for stride in strides[:-1]:
         total = added(total, permuted(total, back(prompt_route(stride)))).astype(BF16)
     keys_far = permuted(total, [(top, 0)])
     values_far = permuted(total, [(top + 1, 0)])
     values_next = permuted(total, [(1, 0)])
-    four = after(four.astype(BF16), values_next)
-    mine = added(mine, permuted(four, back(far_route)))
-    if small:
-        mine = added(mine, permuted(after(six, values_next), back(six_route)))
     own = []
     for side, local, prompt in ((0, dk, added(total, keys_far)), (1, dv, added(values_far, values_next))):
         whole = local + jnp.where(device == 0, prompt, 0.0)

time: 69.4 us -> 63.7 us (0.918)
  the two profiles are of different devices: /device:TPU:6 before, /device:TPU:0 now
where the time goes in v6:
time: 63.7 us; the launch traced here: 63.4 us
  starting transfers between devices  28.5 us (45%)
  waiting for transfers between devices  21.3 us (33%)
  Pallas kernels  11.4 us (18%)
  between operations  0.93 us (1%)
  local copies, waits for them, and re-layouts  0.78 us (1%)
    ppermute x15, starting transfers between devices, permuted(): return lax.ppermute(block, 'node', route)  28.5 us
    ppermute x15, waiting for transfers between devices, permuted(): return lax.ppermute(block, 'node', route)  21.3 us
    pallas_call x4, Pallas kernels, call(): pl.pallas_call(kernel, in_specs=[place] * len(operands), out_specs=[VMEM]...  11.4 us
  transfers between devices with their start and end apart: 15, of which 6 were waited for; matrix products, arithmetic and copies ran while one was open for 0% of the time, Pallas kernels for 8%

profile of v6, /device:TPU:0, one launch (start us, length us, event | category | flops | bytes accessed | tf_op | source)
XLA Modules:
  0.0 63.4 jit_solution(9675566005740610887)
XLA Ops:
  0.6 5.9 %collective-permute-start.2 = (bf16[512,128]{1,0:T(8,128)(2,1)}, bf16[512,128]{1,0:T(8,128)(2,1)S(1)}, u32[]{:S(2)}, u32[]{:S(2)}) collective-permute-start(bf16[512,128]{1,0:T(8,128)(2,1)} %bitcast.6), channel_id=1, source_target_pairs={{0,8},{1,9},{16,24},{17,25}} | collective-permute-start | bytes 393224 | tf_op jit(solution)/shard_map/ppermute | solution.py:22
  6.6 1.6 %collective-permute-start.1 = (bf16[512,128]{1,0:T(8,128)(2,1)}, bf16[512,128]{1,0:T(8,128)(2,1)S(1)}, u32[]{:S(2)}, u32[]{:S(2)}) collective-permute-start(bf16[512,128]{1,0:T(8,128)(2,1)} %bitcast.8), channel_id=1, source_target_pairs={{0,10},{1,11},{16,26},{17,27}} | collective-permute-start | bytes 393224 | tf_op jit(solution)/shard_map/ppermute | solution.py:22
  8.2 1.3 %collective-permute-start = (bf16[512,128]{1,0:T(8,128)(2,1)}, bf16[512,128]{1,0:T(8,128)(2,1)S(1)}, u32[]{:S(2)}, u32[]{:S(2)}) collective-permute-start(bf16[512,128]{1,0:T(8,128)(2,1)} %bitcast.9), channel_id=1, source_target_pairs={{0,2},{1,3},{16,18},{17,19}} | collective-permute-start | bytes 393224 | tf_op jit(solution)/shard_map/ppermute | solution.py:22
  9.5 1.2 %load.1 = (bf16[256,128]{1,0:T(8,128)(2,1)S(1)}, bf16[512,128]{1,0:T(8,128)(2,1)S(1)}, bf16[4,128,128]{2,1,0:T(8,128)(2,1)S(1)}, bf16[4,128,128]{2,1,0:T(8,128)(...) custom-call(s32[64]{0:T(128)} %refs_0_.1, s32[64]{0:T(128)} %refs_1_.1, bf16[512,128]{1,0:T(8,128)(2,1)} %bitcast.7, ...), custom_call_target="tpu_custom_call" | custom-call | flops 1048576 | bytes 983552 | tf_op jit(solution)/shard_map/load/pallas_call | solution.py:213
  10.7 1.6 %pack.1 = (bf16[4,1024,128]{2,1,0:T(8,128)(2,1)S(1)}, bf16[4,1024,128]{2,1,0:T(8,128)(2,1)S(1)}) custom-call(bf16[128,32,128]{2,1,0:T(8,128)(2,1)} %q_ref.1, bf16[128,32,128]{2,1,0:T(8,128)(2,1)} %g_ref.1), custom_call_target="tpu_custom_call" | custom-call | flops 1048576 | bytes 4194304 | tf_op jit(solution)/shard_map/pack/pallas_call | solution.py:213
  12.4 0.0 collective-permute-done.2
  12.4 0.7 %collective-permute-start.4 = (bf16[256,128]{1,0:T(8,128)(2,1)S(1)}, bf16[256,128]{1,0:T(8,128)(2,1)S(1)}, u32[]{:S(2)}, u32[]{:S(2)}) collective-permute-start(bf16[256,128]{1,0:T(8,128)(2,1)S(1)} %get-tuple-element.52), channel_id=1, source_target_pairs={{2,14},{3,15},{18,30},{19,31}} | collective-permute-start | bytes 196616 | tf_op jit(solution)/shard_map/ppermute | solution.py:22
  13.0 0.7 %collective-permute-start.3 = (bf16[256,128]{1,0:T(8,128)(2,1)S(1)}, bf16[256,128]{1,0:T(8,128)(2,1)S(1)}, u32[]{:S(2)}, u32[]{:S(2)}) collective-permute-start(bf16[256,128]{1,0:T(8,128)(2,1)S(1)} %get-tuple-element.52), channel_id=1, source_target_pairs={{2,10},{4,12},{6,14},{3,11},{5,13},{7,15},{18,26},{20,28},{22,30},... | collective-permute-start | bytes 196616 | tf_op jit(solution)/shard_map/ppermute | solution.py:22
  13.7 0.0 collective-permute-done.1
  13.7 0.0 collective-permute-done
  13.7 0.1 add_convert_fusion.2
  13.8 0.0 collective-permute-done.4.refs_12_
  13.8 0.0 collective-permute-done.3.refs_11_
  13.9 3.7 %collective-permute-start.5 = (bf16[768,128]{1,0:T(8,128)(2,1)S(1)}, bf16[768,128]{1,0:T(8,128)(2,1)S(1)}, u32[]{:S(2)}, u32[]{:S(2)}) collective-permute-start(bf16[768,128]{1,0:T(8,128)(2,1)S(1)} %pad_maximum_fusion), channel_id=1, source_target_pairs={{0,4},{2,6},{4,8},{6,10},{8,12},{10,14},{1,5},{3,7},{5,9},{7,11},{... | collective-permute-start | bytes 589832 | tf_op jit(solution)/shard_map/ppermute | solution.py:22
  17.6 4.0 %collective-permute-start.6 = (bf16[512,128]{1,0:T(8,128)(2,1)S(1)}, bf16[512,128]{1,0:T(8,128)(2,1)S(1)}, u32[]{:S(2)}, u32[]{:S(2)}) collective-permute-start(bf16[512,128]{1,0:T(8,128)(2,1)S(1)} %maximum_select_fusion), channel_id=1, source_target_pairs={{0,2},{2,0},{4,6},{6,4},{8,10},{10,8},{12,14},{14,12},{1,3},{3,1},... | collective-permute-start | bytes 393224 | tf_op jit(solution)/shard_map/ppermute | solution.py:22
  21.7 0.0 collective-permute-done.5.refs_9_
  21.7 2.9 %collective-permute-done.6.refs_10_ = bf16[512,128]{1,0:T(8,128)(2,1)S(1)} collective-permute-done((bf16[512,128]{1,0:T(8,128)(2,1)S(1)}, bf16[512,128]{1,0:T(8,128)(2,1)S(1)}, u32[]{:S(2)}, u32[]{:S(2)}) %collective-permute-start.6) | collective-permute-done | bytes 131104 | tf_op jit(solution)/shard_map/ppermute | solution.py:22
  24.6 2.0 %collective-permute-start.7 = (bf16[768,128]{1,0:T(8,128)(2,1)S(1)}, bf16[768,128]{1,0:T(8,128)(2,1)S(1)}, u32[]{:S(2)}, u32[]{:S(2)}) collective-permute-start(bf16[768,128]{1,0:T(8,128)(2,1)S(1)} %pad_maximum_fusion.1), channel_id=1, source_target_pairs={{0,2},{2,0},{4,6},{6,4},{8,10},{10,8},{12,14},{14,12},{1,3},{3,1},... | collective-permute-start | bytes 589832 | tf_op jit(solution)/shard_map/ppermute | solution.py:22
  26.6 3.6 %collective-permute-done.7.refs_8_ = bf16[768,128]{1,0:T(8,128)(2,1)S(1)} collective-permute-done((bf16[768,128]{1,0:T(8,128)(2,1)S(1)}, bf16[768,128]{1,0:T(8,128)(2,1)S(1)}, u32[]{:S(2)}, u32[]{:S(2)}) %collective-permute-start.7) | collective-permute-done | bytes 196640 | tf_op jit(solution)/shard_map/ppermute | solution.py:22
  30.3 6.1 %probs.1 = (bf16[1280,128]{1,0:T(8,128)(2,1)S(1)}, bf16[1280,128]{1,0:T(8,128)(2,1)S(1)}, bf16[4,448,128]{2,1,0:T(8,128)(2,1)S(1)}, bf16[4,448,1024]{2,1,0:T(8,128)(2,1)S(1)}, bf16[4,128,1024]{2,1,0:T(8,128)(2,1)S(1)}) custom-call(bf16[512,128]{1,0:T(8,128)(2,1)S(1)} %get-tuple-element.73.refs_0_, bf16[512,128]{1,0:T(8,128)(2,1)S(1)} %get-tuple-element.72.refs_1_, ...), custom_call_target="tpu_custom_call" | custom-call | flops 1879048192 | bytes 9371648 | tf_op jit(solution)/shard_map/probs/pallas_call | solution.py:213
  36.4 2.1 %collective-permute-start.8 = (bf16[1280,128]{1,0:T(8,128)(2,1)S(1)}, bf16[1280,128]{1,0:T(8,128)(2,1)S(1)}, u32[]{:S(2)}, u32[]{:S(2)}) collective-permute-start(bf16[1280,128]{1,0:T(8,128)(2,1)S(1)} %get-tuple-element.65), channel_id=1, source_target_pairs={{0,2},{2,0},{4,6},{6,4},{8,10},{10,8},{12,14},{14,12},{1,3},{3,1},... | collective-permute-start | bytes 983048 | tf_op jit(solution)/shard_map/ppermute | solution.py:22
  38.5 2.4 %grads.1 = (bf16[128,32,128]{2,1,0:T(8,128)(2,1)}, f32[512,128]{1,0:T(8,128)S(1)}, f32[512,128]{1,0:T(8,128)S(1)}) custom-call(bf16[4,1024,128]{2,1,0:T(8,128)(2,1)S(1)} %get-tuple-element.48.refs_4_.refs_0_, bf16[4,1024,128]{2,1,0:T(8,128)(2,1)S(1)} %get-tuple-element.49.refs_5_.refs_1_, bf16[4,448,128]{2,1,0:T(8,128)(2,1)S(1)} %get-tuple-element.59.refs_2_, ...), custom_call_target="tpu_custom_call" | custom-call | flops 939524096 | bytes 8847360 | tf_op jit(solution)/shard_map/grads/pallas_call | solution.py:213
  40.9 2.6 %collective-permute-done.8 = bf16[1280,128]{1,0:T(8,128)(2,1)S(1)} collective-permute-done((bf16[1280,128]{1,0:T(8,128)(2,1)S(1)}, bf16[1280,128]{1,0:T(8,128)(2,1)S(1)}, u32[]{:S(2)}, u32[]{:S(2)}) %collective-permute-start.8) | collective-permute-done | bytes 327712 | tf_op jit(solution)/shard_map/ppermute | solution.py:22
  43.6 0.1 add_convert_fusion.3
  43.7 1.3 %collective-permute-start.9 = (bf16[768,128]{1,0:T(8,128)(2,1)S(1)}, bf16[768,128]{1,0:T(8,128)(2,1)S(1)}, u32[]{:S(2)}, u32[]{:S(2)}) collective-permute-start(bf16[768,128]{1,0:T(8,128)(2,1)S(1)} %pad_maximum_fusion.2), channel_id=1, source_target_pairs={{4,0},{6,2},{8,4},{10,6},{12,8},{14,10},{5,1},{7,3},{9,5},{11,7},{... | collective-permute-start | bytes 589832 | tf_op jit(solution)/shard_map/ppermute | solution.py:22
  45.0 0.7 %collective-permute-start.11 = (bf16[256,128]{1,0:T(8,128)(2,1)S(1)}, bf16[256,128]{1,0:T(8,128)(2,1)S(1)}, u32[]{:S(2)}, u32[]{:S(2)}) collective-permute-start(bf16[256,128]{1,0:T(8,128)(2,1)S(1)} %get-tuple-element.69), channel_id=1, source_target_pairs={{14,2},{15,3},{30,18},{31,19}} | collective-permute-start | bytes 196616 | tf_op jit(solution)/shard_map/ppermute | solution.py:22
  45.7 0.7 %collective-permute-start.10 = (bf16[256,128]{1,0:T(8,128)(2,1)S(1)}, bf16[256,128]{1,0:T(8,128)(2,1)S(1)}, u32[]{:S(2)}, u32[]{:S(2)}) collective-permute-start(bf16[256,128]{1,0:T(8,128)(2,1)S(1)} %get-tuple-element.70), channel_id=1, source_target_pairs={{10,2},{12,4},{14,6},{11,3},{13,5},{15,7},{26,18},{28,20},{30,22},... | collective-permute-start | bytes 196616 | tf_op jit(solution)/shard_map/ppermute | solution.py:22
  46.3 4.9 %collective-permute-done.9 = bf16[768,128]{1,0:T(8,128)(2,1)S(1)} collective-permute-done((bf16[768,128]{1,0:T(8,128)(2,1)S(1)}, bf16[768,128]{1,0:T(8,128)(2,1)S(1)}, u32[]{:S(2)}, u32[]{:S(2)}) %collective-permute-start.9) | collective-permute-done | bytes 196640 | tf_op jit(solution)/shard_map/ppermute | solution.py:22
  51.3 0.0 collective-permute-done.11
  51.3 0.0 collective-permute-done.10
  51.3 1.3 %collective-permute-start.14 = (bf16[512,128]{1,0:T(8,128)(2,1)S(1)}, bf16[512,128]{1,0:T(8,128)(2,1)S(1)}, u32[]{:S(2)}, u32[]{:S(2)}) collective-permute-start(bf16[512,128]{1,0:T(8,128)(2,1)S(1)} %add_convert_fusion), channel_id=1, source_target_pairs={{2,0},{3,1},{18,16},{19,17}} | collective-permute-start | bytes 393224 | tf_op jit(solution)/shard_map/ppermute | solution.py:22
  52.6 1.3 %collective-permute-start.13 = (bf16[512,128]{1,0:T(8,128)(2,1)S(1)}, bf16[512,128]{1,0:T(8,128)(2,1)S(1)}, u32[]{:S(2)}, u32[]{:S(2)}) collective-permute-start(bf16[512,128]{1,0:T(8,128)(2,1)S(1)} %add_convert_fusion), channel_id=1, source_target_pairs={{10,0},{11,1},{26,16},{27,17}} | collective-permute-start | bytes 393224 | tf_op jit(solution)/shard_map/ppermute | solution.py:22
  53.9 1.3 %collective-permute-start.12 = (bf16[512,128]{1,0:T(8,128)(2,1)S(1)}, bf16[512,128]{1,0:T(8,128)(2,1)S(1)}, u32[]{:S(2)}, u32[]{:S(2)}) collective-permute-start(bf16[512,128]{1,0:T(8,128)(2,1)S(1)} %add_convert_fusion), channel_id=1, source_target_pairs={{8,0},{9,1},{24,16},{25,17}} | collective-permute-start | bytes 393224 | tf_op jit(solution)/shard_map/ppermute | solution.py:22
  55.3 6.4 %collective-permute-done.12 = bf16[512,128]{1,0:T(8,128)(2,1)S(1)} collective-permute-done((bf16[512,128]{1,0:T(8,128)(2,1)S(1)}, bf16[512,128]{1,0:T(8,128)(2,1)S(1)}, u32[]{:S(2)}, u32[]{:S(2)}) %collective-permute-start.12) | collective-permute-done | bytes 131104 | tf_op jit(solution)/shard_map/ppermute | solution.py:22
  61.7 0.8 %collective-permute-done.14 = bf16[512,128]{1,0:T(8,128)(2,1)S(1)} collective-permute-done((bf16[512,128]{1,0:T(8,128)(2,1)S(1)}, bf16[512,128]{1,0:T(8,128)(2,1)S(1)}, u32[]{:S(2)}, u32[]{:S(2)}) %collective-permute-start.14) | collective-permute-done | bytes 131104 | tf_op jit(solution)/shard_map/ppermute | solution.py:22
  62.5 0.0 collective-permute-done.13
  62.6 0.0 copy-start
  62.6 0.0 copy-start.1
  62.6 0.7 %copy-done = f32[512,128]{1,0:T(8,128)} copy-done((f32[512,128]{1,0:T(8,128)}, f32[512,128]{1,0:T(8,128)S(1)}, u32[]{:S(2)}) %copy-start) | copy-done | bytes 262168
  63.3 0.1 copy-done.1
  (13 shorter events, 0.4 us)
Async XLA Ops:
  0.6 11.7 %collective-permute-start.2 = (bf16[512,128]{1,0:T(8,128)(2,1)}, bf16[512,128]{1,0:T(8,128)(2,1)S(1)}, u32[]{:S(2)}, u32[]{:S(2)}) collective-permute-start(bf16[512,128]{1,0:T(8,128)(2,1)} %bitcast.6), channel_id=1, source_target_pairs={{0,8},{1,9},{16,24},{17,25}} | collective-permute-start | bytes 393224 | tf_op jit(solution)/shard_map/ppermute | solution.py:22
  6.6 7.1 %collective-permute-start.1 = (bf16[512,128]{1,0:T(8,128)(2,1)}, bf16[512,128]{1,0:T(8,128)(2,1)S(1)}, u32[]{:S(2)}, u32[]{:S(2)}) collective-permute-start(bf16[512,128]{1,0:T(8,128)(2,1)} %bitcast.8), channel_id=1, source_target_pairs={{0,10},{1,11},{16,26},{17,27}} | collective-permute-start | bytes 393224 | tf_op jit(solution)/shard_map/ppermute | solution.py:22
  8.2 5.5 %collective-permute-start = (bf16[512,128]{1,0:T(8,128)(2,1)}, bf16[512,128]{1,0:T(8,128)(2,1)S(1)}, u32[]{:S(2)}, u32[]{:S(2)}) collective-permute-start(bf16[512,128]{1,0:T(8,128)(2,1)} %bitcast.9), channel_id=1, source_target_pairs={{0,2},{1,3},{16,18},{17,19}} | collective-permute-start | bytes 393224 | tf_op jit(solution)/shard_map/ppermute | solution.py:22
  12.4 1.4 %collective-permute-start.4 = (bf16[256,128]{1,0:T(8,128)(2,1)S(1)}, bf16[256,128]{1,0:T(8,128)(2,1)S(1)}, u32[]{:S(2)}, u32[]{:S(2)}) collective-permute-start(bf16[256,128]{1,0:T(8,128)(2,1)S(1)} %get-tuple-element.52), channel_id=1, source_target_pairs={{2,14},{3,15},{18,30},{19,31}} | collective-permute-start | bytes 196616 | tf_op jit(solution)/shard_map/ppermute | solution.py:22
  13.0 0.8 %collective-permute-start.3 = (bf16[256,128]{1,0:T(8,128)(2,1)S(1)}, bf16[256,128]{1,0:T(8,128)(2,1)S(1)}, u32[]{:S(2)}, u32[]{:S(2)}) collective-permute-start(bf16[256,128]{1,0:T(8,128)(2,1)S(1)} %get-tuple-element.52), channel_id=1, source_target_pairs={{2,10},{4,12},{6,14},{3,11},{5,13},{7,15},{18,26},{20,28},{22,30},... | collective-permute-start | bytes 196616 | tf_op jit(solution)/shard_map/ppermute | solution.py:22
  13.9 7.8 %collective-permute-start.5 = (bf16[768,128]{1,0:T(8,128)(2,1)S(1)}, bf16[768,128]{1,0:T(8,128)(2,1)S(1)}, u32[]{:S(2)}, u32[]{:S(2)}) collective-permute-start(bf16[768,128]{1,0:T(8,128)(2,1)S(1)} %pad_maximum_fusion), channel_id=1, source_target_pairs={{0,4},{2,6},{4,8},{6,10},{8,12},{10,14},{1,5},{3,7},{5,9},{7,11},{... | collective-permute-start | bytes 589832 | tf_op jit(solution)/shard_map/ppermute | solution.py:22
  17.6 7.0 %collective-permute-start.6 = (bf16[512,128]{1,0:T(8,128)(2,1)S(1)}, bf16[512,128]{1,0:T(8,128)(2,1)S(1)}, u32[]{:S(2)}, u32[]{:S(2)}) collective-permute-start(bf16[512,128]{1,0:T(8,128)(2,1)S(1)} %maximum_select_fusion), channel_id=1, source_target_pairs={{0,2},{2,0},{4,6},{6,4},{8,10},{10,8},{12,14},{14,12},{1,3},{3,1},... | collective-permute-start | bytes 393224 | tf_op jit(solution)/shard_map/ppermute | solution.py:22
  24.6 5.7 %collective-permute-start.7 = (bf16[768,128]{1,0:T(8,128)(2,1)S(1)}, bf16[768,128]{1,0:T(8,128)(2,1)S(1)}, u32[]{:S(2)}, u32[]{:S(2)}) collective-permute-start(bf16[768,128]{1,0:T(8,128)(2,1)S(1)} %pad_maximum_fusion.1), channel_id=1, source_target_pairs={{0,2},{2,0},{4,6},{6,4},{8,10},{10,8},{12,14},{14,12},{1,3},{3,1},... | collective-permute-start | bytes 589832 | tf_op jit(solution)/shard_map/ppermute | solution.py:22
  36.4 7.1 %collective-permute-start.8 = (bf16[1280,128]{1,0:T(8,128)(2,1)S(1)}, bf16[1280,128]{1,0:T(8,128)(2,1)S(1)}, u32[]{:S(2)}, u32[]{:S(2)}) collective-permute-start(bf16[1280,128]{1,0:T(8,128)(2,1)S(1)} %get-tuple-element.65), channel_id=1, source_target_pairs={{0,2},{2,0},{4,6},{6,4},{8,10},{10,8},{12,14},{14,12},{1,3},{3,1},... | collective-permute-start | bytes 983048 | tf_op jit(solution)/shard_map/ppermute | solution.py:22
  43.7 7.6 %collective-permute-start.9 = (bf16[768,128]{1,0:T(8,128)(2,1)S(1)}, bf16[768,128]{1,0:T(8,128)(2,1)S(1)}, u32[]{:S(2)}, u32[]{:S(2)}) collective-permute-start(bf16[768,128]{1,0:T(8,128)(2,1)S(1)} %pad_maximum_fusion.2), channel_id=1, source_target_pairs={{4,0},{6,2},{8,4},{10,6},{12,8},{14,10},{5,1},{7,3},{9,5},{11,7},{... | collective-permute-start | bytes 589832 | tf_op jit(solution)/shard_map/ppermute | solution.py:22
  45.0 6.3 %collective-permute-start.11 = (bf16[256,128]{1,0:T(8,128)(2,1)S(1)}, bf16[256,128]{1,0:T(8,128)(2,1)S(1)}, u32[]{:S(2)}, u32[]{:S(2)}) collective-permute-start(bf16[256,128]{1,0:T(8,128)(2,1)S(1)} %get-tuple-element.69), channel_id=1, source_target_pairs={{14,2},{15,3},{30,18},{31,19}} | collective-permute-start | bytes 196616 | tf_op jit(solution)/shard_map/ppermute | solution.py:22
  45.7 5.6 %collective-permute-start.10 = (bf16[256,128]{1,0:T(8,128)(2,1)S(1)}, bf16[256,128]{1,0:T(8,128)(2,1)S(1)}, u32[]{:S(2)}, u32[]{:S(2)}) collective-permute-start(bf16[256,128]{1,0:T(8,128)(2,1)S(1)} %get-tuple-element.70), channel_id=1, source_target_pairs={{10,2},{12,4},{14,6},{11,3},{13,5},{15,7},{26,18},{28,20},{30,22},... | collective-permute-start | bytes 196616 | tf_op jit(solution)/shard_map/ppermute | solution.py:22
  51.3 11.2 %collective-permute-start.14 = (bf16[512,128]{1,0:T(8,128)(2,1)S(1)}, bf16[512,128]{1,0:T(8,128)(2,1)S(1)}, u32[]{:S(2)}, u32[]{:S(2)}) collective-permute-start(bf16[512,128]{1,0:T(8,128)(2,1)S(1)} %add_convert_fusion), channel_id=1, source_target_pairs={{2,0},{3,1},{18,16},{19,17}} | collective-permute-start | bytes 393224 | tf_op jit(solution)/shard_map/ppermute | solution.py:22
  52.6 9.9 %collective-permute-start.13 = (bf16[512,128]{1,0:T(8,128)(2,1)S(1)}, bf16[512,128]{1,0:T(8,128)(2,1)S(1)}, u32[]{:S(2)}, u32[]{:S(2)}) collective-permute-start(bf16[512,128]{1,0:T(8,128)(2,1)S(1)} %add_convert_fusion), channel_id=1, source_target_pairs={{10,0},{11,1},{26,16},{27,17}} | collective-permute-start | bytes 393224 | tf_op jit(solution)/shard_map/ppermute | solution.py:22
  53.9 7.8 %collective-permute-start.12 = (bf16[512,128]{1,0:T(8,128)(2,1)S(1)}, bf16[512,128]{1,0:T(8,128)(2,1)S(1)}, u32[]{:S(2)}, u32[]{:S(2)}) collective-permute-start(bf16[512,128]{1,0:T(8,128)(2,1)S(1)} %add_convert_fusion), channel_id=1, source_target_pairs={{8,0},{9,1},{24,16},{25,17}} | collective-permute-start | bytes 393224 | tf_op jit(solution)/shard_map/ppermute | solution.py:22
  62.6 0.7 %copy-start = (f32[512,128]{1,0:T(8,128)}, f32[512,128]{1,0:T(8,128)S(1)}, u32[]{:S(2)}) copy-start(f32[512,128]{1,0:T(8,128)S(1)} %get-tuple-element.75) | copy-start | bytes 786436
  62.6 0.8 %copy-start.1 = (f32[512,128]{1,0:T(8,128)}, f32[512,128]{1,0:T(8,128)S(1)}, u32[]{:S(2)}) copy-start(f32[512,128]{1,0:T(8,128)S(1)} %get-tuple-element.74) | copy-start | bytes 786436

commit v7 on v6

--- a/solution.py
+++ b/solution.py
@@ -356,11 +356,11 @@
         return [array[start + i * unit : start + (i + 1) * unit] for i in range(count)]
 
     head, held, *own = load(order, keys, values, parents, lengths, tokens)
-    qh, gh = pack(queries, grad_out, heads_kv)
     keys_far = permuted(keys, [(0, top)])
     values_far = permuted(values, [(0, top + 1)])
     values_next = permuted(values, [(0, 1)])
-    head = after(head, keys_far)
+    head, queries = lax.optimization_barrier((head, queries, keys_far))[:2]
+    qh, gh = pack(queries, grad_out, heads_kv)
     far = permuted(head, far_route)
     held = added(held, values_next, values_far, keys_far).astype(BF16)
     for stride in reversed(strides[:-1]):
@@ -408,15 +408,16 @@
     four = permuted(four.astype(BF16), back(far_route))
     mine = added(mine, four)
     total = added(total, jnp.where(lower, second[:rows], jnp.zeros_like(total))).astype(BF16)
+    for stride in strides[:-1]:
+        total = added(total, permuted(total, back(prompt_route(stride)))).astype(BF16)
     if small:
         total = after(total, four, six)
-    for stride in strides[:-1]:
-        total = added(total, permuted(total, back(prompt_route(stride)))).astype(BF16)
     keys_far = permuted(total, [(top, 0)])
     values_far = permuted(total, [(top + 1, 0)])
     values_next = permuted(total, [(1, 0)])
+    prompt_v, prompt_k = lax.optimization_barrier((added(values_next, values_far), added(total, keys_far)))
     own = []
-    for side, local, prompt in ((0, dk, added(total, keys_far)), (1, dv, added(values_far, values_next))):
+    for side, local, prompt in ((0, dk, prompt_k), (1, dv, prompt_v)):
         whole = local + jnp.where(device == 0, prompt, 0.0)
         own.append(whole.at[:one].add(mine[side * one : (side + 1) * one]).reshape(tokens, heads_kv, head_size))
     return grad_queries, own[0], own[1]

time: 63.7 us -> 63 us (0.989)
  starting transfers between devices: 28.5 us -> 26.4 us
  waiting for transfers between devices: 21.3 us -> 22.7 us
    ppermute x15, starting transfers between devices: 28.5 us -> 26.4 us  [permuted(): return lax.ppermute(block, 'node', route)]
    ppermute x15, waiting for transfers between devices: 21.3 us -> 22.7 us  [permuted(): return lax.ppermute(block, 'node', route)]
  transfers between devices with their start and end apart: 15 -> 15, of which waited for: 6 -> 11; matrix products, arithmetic and copies ran while one was open for 0% -> 0% of each run, Pallas kernels for 8% -> 8%
where the time goes in v7:
time: 63 us; the launch traced here: 62.7 us
  starting transfers between devices  26.4 us (42%)
  waiting for transfers between devices  22.7 us (36%)
  Pallas kernels  11.4 us (18%)
  between operations  0.91 us (1%)
  local copies, waits for them, and re-layouts  0.78 us (1%)
    ppermute x15, starting transfers between devices, permuted(): return lax.ppermute(block, 'node', route)  26.4 us
    ppermute x15, waiting for transfers between devices, permuted(): return lax.ppermute(block, 'node', route)  22.7 us
    pallas_call x4, Pallas kernels, call(): pl.pallas_call(kernel, in_specs=[place] * len(operands), out_specs=[VMEM]...  11.4 us
  transfers between devices with their start and end apart: 15, of which 11 were waited for; matrix products, arithmetic and copies ran while one was open for 0% of the time, Pallas kernels for 8%

profile of v7, /device:TPU:0, one launch (start us, length us, event | category | flops | bytes accessed | tf_op | source)
XLA Modules:
  0.0 62.7 jit_solution(14984143517939600945)
XLA Ops:
  0.6 5.9 %collective-permute-start = (bf16[512,128]{1,0:T(8,128)(2,1)}, bf16[512,128]{1,0:T(8,128)(2,1)S(1)}, u32[]{:S(2)}, u32[]{:S(2)}) collective-permute-start(bf16[512,128]{1,0:T(8,128)(2,1)} %bitcast.6), channel_id=1, source_target_pairs={{0,8},{1,9},{16,24},{17,25}} | collective-permute-start | bytes 393224 | tf_op jit(solution)/shard_map/ppermute | solution.py:22
  6.6 1.6 %collective-permute-start.2 = (bf16[512,128]{1,0:T(8,128)(2,1)}, bf16[512,128]{1,0:T(8,128)(2,1)S(1)}, u32[]{:S(2)}, u32[]{:S(2)}) collective-permute-start(bf16[512,128]{1,0:T(8,128)(2,1)} %bitcast.8), channel_id=1, source_target_pairs={{0,10},{1,11},{16,26},{17,27}} | collective-permute-start | bytes 393224 | tf_op jit(solution)/shard_map/ppermute | solution.py:22
  8.2 1.3 %collective-permute-start.1 = (bf16[512,128]{1,0:T(8,128)(2,1)}, bf16[512,128]{1,0:T(8,128)(2,1)S(1)}, u32[]{:S(2)}, u32[]{:S(2)}) collective-permute-start(bf16[512,128]{1,0:T(8,128)(2,1)} %bitcast.9), channel_id=1, source_target_pairs={{0,2},{1,3},{16,18},{17,19}} | collective-permute-start | bytes 393224 | tf_op jit(solution)/shard_map/ppermute | solution.py:22
  9.5 1.2 %load.1 = (bf16[256,128]{1,0:T(8,128)(2,1)S(1)}, bf16[512,128]{1,0:T(8,128)(2,1)S(1)}, bf16[4,128,128]{2,1,0:T(8,128)(2,1)S(1)}, bf16[4,128,128]{2,1,0:T(8,128)(...) custom-call(s32[64]{0:T(128)} %refs_0_.1, s32[64]{0:T(128)} %refs_1_.1, bf16[512,128]{1,0:T(8,128)(2,1)} %bitcast.7, ...), custom_call_target="tpu_custom_call" | custom-call | flops 1048576 | bytes 983552 | tf_op jit(solution)/shard_map/load/pallas_call | solution.py:213
  10.7 0.1 collective-permute-done
  10.8 0.7 %collective-permute-start.4 = (bf16[256,128]{1,0:T(8,128)(2,1)S(1)}, bf16[256,128]{1,0:T(8,128)(2,1)S(1)}, u32[]{:S(2)}, u32[]{:S(2)}) collective-permute-start(bf16[256,128]{1,0:T(8,128)(2,1)S(1)} %get-tuple-element.56), channel_id=1, source_target_pairs={{2,14},{3,15},{18,30},{19,31}} | collective-permute-start | bytes 196616 | tf_op jit(solution)/shard_map/ppermute | solution.py:22
  11.4 0.7 %collective-permute-start.3 = (bf16[256,128]{1,0:T(8,128)(2,1)S(1)}, bf16[256,128]{1,0:T(8,128)(2,1)S(1)}, u32[]{:S(2)}, u32[]{:S(2)}) collective-permute-start(bf16[256,128]{1,0:T(8,128)(2,1)S(1)} %get-tuple-element.56), channel_id=1, source_target_pairs={{2,10},{4,12},{6,14},{3,11},{5,13},{7,15},{18,26},{20,28},{22,30},... | collective-permute-start | bytes 196616 | tf_op jit(solution)/shard_map/ppermute | solution.py:22
  12.1 0.4 collective-permute-done.2
  12.5 0.1 collective-permute-done.1
  12.5 0.1 add_convert_fusion.2
  12.6 1.6 %pack.1 = (bf16[4,1024,128]{2,1,0:T(8,128)(2,1)S(1)}, bf16[4,1024,128]{2,1,0:T(8,128)(2,1)S(1)}) custom-call(bf16[128,32,128]{2,1,0:T(8,128)(2,1)} %q_ref, bf16[128,32,128]{2,1,0:T(8,128)(2,1)} %g_ref.1), custom_call_target="tpu_custom_call" | custom-call | flops 1048576 | bytes 4194304 | tf_op jit(solution)/shard_map/pack/pallas_call | solution.py:213
  14.3 0.0 collective-permute-done.4.refs_12_
  14.3 0.0 collective-permute-done.3.refs_11_
  14.3 2.8 %collective-permute-start.5 = (bf16[768,128]{1,0:T(8,128)(2,1)S(1)}, bf16[768,128]{1,0:T(8,128)(2,1)S(1)}, u32[]{:S(2)}, u32[]{:S(2)}) collective-permute-start(bf16[768,128]{1,0:T(8,128)(2,1)S(1)} %pad_maximum_fusion), channel_id=1, source_target_pairs={{0,4},{2,6},{4,8},{6,10},{8,12},{10,14},{1,5},{3,7},{5,9},{7,11},{... | collective-permute-start | bytes 589832 | tf_op jit(solution)/shard_map/ppermute | solution.py:22
  17.2 2.8 %collective-permute-start.6 = (bf16[512,128]{1,0:T(8,128)(2,1)S(1)}, bf16[512,128]{1,0:T(8,128)(2,1)S(1)}, u32[]{:S(2)}, u32[]{:S(2)}) collective-permute-start(bf16[512,128]{1,0:T(8,128)(2,1)S(1)} %maximum_select_fusion), channel_id=1, source_target_pairs={{0,2},{2,0},{4,6},{6,4},{8,10},{10,8},{12,14},{14,12},{1,3},{3,1},... | collective-permute-start | bytes 393224 | tf_op jit(solution)/shard_map/ppermute | solution.py:22
  20.0 1.5 %collective-permute-done.5.refs_9_ = bf16[768,128]{1,0:T(8,128)(2,1)S(1)} collective-permute-done((bf16[768,128]{1,0:T(8,128)(2,1)S(1)}, bf16[768,128]{1,0:T(8,128)(2,1)S(1)}, u32[]{:S(2)}, u32[]{:S(2)}) %collective-permute-start.5) | collective-permute-done | bytes 196640 | tf_op jit(solution)/shard_map/ppermute | solution.py:22
  21.5 1.4 %collective-permute-done.6.refs_10_ = bf16[512,128]{1,0:T(8,128)(2,1)S(1)} collective-permute-done((bf16[512,128]{1,0:T(8,128)(2,1)S(1)}, bf16[512,128]{1,0:T(8,128)(2,1)S(1)}, u32[]{:S(2)}, u32[]{:S(2)}) %collective-permute-start.6) | collective-permute-done | bytes 131104 | tf_op jit(solution)/shard_map/ppermute | solution.py:22
  23.0 2.0 %collective-permute-start.7 = (bf16[768,128]{1,0:T(8,128)(2,1)S(1)}, bf16[768,128]{1,0:T(8,128)(2,1)S(1)}, u32[]{:S(2)}, u32[]{:S(2)}) collective-permute-start(bf16[768,128]{1,0:T(8,128)(2,1)S(1)} %pad_maximum_fusion.1), channel_id=1, source_target_pairs={{0,2},{2,0},{4,6},{6,4},{8,10},{10,8},{12,14},{14,12},{1,3},{3,1},... | collective-permute-start | bytes 589832 | tf_op jit(solution)/shard_map/ppermute | solution.py:22
  25.0 3.6 %collective-permute-done.7.refs_8_ = bf16[768,128]{1,0:T(8,128)(2,1)S(1)} collective-permute-done((bf16[768,128]{1,0:T(8,128)(2,1)S(1)}, bf16[768,128]{1,0:T(8,128)(2,1)S(1)}, u32[]{:S(2)}, u32[]{:S(2)}) %collective-permute-start.7) | collective-permute-done | bytes 196640 | tf_op jit(solution)/shard_map/ppermute | solution.py:22
  28.7 6.1 %probs.1 = (bf16[1280,128]{1,0:T(8,128)(2,1)S(1)}, bf16[1280,128]{1,0:T(8,128)(2,1)S(1)}, bf16[4,448,128]{2,1,0:T(8,128)(2,1)S(1)}, bf16[4,448,1024]{2,1,0:T(8,128)(2,1)S(1)}, bf16[4,128,1024]{2,1,0:T(8,128)(2,1)S(1)}) custom-call(bf16[512,128]{1,0:T(8,128)(2,1)S(1)} %get-tuple-element.79.refs_0_, bf16[512,128]{1,0:T(8,128)(2,1)S(1)} %get-tuple-element.78.refs_1_, ...), custom_call_target="tpu_custom_call" | custom-call | flops 1879048192 | bytes 9371648 | tf_op jit(solution)/shard_map/probs/pallas_call | solution.py:213
  34.8 2.1 %collective-permute-start.8 = (bf16[1280,128]{1,0:T(8,128)(2,1)S(1)}, bf16[1280,128]{1,0:T(8,128)(2,1)S(1)}, u32[]{:S(2)}, u32[]{:S(2)}) collective-permute-start(bf16[1280,128]{1,0:T(8,128)(2,1)S(1)} %get-tuple-element.69), channel_id=1, source_target_pairs={{0,2},{2,0},{4,6},{6,4},{8,10},{10,8},{12,14},{14,12},{1,3},{3,1},... | collective-permute-start | bytes 983048 | tf_op jit(solution)/shard_map/ppermute | solution.py:22
  36.8 2.4 %grads.1 = (bf16[128,32,128]{2,1,0:T(8,128)(2,1)}, f32[512,128]{1,0:T(8,128)S(1)}, f32[512,128]{1,0:T(8,128)S(1)}) custom-call(bf16[4,1024,128]{2,1,0:T(8,128)(2,1)S(1)} %get-tuple-element.53.refs_4_.refs_0_, bf16[4,1024,128]{2,1,0:T(8,128)(2,1)S(1)} %get-tuple-element.54.refs_5_.refs_1_, bf16[4,448,128]{2,1,0:T(8,128)(2,1)S(1)} %get-tuple-element.63.refs_2_, ...), custom_call_target="tpu_custom_call" | custom-call | flops 939524096 | bytes 8847360 | tf_op jit(solution)/shard_map/grads/pallas_call | solution.py:213
  39.3 2.6 %collective-permute-done.8 = bf16[1280,128]{1,0:T(8,128)(2,1)S(1)} collective-permute-done((bf16[1280,128]{1,0:T(8,128)(2,1)S(1)}, bf16[1280,128]{1,0:T(8,128)(2,1)S(1)}, u32[]{:S(2)}, u32[]{:S(2)}) %collective-permute-start.8) | collective-permute-done | bytes 327712 | tf_op jit(solution)/shard_map/ppermute | solution.py:22
  41.9 0.1 add_convert_fusion.3
  42.0 1.3 %collective-permute-start.9 = (bf16[768,128]{1,0:T(8,128)(2,1)S(1)}, bf16[768,128]{1,0:T(8,128)(2,1)S(1)}, u32[]{:S(2)}, u32[]{:S(2)}) collective-permute-start(bf16[768,128]{1,0:T(8,128)(2,1)S(1)} %pad_maximum_fusion.2), channel_id=1, source_target_pairs={{4,0},{6,2},{8,4},{10,6},{12,8},{14,10},{5,1},{7,3},{9,5},{11,7},{... | collective-permute-start | bytes 589832 | tf_op jit(solution)/shard_map/ppermute | solution.py:22
  43.3 0.7 %collective-permute-start.11 = (bf16[256,128]{1,0:T(8,128)(2,1)S(1)}, bf16[256,128]{1,0:T(8,128)(2,1)S(1)}, u32[]{:S(2)}, u32[]{:S(2)}) collective-permute-start(bf16[256,128]{1,0:T(8,128)(2,1)S(1)} %get-tuple-element.75), channel_id=1, source_target_pairs={{14,2},{15,3},{30,18},{31,19}} | collective-permute-start | bytes 196616 | tf_op jit(solution)/shard_map/ppermute | solution.py:22
  44.0 0.7 %collective-permute-start.10 = (bf16[256,128]{1,0:T(8,128)(2,1)S(1)}, bf16[256,128]{1,0:T(8,128)(2,1)S(1)}, u32[]{:S(2)}, u32[]{:S(2)}) collective-permute-start(bf16[256,128]{1,0:T(8,128)(2,1)S(1)} %get-tuple-element.76), channel_id=1, source_target_pairs={{10,2},{12,4},{14,6},{11,3},{13,5},{15,7},{26,18},{28,20},{30,22},... | collective-permute-start | bytes 196616 | tf_op jit(solution)/shard_map/ppermute | solution.py:22
  44.7 4.9 %collective-permute-done.9 = bf16[768,128]{1,0:T(8,128)(2,1)S(1)} collective-permute-done((bf16[768,128]{1,0:T(8,128)(2,1)S(1)}, bf16[768,128]{1,0:T(8,128)(2,1)S(1)}, u32[]{:S(2)}, u32[]{:S(2)}) %collective-permute-start.9) | collective-permute-done | bytes 196640 | tf_op jit(solution)/shard_map/ppermute | solution.py:22
  49.7 0.0 collective-permute-done.11
  49.7 0.0 collective-permute-done.10
  49.7 1.3 %collective-permute-start.14 = (bf16[512,128]{1,0:T(8,128)(2,1)S(1)}, bf16[512,128]{1,0:T(8,128)(2,1)S(1)}, u32[]{:S(2)}, u32[]{:S(2)}) collective-permute-start(bf16[512,128]{1,0:T(8,128)(2,1)S(1)} %add_convert_fusion), channel_id=1, source_target_pairs={{8,0},{9,1},{24,16},{25,17}} | collective-permute-start | bytes 393224 | tf_op jit(solution)/shard_map/ppermute | solution.py:22
  51.0 1.3 %collective-permute-start.13 = (bf16[512,128]{1,0:T(8,128)(2,1)S(1)}, bf16[512,128]{1,0:T(8,128)(2,1)S(1)}, u32[]{:S(2)}, u32[]{:S(2)}) collective-permute-start(bf16[512,128]{1,0:T(8,128)(2,1)S(1)} %add_convert_fusion), channel_id=1, source_target_pairs={{10,0},{11,1},{26,16},{27,17}} | collective-permute-start | bytes 393224 | tf_op jit(solution)/shard_map/ppermute | solution.py:22
  52.3 1.3 %collective-permute-start.12 = (bf16[512,128]{1,0:T(8,128)(2,1)S(1)}, bf16[512,128]{1,0:T(8,128)(2,1)S(1)}, u32[]{:S(2)}, u32[]{:S(2)}) collective-permute-start(bf16[512,128]{1,0:T(8,128)(2,1)S(1)} %add_convert_fusion), channel_id=1, source_target_pairs={{2,0},{3,1},{18,16},{19,17}} | collective-permute-start | bytes 393224 | tf_op jit(solution)/shard_map/ppermute | solution.py:22
  53.6 3.9 %collective-permute-done.14 = bf16[512,128]{1,0:T(8,128)(2,1)S(1)} collective-permute-done((bf16[512,128]{1,0:T(8,128)(2,1)S(1)}, bf16[512,128]{1,0:T(8,128)(2,1)S(1)}, u32[]{:S(2)}, u32[]{:S(2)}) %collective-permute-start.14) | collective-permute-done | bytes 131104 | tf_op jit(solution)/shard_map/ppermute | solution.py:22
  57.6 2.1 %collective-permute-done.13 = bf16[512,128]{1,0:T(8,128)(2,1)S(1)} collective-permute-done((bf16[512,128]{1,0:T(8,128)(2,1)S(1)}, bf16[512,128]{1,0:T(8,128)(2,1)S(1)}, u32[]{:S(2)}, u32[]{:S(2)}) %collective-permute-start.13) | collective-permute-done | bytes 131104 | tf_op jit(solution)/shard_map/ppermute | solution.py:22
  59.6 2.1 %collective-permute-done.12 = bf16[512,128]{1,0:T(8,128)(2,1)S(1)} collective-permute-done((bf16[512,128]{1,0:T(8,128)(2,1)S(1)}, bf16[512,128]{1,0:T(8,128)(2,1)S(1)}, u32[]{:S(2)}, u32[]{:S(2)}) %collective-permute-start.12) | collective-permute-done | bytes 131104 | tf_op jit(solution)/shard_map/ppermute | solution.py:22
  61.8 0.1 select_add_fusion
  61.9 0.0 copy-start
  61.9 0.0 copy-start.1
  61.9 0.7 %copy-done = f32[512,128]{1,0:T(8,128)} copy-done((f32[512,128]{1,0:T(8,128)}, f32[512,128]{1,0:T(8,128)S(1)}, u32[]{:S(2)}) %copy-start) | copy-done | bytes 262168
  62.6 0.1 copy-done.1
  (13 shorter events, 0.3 us)
Async XLA Ops:
  0.6 10.1 %collective-permute-start = (bf16[512,128]{1,0:T(8,128)(2,1)}, bf16[512,128]{1,0:T(8,128)(2,1)S(1)}, u32[]{:S(2)}, u32[]{:S(2)}) collective-permute-start(bf16[512,128]{1,0:T(8,128)(2,1)} %bitcast.6), channel_id=1, source_target_pairs={{0,8},{1,9},{16,24},{17,25}} | collective-permute-start | bytes 393224 | tf_op jit(solution)/shard_map/ppermute | solution.py:22
  6.6 5.9 %collective-permute-start.2 = (bf16[512,128]{1,0:T(8,128)(2,1)}, bf16[512,128]{1,0:T(8,128)(2,1)S(1)}, u32[]{:S(2)}, u32[]{:S(2)}) collective-permute-start(bf16[512,128]{1,0:T(8,128)(2,1)} %bitcast.8), channel_id=1, source_target_pairs={{0,10},{1,11},{16,26},{17,27}} | collective-permute-start | bytes 393224 | tf_op jit(solution)/shard_map/ppermute | solution.py:22
  8.2 4.4 %collective-permute-start.1 = (bf16[512,128]{1,0:T(8,128)(2,1)}, bf16[512,128]{1,0:T(8,128)(2,1)S(1)}, u32[]{:S(2)}, u32[]{:S(2)}) collective-permute-start(bf16[512,128]{1,0:T(8,128)(2,1)} %bitcast.9), channel_id=1, source_target_pairs={{0,2},{1,3},{16,18},{17,19}} | collective-permute-start | bytes 393224 | tf_op jit(solution)/shard_map/ppermute | solution.py:22
  10.8 3.5 %collective-permute-start.4 = (bf16[256,128]{1,0:T(8,128)(2,1)S(1)}, bf16[256,128]{1,0:T(8,128)(2,1)S(1)}, u32[]{:S(2)}, u32[]{:S(2)}) collective-permute-start(bf16[256,128]{1,0:T(8,128)(2,1)S(1)} %get-tuple-element.56), channel_id=1, source_target_pairs={{2,14},{3,15},{18,30},{19,31}} | collective-permute-start | bytes 196616 | tf_op jit(solution)/shard_map/ppermute | solution.py:22
  11.4 2.8 %collective-permute-start.3 = (bf16[256,128]{1,0:T(8,128)(2,1)S(1)}, bf16[256,128]{1,0:T(8,128)(2,1)S(1)}, u32[]{:S(2)}, u32[]{:S(2)}) collective-permute-start(bf16[256,128]{1,0:T(8,128)(2,1)S(1)} %get-tuple-element.56), channel_id=1, source_target_pairs={{2,10},{4,12},{6,14},{3,11},{5,13},{7,15},{18,26},{20,28},{22,30},... | collective-permute-start | bytes 196616 | tf_op jit(solution)/shard_map/ppermute | solution.py:22
  14.3 7.1 %collective-permute-start.5 = (bf16[768,128]{1,0:T(8,128)(2,1)S(1)}, bf16[768,128]{1,0:T(8,128)(2,1)S(1)}, u32[]{:S(2)}, u32[]{:S(2)}) collective-permute-start(bf16[768,128]{1,0:T(8,128)(2,1)S(1)} %pad_maximum_fusion), channel_id=1, source_target_pairs={{0,4},{2,6},{4,8},{6,10},{8,12},{10,14},{1,5},{3,7},{5,9},{7,11},{... | collective-permute-start | bytes 589832 | tf_op jit(solution)/shard_map/ppermute | solution.py:22
  17.2 5.8 %collective-permute-start.6 = (bf16[512,128]{1,0:T(8,128)(2,1)S(1)}, bf16[512,128]{1,0:T(8,128)(2,1)S(1)}, u32[]{:S(2)}, u32[]{:S(2)}) collective-permute-start(bf16[512,128]{1,0:T(8,128)(2,1)S(1)} %maximum_select_fusion), channel_id=1, source_target_pairs={{0,2},{2,0},{4,6},{6,4},{8,10},{10,8},{12,14},{14,12},{1,3},{3,1},... | collective-permute-start | bytes 393224 | tf_op jit(solution)/shard_map/ppermute | solution.py:22
  23.0 5.7 %collective-permute-start.7 = (bf16[768,128]{1,0:T(8,128)(2,1)S(1)}, bf16[768,128]{1,0:T(8,128)(2,1)S(1)}, u32[]{:S(2)}, u32[]{:S(2)}) collective-permute-start(bf16[768,128]{1,0:T(8,128)(2,1)S(1)} %pad_maximum_fusion.1), channel_id=1, source_target_pairs={{0,2},{2,0},{4,6},{6,4},{8,10},{10,8},{12,14},{14,12},{1,3},{3,1},... | collective-permute-start | bytes 589832 | tf_op jit(solution)/shard_map/ppermute | solution.py:22
  34.8 7.1 %collective-permute-start.8 = (bf16[1280,128]{1,0:T(8,128)(2,1)S(1)}, bf16[1280,128]{1,0:T(8,128)(2,1)S(1)}, u32[]{:S(2)}, u32[]{:S(2)}) collective-permute-start(bf16[1280,128]{1,0:T(8,128)(2,1)S(1)} %get-tuple-element.69), channel_id=1, source_target_pairs={{0,2},{2,0},{4,6},{6,4},{8,10},{10,8},{12,14},{14,12},{1,3},{3,1},... | collective-permute-start | bytes 983048 | tf_op jit(solution)/shard_map/ppermute | solution.py:22
  42.0 7.6 %collective-permute-start.9 = (bf16[768,128]{1,0:T(8,128)(2,1)S(1)}, bf16[768,128]{1,0:T(8,128)(2,1)S(1)}, u32[]{:S(2)}, u32[]{:S(2)}) collective-permute-start(bf16[768,128]{1,0:T(8,128)(2,1)S(1)} %pad_maximum_fusion.2), channel_id=1, source_target_pairs={{4,0},{6,2},{8,4},{10,6},{12,8},{14,10},{5,1},{7,3},{9,5},{11,7},{... | collective-permute-start | bytes 589832 | tf_op jit(solution)/shard_map/ppermute | solution.py:22
  43.3 6.3 %collective-permute-start.11 = (bf16[256,128]{1,0:T(8,128)(2,1)S(1)}, bf16[256,128]{1,0:T(8,128)(2,1)S(1)}, u32[]{:S(2)}, u32[]{:S(2)}) collective-permute-start(bf16[256,128]{1,0:T(8,128)(2,1)S(1)} %get-tuple-element.75), channel_id=1, source_target_pairs={{14,2},{15,3},{30,18},{31,19}} | collective-permute-start | bytes 196616 | tf_op jit(solution)/shard_map/ppermute | solution.py:22
  44.0 5.6 %collective-permute-start.10 = (bf16[256,128]{1,0:T(8,128)(2,1)S(1)}, bf16[256,128]{1,0:T(8,128)(2,1)S(1)}, u32[]{:S(2)}, u32[]{:S(2)}) collective-permute-start(bf16[256,128]{1,0:T(8,128)(2,1)S(1)} %get-tuple-element.76), channel_id=1, source_target_pairs={{10,2},{12,4},{14,6},{11,3},{13,5},{15,7},{26,18},{28,20},{30,22},... | collective-permute-start | bytes 196616 | tf_op jit(solution)/shard_map/ppermute | solution.py:22
  49.7 7.8 %collective-permute-start.14 = (bf16[512,128]{1,0:T(8,128)(2,1)S(1)}, bf16[512,128]{1,0:T(8,128)(2,1)S(1)}, u32[]{:S(2)}, u32[]{:S(2)}) collective-permute-start(bf16[512,128]{1,0:T(8,128)(2,1)S(1)} %add_convert_fusion), channel_id=1, source_target_pairs={{8,0},{9,1},{24,16},{25,17}} | collective-permute-start | bytes 393224 | tf_op jit(solution)/shard_map/ppermute | solution.py:22
  51.0 8.7 %collective-permute-start.13 = (bf16[512,128]{1,0:T(8,128)(2,1)S(1)}, bf16[512,128]{1,0:T(8,128)(2,1)S(1)}, u32[]{:S(2)}, u32[]{:S(2)}) collective-permute-start(bf16[512,128]{1,0:T(8,128)(2,1)S(1)} %add_convert_fusion), channel_id=1, source_target_pairs={{10,0},{11,1},{26,16},{27,17}} | collective-permute-start | bytes 393224 | tf_op jit(solution)/shard_map/ppermute | solution.py:22
  52.3 9.5 %collective-permute-start.12 = (bf16[512,128]{1,0:T(8,128)(2,1)S(1)}, bf16[512,128]{1,0:T(8,128)(2,1)S(1)}, u32[]{:S(2)}, u32[]{:S(2)}) collective-permute-start(bf16[512,128]{1,0:T(8,128)(2,1)S(1)} %add_convert_fusion), channel_id=1, source_target_pairs={{2,0},{3,1},{18,16},{19,17}} | collective-permute-start | bytes 393224 | tf_op jit(solution)/shard_map/ppermute | solution.py:22
  61.9 0.7 %copy-start = (f32[512,128]{1,0:T(8,128)}, f32[512,128]{1,0:T(8,128)S(1)}, u32[]{:S(2)}) copy-start(f32[512,128]{1,0:T(8,128)S(1)} %get-tuple-element.80) | copy-start | bytes 786436
  61.9 0.8 %copy-start.1 = (f32[512,128]{1,0:T(8,128)}, f32[512,128]{1,0:T(8,128)S(1)}, u32[]{:S(2)}) copy-start(f32[512,128]{1,0:T(8,128)S(1)} %get-tuple-element.81) | copy-start | bytes 786436

commit v8 on v7

--- a/solution.py
+++ b/solution.py
@@ -323,102 +323,113 @@
     return lax.optimization_barrier((array, *earlier))[0]
 
 
+def units(array, start, unit, count):
+    return [array[start + i * unit : start + (i + 1) * unit] for i in range(count)]
+
+
+def prompt_route(stride, size):
+    return [(i + j, i + j + stride) for i in range(0, size, 2 * stride) for j in (0, 1)]
+
+
+def collect(size, unit, rows, device, keys, values, head, held, queries):
+    even = lax.rem(device, 2) == 0
+    lower = lax.rem(device, 4) < 2
+    neighbours = [(i, i ^ 1) for i in range(size)]
+    far_route = shift_route(4, size)[1:]
+    near_route = shift_route(2, size)
+    if size == W + 1:
+        keys_far = permuted(keys, [(0, 4)])
+        values_far = permuted(values, [(0, 5)])
+        values_next = permuted(values, [(0, 1)])
+        head, queries = lax.optimization_barrier((head, queries, keys_far))[:2]
+        far = permuted(head, far_route)
+        six = permuted(head, [(1, 7)])
+        held = after(added(held, values_far, values_next, keys_far).astype(BF16), far, six)
+        second = permuted(jnp.concatenate([held, head]), near_route)
+        crossed = jnp.where(even, jnp.concatenate([head, far]), jnp.concatenate([far, six]))
+        crossed = permuted(crossed, neighbours)
+        held = jnp.where(lower, held, second[:rows])
+        third = permuted(after(jnp.concatenate([held, second[rows:]]), crossed), neighbours)
+        sources = [(0, rows), (1, rows), (2, 0), (3, 0), (2, unit), (4, 0)]
+        return held, third[:rows], sources, (third, second, crossed, far, six), queries
+    strides = [2**i for i in range(2, size.bit_length()) if 2**i < size]
+    top = strides[-1]
+    keys_far = permuted(keys, [(0, top)])
+    values_far = permuted(values, [(0, top + 1)])
+    values_next = permuted(values, [(0, 1)])
+    far = permuted(head, far_route)
+    held = added(held, values_next, values_far, keys_far).astype(BF16)
+    for stride in reversed(strides[:-1]):
+        held = added(held, permuted(held, prompt_route(stride, size))).astype(BF16)
+    second = permuted(jnp.concatenate([held, head, far]), near_route)
+    held = jnp.where(lower, held, second[:rows])
+    near, six = units(second, rows, unit, 2)
+    third = permuted(jnp.concatenate([head, near, far, six]), shift_route(1, size))
+    other = permuted(held, neighbours)
+    sources = [(0, 0), (1, rows), (0, unit), (2, 0), (0, 2 * unit), (1, rows + unit), (0, 3 * unit)]
+    return held, other, sources, (third, second, far), queries
+
+
+def give_back(size, unit, rows, device, send, keep, ready):
+    even = lax.rem(device, 2) == 0
+    lower = lax.rem(device, 4) < 2
+    neighbours = [(i, i ^ 1) for i in range(size)]
+    far_route = back(shift_route(4, size)[1:])
+    two, four, six = units(keep, rows, unit, 3)
+    if size == W + 1:
+        third = permuted(send, neighbours)
+        total = after(added(keep[:rows], third[:rows]).astype(BF16), ready)
+        near, first, last = units(third, rows, unit, 3)
+        none = jnp.zeros_like(first)
+        parts = [permuted(total, [(j, 0), (j + 1, 1)]) for j in range(2, size, 2)]
+        two = permuted(added(two, near).astype(BF16), back(shift_route(2, size)[1:]))
+        four = permuted(added(four, jnp.where(even, last, first)).astype(BF16), far_route)
+        six = permuted(added(six, jnp.where(even, none, last)).astype(BF16), [(7, 1)])
+        total = added(total, *parts).astype(BF16)
+        mine = added(jnp.where(even, first, none), two, four, six)
+        return total, permuted(total, [(1, 0)]).astype(F32), mine
+    strides = [2**i for i in range(2, size.bit_length()) if 2**i < size]
+    top = strides[-1]
+    zero, *third = units(permuted(send[rows:], back(shift_route(1, size))), 0, unit, 4)
+    total = added(keep[:rows], permuted(send[:rows], neighbours)).astype(BF16)
+    two, four, six = (added(x, y).astype(BF16) for x, y in zip((two, four, six), third))
+    second = permuted(jnp.concatenate([total, two, six]), back(shift_route(2, size)))
+    four = added(four, second[rows + unit :])
+    mine = added(zero, second[rows : rows + unit], permuted(four.astype(BF16), far_route))
+    total = added(total, jnp.where(lower, second[:rows], jnp.zeros_like(total))).astype(BF16)
+    for stride in strides[:-1]:
+        total = added(total, permuted(total, back(prompt_route(stride, size)))).astype(BF16)
+    keys_far = permuted(total, [(top, 0)])
+    values_far = permuted(total, [(top + 1, 0)])
+    values_next = permuted(total, [(1, 0)])
+    return added(total, keys_far), added(values_next, values_far), mine
+
+
 def per_device(size, queries, keys, values, grad_out, parents, lengths):
     tokens, heads_kv, head_size = keys.shape
     rows = tokens * heads_kv
     one = CAP * TILE * heads_kv
     unit = 2 * one
+    window = min(W, size - 2)
     device = lax.axis_index("node")
     even = lax.rem(device, 2) == 0
-    lower = lax.rem(device, 4) < 2
     keys = keys.reshape(rows, head_size)
     values = values.reshape(rows, head_size)
-    strides = [2**i for i in range(2, size.bit_length()) if 2**i < size]
-    top = strides[-1]
-    neighbours = [(i, i ^ 1) for i in range(size)]
-    far_route = shift_route(4, size)[1:]
-    near_route = shift_route(2, size)
-    six_route = [(1, 7)]
-    small = size == W + 1
-    if small:
-        order = [(1, 3), (2, 2), (3, 1), (4, 4), (5, 5), (6, 6)]
-        sources = [(0, rows), (1, rows), (2, 0), (3, 0), (2, unit), (4, 0)]
-        targets = [(k % 2, rows + k // 2 * unit) for k in range(6)]
-    else:
-        order = [(k, k) for k in range(1, W + 1)]
-        sources = [(0, 0), (1, rows), (0, unit), (2, 0), (0, 2 * unit), (1, rows + unit), (0, 3 * unit)]
-        targets = [(1 - k % 2, rows + (k - 1) // 2 * unit) for k in range(1, W + 1)]
-
-    def prompt_route(stride):
-        return [(i + j, i + j + stride) for i in range(0, size, 2 * stride) for j in (0, 1)]
-
-    def units(array, start, count):
-        return [array[start + i * unit : start + (i + 1) * unit] for i in range(count)]
-
+
+    order = [(k, k) for k in range(1, window + 1)]
+    if size == W + 1:
+        order[0], order[2] = (1, 3), (3, 1)
     head, held, *own = load(order, keys, values, parents, lengths, tokens)
-    keys_far = permuted(keys, [(0, top)])
-    values_far = permuted(values, [(0, top + 1)])
-    values_next = permuted(values, [(0, 1)])
-    head, queries = lax.optimization_barrier((head, queries, keys_far))[:2]
+    held, other, sources, blocks, queries = collect(size, unit, rows, device, keys, values, head, held, queries)
     qh, gh = pack(queries, grad_out, heads_kv)
-    far = permuted(head, far_route)
-    held = added(held, values_next, values_far, keys_far).astype(BF16)
-    for stride in reversed(strides[:-1]):
-        held = added(held, permuted(held, prompt_route(stride))).astype(BF16)
-    if small:
-        six = permuted(head, six_route)
-        held = after(held, far, six, qh)
-        second = permuted(jnp.concatenate([held, head]), near_route)
-        crossed = jnp.where(even, jnp.concatenate([head, far]), jnp.concatenate([far, six]))
-        crossed = permuted(crossed, neighbours)
-        held = jnp.where(lower, held, second[:rows])
-        third = permuted(after(jnp.concatenate([held, second[rows:]]), crossed), neighbours)
-        other = third[:rows]
-        blocks = (third, second, crossed, far, six)
-    else:
-        second = permuted(jnp.concatenate([held, head, far]), near_route)
-        held = jnp.where(lower, held, second[:rows])
-        third = permuted(jnp.concatenate([head, second[rows : rows + unit], far, second[rows + unit :]]), shift_route(1, size))
-        other = permuted(held, neighbours)
-        blocks = (third, second, far)
-
-    *sent, kh, ds, p_own = probs(
-        sources, targets, jnp.where(even, held, other), jnp.where(even, other, held), qh, gh, own, blocks
-    )
+    prompt_k, prompt_v = jnp.where(even, held, other), jnp.where(even, other, held)
+    targets = [(1 - k % 2, rows + (k - 1) // 2 * unit) for k in range(1, window + 1)]
+    send, keep, kh, ds, p_own = probs(sources, targets, prompt_k, prompt_v, qh, gh, own, blocks)
     grad_queries, dk, dv = grads(qh, gh, kh, ds, p_own)
-
-    send, keep = sent[:2]
-    two, four, six = units(keep, rows, 3)
-    if small:
-        third = permuted(send, neighbours)
-        total = after(added(keep[:rows], third[:rows]).astype(BF16), dk)
-        near, first, last = units(third, rows, 3)
-        none = jnp.zeros_like(first)
-        second = permuted(jnp.concatenate([total, added(two, near).astype(BF16)]), back(near_route))
-        four = added(four, jnp.where(even, last, first))
-        six = permuted(added(six, jnp.where(even, none, last)).astype(BF16), back(six_route))
-        mine = added(jnp.where(even, first, none), second[rows:], six)
-    else:
-        zero, *third = units(permuted(send[rows:], back(shift_route(1, size))), 0, 4)
-        total = added(keep[:rows], permuted(send[:rows], neighbours)).astype(BF16)
-        two, four, six = (added(x, y).astype(BF16) for x, y in zip((two, four, six), third))
-        second = permuted(jnp.concatenate([total, two, six]), back(near_route))
-        mine = added(zero, second[rows : rows + unit])
-        four = added(four, second[rows + unit :])
-    four = permuted(four.astype(BF16), back(far_route))
-    mine = added(mine, four)
-    total = added(total, jnp.where(lower, second[:rows], jnp.zeros_like(total))).astype(BF16)
-    for stride in strides[:-1]:
-        total = added(total, permuted(total, back(prompt_route(stride)))).astype(BF16)
-    if small:
-        total = after(total, four, six)
-    keys_far = permuted(total, [(top, 0)])
-    values_far = permuted(total, [(top + 1, 0)])
-    values_next = permuted(total, [(1, 0)])
-    prompt_v, prompt_k = lax.optimization_barrier((added(values_next, values_far), added(total, keys_far)))
+    prompt_k, prompt_v, mine = give_back(size, unit, rows, device, send, keep, dk)
     own = []
     for side, local, prompt in ((0, dk, prompt_k), (1, dv, prompt_v)):
-        whole = local + jnp.where(device == 0, prompt, 0.0)
+        whole = local + jnp.where(device == 0, prompt.astype(F32), 0.0)
         own.append(whole.at[:one].add(mine[side * one : (side + 1) * one]).reshape(tokens, heads_kv, head_size))
     return grad_queries, own[0], own[1]
 

time: 63 us -> 68.1 us (1.081)
  local copies, waits for them, and re-layouts: 0.78 us -> 8.2 us
  waiting for transfers between devices: 22.7 us -> 17.9 us
  other arithmetic: 0.54 us -> 3.11 us
  starting transfers between devices: 26.4 us -> 25.2 us
  Pallas kernels: 11.4 us -> 12.1 us
    unnamed x4 -> x36, local copies, waits for them, and re-layouts: 0.78 us -> 8.2 us
    ppermute x15 -> x16, waiting for transfers between devices: 22.7 us -> 17.9 us  [permuted(): return lax.ppermute(block, 'node', route)]
    convert_element_type x4 -> x3, other arithmetic: 0.22 us -> 1.98 us  [the longest x1 0.97 us: give_back(): added(two, near).astype(BF16)]
    ppermute x15 -> x16, starting transfers between devices: 26.4 us -> 25.2 us  [permuted(): return lax.ppermute(block, 'node', route)]
    add x3 -> x1, other arithmetic: 0.1 us -> 0.88 us  [added(): total = total + block.astype(F32)]
  transfers between devices with their start and end apart: 15 -> 16, of which waited for: 11 -> 9; matrix products, arithmetic and copies ran while one was open for 0% -> 3% of each run, Pallas kernels for 8% -> 8%
where the time goes in v8:
time: 68.1 us; the launch traced here: 67.5 us
  starting transfers between devices  25.2 us (37%)
  waiting for transfers between devices  17.9 us (26%)
  Pallas kernels  12.1 us (18%)
  local copies, waits for them, and re-layouts  8.2 us (12%)
  other arithmetic  3.11 us (5%)
  between operations  1.04 us (2%)
    ppermute x16, starting transfers between devices, permuted(): return lax.ppermute(block, 'node', route)  25.2 us
    ppermute x16, waiting for transfers between devices, permuted(): return lax.ppermute(block, 'node', route)  17.9 us
    pallas_call x4, Pallas kernels, call(): pl.pallas_call(kernel, in_specs=[place] * len(operands), out_specs=[VMEM]...  12.1 us
    unnamed x36, local copies, waits for them, and re-layouts  8.2 us
  transfers between devices with their start and end apart: 16, of which 9 were waited for; matrix products, arithmetic and copies ran while one was open for 3% of the time, Pallas kernels for 8%

profile of v8, /device:TPU:0, one launch (start us, length us, event | category | flops | bytes accessed | tf_op | source)
XLA Modules:
  0.0 67.5 jit_solution(8560010547166245279)
XLA Ops:
  0.6 5.9 %collective-permute-start = (bf16[512,128]{1,0:T(8,128)(2,1)}, bf16[512,128]{1,0:T(8,128)(2,1)S(1)}, u32[]{:S(2)}, u32[]{:S(2)}) collective-permute-start(bf16[512,128]{1,0:T(8,128)(2,1)} %bitcast.6), channel_id=1, source_target_pairs={{0,8},{1,9},{16,24},{17,25}} | collective-permute-start | bytes 393224 | tf_op jit(solution)/shard_map/ppermute | solution.py:22
  6.6 1.6 %collective-permute-start.1 = (bf16[512,128]{1,0:T(8,128)(2,1)}, bf16[512,128]{1,0:T(8,128)(2,1)S(1)}, u32[]{:S(2)}, u32[]{:S(2)}) collective-permute-start(bf16[512,128]{1,0:T(8,128)(2,1)} %bitcast.8), channel_id=1, source_target_pairs={{0,10},{1,11},{16,26},{17,27}} | collective-permute-start | bytes 393224 | tf_op jit(solution)/shard_map/ppermute | solution.py:22
  8.2 1.3 %collective-permute-start.2 = (bf16[512,128]{1,0:T(8,128)(2,1)}, bf16[512,128]{1,0:T(8,128)(2,1)S(1)}, u32[]{:S(2)}, u32[]{:S(2)}) collective-permute-start(bf16[512,128]{1,0:T(8,128)(2,1)} %bitcast.9), channel_id=1, source_target_pairs={{0,2},{1,3},{16,18},{17,19}} | collective-permute-start | bytes 393224 | tf_op jit(solution)/shard_map/ppermute | solution.py:22
  9.5 1.2 %load.1 = (bf16[256,128]{1,0:T(8,128)(2,1)S(1)}, bf16[512,128]{1,0:T(8,128)(2,1)S(1)}, bf16[4,128,128]{2,1,0:T(8,128)(2,1)S(1)}, bf16[4,128,128]{2,1,0:T(8,128)(...) custom-call(s32[64]{0:T(128)} %refs_0_.1, s32[64]{0:T(128)} %refs_1_.1, bf16[512,128]{1,0:T(8,128)(2,1)} %bitcast.7, ...), custom_call_target="tpu_custom_call" | custom-call | flops 1048576 | bytes 983552 | tf_op jit(solution)/shard_map/load/pallas_call | solution.py:213
  10.7 0.0 copy-start.8
  10.7 0.0 copy-start.10
  10.8 0.0 collective-permute-done
  10.8 0.7 collective-permute-start.3
  11.4 0.7 collective-permute-start.4
  12.1 0.4 collective-permute-done.1
  12.5 0.1 collective-permute-done.2
  12.5 0.1 add_convert_fusion.2
  12.7 4.5 %collective-permute-start.5 = (bf16[768,128]{1,0:T(8,128)(2,1)S(1)}, bf16[768,128]{1,0:T(8,128)(2,1)S(1)}, u32[]{:S(2)}, u32[]{:S(2)}) collective-permute-start(bf16[768,128]{1,0:T(8,128)(2,1)S(1)} %pad_maximum_fusion), channel_id=1, source_target_pairs={{0,4},{2,6},{4,8},{6,10},{8,12},{10,14},{1,5},{3,7},{5,9},{7,11},{... | collective-permute-start | bytes 589832 | tf_op jit(solution)/shard_map/ppermute | solution.py:22
  17.2 0.0 copy-start.9
  17.3 1.3 %collective-permute-start.6 = (bf16[512,128]{1,0:T(8,128)(2,1)S(1)}, bf16[512,128]{1,0:T(8,128)(2,1)S(1)}, u32[]{:S(2)}, u32[]{:S(2)}) collective-permute-start(bf16[512,128]{1,0:T(8,128)(2,1)S(1)} %maximum_select_fusion), channel_id=1, source_target_pairs={{0,2},{2,0},{4,6},{6,4},{8,10},{10,8},{12,14},{14,12},{1,3},{3,1},... | collective-permute-start | bytes 393224 | tf_op jit(solution)/shard_map/ppermute | solution.py:22
  18.6 2.9 %collective-permute-done.5.refs_9_ = bf16[768,128]{1,0:T(8,128)(2,1)S(1)} collective-permute-done((bf16[768,128]{1,0:T(8,128)(2,1)S(1)}, bf16[768,128]{1,0:T(8,128)(2,1)S(1)}, u32[]{:S(2)}, u32[]{:S(2)}) %collective-permute-start.5) | collective-permute-done | bytes 196640 | tf_op jit(solution)/shard_map/ppermute | solution.py:22
  21.5 1.0 %collective-permute-done.6.refs_10_ = bf16[512,128]{1,0:T(8,128)(2,1)S(1)} collective-permute-done((bf16[512,128]{1,0:T(8,128)(2,1)S(1)}, bf16[512,128]{1,0:T(8,128)(2,1)S(1)}, u32[]{:S(2)}, u32[]{:S(2)}) %collective-permute-start.6) | collective-permute-done | bytes 131104 | tf_op jit(solution)/shard_map/ppermute | solution.py:22
  22.5 1.0 %collective-permute-start.7 = (bf16[768,128]{1,0:T(8,128)(2,1)S(1)}, bf16[768,128]{1,0:T(8,128)(2,1)S(1)}, u32[]{:S(2)}, u32[]{:S(2)}) collective-permute-start(bf16[768,128]{1,0:T(8,128)(2,1)S(1)} %pad_maximum_fusion.1), channel_id=1, source_target_pairs={{0,2},{2,0},{4,6},{6,4},{8,10},{10,8},{12,14},{14,12},{1,3},{3,1},... | collective-permute-start | bytes 589832 | tf_op jit(solution)/shard_map/ppermute | solution.py:22
  23.5 1.6 %pack.1 = (bf16[4,1024,128]{2,1,0:T(8,128)(2,1)S(1)}, bf16[4,1024,128]{2,1,0:T(8,128)(2,1)S(1)}) custom-call(bf16[128,32,128]{2,1,0:T(8,128)(2,1)} %q_ref, bf16[128,32,128]{2,1,0:T(8,128)(2,1)} %g_ref.1), custom_call_target="tpu_custom_call" | custom-call | flops 1048576 | bytes 4194304 | tf_op jit(solution)/shard_map/pack/pallas_call | solution.py:213
  25.2 3.0 %collective-permute-done.7.refs_8_ = bf16[768,128]{1,0:T(8,128)(2,1)S(1)} collective-permute-done((bf16[768,128]{1,0:T(8,128)(2,1)S(1)}, bf16[768,128]{1,0:T(8,128)(2,1)S(1)}, u32[]{:S(2)}, u32[]{:S(2)}) %collective-permute-start.7) | collective-permute-done | bytes 196640 | tf_op jit(solution)/shard_map/ppermute | solution.py:22
  28.2 0.0 copy-start.5
  28.2 0.9 %copy-done.5 = bf16[768,128]{1,0:T(8,128)(2,1)S(1)} copy-done((bf16[768,128]{1,0:T(8,128)(2,1)S(1)}, bf16[768,128]{1,0:T(8,128)(2,1)}, u32[]{:S(2)}) %copy-start.5) | copy-done | bytes 196632
  29.2 0.8 %copy-done.7 = bf16[256,128]{1,0:T(8,128)(2,1)S(1)} copy-done((bf16[256,128]{1,0:T(8,128)(2,1)S(1)}, bf16[256,128]{1,0:T(8,128)(2,1)}, u32[]{:S(2)}) %copy-start.7) | copy-done | bytes 65560
  30.0 6.8 %probs.1 = (bf16[1280,128]{1,0:T(8,128)(2,1)}, bf16[1280,128]{1,0:T(8,128)(2,1)S(1)}, bf16[4,448,128]{2,1,0:T(8,128)(2,1)S(1)}, bf16[4,448,1024]{2,1,0:T(8,128)(2,1)S(1)}, bf16[4,128,1024]{2,1,0:T(8,128)(2,1)S(1)}) custom-call(bf16[512,128]{1,0:T(8,128)(2,1)S(1)} %get-tuple-element.75.refs_0_, bf16[512,128]{1,0:T(8,128)(2,1)S(1)} %get-tuple-element.74.refs_1_, ...), custom_call_target="tpu_custom_call" | custom-call | flops 1879048192 | bytes 9371648 | tf_op jit(solution)/shard_map/probs/pallas_call | solution.py:213
  36.8 1.8 %copy-done = bf16[4,448,1024]{2,1,0:T(8,128)(2,1)} copy-done((bf16[4,448,1024]{2,1,0:T(8,128)(2,1)}, bf16[4,448,1024]{2,1,0:T(8,128)(2,1)S(1)}, u32[]{:S(2)}) %copy-start) | copy-done | bytes 3670040
  38.6 0.8 %copy-done.2 = bf16[4,448,128]{2,1,0:T(8,128)(2,1)} copy-done((bf16[4,448,128]{2,1,0:T(8,128)(2,1)}, bf16[4,448,128]{2,1,0:T(8,128)(2,1)S(1)}, u32[]{:S(2)}) %copy-start.2) | copy-done | bytes 458776
  39.4 1.1 %collective-permute-start.8 = (bf16[1280,128]{1,0:T(8,128)(2,1)}, bf16[1280,128]{1,0:T(8,128)(2,1)}, u32[]{:S(2)}, u32[]{:S(2)}) collective-permute-start(bf16[1280,128]{1,0:T(8,128)(2,1)} %get-tuple-element.66), channel_id=1, source_target_pairs={{0,2},{2,0},{4,6},{6,4},{8,10},{10,8},{12,14},{14,12},{1,3},{3,1},... | collective-permute-start | bytes 983048 | tf_op jit(solution)/shard_map/ppermute | solution.py:22
  40.4 2.0 %copy-done.1 = bf16[4,448,1024]{2,1,0:T(8,128)(2,1)S(1)} copy-done((bf16[4,448,1024]{2,1,0:T(8,128)(2,1)S(1)}, bf16[4,448,1024]{2,1,0:T(8,128)(2,1)}, u32[]{:S(2)}) %copy-start.1) | copy-done | bytes 3670040
  42.5 1.0 %copy-done.3 = bf16[4,448,128]{2,1,0:T(8,128)(2,1)S(1)} copy-done((bf16[4,448,128]{2,1,0:T(8,128)(2,1)S(1)}, bf16[4,448,128]{2,1,0:T(8,128)(2,1)}, u32[]{:S(2)}) %copy-start.3) | copy-done | bytes 458776
  43.5 2.4 %grads.1 = (bf16[128,32,128]{2,1,0:T(8,128)(2,1)}, f32[512,128]{1,0:T(8,128)S(1)}, f32[512,128]{1,0:T(8,128)S(1)}) custom-call(bf16[4,1024,128]{2,1,0:T(8,128)(2,1)S(1)} %get-tuple-element.50.refs_4_.refs_0_, bf16[4,1024,128]{2,1,0:T(8,128)(2,1)S(1)} %get-tuple-element.51.refs_5_.refs_1_, bf16[4,448,128]{2,1,0:T(8,128)(2,1)S(1)} %copy-done.3, ...), custom_call_target="tpu_custom_call" | custom-call | flops 939524096 | bytes 8847360 | tf_op jit(solution)/shard_map/grads/pallas_call | solution.py:213
  45.9 1.1 %collective-permute-done.8 = bf16[1280,128]{1,0:T(8,128)(2,1)} collective-permute-done((bf16[1280,128]{1,0:T(8,128)(2,1)}, bf16[1280,128]{1,0:T(8,128)(2,1)}, u32[]{:S(2)}, u32[]{:S(2)}) %collective-permute-start.8) | collective-permute-done | bytes 327712 | tf_op jit(solution)/shard_map/ppermute | solution.py:22
  47.0 0.9 %add_convert_fusion.1 = bf16[512,128]{1,0:T(8,128)(2,1)S(1)} fusion(bf16[1280,128]{1,0:T(8,128)(2,1)} %collective-permute-done.8, bf16[1280,128]{1,0:T(8,128)(2,1)S(1)} %get-tuple-element.65), kind=kLoop, calls=%fused_computation.3 | loop fusion | flops 262144 | bytes 393216 | tf_op jit(solution)/shard_map/convert_element_type | solution.py:381
  47.9 1.3 %collective-permute-start.10 = (bf16[512,128]{1,0:T(8,128)(2,1)S(1)}, bf16[512,128]{1,0:T(8,128)(2,1)S(1)}, u32[]{:S(2)}, u32[]{:S(2)}) collective-permute-start(bf16[512,128]{1,0:T(8,128)(2,1)S(1)} %add_convert_fusion.1), channel_id=1, source_target_pairs={{8,0},{10,2},{9,1},{11,3},{24,16},{26,18},{25,17},{27,19}} | collective-permute-start | bytes 393224 | tf_op jit(solution)/shard_map/ppermute | solution.py:22
  49.2 1.3 %collective-permute-start.11 = (bf16[512,128]{1,0:T(8,128)(2,1)S(1)}, bf16[512,128]{1,0:T(8,128)(2,1)S(1)}, u32[]{:S(2)}, u32[]{:S(2)}) collective-permute-start(bf16[512,128]{1,0:T(8,128)(2,1)S(1)} %add_convert_fusion.1), channel_id=1, source_target_pairs={{12,0},{14,2},{13,1},{15,3},{28,16},{30,18},{29,17},{31,19}} | collective-permute-start | bytes 393224 | tf_op jit(solution)/shard_map/ppermute | solution.py:22
  50.5 1.3 %collective-permute-start.9 = (bf16[512,128]{1,0:T(8,128)(2,1)S(1)}, bf16[512,128]{1,0:T(8,128)(2,1)S(1)}, u32[]{:S(2)}, u32[]{:S(2)}) collective-permute-start(bf16[512,128]{1,0:T(8,128)(2,1)S(1)} %add_convert_fusion.1), channel_id=1, source_target_pairs={{4,0},{6,2},{5,1},{7,3},{20,16},{22,18},{21,17},{23,19}} | collective-permute-start | bytes 393224 | tf_op jit(solution)/shard_map/ppermute | solution.py:22
  51.8 1.0 %add_convert_fusion.5 = (bf16[256,128]{1,0:T(8,128)(2,1)S(1)}, bf16[256,128]{1,0:T(8,128)(2,1)S(1)}, bf16[256,128]{1,0:T(8,128)(2,1)S(1)}) fusion(bf16[1280,128]{1,0:T(8,128)(2,1)} %collective-permute-done.8, bf16[1280,128]{1,0:T(8,128)(2,1)S(1)} %get-tuple-element.65, pred[]{:T(512)S(6)} %eq.4), kind=kLoop, calls=%fused_computation.12 | loop fusion | flops 458752 | bytes 589825 | tf_op jit(solution)/shard_map/convert_element_type | solution.py:385
  52.8 0.7 collective-permute-start.12
  53.5 0.7 collective-permute-start.13
  54.1 3.6 %collective-permute-done.10 = bf16[512,128]{1,0:T(8,128)(2,1)S(1)} collective-permute-done((bf16[512,128]{1,0:T(8,128)(2,1)S(1)}, bf16[512,128]{1,0:T(8,128)(2,1)S(1)}, u32[]{:S(2)}, u32[]{:S(2)}) %collective-permute-start.10) | collective-permute-done | bytes 131104 | tf_op jit(solution)/shard_map/ppermute | solution.py:22
  57.7 0.7 collective-permute-start.14
  58.4 1.3 %collective-permute-done.11 = bf16[512,128]{1,0:T(8,128)(2,1)S(1)} collective-permute-done((bf16[512,128]{1,0:T(8,128)(2,1)S(1)}, bf16[512,128]{1,0:T(8,128)(2,1)S(1)}, u32[]{:S(2)}, u32[]{:S(2)}) %collective-permute-start.11) | collective-permute-done | bytes 131104 | tf_op jit(solution)/shard_map/ppermute | solution.py:22
  59.7 0.1 select_add_fusion.1
  59.8 1.3 %collective-permute-start.15 = (bf16[512,128]{1,0:T(8,128)(2,1)S(1)}, bf16[512,128]{1,0:T(8,128)(2,1)S(1)}, u32[]{:S(2)}, u32[]{:S(2)}) collective-permute-start(bf16[512,128]{1,0:T(8,128)(2,1)S(1)} %get-tuple-element.70), channel_id=1, source_target_pairs={{2,0},{3,1},{18,16},{19,17}} | collective-permute-start | bytes 393224 | tf_op jit(solution)/shard_map/ppermute | solution.py:22
  61.1 0.9 %convert_add_fusion = f32[256,128]{1,0:T(8,128)S(1)} fusion(bf16[256,128]{1,0:T(8,128)(2,1)S(1)} %collective-permute-done.14, bf16[256,128]{1,0:T(8,128)(2,1)S(1)} %collective-permute-done.13, bf16[256,128]{1,0:T(8,128)(2,1)S(1)} %collective-permute-done.12, pred[]{:T(512)S(6)} %eq.4, bf16[1280,128]{1,0:T(8,128)(2,1)} %collective-permute-done.8), kind=kLoop, calls=%fused_computation.9 | loop fusion | flops 262144 | bytes 393217 | tf_op jit(solution)/shard_map/add | solution.py:318
  62.0 4.6 %collective-permute-done.15 = bf16[512,128]{1,0:T(8,128)(2,1)S(1)} collective-permute-done((bf16[512,128]{1,0:T(8,128)(2,1)S(1)}, bf16[512,128]{1,0:T(8,128)(2,1)S(1)}, u32[]{:S(2)}, u32[]{:S(2)}) %collective-permute-start.15) | collective-permute-done | bytes 131104 | tf_op jit(solution)/shard_map/ppermute | solution.py:22
  66.7 0.0 copy-start.16
  66.7 0.7 %copy-done.16 = f32[512,128]{1,0:T(8,128)} copy-done((f32[512,128]{1,0:T(8,128)}, f32[512,128]{1,0:T(8,128)S(1)}, u32[]{:S(2)}) %copy-start.16) | copy-done | bytes 262168
  67.4 0.1 copy-done.17
  (37 shorter events, 0.2 us)
Async XLA Ops:
  0.6 10.1 %collective-permute-start = (bf16[512,128]{1,0:T(8,128)(2,1)}, bf16[512,128]{1,0:T(8,128)(2,1)S(1)}, u32[]{:S(2)}, u32[]{:S(2)}) collective-permute-start(bf16[512,128]{1,0:T(8,128)(2,1)} %bitcast.6), channel_id=1, source_target_pairs={{0,8},{1,9},{16,24},{17,25}} | collective-permute-start | bytes 393224 | tf_op jit(solution)/shard_map/ppermute | solution.py:22
  6.6 5.9 %collective-permute-start.1 = (bf16[512,128]{1,0:T(8,128)(2,1)}, bf16[512,128]{1,0:T(8,128)(2,1)S(1)}, u32[]{:S(2)}, u32[]{:S(2)}) collective-permute-start(bf16[512,128]{1,0:T(8,128)(2,1)} %bitcast.8), channel_id=1, source_target_pairs={{0,10},{1,11},{16,26},{17,27}} | collective-permute-start | bytes 393224 | tf_op jit(solution)/shard_map/ppermute | solution.py:22
  8.2 4.4 %collective-permute-start.2 = (bf16[512,128]{1,0:T(8,128)(2,1)}, bf16[512,128]{1,0:T(8,128)(2,1)S(1)}, u32[]{:S(2)}, u32[]{:S(2)}) collective-permute-start(bf16[512,128]{1,0:T(8,128)(2,1)} %bitcast.9), channel_id=1, source_target_pairs={{0,2},{1,3},{16,18},{17,19}} | collective-permute-start | bytes 393224 | tf_op jit(solution)/shard_map/ppermute | solution.py:22
  10.7 1.9 %copy-start.8 = (f32[448,128]{1,0:T(8,128)}, f32[448,128]{1,0:T(8,128)S(1)}, u32[]{:S(2)}) copy-start(f32[448,128]{1,0:T(8,128)S(1)} %get-tuple-element.58.refs_6_) | copy-start | bytes 688132
  10.7 2.0 %copy-start.10 = (bf16[4,128,128]{2,1,0:T(8,128)(2,1)}, bf16[4,128,128]{2,1,0:T(8,128)(2,1)S(1)}, u32[]{:S(2)}) copy-start(bf16[4,128,128]{2,1,0:T(8,128)(2,1)S(1)} %get-tuple-element.56.refs_2_) | copy-start | bytes 393220
  10.7 6.4 %copy-start.12 = (bf16[4,128,128]{2,1,0:T(8,128)(2,1)}, bf16[4,128,128]{2,1,0:T(8,128)(2,1)S(1)}, u32[]{:S(2)}) copy-start(bf16[4,128,128]{2,1,0:T(8,128)(2,1)S(1)} %get-tuple-element.57.refs_3_) | copy-start | bytes 393220
  10.7 6.4 %copy-start.14 = (f32[8,1024]{1,0:T(8,128)}, f32[8,1024]{1,0:T(8,128)S(1)}, u32[]{:S(2)}) copy-start(f32[8,1024]{1,0:T(8,128)S(1)} %get-tuple-element.59.refs_7_) | copy-start | bytes 98308
  10.8 1.8 %collective-permute-start.3 = (bf16[256,128]{1,0:T(8,128)(2,1)S(1)}, bf16[256,128]{1,0:T(8,128)(2,1)S(1)}, u32[]{:S(2)}, u32[]{:S(2)}) collective-permute-start(bf16[256,128]{1,0:T(8,128)(2,1)S(1)} %get-tuple-element.53), channel_id=1, source_target_pairs={{2,10},{4,12},{6,14},{3,11},{5,13},{7,15},{18,26},{20,28},{22,30},... | collective-permute-start | bytes 196616 | tf_op jit(solution)/shard_map/ppermute | solution.py:22
  11.4 1.2 %collective-permute-start.4 = (bf16[256,128]{1,0:T(8,128)(2,1)S(1)}, bf16[256,128]{1,0:T(8,128)(2,1)S(1)}, u32[]{:S(2)}, u32[]{:S(2)}) collective-permute-start(bf16[256,128]{1,0:T(8,128)(2,1)S(1)} %get-tuple-element.53), channel_id=1, source_target_pairs={{2,14},{3,15},{18,30},{19,31}} | collective-permute-start | bytes 196616 | tf_op jit(solution)/shard_map/ppermute | solution.py:22
  12.6 9.8 %copy-start.6 = (bf16[256,128]{1,0:T(8,128)(2,1)}, bf16[256,128]{1,0:T(8,128)(2,1)S(1)}, u32[]{:S(2)}) copy-start(bf16[256,128]{1,0:T(8,128)(2,1)S(1)} %collective-permute-done.4.refs_12_) | copy-start | bytes 196612
  12.7 8.8 %collective-permute-start.5 = (bf16[768,128]{1,0:T(8,128)(2,1)S(1)}, bf16[768,128]{1,0:T(8,128)(2,1)S(1)}, u32[]{:S(2)}, u32[]{:S(2)}) collective-permute-start(bf16[768,128]{1,0:T(8,128)(2,1)S(1)} %pad_maximum_fusion), channel_id=1, source_target_pairs={{0,4},{2,6},{4,8},{6,10},{8,12},{10,14},{1,5},{3,7},{5,9},{7,11},{... | collective-permute-start | bytes 589832 | tf_op jit(solution)/shard_map/ppermute | solution.py:22
  17.2 11.0 %copy-start.9 = (f32[448,128]{1,0:T(8,128)S(1)}, f32[448,128]{1,0:T(8,128)}, u32[]{:S(2)}) copy-start(f32[448,128]{1,0:T(8,128)} %copy-done.8) | copy-start | bytes 688132
  17.2 11.0 %copy-start.11 = (bf16[4,128,128]{2,1,0:T(8,128)(2,1)S(1)}, bf16[4,128,128]{2,1,0:T(8,128)(2,1)}, u32[]{:S(2)}) copy-start(bf16[4,128,128]{2,1,0:T(8,128)(2,1)} %copy-done.10) | copy-start | bytes 393220
  17.2 11.0 %copy-start.13 = (bf16[4,128,128]{2,1,0:T(8,128)(2,1)S(1)}, bf16[4,128,128]{2,1,0:T(8,128)(2,1)}, u32[]{:S(2)}) copy-start(bf16[4,128,128]{2,1,0:T(8,128)(2,1)} %copy-done.12) | copy-start | bytes 393220
  17.2 11.0 %copy-start.15 = (f32[8,1024]{1,0:T(8,128)S(1)}, f32[8,1024]{1,0:T(8,128)}, u32[]{:S(2)}) copy-start(f32[8,1024]{1,0:T(8,128)} %copy-done.14) | copy-start | bytes 98308
  17.3 5.2 %collective-permute-start.6 = (bf16[512,128]{1,0:T(8,128)(2,1)S(1)}, bf16[512,128]{1,0:T(8,128)(2,1)S(1)}, u32[]{:S(2)}, u32[]{:S(2)}) collective-permute-start(bf16[512,128]{1,0:T(8,128)(2,1)S(1)} %maximum_select_fusion), channel_id=1, source_target_pairs={{0,2},{2,0},{4,6},{6,4},{8,10},{10,8},{12,14},{14,12},{1,3},{3,1},... | collective-permute-start | bytes 393224 | tf_op jit(solution)/shard_map/ppermute | solution.py:22
  21.5 1.0 %copy-start.4 = (bf16[768,128]{1,0:T(8,128)(2,1)}, bf16[768,128]{1,0:T(8,128)(2,1)S(1)}, u32[]{:S(2)}) copy-start(bf16[768,128]{1,0:T(8,128)(2,1)S(1)} %collective-permute-done.5.refs_9_) | copy-start | bytes 589828
  22.5 5.7 %collective-permute-start.7 = (bf16[768,128]{1,0:T(8,128)(2,1)S(1)}, bf16[768,128]{1,0:T(8,128)(2,1)S(1)}, u32[]{:S(2)}, u32[]{:S(2)}) collective-permute-start(bf16[768,128]{1,0:T(8,128)(2,1)S(1)} %pad_maximum_fusion.1), channel_id=1, source_target_pairs={{0,2},{2,0},{4,6},{6,4},{8,10},{10,8},{12,14},{14,12},{1,3},{3,1},... | collective-permute-start | bytes 589832 | tf_op jit(solution)/shard_map/ppermute | solution.py:22
  28.2 0.9 %copy-start.5 = (bf16[768,128]{1,0:T(8,128)(2,1)S(1)}, bf16[768,128]{1,0:T(8,128)(2,1)}, u32[]{:S(2)}) copy-start(bf16[768,128]{1,0:T(8,128)(2,1)} %copy-done.4) | copy-start | bytes 589828
  29.2 0.8 %copy-start.7 = (bf16[256,128]{1,0:T(8,128)(2,1)S(1)}, bf16[256,128]{1,0:T(8,128)(2,1)}, u32[]{:S(2)}) copy-start(bf16[256,128]{1,0:T(8,128)(2,1)} %copy-done.6) | copy-start | bytes 196612
  36.8 1.8 %copy-start = (bf16[4,448,1024]{2,1,0:T(8,128)(2,1)}, bf16[4,448,1024]{2,1,0:T(8,128)(2,1)S(1)}, u32[]{:S(2)}) copy-start(bf16[4,448,1024]{2,1,0:T(8,128)(2,1)S(1)} %get-tuple-element.61.refs_3_) | copy-start | bytes 11010052
  38.6 0.8 %copy-start.2 = (bf16[4,448,128]{2,1,0:T(8,128)(2,1)}, bf16[4,448,128]{2,1,0:T(8,128)(2,1)S(1)}, u32[]{:S(2)}) copy-start(bf16[4,448,128]{2,1,0:T(8,128)(2,1)S(1)} %get-tuple-element.60.refs_2_) | copy-start | bytes 1376260
  39.4 7.6 %collective-permute-start.8 = (bf16[1280,128]{1,0:T(8,128)(2,1)}, bf16[1280,128]{1,0:T(8,128)(2,1)}, u32[]{:S(2)}, u32[]{:S(2)}) collective-permute-start(bf16[1280,128]{1,0:T(8,128)(2,1)} %get-tuple-element.66), channel_id=1, source_target_pairs={{0,2},{2,0},{4,6},{6,4},{8,10},{10,8},{12,14},{14,12},{1,3},{3,1},... | collective-permute-start | bytes 983048 | tf_op jit(solution)/shard_map/ppermute | solution.py:22
  40.4 2.0 %copy-start.1 = (bf16[4,448,1024]{2,1,0:T(8,128)(2,1)S(1)}, bf16[4,448,1024]{2,1,0:T(8,128)(2,1)}, u32[]{:S(2)}) copy-start(bf16[4,448,1024]{2,1,0:T(8,128)(2,1)} %copy-done) | copy-start | bytes 11010052
  42.5 1.0 %copy-start.3 = (bf16[4,448,128]{2,1,0:T(8,128)(2,1)S(1)}, bf16[4,448,128]{2,1,0:T(8,128)(2,1)}, u32[]{:S(2)}) copy-start(bf16[4,448,128]{2,1,0:T(8,128)(2,1)} %copy-done.2) | copy-start | bytes 1376260
  47.9 9.8 %collective-permute-start.10 = (bf16[512,128]{1,0:T(8,128)(2,1)S(1)}, bf16[512,128]{1,0:T(8,128)(2,1)S(1)}, u32[]{:S(2)}, u32[]{:S(2)}) collective-permute-start(bf16[512,128]{1,0:T(8,128)(2,1)S(1)} %add_convert_fusion.1), channel_id=1, source_target_pairs={{8,0},{10,2},{9,1},{11,3},{24,16},{26,18},{25,17},{27,19}} | collective-permute-start | bytes 393224 | tf_op jit(solution)/shard_map/ppermute | solution.py:22
  49.2 10.4 %collective-permute-start.11 = (bf16[512,128]{1,0:T(8,128)(2,1)S(1)}, bf16[512,128]{1,0:T(8,128)(2,1)S(1)}, u32[]{:S(2)}, u32[]{:S(2)}) collective-permute-start(bf16[512,128]{1,0:T(8,128)(2,1)S(1)} %add_convert_fusion.1), channel_id=1, source_target_pairs={{12,0},{14,2},{13,1},{15,3},{28,16},{30,18},{29,17},{31,19}} | collective-permute-start | bytes 393224 | tf_op jit(solution)/shard_map/ppermute | solution.py:22
  50.5 9.1 %collective-permute-start.9 = (bf16[512,128]{1,0:T(8,128)(2,1)S(1)}, bf16[512,128]{1,0:T(8,128)(2,1)S(1)}, u32[]{:S(2)}, u32[]{:S(2)}) collective-permute-start(bf16[512,128]{1,0:T(8,128)(2,1)S(1)} %add_convert_fusion.1), channel_id=1, source_target_pairs={{4,0},{6,2},{5,1},{7,3},{20,16},{22,18},{21,17},{23,19}} | collective-permute-start | bytes 393224 | tf_op jit(solution)/shard_map/ppermute | solution.py:22
  52.8 8.3 %collective-permute-start.12 = (bf16[256,128]{1,0:T(8,128)(2,1)S(1)}, bf16[256,128]{1,0:T(8,128)(2,1)S(1)}, u32[]{:S(2)}, u32[]{:S(2)}) collective-permute-start(bf16[256,128]{1,0:T(8,128)(2,1)S(1)} %get-tuple-element.71), channel_id=1, source_target_pairs={{6,2},{8,4},{10,6},{12,8},{14,10},{7,3},{9,5},{11,7},{13,9},{15,11... | collective-permute-start | bytes 196616 | tf_op jit(solution)/shard_map/ppermute | solution.py:22
  53.5 7.6 %collective-permute-start.13 = (bf16[256,128]{1,0:T(8,128)(2,1)S(1)}, bf16[256,128]{1,0:T(8,128)(2,1)S(1)}, u32[]{:S(2)}, u32[]{:S(2)}) collective-permute-start(bf16[256,128]{1,0:T(8,128)(2,1)S(1)} %get-tuple-element.73), channel_id=1, source_target_pairs={{10,2},{12,4},{14,6},{11,3},{13,5},{15,7},{26,18},{28,20},{30,22},... | collective-permute-start | bytes 196616 | tf_op jit(solution)/shard_map/ppermute | solution.py:22
  57.7 3.4 %collective-permute-start.14 = (bf16[256,128]{1,0:T(8,128)(2,1)S(1)}, bf16[256,128]{1,0:T(8,128)(2,1)S(1)}, u32[]{:S(2)}, u32[]{:S(2)}) collective-permute-start(bf16[256,128]{1,0:T(8,128)(2,1)S(1)} %get-tuple-element.72), channel_id=1, source_target_pairs={{14,2},{15,3},{30,18},{31,19}} | collective-permute-start | bytes 196616 | tf_op jit(solution)/shard_map/ppermute | solution.py:22
  59.8 6.9 %collective-permute-start.15 = (bf16[512,128]{1,0:T(8,128)(2,1)S(1)}, bf16[512,128]{1,0:T(8,128)(2,1)S(1)}, u32[]{:S(2)}, u32[]{:S(2)}) collective-permute-start(bf16[512,128]{1,0:T(8,128)(2,1)S(1)} %get-tuple-element.70), channel_id=1, source_target_pairs={{2,0},{3,1},{18,16},{19,17}} | collective-permute-start | bytes 393224 | tf_op jit(solution)/shard_map/ppermute | solution.py:22
  66.7 0.7 %copy-start.16 = (f32[512,128]{1,0:T(8,128)}, f32[512,128]{1,0:T(8,128)S(1)}, u32[]{:S(2)}) copy-start(f32[512,128]{1,0:T(8,128)S(1)} %get-tuple-element.76) | copy-start | bytes 786436
  66.7 0.8 %copy-start.17 = (f32[512,128]{1,0:T(8,128)}, f32[512,128]{1,0:T(8,128)S(1)}, u32[]{:S(2)}) copy-start(f32[512,128]{1,0:T(8,128)S(1)} %get-tuple-element.77) | copy-start | bytes 786436

commit v9 on v8

--- a/solution.py
+++ b/solution.py
@@ -216,7 +216,7 @@
         out_specs=[VMEM] * len(outputs),
         out_shape=outputs,
         scratch_shapes=scratch,
-        compiler_params=pltpu.CompilerParams(vmem_limit_bytes=28 * 1024 * 1024),
+        compiler_params=pltpu.CompilerParams(vmem_limit_bytes=16 * 1024 * 1024),
         cost_estimate=pl.CostEstimate(flops=flops, bytes_accessed=sum(sizes), transcendentals=transcendentals),
         name=name,
     )(*operands)
@@ -331,9 +331,8 @@
     return [(i + j, i + j + stride) for i in range(0, size, 2 * stride) for j in (0, 1)]
 
 
-def collect(size, unit, rows, device, keys, values, head, held, queries):
-    even = lax.rem(device, 2) == 0
-    lower = lax.rem(device, 4) < 2
+def collect(size, unit, rows, where, keys, values, head, held, queries):
+    even, lower, _ = where
     neighbours = [(i, i ^ 1) for i in range(size)]
     far_route = shift_route(4, size)[1:]
     near_route = shift_route(2, size)
@@ -370,9 +369,8 @@
     return held, other, sources, (third, second, far), queries
 
 
-def give_back(size, unit, rows, device, send, keep, ready):
-    even = lax.rem(device, 2) == 0
-    lower = lax.rem(device, 4) < 2
+def give_back(size, unit, rows, where, send, keep, ready):
+    even, lower, _ = where
     neighbours = [(i, i ^ 1) for i in range(size)]
     far_route = back(shift_route(4, size)[1:])
     two, four, six = units(keep, rows, unit, 3)
@@ -412,7 +410,6 @@
     unit = 2 * one
     window = min(W, size - 2)
     device = lax.axis_index("node")
-    even = lax.rem(device, 2) == 0
     keys = keys.reshape(rows, head_size)
     values = values.reshape(rows, head_size)
 
@@ -420,16 +417,18 @@
     if size == W + 1:
         order[0], order[2] = (1, 3), (3, 1)
     head, held, *own = load(order, keys, values, parents, lengths, tokens)
-    held, other, sources, blocks, queries = collect(size, unit, rows, device, keys, values, head, held, queries)
+    head, *where = lax.optimization_barrier((head, lax.rem(device, 2) == 0, lax.rem(device, 4) < 2, device == 0))
+    even, _, root = where
+    held, other, sources, blocks, queries = collect(size, unit, rows, where, keys, values, head, held, queries)
     qh, gh = pack(queries, grad_out, heads_kv)
     prompt_k, prompt_v = jnp.where(even, held, other), jnp.where(even, other, held)
     targets = [(1 - k % 2, rows + (k - 1) // 2 * unit) for k in range(1, window + 1)]
     send, keep, kh, ds, p_own = probs(sources, targets, prompt_k, prompt_v, qh, gh, own, blocks)
     grad_queries, dk, dv = grads(qh, gh, kh, ds, p_own)
-    prompt_k, prompt_v, mine = give_back(size, unit, rows, device, send, keep, dk)
+    prompt_k, prompt_v, mine = give_back(size, unit, rows, where, send, keep, dk)
     own = []
     for side, local, prompt in ((0, dk, prompt_k), (1, dv, prompt_v)):
-        whole = local + jnp.where(device == 0, prompt.astype(F32), 0.0)
+        whole = local + jnp.where(root, prompt.astype(F32), 0.0)
         own.append(whole.at[:one].add(mine[side * one : (side + 1) * one]).reshape(tokens, heads_kv, head_size))
     return grad_queries, own[0], own[1]
 

time: 68.1 us -> 61.6 us (0.905)
  local copies, waits for them, and re-layouts: 8.2 us -> 0.78 us
  waiting for transfers between devices: 17.9 us -> 22.6 us
  other arithmetic: 3.11 us -> 0.47 us
  Pallas kernels: 12.1 us -> 11.4 us
    unnamed x36 -> x4, local copies, waits for them, and re-layouts: 8.2 us -> 0.78 us
    ppermute x16, waiting for transfers between devices: 17.9 us -> 22.6 us  [permuted(): return lax.ppermute(block, 'node', route)]
    convert_element_type x1, other arithmetic: 0.97 us -> 0.06 us  [give_back(): added(two, near).astype(BF16)]
    convert_element_type x1, other arithmetic: 0.94 us -> 0.04 us  [give_back(): total = after(added(keep[:rows], third[:rows]).astype(BF16), ready)]
    add x1, other arithmetic: 0.88 us -> 0.04 us  [added(): total = total + block.astype(F32)]
    pallas_call x4, Pallas kernels: 12.1 us -> 11.4 us  [call(): pl.pallas_call(kernel, in_specs=[place] * len(operands), out_specs=[VMEM]...]
  transfers between devices with their start and end apart: 16 -> 16, of which waited for: 9 -> 9; matrix products, arithmetic and copies ran while one was open for 3% -> 1% of each run, Pallas kernels for 8% -> 9%
where the time goes in v9:
time: 61.6 us; the launch traced here: 61.3 us
  starting transfers between devices  25.1 us (41%)
  waiting for transfers between devices  22.6 us (37%)
  Pallas kernels  11.4 us (19%)
  between operations  0.92 us (1%)
  local copies, waits for them, and re-layouts  0.78 us (1%)
    ppermute x16, starting transfers between devices, permuted(): return lax.ppermute(block, 'node', route)  25.1 us
    ppermute x16, waiting for transfers between devices, permuted(): return lax.ppermute(block, 'node', route)  22.6 us
    pallas_call x4, Pallas kernels, call(): pl.pallas_call(kernel, in_specs=[place] * len(operands), out_specs=[VMEM]...  11.4 us
  transfers between devices with their start and end apart: 16, of which 9 were waited for; matrix products, arithmetic and copies ran while one was open for 1% of the time, Pallas kernels for 9%

profile of v9, /device:TPU:0, one launch (start us, length us, event | category | flops | bytes accessed | tf_op | source)
XLA Modules:
  0.0 61.3 jit_solution(12207707595691724328)
XLA Ops:
  0.6 5.9 %collective-permute-start = (bf16[512,128]{1,0:T(8,128)(2,1)}, bf16[512,128]{1,0:T(8,128)(2,1)S(1)}, u32[]{:S(2)}, u32[]{:S(2)}) collective-permute-start(bf16[512,128]{1,0:T(8,128)(2,1)} %bitcast.6), channel_id=1, source_target_pairs={{0,8},{1,9},{16,24},{17,25}} | collective-permute-start | bytes 393224 | tf_op jit(solution)/shard_map/ppermute | solution.py:22
  6.6 1.6 %collective-permute-start.1 = (bf16[512,128]{1,0:T(8,128)(2,1)}, bf16[512,128]{1,0:T(8,128)(2,1)S(1)}, u32[]{:S(2)}, u32[]{:S(2)}) collective-permute-start(bf16[512,128]{1,0:T(8,128)(2,1)} %bitcast.8), channel_id=1, source_target_pairs={{0,10},{1,11},{16,26},{17,27}} | collective-permute-start | bytes 393224 | tf_op jit(solution)/shard_map/ppermute | solution.py:22
  8.2 1.3 %collective-permute-start.2 = (bf16[512,128]{1,0:T(8,128)(2,1)}, bf16[512,128]{1,0:T(8,128)(2,1)S(1)}, u32[]{:S(2)}, u32[]{:S(2)}) collective-permute-start(bf16[512,128]{1,0:T(8,128)(2,1)} %bitcast.9), channel_id=1, source_target_pairs={{0,2},{1,3},{16,18},{17,19}} | collective-permute-start | bytes 393224 | tf_op jit(solution)/shard_map/ppermute | solution.py:22
  9.5 1.2 %load.1 = (bf16[256,128]{1,0:T(8,128)(2,1)S(1)}, bf16[512,128]{1,0:T(8,128)(2,1)S(1)}, bf16[4,128,128]{2,1,0:T(8,128)(2,1)S(1)}, bf16[4,128,128]{2,1,0:T(8,128)(...) custom-call(s32[64]{0:T(128)} %refs_0_.1, s32[64]{0:T(128)} %refs_1_.1, bf16[512,128]{1,0:T(8,128)(2,1)} %bitcast.7, ...), custom_call_target="tpu_custom_call" | custom-call | flops 1048576 | bytes 983552 | tf_op jit(solution)/shard_map/load/pallas_call | solution.py:213
  10.7 0.1 collective-permute-done
  10.8 0.7 %collective-permute-start.3 = (bf16[256,128]{1,0:T(8,128)(2,1)S(1)}, bf16[256,128]{1,0:T(8,128)(2,1)S(1)}, u32[]{:S(2)}, u32[]{:S(2)}) collective-permute-start(bf16[256,128]{1,0:T(8,128)(2,1)S(1)} %get-tuple-element.60), channel_id=1, source_target_pairs={{2,10},{4,12},{6,14},{3,11},{5,13},{7,15},{18,26},{20,28},{22,30},... | collective-permute-start | bytes 196616 | tf_op jit(solution)/shard_map/ppermute | solution.py:22
  11.4 0.7 %collective-permute-start.4 = (bf16[256,128]{1,0:T(8,128)(2,1)S(1)}, bf16[256,128]{1,0:T(8,128)(2,1)S(1)}, u32[]{:S(2)}, u32[]{:S(2)}) collective-permute-start(bf16[256,128]{1,0:T(8,128)(2,1)S(1)} %get-tuple-element.60), channel_id=1, source_target_pairs={{2,14},{3,15},{18,30},{19,31}} | collective-permute-start | bytes 196616 | tf_op jit(solution)/shard_map/ppermute | solution.py:22
  12.1 0.4 collective-permute-done.1
  12.5 0.1 collective-permute-done.2
  12.5 0.1 add_convert_fusion.2
  12.6 0.0 collective-permute-done.3.refs_11_
  12.6 0.0 collective-permute-done.4.refs_12_
  12.7 4.5 %collective-permute-start.5 = (bf16[768,128]{1,0:T(8,128)(2,1)S(1)}, bf16[768,128]{1,0:T(8,128)(2,1)S(1)}, u32[]{:S(2)}, u32[]{:S(2)}) collective-permute-start(bf16[768,128]{1,0:T(8,128)(2,1)S(1)} %pad_maximum_fusion), channel_id=1, source_target_pairs={{0,4},{2,6},{4,8},{6,10},{8,12},{10,14},{1,5},{3,7},{5,9},{7,11},{... | collective-permute-start | bytes 589832 | tf_op jit(solution)/shard_map/ppermute | solution.py:22
  17.2 1.3 %collective-permute-start.6 = (bf16[512,128]{1,0:T(8,128)(2,1)S(1)}, bf16[512,128]{1,0:T(8,128)(2,1)S(1)}, u32[]{:S(2)}, u32[]{:S(2)}) collective-permute-start(bf16[512,128]{1,0:T(8,128)(2,1)S(1)} %maximum_select_fusion), channel_id=1, source_target_pairs={{0,2},{2,0},{4,6},{6,4},{8,10},{10,8},{12,14},{14,12},{1,3},{3,1},... | collective-permute-start | bytes 393224 | tf_op jit(solution)/shard_map/ppermute | solution.py:22
  18.4 3.0 %collective-permute-done.5.refs_9_ = bf16[768,128]{1,0:T(8,128)(2,1)S(1)} collective-permute-done((bf16[768,128]{1,0:T(8,128)(2,1)S(1)}, bf16[768,128]{1,0:T(8,128)(2,1)S(1)}, u32[]{:S(2)}, u32[]{:S(2)}) %collective-permute-start.5) | collective-permute-done | bytes 196640 | tf_op jit(solution)/shard_map/ppermute | solution.py:22
  21.5 0.9 %collective-permute-done.6.refs_10_ = bf16[512,128]{1,0:T(8,128)(2,1)S(1)} collective-permute-done((bf16[512,128]{1,0:T(8,128)(2,1)S(1)}, bf16[512,128]{1,0:T(8,128)(2,1)S(1)}, u32[]{:S(2)}, u32[]{:S(2)}) %collective-permute-start.6) | collective-permute-done | bytes 131104 | tf_op jit(solution)/shard_map/ppermute | solution.py:22
  22.4 1.0 %collective-permute-start.7 = (bf16[768,128]{1,0:T(8,128)(2,1)S(1)}, bf16[768,128]{1,0:T(8,128)(2,1)S(1)}, u32[]{:S(2)}, u32[]{:S(2)}) collective-permute-start(bf16[768,128]{1,0:T(8,128)(2,1)S(1)} %pad_maximum_fusion.1), channel_id=1, source_target_pairs={{0,2},{2,0},{4,6},{6,4},{8,10},{10,8},{12,14},{14,12},{1,3},{3,1},... | collective-permute-start | bytes 589832 | tf_op jit(solution)/shard_map/ppermute | solution.py:22
  23.4 1.6 %pack.1 = (bf16[4,1024,128]{2,1,0:T(8,128)(2,1)S(1)}, bf16[4,1024,128]{2,1,0:T(8,128)(2,1)S(1)}) custom-call(bf16[128,32,128]{2,1,0:T(8,128)(2,1)} %q_ref, bf16[128,32,128]{2,1,0:T(8,128)(2,1)} %g_ref.1), custom_call_target="tpu_custom_call" | custom-call | flops 1048576 | bytes 4194304 | tf_op jit(solution)/shard_map/pack/pallas_call | solution.py:213
  25.1 3.0 %collective-permute-done.7.refs_8_ = bf16[768,128]{1,0:T(8,128)(2,1)S(1)} collective-permute-done((bf16[768,128]{1,0:T(8,128)(2,1)S(1)}, bf16[768,128]{1,0:T(8,128)(2,1)S(1)}, u32[]{:S(2)}, u32[]{:S(2)}) %collective-permute-start.7) | collective-permute-done | bytes 196640 | tf_op jit(solution)/shard_map/ppermute | solution.py:22
  28.1 6.1 %probs.1 = (bf16[1280,128]{1,0:T(8,128)(2,1)S(1)}, bf16[1280,128]{1,0:T(8,128)(2,1)S(1)}, bf16[4,448,128]{2,1,0:T(8,128)(2,1)S(1)}, bf16[4,448,1024]{2,1,0:T(8,128)(2,1)S(1)}, bf16[4,128,1024]{2,1,0:T(8,128)(2,1)S(1)}) custom-call(bf16[512,128]{1,0:T(8,128)(2,1)S(1)} %get-tuple-element.83.refs_0_, bf16[512,128]{1,0:T(8,128)(2,1)S(1)} %get-tuple-element.82.refs_1_, ...), custom_call_target="tpu_custom_call" | custom-call | flops 1879048192 | bytes 9371648 | tf_op jit(solution)/shard_map/probs/pallas_call | solution.py:213
  34.2 1.1 %collective-permute-start.8 = (bf16[1280,128]{1,0:T(8,128)(2,1)S(1)}, bf16[1280,128]{1,0:T(8,128)(2,1)S(1)}, u32[]{:S(2)}, u32[]{:S(2)}) collective-permute-start(bf16[1280,128]{1,0:T(8,128)(2,1)S(1)} %get-tuple-element.74), channel_id=1, source_target_pairs={{0,2},{2,0},{4,6},{6,4},{8,10},{10,8},{12,14},{14,12},{1,3},{3,1},... | collective-permute-start | bytes 983048 | tf_op jit(solution)/shard_map/ppermute | solution.py:22
  35.3 2.4 %grads.1 = (bf16[128,32,128]{2,1,0:T(8,128)(2,1)}, f32[512,128]{1,0:T(8,128)S(1)}, f32[512,128]{1,0:T(8,128)S(1)}) custom-call(bf16[4,1024,128]{2,1,0:T(8,128)(2,1)S(1)} %get-tuple-element.55.refs_4_.refs_0_, bf16[4,1024,128]{2,1,0:T(8,128)(2,1)S(1)} %get-tuple-element.56.refs_5_.refs_1_, bf16[4,448,128]{2,1,0:T(8,128)(2,1)S(1)} %get-tuple-element.67.refs_2_, ...), custom_call_target="tpu_custom_call" | custom-call | flops 939524096 | bytes 8847360 | tf_op jit(solution)/shard_map/grads/pallas_call | solution.py:213
  37.7 3.9 %collective-permute-done.8 = bf16[1280,128]{1,0:T(8,128)(2,1)S(1)} collective-permute-done((bf16[1280,128]{1,0:T(8,128)(2,1)S(1)}, bf16[1280,128]{1,0:T(8,128)(2,1)S(1)}, u32[]{:S(2)}, u32[]{:S(2)}) %collective-permute-start.8) | collective-permute-done | bytes 327712 | tf_op jit(solution)/shard_map/ppermute | solution.py:22
  41.6 1.3 %collective-permute-start.10 = (bf16[512,128]{1,0:T(8,128)(2,1)S(1)}, bf16[512,128]{1,0:T(8,128)(2,1)S(1)}, u32[]{:S(2)}, u32[]{:S(2)}) collective-permute-start(bf16[512,128]{1,0:T(8,128)(2,1)S(1)} %add_convert_fusion.1), channel_id=1, source_target_pairs={{8,0},{10,2},{9,1},{11,3},{24,16},{26,18},{25,17},{27,19}} | collective-permute-start | bytes 393224 | tf_op jit(solution)/shard_map/ppermute | solution.py:22
  42.9 1.3 %collective-permute-start.11 = (bf16[512,128]{1,0:T(8,128)(2,1)S(1)}, bf16[512,128]{1,0:T(8,128)(2,1)S(1)}, u32[]{:S(2)}, u32[]{:S(2)}) collective-permute-start(bf16[512,128]{1,0:T(8,128)(2,1)S(1)} %add_convert_fusion.1), channel_id=1, source_target_pairs={{12,0},{14,2},{13,1},{15,3},{28,16},{30,18},{29,17},{31,19}} | collective-permute-start | bytes 393224 | tf_op jit(solution)/shard_map/ppermute | solution.py:22
  44.2 1.3 %collective-permute-start.9 = (bf16[512,128]{1,0:T(8,128)(2,1)S(1)}, bf16[512,128]{1,0:T(8,128)(2,1)S(1)}, u32[]{:S(2)}, u32[]{:S(2)}) collective-permute-start(bf16[512,128]{1,0:T(8,128)(2,1)S(1)} %add_convert_fusion.1), channel_id=1, source_target_pairs={{4,0},{6,2},{5,1},{7,3},{20,16},{22,18},{21,17},{23,19}} | collective-permute-start | bytes 393224 | tf_op jit(solution)/shard_map/ppermute | solution.py:22
  45.5 0.1 add_convert_fusion.5
  45.6 0.7 %collective-permute-start.12 = (bf16[256,128]{1,0:T(8,128)(2,1)S(1)}, bf16[256,128]{1,0:T(8,128)(2,1)S(1)}, u32[]{:S(2)}, u32[]{:S(2)}) collective-permute-start(bf16[256,128]{1,0:T(8,128)(2,1)S(1)} %get-tuple-element.79), channel_id=1, source_target_pairs={{6,2},{8,4},{10,6},{12,8},{14,10},{7,3},{9,5},{11,7},{13,9},{15,11... | collective-permute-start | bytes 196616 | tf_op jit(solution)/shard_map/ppermute | solution.py:22
  46.3 0.7 %collective-permute-start.13 = (bf16[256,128]{1,0:T(8,128)(2,1)S(1)}, bf16[256,128]{1,0:T(8,128)(2,1)S(1)}, u32[]{:S(2)}, u32[]{:S(2)}) collective-permute-start(bf16[256,128]{1,0:T(8,128)(2,1)S(1)} %get-tuple-element.81), channel_id=1, source_target_pairs={{10,2},{12,4},{14,6},{11,3},{13,5},{15,7},{26,18},{28,20},{30,22},... | collective-permute-start | bytes 196616 | tf_op jit(solution)/shard_map/ppermute | solution.py:22
  46.9 5.8 %collective-permute-done.10 = bf16[512,128]{1,0:T(8,128)(2,1)S(1)} collective-permute-done((bf16[512,128]{1,0:T(8,128)(2,1)S(1)}, bf16[512,128]{1,0:T(8,128)(2,1)S(1)}, u32[]{:S(2)}, u32[]{:S(2)}) %collective-permute-start.10) | collective-permute-done | bytes 131104 | tf_op jit(solution)/shard_map/ppermute | solution.py:22
  52.8 0.7 %collective-permute-start.14 = (bf16[256,128]{1,0:T(8,128)(2,1)S(1)}, bf16[256,128]{1,0:T(8,128)(2,1)S(1)}, u32[]{:S(2)}, u32[]{:S(2)}) collective-permute-start(bf16[256,128]{1,0:T(8,128)(2,1)S(1)} %get-tuple-element.80), channel_id=1, source_target_pairs={{14,2},{15,3},{30,18},{31,19}} | collective-permute-start | bytes 196616 | tf_op jit(solution)/shard_map/ppermute | solution.py:22
  53.4 0.0 collective-permute-done.11
  53.4 0.0 collective-permute-done.9
  53.5 0.1 select_add_fusion.1
  53.6 1.3 %collective-permute-start.15 = (bf16[512,128]{1,0:T(8,128)(2,1)S(1)}, bf16[512,128]{1,0:T(8,128)(2,1)S(1)}, u32[]{:S(2)}, u32[]{:S(2)}) collective-permute-start(bf16[512,128]{1,0:T(8,128)(2,1)S(1)} %get-tuple-element.78), channel_id=1, source_target_pairs={{2,0},{3,1},{18,16},{19,17}} | collective-permute-start | bytes 393224 | tf_op jit(solution)/shard_map/ppermute | solution.py:22
  54.9 0.0 collective-permute-done.12
  54.9 0.0 collective-permute-done.13
  54.9 0.0 collective-permute-done.14
  54.9 5.5 %collective-permute-done.15 = bf16[512,128]{1,0:T(8,128)(2,1)S(1)} collective-permute-done((bf16[512,128]{1,0:T(8,128)(2,1)S(1)}, bf16[512,128]{1,0:T(8,128)(2,1)S(1)}, u32[]{:S(2)}, u32[]{:S(2)}) %collective-permute-start.15) | collective-permute-done | bytes 131104 | tf_op jit(solution)/shard_map/ppermute | solution.py:22
  60.5 0.0 copy-start
  60.5 0.0 copy-start.1
  60.5 0.7 %copy-done = f32[512,128]{1,0:T(8,128)} copy-done((f32[512,128]{1,0:T(8,128)}, f32[512,128]{1,0:T(8,128)S(1)}, u32[]{:S(2)}) %copy-start) | copy-done | bytes 262168
  61.2 0.1 copy-done.1
  (10 shorter events, 0.2 us)
Async XLA Ops:
  0.6 10.1 %collective-permute-start = (bf16[512,128]{1,0:T(8,128)(2,1)}, bf16[512,128]{1,0:T(8,128)(2,1)S(1)}, u32[]{:S(2)}, u32[]{:S(2)}) collective-permute-start(bf16[512,128]{1,0:T(8,128)(2,1)} %bitcast.6), channel_id=1, source_target_pairs={{0,8},{1,9},{16,24},{17,25}} | collective-permute-start | bytes 393224 | tf_op jit(solution)/shard_map/ppermute | solution.py:22
  6.6 5.9 %collective-permute-start.1 = (bf16[512,128]{1,0:T(8,128)(2,1)}, bf16[512,128]{1,0:T(8,128)(2,1)S(1)}, u32[]{:S(2)}, u32[]{:S(2)}) collective-permute-start(bf16[512,128]{1,0:T(8,128)(2,1)} %bitcast.8), channel_id=1, source_target_pairs={{0,10},{1,11},{16,26},{17,27}} | collective-permute-start | bytes 393224 | tf_op jit(solution)/shard_map/ppermute | solution.py:22
  8.2 4.4 %collective-permute-start.2 = (bf16[512,128]{1,0:T(8,128)(2,1)}, bf16[512,128]{1,0:T(8,128)(2,1)S(1)}, u32[]{:S(2)}, u32[]{:S(2)}) collective-permute-start(bf16[512,128]{1,0:T(8,128)(2,1)} %bitcast.9), channel_id=1, source_target_pairs={{0,2},{1,3},{16,18},{17,19}} | collective-permute-start | bytes 393224 | tf_op jit(solution)/shard_map/ppermute | solution.py:22
  10.8 1.8 %collective-permute-start.3 = (bf16[256,128]{1,0:T(8,128)(2,1)S(1)}, bf16[256,128]{1,0:T(8,128)(2,1)S(1)}, u32[]{:S(2)}, u32[]{:S(2)}) collective-permute-start(bf16[256,128]{1,0:T(8,128)(2,1)S(1)} %get-tuple-element.60), channel_id=1, source_target_pairs={{2,10},{4,12},{6,14},{3,11},{5,13},{7,15},{18,26},{20,28},{22,30},... | collective-permute-start | bytes 196616 | tf_op jit(solution)/shard_map/ppermute | solution.py:22
  11.4 1.2 %collective-permute-start.4 = (bf16[256,128]{1,0:T(8,128)(2,1)S(1)}, bf16[256,128]{1,0:T(8,128)(2,1)S(1)}, u32[]{:S(2)}, u32[]{:S(2)}) collective-permute-start(bf16[256,128]{1,0:T(8,128)(2,1)S(1)} %get-tuple-element.60), channel_id=1, source_target_pairs={{2,14},{3,15},{18,30},{19,31}} | collective-permute-start | bytes 196616 | tf_op jit(solution)/shard_map/ppermute | solution.py:22
  12.7 8.8 %collective-permute-start.5 = (bf16[768,128]{1,0:T(8,128)(2,1)S(1)}, bf16[768,128]{1,0:T(8,128)(2,1)S(1)}, u32[]{:S(2)}, u32[]{:S(2)}) collective-permute-start(bf16[768,128]{1,0:T(8,128)(2,1)S(1)} %pad_maximum_fusion), channel_id=1, source_target_pairs={{0,4},{2,6},{4,8},{6,10},{8,12},{10,14},{1,5},{3,7},{5,9},{7,11},{... | collective-permute-start | bytes 589832 | tf_op jit(solution)/shard_map/ppermute | solution.py:22
  17.2 5.2 %collective-permute-start.6 = (bf16[512,128]{1,0:T(8,128)(2,1)S(1)}, bf16[512,128]{1,0:T(8,128)(2,1)S(1)}, u32[]{:S(2)}, u32[]{:S(2)}) collective-permute-start(bf16[512,128]{1,0:T(8,128)(2,1)S(1)} %maximum_select_fusion), channel_id=1, source_target_pairs={{0,2},{2,0},{4,6},{6,4},{8,10},{10,8},{12,14},{14,12},{1,3},{3,1},... | collective-permute-start | bytes 393224 | tf_op jit(solution)/shard_map/ppermute | solution.py:22
  22.4 5.7 %collective-permute-start.7 = (bf16[768,128]{1,0:T(8,128)(2,1)S(1)}, bf16[768,128]{1,0:T(8,128)(2,1)S(1)}, u32[]{:S(2)}, u32[]{:S(2)}) collective-permute-start(bf16[768,128]{1,0:T(8,128)(2,1)S(1)} %pad_maximum_fusion.1), channel_id=1, source_target_pairs={{0,2},{2,0},{4,6},{6,4},{8,10},{10,8},{12,14},{14,12},{1,3},{3,1},... | collective-permute-start | bytes 589832 | tf_op jit(solution)/shard_map/ppermute | solution.py:22
  34.2 7.4 %collective-permute-start.8 = (bf16[1280,128]{1,0:T(8,128)(2,1)S(1)}, bf16[1280,128]{1,0:T(8,128)(2,1)S(1)}, u32[]{:S(2)}, u32[]{:S(2)}) collective-permute-start(bf16[1280,128]{1,0:T(8,128)(2,1)S(1)} %get-tuple-element.74), channel_id=1, source_target_pairs={{0,2},{2,0},{4,6},{6,4},{8,10},{10,8},{12,14},{14,12},{1,3},{3,1},... | collective-permute-start | bytes 983048 | tf_op jit(solution)/shard_map/ppermute | solution.py:22
  41.6 11.2 %collective-permute-start.10 = (bf16[512,128]{1,0:T(8,128)(2,1)S(1)}, bf16[512,128]{1,0:T(8,128)(2,1)S(1)}, u32[]{:S(2)}, u32[]{:S(2)}) collective-permute-start(bf16[512,128]{1,0:T(8,128)(2,1)S(1)} %add_convert_fusion.1), channel_id=1, source_target_pairs={{8,0},{10,2},{9,1},{11,3},{24,16},{26,18},{25,17},{27,19}} | collective-permute-start | bytes 393224 | tf_op jit(solution)/shard_map/ppermute | solution.py:22
  42.9 10.5 %collective-permute-start.11 = (bf16[512,128]{1,0:T(8,128)(2,1)S(1)}, bf16[512,128]{1,0:T(8,128)(2,1)S(1)}, u32[]{:S(2)}, u32[]{:S(2)}) collective-permute-start(bf16[512,128]{1,0:T(8,128)(2,1)S(1)} %add_convert_fusion.1), channel_id=1, source_target_pairs={{12,0},{14,2},{13,1},{15,3},{28,16},{30,18},{29,17},{31,19}} | collective-permute-start | bytes 393224 | tf_op jit(solution)/shard_map/ppermute | solution.py:22
  44.2 9.2 %collective-permute-start.9 = (bf16[512,128]{1,0:T(8,128)(2,1)S(1)}, bf16[512,128]{1,0:T(8,128)(2,1)S(1)}, u32[]{:S(2)}, u32[]{:S(2)}) collective-permute-start(bf16[512,128]{1,0:T(8,128)(2,1)S(1)} %add_convert_fusion.1), channel_id=1, source_target_pairs={{4,0},{6,2},{5,1},{7,3},{20,16},{22,18},{21,17},{23,19}} | collective-permute-start | bytes 393224 | tf_op jit(solution)/shard_map/ppermute | solution.py:22
  45.6 9.3 %collective-permute-start.12 = (bf16[256,128]{1,0:T(8,128)(2,1)S(1)}, bf16[256,128]{1,0:T(8,128)(2,1)S(1)}, u32[]{:S(2)}, u32[]{:S(2)}) collective-permute-start(bf16[256,128]{1,0:T(8,128)(2,1)S(1)} %get-tuple-element.79), channel_id=1, source_target_pairs={{6,2},{8,4},{10,6},{12,8},{14,10},{7,3},{9,5},{11,7},{13,9},{15,11... | collective-permute-start | bytes 196616 | tf_op jit(solution)/shard_map/ppermute | solution.py:22
  46.3 8.6 %collective-permute-start.13 = (bf16[256,128]{1,0:T(8,128)(2,1)S(1)}, bf16[256,128]{1,0:T(8,128)(2,1)S(1)}, u32[]{:S(2)}, u32[]{:S(2)}) collective-permute-start(bf16[256,128]{1,0:T(8,128)(2,1)S(1)} %get-tuple-element.81), channel_id=1, source_target_pairs={{10,2},{12,4},{14,6},{11,3},{13,5},{15,7},{26,18},{28,20},{30,22},... | collective-permute-start | bytes 196616 | tf_op jit(solution)/shard_map/ppermute | solution.py:22
  52.8 2.1 %collective-permute-start.14 = (bf16[256,128]{1,0:T(8,128)(2,1)S(1)}, bf16[256,128]{1,0:T(8,128)(2,1)S(1)}, u32[]{:S(2)}, u32[]{:S(2)}) collective-permute-start(bf16[256,128]{1,0:T(8,128)(2,1)S(1)} %get-tuple-element.80), channel_id=1, source_target_pairs={{14,2},{15,3},{30,18},{31,19}} | collective-permute-start | bytes 196616 | tf_op jit(solution)/shard_map/ppermute | solution.py:22
  53.6 6.9 %collective-permute-start.15 = (bf16[512,128]{1,0:T(8,128)(2,1)S(1)}, bf16[512,128]{1,0:T(8,128)(2,1)S(1)}, u32[]{:S(2)}, u32[]{:S(2)}) collective-permute-start(bf16[512,128]{1,0:T(8,128)(2,1)S(1)} %get-tuple-element.78), channel_id=1, source_target_pairs={{2,0},{3,1},{18,16},{19,17}} | collective-permute-start | bytes 393224 | tf_op jit(solution)/shard_map/ppermute | solution.py:22
  60.5 0.7 %copy-start = (f32[512,128]{1,0:T(8,128)}, f32[512,128]{1,0:T(8,128)S(1)}, u32[]{:S(2)}) copy-start(f32[512,128]{1,0:T(8,128)S(1)} %get-tuple-element.84) | copy-start | bytes 786436
  60.5 0.8 %copy-start.1 = (f32[512,128]{1,0:T(8,128)}, f32[512,128]{1,0:T(8,128)S(1)}, u32[]{:S(2)}) copy-start(f32[512,128]{1,0:T(8,128)S(1)} %get-tuple-element.85) | copy-start | bytes 786436

commit v10 on v9

--- a/solution.py
+++ b/solution.py
@@ -369,23 +369,30 @@
     return held, other, sources, (third, second, far), queries
 
 
-def give_back(size, unit, rows, where, send, keep, ready):
+def give_back(size, unit, rows, where, sent, ready):
     even, lower, _ = where
     neighbours = [(i, i ^ 1) for i in range(size)]
     far_route = back(shift_route(4, size)[1:])
+    send, keep = sent[:2]
     two, four, six = units(keep, rows, unit, 3)
     if size == W + 1:
         third = permuted(send, neighbours)
         total = after(added(keep[:rows], third[:rows]).astype(BF16), ready)
-        near, first, last = units(third, rows, unit, 3)
+        near = third[rows:]
+        first, last = units(permuted(after(sent[2], third), neighbours), 0, unit, 2)
         none = jnp.zeros_like(first)
         parts = [permuted(total, [(j, 0), (j + 1, 1)]) for j in range(2, size, 2)]
-        two = permuted(added(two, near).astype(BF16), back(shift_route(2, size)[1:]))
-        four = permuted(added(four, jnp.where(even, last, first)).astype(BF16), far_route)
-        six = permuted(added(six, jnp.where(even, none, last)).astype(BF16), [(7, 1)])
         total = added(total, *parts).astype(BF16)
-        mine = added(jnp.where(even, first, none), two, four, six)
-        return total, permuted(total, [(1, 0)]).astype(F32), mine
+        two, near, first, last, _ = lax.optimization_barrier((two, near, first, last, total))
+        two = added(two, near).astype(BF16)
+        four = added(four, jnp.where(even, last, first)).astype(BF16)
+        six = added(six, jnp.where(even, none, last)).astype(BF16)
+        two = permuted(two, back(shift_route(2, size)[1:]))
+        four = permuted(four, far_route)
+        six = permuted(six, [(7, 1)])
+        values_next = permuted(total, [(1, 0)])
+        two, four, six, values_next = lax.optimization_barrier((two, four, six, values_next))
+        return total, values_next, added(jnp.where(even, first, none), two, four, six)
     strides = [2**i for i in range(2, size.bit_length()) if 2**i < size]
     top = strides[-1]
     zero, *third = units(permuted(send[rows:], back(shift_route(1, size))), 0, unit, 4)
@@ -423,9 +430,11 @@
     qh, gh = pack(queries, grad_out, heads_kv)
     prompt_k, prompt_v = jnp.where(even, held, other), jnp.where(even, other, held)
     targets = [(1 - k % 2, rows + (k - 1) // 2 * unit) for k in range(1, window + 1)]
-    send, keep, kh, ds, p_own = probs(sources, targets, prompt_k, prompt_v, qh, gh, own, blocks)
+    if size == W + 1:
+        targets[2], targets[4] = (2, 0), (2, unit)
+    *sent, kh, ds, p_own = probs(sources, targets, prompt_k, prompt_v, qh, gh, own, blocks)
     grad_queries, dk, dv = grads(qh, gh, kh, ds, p_own)
-    prompt_k, prompt_v, mine = give_back(size, unit, rows, where, send, keep, dk)
+    prompt_k, prompt_v, mine = give_back(size, unit, rows, where, sent, dk)
     own = []
     for side, local, prompt in ((0, dk, prompt_k), (1, dv, prompt_v)):
         whole = local + jnp.where(root, prompt.astype(F32), 0.0)

time: 61.6 us -> 64.6 us (1.049)
  the two profiles are of different devices: /device:TPU:0 before, /device:TPU:10 now
where the time goes in v10:
time: 64.6 us; the launch traced here: 64.3 us
  waiting for transfers between devices  25.9 us (40%)
  starting transfers between devices  24.8 us (38%)
  Pallas kernels  11.4 us (18%)
  between operations  0.97 us (2%)
  local copies, waits for them, and re-layouts  0.81 us (1%)
    ppermute x17, waiting for transfers between devices, permuted(): return lax.ppermute(block, 'node', route)  25.9 us
    ppermute x17, starting transfers between devices, permuted(): return lax.ppermute(block, 'node', route)  24.8 us
    pallas_call x4, Pallas kernels, call(): pl.pallas_call(kernel, in_specs=[place] * len(operands), out_specs=[VMEM]...  11.4 us
  transfers between devices with their start and end apart: 17, of which 7 were waited for; matrix products, arithmetic and copies ran while one was open for 1% of the time, Pallas kernels for 8%

profile of v10, /device:TPU:10, one launch (start us, length us, event | category | flops | bytes accessed | tf_op | source)
XLA Modules:
  0.0 64.3 jit_solution(6173982263642049734)
XLA Ops:
  0.6 0.7 %collective-permute-start = (bf16[512,128]{1,0:T(8,128)(2,1)}, bf16[512,128]{1,0:T(8,128)(2,1)S(1)}, u32[]{:S(2)}, u32[]{:S(2)}) collective-permute-start(bf16[512,128]{1,0:T(8,128)(2,1)} %bitcast.6), channel_id=1, source_target_pairs={{0,8},{1,9},{16,24},{17,25}} | collective-permute-start | bytes 393224 | tf_op jit(solution)/shard_map/ppermute | solution.py:22
  1.3 0.7 %collective-permute-start.2 = (bf16[512,128]{1,0:T(8,128)(2,1)}, bf16[512,128]{1,0:T(8,128)(2,1)S(1)}, u32[]{:S(2)}, u32[]{:S(2)}) collective-permute-start(bf16[512,128]{1,0:T(8,128)(2,1)} %bitcast.8), channel_id=1, source_target_pairs={{0,2},{1,3},{16,18},{17,19}} | collective-permute-start | bytes 393224 | tf_op jit(solution)/shard_map/ppermute | solution.py:22
  2.0 0.7 %collective-permute-start.1 = (bf16[512,128]{1,0:T(8,128)(2,1)}, bf16[512,128]{1,0:T(8,128)(2,1)S(1)}, u32[]{:S(2)}, u32[]{:S(2)}) collective-permute-start(bf16[512,128]{1,0:T(8,128)(2,1)} %bitcast.9), channel_id=1, source_target_pairs={{0,10},{1,11},{16,26},{17,27}} | collective-permute-start | bytes 393224 | tf_op jit(solution)/shard_map/ppermute | solution.py:22
  2.7 1.2 %load.1 = (bf16[256,128]{1,0:T(8,128)(2,1)S(1)}, bf16[512,128]{1,0:T(8,128)(2,1)S(1)}, bf16[4,128,128]{2,1,0:T(8,128)(2,1)S(1)}, bf16[4,128,128]{2,1,0:T(8,128)(...) custom-call(s32[64]{0:T(128)} %refs_0_.1, s32[64]{0:T(128)} %refs_1_.1, bf16[512,128]{1,0:T(8,128)(2,1)} %bitcast.7, ...), custom_call_target="tpu_custom_call" | custom-call | flops 1048576 | bytes 983552 | tf_op jit(solution)/shard_map/load/pallas_call | solution.py:213
  3.9 0.0 collective-permute-done
  3.9 0.7 %collective-permute-start.4 = (bf16[256,128]{1,0:T(8,128)(2,1)S(1)}, bf16[256,128]{1,0:T(8,128)(2,1)S(1)}, u32[]{:S(2)}, u32[]{:S(2)}) collective-permute-start(bf16[256,128]{1,0:T(8,128)(2,1)S(1)} %get-tuple-element.70), channel_id=1, source_target_pairs={{2,14},{3,15},{18,30},{19,31}} | collective-permute-start | bytes 196616 | tf_op jit(solution)/shard_map/ppermute | solution.py:22
  4.6 5.1 %collective-permute-start.3 = (bf16[256,128]{1,0:T(8,128)(2,1)S(1)}, bf16[256,128]{1,0:T(8,128)(2,1)S(1)}, u32[]{:S(2)}, u32[]{:S(2)}) collective-permute-start(bf16[256,128]{1,0:T(8,128)(2,1)S(1)} %get-tuple-element.70), channel_id=1, source_target_pairs={{2,10},{4,12},{6,14},{3,11},{5,13},{7,15},{18,26},{20,28},{22,30},... | collective-permute-start | bytes 196616 | tf_op jit(solution)/shard_map/ppermute | solution.py:22
  9.7 0.0 collective-permute-done.2
  9.7 0.0 collective-permute-done.1
  9.7 0.1 add_convert_fusion.2
  9.8 0.0 collective-permute-done.4.refs_12_
  9.8 3.6 %collective-permute-done.3.refs_11_ = bf16[256,128]{1,0:T(8,128)(2,1)S(1)} collective-permute-done((bf16[256,128]{1,0:T(8,128)(2,1)S(1)}, bf16[256,128]{1,0:T(8,128)(2,1)S(1)}, u32[]{:S(2)}, u32[]{:S(2)}) %collective-permute-start.3) | collective-permute-done | bytes 65568 | tf_op jit(solution)/shard_map/ppermute | solution.py:22
  13.5 3.4 %collective-permute-start.5 = (bf16[768,128]{1,0:T(8,128)(2,1)S(1)}, bf16[768,128]{1,0:T(8,128)(2,1)S(1)}, u32[]{:S(2)}, u32[]{:S(2)}) collective-permute-start(bf16[768,128]{1,0:T(8,128)(2,1)S(1)} %pad_maximum_fusion), channel_id=1, source_target_pairs={{0,4},{2,6},{4,8},{6,10},{8,12},{10,14},{1,5},{3,7},{5,9},{7,11},{... | collective-permute-start | bytes 589832 | tf_op jit(solution)/shard_map/ppermute | solution.py:22
  16.9 0.1 collective-permute-start.6
  17.0 4.7 %collective-permute-done.5.refs_9_ = bf16[768,128]{1,0:T(8,128)(2,1)S(1)} collective-permute-done((bf16[768,128]{1,0:T(8,128)(2,1)S(1)}, bf16[768,128]{1,0:T(8,128)(2,1)S(1)}, u32[]{:S(2)}, u32[]{:S(2)}) %collective-permute-start.5) | collective-permute-done | bytes 196640 | tf_op jit(solution)/shard_map/ppermute | solution.py:22
  21.7 0.2 collective-permute-done.6.refs_10_
  22.0 0.0 collective-permute-start.7
  22.0 1.6 %pack.1 = (bf16[4,1024,128]{2,1,0:T(8,128)(2,1)S(1)}, bf16[4,1024,128]{2,1,0:T(8,128)(2,1)S(1)}) custom-call(bf16[128,32,128]{2,1,0:T(8,128)(2,1)} %q_ref, bf16[128,32,128]{2,1,0:T(8,128)(2,1)} %g_ref.1), custom_call_target="tpu_custom_call" | custom-call | flops 1048576 | bytes 4194304 | tf_op jit(solution)/shard_map/pack/pallas_call | solution.py:213
  23.6 4.0 %collective-permute-done.7.refs_8_ = bf16[768,128]{1,0:T(8,128)(2,1)S(1)} collective-permute-done((bf16[768,128]{1,0:T(8,128)(2,1)S(1)}, bf16[768,128]{1,0:T(8,128)(2,1)S(1)}, u32[]{:S(2)}, u32[]{:S(2)}) %collective-permute-start.7) | collective-permute-done | bytes 196640 | tf_op jit(solution)/shard_map/ppermute | solution.py:22
  27.7 6.1 %probs.1 = (bf16[768,128]{1,0:T(8,128)(2,1)S(1)}, bf16[1280,128]{1,0:T(8,128)(2,1)S(1)}, bf16[512,128]{1,0:T(8,128)(2,1)S(1)}, bf16[4,448,128]{2,1,0:T(8,128)(2,...) custom-call(bf16[512,128]{1,0:T(8,128)(2,1)S(1)} %get-tuple-element.102.refs_0_, ...), custom_call_target="tpu_custom_call" | custom-call | flops 1879048192 | bytes 9371648 | tf_op jit(solution)/shard_map/probs/pallas_call | solution.py:213
  33.8 0.1 collective-permute-start.8
  33.8 2.4 %grads.1 = (bf16[128,32,128]{2,1,0:T(8,128)(2,1)}, f32[512,128]{1,0:T(8,128)S(1)}, f32[512,128]{1,0:T(8,128)S(1)}) custom-call(bf16[4,1024,128]{2,1,0:T(8,128)(2,1)S(1)} %get-tuple-element.65.refs_4_.refs_0_, bf16[4,1024,128]{2,1,0:T(8,128)(2,1)S(1)} %get-tuple-element.66.refs_5_.refs_1_, bf16[4,448,128]{2,1,0:T(8,128)(2,1)S(1)} %get-tuple-element.77.refs_2_, ...), custom_call_target="tpu_custom_call" | custom-call | flops 939524096 | bytes 8847360 | tf_op jit(solution)/shard_map/grads/pallas_call | solution.py:213
  36.3 3.2 %collective-permute-done.8 = bf16[768,128]{1,0:T(8,128)(2,1)S(1)} collective-permute-done((bf16[768,128]{1,0:T(8,128)(2,1)S(1)}, bf16[768,128]{1,0:T(8,128)(2,1)S(1)}, u32[]{:S(2)}, u32[]{:S(2)}) %collective-permute-start.8) | collective-permute-done | bytes 196640 | tf_op jit(solution)/shard_map/ppermute | solution.py:22
  39.5 0.7 %collective-permute-start.11 = (bf16[512,128]{1,0:T(8,128)(2,1)S(1)}, bf16[512,128]{1,0:T(8,128)(2,1)S(1)}, u32[]{:S(2)}, u32[]{:S(2)}) collective-permute-start(bf16[512,128]{1,0:T(8,128)(2,1)S(1)} %add_convert_fusion.1), channel_id=1, source_target_pairs={{12,0},{14,2},{13,1},{15,3},{28,16},{30,18},{29,17},{31,19}} | collective-permute-start | bytes 393224 | tf_op jit(solution)/shard_map/ppermute | solution.py:22
  40.2 0.7 %collective-permute-start.10 = (bf16[512,128]{1,0:T(8,128)(2,1)S(1)}, bf16[512,128]{1,0:T(8,128)(2,1)S(1)}, u32[]{:S(2)}, u32[]{:S(2)}) collective-permute-start(bf16[512,128]{1,0:T(8,128)(2,1)S(1)} %add_convert_fusion.1), channel_id=1, source_target_pairs={{8,0},{10,2},{9,1},{11,3},{24,16},{26,18},{25,17},{27,19}} | collective-permute-start | bytes 393224 | tf_op jit(solution)/shard_map/ppermute | solution.py:22
  40.9 3.7 %collective-permute-start.9 = (bf16[512,128]{1,0:T(8,128)(2,1)S(1)}, bf16[512,128]{1,0:T(8,128)(2,1)S(1)}, u32[]{:S(2)}, u32[]{:S(2)}) collective-permute-start(bf16[512,128]{1,0:T(8,128)(2,1)S(1)} %add_convert_fusion.1), channel_id=1, source_target_pairs={{4,0},{6,2},{5,1},{7,3},{20,16},{22,18},{21,17},{23,19}} | collective-permute-start | bytes 393224 | tf_op jit(solution)/shard_map/ppermute | solution.py:22
  44.6 0.1 collective-permute-start.12
  44.7 0.0 collective-permute-done.11
  44.7 0.0 collective-permute-done.10
  44.7 4.3 %collective-permute-done.9 = bf16[512,128]{1,0:T(8,128)(2,1)S(1)} collective-permute-done((bf16[512,128]{1,0:T(8,128)(2,1)S(1)}, bf16[512,128]{1,0:T(8,128)(2,1)S(1)}, u32[]{:S(2)}, u32[]{:S(2)}) %collective-permute-start.9) | collective-permute-done | bytes 131104 | tf_op jit(solution)/shard_map/ppermute | solution.py:22
  49.1 0.1 select_add_fusion.1
  49.1 0.7 %collective-permute-start.16 = (bf16[512,128]{1,0:T(8,128)(2,1)S(1)}, bf16[512,128]{1,0:T(8,128)(2,1)S(1)}, u32[]{:S(2)}, u32[]{:S(2)}) collective-permute-start(bf16[512,128]{1,0:T(8,128)(2,1)S(1)} %get-tuple-element.98), channel_id=1, source_target_pairs={{2,0},{3,1},{18,16},{19,17}} | collective-permute-start | bytes 393224 | tf_op jit(solution)/shard_map/ppermute | solution.py:22
  49.8 0.0 collective-permute-done.12
  49.9 5.7 %collective-permute-start.13 = (bf16[256,128]{1,0:T(8,128)(2,1)S(1)}, bf16[256,128]{1,0:T(8,128)(2,1)S(1)}, u32[]{:S(2)}, u32[]{:S(2)}) collective-permute-start(bf16[256,128]{1,0:T(8,128)(2,1)S(1)} %add_convert_fusion.5), channel_id=1, source_target_pairs={{6,2},{8,4},{10,6},{12,8},{14,10},{7,3},{9,5},{11,7},{13,9},{15,11... | collective-permute-start | bytes 196616 | tf_op jit(solution)/shard_map/ppermute | solution.py:22
  55.6 0.7 %collective-permute-start.15 = (bf16[256,128]{1,0:T(8,128)(2,1)S(1)}, bf16[256,128]{1,0:T(8,128)(2,1)S(1)}, u32[]{:S(2)}, u32[]{:S(2)}) collective-permute-start(bf16[256,128]{1,0:T(8,128)(2,1)S(1)} %get-tuple-element.99), channel_id=1, source_target_pairs={{14,2},{15,3},{30,18},{31,19}} | collective-permute-start | bytes 196616 | tf_op jit(solution)/shard_map/ppermute | solution.py:22
  56.3 1.3 %collective-permute-start.14 = (bf16[256,128]{1,0:T(8,128)(2,1)S(1)}, bf16[256,128]{1,0:T(8,128)(2,1)S(1)}, u32[]{:S(2)}, u32[]{:S(2)}) collective-permute-start(bf16[256,128]{1,0:T(8,128)(2,1)S(1)} %get-tuple-element.100), channel_id=1, source_target_pairs={{10,2},{12,4},{14,6},{11,3},{13,5},{15,7},{26,18},{28,20},{30,22},... | collective-permute-start | bytes 196616 | tf_op jit(solution)/shard_map/ppermute | solution.py:22
  57.6 0.0 collective-permute-done.13
  57.6 0.0 collective-permute-done.15
  57.7 5.7 %collective-permute-done.14 = bf16[256,128]{1,0:T(8,128)(2,1)S(1)} collective-permute-done((bf16[256,128]{1,0:T(8,128)(2,1)S(1)}, bf16[256,128]{1,0:T(8,128)(2,1)S(1)}, u32[]{:S(2)}, u32[]{:S(2)}) %collective-permute-start.14) | collective-permute-done | bytes 65568 | tf_op jit(solution)/shard_map/ppermute | solution.py:22
  63.4 0.0 collective-permute-done.16
  63.5 0.0 copy-start
  63.5 0.0 copy-start.1
  63.5 0.7 %copy-done = f32[512,128]{1,0:T(8,128)} copy-done((f32[512,128]{1,0:T(8,128)}, f32[512,128]{1,0:T(8,128)S(1)}, u32[]{:S(2)}) %copy-start) | copy-done | bytes 262168
  64.2 0.1 copy-done.1
  (15 shorter events, 0.3 us)
Async XLA Ops:
  0.6 3.3 %collective-permute-start = (bf16[512,128]{1,0:T(8,128)(2,1)}, bf16[512,128]{1,0:T(8,128)(2,1)S(1)}, u32[]{:S(2)}, u32[]{:S(2)}) collective-permute-start(bf16[512,128]{1,0:T(8,128)(2,1)} %bitcast.6), channel_id=1, source_target_pairs={{0,8},{1,9},{16,24},{17,25}} | collective-permute-start | bytes 393224 | tf_op jit(solution)/shard_map/ppermute | solution.py:22
  1.3 8.4 %collective-permute-start.2 = (bf16[512,128]{1,0:T(8,128)(2,1)}, bf16[512,128]{1,0:T(8,128)(2,1)S(1)}, u32[]{:S(2)}, u32[]{:S(2)}) collective-permute-start(bf16[512,128]{1,0:T(8,128)(2,1)} %bitcast.8), channel_id=1, source_target_pairs={{0,2},{1,3},{16,18},{17,19}} | collective-permute-start | bytes 393224 | tf_op jit(solution)/shard_map/ppermute | solution.py:22
  2.0 7.7 %collective-permute-start.1 = (bf16[512,128]{1,0:T(8,128)(2,1)}, bf16[512,128]{1,0:T(8,128)(2,1)S(1)}, u32[]{:S(2)}, u32[]{:S(2)}) collective-permute-start(bf16[512,128]{1,0:T(8,128)(2,1)} %bitcast.9), channel_id=1, source_target_pairs={{0,10},{1,11},{16,26},{17,27}} | collective-permute-start | bytes 393224 | tf_op jit(solution)/shard_map/ppermute | solution.py:22
  3.9 5.9 %collective-permute-start.4 = (bf16[256,128]{1,0:T(8,128)(2,1)S(1)}, bf16[256,128]{1,0:T(8,128)(2,1)S(1)}, u32[]{:S(2)}, u32[]{:S(2)}) collective-permute-start(bf16[256,128]{1,0:T(8,128)(2,1)S(1)} %get-tuple-element.70), channel_id=1, source_target_pairs={{2,14},{3,15},{18,30},{19,31}} | collective-permute-start | bytes 196616 | tf_op jit(solution)/shard_map/ppermute | solution.py:22
  4.6 8.9 %collective-permute-start.3 = (bf16[256,128]{1,0:T(8,128)(2,1)S(1)}, bf16[256,128]{1,0:T(8,128)(2,1)S(1)}, u32[]{:S(2)}, u32[]{:S(2)}) collective-permute-start(bf16[256,128]{1,0:T(8,128)(2,1)S(1)} %get-tuple-element.70), channel_id=1, source_target_pairs={{2,10},{4,12},{6,14},{3,11},{5,13},{7,15},{18,26},{20,28},{22,30},... | collective-permute-start | bytes 196616 | tf_op jit(solution)/shard_map/ppermute | solution.py:22
  13.5 8.2 %collective-permute-start.5 = (bf16[768,128]{1,0:T(8,128)(2,1)S(1)}, bf16[768,128]{1,0:T(8,128)(2,1)S(1)}, u32[]{:S(2)}, u32[]{:S(2)}) collective-permute-start(bf16[768,128]{1,0:T(8,128)(2,1)S(1)} %pad_maximum_fusion), channel_id=1, source_target_pairs={{0,4},{2,6},{4,8},{6,10},{8,12},{10,14},{1,5},{3,7},{5,9},{7,11},{... | collective-permute-start | bytes 589832 | tf_op jit(solution)/shard_map/ppermute | solution.py:22
  16.9 5.0 %collective-permute-start.6 = (bf16[512,128]{1,0:T(8,128)(2,1)S(1)}, bf16[512,128]{1,0:T(8,128)(2,1)S(1)}, u32[]{:S(2)}, u32[]{:S(2)}) collective-permute-start(bf16[512,128]{1,0:T(8,128)(2,1)S(1)} %maximum_select_fusion), channel_id=1, source_target_pairs={{0,2},{2,0},{4,6},{6,4},{8,10},{10,8},{12,14},{14,12},{1,3},{3,1},... | collective-permute-start | bytes 393224 | tf_op jit(solution)/shard_map/ppermute | solution.py:22
  22.0 5.7 %collective-permute-start.7 = (bf16[768,128]{1,0:T(8,128)(2,1)S(1)}, bf16[768,128]{1,0:T(8,128)(2,1)S(1)}, u32[]{:S(2)}, u32[]{:S(2)}) collective-permute-start(bf16[768,128]{1,0:T(8,128)(2,1)S(1)} %pad_maximum_fusion.1), channel_id=1, source_target_pairs={{0,2},{2,0},{4,6},{6,4},{8,10},{10,8},{12,14},{14,12},{1,3},{3,1},... | collective-permute-start | bytes 589832 | tf_op jit(solution)/shard_map/ppermute | solution.py:22
  33.8 5.7 %collective-permute-start.8 = (bf16[768,128]{1,0:T(8,128)(2,1)S(1)}, bf16[768,128]{1,0:T(8,128)(2,1)S(1)}, u32[]{:S(2)}, u32[]{:S(2)}) collective-permute-start(bf16[768,128]{1,0:T(8,128)(2,1)S(1)} %get-tuple-element.84), channel_id=1, source_target_pairs={{0,2},{2,0},{4,6},{6,4},{8,10},{10,8},{12,14},{14,12},{1,3},{3,1},... | collective-permute-start | bytes 589832 | tf_op jit(solution)/shard_map/ppermute | solution.py:22
  39.5 5.2 %collective-permute-start.11 = (bf16[512,128]{1,0:T(8,128)(2,1)S(1)}, bf16[512,128]{1,0:T(8,128)(2,1)S(1)}, u32[]{:S(2)}, u32[]{:S(2)}) collective-permute-start(bf16[512,128]{1,0:T(8,128)(2,1)S(1)} %add_convert_fusion.1), channel_id=1, source_target_pairs={{12,0},{14,2},{13,1},{15,3},{28,16},{30,18},{29,17},{31,19}} | collective-permute-start | bytes 393224 | tf_op jit(solution)/shard_map/ppermute | solution.py:22
  40.2 4.5 %collective-permute-start.10 = (bf16[512,128]{1,0:T(8,128)(2,1)S(1)}, bf16[512,128]{1,0:T(8,128)(2,1)S(1)}, u32[]{:S(2)}, u32[]{:S(2)}) collective-permute-start(bf16[512,128]{1,0:T(8,128)(2,1)S(1)} %add_convert_fusion.1), channel_id=1, source_target_pairs={{8,0},{10,2},{9,1},{11,3},{24,16},{26,18},{25,17},{27,19}} | collective-permute-start | bytes 393224 | tf_op jit(solution)/shard_map/ppermute | solution.py:22
  40.9 8.2 %collective-permute-start.9 = (bf16[512,128]{1,0:T(8,128)(2,1)S(1)}, bf16[512,128]{1,0:T(8,128)(2,1)S(1)}, u32[]{:S(2)}, u32[]{:S(2)}) collective-permute-start(bf16[512,128]{1,0:T(8,128)(2,1)S(1)} %add_convert_fusion.1), channel_id=1, source_target_pairs={{4,0},{6,2},{5,1},{7,3},{20,16},{22,18},{21,17},{23,19}} | collective-permute-start | bytes 393224 | tf_op jit(solution)/shard_map/ppermute | solution.py:22
  44.6 5.2 %collective-permute-start.12 = (bf16[512,128]{1,0:T(8,128)(2,1)S(1)}, bf16[512,128]{1,0:T(8,128)(2,1)S(1)}, u32[]{:S(2)}, u32[]{:S(2)}) collective-permute-start(bf16[512,128]{1,0:T(8,128)(2,1)S(1)} %get-tuple-element.87), channel_id=1, source_target_pairs={{0,2},{2,0},{4,6},{6,4},{8,10},{10,8},{12,14},{14,12},{1,3},{3,1},... | collective-permute-start | bytes 393224 | tf_op jit(solution)/shard_map/ppermute | solution.py:22
  49.1 14.2 %collective-permute-start.16 = (bf16[512,128]{1,0:T(8,128)(2,1)S(1)}, bf16[512,128]{1,0:T(8,128)(2,1)S(1)}, u32[]{:S(2)}, u32[]{:S(2)}) collective-permute-start(bf16[512,128]{1,0:T(8,128)(2,1)S(1)} %get-tuple-element.98), channel_id=1, source_target_pairs={{2,0},{3,1},{18,16},{19,17}} | collective-permute-start | bytes 393224 | tf_op jit(solution)/shard_map/ppermute | solution.py:22
  49.9 7.8 %collective-permute-start.13 = (bf16[256,128]{1,0:T(8,128)(2,1)S(1)}, bf16[256,128]{1,0:T(8,128)(2,1)S(1)}, u32[]{:S(2)}, u32[]{:S(2)}) collective-permute-start(bf16[256,128]{1,0:T(8,128)(2,1)S(1)} %add_convert_fusion.5), channel_id=1, source_target_pairs={{6,2},{8,4},{10,6},{12,8},{14,10},{7,3},{9,5},{11,7},{13,9},{15,11... | collective-permute-start | bytes 196616 | tf_op jit(solution)/shard_map/ppermute | solution.py:22
  55.6 2.0 %collective-permute-start.15 = (bf16[256,128]{1,0:T(8,128)(2,1)S(1)}, bf16[256,128]{1,0:T(8,128)(2,1)S(1)}, u32[]{:S(2)}, u32[]{:S(2)}) collective-permute-start(bf16[256,128]{1,0:T(8,128)(2,1)S(1)} %get-tuple-element.99), channel_id=1, source_target_pairs={{14,2},{15,3},{30,18},{31,19}} | collective-permute-start | bytes 196616 | tf_op jit(solution)/shard_map/ppermute | solution.py:22
  56.3 7.1 %collective-permute-start.14 = (bf16[256,128]{1,0:T(8,128)(2,1)S(1)}, bf16[256,128]{1,0:T(8,128)(2,1)S(1)}, u32[]{:S(2)}, u32[]{:S(2)}) collective-permute-start(bf16[256,128]{1,0:T(8,128)(2,1)S(1)} %get-tuple-element.100), channel_id=1, source_target_pairs={{10,2},{12,4},{14,6},{11,3},{13,5},{15,7},{26,18},{28,20},{30,22},... | collective-permute-start | bytes 196616 | tf_op jit(solution)/shard_map/ppermute | solution.py:22
  63.5 0.7 %copy-start = (f32[512,128]{1,0:T(8,128)}, f32[512,128]{1,0:T(8,128)S(1)}, u32[]{:S(2)}) copy-start(f32[512,128]{1,0:T(8,128)S(1)} %get-tuple-element.103) | copy-start | bytes 786436
  63.5 0.8 %copy-start.1 = (f32[512,128]{1,0:T(8,128)}, f32[512,128]{1,0:T(8,128)S(1)}, u32[]{:S(2)}) copy-start(f32[512,128]{1,0:T(8,128)S(1)} %get-tuple-element.104) | copy-start | bytes 786436

commit v11 on v9

--- a/solution.py
+++ b/solution.py
@@ -104,7 +104,7 @@
     prompt_k, prompt_v, own_k, own_v, qh, gh, bias, weight_ref = refs[:8]
     n_in = 1 + max(source for source, _ in sources)
     n_out = 1 + max(target for target, _ in targets)
-    blocks = refs[8 : 8 + n_in]
+    blocks_in = refs[8 : 8 + n_in]
     outs = refs[8 + n_in : 8 + n_in + n_out]
     kh, ds_ref, p_own, vh, p_ref, grads, wide = refs[8 + n_in + n_out :]
     window = len(sources)
@@ -118,32 +118,42 @@
         split_heads(prompt[...], heads_ref, 0, tokens, heads_kv, wide)
         for k, (source, start) in enumerate(sources):
             start += side * front * heads_kv
-            block = blocks[source][start : start + front * heads_kv]
+            block = blocks_in[source][start : start + front * heads_kv]
             split_heads(block, heads_ref, tokens + k * front, front, heads_kv, wide)
         heads_ref[:, before:] = own[...]
 
     column_token = lax.broadcasted_iota(jnp.int32, (CHUNK, columns), 1) // 8
     causal = jnp.where(lax.broadcasted_iota(jnp.int32, (CHUNK, columns), 0) <= column_token, 0.0, MASKED)
-    for head in range(heads_kv):
-        for c in range(tokens // CHUNK):
-            rows = before + (c + 1) * CHUNK
-            span = slice(c * columns, (c + 1) * columns)
-            q = qh[head, span]
-            g = gh[head, span]
-            s = lax.dot_general(kh[head, :rows], q, (((1,), (1,)), ((), ())), preferred_element_type=F32)
-            dp = lax.dot_general(vh[head, :rows], g, (((1,), (1,)), ((), ())), preferred_element_type=F32)
-            s = s + jnp.concatenate([bias[:rows]] * (columns // 128), axis=1)
-            s = jnp.concatenate([s[: rows - CHUNK], s[rows - CHUNK :] + causal], axis=0)
-            top = jnp.max(s, axis=0, keepdims=True)
-            e = jnp.exp2((s - top) * (scale * math.log2(math.e)))
-            total = jnp.sum(e, axis=0, keepdims=True)
-            p = e * (weight_ref[:1, span] / total)
-            delta = jnp.sum(p * dp, axis=0, keepdims=True)
-            ds_ref[head, :rows, span] = (p * (dp - delta) * scale).astype(BF16)
-            p_ref[:, span] = p[:before].astype(BF16)
-            p_own[head, : rows - before, span] = p[before:].astype(BF16)
-        grads[0, head] = jnp.dot(ds_ref[head, :before], qh[head], preferred_element_type=F32)
-        grads[1, head] = jnp.dot(p_ref[...], gh[head], preferred_element_type=F32)
+    blocks = [(head, c) for head in range(heads_kv) for c in range(tokens // CHUNK)]
+
+    def scores(head, c):
+        rows = before + (c + 1) * CHUNK
+        span = slice(c * columns, (c + 1) * columns)
+        outer = (((1,), (1,)), ((), ()))
+        s = lax.dot_general(kh[head, :rows], qh[head, span], outer, preferred_element_type=F32)
+        dp = lax.dot_general(vh[head, :rows], gh[head, span], outer, preferred_element_type=F32)
+        return s, dp
+
+    coming = scores(*blocks[0])
+    for i, (head, c) in enumerate(blocks):
+        s, dp = coming
+        if i + 1 < len(blocks):
+            coming = scores(*blocks[i + 1])
+        rows = before + (c + 1) * CHUNK
+        span = slice(c * columns, (c + 1) * columns)
+        s = s + jnp.concatenate([bias[:rows]] * (columns // 128), axis=1)
+        s = jnp.concatenate([s[: rows - CHUNK], s[rows - CHUNK :] + causal], axis=0)
+        top = jnp.max(s, axis=0, keepdims=True)
+        e = jnp.exp2((s - top) * (scale * math.log2(math.e)))
+        total = jnp.sum(e, axis=0, keepdims=True)
+        p = e * (weight_ref[:1, span] / total)
+        delta = jnp.sum(p * dp, axis=0, keepdims=True)
+        ds_ref[head, :rows, span] = (p * (dp - delta)).astype(BF16)
+        p_ref[head % 2, :, span] = p[:before].astype(BF16)
+        p_own[head, : rows - before, span] = p[before:].astype(BF16)
+        if c == tokens // CHUNK - 1:
+            grads[0, head] = scale * jnp.dot(ds_ref[head, :before], qh[head], preferred_element_type=F32)
+            grads[1, head] = jnp.dot(p_ref[head % 2], gh[head], preferred_element_type=F32)
 
     rows = tokens * heads_kv
     rows_front = front * heads_kv
@@ -167,7 +177,7 @@
             outs[target][start : start + rows_front] = block
 
 
-def grads_kernel(heads_kv, *refs):
+def grads_kernel(heads_kv, scale, *refs):
     qh, gh, kh, ds_ref, p_own, dq_ref, dk_ref, dv_ref, wide = refs
     tokens = TD * TILE
     before = kh.shape[1] - tokens
@@ -183,7 +193,7 @@
                 dq = lax.dot_general(
                     kh[head, :rows], ds_ref[head, :rows, span], (((0,), (0,)), ((), ())), preferred_element_type=F32
                 )
-                parts.append(dq.T.reshape(CHUNK, 8, 128))
+                parts.append((scale * dq.T).reshape(CHUNK, 8, 128))
             dq_ref[c * CHUNK : (c + 1) * CHUNK, pair * 16 : (pair + 1) * 16] = jnp.concatenate(parts, axis=1).astype(BF16)
         for head in (2 * pair, 2 * pair + 1):
             for source, factor, out in ((ds_ref.at[head, before:], qh, dk), (p_own.at[head], gh, dv)):
@@ -196,7 +206,7 @@
                         )
                     )
                 out.append(jnp.concatenate(pieces, axis=0))
-    dk_ref[...] = join_heads(dk, tokens, heads_kv, wide)
+    dk_ref[...] = scale * join_heads(dk, tokens, heads_kv, wide)
     dv_ref[...] = join_heads(dv, tokens, heads_kv, wide)
 
 
@@ -277,7 +287,7 @@
         ],
         [
             pltpu.VMEM((heads_kv, before + tokens, head_size), BF16),
-            pltpu.VMEM((before, tokens * 8), BF16),
+            pltpu.VMEM((2, before, tokens * 8), BF16),
             pltpu.VMEM((2, heads_kv, before, head_size), F32),
             pltpu.VMEM((rows, head_size), F32),
         ],
@@ -291,7 +301,7 @@
     head_size = kh.shape[2]
     array = jax.ShapeDtypeStruct
     return call(
-        functools.partial(grads_kernel, heads_kv),
+        functools.partial(grads_kernel, heads_kv, head_size**-0.5),
         "grads",
         (qh, gh, kh, ds, p_own),
         [

time: 61.6 us -> 61.4 us (level)
  no operation moved by 1% of the time
where the time goes in v11:
time: 61.4 us; the launch traced here: 61.1 us
  starting transfers between devices  25.1 us (41%)
  waiting for transfers between devices  22.6 us (37%)
  Pallas kernels  11.1 us (18%)
  between operations  0.92 us (1%)
  local copies, waits for them, and re-layouts  0.78 us (1%)
    ppermute x16, starting transfers between devices, permuted(): return lax.ppermute(block, 'node', route)  25.1 us
    ppermute x16, waiting for transfers between devices, permuted(): return lax.ppermute(block, 'node', route)  22.6 us
    pallas_call x4, Pallas kernels, call(): pl.pallas_call(kernel, in_specs=[place] * len(operands), out_specs=[VMEM]...  11.1 us
  transfers between devices with their start and end apart: 16, of which 9 were waited for; matrix products, arithmetic and copies ran while one was open for 1% of the time, Pallas kernels for 9%

profile of v11, /device:TPU:0, one launch (start us, length us, event | category | flops | bytes accessed | tf_op | source)
XLA Modules:
  0.0 61.1 jit_solution(12137882750281359425)
XLA Ops:
  0.6 5.9 %collective-permute-start = (bf16[512,128]{1,0:T(8,128)(2,1)}, bf16[512,128]{1,0:T(8,128)(2,1)S(1)}, u32[]{:S(2)}, u32[]{:S(2)}) collective-permute-start(bf16[512,128]{1,0:T(8,128)(2,1)} %bitcast.6), channel_id=1, source_target_pairs={{0,8},{1,9},{16,24},{17,25}} | collective-permute-start | bytes 393224 | tf_op jit(solution)/shard_map/ppermute | solution.py:22
  6.6 1.6 %collective-permute-start.1 = (bf16[512,128]{1,0:T(8,128)(2,1)}, bf16[512,128]{1,0:T(8,128)(2,1)S(1)}, u32[]{:S(2)}, u32[]{:S(2)}) collective-permute-start(bf16[512,128]{1,0:T(8,128)(2,1)} %bitcast.8), channel_id=1, source_target_pairs={{0,10},{1,11},{16,26},{17,27}} | collective-permute-start | bytes 393224 | tf_op jit(solution)/shard_map/ppermute | solution.py:22
  8.2 1.3 %collective-permute-start.2 = (bf16[512,128]{1,0:T(8,128)(2,1)}, bf16[512,128]{1,0:T(8,128)(2,1)S(1)}, u32[]{:S(2)}, u32[]{:S(2)}) collective-permute-start(bf16[512,128]{1,0:T(8,128)(2,1)} %bitcast.9), channel_id=1, source_target_pairs={{0,2},{1,3},{16,18},{17,19}} | collective-permute-start | bytes 393224 | tf_op jit(solution)/shard_map/ppermute | solution.py:22
  9.5 1.2 %load.1 = (bf16[256,128]{1,0:T(8,128)(2,1)S(1)}, bf16[512,128]{1,0:T(8,128)(2,1)S(1)}, bf16[4,128,128]{2,1,0:T(8,128)(2,1)S(1)}, bf16[4,128,128]{2,1,0:T(8,128)(...) custom-call(s32[64]{0:T(128)} %refs_0_.1, s32[64]{0:T(128)} %refs_1_.1, bf16[512,128]{1,0:T(8,128)(2,1)} %bitcast.7, ...), custom_call_target="tpu_custom_call" | custom-call | flops 1048576 | bytes 983552 | tf_op jit(solution)/shard_map/load/pallas_call | solution.py:223
  10.7 0.1 collective-permute-done
  10.8 0.7 %collective-permute-start.3 = (bf16[256,128]{1,0:T(8,128)(2,1)S(1)}, bf16[256,128]{1,0:T(8,128)(2,1)S(1)}, u32[]{:S(2)}, u32[]{:S(2)}) collective-permute-start(bf16[256,128]{1,0:T(8,128)(2,1)S(1)} %get-tuple-element.60), channel_id=1, source_target_pairs={{2,10},{4,12},{6,14},{3,11},{5,13},{7,15},{18,26},{20,28},{22,30},... | collective-permute-start | bytes 196616 | tf_op jit(solution)/shard_map/ppermute | solution.py:22
  11.4 0.7 %collective-permute-start.4 = (bf16[256,128]{1,0:T(8,128)(2,1)S(1)}, bf16[256,128]{1,0:T(8,128)(2,1)S(1)}, u32[]{:S(2)}, u32[]{:S(2)}) collective-permute-start(bf16[256,128]{1,0:T(8,128)(2,1)S(1)} %get-tuple-element.60), channel_id=1, source_target_pairs={{2,14},{3,15},{18,30},{19,31}} | collective-permute-start | bytes 196616 | tf_op jit(solution)/shard_map/ppermute | solution.py:22
  12.1 0.4 collective-permute-done.1
  12.5 0.1 collective-permute-done.2
  12.5 0.1 add_convert_fusion.2
  12.6 0.0 collective-permute-done.3.refs_11_
  12.6 0.0 collective-permute-done.4.refs_12_
  12.7 4.5 %collective-permute-start.5 = (bf16[768,128]{1,0:T(8,128)(2,1)S(1)}, bf16[768,128]{1,0:T(8,128)(2,1)S(1)}, u32[]{:S(2)}, u32[]{:S(2)}) collective-permute-start(bf16[768,128]{1,0:T(8,128)(2,1)S(1)} %pad_maximum_fusion), channel_id=1, source_target_pairs={{0,4},{2,6},{4,8},{6,10},{8,12},{10,14},{1,5},{3,7},{5,9},{7,11},{... | collective-permute-start | bytes 589832 | tf_op jit(solution)/shard_map/ppermute | solution.py:22
  17.2 1.3 %collective-permute-start.6 = (bf16[512,128]{1,0:T(8,128)(2,1)S(1)}, bf16[512,128]{1,0:T(8,128)(2,1)S(1)}, u32[]{:S(2)}, u32[]{:S(2)}) collective-permute-start(bf16[512,128]{1,0:T(8,128)(2,1)S(1)} %maximum_select_fusion), channel_id=1, source_target_pairs={{0,2},{2,0},{4,6},{6,4},{8,10},{10,8},{12,14},{14,12},{1,3},{3,1},... | collective-permute-start | bytes 393224 | tf_op jit(solution)/shard_map/ppermute | solution.py:22
  18.4 3.0 %collective-permute-done.5.refs_9_ = bf16[768,128]{1,0:T(8,128)(2,1)S(1)} collective-permute-done((bf16[768,128]{1,0:T(8,128)(2,1)S(1)}, bf16[768,128]{1,0:T(8,128)(2,1)S(1)}, u32[]{:S(2)}, u32[]{:S(2)}) %collective-permute-start.5) | collective-permute-done | bytes 196640 | tf_op jit(solution)/shard_map/ppermute | solution.py:22
  21.5 0.9 %collective-permute-done.6.refs_10_ = bf16[512,128]{1,0:T(8,128)(2,1)S(1)} collective-permute-done((bf16[512,128]{1,0:T(8,128)(2,1)S(1)}, bf16[512,128]{1,0:T(8,128)(2,1)S(1)}, u32[]{:S(2)}, u32[]{:S(2)}) %collective-permute-start.6) | collective-permute-done | bytes 131104 | tf_op jit(solution)/shard_map/ppermute | solution.py:22
  22.4 1.0 %collective-permute-start.7 = (bf16[768,128]{1,0:T(8,128)(2,1)S(1)}, bf16[768,128]{1,0:T(8,128)(2,1)S(1)}, u32[]{:S(2)}, u32[]{:S(2)}) collective-permute-start(bf16[768,128]{1,0:T(8,128)(2,1)S(1)} %pad_maximum_fusion.1), channel_id=1, source_target_pairs={{0,2},{2,0},{4,6},{6,4},{8,10},{10,8},{12,14},{14,12},{1,3},{3,1},... | collective-permute-start | bytes 589832 | tf_op jit(solution)/shard_map/ppermute | solution.py:22
  23.4 1.6 %pack.1 = (bf16[4,1024,128]{2,1,0:T(8,128)(2,1)S(1)}, bf16[4,1024,128]{2,1,0:T(8,128)(2,1)S(1)}) custom-call(bf16[128,32,128]{2,1,0:T(8,128)(2,1)} %q_ref, bf16[128,32,128]{2,1,0:T(8,128)(2,1)} %g_ref.1), custom_call_target="tpu_custom_call" | custom-call | flops 1048576 | bytes 4194304 | tf_op jit(solution)/shard_map/pack/pallas_call | solution.py:223
  25.1 3.0 %collective-permute-done.7.refs_8_ = bf16[768,128]{1,0:T(8,128)(2,1)S(1)} collective-permute-done((bf16[768,128]{1,0:T(8,128)(2,1)S(1)}, bf16[768,128]{1,0:T(8,128)(2,1)S(1)}, u32[]{:S(2)}, u32[]{:S(2)}) %collective-permute-start.7) | collective-permute-done | bytes 196640 | tf_op jit(solution)/shard_map/ppermute | solution.py:22
  28.1 5.9 %probs.1 = (bf16[1280,128]{1,0:T(8,128)(2,1)S(1)}, bf16[1280,128]{1,0:T(8,128)(2,1)S(1)}, bf16[4,448,128]{2,1,0:T(8,128)(2,1)S(1)}, bf16[4,448,1024]{2,1,0:T(8,128)(2,1)S(1)}, bf16[4,128,1024]{2,1,0:T(8,128)(2,1)S(1)}) custom-call(bf16[512,128]{1,0:T(8,128)(2,1)S(1)} %get-tuple-element.83.refs_0_, bf16[512,128]{1,0:T(8,128)(2,1)S(1)} %get-tuple-element.82.refs_1_, ...), custom_call_target="tpu_custom_call" | custom-call | flops 1879048192 | bytes 9371648 | tf_op jit(solution)/shard_map/probs/pallas_call | solution.py:223
  34.0 1.1 %collective-permute-start.8 = (bf16[1280,128]{1,0:T(8,128)(2,1)S(1)}, bf16[1280,128]{1,0:T(8,128)(2,1)S(1)}, u32[]{:S(2)}, u32[]{:S(2)}) collective-permute-start(bf16[1280,128]{1,0:T(8,128)(2,1)S(1)} %get-tuple-element.74), channel_id=1, source_target_pairs={{0,2},{2,0},{4,6},{6,4},{8,10},{10,8},{12,14},{14,12},{1,3},{3,1},... | collective-permute-start | bytes 983048 | tf_op jit(solution)/shard_map/ppermute | solution.py:22
  35.1 2.4 %grads.1 = (bf16[128,32,128]{2,1,0:T(8,128)(2,1)}, f32[512,128]{1,0:T(8,128)S(1)}, f32[512,128]{1,0:T(8,128)S(1)}) custom-call(bf16[4,1024,128]{2,1,0:T(8,128)(2,1)S(1)} %get-tuple-element.55.refs_4_.refs_0_, bf16[4,1024,128]{2,1,0:T(8,128)(2,1)S(1)} %get-tuple-element.56.refs_5_.refs_1_, bf16[4,448,128]{2,1,0:T(8,128)(2,1)S(1)} %get-tuple-element.67.refs_2_, ...), custom_call_target="tpu_custom_call" | custom-call | flops 939524096 | bytes 8847360 | tf_op jit(solution)/shard_map/grads/pallas_call | solution.py:223
  37.5 3.9 %collective-permute-done.8 = bf16[1280,128]{1,0:T(8,128)(2,1)S(1)} collective-permute-done((bf16[1280,128]{1,0:T(8,128)(2,1)S(1)}, bf16[1280,128]{1,0:T(8,128)(2,1)S(1)}, u32[]{:S(2)}, u32[]{:S(2)}) %collective-permute-start.8) | collective-permute-done | bytes 327712 | tf_op jit(solution)/shard_map/ppermute | solution.py:22
  41.4 1.3 %collective-permute-start.10 = (bf16[512,128]{1,0:T(8,128)(2,1)S(1)}, bf16[512,128]{1,0:T(8,128)(2,1)S(1)}, u32[]{:S(2)}, u32[]{:S(2)}) collective-permute-start(bf16[512,128]{1,0:T(8,128)(2,1)S(1)} %add_convert_fusion.1), channel_id=1, source_target_pairs={{8,0},{10,2},{9,1},{11,3},{24,16},{26,18},{25,17},{27,19}} | collective-permute-start | bytes 393224 | tf_op jit(solution)/shard_map/ppermute | solution.py:22
  42.7 1.3 %collective-permute-start.11 = (bf16[512,128]{1,0:T(8,128)(2,1)S(1)}, bf16[512,128]{1,0:T(8,128)(2,1)S(1)}, u32[]{:S(2)}, u32[]{:S(2)}) collective-permute-start(bf16[512,128]{1,0:T(8,128)(2,1)S(1)} %add_convert_fusion.1), channel_id=1, source_target_pairs={{12,0},{14,2},{13,1},{15,3},{28,16},{30,18},{29,17},{31,19}} | collective-permute-start | bytes 393224 | tf_op jit(solution)/shard_map/ppermute | solution.py:22
  44.0 1.3 %collective-permute-start.9 = (bf16[512,128]{1,0:T(8,128)(2,1)S(1)}, bf16[512,128]{1,0:T(8,128)(2,1)S(1)}, u32[]{:S(2)}, u32[]{:S(2)}) collective-permute-start(bf16[512,128]{1,0:T(8,128)(2,1)S(1)} %add_convert_fusion.1), channel_id=1, source_target_pairs={{4,0},{6,2},{5,1},{7,3},{20,16},{22,18},{21,17},{23,19}} | collective-permute-start | bytes 393224 | tf_op jit(solution)/shard_map/ppermute | solution.py:22
  45.3 0.1 add_convert_fusion.5
  45.4 0.7 %collective-permute-start.12 = (bf16[256,128]{1,0:T(8,128)(2,1)S(1)}, bf16[256,128]{1,0:T(8,128)(2,1)S(1)}, u32[]{:S(2)}, u32[]{:S(2)}) collective-permute-start(bf16[256,128]{1,0:T(8,128)(2,1)S(1)} %get-tuple-element.79), channel_id=1, source_target_pairs={{6,2},{8,4},{10,6},{12,8},{14,10},{7,3},{9,5},{11,7},{13,9},{15,11... | collective-permute-start | bytes 196616 | tf_op jit(solution)/shard_map/ppermute | solution.py:22
  46.1 0.7 %collective-permute-start.13 = (bf16[256,128]{1,0:T(8,128)(2,1)S(1)}, bf16[256,128]{1,0:T(8,128)(2,1)S(1)}, u32[]{:S(2)}, u32[]{:S(2)}) collective-permute-start(bf16[256,128]{1,0:T(8,128)(2,1)S(1)} %get-tuple-element.81), channel_id=1, source_target_pairs={{10,2},{12,4},{14,6},{11,3},{13,5},{15,7},{26,18},{28,20},{30,22},... | collective-permute-start | bytes 196616 | tf_op jit(solution)/shard_map/ppermute | solution.py:22
  46.7 5.9 %collective-permute-done.10 = bf16[512,128]{1,0:T(8,128)(2,1)S(1)} collective-permute-done((bf16[512,128]{1,0:T(8,128)(2,1)S(1)}, bf16[512,128]{1,0:T(8,128)(2,1)S(1)}, u32[]{:S(2)}, u32[]{:S(2)}) %collective-permute-start.10) | collective-permute-done | bytes 131104 | tf_op jit(solution)/shard_map/ppermute | solution.py:22
  52.6 0.7 %collective-permute-start.14 = (bf16[256,128]{1,0:T(8,128)(2,1)S(1)}, bf16[256,128]{1,0:T(8,128)(2,1)S(1)}, u32[]{:S(2)}, u32[]{:S(2)}) collective-permute-start(bf16[256,128]{1,0:T(8,128)(2,1)S(1)} %get-tuple-element.80), channel_id=1, source_target_pairs={{14,2},{15,3},{30,18},{31,19}} | collective-permute-start | bytes 196616 | tf_op jit(solution)/shard_map/ppermute | solution.py:22
  53.2 0.0 collective-permute-done.11
  53.3 0.0 collective-permute-done.9
  53.3 0.1 select_add_fusion.1
  53.4 1.3 %collective-permute-start.15 = (bf16[512,128]{1,0:T(8,128)(2,1)S(1)}, bf16[512,128]{1,0:T(8,128)(2,1)S(1)}, u32[]{:S(2)}, u32[]{:S(2)}) collective-permute-start(bf16[512,128]{1,0:T(8,128)(2,1)S(1)} %get-tuple-element.78), channel_id=1, source_target_pairs={{2,0},{3,1},{18,16},{19,17}} | collective-permute-start | bytes 393224 | tf_op jit(solution)/shard_map/ppermute | solution.py:22
  54.7 0.0 collective-permute-done.12
  54.7 0.0 collective-permute-done.13
  54.7 0.0 collective-permute-done.14
  54.7 5.5 %collective-permute-done.15 = bf16[512,128]{1,0:T(8,128)(2,1)S(1)} collective-permute-done((bf16[512,128]{1,0:T(8,128)(2,1)S(1)}, bf16[512,128]{1,0:T(8,128)(2,1)S(1)}, u32[]{:S(2)}, u32[]{:S(2)}) %collective-permute-start.15) | collective-permute-done | bytes 131104 | tf_op jit(solution)/shard_map/ppermute | solution.py:22
  60.3 0.0 copy-start
  60.3 0.0 copy-start.1
  60.3 0.7 %copy-done = f32[512,128]{1,0:T(8,128)} copy-done((f32[512,128]{1,0:T(8,128)}, f32[512,128]{1,0:T(8,128)S(1)}, u32[]{:S(2)}) %copy-start) | copy-done | bytes 262168
  61.0 0.1 copy-done.1
  (10 shorter events, 0.2 us)
Async XLA Ops:
  0.6 10.1 %collective-permute-start = (bf16[512,128]{1,0:T(8,128)(2,1)}, bf16[512,128]{1,0:T(8,128)(2,1)S(1)}, u32[]{:S(2)}, u32[]{:S(2)}) collective-permute-start(bf16[512,128]{1,0:T(8,128)(2,1)} %bitcast.6), channel_id=1, source_target_pairs={{0,8},{1,9},{16,24},{17,25}} | collective-permute-start | bytes 393224 | tf_op jit(solution)/shard_map/ppermute | solution.py:22
  6.6 5.9 %collective-permute-start.1 = (bf16[512,128]{1,0:T(8,128)(2,1)}, bf16[512,128]{1,0:T(8,128)(2,1)S(1)}, u32[]{:S(2)}, u32[]{:S(2)}) collective-permute-start(bf16[512,128]{1,0:T(8,128)(2,1)} %bitcast.8), channel_id=1, source_target_pairs={{0,10},{1,11},{16,26},{17,27}} | collective-permute-start | bytes 393224 | tf_op jit(solution)/shard_map/ppermute | solution.py:22
  8.2 4.4 %collective-permute-start.2 = (bf16[512,128]{1,0:T(8,128)(2,1)}, bf16[512,128]{1,0:T(8,128)(2,1)S(1)}, u32[]{:S(2)}, u32[]{:S(2)}) collective-permute-start(bf16[512,128]{1,0:T(8,128)(2,1)} %bitcast.9), channel_id=1, source_target_pairs={{0,2},{1,3},{16,18},{17,19}} | collective-permute-start | bytes 393224 | tf_op jit(solution)/shard_map/ppermute | solution.py:22
  10.8 1.8 %collective-permute-start.3 = (bf16[256,128]{1,0:T(8,128)(2,1)S(1)}, bf16[256,128]{1,0:T(8,128)(2,1)S(1)}, u32[]{:S(2)}, u32[]{:S(2)}) collective-permute-start(bf16[256,128]{1,0:T(8,128)(2,1)S(1)} %get-tuple-element.60), channel_id=1, source_target_pairs={{2,10},{4,12},{6,14},{3,11},{5,13},{7,15},{18,26},{20,28},{22,30},... | collective-permute-start | bytes 196616 | tf_op jit(solution)/shard_map/ppermute | solution.py:22
  11.4 1.2 %collective-permute-start.4 = (bf16[256,128]{1,0:T(8,128)(2,1)S(1)}, bf16[256,128]{1,0:T(8,128)(2,1)S(1)}, u32[]{:S(2)}, u32[]{:S(2)}) collective-permute-start(bf16[256,128]{1,0:T(8,128)(2,1)S(1)} %get-tuple-element.60), channel_id=1, source_target_pairs={{2,14},{3,15},{18,30},{19,31}} | collective-permute-start | bytes 196616 | tf_op jit(solution)/shard_map/ppermute | solution.py:22
  12.7 8.8 %collective-permute-start.5 = (bf16[768,128]{1,0:T(8,128)(2,1)S(1)}, bf16[768,128]{1,0:T(8,128)(2,1)S(1)}, u32[]{:S(2)}, u32[]{:S(2)}) collective-permute-start(bf16[768,128]{1,0:T(8,128)(2,1)S(1)} %pad_maximum_fusion), channel_id=1, source_target_pairs={{0,4},{2,6},{4,8},{6,10},{8,12},{10,14},{1,5},{3,7},{5,9},{7,11},{... | collective-permute-start | bytes 589832 | tf_op jit(solution)/shard_map/ppermute | solution.py:22
  17.2 5.2 %collective-permute-start.6 = (bf16[512,128]{1,0:T(8,128)(2,1)S(1)}, bf16[512,128]{1,0:T(8,128)(2,1)S(1)}, u32[]{:S(2)}, u32[]{:S(2)}) collective-permute-start(bf16[512,128]{1,0:T(8,128)(2,1)S(1)} %maximum_select_fusion), channel_id=1, source_target_pairs={{0,2},{2,0},{4,6},{6,4},{8,10},{10,8},{12,14},{14,12},{1,3},{3,1},... | collective-permute-start | bytes 393224 | tf_op jit(solution)/shard_map/ppermute | solution.py:22
  22.4 5.7 %collective-permute-start.7 = (bf16[768,128]{1,0:T(8,128)(2,1)S(1)}, bf16[768,128]{1,0:T(8,128)(2,1)S(1)}, u32[]{:S(2)}, u32[]{:S(2)}) collective-permute-start(bf16[768,128]{1,0:T(8,128)(2,1)S(1)} %pad_maximum_fusion.1), channel_id=1, source_target_pairs={{0,2},{2,0},{4,6},{6,4},{8,10},{10,8},{12,14},{14,12},{1,3},{3,1},... | collective-permute-start | bytes 589832 | tf_op jit(solution)/shard_map/ppermute | solution.py:22
  34.0 7.4 %collective-permute-start.8 = (bf16[1280,128]{1,0:T(8,128)(2,1)S(1)}, bf16[1280,128]{1,0:T(8,128)(2,1)S(1)}, u32[]{:S(2)}, u32[]{:S(2)}) collective-permute-start(bf16[1280,128]{1,0:T(8,128)(2,1)S(1)} %get-tuple-element.74), channel_id=1, source_target_pairs={{0,2},{2,0},{4,6},{6,4},{8,10},{10,8},{12,14},{14,12},{1,3},{3,1},... | collective-permute-start | bytes 983048 | tf_op jit(solution)/shard_map/ppermute | solution.py:22
  41.4 11.2 %collective-permute-start.10 = (bf16[512,128]{1,0:T(8,128)(2,1)S(1)}, bf16[512,128]{1,0:T(8,128)(2,1)S(1)}, u32[]{:S(2)}, u32[]{:S(2)}) collective-permute-start(bf16[512,128]{1,0:T(8,128)(2,1)S(1)} %add_convert_fusion.1), channel_id=1, source_target_pairs={{8,0},{10,2},{9,1},{11,3},{24,16},{26,18},{25,17},{27,19}} | collective-permute-start | bytes 393224 | tf_op jit(solution)/shard_map/ppermute | solution.py:22
  42.7 10.5 %collective-permute-start.11 = (bf16[512,128]{1,0:T(8,128)(2,1)S(1)}, bf16[512,128]{1,0:T(8,128)(2,1)S(1)}, u32[]{:S(2)}, u32[]{:S(2)}) collective-permute-start(bf16[512,128]{1,0:T(8,128)(2,1)S(1)} %add_convert_fusion.1), channel_id=1, source_target_pairs={{12,0},{14,2},{13,1},{15,3},{28,16},{30,18},{29,17},{31,19}} | collective-permute-start | bytes 393224 | tf_op jit(solution)/shard_map/ppermute | solution.py:22
  44.0 9.2 %collective-permute-start.9 = (bf16[512,128]{1,0:T(8,128)(2,1)S(1)}, bf16[512,128]{1,0:T(8,128)(2,1)S(1)}, u32[]{:S(2)}, u32[]{:S(2)}) collective-permute-start(bf16[512,128]{1,0:T(8,128)(2,1)S(1)} %add_convert_fusion.1), channel_id=1, source_target_pairs={{4,0},{6,2},{5,1},{7,3},{20,16},{22,18},{21,17},{23,19}} | collective-permute-start | bytes 393224 | tf_op jit(solution)/shard_map/ppermute | solution.py:22
  45.4 9.3 %collective-permute-start.12 = (bf16[256,128]{1,0:T(8,128)(2,1)S(1)}, bf16[256,128]{1,0:T(8,128)(2,1)S(1)}, u32[]{:S(2)}, u32[]{:S(2)}) collective-permute-start(bf16[256,128]{1,0:T(8,128)(2,1)S(1)} %get-tuple-element.79), channel_id=1, source_target_pairs={{6,2},{8,4},{10,6},{12,8},{14,10},{7,3},{9,5},{11,7},{13,9},{15,11... | collective-permute-start | bytes 196616 | tf_op jit(solution)/shard_map/ppermute | solution.py:22
  46.1 8.6 %collective-permute-start.13 = (bf16[256,128]{1,0:T(8,128)(2,1)S(1)}, bf16[256,128]{1,0:T(8,128)(2,1)S(1)}, u32[]{:S(2)}, u32[]{:S(2)}) collective-permute-start(bf16[256,128]{1,0:T(8,128)(2,1)S(1)} %get-tuple-element.81), channel_id=1, source_target_pairs={{10,2},{12,4},{14,6},{11,3},{13,5},{15,7},{26,18},{28,20},{30,22},... | collective-permute-start | bytes 196616 | tf_op jit(solution)/shard_map/ppermute | solution.py:22
  52.6 2.1 %collective-permute-start.14 = (bf16[256,128]{1,0:T(8,128)(2,1)S(1)}, bf16[256,128]{1,0:T(8,128)(2,1)S(1)}, u32[]{:S(2)}, u32[]{:S(2)}) collective-permute-start(bf16[256,128]{1,0:T(8,128)(2,1)S(1)} %get-tuple-element.80), channel_id=1, source_target_pairs={{14,2},{15,3},{30,18},{31,19}} | collective-permute-start | bytes 196616 | tf_op jit(solution)/shard_map/ppermute | solution.py:22
  53.4 6.9 %collective-permute-start.15 = (bf16[512,128]{1,0:T(8,128)(2,1)S(1)}, bf16[512,128]{1,0:T(8,128)(2,1)S(1)}, u32[]{:S(2)}, u32[]{:S(2)}) collective-permute-start(bf16[512,128]{1,0:T(8,128)(2,1)S(1)} %get-tuple-element.78), channel_id=1, source_target_pairs={{2,0},{3,1},{18,16},{19,17}} | collective-permute-start | bytes 393224 | tf_op jit(solution)/shard_map/ppermute | solution.py:22
  60.3 0.7 %copy-start = (f32[512,128]{1,0:T(8,128)}, f32[512,128]{1,0:T(8,128)S(1)}, u32[]{:S(2)}) copy-start(f32[512,128]{1,0:T(8,128)S(1)} %get-tuple-element.84) | copy-start | bytes 786436
  60.3 0.8 %copy-start.1 = (f32[512,128]{1,0:T(8,128)}, f32[512,128]{1,0:T(8,128)S(1)}, u32[]{:S(2)}) copy-start(f32[512,128]{1,0:T(8,128)S(1)} %get-tuple-element.85) | copy-start | bytes 786436

commit v12 on v9

--- a/solution.py
+++ b/solution.py
@@ -100,50 +100,89 @@
             out[2 * pair + part] = both[:, part * 8 : (part + 1) * 8].reshape(tokens * 8, 128).astype(BF16)
 
 
-def probs_kernel(sources, targets, heads_kv, scale, *refs):
-    prompt_k, prompt_v, own_k, own_v, qh, gh, bias, weight_ref = refs[:8]
-    n_in = 1 + max(source for source, _ in sources)
-    n_out = 1 + max(target for target, _ in targets)
-    blocks = refs[8 : 8 + n_in]
-    outs = refs[8 + n_in : 8 + n_in + n_out]
-    kh, ds_ref, p_own, vh, p_ref, grads, wide = refs[8 + n_in + n_out :]
-    window = len(sources)
+def causal_bias(columns):
+    column_token = lax.broadcasted_iota(jnp.int32, (CHUNK, columns), 1) // 8
+    return jnp.where(lax.broadcasted_iota(jnp.int32, (CHUNK, columns), 0) <= column_token, 0.0, MASKED)
+
+
+def outer_product(rows, columns):
+    return lax.dot_general(rows, columns, (((1,), (1,)), ((), ())), preferred_element_type=F32)
+
+
+def early_kernel(fresh, sources, heads_kv, scale, *refs):
+    own_k, own_v, qh, gh, bias = refs[:5]
+    blocks, (kh, e_ref, dp_ref, stats, vh, wide) = refs[5:-6], refs[-6:]
     tokens = TD * TILE
     front = CAP * TILE
-    before = tokens + window * front
+    behind = len(sources) * front
+    start = tokens + fresh * front
     columns = CHUNK * 8
-    device = lax.axis_index("node")
-
-    for side, heads_ref, prompt, own in ((0, kh, prompt_k, own_k), (1, vh, prompt_v, own_v)):
-        split_heads(prompt[...], heads_ref, 0, tokens, heads_kv, wide)
-        for k, (source, start) in enumerate(sources):
-            start += side * front * heads_kv
-            block = blocks[source][start : start + front * heads_kv]
-            split_heads(block, heads_ref, tokens + k * front, front, heads_kv, wide)
-        heads_ref[:, before:] = own[...]
-
-    column_token = lax.broadcasted_iota(jnp.int32, (CHUNK, columns), 1) // 8
-    causal = jnp.where(lax.broadcasted_iota(jnp.int32, (CHUNK, columns), 0) <= column_token, 0.0, MASKED)
+    for side, heads_ref, own in ((0, kh, own_k), (1, vh, own_v)):
+        for k, (source, at) in enumerate(sources):
+            at += side * front * heads_kv
+            split_heads(blocks[source][at : at + front * heads_kv], heads_ref, k * front, front, heads_kv, wide)
+        heads_ref[:, behind:] = own[...]
+    causal = causal_bias(columns)
     for head in range(heads_kv):
         for c in range(tokens // CHUNK):
-            rows = before + (c + 1) * CHUNK
+            rows = behind + (c + 1) * CHUNK
             span = slice(c * columns, (c + 1) * columns)
-            q = qh[head, span]
-            g = gh[head, span]
-            s = lax.dot_general(kh[head, :rows], q, (((1,), (1,)), ((), ())), preferred_element_type=F32)
-            dp = lax.dot_general(vh[head, :rows], g, (((1,), (1,)), ((), ())), preferred_element_type=F32)
-            s = s + jnp.concatenate([bias[:rows]] * (columns // 128), axis=1)
+            s = outer_product(kh[head, :rows], qh[head, span])
+            dp = outer_product(vh[head, :rows], gh[head, span])
+            s = s + jnp.concatenate([bias[start : start + rows]] * (columns // 128), axis=1)
             s = jnp.concatenate([s[: rows - CHUNK], s[rows - CHUNK :] + causal], axis=0)
             top = jnp.max(s, axis=0, keepdims=True)
             e = jnp.exp2((s - top) * (scale * math.log2(math.e)))
-            total = jnp.sum(e, axis=0, keepdims=True)
-            p = e * (weight_ref[:1, span] / total)
-            delta = jnp.sum(p * dp, axis=0, keepdims=True)
-            ds_ref[head, :rows, span] = (p * (dp - delta) * scale).astype(BF16)
-            p_ref[:, span] = p[:before].astype(BF16)
-            p_own[head, : rows - before, span] = p[before:].astype(BF16)
-        grads[0, head] = jnp.dot(ds_ref[head, :before], qh[head], preferred_element_type=F32)
-        grads[1, head] = jnp.dot(p_ref[...], gh[head], preferred_element_type=F32)
+            e_ref[head, :rows, span] = e
+            dp_ref[head, :rows, span] = dp
+            stats[head, 0:1, span] = top
+            stats[head, 1:2, span] = jnp.sum(e, axis=0, keepdims=True)
+            stats[head, 2:3, span] = jnp.sum(e * dp, axis=0, keepdims=True)
+
+
+def probs_kernel(sources, targets, heads_kv, scale, *refs):
+    prompt_k, prompt_v, qh, gh, bias, weight_ref, e_ref, dp_ref, stats, block_ref = refs[:10]
+    n_out = 1 + max(target for target, _ in targets)
+    outs = refs[10 : 10 + n_out]
+    kh, ds_ref, p_own, vh, p_ref, grads, wide = refs[10 + n_out :]
+    tokens = TD * TILE
+    front = CAP * TILE
+    fresh = tokens + len(sources) * front
+    before = tokens + len(targets) * front
+    columns = CHUNK * 8
+    rate = scale * math.log2(math.e)
+    device = lax.axis_index("node")
+
+    for side, heads_ref, prompt in ((0, kh, prompt_k), (1, vh, prompt_v)):
+        split_heads(prompt[...], heads_ref, 0, tokens, heads_kv, wide)
+        for k, (_, at) in enumerate(sources):
+            at += side * front * heads_kv
+            split_heads(block_ref[at : at + front * heads_kv], heads_ref, tokens + k * front, front, heads_kv, wide)
+
+    for head in range(heads_kv):
+        for c in range(tokens // CHUNK):
+            rows = before - fresh + (c + 1) * CHUNK
+            span = slice(c * columns, (c + 1) * columns)
+            s = outer_product(kh[head], qh[head, span])
+            dp = outer_product(vh[head], gh[head, span])
+            s = s + jnp.concatenate([bias[:fresh]] * (columns // 128), axis=1)
+            top_early = stats[head, 0:1, span]
+            top = jnp.maximum(jnp.max(s, axis=0, keepdims=True), top_early)
+            e = jnp.exp2((s - top) * rate)
+            shrink = jnp.exp2((top_early - top) * rate)
+            total = jnp.sum(e, axis=0, keepdims=True) + shrink * stats[head, 1:2, span]
+            weight = weight_ref[:1, span] / total
+            weight_early = weight * shrink
+            p = e * weight
+            delta = jnp.sum(p * dp, axis=0, keepdims=True) + weight_early * stats[head, 2:3, span]
+            ds_ref[head, :fresh, span] = (p * (dp - delta)).astype(BF16)
+            p_ref[head % 2, :fresh, span] = p.astype(BF16)
+            p = e_ref[head, :rows, span] * weight_early
+            ds_ref[head, fresh : fresh + rows, span] = (p * (dp_ref[head, :rows, span] - delta)).astype(BF16)
+            p_ref[head % 2, fresh:, span] = p[: before - fresh].astype(BF16)
+            p_own[head, : fresh + rows - before, span] = p[before - fresh :].astype(BF16)
+        grads[0, head] = scale * jnp.dot(ds_ref[head, :before], qh[head], preferred_element_type=F32)
+        grads[1, head] = jnp.dot(p_ref[head % 2], gh[head], preferred_element_type=F32)
 
     rows = tokens * heads_kv
     rows_front = front * heads_kv
@@ -167,10 +206,11 @@
             outs[target][start : start + rows_front] = block
 
 
-def grads_kernel(heads_kv, *refs):
-    qh, gh, kh, ds_ref, p_own, dq_ref, dk_ref, dv_ref, wide = refs
+def grads_kernel(heads_kv, scale, *refs):
+    qh, gh, kh_fresh, kh_early, ds_ref, p_own, dq_ref, dk_ref, dv_ref, wide = refs
     tokens = TD * TILE
-    before = kh.shape[1] - tokens
+    kh = [jnp.concatenate([kh_fresh[h], kh_early[h]], axis=0) for h in range(heads_kv)]
+    before = kh[0].shape[0] - tokens
     columns = CHUNK * 8
     dk = []
     dv = []
@@ -181,9 +221,9 @@
             parts = []
             for head in (2 * pair, 2 * pair + 1):
                 dq = lax.dot_general(
-                    kh[head, :rows], ds_ref[head, :rows, span], (((0,), (0,)), ((), ())), preferred_element_type=F32
+                    kh[head][:rows], ds_ref[head, :rows, span], (((0,), (0,)), ((), ())), preferred_element_type=F32
                 )
-                parts.append(dq.T.reshape(CHUNK, 8, 128))
+                parts.append((scale * dq.T).reshape(CHUNK, 8, 128))
             dq_ref[c * CHUNK : (c + 1) * CHUNK, pair * 16 : (pair + 1) * 16] = jnp.concatenate(parts, axis=1).astype(BF16)
         for head in (2 * pair, 2 * pair + 1):
             for source, factor, out in ((ds_ref.at[head, before:], qh, dk), (p_own.at[head], gh, dv)):
@@ -196,7 +236,7 @@
                         )
                     )
                 out.append(jnp.concatenate(pieces, axis=0))
-    dk_ref[...] = join_heads(dk, tokens, heads_kv, wide)
+    dk_ref[...] = scale * join_heads(dk, tokens, heads_kv, wide)
     dv_ref[...] = join_heads(dv, tokens, heads_kv, wide)
 
 
@@ -255,52 +295,72 @@
     )
 
 
-def probs(sources, targets, prompt_k, prompt_v, qh, gh, own, blocks):
-    own_k, own_v, bias, weight = own
+def early(fresh, sources, qh, gh, own, blocks):
+    own_k, own_v, bias, _ = own
     heads_kv, tokens, head_size = own_k.shape
+    rows = len(sources) * CAP * TILE + tokens
+    array = jax.ShapeDtypeStruct
+    work = heads_kv * tokens * 8 * rows
+    return call(
+        functools.partial(early_kernel, fresh, sources, heads_kv, head_size**-0.5),
+        "early",
+        (own_k, own_v, qh, gh, bias, *blocks),
+        [array((heads_kv, rows, head_size), BF16)]
+        + [array((heads_kv, rows, tokens * 8), F32)] * 2
+        + [array((heads_kv, 8, tokens * 8), F32)],
+        [pltpu.VMEM((heads_kv, rows, head_size), BF16), pltpu.VMEM((CAP * TILE * heads_kv, head_size), F32)],
+        flops=4 * work * head_size,
+        transcendentals=work,
+    )
+
+
+def probs(sources, targets, prompt_k, prompt_v, qh, gh, own, parts, block):
+    _, own_v, bias, weight = own
+    heads_kv, tokens, head_size = own_v.shape
     rows = tokens * heads_kv
     front = CAP * TILE
     unit = 2 * front * heads_kv
-    before = tokens + len(sources) * front
+    fresh = tokens + len(sources) * front
+    before = tokens + len(targets) * front
     sizes = [max(start for target, start in targets if target == t) + unit for t in range(1 + max(targets)[0])]
     array = jax.ShapeDtypeStruct
     work = heads_kv * tokens * 8 * (before + tokens)
     return call(
         functools.partial(probs_kernel, sources, targets, heads_kv, head_size**-0.5),
         "probs",
-        (prompt_k, prompt_v, own_k, own_v, qh, gh, bias, weight, *blocks),
+        (prompt_k, prompt_v, qh, gh, bias, weight, *parts, block),
         [array((size, head_size), BF16) for size in sizes]
         + [
-            array((heads_kv, before + tokens, head_size), BF16),
+            array((heads_kv, fresh, head_size), BF16),
             array((heads_kv, before + tokens, tokens * 8), BF16),
             array((heads_kv, tokens, tokens * 8), BF16),
         ],
         [
-            pltpu.VMEM((heads_kv, before + tokens, head_size), BF16),
-            pltpu.VMEM((before, tokens * 8), BF16),
+            pltpu.VMEM((heads_kv, fresh, head_size), BF16),
+            pltpu.VMEM((2, before, tokens * 8), BF16),
             pltpu.VMEM((2, heads_kv, before, head_size), F32),
             pltpu.VMEM((rows, head_size), F32),
         ],
-        flops=8 * work * head_size,
+        flops=6 * work * head_size,
         transcendentals=work,
     )
 
 
-def grads(qh, gh, kh, ds, p_own):
+def grads(qh, gh, kh_fresh, kh_early, ds, p_own):
     heads_kv, tokens, _ = p_own.shape
-    head_size = kh.shape[2]
+    head_size = kh_fresh.shape[2]
     array = jax.ShapeDtypeStruct
     return call(
-        functools.partial(grads_kernel, heads_kv),
+        functools.partial(grads_kernel, heads_kv, head_size**-0.5),
         "grads",
-        (qh, gh, kh, ds, p_own),
+        (qh, gh, kh_fresh, kh_early, ds, p_own),
         [
             array((tokens, heads_kv * 8, head_size), BF16),
             array((tokens * heads_kv, head_size), F32),
             array((tokens * heads_kv, head_size), F32),
         ],
         [pltpu.VMEM((tokens * heads_kv, head_size), F32)],
-        flops=4 * heads_kv * tokens * 8 * kh.shape[1] * head_size,
+        flops=2 * heads_kv * tokens * 8 * ds.shape[1] * head_size,
     )
 
 
@@ -331,7 +391,7 @@
     return [(i + j, i + j + stride) for i in range(0, size, 2 * stride) for j in (0, 1)]
 
 
-def collect(size, unit, rows, where, keys, values, head, held, queries):
+def collect(size, unit, rows, where, keys, values, head, held, queries, grad_out):
     even, lower, _ = where
     neighbours = [(i, i ^ 1) for i in range(size)]
     far_route = shift_route(4, size)[1:]
@@ -341,16 +401,17 @@
         values_far = permuted(values, [(0, 5)])
         values_next = permuted(values, [(0, 1)])
         head, queries = lax.optimization_barrier((head, queries, keys_far))[:2]
+        qh, gh = pack(queries, grad_out, keys.shape[0] // queries.shape[0])
         far = permuted(head, far_route)
         six = permuted(head, [(1, 7)])
-        held = after(added(held, values_far, values_next, keys_far).astype(BF16), far, six)
+        held = after(added(held, values_far, values_next, keys_far).astype(BF16), far, six, qh)
         second = permuted(jnp.concatenate([held, head]), near_route)
         crossed = jnp.where(even, jnp.concatenate([head, far]), jnp.concatenate([far, six]))
         crossed = permuted(crossed, neighbours)
         held = jnp.where(lower, held, second[:rows])
         third = permuted(after(jnp.concatenate([held, second[rows:]]), crossed), neighbours)
-        sources = [(0, rows), (1, rows), (2, 0), (3, 0), (2, unit), (4, 0)]
-        return held, third[:rows], sources, (third, second, crossed, far, six), queries
+        early_sources = [(0, rows), (1, 0), (2, 0), (1, unit), (3, 0)]
+        return held, third[:rows], third, [(0, rows)], early_sources, (second, crossed, far, six), (qh, gh)
     strides = [2**i for i in range(2, size.bit_length()) if 2**i < size]
     top = strides[-1]
     keys_far = permuted(keys, [(0, top)])
@@ -365,8 +426,9 @@
     near, six = units(second, rows, unit, 2)
     third = permuted(jnp.concatenate([head, near, far, six]), shift_route(1, size))
     other = permuted(held, neighbours)
-    sources = [(0, 0), (1, rows), (0, unit), (2, 0), (0, 2 * unit), (1, rows + unit), (0, 3 * unit)]
-    return held, other, sources, (third, second, far), queries
+    fresh_sources = [(0, i * unit) for i in range(4)]
+    early_sources = [(0, rows), (1, 0), (0, rows + unit)]
+    return held, other, third, fresh_sources, early_sources, (second, far), pack(queries, grad_out, keys.shape[0] // queries.shape[0])
 
 
 def give_back(size, unit, rows, where, send, keep, ready):
@@ -413,18 +475,22 @@
     keys = keys.reshape(rows, head_size)
     values = values.reshape(rows, head_size)
 
-    order = [(k, k) for k in range(1, window + 1)]
     if size == W + 1:
-        order[0], order[2] = (1, 3), (3, 1)
+        order = [(1, 3), (2, 2), (3, 1), (4, 4), (5, 5), (6, 6)]
+        targets = [(k % 2, rows + k // 2 * unit) for k in range(window)]
+    else:
+        order = [(k, k) for k in (1, 3, 5, 7, 2, 4, 6)]
+        targets = [(0, rows + i * unit) for i in range(4)] + [(1, rows + i * unit) for i in range(3)]
     head, held, *own = load(order, keys, values, parents, lengths, tokens)
     head, *where = lax.optimization_barrier((head, lax.rem(device, 2) == 0, lax.rem(device, 4) < 2, device == 0))
     even, _, root = where
-    held, other, sources, blocks, queries = collect(size, unit, rows, where, keys, values, head, held, queries)
-    qh, gh = pack(queries, grad_out, heads_kv)
+    held, other, block, fresh_sources, early_sources, blocks, (qh, gh) = collect(
+        size, unit, rows, where, keys, values, head, held, queries, grad_out
+    )
+    kh_early, *parts = early(len(fresh_sources), early_sources, qh, gh, own, blocks)
     prompt_k, prompt_v = jnp.where(even, held, other), jnp.where(even, other, held)
-    targets = [(1 - k % 2, rows + (k - 1) // 2 * unit) for k in range(1, window + 1)]
-    send, keep, kh, ds, p_own = probs(sources, targets, prompt_k, prompt_v, qh, gh, own, blocks)
-    grad_queries, dk, dv = grads(qh, gh, kh, ds, p_own)
+    send, keep, kh, ds, p_own = probs(fresh_sources, targets, prompt_k, prompt_v, qh, gh, own, parts, block)
+    grad_queries, dk, dv = grads(qh, gh, kh, kh_early, ds, p_own)
     prompt_k, prompt_v, mine = give_back(size, unit, rows, where, send, keep, dk)
     own = []
     for side, local, prompt in ((0, dk, prompt_k), (1, dv, prompt_v)):

time: 61.6 us -> 60.3 us (0.979)
  waiting for transfers between devices: 22.6 us -> 20.2 us
  starting transfers between devices: 25.1 us -> 26.8 us
  Pallas kernels: 11.4 us -> 10.7 us
    ppermute x16, waiting for transfers between devices: 22.6 us -> 20.2 us  [permuted(): return lax.ppermute(block, 'node', route)]
    ppermute x16, starting transfers between devices: 25.1 us -> 26.8 us  [permuted(): return lax.ppermute(block, 'node', route)]
    pallas_call x4 -> x5, Pallas kernels: 11.4 us -> 10.7 us  [call(): pl.pallas_call(kernel, in_specs=[place] * len(operands), out_specs=[VMEM]...]
  transfers between devices with their start and end apart: 16 -> 16, of which waited for: 9 -> 9; matrix products, arithmetic and copies ran while one was open for 1% -> 1% of each run, Pallas kernels for 9% -> 11%
where the time goes in v12:
time: 60.3 us; the launch traced here: 59.9 us
  starting transfers between devices  26.8 us (44%)
  waiting for transfers between devices  20.2 us (33%)
  Pallas kernels  10.7 us (18%)
  between operations  0.92 us (2%)
  local copies, waits for them, and re-layouts  0.78 us (1%)
    ppermute x16, starting transfers between devices, permuted(): return lax.ppermute(block, 'node', route)  26.8 us
    ppermute x16, waiting for transfers between devices, permuted(): return lax.ppermute(block, 'node', route)  20.2 us
    pallas_call x5, Pallas kernels, call(): pl.pallas_call(kernel, in_specs=[place] * len(operands), out_specs=[VMEM]...  10.7 us
  transfers between devices with their start and end apart: 16, of which 9 were waited for; matrix products, arithmetic and copies ran while one was open for 1% of the time, Pallas kernels for 11%

profile of v12, /device:TPU:0, one launch (start us, length us, event | category | flops | bytes accessed | tf_op | source)
XLA Modules:
  0.0 59.9 jit_solution(2203492929909020316)
XLA Ops:
  0.6 5.9 %collective-permute-start = (bf16[512,128]{1,0:T(8,128)(2,1)}, bf16[512,128]{1,0:T(8,128)(2,1)S(1)}, u32[]{:S(2)}, u32[]{:S(2)}) collective-permute-start(bf16[512,128]{1,0:T(8,128)(2,1)} %bitcast.6), channel_id=1, source_target_pairs={{0,8},{1,9},{16,24},{17,25}} | collective-permute-start | bytes 393224 | tf_op jit(solution)/shard_map/ppermute | solution.py:22
  6.6 1.3 %collective-permute-start.2 = (bf16[512,128]{1,0:T(8,128)(2,1)}, bf16[512,128]{1,0:T(8,128)(2,1)S(1)}, u32[]{:S(2)}, u32[]{:S(2)}) collective-permute-start(bf16[512,128]{1,0:T(8,128)(2,1)} %bitcast.8), channel_id=1, source_target_pairs={{0,2},{1,3},{16,18},{17,19}} | collective-permute-start | bytes 393224 | tf_op jit(solution)/shard_map/ppermute | solution.py:22
  7.9 1.3 %collective-permute-start.1 = (bf16[512,128]{1,0:T(8,128)(2,1)}, bf16[512,128]{1,0:T(8,128)(2,1)S(1)}, u32[]{:S(2)}, u32[]{:S(2)}) collective-permute-start(bf16[512,128]{1,0:T(8,128)(2,1)} %bitcast.9), channel_id=1, source_target_pairs={{0,10},{1,11},{16,26},{17,27}} | collective-permute-start | bytes 393224 | tf_op jit(solution)/shard_map/ppermute | solution.py:22
  9.2 1.2 %load.1 = (bf16[256,128]{1,0:T(8,128)(2,1)S(1)}, bf16[512,128]{1,0:T(8,128)(2,1)S(1)}, bf16[4,128,128]{2,1,0:T(8,128)(2,1)S(1)}, bf16[4,128,128]{2,1,0:T(8,128)(...) custom-call(s32[64]{0:T(128)} %refs_0_.1, s32[64]{0:T(128)} %refs_1_.1, bf16[512,128]{1,0:T(8,128)(2,1)} %bitcast.7, ...), custom_call_target="tpu_custom_call" | custom-call | flops 1048576 | bytes 983552 | tf_op jit(solution)/shard_map/load/pallas_call | solution.py:253
  10.4 0.0 collective-permute-done
  10.4 0.7 %collective-permute-start.4 = (bf16[256,128]{1,0:T(8,128)(2,1)S(1)}, bf16[256,128]{1,0:T(8,128)(2,1)S(1)}, u32[]{:S(2)}, u32[]{:S(2)}) collective-permute-start(bf16[256,128]{1,0:T(8,128)(2,1)S(1)} %get-tuple-element.64), channel_id=1, source_target_pairs={{2,14},{3,15},{18,30},{19,31}} | collective-permute-start | bytes 196616 | tf_op jit(solution)/shard_map/ppermute | solution.py:22
  11.1 0.7 %collective-permute-start.3 = (bf16[256,128]{1,0:T(8,128)(2,1)S(1)}, bf16[256,128]{1,0:T(8,128)(2,1)S(1)}, u32[]{:S(2)}, u32[]{:S(2)}) collective-permute-start(bf16[256,128]{1,0:T(8,128)(2,1)S(1)} %get-tuple-element.64), channel_id=1, source_target_pairs={{2,10},{4,12},{6,14},{3,11},{5,13},{7,15},{18,26},{20,28},{22,30},... | collective-permute-start | bytes 196616 | tf_op jit(solution)/shard_map/ppermute | solution.py:22
  11.8 0.0 collective-permute-done.2
  11.8 0.7 %collective-permute-done.1 = bf16[512,128]{1,0:T(8,128)(2,1)S(1)} collective-permute-done((bf16[512,128]{1,0:T(8,128)(2,1)}, bf16[512,128]{1,0:T(8,128)(2,1)S(1)}, u32[]{:S(2)}, u32[]{:S(2)}) %collective-permute-start.1) | collective-permute-done | bytes 131104 | tf_op jit(solution)/shard_map/ppermute | solution.py:22
  12.5 0.1 add_convert_fusion.2
  12.5 1.6 %pack.1 = (bf16[4,1024,128]{2,1,0:T(8,128)(2,1)S(1)}, bf16[4,1024,128]{2,1,0:T(8,128)(2,1)S(1)}) custom-call(bf16[128,32,128]{2,1,0:T(8,128)(2,1)} %q_ref, bf16[128,32,128]{2,1,0:T(8,128)(2,1)} %g_ref.1), custom_call_target="tpu_custom_call" | custom-call | flops 1048576 | bytes 4194304 | tf_op jit(solution)/shard_map/pack/pallas_call | solution.py:253
  14.2 0.0 collective-permute-done.4.refs_8_
  14.2 0.0 collective-permute-done.3.refs_7_
  14.2 2.9 %collective-permute-start.5 = (bf16[768,128]{1,0:T(8,128)(2,1)S(1)}, bf16[768,128]{1,0:T(8,128)(2,1)S(1)}, u32[]{:S(2)}, u32[]{:S(2)}) collective-permute-start(bf16[768,128]{1,0:T(8,128)(2,1)S(1)} %pad_maximum_fusion), channel_id=1, source_target_pairs={{0,4},{2,6},{4,8},{6,10},{8,12},{10,14},{1,5},{3,7},{5,9},{7,11},{... | collective-permute-start | bytes 589832 | tf_op jit(solution)/shard_map/ppermute | solution.py:22
  17.2 2.8 %collective-permute-start.6 = (bf16[512,128]{1,0:T(8,128)(2,1)S(1)}, bf16[512,128]{1,0:T(8,128)(2,1)S(1)}, u32[]{:S(2)}, u32[]{:S(2)}) collective-permute-start(bf16[512,128]{1,0:T(8,128)(2,1)S(1)} %maximum_select_fusion), channel_id=1, source_target_pairs={{0,2},{2,0},{4,6},{6,4},{8,10},{10,8},{12,14},{14,12},{1,3},{3,1},... | collective-permute-start | bytes 393224 | tf_op jit(solution)/shard_map/ppermute | solution.py:22
  20.0 1.4 %collective-permute-done.5.refs_5_ = bf16[768,128]{1,0:T(8,128)(2,1)S(1)} collective-permute-done((bf16[768,128]{1,0:T(8,128)(2,1)S(1)}, bf16[768,128]{1,0:T(8,128)(2,1)S(1)}, u32[]{:S(2)}, u32[]{:S(2)}) %collective-permute-start.5) | collective-permute-done | bytes 196640 | tf_op jit(solution)/shard_map/ppermute | solution.py:22
  21.5 1.4 %collective-permute-done.6.refs_6_ = bf16[512,128]{1,0:T(8,128)(2,1)S(1)} collective-permute-done((bf16[512,128]{1,0:T(8,128)(2,1)S(1)}, bf16[512,128]{1,0:T(8,128)(2,1)S(1)}, u32[]{:S(2)}, u32[]{:S(2)}) %collective-permute-start.6) | collective-permute-done | bytes 131104 | tf_op jit(solution)/shard_map/ppermute | solution.py:22
  23.0 2.0 %collective-permute-start.7 = (bf16[768,128]{1,0:T(8,128)(2,1)S(1)}, bf16[768,128]{1,0:T(8,128)(2,1)S(1)}, u32[]{:S(2)}, u32[]{:S(2)}) collective-permute-start(bf16[768,128]{1,0:T(8,128)(2,1)S(1)} %pad_maximum_fusion.1), channel_id=1, source_target_pairs={{0,2},{2,0},{4,6},{6,4},{8,10},{10,8},{12,14},{14,12},{1,3},{3,1},... | collective-permute-start | bytes 589832 | tf_op jit(solution)/shard_map/ppermute | solution.py:22
  25.0 1.6 %early.1 = (bf16[4,288,128]{2,1,0:T(8,128)(2,1)S(1)}, f32[4,288,1024]{2,1,0:T(8,128)S(1)}, f32[4,288,1024]{2,1,0:T(8,128)S(1)}, f32[4,8,1024]{2,1,0:T(8,128)S(1)}) custom-call(bf16[4,128,128]{2,1,0:T(8,128)(2,1)S(1)} %get-tuple-element.69.refs_0_, bf16[4,128,128]{2,1,0:T(8,128)(2,1)S(1)} %get-tuple-element.70.refs_1_, ...), custom_call_target="tpu_custom_call" | custom-call | flops 603979776 | bytes 12910592 | tf_op jit(solution)/shard_map/early/pallas_call | solution.py:253
  26.6 2.0 %collective-permute-done.7.refs_9_ = bf16[768,128]{1,0:T(8,128)(2,1)S(1)} collective-permute-done((bf16[768,128]{1,0:T(8,128)(2,1)S(1)}, bf16[768,128]{1,0:T(8,128)(2,1)S(1)}, u32[]{:S(2)}, u32[]{:S(2)}) %collective-permute-start.7) | collective-permute-done | bytes 196640 | tf_op jit(solution)/shard_map/ppermute | solution.py:22
  28.7 3.9 %probs.1 = (bf16[1280,128]{1,0:T(8,128)(2,1)S(1)}, bf16[1280,128]{1,0:T(8,128)(2,1)S(1)}, bf16[4,160,128]{2,1,0:T(8,128)(2,1)S(1)}, bf16[4,448,1024]{2,1,0:T(8,128)(2,1)S(1)}, bf16[4,128,1024]{2,1,0:T(8,128)(2,1)S(1)}) custom-call(bf16[512,128]{1,0:T(8,128)(2,1)S(1)} %get-tuple-element.91.refs_0_, bf16[512,128]{1,0:T(8,128)(2,1)S(1)} %get-tuple-element.90.refs_1_, ...), custom_call_target="tpu_custom_call" | custom-call | flops 1409286144 | bytes 17924096 | tf_op jit(solution)/shard_map/probs/pallas_call | solution.py:253
  32.5 2.1 %collective-permute-start.8 = (bf16[1280,128]{1,0:T(8,128)(2,1)S(1)}, bf16[1280,128]{1,0:T(8,128)(2,1)S(1)}, u32[]{:S(2)}, u32[]{:S(2)}) collective-permute-start(bf16[1280,128]{1,0:T(8,128)(2,1)S(1)} %get-tuple-element.82), channel_id=1, source_target_pairs={{0,2},{2,0},{4,6},{6,4},{8,10},{10,8},{12,14},{14,12},{1,3},{3,1},... | collective-permute-start | bytes 983048 | tf_op jit(solution)/shard_map/ppermute | solution.py:22
  34.6 2.4 %grads.1 = (bf16[128,32,128]{2,1,0:T(8,128)(2,1)}, f32[512,128]{1,0:T(8,128)S(1)}, f32[512,128]{1,0:T(8,128)S(1)}) custom-call(bf16[4,1024,128]{2,1,0:T(8,128)(2,1)S(1)} %get-tuple-element.59.refs_2_.refs_0_, bf16[4,1024,128]{2,1,0:T(8,128)(2,1)S(1)} %get-tuple-element.60.refs_3_.refs_1_, bf16[4,160,128]{2,1,0:T(8,128)(2,1)S(1)} %get-tuple-element.74.refs_2_, ...), custom_call_target="tpu_custom_call" | custom-call | flops 469762048 | bytes 8847360 | tf_op jit(solution)/shard_map/grads/pallas_call | solution.py:253
  37.0 2.7 %collective-permute-done.8 = bf16[1280,128]{1,0:T(8,128)(2,1)S(1)} collective-permute-done((bf16[1280,128]{1,0:T(8,128)(2,1)S(1)}, bf16[1280,128]{1,0:T(8,128)(2,1)S(1)}, u32[]{:S(2)}, u32[]{:S(2)}) %collective-permute-start.8) | collective-permute-done | bytes 327712 | tf_op jit(solution)/shard_map/ppermute | solution.py:22
  39.7 1.3 %collective-permute-start.11 = (bf16[512,128]{1,0:T(8,128)(2,1)S(1)}, bf16[512,128]{1,0:T(8,128)(2,1)S(1)}, u32[]{:S(2)}, u32[]{:S(2)}) collective-permute-start(bf16[512,128]{1,0:T(8,128)(2,1)S(1)} %add_convert_fusion.1), channel_id=1, source_target_pairs={{12,0},{14,2},{13,1},{15,3},{28,16},{30,18},{29,17},{31,19}} | collective-permute-start | bytes 393224 | tf_op jit(solution)/shard_map/ppermute | solution.py:22
  41.0 1.3 %collective-permute-start.10 = (bf16[512,128]{1,0:T(8,128)(2,1)S(1)}, bf16[512,128]{1,0:T(8,128)(2,1)S(1)}, u32[]{:S(2)}, u32[]{:S(2)}) collective-permute-start(bf16[512,128]{1,0:T(8,128)(2,1)S(1)} %add_convert_fusion.1), channel_id=1, source_target_pairs={{8,0},{10,2},{9,1},{11,3},{24,16},{26,18},{25,17},{27,19}} | collective-permute-start | bytes 393224 | tf_op jit(solution)/shard_map/ppermute | solution.py:22
  42.3 1.3 %collective-permute-start.9 = (bf16[512,128]{1,0:T(8,128)(2,1)S(1)}, bf16[512,128]{1,0:T(8,128)(2,1)S(1)}, u32[]{:S(2)}, u32[]{:S(2)}) collective-permute-start(bf16[512,128]{1,0:T(8,128)(2,1)S(1)} %add_convert_fusion.1), channel_id=1, source_target_pairs={{4,0},{6,2},{5,1},{7,3},{20,16},{22,18},{21,17},{23,19}} | collective-permute-start | bytes 393224 | tf_op jit(solution)/shard_map/ppermute | solution.py:22
  43.6 0.1 add_convert_fusion.5
  43.7 0.7 %collective-permute-start.12 = (bf16[256,128]{1,0:T(8,128)(2,1)S(1)}, bf16[256,128]{1,0:T(8,128)(2,1)S(1)}, u32[]{:S(2)}, u32[]{:S(2)}) collective-permute-start(bf16[256,128]{1,0:T(8,128)(2,1)S(1)} %get-tuple-element.87), channel_id=1, source_target_pairs={{6,2},{8,4},{10,6},{12,8},{14,10},{7,3},{9,5},{11,7},{13,9},{15,11... | collective-permute-start | bytes 196616 | tf_op jit(solution)/shard_map/ppermute | solution.py:22
  44.3 0.7 %collective-permute-start.14 = (bf16[256,128]{1,0:T(8,128)(2,1)S(1)}, bf16[256,128]{1,0:T(8,128)(2,1)S(1)}, u32[]{:S(2)}, u32[]{:S(2)}) collective-permute-start(bf16[256,128]{1,0:T(8,128)(2,1)S(1)} %get-tuple-element.88), channel_id=1, source_target_pairs={{14,2},{15,3},{30,18},{31,19}} | collective-permute-start | bytes 196616 | tf_op jit(solution)/shard_map/ppermute | solution.py:22
  45.0 4.4 %collective-permute-done.11 = bf16[512,128]{1,0:T(8,128)(2,1)S(1)} collective-permute-done((bf16[512,128]{1,0:T(8,128)(2,1)S(1)}, bf16[512,128]{1,0:T(8,128)(2,1)S(1)}, u32[]{:S(2)}, u32[]{:S(2)}) %collective-permute-start.11) | collective-permute-done | bytes 131104 | tf_op jit(solution)/shard_map/ppermute | solution.py:22
  49.4 0.7 %collective-permute-start.13 = (bf16[256,128]{1,0:T(8,128)(2,1)S(1)}, bf16[256,128]{1,0:T(8,128)(2,1)S(1)}, u32[]{:S(2)}, u32[]{:S(2)}) collective-permute-start(bf16[256,128]{1,0:T(8,128)(2,1)S(1)} %get-tuple-element.89), channel_id=1, source_target_pairs={{10,2},{12,4},{14,6},{11,3},{13,5},{15,7},{26,18},{28,20},{30,22},... | collective-permute-start | bytes 196616 | tf_op jit(solution)/shard_map/ppermute | solution.py:22
  50.0 0.9 %collective-permute-done.10 = bf16[512,128]{1,0:T(8,128)(2,1)S(1)} collective-permute-done((bf16[512,128]{1,0:T(8,128)(2,1)S(1)}, bf16[512,128]{1,0:T(8,128)(2,1)S(1)}, u32[]{:S(2)}, u32[]{:S(2)}) %collective-permute-start.10) | collective-permute-done | bytes 131104 | tf_op jit(solution)/shard_map/ppermute | solution.py:22
  51.0 0.6 collective-permute-done.9
  51.6 0.1 select_add_fusion.1
  51.7 1.3 %collective-permute-start.15 = (bf16[512,128]{1,0:T(8,128)(2,1)S(1)}, bf16[512,128]{1,0:T(8,128)(2,1)S(1)}, u32[]{:S(2)}, u32[]{:S(2)}) collective-permute-start(bf16[512,128]{1,0:T(8,128)(2,1)S(1)} %get-tuple-element.86), channel_id=1, source_target_pairs={{2,0},{3,1},{18,16},{19,17}} | collective-permute-start | bytes 393224 | tf_op jit(solution)/shard_map/ppermute | solution.py:22
  53.0 0.0 collective-permute-done.12
  53.0 0.0 collective-permute-done.14
  53.0 0.0 collective-permute-done.13
  53.0 6.0 %collective-permute-done.15 = bf16[512,128]{1,0:T(8,128)(2,1)S(1)} collective-permute-done((bf16[512,128]{1,0:T(8,128)(2,1)S(1)}, bf16[512,128]{1,0:T(8,128)(2,1)S(1)}, u32[]{:S(2)}, u32[]{:S(2)}) %collective-permute-start.15) | collective-permute-done | bytes 131104 | tf_op jit(solution)/shard_map/ppermute | solution.py:22
  59.1 0.0 copy-start
  59.1 0.0 copy-start.1
  59.2 0.7 %copy-done = f32[512,128]{1,0:T(8,128)} copy-done((f32[512,128]{1,0:T(8,128)}, f32[512,128]{1,0:T(8,128)S(1)}, u32[]{:S(2)}) %copy-start) | copy-done | bytes 262168
  59.8 0.1 copy-done.1
  (10 shorter events, 0.2 us)
Async XLA Ops:
  0.6 9.8 %collective-permute-start = (bf16[512,128]{1,0:T(8,128)(2,1)}, bf16[512,128]{1,0:T(8,128)(2,1)S(1)}, u32[]{:S(2)}, u32[]{:S(2)}) collective-permute-start(bf16[512,128]{1,0:T(8,128)(2,1)} %bitcast.6), channel_id=1, source_target_pairs={{0,8},{1,9},{16,24},{17,25}} | collective-permute-start | bytes 393224 | tf_op jit(solution)/shard_map/ppermute | solution.py:22
  6.6 5.2 %collective-permute-start.2 = (bf16[512,128]{1,0:T(8,128)(2,1)}, bf16[512,128]{1,0:T(8,128)(2,1)S(1)}, u32[]{:S(2)}, u32[]{:S(2)}) collective-permute-start(bf16[512,128]{1,0:T(8,128)(2,1)} %bitcast.8), channel_id=1, source_target_pairs={{0,2},{1,3},{16,18},{17,19}} | collective-permute-start | bytes 393224 | tf_op jit(solution)/shard_map/ppermute | solution.py:22
  7.9 4.6 %collective-permute-start.1 = (bf16[512,128]{1,0:T(8,128)(2,1)}, bf16[512,128]{1,0:T(8,128)(2,1)S(1)}, u32[]{:S(2)}, u32[]{:S(2)}) collective-permute-start(bf16[512,128]{1,0:T(8,128)(2,1)} %bitcast.9), channel_id=1, source_target_pairs={{0,10},{1,11},{16,26},{17,27}} | collective-permute-start | bytes 393224 | tf_op jit(solution)/shard_map/ppermute | solution.py:22
  10.4 3.8 %collective-permute-start.4 = (bf16[256,128]{1,0:T(8,128)(2,1)S(1)}, bf16[256,128]{1,0:T(8,128)(2,1)S(1)}, u32[]{:S(2)}, u32[]{:S(2)}) collective-permute-start(bf16[256,128]{1,0:T(8,128)(2,1)S(1)} %get-tuple-element.64), channel_id=1, source_target_pairs={{2,14},{3,15},{18,30},{19,31}} | collective-permute-start | bytes 196616 | tf_op jit(solution)/shard_map/ppermute | solution.py:22
  11.1 3.1 %collective-permute-start.3 = (bf16[256,128]{1,0:T(8,128)(2,1)S(1)}, bf16[256,128]{1,0:T(8,128)(2,1)S(1)}, u32[]{:S(2)}, u32[]{:S(2)}) collective-permute-start(bf16[256,128]{1,0:T(8,128)(2,1)S(1)} %get-tuple-element.64), channel_id=1, source_target_pairs={{2,10},{4,12},{6,14},{3,11},{5,13},{7,15},{18,26},{20,28},{22,30},... | collective-permute-start | bytes 196616 | tf_op jit(solution)/shard_map/ppermute | solution.py:22
  14.2 7.2 %collective-permute-start.5 = (bf16[768,128]{1,0:T(8,128)(2,1)S(1)}, bf16[768,128]{1,0:T(8,128)(2,1)S(1)}, u32[]{:S(2)}, u32[]{:S(2)}) collective-permute-start(bf16[768,128]{1,0:T(8,128)(2,1)S(1)} %pad_maximum_fusion), channel_id=1, source_target_pairs={{0,4},{2,6},{4,8},{6,10},{8,12},{10,14},{1,5},{3,7},{5,9},{7,11},{... | collective-permute-start | bytes 589832 | tf_op jit(solution)/shard_map/ppermute | solution.py:22
  17.2 5.8 %collective-permute-start.6 = (bf16[512,128]{1,0:T(8,128)(2,1)S(1)}, bf16[512,128]{1,0:T(8,128)(2,1)S(1)}, u32[]{:S(2)}, u32[]{:S(2)}) collective-permute-start(bf16[512,128]{1,0:T(8,128)(2,1)S(1)} %maximum_select_fusion), channel_id=1, source_target_pairs={{0,2},{2,0},{4,6},{6,4},{8,10},{10,8},{12,14},{14,12},{1,3},{3,1},... | collective-permute-start | bytes 393224 | tf_op jit(solution)/shard_map/ppermute | solution.py:22
  23.0 5.7 %collective-permute-start.7 = (bf16[768,128]{1,0:T(8,128)(2,1)S(1)}, bf16[768,128]{1,0:T(8,128)(2,1)S(1)}, u32[]{:S(2)}, u32[]{:S(2)}) collective-permute-start(bf16[768,128]{1,0:T(8,128)(2,1)S(1)} %pad_maximum_fusion.1), channel_id=1, source_target_pairs={{0,2},{2,0},{4,6},{6,4},{8,10},{10,8},{12,14},{14,12},{1,3},{3,1},... | collective-permute-start | bytes 589832 | tf_op jit(solution)/shard_map/ppermute | solution.py:22
  32.5 7.1 %collective-permute-start.8 = (bf16[1280,128]{1,0:T(8,128)(2,1)S(1)}, bf16[1280,128]{1,0:T(8,128)(2,1)S(1)}, u32[]{:S(2)}, u32[]{:S(2)}) collective-permute-start(bf16[1280,128]{1,0:T(8,128)(2,1)S(1)} %get-tuple-element.82), channel_id=1, source_target_pairs={{0,2},{2,0},{4,6},{6,4},{8,10},{10,8},{12,14},{14,12},{1,3},{3,1},... | collective-permute-start | bytes 983048 | tf_op jit(solution)/shard_map/ppermute | solution.py:22
  39.7 9.7 %collective-permute-start.11 = (bf16[512,128]{1,0:T(8,128)(2,1)S(1)}, bf16[512,128]{1,0:T(8,128)(2,1)S(1)}, u32[]{:S(2)}, u32[]{:S(2)}) collective-permute-start(bf16[512,128]{1,0:T(8,128)(2,1)S(1)} %add_convert_fusion.1), channel_id=1, source_target_pairs={{12,0},{14,2},{13,1},{15,3},{28,16},{30,18},{29,17},{31,19}} | collective-permute-start | bytes 393224 | tf_op jit(solution)/shard_map/ppermute | solution.py:22
  41.0 10.0 %collective-permute-start.10 = (bf16[512,128]{1,0:T(8,128)(2,1)S(1)}, bf16[512,128]{1,0:T(8,128)(2,1)S(1)}, u32[]{:S(2)}, u32[]{:S(2)}) collective-permute-start(bf16[512,128]{1,0:T(8,128)(2,1)S(1)} %add_convert_fusion.1), channel_id=1, source_target_pairs={{8,0},{10,2},{9,1},{11,3},{24,16},{26,18},{25,17},{27,19}} | collective-permute-start | bytes 393224 | tf_op jit(solution)/shard_map/ppermute | solution.py:22
  42.3 9.3 %collective-permute-start.9 = (bf16[512,128]{1,0:T(8,128)(2,1)S(1)}, bf16[512,128]{1,0:T(8,128)(2,1)S(1)}, u32[]{:S(2)}, u32[]{:S(2)}) collective-permute-start(bf16[512,128]{1,0:T(8,128)(2,1)S(1)} %add_convert_fusion.1), channel_id=1, source_target_pairs={{4,0},{6,2},{5,1},{7,3},{20,16},{22,18},{21,17},{23,19}} | collective-permute-start | bytes 393224 | tf_op jit(solution)/shard_map/ppermute | solution.py:22
  43.7 9.3 %collective-permute-start.12 = (bf16[256,128]{1,0:T(8,128)(2,1)S(1)}, bf16[256,128]{1,0:T(8,128)(2,1)S(1)}, u32[]{:S(2)}, u32[]{:S(2)}) collective-permute-start(bf16[256,128]{1,0:T(8,128)(2,1)S(1)} %get-tuple-element.87), channel_id=1, source_target_pairs={{6,2},{8,4},{10,6},{12,8},{14,10},{7,3},{9,5},{11,7},{13,9},{15,11... | collective-permute-start | bytes 196616 | tf_op jit(solution)/shard_map/ppermute | solution.py:22
  44.3 8.6 %collective-permute-start.14 = (bf16[256,128]{1,0:T(8,128)(2,1)S(1)}, bf16[256,128]{1,0:T(8,128)(2,1)S(1)}, u32[]{:S(2)}, u32[]{:S(2)}) collective-permute-start(bf16[256,128]{1,0:T(8,128)(2,1)S(1)} %get-tuple-element.88), channel_id=1, source_target_pairs={{14,2},{15,3},{30,18},{31,19}} | collective-permute-start | bytes 196616 | tf_op jit(solution)/shard_map/ppermute | solution.py:22
  49.4 3.6 %collective-permute-start.13 = (bf16[256,128]{1,0:T(8,128)(2,1)S(1)}, bf16[256,128]{1,0:T(8,128)(2,1)S(1)}, u32[]{:S(2)}, u32[]{:S(2)}) collective-permute-start(bf16[256,128]{1,0:T(8,128)(2,1)S(1)} %get-tuple-element.89), channel_id=1, source_target_pairs={{10,2},{12,4},{14,6},{11,3},{13,5},{15,7},{26,18},{28,20},{30,22},... | collective-permute-start | bytes 196616 | tf_op jit(solution)/shard_map/ppermute | solution.py:22
  51.7 7.4 %collective-permute-start.15 = (bf16[512,128]{1,0:T(8,128)(2,1)S(1)}, bf16[512,128]{1,0:T(8,128)(2,1)S(1)}, u32[]{:S(2)}, u32[]{:S(2)}) collective-permute-start(bf16[512,128]{1,0:T(8,128)(2,1)S(1)} %get-tuple-element.86), channel_id=1, source_target_pairs={{2,0},{3,1},{18,16},{19,17}} | collective-permute-start | bytes 393224 | tf_op jit(solution)/shard_map/ppermute | solution.py:22
  59.1 0.7 %copy-start = (f32[512,128]{1,0:T(8,128)}, f32[512,128]{1,0:T(8,128)S(1)}, u32[]{:S(2)}) copy-start(f32[512,128]{1,0:T(8,128)S(1)} %get-tuple-element.92) | copy-start | bytes 786436
  59.1 0.8 %copy-start.1 = (f32[512,128]{1,0:T(8,128)}, f32[512,128]{1,0:T(8,128)S(1)}, u32[]{:S(2)}) copy-start(f32[512,128]{1,0:T(8,128)S(1)} %get-tuple-element.93) | copy-start | bytes 786436

commit v13 on v12

--- a/solution.py
+++ b/solution.py
@@ -140,15 +140,14 @@
             stats[head, 2:3, span] = jnp.sum(e * dp, axis=0, keepdims=True)
 
 
-def probs_kernel(sources, targets, heads_kv, scale, *refs):
+def probs_kernel(sources, heads_kv, scale, *refs):
     prompt_k, prompt_v, qh, gh, bias, weight_ref, e_ref, dp_ref, stats, block_ref = refs[:10]
-    n_out = 1 + max(target for target, _ in targets)
-    outs = refs[10 : 10 + n_out]
-    kh, ds_ref, p_own, vh, p_ref, grads, wide = refs[10 + n_out :]
+    send_ref, keep_ref, kh, ds_ref, p_behind, p_own, vh, p_ref, grads, wide = refs[10:]
     tokens = TD * TILE
     front = CAP * TILE
     fresh = tokens + len(sources) * front
-    before = tokens + len(targets) * front
+    behind = p_behind.shape[1]
+    before = tokens + behind
     columns = CHUNK * 8
     rate = scale * math.log2(math.e)
     device = lax.axis_index("node")
@@ -176,34 +175,43 @@
             p = e * weight
             delta = jnp.sum(p * dp, axis=0, keepdims=True) + weight_early * stats[head, 2:3, span]
             ds_ref[head, :fresh, span] = (p * (dp - delta)).astype(BF16)
-            p_ref[head % 2, :fresh, span] = p.astype(BF16)
+            p_ref[head % 2, :, span] = p[:tokens].astype(BF16)
+            p_behind[head, : fresh - tokens, span] = p[tokens:].astype(BF16)
             p = e_ref[head, :rows, span] * weight_early
             ds_ref[head, fresh : fresh + rows, span] = (p * (dp_ref[head, :rows, span] - delta)).astype(BF16)
-            p_ref[head % 2, fresh:, span] = p[: before - fresh].astype(BF16)
+            p_behind[head, fresh - tokens :, span] = p[: before - fresh].astype(BF16)
             p_own[head, : fresh + rows - before, span] = p[before - fresh :].astype(BF16)
-        grads[0, head] = scale * jnp.dot(ds_ref[head, :before], qh[head], preferred_element_type=F32)
+        grads[0, head] = scale * jnp.dot(ds_ref[head, :tokens], qh[head], preferred_element_type=F32)
         grads[1, head] = jnp.dot(p_ref[head % 2], gh[head], preferred_element_type=F32)
 
-    rows = tokens * heads_kv
-    rows_front = front * heads_kv
     even = lax.rem(device, 2) == 0
     for side in range(2):
-        dprompt = join_heads([grads[side, h, :tokens] for h in range(heads_kv)], tokens, heads_kv, wide).astype(BF16)
+        dprompt = join_heads([grads[side, h] for h in range(heads_kv)], tokens, heads_kv, wide).astype(BF16)
         kept = even if side == 0 else jnp.logical_not(even)
 
         @pl.when(kept)
         def _():
-            outs[1][:rows] = dprompt
+            keep_ref[...] = dprompt
 
         @pl.when(jnp.logical_not(kept))
         def _():
-            outs[0][:rows] = dprompt
-
+            send_ref[...] = dprompt
+
+
+def windows_kernel(targets, heads_kv, scale, qh, gh, ds_ref, p_behind, send_ref, keep_ref, grads, wide):
+    front = CAP * TILE
+    tokens = TD * TILE
+    behind = p_behind.shape[1]
+    for head in range(heads_kv):
+        ds = ds_ref[head, tokens : tokens + behind]
+        grads[0, head] = scale * jnp.dot(ds, qh[head], preferred_element_type=F32)
+        grads[1, head] = jnp.dot(p_behind[head], gh[head], preferred_element_type=F32)
+    for side in range(2):
         for k, (target, start) in enumerate(targets):
-            span = slice(tokens + k * front, tokens + (k + 1) * front)
+            span = slice(k * front, (k + 1) * front)
             block = join_heads([grads[side, h, span] for h in range(heads_kv)], front, heads_kv, wide).astype(BF16)
-            start += side * rows_front
-            outs[target][start : start + rows_front] = block
+            start += side * front * heads_kv
+            (send_ref, keep_ref)[target][start : start + front * heads_kv] = block
 
 
 def grads_kernel(heads_kv, scale, *refs):
@@ -314,35 +322,50 @@
     )
 
 
-def probs(sources, targets, prompt_k, prompt_v, qh, gh, own, parts, block):
+def probs(sources, behind, prompt_k, prompt_v, qh, gh, own, parts, block):
     _, own_v, bias, weight = own
     heads_kv, tokens, head_size = own_v.shape
     rows = tokens * heads_kv
     front = CAP * TILE
-    unit = 2 * front * heads_kv
     fresh = tokens + len(sources) * front
-    before = tokens + len(targets) * front
-    sizes = [max(start for target, start in targets if target == t) + unit for t in range(1 + max(targets)[0])]
+    before = tokens + behind * front
     array = jax.ShapeDtypeStruct
     work = heads_kv * tokens * 8 * (before + tokens)
     return call(
-        functools.partial(probs_kernel, sources, targets, heads_kv, head_size**-0.5),
+        functools.partial(probs_kernel, sources, heads_kv, head_size**-0.5),
         "probs",
         (prompt_k, prompt_v, qh, gh, bias, weight, *parts, block),
-        [array((size, head_size), BF16) for size in sizes]
+        [array((rows, head_size), BF16)] * 2
         + [
             array((heads_kv, fresh, head_size), BF16),
             array((heads_kv, before + tokens, tokens * 8), BF16),
+            array((heads_kv, behind * front, tokens * 8), BF16),
             array((heads_kv, tokens, tokens * 8), BF16),
         ],
         [
             pltpu.VMEM((heads_kv, fresh, head_size), BF16),
-            pltpu.VMEM((2, before, tokens * 8), BF16),
-            pltpu.VMEM((2, heads_kv, before, head_size), F32),
+            pltpu.VMEM((2, tokens, tokens * 8), BF16),
+            pltpu.VMEM((2, heads_kv, tokens, head_size), F32),
             pltpu.VMEM((rows, head_size), F32),
         ],
-        flops=6 * work * head_size,
+        flops=5 * work * head_size,
         transcendentals=work,
+    )
+
+
+def windows(targets, qh, gh, ds, p_behind):
+    heads_kv, behind, _ = p_behind.shape
+    head_size = qh.shape[2]
+    front = CAP * TILE * heads_kv
+    count = [sum(target == t for target, _ in targets) for t in (0, 1)]
+    array = jax.ShapeDtypeStruct
+    return call(
+        functools.partial(windows_kernel, targets, heads_kv, head_size**-0.5),
+        "windows",
+        (qh, gh, ds, p_behind),
+        [array((2 * front * n, head_size), BF16) for n in count],
+        [pltpu.VMEM((2, heads_kv, behind, head_size), F32), pltpu.VMEM((front, head_size), F32)],
+        flops=4 * p_behind.size * head_size,
     )
 
 
@@ -431,27 +454,30 @@
     return held, other, third, fresh_sources, early_sources, (second, far), pack(queries, grad_out, keys.shape[0] // queries.shape[0])
 
 
-def give_back(size, unit, rows, where, send, keep, ready):
+def give_back(size, unit, where, prompt, behind, finish):
     even, lower, _ = where
     neighbours = [(i, i ^ 1) for i in range(size)]
     far_route = back(shift_route(4, size)[1:])
-    two, four, six = units(keep, rows, unit, 3)
+    send, keep = prompt
+    rows = keep.shape[0]
+    two, four, six = units(behind[1], 0, unit, 3)
     if size == W + 1:
-        third = permuted(send, neighbours)
-        total = after(added(keep[:rows], third[:rows]).astype(BF16), ready)
-        near, first, last = units(third, rows, unit, 3)
+        total = added(keep, permuted(send, neighbours)).astype(BF16)
+        finished = finish(total)
+        near, first, last = units(permuted(behind[0], neighbours), 0, unit, 3)
         none = jnp.zeros_like(first)
         parts = [permuted(total, [(j, 0), (j + 1, 1)]) for j in range(2, size, 2)]
         two = permuted(added(two, near).astype(BF16), back(shift_route(2, size)[1:]))
-        four = permuted(added(four, jnp.where(even, last, first)).astype(BF16), far_route)
+        four = after(added(four, jnp.where(even, last, first)).astype(BF16), finished[1])
+        four = permuted(four, far_route)
         six = permuted(added(six, jnp.where(even, none, last)).astype(BF16), [(7, 1)])
         total = added(total, *parts).astype(BF16)
         mine = added(jnp.where(even, first, none), two, four, six)
-        return total, permuted(total, [(1, 0)]).astype(F32), mine
+        return finished, total, permuted(total, [(1, 0)]).astype(F32), mine
     strides = [2**i for i in range(2, size.bit_length()) if 2**i < size]
     top = strides[-1]
-    zero, *third = units(permuted(send[rows:], back(shift_route(1, size))), 0, unit, 4)
-    total = added(keep[:rows], permuted(send[:rows], neighbours)).astype(BF16)
+    zero, *third = units(permuted(behind[0], back(shift_route(1, size))), 0, unit, 4)
+    total = added(keep, permuted(send, neighbours)).astype(BF16)
     two, four, six = (added(x, y).astype(BF16) for x, y in zip((two, four, six), third))
     second = permuted(jnp.concatenate([total, two, six]), back(shift_route(2, size)))
     four = added(four, second[rows + unit :])
@@ -462,7 +488,7 @@
     keys_far = permuted(total, [(top, 0)])
     values_far = permuted(total, [(top + 1, 0)])
     values_next = permuted(total, [(1, 0)])
-    return added(total, keys_far), added(values_next, values_far), mine
+    return finish(send), added(total, keys_far), added(values_next, values_far), mine
 
 
 def per_device(size, queries, keys, values, grad_out, parents, lengths):
@@ -477,10 +503,10 @@
 
     if size == W + 1:
         order = [(1, 3), (2, 2), (3, 1), (4, 4), (5, 5), (6, 6)]
-        targets = [(k % 2, rows + k // 2 * unit) for k in range(window)]
+        targets = [(k % 2, k // 2 * unit) for k in range(window)]
     else:
         order = [(k, k) for k in (1, 3, 5, 7, 2, 4, 6)]
-        targets = [(0, rows + i * unit) for i in range(4)] + [(1, rows + i * unit) for i in range(3)]
+        targets = [(0, i * unit) for i in range(4)] + [(1, i * unit) for i in range(3)]
     head, held, *own = load(order, keys, values, parents, lengths, tokens)
     head, *where = lax.optimization_barrier((head, lax.rem(device, 2) == 0, lax.rem(device, 4) < 2, device == 0))
     even, _, root = where
@@ -489,9 +515,15 @@
     )
     kh_early, *parts = early(len(fresh_sources), early_sources, qh, gh, own, blocks)
     prompt_k, prompt_v = jnp.where(even, held, other), jnp.where(even, other, held)
-    send, keep, kh, ds, p_own = probs(fresh_sources, targets, prompt_k, prompt_v, qh, gh, own, parts, block)
-    grad_queries, dk, dv = grads(qh, gh, kh, kh_early, ds, p_own)
-    prompt_k, prompt_v, mine = give_back(size, unit, rows, where, send, keep, dk)
+    *prompt, kh, ds, p_behind, p_own = probs(
+        fresh_sources, len(targets), prompt_k, prompt_v, qh, gh, own, parts, block
+    )
+    behind = windows(targets, qh, gh, ds, p_behind)
+
+    def finish(earlier):
+        return grads(qh, gh, kh, kh_early, ds, after(p_own, earlier))
+
+    (grad_queries, dk, dv), prompt_k, prompt_v, mine = give_back(size, unit, where, prompt, behind, finish)
     own = []
     for side, local, prompt in ((0, dk, prompt_k), (1, dv, prompt_v)):
         whole = local + jnp.where(root, prompt.astype(F32), 0.0)

time: 60.3 us -> 59.7 us (0.990)
  waiting for transfers between devices: 20.2 us -> 18.4 us
  Pallas kernels: 10.7 us -> 11.8 us
    ppermute x16 -> x17, waiting for transfers between devices: 20.2 us -> 18.4 us  [permuted(): return lax.ppermute(block, 'node', route)]
    pallas_call x5 -> x6, Pallas kernels: 10.7 us -> 11.8 us  [call(): pl.pallas_call(kernel, in_specs=[place] * len(operands), out_specs=[VMEM]...]
    ppermute x16 -> x17, starting transfers between devices: 26.8 us -> 26.9 us  [permuted(): return lax.ppermute(block, 'node', route)]
  transfers between devices with their start and end apart: 16 -> 17, of which waited for: 9 -> 8; matrix products, arithmetic and copies ran while one was open for 1% -> 1% of each run, Pallas kernels for 11% -> 13%
where the time goes in v13:
time: 59.7 us; the launch traced here: 59.3 us
  starting transfers between devices  26.9 us (45%)
  waiting for transfers between devices  18.4 us (31%)
  Pallas kernels  11.8 us (20%)
  between operations  0.93 us (2%)
  local copies, waits for them, and re-layouts  0.78 us (1%)
    ppermute x17, starting transfers between devices, permuted(): return lax.ppermute(block, 'node', route)  26.9 us
    ppermute x17, waiting for transfers between devices, permuted(): return lax.ppermute(block, 'node', route)  18.4 us
    pallas_call x6, Pallas kernels, call(): pl.pallas_call(kernel, in_specs=[place] * len(operands), out_specs=[VMEM]...  11.8 us
  transfers between devices with their start and end apart: 17, of which 8 were waited for; matrix products, arithmetic and copies ran while one was open for 1% of the time, Pallas kernels for 13%

profile of v13, /device:TPU:0, one launch (start us, length us, event | category | flops | bytes accessed | tf_op | source)
XLA Modules:
  0.0 59.3 jit_solution(8762249631729172251)
XLA Ops:
  0.6 5.9 %collective-permute-start = (bf16[512,128]{1,0:T(8,128)(2,1)}, bf16[512,128]{1,0:T(8,128)(2,1)S(1)}, u32[]{:S(2)}, u32[]{:S(2)}) collective-permute-start(bf16[512,128]{1,0:T(8,128)(2,1)} %bitcast.6), channel_id=1, source_target_pairs={{0,8},{1,9},{16,24},{17,25}} | collective-permute-start | bytes 393224 | tf_op jit(solution)/shard_map/ppermute | solution.py:22
  6.6 1.3 %collective-permute-start.2 = (bf16[512,128]{1,0:T(8,128)(2,1)}, bf16[512,128]{1,0:T(8,128)(2,1)S(1)}, u32[]{:S(2)}, u32[]{:S(2)}) collective-permute-start(bf16[512,128]{1,0:T(8,128)(2,1)} %bitcast.8), channel_id=1, source_target_pairs={{0,2},{1,3},{16,18},{17,19}} | collective-permute-start | bytes 393224 | tf_op jit(solution)/shard_map/ppermute | solution.py:22
  7.9 1.3 %collective-permute-start.1 = (bf16[512,128]{1,0:T(8,128)(2,1)}, bf16[512,128]{1,0:T(8,128)(2,1)S(1)}, u32[]{:S(2)}, u32[]{:S(2)}) collective-permute-start(bf16[512,128]{1,0:T(8,128)(2,1)} %bitcast.9), channel_id=1, source_target_pairs={{0,10},{1,11},{16,26},{17,27}} | collective-permute-start | bytes 393224 | tf_op jit(solution)/shard_map/ppermute | solution.py:22
  9.2 1.2 %load.1 = (bf16[256,128]{1,0:T(8,128)(2,1)S(1)}, bf16[512,128]{1,0:T(8,128)(2,1)S(1)}, bf16[4,128,128]{2,1,0:T(8,128)(2,1)S(1)}, bf16[4,128,128]{2,1,0:T(8,128)(...) custom-call(s32[64]{0:T(128)} %refs_0_.1, s32[64]{0:T(128)} %refs_1_.1, bf16[512,128]{1,0:T(8,128)(2,1)} %bitcast.7, ...), custom_call_target="tpu_custom_call" | custom-call | flops 1048576 | bytes 983552 | tf_op jit(solution)/shard_map/load/pallas_call | solution.py:261
  10.4 0.0 collective-permute-done
  10.4 0.7 %collective-permute-start.4 = (bf16[256,128]{1,0:T(8,128)(2,1)S(1)}, bf16[256,128]{1,0:T(8,128)(2,1)S(1)}, u32[]{:S(2)}, u32[]{:S(2)}) collective-permute-start(bf16[256,128]{1,0:T(8,128)(2,1)S(1)} %get-tuple-element.68), channel_id=1, source_target_pairs={{2,14},{3,15},{18,30},{19,31}} | collective-permute-start | bytes 196616 | tf_op jit(solution)/shard_map/ppermute | solution.py:22
  11.1 0.7 %collective-permute-start.3 = (bf16[256,128]{1,0:T(8,128)(2,1)S(1)}, bf16[256,128]{1,0:T(8,128)(2,1)S(1)}, u32[]{:S(2)}, u32[]{:S(2)}) collective-permute-start(bf16[256,128]{1,0:T(8,128)(2,1)S(1)} %get-tuple-element.68), channel_id=1, source_target_pairs={{2,10},{4,12},{6,14},{3,11},{5,13},{7,15},{18,26},{20,28},{22,30},... | collective-permute-start | bytes 196616 | tf_op jit(solution)/shard_map/ppermute | solution.py:22
  11.8 0.0 collective-permute-done.2
  11.8 0.7 %collective-permute-done.1 = bf16[512,128]{1,0:T(8,128)(2,1)S(1)} collective-permute-done((bf16[512,128]{1,0:T(8,128)(2,1)}, bf16[512,128]{1,0:T(8,128)(2,1)S(1)}, u32[]{:S(2)}, u32[]{:S(2)}) %collective-permute-start.1) | collective-permute-done | bytes 131104 | tf_op jit(solution)/shard_map/ppermute | solution.py:22
  12.5 0.1 add_convert_fusion.2
  12.5 1.6 %pack.1 = (bf16[4,1024,128]{2,1,0:T(8,128)(2,1)S(1)}, bf16[4,1024,128]{2,1,0:T(8,128)(2,1)S(1)}) custom-call(bf16[128,32,128]{2,1,0:T(8,128)(2,1)} %q_ref, bf16[128,32,128]{2,1,0:T(8,128)(2,1)} %g_ref.1), custom_call_target="tpu_custom_call" | custom-call | flops 1048576 | bytes 4194304 | tf_op jit(solution)/shard_map/pack/pallas_call | solution.py:261
  14.2 0.0 collective-permute-done.4.refs_8_
  14.2 0.0 collective-permute-done.3.refs_7_
  14.2 2.9 %collective-permute-start.5 = (bf16[768,128]{1,0:T(8,128)(2,1)S(1)}, bf16[768,128]{1,0:T(8,128)(2,1)S(1)}, u32[]{:S(2)}, u32[]{:S(2)}) collective-permute-start(bf16[768,128]{1,0:T(8,128)(2,1)S(1)} %pad_maximum_fusion), channel_id=1, source_target_pairs={{0,4},{2,6},{4,8},{6,10},{8,12},{10,14},{1,5},{3,7},{5,9},{7,11},{... | collective-permute-start | bytes 589832 | tf_op jit(solution)/shard_map/ppermute | solution.py:22
  17.2 2.8 %collective-permute-start.6 = (bf16[512,128]{1,0:T(8,128)(2,1)S(1)}, bf16[512,128]{1,0:T(8,128)(2,1)S(1)}, u32[]{:S(2)}, u32[]{:S(2)}) collective-permute-start(bf16[512,128]{1,0:T(8,128)(2,1)S(1)} %maximum_select_fusion), channel_id=1, source_target_pairs={{0,2},{2,0},{4,6},{6,4},{8,10},{10,8},{12,14},{14,12},{1,3},{3,1},... | collective-permute-start | bytes 393224 | tf_op jit(solution)/shard_map/ppermute | solution.py:22
  20.0 1.4 %collective-permute-done.5.refs_5_ = bf16[768,128]{1,0:T(8,128)(2,1)S(1)} collective-permute-done((bf16[768,128]{1,0:T(8,128)(2,1)S(1)}, bf16[768,128]{1,0:T(8,128)(2,1)S(1)}, u32[]{:S(2)}, u32[]{:S(2)}) %collective-permute-start.5) | collective-permute-done | bytes 196640 | tf_op jit(solution)/shard_map/ppermute | solution.py:22
  21.5 1.4 %collective-permute-done.6.refs_6_ = bf16[512,128]{1,0:T(8,128)(2,1)S(1)} collective-permute-done((bf16[512,128]{1,0:T(8,128)(2,1)S(1)}, bf16[512,128]{1,0:T(8,128)(2,1)S(1)}, u32[]{:S(2)}, u32[]{:S(2)}) %collective-permute-start.6) | collective-permute-done | bytes 131104 | tf_op jit(solution)/shard_map/ppermute | solution.py:22
  23.0 2.0 %collective-permute-start.7 = (bf16[768,128]{1,0:T(8,128)(2,1)S(1)}, bf16[768,128]{1,0:T(8,128)(2,1)S(1)}, u32[]{:S(2)}, u32[]{:S(2)}) collective-permute-start(bf16[768,128]{1,0:T(8,128)(2,1)S(1)} %pad_maximum_fusion.1), channel_id=1, source_target_pairs={{0,2},{2,0},{4,6},{6,4},{8,10},{10,8},{12,14},{14,12},{1,3},{3,1},... | collective-permute-start | bytes 589832 | tf_op jit(solution)/shard_map/ppermute | solution.py:22
  25.0 1.6 %early.1 = (bf16[4,288,128]{2,1,0:T(8,128)(2,1)S(1)}, f32[4,288,1024]{2,1,0:T(8,128)S(1)}, f32[4,288,1024]{2,1,0:T(8,128)S(1)}, f32[4,8,1024]{2,1,0:T(8,128)S(1)}) custom-call(bf16[4,128,128]{2,1,0:T(8,128)(2,1)S(1)} %get-tuple-element.73.refs_0_, bf16[4,128,128]{2,1,0:T(8,128)(2,1)S(1)} %get-tuple-element.74.refs_1_, ...), custom_call_target="tpu_custom_call" | custom-call | flops 603979776 | bytes 12910592 | tf_op jit(solution)/shard_map/early/pallas_call | solution.py:261
  26.6 2.0 %collective-permute-done.7.refs_9_ = bf16[768,128]{1,0:T(8,128)(2,1)S(1)} collective-permute-done((bf16[768,128]{1,0:T(8,128)(2,1)S(1)}, bf16[768,128]{1,0:T(8,128)(2,1)S(1)}, u32[]{:S(2)}, u32[]{:S(2)}) %collective-permute-start.7) | collective-permute-done | bytes 196640 | tf_op jit(solution)/shard_map/ppermute | solution.py:22
  28.7 4.0 %probs.1 = (bf16[512,128]{1,0:T(8,128)(2,1)S(1)}, bf16[512,128]{1,0:T(8,128)(2,1)S(1)}, bf16[4,160,128]{2,1,0:T(8,128)(2,1)S(1)}, bf16[4,448,1024]{2,1,0:T(8,128...) custom-call(bf16[512,128]{1,0:T(8,128)(2,1)S(1)} %get-tuple-element.99.refs_0_, ...), custom_call_target="tpu_custom_call" | custom-call | flops 1174405120 | bytes 19103744 | tf_op jit(solution)/shard_map/probs/pallas_call | solution.py:261
  32.6 2.1 %collective-permute-start.8 = (bf16[512,128]{1,0:T(8,128)(2,1)S(1)}, bf16[512,128]{1,0:T(8,128)(2,1)S(1)}, u32[]{:S(2)}, u32[]{:S(2)}) collective-permute-start(bf16[512,128]{1,0:T(8,128)(2,1)S(1)} %get-tuple-element.83), channel_id=1, source_target_pairs={{0,2},{2,0},{4,6},{6,4},{8,10},{10,8},{12,14},{14,12},{1,3},{3,1},... | collective-permute-start | bytes 393224 | tf_op jit(solution)/shard_map/ppermute | solution.py:22
  34.7 1.0 %windows.1 = (bf16[768,128]{1,0:T(8,128)(2,1)S(1)}, bf16[768,128]{1,0:T(8,128)(2,1)S(1)}) custom-call(bf16[4,1024,128]{2,1,0:T(8,128)(2,1)S(1)} %get-tuple-element.63.refs_2_.refs_0_.qh, bf16[4,1024,128]{2,1,0:T(8,128)(2,1)S(1)} %get-tuple-element.64.refs_3_.refs_1_.gh, bf16[4,448,1024]{2,1,0:T(8,128)(2,1)S(1)} %get-tuple-element.80.refs_4_.ds_ref, ...), custom_call_target="tpu_custom_call" | custom-call | flops 402653184 | bytes 7733248 | tf_op jit(solution)/shard_map/windows/pallas_call | solution.py:261
  35.7 0.1 collective-permute-start.12
  35.8 2.7 %collective-permute-done.8 = bf16[512,128]{1,0:T(8,128)(2,1)S(1)} collective-permute-done((bf16[512,128]{1,0:T(8,128)(2,1)S(1)}, bf16[512,128]{1,0:T(8,128)(2,1)S(1)}, u32[]{:S(2)}, u32[]{:S(2)}) %collective-permute-start.8) | collective-permute-done | bytes 131104 | tf_op jit(solution)/shard_map/ppermute | solution.py:22
  38.6 1.3 %collective-permute-start.11 = (bf16[512,128]{1,0:T(8,128)(2,1)S(1)}, bf16[512,128]{1,0:T(8,128)(2,1)S(1)}, u32[]{:S(2)}, u32[]{:S(2)}) collective-permute-start(bf16[512,128]{1,0:T(8,128)(2,1)S(1)} %add_convert_fusion.1), channel_id=1, source_target_pairs={{12,0},{14,2},{13,1},{15,3},{28,16},{30,18},{29,17},{31,19}} | collective-permute-start | bytes 393224 | tf_op jit(solution)/shard_map/ppermute | solution.py:22
  39.9 1.3 %collective-permute-start.10 = (bf16[512,128]{1,0:T(8,128)(2,1)S(1)}, bf16[512,128]{1,0:T(8,128)(2,1)S(1)}, u32[]{:S(2)}, u32[]{:S(2)}) collective-permute-start(bf16[512,128]{1,0:T(8,128)(2,1)S(1)} %add_convert_fusion.1), channel_id=1, source_target_pairs={{8,0},{10,2},{9,1},{11,3},{24,16},{26,18},{25,17},{27,19}} | collective-permute-start | bytes 393224 | tf_op jit(solution)/shard_map/ppermute | solution.py:22
  41.2 1.3 %collective-permute-start.9 = (bf16[512,128]{1,0:T(8,128)(2,1)S(1)}, bf16[512,128]{1,0:T(8,128)(2,1)S(1)}, u32[]{:S(2)}, u32[]{:S(2)}) collective-permute-start(bf16[512,128]{1,0:T(8,128)(2,1)S(1)} %add_convert_fusion.1), channel_id=1, source_target_pairs={{4,0},{6,2},{5,1},{7,3},{20,16},{22,18},{21,17},{23,19}} | collective-permute-start | bytes 393224 | tf_op jit(solution)/shard_map/ppermute | solution.py:22
  42.5 2.4 %grads.1 = (bf16[128,32,128]{2,1,0:T(8,128)(2,1)}, f32[512,128]{1,0:T(8,128)S(1)}, f32[512,128]{1,0:T(8,128)S(1)}) custom-call(bf16[4,1024,128]{2,1,0:T(8,128)(2,1)S(1)} %get-tuple-element.63.refs_2_.refs_0_.qh, bf16[4,1024,128]{2,1,0:T(8,128)(2,1)S(1)} %get-tuple-element.64.refs_3_.refs_1_.gh, bf16[4,160,128]{2,1,0:T(8,128)(2,1)S(1)} %get-tuple-element.78.refs_2_, ...), custom_call_target="tpu_custom_call" | custom-call | flops 469762048 | bytes 8847360 | tf_op jit(solution)/shard_map/grads/pallas_call | solution.py:261
  44.9 0.0 collective-permute-done.12
  44.9 0.1 add_convert_fusion.5
  45.0 0.7 %collective-permute-start.14 = (bf16[256,128]{1,0:T(8,128)(2,1)S(1)}, bf16[256,128]{1,0:T(8,128)(2,1)S(1)}, u32[]{:S(2)}, u32[]{:S(2)}) collective-permute-start(bf16[256,128]{1,0:T(8,128)(2,1)S(1)} %get-tuple-element.91), channel_id=1, source_target_pairs={{10,2},{12,4},{14,6},{11,3},{13,5},{15,7},{26,18},{28,20},{30,22},... | collective-permute-start | bytes 196616 | tf_op jit(solution)/shard_map/ppermute | solution.py:22
  45.6 0.7 %collective-permute-start.13 = (bf16[256,128]{1,0:T(8,128)(2,1)S(1)}, bf16[256,128]{1,0:T(8,128)(2,1)S(1)}, u32[]{:S(2)}, u32[]{:S(2)}) collective-permute-start(bf16[256,128]{1,0:T(8,128)(2,1)S(1)} %get-tuple-element.95), channel_id=1, source_target_pairs={{6,2},{8,4},{10,6},{12,8},{14,10},{7,3},{9,5},{11,7},{13,9},{15,11... | collective-permute-start | bytes 196616 | tf_op jit(solution)/shard_map/ppermute | solution.py:22
  46.3 2.1 %collective-permute-done.11 = bf16[512,128]{1,0:T(8,128)(2,1)S(1)} collective-permute-done((bf16[512,128]{1,0:T(8,128)(2,1)S(1)}, bf16[512,128]{1,0:T(8,128)(2,1)S(1)}, u32[]{:S(2)}, u32[]{:S(2)}) %collective-permute-start.11) | collective-permute-done | bytes 131104 | tf_op jit(solution)/shard_map/ppermute | solution.py:22
  48.3 0.7 %collective-permute-start.15 = (bf16[256,128]{1,0:T(8,128)(2,1)S(1)}, bf16[256,128]{1,0:T(8,128)(2,1)S(1)}, u32[]{:S(2)}, u32[]{:S(2)}) collective-permute-start(bf16[256,128]{1,0:T(8,128)(2,1)S(1)} %get-tuple-element.96), channel_id=1, source_target_pairs={{14,2},{15,3},{30,18},{31,19}} | collective-permute-start | bytes 196616 | tf_op jit(solution)/shard_map/ppermute | solution.py:22
  49.0 1.5 %collective-permute-done.10 = bf16[512,128]{1,0:T(8,128)(2,1)S(1)} collective-permute-done((bf16[512,128]{1,0:T(8,128)(2,1)S(1)}, bf16[512,128]{1,0:T(8,128)(2,1)S(1)}, u32[]{:S(2)}, u32[]{:S(2)}) %collective-permute-start.10) | collective-permute-done | bytes 131104 | tf_op jit(solution)/shard_map/ppermute | solution.py:22
  50.5 0.0 collective-permute-done.9
  50.5 0.1 select_add_fusion.1
  50.6 1.3 %collective-permute-start.16 = (bf16[512,128]{1,0:T(8,128)(2,1)S(1)}, bf16[512,128]{1,0:T(8,128)(2,1)S(1)}, u32[]{:S(2)}, u32[]{:S(2)}) collective-permute-start(bf16[512,128]{1,0:T(8,128)(2,1)S(1)} %get-tuple-element.94), channel_id=1, source_target_pairs={{2,0},{3,1},{18,16},{19,17}} | collective-permute-start | bytes 393224 | tf_op jit(solution)/shard_map/ppermute | solution.py:22
  51.9 0.0 collective-permute-done.14
  51.9 0.0 collective-permute-done.13
  51.9 0.0 collective-permute-done.15
  52.0 6.5 %collective-permute-done.16 = bf16[512,128]{1,0:T(8,128)(2,1)S(1)} collective-permute-done((bf16[512,128]{1,0:T(8,128)(2,1)S(1)}, bf16[512,128]{1,0:T(8,128)(2,1)S(1)}, u32[]{:S(2)}, u32[]{:S(2)}) %collective-permute-start.16) | collective-permute-done | bytes 131104 | tf_op jit(solution)/shard_map/ppermute | solution.py:22
  58.5 0.0 copy-start
  58.5 0.0 copy-start.1
  58.5 0.7 %copy-done = f32[512,128]{1,0:T(8,128)} copy-done((f32[512,128]{1,0:T(8,128)}, f32[512,128]{1,0:T(8,128)S(1)}, u32[]{:S(2)}) %copy-start) | copy-done | bytes 262168
  59.2 0.1 copy-done.1
  (10 shorter events, 0.2 us)
Async XLA Ops:
  0.6 9.8 %collective-permute-start = (bf16[512,128]{1,0:T(8,128)(2,1)}, bf16[512,128]{1,0:T(8,128)(2,1)S(1)}, u32[]{:S(2)}, u32[]{:S(2)}) collective-permute-start(bf16[512,128]{1,0:T(8,128)(2,1)} %bitcast.6), channel_id=1, source_target_pairs={{0,8},{1,9},{16,24},{17,25}} | collective-permute-start | bytes 393224 | tf_op jit(solution)/shard_map/ppermute | solution.py:22
  6.6 5.2 %collective-permute-start.2 = (bf16[512,128]{1,0:T(8,128)(2,1)}, bf16[512,128]{1,0:T(8,128)(2,1)S(1)}, u32[]{:S(2)}, u32[]{:S(2)}) collective-permute-start(bf16[512,128]{1,0:T(8,128)(2,1)} %bitcast.8), channel_id=1, source_target_pairs={{0,2},{1,3},{16,18},{17,19}} | collective-permute-start | bytes 393224 | tf_op jit(solution)/shard_map/ppermute | solution.py:22
  7.9 4.6 %collective-permute-start.1 = (bf16[512,128]{1,0:T(8,128)(2,1)}, bf16[512,128]{1,0:T(8,128)(2,1)S(1)}, u32[]{:S(2)}, u32[]{:S(2)}) collective-permute-start(bf16[512,128]{1,0:T(8,128)(2,1)} %bitcast.9), channel_id=1, source_target_pairs={{0,10},{1,11},{16,26},{17,27}} | collective-permute-start | bytes 393224 | tf_op jit(solution)/shard_map/ppermute | solution.py:22
  10.4 3.8 %collective-permute-start.4 = (bf16[256,128]{1,0:T(8,128)(2,1)S(1)}, bf16[256,128]{1,0:T(8,128)(2,1)S(1)}, u32[]{:S(2)}, u32[]{:S(2)}) collective-permute-start(bf16[256,128]{1,0:T(8,128)(2,1)S(1)} %get-tuple-element.68), channel_id=1, source_target_pairs={{2,14},{3,15},{18,30},{19,31}} | collective-permute-start | bytes 196616 | tf_op jit(solution)/shard_map/ppermute | solution.py:22
  11.1 3.1 %collective-permute-start.3 = (bf16[256,128]{1,0:T(8,128)(2,1)S(1)}, bf16[256,128]{1,0:T(8,128)(2,1)S(1)}, u32[]{:S(2)}, u32[]{:S(2)}) collective-permute-start(bf16[256,128]{1,0:T(8,128)(2,1)S(1)} %get-tuple-element.68), channel_id=1, source_target_pairs={{2,10},{4,12},{6,14},{3,11},{5,13},{7,15},{18,26},{20,28},{22,30},... | collective-permute-start | bytes 196616 | tf_op jit(solution)/shard_map/ppermute | solution.py:22
  14.2 7.2 %collective-permute-start.5 = (bf16[768,128]{1,0:T(8,128)(2,1)S(1)}, bf16[768,128]{1,0:T(8,128)(2,1)S(1)}, u32[]{:S(2)}, u32[]{:S(2)}) collective-permute-start(bf16[768,128]{1,0:T(8,128)(2,1)S(1)} %pad_maximum_fusion), channel_id=1, source_target_pairs={{0,4},{2,6},{4,8},{6,10},{8,12},{10,14},{1,5},{3,7},{5,9},{7,11},{... | collective-permute-start | bytes 589832 | tf_op jit(solution)/shard_map/ppermute | solution.py:22
  17.2 5.8 %collective-permute-start.6 = (bf16[512,128]{1,0:T(8,128)(2,1)S(1)}, bf16[512,128]{1,0:T(8,128)(2,1)S(1)}, u32[]{:S(2)}, u32[]{:S(2)}) collective-permute-start(bf16[512,128]{1,0:T(8,128)(2,1)S(1)} %maximum_select_fusion), channel_id=1, source_target_pairs={{0,2},{2,0},{4,6},{6,4},{8,10},{10,8},{12,14},{14,12},{1,3},{3,1},... | collective-permute-start | bytes 393224 | tf_op jit(solution)/shard_map/ppermute | solution.py:22
  23.0 5.7 %collective-permute-start.7 = (bf16[768,128]{1,0:T(8,128)(2,1)S(1)}, bf16[768,128]{1,0:T(8,128)(2,1)S(1)}, u32[]{:S(2)}, u32[]{:S(2)}) collective-permute-start(bf16[768,128]{1,0:T(8,128)(2,1)S(1)} %pad_maximum_fusion.1), channel_id=1, source_target_pairs={{0,2},{2,0},{4,6},{6,4},{8,10},{10,8},{12,14},{14,12},{1,3},{3,1},... | collective-permute-start | bytes 589832 | tf_op jit(solution)/shard_map/ppermute | solution.py:22
  32.6 6.0 %collective-permute-start.8 = (bf16[512,128]{1,0:T(8,128)(2,1)S(1)}, bf16[512,128]{1,0:T(8,128)(2,1)S(1)}, u32[]{:S(2)}, u32[]{:S(2)}) collective-permute-start(bf16[512,128]{1,0:T(8,128)(2,1)S(1)} %get-tuple-element.83), channel_id=1, source_target_pairs={{0,2},{2,0},{4,6},{6,4},{8,10},{10,8},{12,14},{14,12},{1,3},{3,1},... | collective-permute-start | bytes 393224 | tf_op jit(solution)/shard_map/ppermute | solution.py:22
  35.7 9.2 %collective-permute-start.12 = (bf16[768,128]{1,0:T(8,128)(2,1)S(1)}, bf16[768,128]{1,0:T(8,128)(2,1)S(1)}, u32[]{:S(2)}, u32[]{:S(2)}) collective-permute-start(bf16[768,128]{1,0:T(8,128)(2,1)S(1)} %get-tuple-element.89), channel_id=1, source_target_pairs={{0,2},{2,0},{4,6},{6,4},{8,10},{10,8},{12,14},{14,12},{1,3},{3,1},... | collective-permute-start | bytes 589832 | tf_op jit(solution)/shard_map/ppermute | solution.py:22
  38.6 9.7 %collective-permute-start.11 = (bf16[512,128]{1,0:T(8,128)(2,1)S(1)}, bf16[512,128]{1,0:T(8,128)(2,1)S(1)}, u32[]{:S(2)}, u32[]{:S(2)}) collective-permute-start(bf16[512,128]{1,0:T(8,128)(2,1)S(1)} %add_convert_fusion.1), channel_id=1, source_target_pairs={{12,0},{14,2},{13,1},{15,3},{28,16},{30,18},{29,17},{31,19}} | collective-permute-start | bytes 393224 | tf_op jit(solution)/shard_map/ppermute | solution.py:22
  39.9 10.6 %collective-permute-start.10 = (bf16[512,128]{1,0:T(8,128)(2,1)S(1)}, bf16[512,128]{1,0:T(8,128)(2,1)S(1)}, u32[]{:S(2)}, u32[]{:S(2)}) collective-permute-start(bf16[512,128]{1,0:T(8,128)(2,1)S(1)} %add_convert_fusion.1), channel_id=1, source_target_pairs={{8,0},{10,2},{9,1},{11,3},{24,16},{26,18},{25,17},{27,19}} | collective-permute-start | bytes 393224 | tf_op jit(solution)/shard_map/ppermute | solution.py:22
  41.2 9.3 %collective-permute-start.9 = (bf16[512,128]{1,0:T(8,128)(2,1)S(1)}, bf16[512,128]{1,0:T(8,128)(2,1)S(1)}, u32[]{:S(2)}, u32[]{:S(2)}) collective-permute-start(bf16[512,128]{1,0:T(8,128)(2,1)S(1)} %add_convert_fusion.1), channel_id=1, source_target_pairs={{4,0},{6,2},{5,1},{7,3},{20,16},{22,18},{21,17},{23,19}} | collective-permute-start | bytes 393224 | tf_op jit(solution)/shard_map/ppermute | solution.py:22
  45.0 6.9 %collective-permute-start.14 = (bf16[256,128]{1,0:T(8,128)(2,1)S(1)}, bf16[256,128]{1,0:T(8,128)(2,1)S(1)}, u32[]{:S(2)}, u32[]{:S(2)}) collective-permute-start(bf16[256,128]{1,0:T(8,128)(2,1)S(1)} %get-tuple-element.91), channel_id=1, source_target_pairs={{10,2},{12,4},{14,6},{11,3},{13,5},{15,7},{26,18},{28,20},{30,22},... | collective-permute-start | bytes 196616 | tf_op jit(solution)/shard_map/ppermute | solution.py:22
  45.6 6.3 %collective-permute-start.13 = (bf16[256,128]{1,0:T(8,128)(2,1)S(1)}, bf16[256,128]{1,0:T(8,128)(2,1)S(1)}, u32[]{:S(2)}, u32[]{:S(2)}) collective-permute-start(bf16[256,128]{1,0:T(8,128)(2,1)S(1)} %get-tuple-element.95), channel_id=1, source_target_pairs={{6,2},{8,4},{10,6},{12,8},{14,10},{7,3},{9,5},{11,7},{13,9},{15,11... | collective-permute-start | bytes 196616 | tf_op jit(solution)/shard_map/ppermute | solution.py:22
  48.3 3.5 %collective-permute-start.15 = (bf16[256,128]{1,0:T(8,128)(2,1)S(1)}, bf16[256,128]{1,0:T(8,128)(2,1)S(1)}, u32[]{:S(2)}, u32[]{:S(2)}) collective-permute-start(bf16[256,128]{1,0:T(8,128)(2,1)S(1)} %get-tuple-element.96), channel_id=1, source_target_pairs={{14,2},{15,3},{30,18},{31,19}} | collective-permute-start | bytes 196616 | tf_op jit(solution)/shard_map/ppermute | solution.py:22
  50.6 7.9 %collective-permute-start.16 = (bf16[512,128]{1,0:T(8,128)(2,1)S(1)}, bf16[512,128]{1,0:T(8,128)(2,1)S(1)}, u32[]{:S(2)}, u32[]{:S(2)}) collective-permute-start(bf16[512,128]{1,0:T(8,128)(2,1)S(1)} %get-tuple-element.94), channel_id=1, source_target_pairs={{2,0},{3,1},{18,16},{19,17}} | collective-permute-start | bytes 393224 | tf_op jit(solution)/shard_map/ppermute | solution.py:22
  58.5 0.7 %copy-start = (f32[512,128]{1,0:T(8,128)}, f32[512,128]{1,0:T(8,128)S(1)}, u32[]{:S(2)}) copy-start(f32[512,128]{1,0:T(8,128)S(1)} %get-tuple-element.100) | copy-start | bytes 786436
  58.5 0.8 %copy-start.1 = (f32[512,128]{1,0:T(8,128)}, f32[512,128]{1,0:T(8,128)S(1)}, u32[]{:S(2)}) copy-start(f32[512,128]{1,0:T(8,128)S(1)} %get-tuple-element.101) | copy-start | bytes 786436

commit v14 on v13

--- a/solution.py
+++ b/solution.py
@@ -466,14 +466,16 @@
         finished = finish(total)
         near, first, last = units(permuted(behind[0], neighbours), 0, unit, 3)
         none = jnp.zeros_like(first)
-        parts = [permuted(total, [(j, 0), (j + 1, 1)]) for j in range(2, size, 2)]
+        parts = [permuted(total, [(j, 0), (j + 1, 1)]) for j in (2, 4)]
+        keys_last, values_last = permuted(total, [(6, 0)]), permuted(total, [(7, 0)])
         two = permuted(added(two, near).astype(BF16), back(shift_route(2, size)[1:]))
         four = after(added(four, jnp.where(even, last, first)).astype(BF16), finished[1])
         four = permuted(four, far_route)
         six = permuted(added(six, jnp.where(even, none, last)).astype(BF16), [(7, 1)])
         total = added(total, *parts).astype(BF16)
         mine = added(jnp.where(even, first, none), two, four, six)
-        return finished, total, permuted(total, [(1, 0)]).astype(F32), mine
+        values_next = permuted(total, [(1, 0)])
+        return finished, added(total, keys_last), added(values_next, values_last), mine
     strides = [2**i for i in range(2, size.bit_length()) if 2**i < size]
     top = strides[-1]
     zero, *third = units(permuted(behind[0], back(shift_route(1, size))), 0, unit, 4)

time: 59.7 us -> 60.3 us (1.010)
  starting transfers between devices: 26.9 us -> 28.2 us
  waiting for transfers between devices: 18.4 us -> 17.6 us
    ppermute x17 -> x18, starting transfers between devices: 26.9 us -> 28.2 us  [permuted(): return lax.ppermute(block, 'node', route)]
    ppermute x17 -> x18, waiting for transfers between devices: 18.4 us -> 17.6 us  [permuted(): return lax.ppermute(block, 'node', route)]
  transfers between devices with their start and end apart: 17 -> 18, of which waited for: 8 -> 8; matrix products, arithmetic and copies ran while one was open for 1% -> 1% of each run, Pallas kernels for 13% -> 13%
where the time goes in v14:
time: 60.3 us; the launch traced here: 59.9 us
  starting transfers between devices  28.2 us (47%)
  waiting for transfers between devices  17.6 us (29%)
  Pallas kernels  11.8 us (20%)
  between operations  0.96 us (2%)
  local copies, waits for them, and re-layouts  0.78 us (1%)
    ppermute x18, starting transfers between devices, permuted(): return lax.ppermute(block, 'node', route)  28.2 us
    ppermute x18, waiting for transfers between devices, permuted(): return lax.ppermute(block, 'node', route)  17.6 us
    pallas_call x6, Pallas kernels, call(): pl.pallas_call(kernel, in_specs=[place] * len(operands), out_specs=[VMEM]...  11.8 us
  transfers between devices with their start and end apart: 18, of which 8 were waited for; matrix products, arithmetic and copies ran while one was open for 1% of the time, Pallas kernels for 13%

profile of v14, /device:TPU:0, one launch (start us, length us, event | category | flops | bytes accessed | tf_op | source)
XLA Modules:
  0.0 59.9 jit_solution(17302851468502170396)
XLA Ops:
  0.6 5.9 %collective-permute-start = (bf16[512,128]{1,0:T(8,128)(2,1)}, bf16[512,128]{1,0:T(8,128)(2,1)S(1)}, u32[]{:S(2)}, u32[]{:S(2)}) collective-permute-start(bf16[512,128]{1,0:T(8,128)(2,1)} %bitcast.6), channel_id=1, source_target_pairs={{0,8},{1,9},{16,24},{17,25}} | collective-permute-start | bytes 393224 | tf_op jit(solution)/shard_map/ppermute | solution.py:22
  6.6 1.3 %collective-permute-start.2 = (bf16[512,128]{1,0:T(8,128)(2,1)}, bf16[512,128]{1,0:T(8,128)(2,1)S(1)}, u32[]{:S(2)}, u32[]{:S(2)}) collective-permute-start(bf16[512,128]{1,0:T(8,128)(2,1)} %bitcast.8), channel_id=1, source_target_pairs={{0,2},{1,3},{16,18},{17,19}} | collective-permute-start | bytes 393224 | tf_op jit(solution)/shard_map/ppermute | solution.py:22
  7.9 1.3 %collective-permute-start.1 = (bf16[512,128]{1,0:T(8,128)(2,1)}, bf16[512,128]{1,0:T(8,128)(2,1)S(1)}, u32[]{:S(2)}, u32[]{:S(2)}) collective-permute-start(bf16[512,128]{1,0:T(8,128)(2,1)} %bitcast.9), channel_id=1, source_target_pairs={{0,10},{1,11},{16,26},{17,27}} | collective-permute-start | bytes 393224 | tf_op jit(solution)/shard_map/ppermute | solution.py:22
  9.2 1.2 %load.1 = (bf16[256,128]{1,0:T(8,128)(2,1)S(1)}, bf16[512,128]{1,0:T(8,128)(2,1)S(1)}, bf16[4,128,128]{2,1,0:T(8,128)(2,1)S(1)}, bf16[4,128,128]{2,1,0:T(8,128)(...) custom-call(s32[64]{0:T(128)} %refs_0_.1, s32[64]{0:T(128)} %refs_1_.1, bf16[512,128]{1,0:T(8,128)(2,1)} %bitcast.7, ...), custom_call_target="tpu_custom_call" | custom-call | flops 1048576 | bytes 983552 | tf_op jit(solution)/shard_map/load/pallas_call | solution.py:261
  10.4 0.0 collective-permute-done
  10.4 0.7 %collective-permute-start.4 = (bf16[256,128]{1,0:T(8,128)(2,1)S(1)}, bf16[256,128]{1,0:T(8,128)(2,1)S(1)}, u32[]{:S(2)}, u32[]{:S(2)}) collective-permute-start(bf16[256,128]{1,0:T(8,128)(2,1)S(1)} %get-tuple-element.68), channel_id=1, source_target_pairs={{2,14},{3,15},{18,30},{19,31}} | collective-permute-start | bytes 196616 | tf_op jit(solution)/shard_map/ppermute | solution.py:22
  11.1 0.7 %collective-permute-start.3 = (bf16[256,128]{1,0:T(8,128)(2,1)S(1)}, bf16[256,128]{1,0:T(8,128)(2,1)S(1)}, u32[]{:S(2)}, u32[]{:S(2)}) collective-permute-start(bf16[256,128]{1,0:T(8,128)(2,1)S(1)} %get-tuple-element.68), channel_id=1, source_target_pairs={{2,10},{4,12},{6,14},{3,11},{5,13},{7,15},{18,26},{20,28},{22,30},... | collective-permute-start | bytes 196616 | tf_op jit(solution)/shard_map/ppermute | solution.py:22
  11.8 0.0 collective-permute-done.2
  11.8 0.7 %collective-permute-done.1 = bf16[512,128]{1,0:T(8,128)(2,1)S(1)} collective-permute-done((bf16[512,128]{1,0:T(8,128)(2,1)}, bf16[512,128]{1,0:T(8,128)(2,1)S(1)}, u32[]{:S(2)}, u32[]{:S(2)}) %collective-permute-start.1) | collective-permute-done | bytes 131104 | tf_op jit(solution)/shard_map/ppermute | solution.py:22
  12.5 0.1 add_convert_fusion.2
  12.5 1.6 %pack.1 = (bf16[4,1024,128]{2,1,0:T(8,128)(2,1)S(1)}, bf16[4,1024,128]{2,1,0:T(8,128)(2,1)S(1)}) custom-call(bf16[128,32,128]{2,1,0:T(8,128)(2,1)} %q_ref, bf16[128,32,128]{2,1,0:T(8,128)(2,1)} %g_ref.1), custom_call_target="tpu_custom_call" | custom-call | flops 1048576 | bytes 4194304 | tf_op jit(solution)/shard_map/pack/pallas_call | solution.py:261
  14.2 0.0 collective-permute-done.4.refs_8_
  14.2 0.0 collective-permute-done.3.refs_7_
  14.2 2.9 %collective-permute-start.5 = (bf16[768,128]{1,0:T(8,128)(2,1)S(1)}, bf16[768,128]{1,0:T(8,128)(2,1)S(1)}, u32[]{:S(2)}, u32[]{:S(2)}) collective-permute-start(bf16[768,128]{1,0:T(8,128)(2,1)S(1)} %pad_maximum_fusion), channel_id=1, source_target_pairs={{0,4},{2,6},{4,8},{6,10},{8,12},{10,14},{1,5},{3,7},{5,9},{7,11},{... | collective-permute-start | bytes 589832 | tf_op jit(solution)/shard_map/ppermute | solution.py:22
  17.2 2.8 %collective-permute-start.6 = (bf16[512,128]{1,0:T(8,128)(2,1)S(1)}, bf16[512,128]{1,0:T(8,128)(2,1)S(1)}, u32[]{:S(2)}, u32[]{:S(2)}) collective-permute-start(bf16[512,128]{1,0:T(8,128)(2,1)S(1)} %maximum_select_fusion), channel_id=1, source_target_pairs={{0,2},{2,0},{4,6},{6,4},{8,10},{10,8},{12,14},{14,12},{1,3},{3,1},... | collective-permute-start | bytes 393224 | tf_op jit(solution)/shard_map/ppermute | solution.py:22
  20.0 1.4 %collective-permute-done.5.refs_5_ = bf16[768,128]{1,0:T(8,128)(2,1)S(1)} collective-permute-done((bf16[768,128]{1,0:T(8,128)(2,1)S(1)}, bf16[768,128]{1,0:T(8,128)(2,1)S(1)}, u32[]{:S(2)}, u32[]{:S(2)}) %collective-permute-start.5) | collective-permute-done | bytes 196640 | tf_op jit(solution)/shard_map/ppermute | solution.py:22
  21.5 1.4 %collective-permute-done.6.refs_6_ = bf16[512,128]{1,0:T(8,128)(2,1)S(1)} collective-permute-done((bf16[512,128]{1,0:T(8,128)(2,1)S(1)}, bf16[512,128]{1,0:T(8,128)(2,1)S(1)}, u32[]{:S(2)}, u32[]{:S(2)}) %collective-permute-start.6) | collective-permute-done | bytes 131104 | tf_op jit(solution)/shard_map/ppermute | solution.py:22
  23.0 2.0 %collective-permute-start.7 = (bf16[768,128]{1,0:T(8,128)(2,1)S(1)}, bf16[768,128]{1,0:T(8,128)(2,1)S(1)}, u32[]{:S(2)}, u32[]{:S(2)}) collective-permute-start(bf16[768,128]{1,0:T(8,128)(2,1)S(1)} %pad_maximum_fusion.1), channel_id=1, source_target_pairs={{0,2},{2,0},{4,6},{6,4},{8,10},{10,8},{12,14},{14,12},{1,3},{3,1},... | collective-permute-start | bytes 589832 | tf_op jit(solution)/shard_map/ppermute | solution.py:22
  25.0 1.6 %early.1 = (bf16[4,288,128]{2,1,0:T(8,128)(2,1)S(1)}, f32[4,288,1024]{2,1,0:T(8,128)S(1)}, f32[4,288,1024]{2,1,0:T(8,128)S(1)}, f32[4,8,1024]{2,1,0:T(8,128)S(1)}) custom-call(bf16[4,128,128]{2,1,0:T(8,128)(2,1)S(1)} %get-tuple-element.73.refs_0_, bf16[4,128,128]{2,1,0:T(8,128)(2,1)S(1)} %get-tuple-element.74.refs_1_, ...), custom_call_target="tpu_custom_call" | custom-call | flops 603979776 | bytes 12910592 | tf_op jit(solution)/shard_map/early/pallas_call | solution.py:261
  26.6 2.0 %collective-permute-done.7.refs_9_ = bf16[768,128]{1,0:T(8,128)(2,1)S(1)} collective-permute-done((bf16[768,128]{1,0:T(8,128)(2,1)S(1)}, bf16[768,128]{1,0:T(8,128)(2,1)S(1)}, u32[]{:S(2)}, u32[]{:S(2)}) %collective-permute-start.7) | collective-permute-done | bytes 196640 | tf_op jit(solution)/shard_map/ppermute | solution.py:22
  28.7 4.0 %probs.1 = (bf16[512,128]{1,0:T(8,128)(2,1)S(1)}, bf16[512,128]{1,0:T(8,128)(2,1)S(1)}, bf16[4,160,128]{2,1,0:T(8,128)(2,1)S(1)}, bf16[4,448,1024]{2,1,0:T(8,128...) custom-call(bf16[512,128]{1,0:T(8,128)(2,1)S(1)} %get-tuple-element.99.refs_0_, ...), custom_call_target="tpu_custom_call" | custom-call | flops 1174405120 | bytes 19103744 | tf_op jit(solution)/shard_map/probs/pallas_call | solution.py:261
  32.6 2.1 %collective-permute-start.8 = (bf16[512,128]{1,0:T(8,128)(2,1)S(1)}, bf16[512,128]{1,0:T(8,128)(2,1)S(1)}, u32[]{:S(2)}, u32[]{:S(2)}) collective-permute-start(bf16[512,128]{1,0:T(8,128)(2,1)S(1)} %get-tuple-element.83), channel_id=1, source_target_pairs={{0,2},{2,0},{4,6},{6,4},{8,10},{10,8},{12,14},{14,12},{1,3},{3,1},... | collective-permute-start | bytes 393224 | tf_op jit(solution)/shard_map/ppermute | solution.py:22
  34.7 1.0 %windows.1 = (bf16[768,128]{1,0:T(8,128)(2,1)S(1)}, bf16[768,128]{1,0:T(8,128)(2,1)S(1)}) custom-call(bf16[4,1024,128]{2,1,0:T(8,128)(2,1)S(1)} %get-tuple-element.63.refs_2_.refs_0_.qh, bf16[4,1024,128]{2,1,0:T(8,128)(2,1)S(1)} %get-tuple-element.64.refs_3_.refs_1_.gh, bf16[4,448,1024]{2,1,0:T(8,128)(2,1)S(1)} %get-tuple-element.80.refs_4_.ds_ref, ...), custom_call_target="tpu_custom_call" | custom-call | flops 402653184 | bytes 7733248 | tf_op jit(solution)/shard_map/windows/pallas_call | solution.py:261
  35.7 0.1 collective-permute-start.12
  35.8 2.7 %collective-permute-done.8 = bf16[512,128]{1,0:T(8,128)(2,1)S(1)} collective-permute-done((bf16[512,128]{1,0:T(8,128)(2,1)S(1)}, bf16[512,128]{1,0:T(8,128)(2,1)S(1)}, u32[]{:S(2)}, u32[]{:S(2)}) %collective-permute-start.8) | collective-permute-done | bytes 131104 | tf_op jit(solution)/shard_map/ppermute | solution.py:22
  38.6 1.3 %collective-permute-start.17 = (bf16[512,128]{1,0:T(8,128)(2,1)S(1)}, bf16[512,128]{1,0:T(8,128)(2,1)S(1)}, u32[]{:S(2)}, u32[]{:S(2)}) collective-permute-start(bf16[512,128]{1,0:T(8,128)(2,1)S(1)} %add_convert_fusion.1), channel_id=1, source_target_pairs={{14,0},{15,1},{30,16},{31,17}} | collective-permute-start | bytes 393224 | tf_op jit(solution)/shard_map/ppermute | solution.py:22
  39.9 1.3 %collective-permute-start.11 = (bf16[512,128]{1,0:T(8,128)(2,1)S(1)}, bf16[512,128]{1,0:T(8,128)(2,1)S(1)}, u32[]{:S(2)}, u32[]{:S(2)}) collective-permute-start(bf16[512,128]{1,0:T(8,128)(2,1)S(1)} %add_convert_fusion.1), channel_id=1, source_target_pairs={{12,0},{13,1},{28,16},{29,17}} | collective-permute-start | bytes 393224 | tf_op jit(solution)/shard_map/ppermute | solution.py:22
  41.2 1.3 %collective-permute-start.10 = (bf16[512,128]{1,0:T(8,128)(2,1)S(1)}, bf16[512,128]{1,0:T(8,128)(2,1)S(1)}, u32[]{:S(2)}, u32[]{:S(2)}) collective-permute-start(bf16[512,128]{1,0:T(8,128)(2,1)S(1)} %add_convert_fusion.1), channel_id=1, source_target_pairs={{8,0},{10,2},{9,1},{11,3},{24,16},{26,18},{25,17},{27,19}} | collective-permute-start | bytes 393224 | tf_op jit(solution)/shard_map/ppermute | solution.py:22
  42.5 1.3 %collective-permute-start.9 = (bf16[512,128]{1,0:T(8,128)(2,1)S(1)}, bf16[512,128]{1,0:T(8,128)(2,1)S(1)}, u32[]{:S(2)}, u32[]{:S(2)}) collective-permute-start(bf16[512,128]{1,0:T(8,128)(2,1)S(1)} %add_convert_fusion.1), channel_id=1, source_target_pairs={{4,0},{6,2},{5,1},{7,3},{20,16},{22,18},{21,17},{23,19}} | collective-permute-start | bytes 393224 | tf_op jit(solution)/shard_map/ppermute | solution.py:22
  43.8 2.4 %grads.1 = (bf16[128,32,128]{2,1,0:T(8,128)(2,1)}, f32[512,128]{1,0:T(8,128)S(1)}, f32[512,128]{1,0:T(8,128)S(1)}) custom-call(bf16[4,1024,128]{2,1,0:T(8,128)(2,1)S(1)} %get-tuple-element.63.refs_2_.refs_0_.qh, bf16[4,1024,128]{2,1,0:T(8,128)(2,1)S(1)} %get-tuple-element.64.refs_3_.refs_1_.gh, bf16[4,160,128]{2,1,0:T(8,128)(2,1)S(1)} %get-tuple-element.78.refs_2_, ...), custom_call_target="tpu_custom_call" | custom-call | flops 469762048 | bytes 8847360 | tf_op jit(solution)/shard_map/grads/pallas_call | solution.py:261
  46.2 0.0 collective-permute-done.12
  46.2 0.1 add_convert_fusion.5
  46.2 0.7 %collective-permute-start.14 = (bf16[256,128]{1,0:T(8,128)(2,1)S(1)}, bf16[256,128]{1,0:T(8,128)(2,1)S(1)}, u32[]{:S(2)}, u32[]{:S(2)}) collective-permute-start(bf16[256,128]{1,0:T(8,128)(2,1)S(1)} %get-tuple-element.91), channel_id=1, source_target_pairs={{10,2},{12,4},{14,6},{11,3},{13,5},{15,7},{26,18},{28,20},{30,22},... | collective-permute-start | bytes 196616 | tf_op jit(solution)/shard_map/ppermute | solution.py:22
  46.9 1.8 %collective-permute-done.11 = bf16[512,128]{1,0:T(8,128)(2,1)S(1)} collective-permute-done((bf16[512,128]{1,0:T(8,128)(2,1)S(1)}, bf16[512,128]{1,0:T(8,128)(2,1)S(1)}, u32[]{:S(2)}, u32[]{:S(2)}) %collective-permute-start.11) | collective-permute-done | bytes 131104 | tf_op jit(solution)/shard_map/ppermute | solution.py:22
  48.7 0.7 %collective-permute-start.13 = (bf16[256,128]{1,0:T(8,128)(2,1)S(1)}, bf16[256,128]{1,0:T(8,128)(2,1)S(1)}, u32[]{:S(2)}, u32[]{:S(2)}) collective-permute-start(bf16[256,128]{1,0:T(8,128)(2,1)S(1)} %get-tuple-element.95), channel_id=1, source_target_pairs={{6,2},{8,4},{10,6},{12,8},{14,10},{7,3},{9,5},{11,7},{13,9},{15,11... | collective-permute-start | bytes 196616 | tf_op jit(solution)/shard_map/ppermute | solution.py:22
  49.4 2.0 %collective-permute-done.10 = bf16[512,128]{1,0:T(8,128)(2,1)S(1)} collective-permute-done((bf16[512,128]{1,0:T(8,128)(2,1)S(1)}, bf16[512,128]{1,0:T(8,128)(2,1)S(1)}, u32[]{:S(2)}, u32[]{:S(2)}) %collective-permute-start.10) | collective-permute-done | bytes 131104 | tf_op jit(solution)/shard_map/ppermute | solution.py:22
  51.4 0.7 %collective-permute-start.15 = (bf16[256,128]{1,0:T(8,128)(2,1)S(1)}, bf16[256,128]{1,0:T(8,128)(2,1)S(1)}, u32[]{:S(2)}, u32[]{:S(2)}) collective-permute-start(bf16[256,128]{1,0:T(8,128)(2,1)S(1)} %get-tuple-element.96), channel_id=1, source_target_pairs={{14,2},{15,3},{30,18},{31,19}} | collective-permute-start | bytes 196616 | tf_op jit(solution)/shard_map/ppermute | solution.py:22
  52.0 0.0 collective-permute-done.9
  52.0 0.1 select_add_fusion.1
  52.1 1.3 %collective-permute-start.16 = (bf16[512,128]{1,0:T(8,128)(2,1)S(1)}, bf16[512,128]{1,0:T(8,128)(2,1)S(1)}, u32[]{:S(2)}, u32[]{:S(2)}) collective-permute-start(bf16[512,128]{1,0:T(8,128)(2,1)S(1)} %get-tuple-element.94), channel_id=1, source_target_pairs={{2,0},{3,1},{18,16},{19,17}} | collective-permute-start | bytes 393224 | tf_op jit(solution)/shard_map/ppermute | solution.py:22
  53.4 0.0 collective-permute-done.14
  53.4 0.0 collective-permute-done.13
  53.5 0.0 collective-permute-done.17
  53.5 5.5 %collective-permute-done.16 = bf16[512,128]{1,0:T(8,128)(2,1)S(1)} collective-permute-done((bf16[512,128]{1,0:T(8,128)(2,1)S(1)}, bf16[512,128]{1,0:T(8,128)(2,1)S(1)}, u32[]{:S(2)}, u32[]{:S(2)}) %collective-permute-start.16) | collective-permute-done | bytes 131104 | tf_op jit(solution)/shard_map/ppermute | solution.py:22
  59.1 0.0 copy-start
  59.1 0.0 copy-start.1
  59.1 0.7 %copy-done = f32[512,128]{1,0:T(8,128)} copy-done((f32[512,128]{1,0:T(8,128)}, f32[512,128]{1,0:T(8,128)S(1)}, u32[]{:S(2)}) %copy-start) | copy-done | bytes 262168
  59.8 0.1 copy-done.1
  (11 shorter events, 0.3 us)
Async XLA Ops:
  0.6 9.8 %collective-permute-start = (bf16[512,128]{1,0:T(8,128)(2,1)}, bf16[512,128]{1,0:T(8,128)(2,1)S(1)}, u32[]{:S(2)}, u32[]{:S(2)}) collective-permute-start(bf16[512,128]{1,0:T(8,128)(2,1)} %bitcast.6), channel_id=1, source_target_pairs={{0,8},{1,9},{16,24},{17,25}} | collective-permute-start | bytes 393224 | tf_op jit(solution)/shard_map/ppermute | solution.py:22
  6.6 5.2 %collective-permute-start.2 = (bf16[512,128]{1,0:T(8,128)(2,1)}, bf16[512,128]{1,0:T(8,128)(2,1)S(1)}, u32[]{:S(2)}, u32[]{:S(2)}) collective-permute-start(bf16[512,128]{1,0:T(8,128)(2,1)} %bitcast.8), channel_id=1, source_target_pairs={{0,2},{1,3},{16,18},{17,19}} | collective-permute-start | bytes 393224 | tf_op jit(solution)/shard_map/ppermute | solution.py:22
  7.9 4.6 %collective-permute-start.1 = (bf16[512,128]{1,0:T(8,128)(2,1)}, bf16[512,128]{1,0:T(8,128)(2,1)S(1)}, u32[]{:S(2)}, u32[]{:S(2)}) collective-permute-start(bf16[512,128]{1,0:T(8,128)(2,1)} %bitcast.9), channel_id=1, source_target_pairs={{0,10},{1,11},{16,26},{17,27}} | collective-permute-start | bytes 393224 | tf_op jit(solution)/shard_map/ppermute | solution.py:22
  10.4 3.8 %collective-permute-start.4 = (bf16[256,128]{1,0:T(8,128)(2,1)S(1)}, bf16[256,128]{1,0:T(8,128)(2,1)S(1)}, u32[]{:S(2)}, u32[]{:S(2)}) collective-permute-start(bf16[256,128]{1,0:T(8,128)(2,1)S(1)} %get-tuple-element.68), channel_id=1, source_target_pairs={{2,14},{3,15},{18,30},{19,31}} | collective-permute-start | bytes 196616 | tf_op jit(solution)/shard_map/ppermute | solution.py:22
  11.1 3.1 %collective-permute-start.3 = (bf16[256,128]{1,0:T(8,128)(2,1)S(1)}, bf16[256,128]{1,0:T(8,128)(2,1)S(1)}, u32[]{:S(2)}, u32[]{:S(2)}) collective-permute-start(bf16[256,128]{1,0:T(8,128)(2,1)S(1)} %get-tuple-element.68), channel_id=1, source_target_pairs={{2,10},{4,12},{6,14},{3,11},{5,13},{7,15},{18,26},{20,28},{22,30},... | collective-permute-start | bytes 196616 | tf_op jit(solution)/shard_map/ppermute | solution.py:22
  14.2 7.2 %collective-permute-start.5 = (bf16[768,128]{1,0:T(8,128)(2,1)S(1)}, bf16[768,128]{1,0:T(8,128)(2,1)S(1)}, u32[]{:S(2)}, u32[]{:S(2)}) collective-permute-start(bf16[768,128]{1,0:T(8,128)(2,1)S(1)} %pad_maximum_fusion), channel_id=1, source_target_pairs={{0,4},{2,6},{4,8},{6,10},{8,12},{10,14},{1,5},{3,7},{5,9},{7,11},{... | collective-permute-start | bytes 589832 | tf_op jit(solution)/shard_map/ppermute | solution.py:22
  17.2 5.8 %collective-permute-start.6 = (bf16[512,128]{1,0:T(8,128)(2,1)S(1)}, bf16[512,128]{1,0:T(8,128)(2,1)S(1)}, u32[]{:S(2)}, u32[]{:S(2)}) collective-permute-start(bf16[512,128]{1,0:T(8,128)(2,1)S(1)} %maximum_select_fusion), channel_id=1, source_target_pairs={{0,2},{2,0},{4,6},{6,4},{8,10},{10,8},{12,14},{14,12},{1,3},{3,1},... | collective-permute-start | bytes 393224 | tf_op jit(solution)/shard_map/ppermute | solution.py:22
  23.0 5.7 %collective-permute-start.7 = (bf16[768,128]{1,0:T(8,128)(2,1)S(1)}, bf16[768,128]{1,0:T(8,128)(2,1)S(1)}, u32[]{:S(2)}, u32[]{:S(2)}) collective-permute-start(bf16[768,128]{1,0:T(8,128)(2,1)S(1)} %pad_maximum_fusion.1), channel_id=1, source_target_pairs={{0,2},{2,0},{4,6},{6,4},{8,10},{10,8},{12,14},{14,12},{1,3},{3,1},... | collective-permute-start | bytes 589832 | tf_op jit(solution)/shard_map/ppermute | solution.py:22
  32.6 5.9 %collective-permute-start.8 = (bf16[512,128]{1,0:T(8,128)(2,1)S(1)}, bf16[512,128]{1,0:T(8,128)(2,1)S(1)}, u32[]{:S(2)}, u32[]{:S(2)}) collective-permute-start(bf16[512,128]{1,0:T(8,128)(2,1)S(1)} %get-tuple-element.83), channel_id=1, source_target_pairs={{0,2},{2,0},{4,6},{6,4},{8,10},{10,8},{12,14},{14,12},{1,3},{3,1},... | collective-permute-start | bytes 393224 | tf_op jit(solution)/shard_map/ppermute | solution.py:22
  35.7 10.4 %collective-permute-start.12 = (bf16[768,128]{1,0:T(8,128)(2,1)S(1)}, bf16[768,128]{1,0:T(8,128)(2,1)S(1)}, u32[]{:S(2)}, u32[]{:S(2)}) collective-permute-start(bf16[768,128]{1,0:T(8,128)(2,1)S(1)} %get-tuple-element.89), channel_id=1, source_target_pairs={{0,2},{2,0},{4,6},{6,4},{8,10},{10,8},{12,14},{14,12},{1,3},{3,1},... | collective-permute-start | bytes 589832 | tf_op jit(solution)/shard_map/ppermute | solution.py:22
  38.6 14.9 %collective-permute-start.17 = (bf16[512,128]{1,0:T(8,128)(2,1)S(1)}, bf16[512,128]{1,0:T(8,128)(2,1)S(1)}, u32[]{:S(2)}, u32[]{:S(2)}) collective-permute-start(bf16[512,128]{1,0:T(8,128)(2,1)S(1)} %add_convert_fusion.1), channel_id=1, source_target_pairs={{14,0},{15,1},{30,16},{31,17}} | collective-permute-start | bytes 393224 | tf_op jit(solution)/shard_map/ppermute | solution.py:22
  39.9 8.8 %collective-permute-start.11 = (bf16[512,128]{1,0:T(8,128)(2,1)S(1)}, bf16[512,128]{1,0:T(8,128)(2,1)S(1)}, u32[]{:S(2)}, u32[]{:S(2)}) collective-permute-start(bf16[512,128]{1,0:T(8,128)(2,1)S(1)} %add_convert_fusion.1), channel_id=1, source_target_pairs={{12,0},{13,1},{28,16},{29,17}} | collective-permute-start | bytes 393224 | tf_op jit(solution)/shard_map/ppermute | solution.py:22
  41.2 10.2 %collective-permute-start.10 = (bf16[512,128]{1,0:T(8,128)(2,1)S(1)}, bf16[512,128]{1,0:T(8,128)(2,1)S(1)}, u32[]{:S(2)}, u32[]{:S(2)}) collective-permute-start(bf16[512,128]{1,0:T(8,128)(2,1)S(1)} %add_convert_fusion.1), channel_id=1, source_target_pairs={{8,0},{10,2},{9,1},{11,3},{24,16},{26,18},{25,17},{27,19}} | collective-permute-start | bytes 393224 | tf_op jit(solution)/shard_map/ppermute | solution.py:22
  42.5 9.5 %collective-permute-start.9 = (bf16[512,128]{1,0:T(8,128)(2,1)S(1)}, bf16[512,128]{1,0:T(8,128)(2,1)S(1)}, u32[]{:S(2)}, u32[]{:S(2)}) collective-permute-start(bf16[512,128]{1,0:T(8,128)(2,1)S(1)} %add_convert_fusion.1), channel_id=1, source_target_pairs={{4,0},{6,2},{5,1},{7,3},{20,16},{22,18},{21,17},{23,19}} | collective-permute-start | bytes 393224 | tf_op jit(solution)/shard_map/ppermute | solution.py:22
  46.2 7.2 %collective-permute-start.14 = (bf16[256,128]{1,0:T(8,128)(2,1)S(1)}, bf16[256,128]{1,0:T(8,128)(2,1)S(1)}, u32[]{:S(2)}, u32[]{:S(2)}) collective-permute-start(bf16[256,128]{1,0:T(8,128)(2,1)S(1)} %get-tuple-element.91), channel_id=1, source_target_pairs={{10,2},{12,4},{14,6},{11,3},{13,5},{15,7},{26,18},{28,20},{30,22},... | collective-permute-start | bytes 196616 | tf_op jit(solution)/shard_map/ppermute | solution.py:22
  48.7 4.7 %collective-permute-start.13 = (bf16[256,128]{1,0:T(8,128)(2,1)S(1)}, bf16[256,128]{1,0:T(8,128)(2,1)S(1)}, u32[]{:S(2)}, u32[]{:S(2)}) collective-permute-start(bf16[256,128]{1,0:T(8,128)(2,1)S(1)} %get-tuple-element.95), channel_id=1, source_target_pairs={{6,2},{8,4},{10,6},{12,8},{14,10},{7,3},{9,5},{11,7},{13,9},{15,11... | collective-permute-start | bytes 196616 | tf_op jit(solution)/shard_map/ppermute | solution.py:22
  51.4 2.1 %collective-permute-start.15 = (bf16[256,128]{1,0:T(8,128)(2,1)S(1)}, bf16[256,128]{1,0:T(8,128)(2,1)S(1)}, u32[]{:S(2)}, u32[]{:S(2)}) collective-permute-start(bf16[256,128]{1,0:T(8,128)(2,1)S(1)} %get-tuple-element.96), channel_id=1, source_target_pairs={{14,2},{15,3},{30,18},{31,19}} | collective-permute-start | bytes 196616 | tf_op jit(solution)/shard_map/ppermute | solution.py:22
  52.1 6.9 %collective-permute-start.16 = (bf16[512,128]{1,0:T(8,128)(2,1)S(1)}, bf16[512,128]{1,0:T(8,128)(2,1)S(1)}, u32[]{:S(2)}, u32[]{:S(2)}) collective-permute-start(bf16[512,128]{1,0:T(8,128)(2,1)S(1)} %get-tuple-element.94), channel_id=1, source_target_pairs={{2,0},{3,1},{18,16},{19,17}} | collective-permute-start | bytes 393224 | tf_op jit(solution)/shard_map/ppermute | solution.py:22
  59.1 0.7 %copy-start = (f32[512,128]{1,0:T(8,128)}, f32[512,128]{1,0:T(8,128)S(1)}, u32[]{:S(2)}) copy-start(f32[512,128]{1,0:T(8,128)S(1)} %get-tuple-element.101) | copy-start | bytes 786436
  59.1 0.8 %copy-start.1 = (f32[512,128]{1,0:T(8,128)}, f32[512,128]{1,0:T(8,128)S(1)}, u32[]{:S(2)}) copy-start(f32[512,128]{1,0:T(8,128)S(1)} %get-tuple-element.100) | copy-start | bytes 786436

commit v15 on v13

--- a/solution.py
+++ b/solution.py
@@ -141,13 +141,10 @@
 
 
 def probs_kernel(sources, heads_kv, scale, *refs):
-    prompt_k, prompt_v, qh, gh, bias, weight_ref, e_ref, dp_ref, stats, block_ref = refs[:10]
-    send_ref, keep_ref, kh, ds_ref, p_behind, p_own, vh, p_ref, grads, wide = refs[10:]
+    prompt_k, prompt_v, qh, gh, bias, weight_ref, stats, block_ref = refs[:8]
+    send_ref, keep_ref, kh, ds_ref, p_behind, terms, vh, p_ref, grads, wide = refs[8:]
     tokens = TD * TILE
     front = CAP * TILE
-    fresh = tokens + len(sources) * front
-    behind = p_behind.shape[1]
-    before = tokens + behind
     columns = CHUNK * 8
     rate = scale * math.log2(math.e)
     device = lax.axis_index("node")
@@ -160,11 +157,10 @@
 
     for head in range(heads_kv):
         for c in range(tokens // CHUNK):
-            rows = before - fresh + (c + 1) * CHUNK
             span = slice(c * columns, (c + 1) * columns)
             s = outer_product(kh[head], qh[head, span])
             dp = outer_product(vh[head], gh[head, span])
-            s = s + jnp.concatenate([bias[:fresh]] * (columns // 128), axis=1)
+            s = s + jnp.concatenate([bias[: s.shape[0]]] * (columns // 128), axis=1)
             top_early = stats[head, 0:1, span]
             top = jnp.maximum(jnp.max(s, axis=0, keepdims=True), top_early)
             e = jnp.exp2((s - top) * rate)
@@ -174,13 +170,11 @@
             weight_early = weight * shrink
             p = e * weight
             delta = jnp.sum(p * dp, axis=0, keepdims=True) + weight_early * stats[head, 2:3, span]
-            ds_ref[head, :fresh, span] = (p * (dp - delta)).astype(BF16)
+            ds_ref[head, :, span] = (p * (dp - delta)).astype(BF16)
             p_ref[head % 2, :, span] = p[:tokens].astype(BF16)
-            p_behind[head, : fresh - tokens, span] = p[tokens:].astype(BF16)
-            p = e_ref[head, :rows, span] * weight_early
-            ds_ref[head, fresh : fresh + rows, span] = (p * (dp_ref[head, :rows, span] - delta)).astype(BF16)
-            p_behind[head, fresh - tokens :, span] = p[: before - fresh].astype(BF16)
-            p_own[head, : fresh + rows - before, span] = p[before - fresh :].astype(BF16)
+            p_behind[head, :, span] = p[tokens:].astype(BF16)
+            terms[head, 0:1, span] = weight_early
+            terms[head, 1:2, span] = delta
         grads[0, head] = scale * jnp.dot(ds_ref[head, :tokens], qh[head], preferred_element_type=F32)
         grads[1, head] = jnp.dot(p_ref[head % 2], gh[head], preferred_element_type=F32)
 
@@ -198,14 +192,24 @@
             send_ref[...] = dprompt
 
 
-def windows_kernel(targets, heads_kv, scale, qh, gh, ds_ref, p_behind, send_ref, keep_ref, grads, wide):
+def windows_kernel(targets, heads_kv, scale, *refs):
+    qh, gh, ds_fresh, p_behind, e_ref, dp_ref, terms, send_ref, keep_ref, ds_ref, p_own, p_ref, grads, wide = refs
     front = CAP * TILE
     tokens = TD * TILE
-    behind = p_behind.shape[1]
+    early = ds_ref.shape[1] - tokens
+    columns = CHUNK * 8
     for head in range(heads_kv):
-        ds = ds_ref[head, tokens : tokens + behind]
+        for c in range(tokens // CHUNK):
+            rows = early + (c + 1) * CHUNK
+            span = slice(c * columns, (c + 1) * columns)
+            p = e_ref[head, :rows, span] * terms[head, 0:1, span]
+            ds_ref[head, :rows, span] = (p * (dp_ref[head, :rows, span] - terms[head, 1:2, span])).astype(BF16)
+            p_ref[head % 2, :, span] = p[:early].astype(BF16)
+            p_own[head, : rows - early, span] = p[early:].astype(BF16)
+        ds = jnp.concatenate([ds_fresh[head, tokens:], ds_ref[head, :early]], axis=0)
         grads[0, head] = scale * jnp.dot(ds, qh[head], preferred_element_type=F32)
-        grads[1, head] = jnp.dot(p_behind[head], gh[head], preferred_element_type=F32)
+        p = jnp.concatenate([p_behind[head], p_ref[head % 2]], axis=0)
+        grads[1, head] = jnp.dot(p, gh[head], preferred_element_type=F32)
     for side in range(2):
         for k, (target, start) in enumerate(targets):
             span = slice(k * front, (k + 1) * front)
@@ -215,7 +219,7 @@
 
 
 def grads_kernel(heads_kv, scale, *refs):
-    qh, gh, kh_fresh, kh_early, ds_ref, p_own, dq_ref, dk_ref, dv_ref, wide = refs
+    qh, gh, kh_fresh, kh_early, ds_fresh, ds_early, p_own, dq_ref, dk_ref, dv_ref, wide = refs
     tokens = TD * TILE
     kh = [jnp.concatenate([kh_fresh[h], kh_early[h]], axis=0) for h in range(heads_kv)]
     before = kh[0].shape[0] - tokens
@@ -228,13 +232,13 @@
             span = slice(c * columns, (c + 1) * columns)
             parts = []
             for head in (2 * pair, 2 * pair + 1):
-                dq = lax.dot_general(
-                    kh[head][:rows], ds_ref[head, :rows, span], (((0,), (0,)), ((), ())), preferred_element_type=F32
-                )
+                fresh = ds_fresh.shape[1]
+                ds = jnp.concatenate([ds_fresh[head, :, span], ds_early[head, : rows - fresh, span]], axis=0)
+                dq = lax.dot_general(kh[head][:rows], ds, (((0,), (0,)), ((), ())), preferred_element_type=F32)
                 parts.append((scale * dq.T).reshape(CHUNK, 8, 128))
             dq_ref[c * CHUNK : (c + 1) * CHUNK, pair * 16 : (pair + 1) * 16] = jnp.concatenate(parts, axis=1).astype(BF16)
         for head in (2 * pair, 2 * pair + 1):
-            for source, factor, out in ((ds_ref.at[head, before:], qh, dk), (p_own.at[head], gh, dv)):
+            for source, factor, out in ((ds_early.at[head, before - fresh :], qh, dk), (p_own.at[head], gh, dv)):
                 pieces = []
                 for c in range(tokens // CHUNK):
                     start = c * columns
@@ -322,25 +326,23 @@
     )
 
 
-def probs(sources, behind, prompt_k, prompt_v, qh, gh, own, parts, block):
+def probs(sources, prompt_k, prompt_v, qh, gh, own, stats, block):
     _, own_v, bias, weight = own
     heads_kv, tokens, head_size = own_v.shape
     rows = tokens * heads_kv
-    front = CAP * TILE
-    fresh = tokens + len(sources) * front
-    before = tokens + behind * front
+    fresh = tokens + len(sources) * CAP * TILE
     array = jax.ShapeDtypeStruct
-    work = heads_kv * tokens * 8 * (before + tokens)
+    work = heads_kv * tokens * 8 * fresh
     return call(
         functools.partial(probs_kernel, sources, heads_kv, head_size**-0.5),
         "probs",
-        (prompt_k, prompt_v, qh, gh, bias, weight, *parts, block),
+        (prompt_k, prompt_v, qh, gh, bias, weight, stats, block),
         [array((rows, head_size), BF16)] * 2
         + [
             array((heads_kv, fresh, head_size), BF16),
-            array((heads_kv, before + tokens, tokens * 8), BF16),
-            array((heads_kv, behind * front, tokens * 8), BF16),
-            array((heads_kv, tokens, tokens * 8), BF16),
+            array((heads_kv, fresh, tokens * 8), BF16),
+            array((heads_kv, fresh - tokens, tokens * 8), BF16),
+            array((heads_kv, 8, tokens * 8), F32),
         ],
         [
             pltpu.VMEM((heads_kv, fresh, head_size), BF16),
@@ -348,42 +350,49 @@
             pltpu.VMEM((2, heads_kv, tokens, head_size), F32),
             pltpu.VMEM((rows, head_size), F32),
         ],
-        flops=5 * work * head_size,
+        flops=8 * work * head_size,
         transcendentals=work,
     )
 
 
-def windows(targets, qh, gh, ds, p_behind):
-    heads_kv, behind, _ = p_behind.shape
+def windows(targets, qh, gh, ds_fresh, p_behind, e, dp, terms):
+    heads_kv, early, columns = e.shape
     head_size = qh.shape[2]
+    tokens = TD * TILE
     front = CAP * TILE * heads_kv
+    behind = early - tokens + p_behind.shape[1]
     count = [sum(target == t for target, _ in targets) for t in (0, 1)]
     array = jax.ShapeDtypeStruct
     return call(
         functools.partial(windows_kernel, targets, heads_kv, head_size**-0.5),
         "windows",
-        (qh, gh, ds, p_behind),
-        [array((2 * front * n, head_size), BF16) for n in count],
-        [pltpu.VMEM((2, heads_kv, behind, head_size), F32), pltpu.VMEM((front, head_size), F32)],
-        flops=4 * p_behind.size * head_size,
-    )
-
-
-def grads(qh, gh, kh_fresh, kh_early, ds, p_own):
+        (qh, gh, ds_fresh, p_behind, e, dp, terms),
+        [array((2 * front * n, head_size), BF16) for n in count]
+        + [array((heads_kv, early, columns), BF16), array((heads_kv, tokens, columns), BF16)],
+        [
+            pltpu.VMEM((2, early - tokens, columns), BF16),
+            pltpu.VMEM((2, heads_kv, behind, head_size), F32),
+            pltpu.VMEM((front, head_size), F32),
+        ],
+        flops=4 * heads_kv * behind * columns * head_size,
+    )
+
+
+def grads(qh, gh, kh_fresh, kh_early, ds_fresh, ds_early, p_own):
     heads_kv, tokens, _ = p_own.shape
     head_size = kh_fresh.shape[2]
     array = jax.ShapeDtypeStruct
     return call(
         functools.partial(grads_kernel, heads_kv, head_size**-0.5),
         "grads",
-        (qh, gh, kh_fresh, kh_early, ds, p_own),
+        (qh, gh, kh_fresh, kh_early, ds_fresh, ds_early, p_own),
         [
             array((tokens, heads_kv * 8, head_size), BF16),
             array((tokens * heads_kv, head_size), F32),
             array((tokens * heads_kv, head_size), F32),
         ],
         [pltpu.VMEM((tokens * heads_kv, head_size), F32)],
-        flops=2 * heads_kv * tokens * 8 * ds.shape[1] * head_size,
+        flops=2 * tokens * 8 * (ds_fresh.size + ds_early.size) // (tokens * 8) * head_size,
     )
 
 
@@ -513,15 +522,13 @@
     held, other, block, fresh_sources, early_sources, blocks, (qh, gh) = collect(
         size, unit, rows, where, keys, values, head, held, queries, grad_out
     )
-    kh_early, *parts = early(len(fresh_sources), early_sources, qh, gh, own, blocks)
+    kh_early, e, dp, stats = early(len(fresh_sources), early_sources, qh, gh, own, blocks)
     prompt_k, prompt_v = jnp.where(even, held, other), jnp.where(even, other, held)
-    *prompt, kh, ds, p_behind, p_own = probs(
-        fresh_sources, len(targets), prompt_k, prompt_v, qh, gh, own, parts, block
-    )
-    behind = windows(targets, qh, gh, ds, p_behind)
+    *prompt, kh, ds, p_behind, terms = probs(fresh_sources, prompt_k, prompt_v, qh, gh, own, stats, block)
+    *behind, ds_early, p_own = windows(targets, qh, gh, ds, p_behind, e, dp, terms)
 
     def finish(earlier):
-        return grads(qh, gh, kh, kh_early, ds, after(p_own, earlier))
+        return grads(qh, gh, kh, kh_early, ds, ds_early, after(p_own, earlier))
 
     (grad_queries, dk, dv), prompt_k, prompt_v, mine = give_back(size, unit, where, prompt, behind, finish)
     own = []

time: 59.7 us -> 58.4 us (0.978)
  Pallas kernels: 11.8 us -> 10.8 us
    pallas_call x6, Pallas kernels: 11.8 us -> 10.8 us  [call(): pl.pallas_call(kernel, in_specs=[place] * len(operands), out_specs=[VMEM]...]
  transfers between devices with their start and end apart: 17 -> 17, of which waited for: 8 -> 8; matrix products, arithmetic and copies ran while one was open for 1% -> 1% of each run, Pallas kernels for 13% -> 14%
where the time goes in v15:
time: 58.4 us; the launch traced here: 58.1 us
  starting transfers between devices  26.9 us (46%)
  waiting for transfers between devices  18.2 us (31%)
  Pallas kernels  10.8 us (18%)
  between operations  0.93 us (2%)
  local copies, waits for them, and re-layouts  0.78 us (1%)
    ppermute x17, starting transfers between devices, permuted(): return lax.ppermute(block, 'node', route)  26.9 us
    ppermute x17, waiting for transfers between devices, permuted(): return lax.ppermute(block, 'node', route)  18.2 us
    pallas_call x6, Pallas kernels, call(): pl.pallas_call(kernel, in_specs=[place] * len(operands), out_specs=[VMEM]...  10.8 us
  transfers between devices with their start and end apart: 17, of which 8 were waited for; matrix products, arithmetic and copies ran while one was open for 1% of the time, Pallas kernels for 14%

profile of v15, /device:TPU:0, one launch (start us, length us, event | category | flops | bytes accessed | tf_op | source)
XLA Modules:
  0.0 58.1 jit_solution(6501219459287080665)
XLA Ops:
  0.6 5.9 %collective-permute-start = (bf16[512,128]{1,0:T(8,128)(2,1)}, bf16[512,128]{1,0:T(8,128)(2,1)S(1)}, u32[]{:S(2)}, u32[]{:S(2)}) collective-permute-start(bf16[512,128]{1,0:T(8,128)(2,1)} %bitcast.6), channel_id=1, source_target_pairs={{0,8},{1,9},{16,24},{17,25}} | collective-permute-start | bytes 393224 | tf_op jit(solution)/shard_map/ppermute | solution.py:22
  6.6 1.3 %collective-permute-start.2 = (bf16[512,128]{1,0:T(8,128)(2,1)}, bf16[512,128]{1,0:T(8,128)(2,1)S(1)}, u32[]{:S(2)}, u32[]{:S(2)}) collective-permute-start(bf16[512,128]{1,0:T(8,128)(2,1)} %bitcast.8), channel_id=1, source_target_pairs={{0,2},{1,3},{16,18},{17,19}} | collective-permute-start | bytes 393224 | tf_op jit(solution)/shard_map/ppermute | solution.py:22
  7.9 1.3 %collective-permute-start.1 = (bf16[512,128]{1,0:T(8,128)(2,1)}, bf16[512,128]{1,0:T(8,128)(2,1)S(1)}, u32[]{:S(2)}, u32[]{:S(2)}) collective-permute-start(bf16[512,128]{1,0:T(8,128)(2,1)} %bitcast.9), channel_id=1, source_target_pairs={{0,10},{1,11},{16,26},{17,27}} | collective-permute-start | bytes 393224 | tf_op jit(solution)/shard_map/ppermute | solution.py:22
  9.2 1.2 %load.1 = (bf16[256,128]{1,0:T(8,128)(2,1)S(1)}, bf16[512,128]{1,0:T(8,128)(2,1)S(1)}, bf16[4,128,128]{2,1,0:T(8,128)(2,1)S(1)}, bf16[4,128,128]{2,1,0:T(8,128)(...) custom-call(s32[64]{0:T(128)} %refs_0_.1, s32[64]{0:T(128)} %refs_1_.1, bf16[512,128]{1,0:T(8,128)(2,1)} %bitcast.7, ...), custom_call_target="tpu_custom_call" | custom-call | flops 1048576 | bytes 983552 | tf_op jit(solution)/shard_map/load/pallas_call | solution.py:265
  10.4 0.0 collective-permute-done
  10.4 0.7 %collective-permute-start.4 = (bf16[256,128]{1,0:T(8,128)(2,1)S(1)}, bf16[256,128]{1,0:T(8,128)(2,1)S(1)}, u32[]{:S(2)}, u32[]{:S(2)}) collective-permute-start(bf16[256,128]{1,0:T(8,128)(2,1)S(1)} %get-tuple-element.70), channel_id=1, source_target_pairs={{2,14},{3,15},{18,30},{19,31}} | collective-permute-start | bytes 196616 | tf_op jit(solution)/shard_map/ppermute | solution.py:22
  11.1 0.7 %collective-permute-start.3 = (bf16[256,128]{1,0:T(8,128)(2,1)S(1)}, bf16[256,128]{1,0:T(8,128)(2,1)S(1)}, u32[]{:S(2)}, u32[]{:S(2)}) collective-permute-start(bf16[256,128]{1,0:T(8,128)(2,1)S(1)} %get-tuple-element.70), channel_id=1, source_target_pairs={{2,10},{4,12},{6,14},{3,11},{5,13},{7,15},{18,26},{20,28},{22,30},... | collective-permute-start | bytes 196616 | tf_op jit(solution)/shard_map/ppermute | solution.py:22
  11.8 0.0 collective-permute-done.2
  11.8 0.7 %collective-permute-done.1 = bf16[512,128]{1,0:T(8,128)(2,1)S(1)} collective-permute-done((bf16[512,128]{1,0:T(8,128)(2,1)}, bf16[512,128]{1,0:T(8,128)(2,1)S(1)}, u32[]{:S(2)}, u32[]{:S(2)}) %collective-permute-start.1) | collective-permute-done | bytes 131104 | tf_op jit(solution)/shard_map/ppermute | solution.py:22
  12.5 0.1 add_convert_fusion.2
  12.5 1.6 %pack.1 = (bf16[4,1024,128]{2,1,0:T(8,128)(2,1)S(1)}, bf16[4,1024,128]{2,1,0:T(8,128)(2,1)S(1)}) custom-call(bf16[128,32,128]{2,1,0:T(8,128)(2,1)} %q_ref, bf16[128,32,128]{2,1,0:T(8,128)(2,1)} %g_ref.1), custom_call_target="tpu_custom_call" | custom-call | flops 1048576 | bytes 4194304 | tf_op jit(solution)/shard_map/pack/pallas_call | solution.py:265
  14.2 0.0 collective-permute-done.4.refs_8_
  14.2 0.0 collective-permute-done.3.refs_7_
  14.2 2.9 %collective-permute-start.5 = (bf16[768,128]{1,0:T(8,128)(2,1)S(1)}, bf16[768,128]{1,0:T(8,128)(2,1)S(1)}, u32[]{:S(2)}, u32[]{:S(2)}) collective-permute-start(bf16[768,128]{1,0:T(8,128)(2,1)S(1)} %pad_maximum_fusion), channel_id=1, source_target_pairs={{0,4},{2,6},{4,8},{6,10},{8,12},{10,14},{1,5},{3,7},{5,9},{7,11},{... | collective-permute-start | bytes 589832 | tf_op jit(solution)/shard_map/ppermute | solution.py:22
  17.2 2.8 %collective-permute-start.6 = (bf16[512,128]{1,0:T(8,128)(2,1)S(1)}, bf16[512,128]{1,0:T(8,128)(2,1)S(1)}, u32[]{:S(2)}, u32[]{:S(2)}) collective-permute-start(bf16[512,128]{1,0:T(8,128)(2,1)S(1)} %maximum_select_fusion), channel_id=1, source_target_pairs={{0,2},{2,0},{4,6},{6,4},{8,10},{10,8},{12,14},{14,12},{1,3},{3,1},... | collective-permute-start | bytes 393224 | tf_op jit(solution)/shard_map/ppermute | solution.py:22
  20.0 1.4 %collective-permute-done.5.refs_5_ = bf16[768,128]{1,0:T(8,128)(2,1)S(1)} collective-permute-done((bf16[768,128]{1,0:T(8,128)(2,1)S(1)}, bf16[768,128]{1,0:T(8,128)(2,1)S(1)}, u32[]{:S(2)}, u32[]{:S(2)}) %collective-permute-start.5) | collective-permute-done | bytes 196640 | tf_op jit(solution)/shard_map/ppermute | solution.py:22
  21.5 1.4 %collective-permute-done.6.refs_6_ = bf16[512,128]{1,0:T(8,128)(2,1)S(1)} collective-permute-done((bf16[512,128]{1,0:T(8,128)(2,1)S(1)}, bf16[512,128]{1,0:T(8,128)(2,1)S(1)}, u32[]{:S(2)}, u32[]{:S(2)}) %collective-permute-start.6) | collective-permute-done | bytes 131104 | tf_op jit(solution)/shard_map/ppermute | solution.py:22
  23.0 2.0 %collective-permute-start.7 = (bf16[768,128]{1,0:T(8,128)(2,1)S(1)}, bf16[768,128]{1,0:T(8,128)(2,1)S(1)}, u32[]{:S(2)}, u32[]{:S(2)}) collective-permute-start(bf16[768,128]{1,0:T(8,128)(2,1)S(1)} %pad_maximum_fusion.1), channel_id=1, source_target_pairs={{0,2},{2,0},{4,6},{6,4},{8,10},{10,8},{12,14},{14,12},{1,3},{3,1},... | collective-permute-start | bytes 589832 | tf_op jit(solution)/shard_map/ppermute | solution.py:22
  25.0 1.6 %early.1 = (bf16[4,288,128]{2,1,0:T(8,128)(2,1)S(1)}, f32[4,288,1024]{2,1,0:T(8,128)S(1)}, f32[4,288,1024]{2,1,0:T(8,128)S(1)}, f32[4,8,1024]{2,1,0:T(8,128)S(1)}) custom-call(bf16[4,128,128]{2,1,0:T(8,128)(2,1)S(1)} %get-tuple-element.75.refs_0_, bf16[4,128,128]{2,1,0:T(8,128)(2,1)S(1)} %get-tuple-element.76.refs_1_, ...), custom_call_target="tpu_custom_call" | custom-call | flops 603979776 | bytes 12910592 | tf_op jit(solution)/shard_map/early/pallas_call | solution.py:265
  26.6 2.0 %collective-permute-done.7.refs_7_ = bf16[768,128]{1,0:T(8,128)(2,1)S(1)} collective-permute-done((bf16[768,128]{1,0:T(8,128)(2,1)S(1)}, bf16[768,128]{1,0:T(8,128)(2,1)S(1)}, u32[]{:S(2)}, u32[]{:S(2)}) %collective-permute-start.7) | collective-permute-done | bytes 196640 | tf_op jit(solution)/shard_map/ppermute | solution.py:22
  28.7 2.6 %probs.1 = (bf16[512,128]{1,0:T(8,128)(2,1)S(1)}, bf16[512,128]{1,0:T(8,128)(2,1)S(1)}, bf16[4,160,128]{2,1,0:T(8,128)(2,1)S(1)}, bf16[4,160,1024]{2,1,0:T(8,128...) custom-call(bf16[512,128]{1,0:T(8,128)(2,1)S(1)} %get-tuple-element.103.refs_0_, ...), custom_call_target="tpu_custom_call" | custom-call | flops 671088640 | bytes 5079040 | tf_op jit(solution)/shard_map/probs/pallas_call | solution.py:265
  31.2 2.1 %collective-permute-start.8 = (bf16[512,128]{1,0:T(8,128)(2,1)S(1)}, bf16[512,128]{1,0:T(8,128)(2,1)S(1)}, u32[]{:S(2)}, u32[]{:S(2)}) collective-permute-start(bf16[512,128]{1,0:T(8,128)(2,1)S(1)} %get-tuple-element.88), channel_id=1, source_target_pairs={{0,2},{2,0},{4,6},{6,4},{8,10},{10,8},{12,14},{14,12},{1,3},{3,1},... | collective-permute-start | bytes 393224 | tf_op jit(solution)/shard_map/ppermute | solution.py:22
  33.3 1.4 %windows.1 = (bf16[768,128]{1,0:T(8,128)(2,1)S(1)}, bf16[768,128]{1,0:T(8,128)(2,1)S(1)}, bf16[4,288,1024]{2,1,0:T(8,128)(2,1)S(1)}, bf16[4,128,1024]{2,1,0:T(8,128)(2,1)S(1)}) custom-call(bf16[4,1024,128]{2,1,0:T(8,128)(2,1)S(1)} %get-tuple-element.65.refs_2_.refs_0_, bf16[4,1024,128]{2,1,0:T(8,128)(2,1)S(1)} %get-tuple-element.66.refs_3_.refs_1_, ...), custom_call_target="tpu_custom_call" | custom-call | flops 402653184 | bytes 17039360 | tf_op jit(solution)/shard_map/windows/pallas_call | solution.py:265
  34.7 0.1 collective-permute-start.12
  34.8 2.8 %collective-permute-done.8 = bf16[512,128]{1,0:T(8,128)(2,1)S(1)} collective-permute-done((bf16[512,128]{1,0:T(8,128)(2,1)S(1)}, bf16[512,128]{1,0:T(8,128)(2,1)S(1)}, u32[]{:S(2)}, u32[]{:S(2)}) %collective-permute-start.8) | collective-permute-done | bytes 131104 | tf_op jit(solution)/shard_map/ppermute | solution.py:22
  37.6 1.3 %collective-permute-start.11 = (bf16[512,128]{1,0:T(8,128)(2,1)S(1)}, bf16[512,128]{1,0:T(8,128)(2,1)S(1)}, u32[]{:S(2)}, u32[]{:S(2)}) collective-permute-start(bf16[512,128]{1,0:T(8,128)(2,1)S(1)} %add_convert_fusion.1), channel_id=1, source_target_pairs={{12,0},{14,2},{13,1},{15,3},{28,16},{30,18},{29,17},{31,19}} | collective-permute-start | bytes 393224 | tf_op jit(solution)/shard_map/ppermute | solution.py:22
  38.9 1.3 %collective-permute-start.10 = (bf16[512,128]{1,0:T(8,128)(2,1)S(1)}, bf16[512,128]{1,0:T(8,128)(2,1)S(1)}, u32[]{:S(2)}, u32[]{:S(2)}) collective-permute-start(bf16[512,128]{1,0:T(8,128)(2,1)S(1)} %add_convert_fusion.1), channel_id=1, source_target_pairs={{8,0},{10,2},{9,1},{11,3},{24,16},{26,18},{25,17},{27,19}} | collective-permute-start | bytes 393224 | tf_op jit(solution)/shard_map/ppermute | solution.py:22
  40.2 1.3 %collective-permute-start.9 = (bf16[512,128]{1,0:T(8,128)(2,1)S(1)}, bf16[512,128]{1,0:T(8,128)(2,1)S(1)}, u32[]{:S(2)}, u32[]{:S(2)}) collective-permute-start(bf16[512,128]{1,0:T(8,128)(2,1)S(1)} %add_convert_fusion.1), channel_id=1, source_target_pairs={{4,0},{6,2},{5,1},{7,3},{20,16},{22,18},{21,17},{23,19}} | collective-permute-start | bytes 393224 | tf_op jit(solution)/shard_map/ppermute | solution.py:22
  41.5 2.4 %grads.1 = (bf16[128,32,128]{2,1,0:T(8,128)(2,1)}, f32[512,128]{1,0:T(8,128)S(1)}, f32[512,128]{1,0:T(8,128)S(1)}) custom-call(bf16[4,1024,128]{2,1,0:T(8,128)(2,1)S(1)} %get-tuple-element.65.refs_2_.refs_0_, bf16[4,1024,128]{2,1,0:T(8,128)(2,1)S(1)} %get-tuple-element.66.refs_3_.refs_1_, bf16[4,160,128]{2,1,0:T(8,128)(2,1)S(1)} %get-tuple-element.78.refs_2_, ...), custom_call_target="tpu_custom_call" | custom-call | flops 469762048 | bytes 8847360 | tf_op jit(solution)/shard_map/grads/pallas_call | solution.py:265
  43.9 0.0 collective-permute-done.12
  43.9 0.1 add_convert_fusion.5
  43.9 0.7 %collective-permute-start.14 = (bf16[256,128]{1,0:T(8,128)(2,1)S(1)}, bf16[256,128]{1,0:T(8,128)(2,1)S(1)}, u32[]{:S(2)}, u32[]{:S(2)}) collective-permute-start(bf16[256,128]{1,0:T(8,128)(2,1)S(1)} %get-tuple-element.95), channel_id=1, source_target_pairs={{10,2},{12,4},{14,6},{11,3},{13,5},{15,7},{26,18},{28,20},{30,22},... | collective-permute-start | bytes 196616 | tf_op jit(solution)/shard_map/ppermute | solution.py:22
  44.6 0.7 %collective-permute-start.13 = (bf16[256,128]{1,0:T(8,128)(2,1)S(1)}, bf16[256,128]{1,0:T(8,128)(2,1)S(1)}, u32[]{:S(2)}, u32[]{:S(2)}) collective-permute-start(bf16[256,128]{1,0:T(8,128)(2,1)S(1)} %get-tuple-element.99), channel_id=1, source_target_pairs={{6,2},{8,4},{10,6},{12,8},{14,10},{7,3},{9,5},{11,7},{13,9},{15,11... | collective-permute-start | bytes 196616 | tf_op jit(solution)/shard_map/ppermute | solution.py:22
  45.3 1.8 %collective-permute-done.11 = bf16[512,128]{1,0:T(8,128)(2,1)S(1)} collective-permute-done((bf16[512,128]{1,0:T(8,128)(2,1)S(1)}, bf16[512,128]{1,0:T(8,128)(2,1)S(1)}, u32[]{:S(2)}, u32[]{:S(2)}) %collective-permute-start.11) | collective-permute-done | bytes 131104 | tf_op jit(solution)/shard_map/ppermute | solution.py:22
  47.1 0.7 %collective-permute-start.15 = (bf16[256,128]{1,0:T(8,128)(2,1)S(1)}, bf16[256,128]{1,0:T(8,128)(2,1)S(1)}, u32[]{:S(2)}, u32[]{:S(2)}) collective-permute-start(bf16[256,128]{1,0:T(8,128)(2,1)S(1)} %get-tuple-element.100), channel_id=1, source_target_pairs={{14,2},{15,3},{30,18},{31,19}} | collective-permute-start | bytes 196616 | tf_op jit(solution)/shard_map/ppermute | solution.py:22
  47.7 1.5 %collective-permute-done.10 = bf16[512,128]{1,0:T(8,128)(2,1)S(1)} collective-permute-done((bf16[512,128]{1,0:T(8,128)(2,1)S(1)}, bf16[512,128]{1,0:T(8,128)(2,1)S(1)}, u32[]{:S(2)}, u32[]{:S(2)}) %collective-permute-start.10) | collective-permute-done | bytes 131104 | tf_op jit(solution)/shard_map/ppermute | solution.py:22
  49.2 0.0 collective-permute-done.9
  49.3 0.1 select_add_fusion.1
  49.3 1.3 %collective-permute-start.16 = (bf16[512,128]{1,0:T(8,128)(2,1)S(1)}, bf16[512,128]{1,0:T(8,128)(2,1)S(1)}, u32[]{:S(2)}, u32[]{:S(2)}) collective-permute-start(bf16[512,128]{1,0:T(8,128)(2,1)S(1)} %get-tuple-element.98), channel_id=1, source_target_pairs={{2,0},{3,1},{18,16},{19,17}} | collective-permute-start | bytes 393224 | tf_op jit(solution)/shard_map/ppermute | solution.py:22
  50.6 0.0 collective-permute-done.14
  50.7 0.0 collective-permute-done.13
  50.7 0.0 collective-permute-done.15
  50.7 6.5 %collective-permute-done.16 = bf16[512,128]{1,0:T(8,128)(2,1)S(1)} collective-permute-done((bf16[512,128]{1,0:T(8,128)(2,1)S(1)}, bf16[512,128]{1,0:T(8,128)(2,1)S(1)}, u32[]{:S(2)}, u32[]{:S(2)}) %collective-permute-start.16) | collective-permute-done | bytes 131104 | tf_op jit(solution)/shard_map/ppermute | solution.py:22
  57.3 0.0 copy-start
  57.3 0.0 copy-start.1
  57.3 0.7 %copy-done = f32[512,128]{1,0:T(8,128)} copy-done((f32[512,128]{1,0:T(8,128)}, f32[512,128]{1,0:T(8,128)S(1)}, u32[]{:S(2)}) %copy-start) | copy-done | bytes 262168
  58.0 0.1 copy-done.1
  (10 shorter events, 0.2 us)
Async XLA Ops:
  0.6 9.8 %collective-permute-start = (bf16[512,128]{1,0:T(8,128)(2,1)}, bf16[512,128]{1,0:T(8,128)(2,1)S(1)}, u32[]{:S(2)}, u32[]{:S(2)}) collective-permute-start(bf16[512,128]{1,0:T(8,128)(2,1)} %bitcast.6), channel_id=1, source_target_pairs={{0,8},{1,9},{16,24},{17,25}} | collective-permute-start | bytes 393224 | tf_op jit(solution)/shard_map/ppermute | solution.py:22
  6.6 5.2 %collective-permute-start.2 = (bf16[512,128]{1,0:T(8,128)(2,1)}, bf16[512,128]{1,0:T(8,128)(2,1)S(1)}, u32[]{:S(2)}, u32[]{:S(2)}) collective-permute-start(bf16[512,128]{1,0:T(8,128)(2,1)} %bitcast.8), channel_id=1, source_target_pairs={{0,2},{1,3},{16,18},{17,19}} | collective-permute-start | bytes 393224 | tf_op jit(solution)/shard_map/ppermute | solution.py:22
  7.9 4.6 %collective-permute-start.1 = (bf16[512,128]{1,0:T(8,128)(2,1)}, bf16[512,128]{1,0:T(8,128)(2,1)S(1)}, u32[]{:S(2)}, u32[]{:S(2)}) collective-permute-start(bf16[512,128]{1,0:T(8,128)(2,1)} %bitcast.9), channel_id=1, source_target_pairs={{0,10},{1,11},{16,26},{17,27}} | collective-permute-start | bytes 393224 | tf_op jit(solution)/shard_map/ppermute | solution.py:22
  10.4 3.8 %collective-permute-start.4 = (bf16[256,128]{1,0:T(8,128)(2,1)S(1)}, bf16[256,128]{1,0:T(8,128)(2,1)S(1)}, u32[]{:S(2)}, u32[]{:S(2)}) collective-permute-start(bf16[256,128]{1,0:T(8,128)(2,1)S(1)} %get-tuple-element.70), channel_id=1, source_target_pairs={{2,14},{3,15},{18,30},{19,31}} | collective-permute-start | bytes 196616 | tf_op jit(solution)/shard_map/ppermute | solution.py:22
  11.1 3.1 %collective-permute-start.3 = (bf16[256,128]{1,0:T(8,128)(2,1)S(1)}, bf16[256,128]{1,0:T(8,128)(2,1)S(1)}, u32[]{:S(2)}, u32[]{:S(2)}) collective-permute-start(bf16[256,128]{1,0:T(8,128)(2,1)S(1)} %get-tuple-element.70), channel_id=1, source_target_pairs={{2,10},{4,12},{6,14},{3,11},{5,13},{7,15},{18,26},{20,28},{22,30},... | collective-permute-start | bytes 196616 | tf_op jit(solution)/shard_map/ppermute | solution.py:22
  14.2 7.2 %collective-permute-start.5 = (bf16[768,128]{1,0:T(8,128)(2,1)S(1)}, bf16[768,128]{1,0:T(8,128)(2,1)S(1)}, u32[]{:S(2)}, u32[]{:S(2)}) collective-permute-start(bf16[768,128]{1,0:T(8,128)(2,1)S(1)} %pad_maximum_fusion), channel_id=1, source_target_pairs={{0,4},{2,6},{4,8},{6,10},{8,12},{10,14},{1,5},{3,7},{5,9},{7,11},{... | collective-permute-start | bytes 589832 | tf_op jit(solution)/shard_map/ppermute | solution.py:22
  17.2 5.8 %collective-permute-start.6 = (bf16[512,128]{1,0:T(8,128)(2,1)S(1)}, bf16[512,128]{1,0:T(8,128)(2,1)S(1)}, u32[]{:S(2)}, u32[]{:S(2)}) collective-permute-start(bf16[512,128]{1,0:T(8,128)(2,1)S(1)} %maximum_select_fusion), channel_id=1, source_target_pairs={{0,2},{2,0},{4,6},{6,4},{8,10},{10,8},{12,14},{14,12},{1,3},{3,1},... | collective-permute-start | bytes 393224 | tf_op jit(solution)/shard_map/ppermute | solution.py:22
  23.0 5.7 %collective-permute-start.7 = (bf16[768,128]{1,0:T(8,128)(2,1)S(1)}, bf16[768,128]{1,0:T(8,128)(2,1)S(1)}, u32[]{:S(2)}, u32[]{:S(2)}) collective-permute-start(bf16[768,128]{1,0:T(8,128)(2,1)S(1)} %pad_maximum_fusion.1), channel_id=1, source_target_pairs={{0,2},{2,0},{4,6},{6,4},{8,10},{10,8},{12,14},{14,12},{1,3},{3,1},... | collective-permute-start | bytes 589832 | tf_op jit(solution)/shard_map/ppermute | solution.py:22
  31.2 6.3 %collective-permute-start.8 = (bf16[512,128]{1,0:T(8,128)(2,1)S(1)}, bf16[512,128]{1,0:T(8,128)(2,1)S(1)}, u32[]{:S(2)}, u32[]{:S(2)}) collective-permute-start(bf16[512,128]{1,0:T(8,128)(2,1)S(1)} %get-tuple-element.88), channel_id=1, source_target_pairs={{0,2},{2,0},{4,6},{6,4},{8,10},{10,8},{12,14},{14,12},{1,3},{3,1},... | collective-permute-start | bytes 393224 | tf_op jit(solution)/shard_map/ppermute | solution.py:22
  34.7 9.2 %collective-permute-start.12 = (bf16[768,128]{1,0:T(8,128)(2,1)S(1)}, bf16[768,128]{1,0:T(8,128)(2,1)S(1)}, u32[]{:S(2)}, u32[]{:S(2)}) collective-permute-start(bf16[768,128]{1,0:T(8,128)(2,1)S(1)} %get-tuple-element.93), channel_id=1, source_target_pairs={{0,2},{2,0},{4,6},{6,4},{8,10},{10,8},{12,14},{14,12},{1,3},{3,1},... | collective-permute-start | bytes 589832 | tf_op jit(solution)/shard_map/ppermute | solution.py:22
  37.6 9.5 %collective-permute-start.11 = (bf16[512,128]{1,0:T(8,128)(2,1)S(1)}, bf16[512,128]{1,0:T(8,128)(2,1)S(1)}, u32[]{:S(2)}, u32[]{:S(2)}) collective-permute-start(bf16[512,128]{1,0:T(8,128)(2,1)S(1)} %add_convert_fusion.1), channel_id=1, source_target_pairs={{12,0},{14,2},{13,1},{15,3},{28,16},{30,18},{29,17},{31,19}} | collective-permute-start | bytes 393224 | tf_op jit(solution)/shard_map/ppermute | solution.py:22
  38.9 10.4 %collective-permute-start.10 = (bf16[512,128]{1,0:T(8,128)(2,1)S(1)}, bf16[512,128]{1,0:T(8,128)(2,1)S(1)}, u32[]{:S(2)}, u32[]{:S(2)}) collective-permute-start(bf16[512,128]{1,0:T(8,128)(2,1)S(1)} %add_convert_fusion.1), channel_id=1, source_target_pairs={{8,0},{10,2},{9,1},{11,3},{24,16},{26,18},{25,17},{27,19}} | collective-permute-start | bytes 393224 | tf_op jit(solution)/shard_map/ppermute | solution.py:22
  40.2 9.1 %collective-permute-start.9 = (bf16[512,128]{1,0:T(8,128)(2,1)S(1)}, bf16[512,128]{1,0:T(8,128)(2,1)S(1)}, u32[]{:S(2)}, u32[]{:S(2)}) collective-permute-start(bf16[512,128]{1,0:T(8,128)(2,1)S(1)} %add_convert_fusion.1), channel_id=1, source_target_pairs={{4,0},{6,2},{5,1},{7,3},{20,16},{22,18},{21,17},{23,19}} | collective-permute-start | bytes 393224 | tf_op jit(solution)/shard_map/ppermute | solution.py:22
  43.9 6.7 %collective-permute-start.14 = (bf16[256,128]{1,0:T(8,128)(2,1)S(1)}, bf16[256,128]{1,0:T(8,128)(2,1)S(1)}, u32[]{:S(2)}, u32[]{:S(2)}) collective-permute-start(bf16[256,128]{1,0:T(8,128)(2,1)S(1)} %get-tuple-element.95), channel_id=1, source_target_pairs={{10,2},{12,4},{14,6},{11,3},{13,5},{15,7},{26,18},{28,20},{30,22},... | collective-permute-start | bytes 196616 | tf_op jit(solution)/shard_map/ppermute | solution.py:22
  44.6 6.0 %collective-permute-start.13 = (bf16[256,128]{1,0:T(8,128)(2,1)S(1)}, bf16[256,128]{1,0:T(8,128)(2,1)S(1)}, u32[]{:S(2)}, u32[]{:S(2)}) collective-permute-start(bf16[256,128]{1,0:T(8,128)(2,1)S(1)} %get-tuple-element.99), channel_id=1, source_target_pairs={{6,2},{8,4},{10,6},{12,8},{14,10},{7,3},{9,5},{11,7},{13,9},{15,11... | collective-permute-start | bytes 196616 | tf_op jit(solution)/shard_map/ppermute | solution.py:22
  47.1 3.6 %collective-permute-start.15 = (bf16[256,128]{1,0:T(8,128)(2,1)S(1)}, bf16[256,128]{1,0:T(8,128)(2,1)S(1)}, u32[]{:S(2)}, u32[]{:S(2)}) collective-permute-start(bf16[256,128]{1,0:T(8,128)(2,1)S(1)} %get-tuple-element.100), channel_id=1, source_target_pairs={{14,2},{15,3},{30,18},{31,19}} | collective-permute-start | bytes 196616 | tf_op jit(solution)/shard_map/ppermute | solution.py:22
  49.3 7.9 %collective-permute-start.16 = (bf16[512,128]{1,0:T(8,128)(2,1)S(1)}, bf16[512,128]{1,0:T(8,128)(2,1)S(1)}, u32[]{:S(2)}, u32[]{:S(2)}) collective-permute-start(bf16[512,128]{1,0:T(8,128)(2,1)S(1)} %get-tuple-element.98), channel_id=1, source_target_pairs={{2,0},{3,1},{18,16},{19,17}} | collective-permute-start | bytes 393224 | tf_op jit(solution)/shard_map/ppermute | solution.py:22
  57.3 0.7 %copy-start = (f32[512,128]{1,0:T(8,128)}, f32[512,128]{1,0:T(8,128)S(1)}, u32[]{:S(2)}) copy-start(f32[512,128]{1,0:T(8,128)S(1)} %get-tuple-element.104) | copy-start | bytes 786436
  57.3 0.8 %copy-start.1 = (f32[512,128]{1,0:T(8,128)}, f32[512,128]{1,0:T(8,128)S(1)}, u32[]{:S(2)}) copy-start(f32[512,128]{1,0:T(8,128)S(1)} %get-tuple-element.105) | copy-start | bytes 786436

commit v16 on v15

--- a/solution.py
+++ b/solution.py
@@ -475,7 +475,7 @@
         finished = finish(total)
         near, first, last = units(permuted(behind[0], neighbours), 0, unit, 3)
         none = jnp.zeros_like(first)
-        parts = [permuted(total, [(j, 0), (j + 1, 1)]) for j in range(2, size, 2)]
+        parts = [permuted(total, [(j, 0), (j + 1, 1)]) for j in reversed(range(2, size, 2))]
         two = permuted(added(two, near).astype(BF16), back(shift_route(2, size)[1:]))
         four = after(added(four, jnp.where(even, last, first)).astype(BF16), finished[1])
         four = permuted(four, far_route)

time: 58.4 us -> 57.4 us (0.983)
  waiting for transfers between devices: 18.2 us -> 17.1 us
    ppermute x17, waiting for transfers between devices: 18.2 us -> 17.1 us  [permuted(): return lax.ppermute(block, 'node', route)]
  transfers between devices with their start and end apart: 17 -> 17, of which waited for: 8 -> 7; matrix products, arithmetic and copies ran while one was open for 1% -> 1% of each run, Pallas kernels for 14% -> 14%
where the time goes in v16:
time: 57.4 us; the launch traced here: 57.1 us
  starting transfers between devices  26.9 us (47%)
  waiting for transfers between devices  17.1 us (30%)
  Pallas kernels  10.8 us (19%)
  between operations  0.94 us (2%)
  local copies, waits for them, and re-layouts  0.78 us (1%)
    ppermute x17, starting transfers between devices, permuted(): return lax.ppermute(block, 'node', route)  26.9 us
    ppermute x17, waiting for transfers between devices, permuted(): return lax.ppermute(block, 'node', route)  17.1 us
    pallas_call x6, Pallas kernels, call(): pl.pallas_call(kernel, in_specs=[place] * len(operands), out_specs=[VMEM]...  10.8 us
  transfers between devices with their start and end apart: 17, of which 7 were waited for; matrix products, arithmetic and copies ran while one was open for 1% of the time, Pallas kernels for 14%

profile of v16, /device:TPU:0, one launch (start us, length us, event | category | flops | bytes accessed | tf_op | source)
XLA Modules:
  0.0 57.1 jit_solution(17796357212323469487)
XLA Ops:
  0.6 5.9 %collective-permute-start = (bf16[512,128]{1,0:T(8,128)(2,1)}, bf16[512,128]{1,0:T(8,128)(2,1)S(1)}, u32[]{:S(2)}, u32[]{:S(2)}) collective-permute-start(bf16[512,128]{1,0:T(8,128)(2,1)} %bitcast.6), channel_id=1, source_target_pairs={{0,8},{1,9},{16,24},{17,25}} | collective-permute-start | bytes 393224 | tf_op jit(solution)/shard_map/ppermute | solution.py:22
  6.6 1.3 %collective-permute-start.2 = (bf16[512,128]{1,0:T(8,128)(2,1)}, bf16[512,128]{1,0:T(8,128)(2,1)S(1)}, u32[]{:S(2)}, u32[]{:S(2)}) collective-permute-start(bf16[512,128]{1,0:T(8,128)(2,1)} %bitcast.8), channel_id=1, source_target_pairs={{0,2},{1,3},{16,18},{17,19}} | collective-permute-start | bytes 393224 | tf_op jit(solution)/shard_map/ppermute | solution.py:22
  7.9 1.3 %collective-permute-start.1 = (bf16[512,128]{1,0:T(8,128)(2,1)}, bf16[512,128]{1,0:T(8,128)(2,1)S(1)}, u32[]{:S(2)}, u32[]{:S(2)}) collective-permute-start(bf16[512,128]{1,0:T(8,128)(2,1)} %bitcast.9), channel_id=1, source_target_pairs={{0,10},{1,11},{16,26},{17,27}} | collective-permute-start | bytes 393224 | tf_op jit(solution)/shard_map/ppermute | solution.py:22
  9.2 1.2 %load.1 = (bf16[256,128]{1,0:T(8,128)(2,1)S(1)}, bf16[512,128]{1,0:T(8,128)(2,1)S(1)}, bf16[4,128,128]{2,1,0:T(8,128)(2,1)S(1)}, bf16[4,128,128]{2,1,0:T(8,128)(...) custom-call(s32[64]{0:T(128)} %refs_0_.1, s32[64]{0:T(128)} %refs_1_.1, bf16[512,128]{1,0:T(8,128)(2,1)} %bitcast.7, ...), custom_call_target="tpu_custom_call" | custom-call | flops 1048576 | bytes 983552 | tf_op jit(solution)/shard_map/load/pallas_call | solution.py:265
  10.4 0.0 collective-permute-done
  10.4 0.7 %collective-permute-start.4 = (bf16[256,128]{1,0:T(8,128)(2,1)S(1)}, bf16[256,128]{1,0:T(8,128)(2,1)S(1)}, u32[]{:S(2)}, u32[]{:S(2)}) collective-permute-start(bf16[256,128]{1,0:T(8,128)(2,1)S(1)} %get-tuple-element.70), channel_id=1, source_target_pairs={{2,14},{3,15},{18,30},{19,31}} | collective-permute-start | bytes 196616 | tf_op jit(solution)/shard_map/ppermute | solution.py:22
  11.1 0.7 %collective-permute-start.3 = (bf16[256,128]{1,0:T(8,128)(2,1)S(1)}, bf16[256,128]{1,0:T(8,128)(2,1)S(1)}, u32[]{:S(2)}, u32[]{:S(2)}) collective-permute-start(bf16[256,128]{1,0:T(8,128)(2,1)S(1)} %get-tuple-element.70), channel_id=1, source_target_pairs={{2,10},{4,12},{6,14},{3,11},{5,13},{7,15},{18,26},{20,28},{22,30},... | collective-permute-start | bytes 196616 | tf_op jit(solution)/shard_map/ppermute | solution.py:22
  11.8 0.0 collective-permute-done.2
  11.8 0.7 %collective-permute-done.1 = bf16[512,128]{1,0:T(8,128)(2,1)S(1)} collective-permute-done((bf16[512,128]{1,0:T(8,128)(2,1)}, bf16[512,128]{1,0:T(8,128)(2,1)S(1)}, u32[]{:S(2)}, u32[]{:S(2)}) %collective-permute-start.1) | collective-permute-done | bytes 131104 | tf_op jit(solution)/shard_map/ppermute | solution.py:22
  12.5 0.1 add_convert_fusion.2
  12.5 1.6 %pack.1 = (bf16[4,1024,128]{2,1,0:T(8,128)(2,1)S(1)}, bf16[4,1024,128]{2,1,0:T(8,128)(2,1)S(1)}) custom-call(bf16[128,32,128]{2,1,0:T(8,128)(2,1)} %q_ref, bf16[128,32,128]{2,1,0:T(8,128)(2,1)} %g_ref.1), custom_call_target="tpu_custom_call" | custom-call | flops 1048576 | bytes 4194304 | tf_op jit(solution)/shard_map/pack/pallas_call | solution.py:265
  14.2 0.0 collective-permute-done.4.refs_8_
  14.2 0.0 collective-permute-done.3.refs_7_
  14.2 2.9 %collective-permute-start.5 = (bf16[768,128]{1,0:T(8,128)(2,1)S(1)}, bf16[768,128]{1,0:T(8,128)(2,1)S(1)}, u32[]{:S(2)}, u32[]{:S(2)}) collective-permute-start(bf16[768,128]{1,0:T(8,128)(2,1)S(1)} %pad_maximum_fusion), channel_id=1, source_target_pairs={{0,4},{2,6},{4,8},{6,10},{8,12},{10,14},{1,5},{3,7},{5,9},{7,11},{... | collective-permute-start | bytes 589832 | tf_op jit(solution)/shard_map/ppermute | solution.py:22
  17.2 2.8 %collective-permute-start.6 = (bf16[512,128]{1,0:T(8,128)(2,1)S(1)}, bf16[512,128]{1,0:T(8,128)(2,1)S(1)}, u32[]{:S(2)}, u32[]{:S(2)}) collective-permute-start(bf16[512,128]{1,0:T(8,128)(2,1)S(1)} %maximum_select_fusion), channel_id=1, source_target_pairs={{0,2},{2,0},{4,6},{6,4},{8,10},{10,8},{12,14},{14,12},{1,3},{3,1},... | collective-permute-start | bytes 393224 | tf_op jit(solution)/shard_map/ppermute | solution.py:22
  20.0 1.4 %collective-permute-done.5.refs_5_ = bf16[768,128]{1,0:T(8,128)(2,1)S(1)} collective-permute-done((bf16[768,128]{1,0:T(8,128)(2,1)S(1)}, bf16[768,128]{1,0:T(8,128)(2,1)S(1)}, u32[]{:S(2)}, u32[]{:S(2)}) %collective-permute-start.5) | collective-permute-done | bytes 196640 | tf_op jit(solution)/shard_map/ppermute | solution.py:22
  21.5 1.4 %collective-permute-done.6.refs_6_ = bf16[512,128]{1,0:T(8,128)(2,1)S(1)} collective-permute-done((bf16[512,128]{1,0:T(8,128)(2,1)S(1)}, bf16[512,128]{1,0:T(8,128)(2,1)S(1)}, u32[]{:S(2)}, u32[]{:S(2)}) %collective-permute-start.6) | collective-permute-done | bytes 131104 | tf_op jit(solution)/shard_map/ppermute | solution.py:22
  23.0 2.0 %collective-permute-start.7 = (bf16[768,128]{1,0:T(8,128)(2,1)S(1)}, bf16[768,128]{1,0:T(8,128)(2,1)S(1)}, u32[]{:S(2)}, u32[]{:S(2)}) collective-permute-start(bf16[768,128]{1,0:T(8,128)(2,1)S(1)} %pad_maximum_fusion.1), channel_id=1, source_target_pairs={{0,2},{2,0},{4,6},{6,4},{8,10},{10,8},{12,14},{14,12},{1,3},{3,1},... | collective-permute-start | bytes 589832 | tf_op jit(solution)/shard_map/ppermute | solution.py:22
  25.0 1.6 %early.1 = (bf16[4,288,128]{2,1,0:T(8,128)(2,1)S(1)}, f32[4,288,1024]{2,1,0:T(8,128)S(1)}, f32[4,288,1024]{2,1,0:T(8,128)S(1)}, f32[4,8,1024]{2,1,0:T(8,128)S(1)}) custom-call(bf16[4,128,128]{2,1,0:T(8,128)(2,1)S(1)} %get-tuple-element.75.refs_0_, bf16[4,128,128]{2,1,0:T(8,128)(2,1)S(1)} %get-tuple-element.76.refs_1_, ...), custom_call_target="tpu_custom_call" | custom-call | flops 603979776 | bytes 12910592 | tf_op jit(solution)/shard_map/early/pallas_call | solution.py:265
  26.6 2.0 %collective-permute-done.7.refs_7_ = bf16[768,128]{1,0:T(8,128)(2,1)S(1)} collective-permute-done((bf16[768,128]{1,0:T(8,128)(2,1)S(1)}, bf16[768,128]{1,0:T(8,128)(2,1)S(1)}, u32[]{:S(2)}, u32[]{:S(2)}) %collective-permute-start.7) | collective-permute-done | bytes 196640 | tf_op jit(solution)/shard_map/ppermute | solution.py:22
  28.7 2.6 %probs.1 = (bf16[512,128]{1,0:T(8,128)(2,1)S(1)}, bf16[512,128]{1,0:T(8,128)(2,1)S(1)}, bf16[4,160,128]{2,1,0:T(8,128)(2,1)S(1)}, bf16[4,160,1024]{2,1,0:T(8,128...) custom-call(bf16[512,128]{1,0:T(8,128)(2,1)S(1)} %get-tuple-element.103.refs_0_, ...), custom_call_target="tpu_custom_call" | custom-call | flops 671088640 | bytes 5079040 | tf_op jit(solution)/shard_map/probs/pallas_call | solution.py:265
  31.2 2.1 %collective-permute-start.8 = (bf16[512,128]{1,0:T(8,128)(2,1)S(1)}, bf16[512,128]{1,0:T(8,128)(2,1)S(1)}, u32[]{:S(2)}, u32[]{:S(2)}) collective-permute-start(bf16[512,128]{1,0:T(8,128)(2,1)S(1)} %get-tuple-element.88), channel_id=1, source_target_pairs={{0,2},{2,0},{4,6},{6,4},{8,10},{10,8},{12,14},{14,12},{1,3},{3,1},... | collective-permute-start | bytes 393224 | tf_op jit(solution)/shard_map/ppermute | solution.py:22
  33.3 1.4 %windows.1 = (bf16[768,128]{1,0:T(8,128)(2,1)S(1)}, bf16[768,128]{1,0:T(8,128)(2,1)S(1)}, bf16[4,288,1024]{2,1,0:T(8,128)(2,1)S(1)}, bf16[4,128,1024]{2,1,0:T(8,128)(2,1)S(1)}) custom-call(bf16[4,1024,128]{2,1,0:T(8,128)(2,1)S(1)} %get-tuple-element.65.refs_2_.refs_0_, bf16[4,1024,128]{2,1,0:T(8,128)(2,1)S(1)} %get-tuple-element.66.refs_3_.refs_1_, ...), custom_call_target="tpu_custom_call" | custom-call | flops 402653184 | bytes 17039360 | tf_op jit(solution)/shard_map/windows/pallas_call | solution.py:265
  34.7 0.1 collective-permute-start.12
  34.8 2.7 %collective-permute-done.8 = bf16[512,128]{1,0:T(8,128)(2,1)S(1)} collective-permute-done((bf16[512,128]{1,0:T(8,128)(2,1)S(1)}, bf16[512,128]{1,0:T(8,128)(2,1)S(1)}, u32[]{:S(2)}, u32[]{:S(2)}) %collective-permute-start.8) | collective-permute-done | bytes 131104 | tf_op jit(solution)/shard_map/ppermute | solution.py:22
  37.6 1.3 %collective-permute-start.11 = (bf16[512,128]{1,0:T(8,128)(2,1)S(1)}, bf16[512,128]{1,0:T(8,128)(2,1)S(1)}, u32[]{:S(2)}, u32[]{:S(2)}) collective-permute-start(bf16[512,128]{1,0:T(8,128)(2,1)S(1)} %add_convert_fusion.1), channel_id=1, source_target_pairs={{4,0},{6,2},{5,1},{7,3},{20,16},{22,18},{21,17},{23,19}} | collective-permute-start | bytes 393224 | tf_op jit(solution)/shard_map/ppermute | solution.py:22
  38.9 1.3 %collective-permute-start.10 = (bf16[512,128]{1,0:T(8,128)(2,1)S(1)}, bf16[512,128]{1,0:T(8,128)(2,1)S(1)}, u32[]{:S(2)}, u32[]{:S(2)}) collective-permute-start(bf16[512,128]{1,0:T(8,128)(2,1)S(1)} %add_convert_fusion.1), channel_id=1, source_target_pairs={{8,0},{10,2},{9,1},{11,3},{24,16},{26,18},{25,17},{27,19}} | collective-permute-start | bytes 393224 | tf_op jit(solution)/shard_map/ppermute | solution.py:22
  40.2 1.3 %collective-permute-start.9 = (bf16[512,128]{1,0:T(8,128)(2,1)S(1)}, bf16[512,128]{1,0:T(8,128)(2,1)S(1)}, u32[]{:S(2)}, u32[]{:S(2)}) collective-permute-start(bf16[512,128]{1,0:T(8,128)(2,1)S(1)} %add_convert_fusion.1), channel_id=1, source_target_pairs={{12,0},{14,2},{13,1},{15,3},{28,16},{30,18},{29,17},{31,19}} | collective-permute-start | bytes 393224 | tf_op jit(solution)/shard_map/ppermute | solution.py:22
  41.5 2.4 %grads.1 = (bf16[128,32,128]{2,1,0:T(8,128)(2,1)}, f32[512,128]{1,0:T(8,128)S(1)}, f32[512,128]{1,0:T(8,128)S(1)}) custom-call(bf16[4,1024,128]{2,1,0:T(8,128)(2,1)S(1)} %get-tuple-element.65.refs_2_.refs_0_, bf16[4,1024,128]{2,1,0:T(8,128)(2,1)S(1)} %get-tuple-element.66.refs_3_.refs_1_, bf16[4,160,128]{2,1,0:T(8,128)(2,1)S(1)} %get-tuple-element.78.refs_2_, ...), custom_call_target="tpu_custom_call" | custom-call | flops 469762048 | bytes 8847360 | tf_op jit(solution)/shard_map/grads/pallas_call | solution.py:265
  43.9 0.0 collective-permute-done.12
  43.9 0.1 add_convert_fusion.5
  43.9 0.7 %collective-permute-start.14 = (bf16[256,128]{1,0:T(8,128)(2,1)S(1)}, bf16[256,128]{1,0:T(8,128)(2,1)S(1)}, u32[]{:S(2)}, u32[]{:S(2)}) collective-permute-start(bf16[256,128]{1,0:T(8,128)(2,1)S(1)} %get-tuple-element.95), channel_id=1, source_target_pairs={{10,2},{12,4},{14,6},{11,3},{13,5},{15,7},{26,18},{28,20},{30,22},... | collective-permute-start | bytes 196616 | tf_op jit(solution)/shard_map/ppermute | solution.py:22
  44.6 0.7 %collective-permute-start.13 = (bf16[256,128]{1,0:T(8,128)(2,1)S(1)}, bf16[256,128]{1,0:T(8,128)(2,1)S(1)}, u32[]{:S(2)}, u32[]{:S(2)}) collective-permute-start(bf16[256,128]{1,0:T(8,128)(2,1)S(1)} %get-tuple-element.99), channel_id=1, source_target_pairs={{6,2},{8,4},{10,6},{12,8},{14,10},{7,3},{9,5},{11,7},{13,9},{15,11... | collective-permute-start | bytes 196616 | tf_op jit(solution)/shard_map/ppermute | solution.py:22
  45.3 0.0 collective-permute-done.11
  45.3 0.7 %collective-permute-start.15 = (bf16[256,128]{1,0:T(8,128)(2,1)S(1)}, bf16[256,128]{1,0:T(8,128)(2,1)S(1)}, u32[]{:S(2)}, u32[]{:S(2)}) collective-permute-start(bf16[256,128]{1,0:T(8,128)(2,1)S(1)} %get-tuple-element.100), channel_id=1, source_target_pairs={{14,2},{15,3},{30,18},{31,19}} | collective-permute-start | bytes 196616 | tf_op jit(solution)/shard_map/ppermute | solution.py:22
  46.0 3.3 %collective-permute-done.10 = bf16[512,128]{1,0:T(8,128)(2,1)S(1)} collective-permute-done((bf16[512,128]{1,0:T(8,128)(2,1)S(1)}, bf16[512,128]{1,0:T(8,128)(2,1)S(1)}, u32[]{:S(2)}, u32[]{:S(2)}) %collective-permute-start.10) | collective-permute-done | bytes 131104 | tf_op jit(solution)/shard_map/ppermute | solution.py:22
  49.2 0.0 collective-permute-done.9
  49.2 0.1 select_add_fusion.1
  49.3 1.3 %collective-permute-start.16 = (bf16[512,128]{1,0:T(8,128)(2,1)S(1)}, bf16[512,128]{1,0:T(8,128)(2,1)S(1)}, u32[]{:S(2)}, u32[]{:S(2)}) collective-permute-start(bf16[512,128]{1,0:T(8,128)(2,1)S(1)} %get-tuple-element.98), channel_id=1, source_target_pairs={{2,0},{3,1},{18,16},{19,17}} | collective-permute-start | bytes 393224 | tf_op jit(solution)/shard_map/ppermute | solution.py:22
  50.6 0.0 collective-permute-done.14
  50.7 0.0 collective-permute-done.13
  50.7 0.0 collective-permute-done.15
  50.7 5.5 %collective-permute-done.16 = bf16[512,128]{1,0:T(8,128)(2,1)S(1)} collective-permute-done((bf16[512,128]{1,0:T(8,128)(2,1)S(1)}, bf16[512,128]{1,0:T(8,128)(2,1)S(1)}, u32[]{:S(2)}, u32[]{:S(2)}) %collective-permute-start.16) | collective-permute-done | bytes 131104 | tf_op jit(solution)/shard_map/ppermute | solution.py:22
  56.3 0.0 copy-start
  56.3 0.0 copy-start.1
  56.3 0.7 %copy-done = f32[512,128]{1,0:T(8,128)} copy-done((f32[512,128]{1,0:T(8,128)}, f32[512,128]{1,0:T(8,128)S(1)}, u32[]{:S(2)}) %copy-start) | copy-done | bytes 262168
  57.0 0.1 copy-done.1
  (10 shorter events, 0.2 us)
Async XLA Ops:
  0.6 9.8 %collective-permute-start = (bf16[512,128]{1,0:T(8,128)(2,1)}, bf16[512,128]{1,0:T(8,128)(2,1)S(1)}, u32[]{:S(2)}, u32[]{:S(2)}) collective-permute-start(bf16[512,128]{1,0:T(8,128)(2,1)} %bitcast.6), channel_id=1, source_target_pairs={{0,8},{1,9},{16,24},{17,25}} | collective-permute-start | bytes 393224 | tf_op jit(solution)/shard_map/ppermute | solution.py:22
  6.6 5.2 %collective-permute-start.2 = (bf16[512,128]{1,0:T(8,128)(2,1)}, bf16[512,128]{1,0:T(8,128)(2,1)S(1)}, u32[]{:S(2)}, u32[]{:S(2)}) collective-permute-start(bf16[512,128]{1,0:T(8,128)(2,1)} %bitcast.8), channel_id=1, source_target_pairs={{0,2},{1,3},{16,18},{17,19}} | collective-permute-start | bytes 393224 | tf_op jit(solution)/shard_map/ppermute | solution.py:22
  7.9 4.6 %collective-permute-start.1 = (bf16[512,128]{1,0:T(8,128)(2,1)}, bf16[512,128]{1,0:T(8,128)(2,1)S(1)}, u32[]{:S(2)}, u32[]{:S(2)}) collective-permute-start(bf16[512,128]{1,0:T(8,128)(2,1)} %bitcast.9), channel_id=1, source_target_pairs={{0,10},{1,11},{16,26},{17,27}} | collective-permute-start | bytes 393224 | tf_op jit(solution)/shard_map/ppermute | solution.py:22
  10.4 3.8 %collective-permute-start.4 = (bf16[256,128]{1,0:T(8,128)(2,1)S(1)}, bf16[256,128]{1,0:T(8,128)(2,1)S(1)}, u32[]{:S(2)}, u32[]{:S(2)}) collective-permute-start(bf16[256,128]{1,0:T(8,128)(2,1)S(1)} %get-tuple-element.70), channel_id=1, source_target_pairs={{2,14},{3,15},{18,30},{19,31}} | collective-permute-start | bytes 196616 | tf_op jit(solution)/shard_map/ppermute | solution.py:22
  11.1 3.1 %collective-permute-start.3 = (bf16[256,128]{1,0:T(8,128)(2,1)S(1)}, bf16[256,128]{1,0:T(8,128)(2,1)S(1)}, u32[]{:S(2)}, u32[]{:S(2)}) collective-permute-start(bf16[256,128]{1,0:T(8,128)(2,1)S(1)} %get-tuple-element.70), channel_id=1, source_target_pairs={{2,10},{4,12},{6,14},{3,11},{5,13},{7,15},{18,26},{20,28},{22,30},... | collective-permute-start | bytes 196616 | tf_op jit(solution)/shard_map/ppermute | solution.py:22
  14.2 7.2 %collective-permute-start.5 = (bf16[768,128]{1,0:T(8,128)(2,1)S(1)}, bf16[768,128]{1,0:T(8,128)(2,1)S(1)}, u32[]{:S(2)}, u32[]{:S(2)}) collective-permute-start(bf16[768,128]{1,0:T(8,128)(2,1)S(1)} %pad_maximum_fusion), channel_id=1, source_target_pairs={{0,4},{2,6},{4,8},{6,10},{8,12},{10,14},{1,5},{3,7},{5,9},{7,11},{... | collective-permute-start | bytes 589832 | tf_op jit(solution)/shard_map/ppermute | solution.py:22
  17.2 5.8 %collective-permute-start.6 = (bf16[512,128]{1,0:T(8,128)(2,1)S(1)}, bf16[512,128]{1,0:T(8,128)(2,1)S(1)}, u32[]{:S(2)}, u32[]{:S(2)}) collective-permute-start(bf16[512,128]{1,0:T(8,128)(2,1)S(1)} %maximum_select_fusion), channel_id=1, source_target_pairs={{0,2},{2,0},{4,6},{6,4},{8,10},{10,8},{12,14},{14,12},{1,3},{3,1},... | collective-permute-start | bytes 393224 | tf_op jit(solution)/shard_map/ppermute | solution.py:22
  23.0 5.7 %collective-permute-start.7 = (bf16[768,128]{1,0:T(8,128)(2,1)S(1)}, bf16[768,128]{1,0:T(8,128)(2,1)S(1)}, u32[]{:S(2)}, u32[]{:S(2)}) collective-permute-start(bf16[768,128]{1,0:T(8,128)(2,1)S(1)} %pad_maximum_fusion.1), channel_id=1, source_target_pairs={{0,2},{2,0},{4,6},{6,4},{8,10},{10,8},{12,14},{14,12},{1,3},{3,1},... | collective-permute-start | bytes 589832 | tf_op jit(solution)/shard_map/ppermute | solution.py:22
  31.2 6.3 %collective-permute-start.8 = (bf16[512,128]{1,0:T(8,128)(2,1)S(1)}, bf16[512,128]{1,0:T(8,128)(2,1)S(1)}, u32[]{:S(2)}, u32[]{:S(2)}) collective-permute-start(bf16[512,128]{1,0:T(8,128)(2,1)S(1)} %get-tuple-element.88), channel_id=1, source_target_pairs={{0,2},{2,0},{4,6},{6,4},{8,10},{10,8},{12,14},{14,12},{1,3},{3,1},... | collective-permute-start | bytes 393224 | tf_op jit(solution)/shard_map/ppermute | solution.py:22
  34.7 9.2 %collective-permute-start.12 = (bf16[768,128]{1,0:T(8,128)(2,1)S(1)}, bf16[768,128]{1,0:T(8,128)(2,1)S(1)}, u32[]{:S(2)}, u32[]{:S(2)}) collective-permute-start(bf16[768,128]{1,0:T(8,128)(2,1)S(1)} %get-tuple-element.93), channel_id=1, source_target_pairs={{0,2},{2,0},{4,6},{6,4},{8,10},{10,8},{12,14},{14,12},{1,3},{3,1},... | collective-permute-start | bytes 589832 | tf_op jit(solution)/shard_map/ppermute | solution.py:22
  37.6 7.7 %collective-permute-start.11 = (bf16[512,128]{1,0:T(8,128)(2,1)S(1)}, bf16[512,128]{1,0:T(8,128)(2,1)S(1)}, u32[]{:S(2)}, u32[]{:S(2)}) collective-permute-start(bf16[512,128]{1,0:T(8,128)(2,1)S(1)} %add_convert_fusion.1), channel_id=1, source_target_pairs={{4,0},{6,2},{5,1},{7,3},{20,16},{22,18},{21,17},{23,19}} | collective-permute-start | bytes 393224 | tf_op jit(solution)/shard_map/ppermute | solution.py:22
  38.9 10.4 %collective-permute-start.10 = (bf16[512,128]{1,0:T(8,128)(2,1)S(1)}, bf16[512,128]{1,0:T(8,128)(2,1)S(1)}, u32[]{:S(2)}, u32[]{:S(2)}) collective-permute-start(bf16[512,128]{1,0:T(8,128)(2,1)S(1)} %add_convert_fusion.1), channel_id=1, source_target_pairs={{8,0},{10,2},{9,1},{11,3},{24,16},{26,18},{25,17},{27,19}} | collective-permute-start | bytes 393224 | tf_op jit(solution)/shard_map/ppermute | solution.py:22
  40.2 9.1 %collective-permute-start.9 = (bf16[512,128]{1,0:T(8,128)(2,1)S(1)}, bf16[512,128]{1,0:T(8,128)(2,1)S(1)}, u32[]{:S(2)}, u32[]{:S(2)}) collective-permute-start(bf16[512,128]{1,0:T(8,128)(2,1)S(1)} %add_convert_fusion.1), channel_id=1, source_target_pairs={{12,0},{14,2},{13,1},{15,3},{28,16},{30,18},{29,17},{31,19}} | collective-permute-start | bytes 393224 | tf_op jit(solution)/shard_map/ppermute | solution.py:22
  43.9 6.7 %collective-permute-start.14 = (bf16[256,128]{1,0:T(8,128)(2,1)S(1)}, bf16[256,128]{1,0:T(8,128)(2,1)S(1)}, u32[]{:S(2)}, u32[]{:S(2)}) collective-permute-start(bf16[256,128]{1,0:T(8,128)(2,1)S(1)} %get-tuple-element.95), channel_id=1, source_target_pairs={{10,2},{12,4},{14,6},{11,3},{13,5},{15,7},{26,18},{28,20},{30,22},... | collective-permute-start | bytes 196616 | tf_op jit(solution)/shard_map/ppermute | solution.py:22
  44.6 6.0 %collective-permute-start.13 = (bf16[256,128]{1,0:T(8,128)(2,1)S(1)}, bf16[256,128]{1,0:T(8,128)(2,1)S(1)}, u32[]{:S(2)}, u32[]{:S(2)}) collective-permute-start(bf16[256,128]{1,0:T(8,128)(2,1)S(1)} %get-tuple-element.99), channel_id=1, source_target_pairs={{6,2},{8,4},{10,6},{12,8},{14,10},{7,3},{9,5},{11,7},{13,9},{15,11... | collective-permute-start | bytes 196616 | tf_op jit(solution)/shard_map/ppermute | solution.py:22
  45.3 5.4 %collective-permute-start.15 = (bf16[256,128]{1,0:T(8,128)(2,1)S(1)}, bf16[256,128]{1,0:T(8,128)(2,1)S(1)}, u32[]{:S(2)}, u32[]{:S(2)}) collective-permute-start(bf16[256,128]{1,0:T(8,128)(2,1)S(1)} %get-tuple-element.100), channel_id=1, source_target_pairs={{14,2},{15,3},{30,18},{31,19}} | collective-permute-start | bytes 196616 | tf_op jit(solution)/shard_map/ppermute | solution.py:22
  49.3 6.9 %collective-permute-start.16 = (bf16[512,128]{1,0:T(8,128)(2,1)S(1)}, bf16[512,128]{1,0:T(8,128)(2,1)S(1)}, u32[]{:S(2)}, u32[]{:S(2)}) collective-permute-start(bf16[512,128]{1,0:T(8,128)(2,1)S(1)} %get-tuple-element.98), channel_id=1, source_target_pairs={{2,0},{3,1},{18,16},{19,17}} | collective-permute-start | bytes 393224 | tf_op jit(solution)/shard_map/ppermute | solution.py:22
  56.3 0.7 %copy-start = (f32[512,128]{1,0:T(8,128)}, f32[512,128]{1,0:T(8,128)S(1)}, u32[]{:S(2)}) copy-start(f32[512,128]{1,0:T(8,128)S(1)} %get-tuple-element.104) | copy-start | bytes 786436
  56.3 0.8 %copy-start.1 = (f32[512,128]{1,0:T(8,128)}, f32[512,128]{1,0:T(8,128)S(1)}, u32[]{:S(2)}) copy-start(f32[512,128]{1,0:T(8,128)S(1)} %get-tuple-element.105) | copy-start | bytes 786436

commit v17 on v16

--- a/solution.py
+++ b/solution.py
@@ -436,7 +436,7 @@
         qh, gh = pack(queries, grad_out, keys.shape[0] // queries.shape[0])
         far = permuted(head, far_route)
         six = permuted(head, [(1, 7)])
-        held = after(added(held, values_far, values_next, keys_far).astype(BF16), far, six, qh)
+        held = after(added(held, values_next, values_far, keys_far).astype(BF16), six, far, qh)
         second = permuted(jnp.concatenate([held, head]), near_route)
         crossed = jnp.where(even, jnp.concatenate([head, far]), jnp.concatenate([far, six]))
         crossed = permuted(crossed, neighbours)

time: 57.4 us -> 56.2 us (0.979)
  starting transfers between devices: 26.9 us -> 24.6 us
  waiting for transfers between devices: 17.1 us -> 18.3 us
    ppermute x17, starting transfers between devices: 26.9 us -> 24.6 us  [permuted(): return lax.ppermute(block, 'node', route)]
    ppermute x17, waiting for transfers between devices: 17.1 us -> 18.3 us  [permuted(): return lax.ppermute(block, 'node', route)]
  transfers between devices with their start and end apart: 17 -> 17, of which waited for: 7 -> 11; matrix products, arithmetic and copies ran while one was open for 1% -> 1% of each run, Pallas kernels for 14% -> 15%
where the time goes in v17:
time: 56.2 us; the launch traced here: 55.8 us
  starting transfers between devices  24.6 us (44%)
  waiting for transfers between devices  18.3 us (33%)
  Pallas kernels  10.8 us (19%)
  between operations  0.92 us (2%)
  local copies, waits for them, and re-layouts  0.78 us (1%)
    ppermute x17, starting transfers between devices, permuted(): return lax.ppermute(block, 'node', route)  24.6 us
    ppermute x17, waiting for transfers between devices, permuted(): return lax.ppermute(block, 'node', route)  18.3 us
    pallas_call x6, Pallas kernels, call(): pl.pallas_call(kernel, in_specs=[place] * len(operands), out_specs=[VMEM]...  10.8 us
  transfers between devices with their start and end apart: 17, of which 11 were waited for; matrix products, arithmetic and copies ran while one was open for 1% of the time, Pallas kernels for 15%

profile of v17, /device:TPU:0, one launch (start us, length us, event | category | flops | bytes accessed | tf_op | source)
XLA Modules:
  0.0 55.8 jit_solution(17713402981025871043)
XLA Ops:
  0.6 5.9 %collective-permute-start = (bf16[512,128]{1,0:T(8,128)(2,1)}, bf16[512,128]{1,0:T(8,128)(2,1)S(1)}, u32[]{:S(2)}, u32[]{:S(2)}) collective-permute-start(bf16[512,128]{1,0:T(8,128)(2,1)} %bitcast.6), channel_id=1, source_target_pairs={{0,8},{1,9},{16,24},{17,25}} | collective-permute-start | bytes 393224 | tf_op jit(solution)/shard_map/ppermute | solution.py:22
  6.6 1.6 %collective-permute-start.2 = (bf16[512,128]{1,0:T(8,128)(2,1)}, bf16[512,128]{1,0:T(8,128)(2,1)S(1)}, u32[]{:S(2)}, u32[]{:S(2)}) collective-permute-start(bf16[512,128]{1,0:T(8,128)(2,1)} %bitcast.8), channel_id=1, source_target_pairs={{0,10},{1,11},{16,26},{17,27}} | collective-permute-start | bytes 393224 | tf_op jit(solution)/shard_map/ppermute | solution.py:22
  8.2 1.3 %collective-permute-start.1 = (bf16[512,128]{1,0:T(8,128)(2,1)}, bf16[512,128]{1,0:T(8,128)(2,1)S(1)}, u32[]{:S(2)}, u32[]{:S(2)}) collective-permute-start(bf16[512,128]{1,0:T(8,128)(2,1)} %bitcast.9), channel_id=1, source_target_pairs={{0,2},{1,3},{16,18},{17,19}} | collective-permute-start | bytes 393224 | tf_op jit(solution)/shard_map/ppermute | solution.py:22
  9.5 1.2 %load.1 = (bf16[256,128]{1,0:T(8,128)(2,1)S(1)}, bf16[512,128]{1,0:T(8,128)(2,1)S(1)}, bf16[4,128,128]{2,1,0:T(8,128)(2,1)S(1)}, bf16[4,128,128]{2,1,0:T(8,128)(...) custom-call(s32[64]{0:T(128)} %refs_0_.1, s32[64]{0:T(128)} %refs_1_.1, bf16[512,128]{1,0:T(8,128)(2,1)} %bitcast.7, ...), custom_call_target="tpu_custom_call" | custom-call | flops 1048576 | bytes 983552 | tf_op jit(solution)/shard_map/load/pallas_call | solution.py:265
  10.7 0.1 collective-permute-done
  10.8 0.7 %collective-permute-start.4 = (bf16[256,128]{1,0:T(8,128)(2,1)S(1)}, bf16[256,128]{1,0:T(8,128)(2,1)S(1)}, u32[]{:S(2)}, u32[]{:S(2)}) collective-permute-start(bf16[256,128]{1,0:T(8,128)(2,1)S(1)} %get-tuple-element.70), channel_id=1, source_target_pairs={{2,10},{4,12},{6,14},{3,11},{5,13},{7,15},{18,26},{20,28},{22,30},... | collective-permute-start | bytes 196616 | tf_op jit(solution)/shard_map/ppermute | solution.py:22
  11.4 0.7 %collective-permute-start.3 = (bf16[256,128]{1,0:T(8,128)(2,1)S(1)}, bf16[256,128]{1,0:T(8,128)(2,1)S(1)}, u32[]{:S(2)}, u32[]{:S(2)}) collective-permute-start(bf16[256,128]{1,0:T(8,128)(2,1)S(1)} %get-tuple-element.70), channel_id=1, source_target_pairs={{2,14},{3,15},{18,30},{19,31}} | collective-permute-start | bytes 196616 | tf_op jit(solution)/shard_map/ppermute | solution.py:22
  12.1 0.4 collective-permute-done.2
  12.5 0.1 collective-permute-done.1
  12.5 0.1 add_convert_fusion.2
  12.6 1.6 %pack.1 = (bf16[4,1024,128]{2,1,0:T(8,128)(2,1)S(1)}, bf16[4,1024,128]{2,1,0:T(8,128)(2,1)S(1)}) custom-call(bf16[128,32,128]{2,1,0:T(8,128)(2,1)} %q_ref, bf16[128,32,128]{2,1,0:T(8,128)(2,1)} %g_ref.1), custom_call_target="tpu_custom_call" | custom-call | flops 1048576 | bytes 4194304 | tf_op jit(solution)/shard_map/pack/pallas_call | solution.py:265
  14.3 0.0 collective-permute-done.4.refs_7_
  14.3 0.0 collective-permute-done.3.refs_8_
  14.3 2.8 %collective-permute-start.5 = (bf16[768,128]{1,0:T(8,128)(2,1)S(1)}, bf16[768,128]{1,0:T(8,128)(2,1)S(1)}, u32[]{:S(2)}, u32[]{:S(2)}) collective-permute-start(bf16[768,128]{1,0:T(8,128)(2,1)S(1)} %pad_maximum_fusion), channel_id=1, source_target_pairs={{0,4},{2,6},{4,8},{6,10},{8,12},{10,14},{1,5},{3,7},{5,9},{7,11},{... | collective-permute-start | bytes 589832 | tf_op jit(solution)/shard_map/ppermute | solution.py:22
  17.2 1.3 %collective-permute-start.6 = (bf16[512,128]{1,0:T(8,128)(2,1)S(1)}, bf16[512,128]{1,0:T(8,128)(2,1)S(1)}, u32[]{:S(2)}, u32[]{:S(2)}) collective-permute-start(bf16[512,128]{1,0:T(8,128)(2,1)S(1)} %maximum_select_fusion), channel_id=1, source_target_pairs={{0,2},{2,0},{4,6},{6,4},{8,10},{10,8},{12,14},{14,12},{1,3},{3,1},... | collective-permute-start | bytes 393224 | tf_op jit(solution)/shard_map/ppermute | solution.py:22
  18.4 3.0 %collective-permute-done.5.refs_5_ = bf16[768,128]{1,0:T(8,128)(2,1)S(1)} collective-permute-done((bf16[768,128]{1,0:T(8,128)(2,1)S(1)}, bf16[768,128]{1,0:T(8,128)(2,1)S(1)}, u32[]{:S(2)}, u32[]{:S(2)}) %collective-permute-start.5) | collective-permute-done | bytes 196640 | tf_op jit(solution)/shard_map/ppermute | solution.py:22
  21.5 0.9 %collective-permute-done.6.refs_6_ = bf16[512,128]{1,0:T(8,128)(2,1)S(1)} collective-permute-done((bf16[512,128]{1,0:T(8,128)(2,1)S(1)}, bf16[512,128]{1,0:T(8,128)(2,1)S(1)}, u32[]{:S(2)}, u32[]{:S(2)}) %collective-permute-start.6) | collective-permute-done | bytes 131104 | tf_op jit(solution)/shard_map/ppermute | solution.py:22
  22.4 1.0 %collective-permute-start.7 = (bf16[768,128]{1,0:T(8,128)(2,1)S(1)}, bf16[768,128]{1,0:T(8,128)(2,1)S(1)}, u32[]{:S(2)}, u32[]{:S(2)}) collective-permute-start(bf16[768,128]{1,0:T(8,128)(2,1)S(1)} %pad_maximum_fusion.1), channel_id=1, source_target_pairs={{0,2},{2,0},{4,6},{6,4},{8,10},{10,8},{12,14},{14,12},{1,3},{3,1},... | collective-permute-start | bytes 589832 | tf_op jit(solution)/shard_map/ppermute | solution.py:22
  23.4 1.6 %early.1 = (bf16[4,288,128]{2,1,0:T(8,128)(2,1)S(1)}, f32[4,288,1024]{2,1,0:T(8,128)S(1)}, f32[4,288,1024]{2,1,0:T(8,128)S(1)}, f32[4,8,1024]{2,1,0:T(8,128)S(1)}) custom-call(bf16[4,128,128]{2,1,0:T(8,128)(2,1)S(1)} %get-tuple-element.75.refs_0_, bf16[4,128,128]{2,1,0:T(8,128)(2,1)S(1)} %get-tuple-element.76.refs_1_, ...), custom_call_target="tpu_custom_call" | custom-call | flops 603979776 | bytes 12910592 | tf_op jit(solution)/shard_map/early/pallas_call | solution.py:265
  25.0 3.0 %collective-permute-done.7.refs_7_ = bf16[768,128]{1,0:T(8,128)(2,1)S(1)} collective-permute-done((bf16[768,128]{1,0:T(8,128)(2,1)S(1)}, bf16[768,128]{1,0:T(8,128)(2,1)S(1)}, u32[]{:S(2)}, u32[]{:S(2)}) %collective-permute-start.7) | collective-permute-done | bytes 196640 | tf_op jit(solution)/shard_map/ppermute | solution.py:22
  28.1 2.6 %probs.1 = (bf16[512,128]{1,0:T(8,128)(2,1)S(1)}, bf16[512,128]{1,0:T(8,128)(2,1)S(1)}, bf16[4,160,128]{2,1,0:T(8,128)(2,1)S(1)}, bf16[4,160,1024]{2,1,0:T(8,128...) custom-call(bf16[512,128]{1,0:T(8,128)(2,1)S(1)} %get-tuple-element.103.refs_0_, ...), custom_call_target="tpu_custom_call" | custom-call | flops 671088640 | bytes 5079040 | tf_op jit(solution)/shard_map/probs/pallas_call | solution.py:265
  30.7 1.1 %collective-permute-start.8 = (bf16[512,128]{1,0:T(8,128)(2,1)S(1)}, bf16[512,128]{1,0:T(8,128)(2,1)S(1)}, u32[]{:S(2)}, u32[]{:S(2)}) collective-permute-start(bf16[512,128]{1,0:T(8,128)(2,1)S(1)} %get-tuple-element.88), channel_id=1, source_target_pairs={{0,2},{2,0},{4,6},{6,4},{8,10},{10,8},{12,14},{14,12},{1,3},{3,1},... | collective-permute-start | bytes 393224 | tf_op jit(solution)/shard_map/ppermute | solution.py:22
  31.8 1.4 %windows.1 = (bf16[768,128]{1,0:T(8,128)(2,1)S(1)}, bf16[768,128]{1,0:T(8,128)(2,1)S(1)}, bf16[4,288,1024]{2,1,0:T(8,128)(2,1)S(1)}, bf16[4,128,1024]{2,1,0:T(8,128)(2,1)S(1)}) custom-call(bf16[4,1024,128]{2,1,0:T(8,128)(2,1)S(1)} %get-tuple-element.65.refs_2_.refs_0_, bf16[4,1024,128]{2,1,0:T(8,128)(2,1)S(1)} %get-tuple-element.66.refs_3_.refs_1_, ...), custom_call_target="tpu_custom_call" | custom-call | flops 402653184 | bytes 17039360 | tf_op jit(solution)/shard_map/windows/pallas_call | solution.py:265
  33.2 1.1 %collective-permute-start.12 = (bf16[768,128]{1,0:T(8,128)(2,1)S(1)}, bf16[768,128]{1,0:T(8,128)(2,1)S(1)}, u32[]{:S(2)}, u32[]{:S(2)}) collective-permute-start(bf16[768,128]{1,0:T(8,128)(2,1)S(1)} %get-tuple-element.93), channel_id=1, source_target_pairs={{0,2},{2,0},{4,6},{6,4},{8,10},{10,8},{12,14},{14,12},{1,3},{3,1},... | collective-permute-start | bytes 589832 | tf_op jit(solution)/shard_map/ppermute | solution.py:22
  34.2 1.8 %collective-permute-done.8 = bf16[512,128]{1,0:T(8,128)(2,1)S(1)} collective-permute-done((bf16[512,128]{1,0:T(8,128)(2,1)S(1)}, bf16[512,128]{1,0:T(8,128)(2,1)S(1)}, u32[]{:S(2)}, u32[]{:S(2)}) %collective-permute-start.8) | collective-permute-done | bytes 131104 | tf_op jit(solution)/shard_map/ppermute | solution.py:22
  36.1 1.3 %collective-permute-start.11 = (bf16[512,128]{1,0:T(8,128)(2,1)S(1)}, bf16[512,128]{1,0:T(8,128)(2,1)S(1)}, u32[]{:S(2)}, u32[]{:S(2)}) collective-permute-start(bf16[512,128]{1,0:T(8,128)(2,1)S(1)} %add_convert_fusion.1), channel_id=1, source_target_pairs={{4,0},{6,2},{5,1},{7,3},{20,16},{22,18},{21,17},{23,19}} | collective-permute-start | bytes 393224 | tf_op jit(solution)/shard_map/ppermute | solution.py:22
  37.4 1.3 %collective-permute-start.10 = (bf16[512,128]{1,0:T(8,128)(2,1)S(1)}, bf16[512,128]{1,0:T(8,128)(2,1)S(1)}, u32[]{:S(2)}, u32[]{:S(2)}) collective-permute-start(bf16[512,128]{1,0:T(8,128)(2,1)S(1)} %add_convert_fusion.1), channel_id=1, source_target_pairs={{8,0},{10,2},{9,1},{11,3},{24,16},{26,18},{25,17},{27,19}} | collective-permute-start | bytes 393224 | tf_op jit(solution)/shard_map/ppermute | solution.py:22
  38.7 1.3 %collective-permute-start.9 = (bf16[512,128]{1,0:T(8,128)(2,1)S(1)}, bf16[512,128]{1,0:T(8,128)(2,1)S(1)}, u32[]{:S(2)}, u32[]{:S(2)}) collective-permute-start(bf16[512,128]{1,0:T(8,128)(2,1)S(1)} %add_convert_fusion.1), channel_id=1, source_target_pairs={{12,0},{14,2},{13,1},{15,3},{28,16},{30,18},{29,17},{31,19}} | collective-permute-start | bytes 393224 | tf_op jit(solution)/shard_map/ppermute | solution.py:22
  40.0 2.4 %grads.1 = (bf16[128,32,128]{2,1,0:T(8,128)(2,1)}, f32[512,128]{1,0:T(8,128)S(1)}, f32[512,128]{1,0:T(8,128)S(1)}) custom-call(bf16[4,1024,128]{2,1,0:T(8,128)(2,1)S(1)} %get-tuple-element.65.refs_2_.refs_0_, bf16[4,1024,128]{2,1,0:T(8,128)(2,1)S(1)} %get-tuple-element.66.refs_3_.refs_1_, bf16[4,160,128]{2,1,0:T(8,128)(2,1)S(1)} %get-tuple-element.78.refs_2_, ...), custom_call_target="tpu_custom_call" | custom-call | flops 469762048 | bytes 8847360 | tf_op jit(solution)/shard_map/grads/pallas_call | solution.py:265
  42.3 0.0 collective-permute-done.12
  42.3 0.1 add_convert_fusion.5
  42.4 0.7 %collective-permute-start.14 = (bf16[256,128]{1,0:T(8,128)(2,1)S(1)}, bf16[256,128]{1,0:T(8,128)(2,1)S(1)}, u32[]{:S(2)}, u32[]{:S(2)}) collective-permute-start(bf16[256,128]{1,0:T(8,128)(2,1)S(1)} %get-tuple-element.95), channel_id=1, source_target_pairs={{10,2},{12,4},{14,6},{11,3},{13,5},{15,7},{26,18},{28,20},{30,22},... | collective-permute-start | bytes 196616 | tf_op jit(solution)/shard_map/ppermute | solution.py:22
  43.1 0.7 %collective-permute-start.13 = (bf16[256,128]{1,0:T(8,128)(2,1)S(1)}, bf16[256,128]{1,0:T(8,128)(2,1)S(1)}, u32[]{:S(2)}, u32[]{:S(2)}) collective-permute-start(bf16[256,128]{1,0:T(8,128)(2,1)S(1)} %get-tuple-element.99), channel_id=1, source_target_pairs={{6,2},{8,4},{10,6},{12,8},{14,10},{7,3},{9,5},{11,7},{13,9},{15,11... | collective-permute-start | bytes 196616 | tf_op jit(solution)/shard_map/ppermute | solution.py:22
  43.7 1.5 %collective-permute-done.11 = bf16[512,128]{1,0:T(8,128)(2,1)S(1)} collective-permute-done((bf16[512,128]{1,0:T(8,128)(2,1)S(1)}, bf16[512,128]{1,0:T(8,128)(2,1)S(1)}, u32[]{:S(2)}, u32[]{:S(2)}) %collective-permute-start.11) | collective-permute-done | bytes 131104 | tf_op jit(solution)/shard_map/ppermute | solution.py:22
  45.3 0.7 %collective-permute-start.15 = (bf16[256,128]{1,0:T(8,128)(2,1)S(1)}, bf16[256,128]{1,0:T(8,128)(2,1)S(1)}, u32[]{:S(2)}, u32[]{:S(2)}) collective-permute-start(bf16[256,128]{1,0:T(8,128)(2,1)S(1)} %get-tuple-element.100), channel_id=1, source_target_pairs={{14,2},{15,3},{30,18},{31,19}} | collective-permute-start | bytes 196616 | tf_op jit(solution)/shard_map/ppermute | solution.py:22
  45.9 0.5 collective-permute-done.10
  46.4 1.6 %collective-permute-done.9 = bf16[512,128]{1,0:T(8,128)(2,1)S(1)} collective-permute-done((bf16[512,128]{1,0:T(8,128)(2,1)S(1)}, bf16[512,128]{1,0:T(8,128)(2,1)S(1)}, u32[]{:S(2)}, u32[]{:S(2)}) %collective-permute-start.9) | collective-permute-done | bytes 131104 | tf_op jit(solution)/shard_map/ppermute | solution.py:22
  48.0 0.1 select_add_fusion.1
  48.1 1.3 %collective-permute-start.16 = (bf16[512,128]{1,0:T(8,128)(2,1)S(1)}, bf16[512,128]{1,0:T(8,128)(2,1)S(1)}, u32[]{:S(2)}, u32[]{:S(2)}) collective-permute-start(bf16[512,128]{1,0:T(8,128)(2,1)S(1)} %get-tuple-element.98), channel_id=1, source_target_pairs={{2,0},{3,1},{18,16},{19,17}} | collective-permute-start | bytes 393224 | tf_op jit(solution)/shard_map/ppermute | solution.py:22
  49.4 0.0 collective-permute-done.14
  49.4 0.0 collective-permute-done.13
  49.4 0.0 collective-permute-done.15
  49.5 5.5 %collective-permute-done.16 = bf16[512,128]{1,0:T(8,128)(2,1)S(1)} collective-permute-done((bf16[512,128]{1,0:T(8,128)(2,1)S(1)}, bf16[512,128]{1,0:T(8,128)(2,1)S(1)}, u32[]{:S(2)}, u32[]{:S(2)}) %collective-permute-start.16) | collective-permute-done | bytes 131104 | tf_op jit(solution)/shard_map/ppermute | solution.py:22
  55.0 0.0 copy-start
  55.1 0.0 copy-start.1
  55.1 0.7 %copy-done = f32[512,128]{1,0:T(8,128)} copy-done((f32[512,128]{1,0:T(8,128)}, f32[512,128]{1,0:T(8,128)S(1)}, u32[]{:S(2)}) %copy-start) | copy-done | bytes 262168
  55.7 0.1 copy-done.1
  (10 shorter events, 0.2 us)
Async XLA Ops:
  0.6 10.1 %collective-permute-start = (bf16[512,128]{1,0:T(8,128)(2,1)}, bf16[512,128]{1,0:T(8,128)(2,1)S(1)}, u32[]{:S(2)}, u32[]{:S(2)}) collective-permute-start(bf16[512,128]{1,0:T(8,128)(2,1)} %bitcast.6), channel_id=1, source_target_pairs={{0,8},{1,9},{16,24},{17,25}} | collective-permute-start | bytes 393224 | tf_op jit(solution)/shard_map/ppermute | solution.py:22
  6.6 5.9 %collective-permute-start.2 = (bf16[512,128]{1,0:T(8,128)(2,1)}, bf16[512,128]{1,0:T(8,128)(2,1)S(1)}, u32[]{:S(2)}, u32[]{:S(2)}) collective-permute-start(bf16[512,128]{1,0:T(8,128)(2,1)} %bitcast.8), channel_id=1, source_target_pairs={{0,10},{1,11},{16,26},{17,27}} | collective-permute-start | bytes 393224 | tf_op jit(solution)/shard_map/ppermute | solution.py:22
  8.2 4.4 %collective-permute-start.1 = (bf16[512,128]{1,0:T(8,128)(2,1)}, bf16[512,128]{1,0:T(8,128)(2,1)S(1)}, u32[]{:S(2)}, u32[]{:S(2)}) collective-permute-start(bf16[512,128]{1,0:T(8,128)(2,1)} %bitcast.9), channel_id=1, source_target_pairs={{0,2},{1,3},{16,18},{17,19}} | collective-permute-start | bytes 393224 | tf_op jit(solution)/shard_map/ppermute | solution.py:22
  10.8 3.5 %collective-permute-start.4 = (bf16[256,128]{1,0:T(8,128)(2,1)S(1)}, bf16[256,128]{1,0:T(8,128)(2,1)S(1)}, u32[]{:S(2)}, u32[]{:S(2)}) collective-permute-start(bf16[256,128]{1,0:T(8,128)(2,1)S(1)} %get-tuple-element.70), channel_id=1, source_target_pairs={{2,10},{4,12},{6,14},{3,11},{5,13},{7,15},{18,26},{20,28},{22,30},... | collective-permute-start | bytes 196616 | tf_op jit(solution)/shard_map/ppermute | solution.py:22
  11.4 2.8 %collective-permute-start.3 = (bf16[256,128]{1,0:T(8,128)(2,1)S(1)}, bf16[256,128]{1,0:T(8,128)(2,1)S(1)}, u32[]{:S(2)}, u32[]{:S(2)}) collective-permute-start(bf16[256,128]{1,0:T(8,128)(2,1)S(1)} %get-tuple-element.70), channel_id=1, source_target_pairs={{2,14},{3,15},{18,30},{19,31}} | collective-permute-start | bytes 196616 | tf_op jit(solution)/shard_map/ppermute | solution.py:22
  14.3 7.2 %collective-permute-start.5 = (bf16[768,128]{1,0:T(8,128)(2,1)S(1)}, bf16[768,128]{1,0:T(8,128)(2,1)S(1)}, u32[]{:S(2)}, u32[]{:S(2)}) collective-permute-start(bf16[768,128]{1,0:T(8,128)(2,1)S(1)} %pad_maximum_fusion), channel_id=1, source_target_pairs={{0,4},{2,6},{4,8},{6,10},{8,12},{10,14},{1,5},{3,7},{5,9},{7,11},{... | collective-permute-start | bytes 589832 | tf_op jit(solution)/shard_map/ppermute | solution.py:22
  17.2 5.2 %collective-permute-start.6 = (bf16[512,128]{1,0:T(8,128)(2,1)S(1)}, bf16[512,128]{1,0:T(8,128)(2,1)S(1)}, u32[]{:S(2)}, u32[]{:S(2)}) collective-permute-start(bf16[512,128]{1,0:T(8,128)(2,1)S(1)} %maximum_select_fusion), channel_id=1, source_target_pairs={{0,2},{2,0},{4,6},{6,4},{8,10},{10,8},{12,14},{14,12},{1,3},{3,1},... | collective-permute-start | bytes 393224 | tf_op jit(solution)/shard_map/ppermute | solution.py:22
  22.4 5.7 %collective-permute-start.7 = (bf16[768,128]{1,0:T(8,128)(2,1)S(1)}, bf16[768,128]{1,0:T(8,128)(2,1)S(1)}, u32[]{:S(2)}, u32[]{:S(2)}) collective-permute-start(bf16[768,128]{1,0:T(8,128)(2,1)S(1)} %pad_maximum_fusion.1), channel_id=1, source_target_pairs={{0,2},{2,0},{4,6},{6,4},{8,10},{10,8},{12,14},{14,12},{1,3},{3,1},... | collective-permute-start | bytes 589832 | tf_op jit(solution)/shard_map/ppermute | solution.py:22
  30.7 5.3 %collective-permute-start.8 = (bf16[512,128]{1,0:T(8,128)(2,1)S(1)}, bf16[512,128]{1,0:T(8,128)(2,1)S(1)}, u32[]{:S(2)}, u32[]{:S(2)}) collective-permute-start(bf16[512,128]{1,0:T(8,128)(2,1)S(1)} %get-tuple-element.88), channel_id=1, source_target_pairs={{0,2},{2,0},{4,6},{6,4},{8,10},{10,8},{12,14},{14,12},{1,3},{3,1},... | collective-permute-start | bytes 393224 | tf_op jit(solution)/shard_map/ppermute | solution.py:22
  33.2 9.2 %collective-permute-start.12 = (bf16[768,128]{1,0:T(8,128)(2,1)S(1)}, bf16[768,128]{1,0:T(8,128)(2,1)S(1)}, u32[]{:S(2)}, u32[]{:S(2)}) collective-permute-start(bf16[768,128]{1,0:T(8,128)(2,1)S(1)} %get-tuple-element.93), channel_id=1, source_target_pairs={{0,2},{2,0},{4,6},{6,4},{8,10},{10,8},{12,14},{14,12},{1,3},{3,1},... | collective-permute-start | bytes 589832 | tf_op jit(solution)/shard_map/ppermute | solution.py:22
  36.1 9.2 %collective-permute-start.11 = (bf16[512,128]{1,0:T(8,128)(2,1)S(1)}, bf16[512,128]{1,0:T(8,128)(2,1)S(1)}, u32[]{:S(2)}, u32[]{:S(2)}) collective-permute-start(bf16[512,128]{1,0:T(8,128)(2,1)S(1)} %add_convert_fusion.1), channel_id=1, source_target_pairs={{4,0},{6,2},{5,1},{7,3},{20,16},{22,18},{21,17},{23,19}} | collective-permute-start | bytes 393224 | tf_op jit(solution)/shard_map/ppermute | solution.py:22
  37.4 9.1 %collective-permute-start.10 = (bf16[512,128]{1,0:T(8,128)(2,1)S(1)}, bf16[512,128]{1,0:T(8,128)(2,1)S(1)}, u32[]{:S(2)}, u32[]{:S(2)}) collective-permute-start(bf16[512,128]{1,0:T(8,128)(2,1)S(1)} %add_convert_fusion.1), channel_id=1, source_target_pairs={{8,0},{10,2},{9,1},{11,3},{24,16},{26,18},{25,17},{27,19}} | collective-permute-start | bytes 393224 | tf_op jit(solution)/shard_map/ppermute | solution.py:22
  38.7 9.4 %collective-permute-start.9 = (bf16[512,128]{1,0:T(8,128)(2,1)S(1)}, bf16[512,128]{1,0:T(8,128)(2,1)S(1)}, u32[]{:S(2)}, u32[]{:S(2)}) collective-permute-start(bf16[512,128]{1,0:T(8,128)(2,1)S(1)} %add_convert_fusion.1), channel_id=1, source_target_pairs={{12,0},{14,2},{13,1},{15,3},{28,16},{30,18},{29,17},{31,19}} | collective-permute-start | bytes 393224 | tf_op jit(solution)/shard_map/ppermute | solution.py:22
  42.4 7.0 %collective-permute-start.14 = (bf16[256,128]{1,0:T(8,128)(2,1)S(1)}, bf16[256,128]{1,0:T(8,128)(2,1)S(1)}, u32[]{:S(2)}, u32[]{:S(2)}) collective-permute-start(bf16[256,128]{1,0:T(8,128)(2,1)S(1)} %get-tuple-element.95), channel_id=1, source_target_pairs={{10,2},{12,4},{14,6},{11,3},{13,5},{15,7},{26,18},{28,20},{30,22},... | collective-permute-start | bytes 196616 | tf_op jit(solution)/shard_map/ppermute | solution.py:22
  43.1 6.4 %collective-permute-start.13 = (bf16[256,128]{1,0:T(8,128)(2,1)S(1)}, bf16[256,128]{1,0:T(8,128)(2,1)S(1)}, u32[]{:S(2)}, u32[]{:S(2)}) collective-permute-start(bf16[256,128]{1,0:T(8,128)(2,1)S(1)} %get-tuple-element.99), channel_id=1, source_target_pairs={{6,2},{8,4},{10,6},{12,8},{14,10},{7,3},{9,5},{11,7},{13,9},{15,11... | collective-permute-start | bytes 196616 | tf_op jit(solution)/shard_map/ppermute | solution.py:22
  45.3 4.2 %collective-permute-start.15 = (bf16[256,128]{1,0:T(8,128)(2,1)S(1)}, bf16[256,128]{1,0:T(8,128)(2,1)S(1)}, u32[]{:S(2)}, u32[]{:S(2)}) collective-permute-start(bf16[256,128]{1,0:T(8,128)(2,1)S(1)} %get-tuple-element.100), channel_id=1, source_target_pairs={{14,2},{15,3},{30,18},{31,19}} | collective-permute-start | bytes 196616 | tf_op jit(solution)/shard_map/ppermute | solution.py:22
  48.1 6.9 %collective-permute-start.16 = (bf16[512,128]{1,0:T(8,128)(2,1)S(1)}, bf16[512,128]{1,0:T(8,128)(2,1)S(1)}, u32[]{:S(2)}, u32[]{:S(2)}) collective-permute-start(bf16[512,128]{1,0:T(8,128)(2,1)S(1)} %get-tuple-element.98), channel_id=1, source_target_pairs={{2,0},{3,1},{18,16},{19,17}} | collective-permute-start | bytes 393224 | tf_op jit(solution)/shard_map/ppermute | solution.py:22
  55.0 0.7 %copy-start = (f32[512,128]{1,0:T(8,128)}, f32[512,128]{1,0:T(8,128)S(1)}, u32[]{:S(2)}) copy-start(f32[512,128]{1,0:T(8,128)S(1)} %get-tuple-element.104) | copy-start | bytes 786436
  55.1 0.8 %copy-start.1 = (f32[512,128]{1,0:T(8,128)}, f32[512,128]{1,0:T(8,128)S(1)}, u32[]{:S(2)}) copy-start(f32[512,128]{1,0:T(8,128)S(1)} %get-tuple-element.105) | copy-start | bytes 786436

commit v18 on v17

--- a/solution.py
+++ b/solution.py
@@ -475,14 +475,16 @@
         finished = finish(total)
         near, first, last = units(permuted(behind[0], neighbours), 0, unit, 3)
         none = jnp.zeros_like(first)
-        parts = [permuted(total, [(j, 0), (j + 1, 1)]) for j in reversed(range(2, size, 2))]
+        parts = [permuted(total, [(j, 0), (j + 1, 1)]) for j in (4, 2)]
+        keys_last, values_last = permuted(total, [(6, 0)]), permuted(total, [(7, 0)])
         two = permuted(added(two, near).astype(BF16), back(shift_route(2, size)[1:]))
         four = after(added(four, jnp.where(even, last, first)).astype(BF16), finished[1])
         four = permuted(four, far_route)
         six = permuted(added(six, jnp.where(even, none, last)).astype(BF16), [(7, 1)])
         total = added(total, *parts).astype(BF16)
         mine = added(jnp.where(even, first, none), two, four, six)
-        return finished, total, permuted(total, [(1, 0)]).astype(F32), mine
+        values_next = permuted(total, [(1, 0)])
+        return finished, added(total, keys_last), added(values_next, values_last), mine
     strides = [2**i for i in range(2, size.bit_length()) if 2**i < size]
     top = strides[-1]
     zero, *third = units(permuted(behind[0], back(shift_route(1, size))), 0, unit, 4)

time: 56.2 us -> 58.3 us (1.037)
  starting transfers between devices: 24.6 us -> 25.9 us
  waiting for transfers between devices: 18.3 us -> 19.1 us
    ppermute x17 -> x18, starting transfers between devices: 24.6 us -> 25.9 us  [permuted(): return lax.ppermute(block, 'node', route)]
    ppermute x17 -> x18, waiting for transfers between devices: 18.3 us -> 19.1 us  [permuted(): return lax.ppermute(block, 'node', route)]
  transfers between devices with their start and end apart: 17 -> 18, of which waited for: 11 -> 10; matrix products, arithmetic and copies ran while one was open for 1% -> 1% of each run, Pallas kernels for 15% -> 14%
where the time goes in v18:
time: 58.3 us; the launch traced here: 57.9 us
  starting transfers between devices  25.9 us (44%)
  waiting for transfers between devices  19.1 us (33%)
  Pallas kernels  10.8 us (19%)
  between operations  0.93 us (2%)
  local copies, waits for them, and re-layouts  0.78 us (1%)
    ppermute x18, starting transfers between devices, permuted(): return lax.ppermute(block, 'node', route)  25.9 us
    ppermute x18, waiting for transfers between devices, permuted(): return lax.ppermute(block, 'node', route)  19.1 us
    pallas_call x6, Pallas kernels, call(): pl.pallas_call(kernel, in_specs=[place] * len(operands), out_specs=[VMEM]...  10.8 us
  transfers between devices with their start and end apart: 18, of which 10 were waited for; matrix products, arithmetic and copies ran while one was open for 1% of the time, Pallas kernels for 14%

profile of v18, /device:TPU:0, one launch (start us, length us, event | category | flops | bytes accessed | tf_op | source)
XLA Modules:
  0.0 57.9 jit_solution(10243794904006710908)
XLA Ops:
  0.6 5.9 %collective-permute-start = (bf16[512,128]{1,0:T(8,128)(2,1)}, bf16[512,128]{1,0:T(8,128)(2,1)S(1)}, u32[]{:S(2)}, u32[]{:S(2)}) collective-permute-start(bf16[512,128]{1,0:T(8,128)(2,1)} %bitcast.6), channel_id=1, source_target_pairs={{0,8},{1,9},{16,24},{17,25}} | collective-permute-start | bytes 393224 | tf_op jit(solution)/shard_map/ppermute | solution.py:22
  6.6 1.6 %collective-permute-start.2 = (bf16[512,128]{1,0:T(8,128)(2,1)}, bf16[512,128]{1,0:T(8,128)(2,1)S(1)}, u32[]{:S(2)}, u32[]{:S(2)}) collective-permute-start(bf16[512,128]{1,0:T(8,128)(2,1)} %bitcast.8), channel_id=1, source_target_pairs={{0,10},{1,11},{16,26},{17,27}} | collective-permute-start | bytes 393224 | tf_op jit(solution)/shard_map/ppermute | solution.py:22
  8.2 1.3 %collective-permute-start.1 = (bf16[512,128]{1,0:T(8,128)(2,1)}, bf16[512,128]{1,0:T(8,128)(2,1)S(1)}, u32[]{:S(2)}, u32[]{:S(2)}) collective-permute-start(bf16[512,128]{1,0:T(8,128)(2,1)} %bitcast.9), channel_id=1, source_target_pairs={{0,2},{1,3},{16,18},{17,19}} | collective-permute-start | bytes 393224 | tf_op jit(solution)/shard_map/ppermute | solution.py:22
  9.5 1.2 %load.1 = (bf16[256,128]{1,0:T(8,128)(2,1)S(1)}, bf16[512,128]{1,0:T(8,128)(2,1)S(1)}, bf16[4,128,128]{2,1,0:T(8,128)(2,1)S(1)}, bf16[4,128,128]{2,1,0:T(8,128)(...) custom-call(s32[64]{0:T(128)} %refs_0_.1, s32[64]{0:T(128)} %refs_1_.1, bf16[512,128]{1,0:T(8,128)(2,1)} %bitcast.7, ...), custom_call_target="tpu_custom_call" | custom-call | flops 1048576 | bytes 983552 | tf_op jit(solution)/shard_map/load/pallas_call | solution.py:265
  10.7 0.1 collective-permute-done
  10.8 0.7 %collective-permute-start.4 = (bf16[256,128]{1,0:T(8,128)(2,1)S(1)}, bf16[256,128]{1,0:T(8,128)(2,1)S(1)}, u32[]{:S(2)}, u32[]{:S(2)}) collective-permute-start(bf16[256,128]{1,0:T(8,128)(2,1)S(1)} %get-tuple-element.70), channel_id=1, source_target_pairs={{2,10},{4,12},{6,14},{3,11},{5,13},{7,15},{18,26},{20,28},{22,30},... | collective-permute-start | bytes 196616 | tf_op jit(solution)/shard_map/ppermute | solution.py:22
  11.4 0.7 %collective-permute-start.3 = (bf16[256,128]{1,0:T(8,128)(2,1)S(1)}, bf16[256,128]{1,0:T(8,128)(2,1)S(1)}, u32[]{:S(2)}, u32[]{:S(2)}) collective-permute-start(bf16[256,128]{1,0:T(8,128)(2,1)S(1)} %get-tuple-element.70), channel_id=1, source_target_pairs={{2,14},{3,15},{18,30},{19,31}} | collective-permute-start | bytes 196616 | tf_op jit(solution)/shard_map/ppermute | solution.py:22
  12.1 0.4 collective-permute-done.2
  12.5 0.1 collective-permute-done.1
  12.5 0.1 add_convert_fusion.2
  12.6 1.6 %pack.1 = (bf16[4,1024,128]{2,1,0:T(8,128)(2,1)S(1)}, bf16[4,1024,128]{2,1,0:T(8,128)(2,1)S(1)}) custom-call(bf16[128,32,128]{2,1,0:T(8,128)(2,1)} %q_ref, bf16[128,32,128]{2,1,0:T(8,128)(2,1)} %g_ref.1), custom_call_target="tpu_custom_call" | custom-call | flops 1048576 | bytes 4194304 | tf_op jit(solution)/shard_map/pack/pallas_call | solution.py:265
  14.3 0.0 collective-permute-done.4.refs_7_
  14.3 0.0 collective-permute-done.3.refs_8_
  14.3 2.8 %collective-permute-start.5 = (bf16[768,128]{1,0:T(8,128)(2,1)S(1)}, bf16[768,128]{1,0:T(8,128)(2,1)S(1)}, u32[]{:S(2)}, u32[]{:S(2)}) collective-permute-start(bf16[768,128]{1,0:T(8,128)(2,1)S(1)} %pad_maximum_fusion), channel_id=1, source_target_pairs={{0,4},{2,6},{4,8},{6,10},{8,12},{10,14},{1,5},{3,7},{5,9},{7,11},{... | collective-permute-start | bytes 589832 | tf_op jit(solution)/shard_map/ppermute | solution.py:22
  17.2 1.3 %collective-permute-start.6 = (bf16[512,128]{1,0:T(8,128)(2,1)S(1)}, bf16[512,128]{1,0:T(8,128)(2,1)S(1)}, u32[]{:S(2)}, u32[]{:S(2)}) collective-permute-start(bf16[512,128]{1,0:T(8,128)(2,1)S(1)} %maximum_select_fusion), channel_id=1, source_target_pairs={{0,2},{2,0},{4,6},{6,4},{8,10},{10,8},{12,14},{14,12},{1,3},{3,1},... | collective-permute-start | bytes 393224 | tf_op jit(solution)/shard_map/ppermute | solution.py:22
  18.4 3.0 %collective-permute-done.5.refs_5_ = bf16[768,128]{1,0:T(8,128)(2,1)S(1)} collective-permute-done((bf16[768,128]{1,0:T(8,128)(2,1)S(1)}, bf16[768,128]{1,0:T(8,128)(2,1)S(1)}, u32[]{:S(2)}, u32[]{:S(2)}) %collective-permute-start.5) | collective-permute-done | bytes 196640 | tf_op jit(solution)/shard_map/ppermute | solution.py:22
  21.5 0.9 %collective-permute-done.6.refs_6_ = bf16[512,128]{1,0:T(8,128)(2,1)S(1)} collective-permute-done((bf16[512,128]{1,0:T(8,128)(2,1)S(1)}, bf16[512,128]{1,0:T(8,128)(2,1)S(1)}, u32[]{:S(2)}, u32[]{:S(2)}) %collective-permute-start.6) | collective-permute-done | bytes 131104 | tf_op jit(solution)/shard_map/ppermute | solution.py:22
  22.4 1.0 %collective-permute-start.7 = (bf16[768,128]{1,0:T(8,128)(2,1)S(1)}, bf16[768,128]{1,0:T(8,128)(2,1)S(1)}, u32[]{:S(2)}, u32[]{:S(2)}) collective-permute-start(bf16[768,128]{1,0:T(8,128)(2,1)S(1)} %pad_maximum_fusion.1), channel_id=1, source_target_pairs={{0,2},{2,0},{4,6},{6,4},{8,10},{10,8},{12,14},{14,12},{1,3},{3,1},... | collective-permute-start | bytes 589832 | tf_op jit(solution)/shard_map/ppermute | solution.py:22
  23.4 1.6 %early.1 = (bf16[4,288,128]{2,1,0:T(8,128)(2,1)S(1)}, f32[4,288,1024]{2,1,0:T(8,128)S(1)}, f32[4,288,1024]{2,1,0:T(8,128)S(1)}, f32[4,8,1024]{2,1,0:T(8,128)S(1)}) custom-call(bf16[4,128,128]{2,1,0:T(8,128)(2,1)S(1)} %get-tuple-element.75.refs_0_, bf16[4,128,128]{2,1,0:T(8,128)(2,1)S(1)} %get-tuple-element.76.refs_1_, ...), custom_call_target="tpu_custom_call" | custom-call | flops 603979776 | bytes 12910592 | tf_op jit(solution)/shard_map/early/pallas_call | solution.py:265
  25.0 3.0 %collective-permute-done.7.refs_7_ = bf16[768,128]{1,0:T(8,128)(2,1)S(1)} collective-permute-done((bf16[768,128]{1,0:T(8,128)(2,1)S(1)}, bf16[768,128]{1,0:T(8,128)(2,1)S(1)}, u32[]{:S(2)}, u32[]{:S(2)}) %collective-permute-start.7) | collective-permute-done | bytes 196640 | tf_op jit(solution)/shard_map/ppermute | solution.py:22
  28.1 2.6 %probs.1 = (bf16[512,128]{1,0:T(8,128)(2,1)S(1)}, bf16[512,128]{1,0:T(8,128)(2,1)S(1)}, bf16[4,160,128]{2,1,0:T(8,128)(2,1)S(1)}, bf16[4,160,1024]{2,1,0:T(8,128...) custom-call(bf16[512,128]{1,0:T(8,128)(2,1)S(1)} %get-tuple-element.103.refs_0_, ...), custom_call_target="tpu_custom_call" | custom-call | flops 671088640 | bytes 5079040 | tf_op jit(solution)/shard_map/probs/pallas_call | solution.py:265
  30.7 1.1 %collective-permute-start.8 = (bf16[512,128]{1,0:T(8,128)(2,1)S(1)}, bf16[512,128]{1,0:T(8,128)(2,1)S(1)}, u32[]{:S(2)}, u32[]{:S(2)}) collective-permute-start(bf16[512,128]{1,0:T(8,128)(2,1)S(1)} %get-tuple-element.88), channel_id=1, source_target_pairs={{0,2},{2,0},{4,6},{6,4},{8,10},{10,8},{12,14},{14,12},{1,3},{3,1},... | collective-permute-start | bytes 393224 | tf_op jit(solution)/shard_map/ppermute | solution.py:22
  31.8 1.4 %windows.1 = (bf16[768,128]{1,0:T(8,128)(2,1)S(1)}, bf16[768,128]{1,0:T(8,128)(2,1)S(1)}, bf16[4,288,1024]{2,1,0:T(8,128)(2,1)S(1)}, bf16[4,128,1024]{2,1,0:T(8,128)(2,1)S(1)}) custom-call(bf16[4,1024,128]{2,1,0:T(8,128)(2,1)S(1)} %get-tuple-element.65.refs_2_.refs_0_, bf16[4,1024,128]{2,1,0:T(8,128)(2,1)S(1)} %get-tuple-element.66.refs_3_.refs_1_, ...), custom_call_target="tpu_custom_call" | custom-call | flops 402653184 | bytes 17039360 | tf_op jit(solution)/shard_map/windows/pallas_call | solution.py:265
  33.2 1.1 %collective-permute-start.12 = (bf16[768,128]{1,0:T(8,128)(2,1)S(1)}, bf16[768,128]{1,0:T(8,128)(2,1)S(1)}, u32[]{:S(2)}, u32[]{:S(2)}) collective-permute-start(bf16[768,128]{1,0:T(8,128)(2,1)S(1)} %get-tuple-element.93), channel_id=1, source_target_pairs={{0,2},{2,0},{4,6},{6,4},{8,10},{10,8},{12,14},{14,12},{1,3},{3,1},... | collective-permute-start | bytes 589832 | tf_op jit(solution)/shard_map/ppermute | solution.py:22
  34.2 1.8 %collective-permute-done.8 = bf16[512,128]{1,0:T(8,128)(2,1)S(1)} collective-permute-done((bf16[512,128]{1,0:T(8,128)(2,1)S(1)}, bf16[512,128]{1,0:T(8,128)(2,1)S(1)}, u32[]{:S(2)}, u32[]{:S(2)}) %collective-permute-start.8) | collective-permute-done | bytes 131104 | tf_op jit(solution)/shard_map/ppermute | solution.py:22
  36.1 1.3 %collective-permute-start.17 = (bf16[512,128]{1,0:T(8,128)(2,1)S(1)}, bf16[512,128]{1,0:T(8,128)(2,1)S(1)}, u32[]{:S(2)}, u32[]{:S(2)}) collective-permute-start(bf16[512,128]{1,0:T(8,128)(2,1)S(1)} %add_convert_fusion.1), channel_id=1, source_target_pairs={{14,0},{15,1},{30,16},{31,17}} | collective-permute-start | bytes 393224 | tf_op jit(solution)/shard_map/ppermute | solution.py:22
  37.4 1.3 %collective-permute-start.11 = (bf16[512,128]{1,0:T(8,128)(2,1)S(1)}, bf16[512,128]{1,0:T(8,128)(2,1)S(1)}, u32[]{:S(2)}, u32[]{:S(2)}) collective-permute-start(bf16[512,128]{1,0:T(8,128)(2,1)S(1)} %add_convert_fusion.1), channel_id=1, source_target_pairs={{12,0},{13,1},{28,16},{29,17}} | collective-permute-start | bytes 393224 | tf_op jit(solution)/shard_map/ppermute | solution.py:22
  38.7 1.3 %collective-permute-start.10 = (bf16[512,128]{1,0:T(8,128)(2,1)S(1)}, bf16[512,128]{1,0:T(8,128)(2,1)S(1)}, u32[]{:S(2)}, u32[]{:S(2)}) collective-permute-start(bf16[512,128]{1,0:T(8,128)(2,1)S(1)} %add_convert_fusion.1), channel_id=1, source_target_pairs={{4,0},{6,2},{5,1},{7,3},{20,16},{22,18},{21,17},{23,19}} | collective-permute-start | bytes 393224 | tf_op jit(solution)/shard_map/ppermute | solution.py:22
  40.0 1.3 %collective-permute-start.9 = (bf16[512,128]{1,0:T(8,128)(2,1)S(1)}, bf16[512,128]{1,0:T(8,128)(2,1)S(1)}, u32[]{:S(2)}, u32[]{:S(2)}) collective-permute-start(bf16[512,128]{1,0:T(8,128)(2,1)S(1)} %add_convert_fusion.1), channel_id=1, source_target_pairs={{8,0},{10,2},{9,1},{11,3},{24,16},{26,18},{25,17},{27,19}} | collective-permute-start | bytes 393224 | tf_op jit(solution)/shard_map/ppermute | solution.py:22
  41.3 2.4 %grads.1 = (bf16[128,32,128]{2,1,0:T(8,128)(2,1)}, f32[512,128]{1,0:T(8,128)S(1)}, f32[512,128]{1,0:T(8,128)S(1)}) custom-call(bf16[4,1024,128]{2,1,0:T(8,128)(2,1)S(1)} %get-tuple-element.65.refs_2_.refs_0_, bf16[4,1024,128]{2,1,0:T(8,128)(2,1)S(1)} %get-tuple-element.66.refs_3_.refs_1_, bf16[4,160,128]{2,1,0:T(8,128)(2,1)S(1)} %get-tuple-element.78.refs_2_, ...), custom_call_target="tpu_custom_call" | custom-call | flops 469762048 | bytes 8847360 | tf_op jit(solution)/shard_map/grads/pallas_call | solution.py:265
  43.6 0.0 collective-permute-done.12
  43.6 0.1 add_convert_fusion.5
  43.7 0.7 %collective-permute-start.14 = (bf16[256,128]{1,0:T(8,128)(2,1)S(1)}, bf16[256,128]{1,0:T(8,128)(2,1)S(1)}, u32[]{:S(2)}, u32[]{:S(2)}) collective-permute-start(bf16[256,128]{1,0:T(8,128)(2,1)S(1)} %get-tuple-element.95), channel_id=1, source_target_pairs={{10,2},{12,4},{14,6},{11,3},{13,5},{15,7},{26,18},{28,20},{30,22},... | collective-permute-start | bytes 196616 | tf_op jit(solution)/shard_map/ppermute | solution.py:22
  44.4 2.0 %collective-permute-done.11 = bf16[512,128]{1,0:T(8,128)(2,1)S(1)} collective-permute-done((bf16[512,128]{1,0:T(8,128)(2,1)S(1)}, bf16[512,128]{1,0:T(8,128)(2,1)S(1)}, u32[]{:S(2)}, u32[]{:S(2)}) %collective-permute-start.11) | collective-permute-done | bytes 131104 | tf_op jit(solution)/shard_map/ppermute | solution.py:22
  46.4 0.7 %collective-permute-start.13 = (bf16[256,128]{1,0:T(8,128)(2,1)S(1)}, bf16[256,128]{1,0:T(8,128)(2,1)S(1)}, u32[]{:S(2)}, u32[]{:S(2)}) collective-permute-start(bf16[256,128]{1,0:T(8,128)(2,1)S(1)} %get-tuple-element.99), channel_id=1, source_target_pairs={{6,2},{8,4},{10,6},{12,8},{14,10},{7,3},{9,5},{11,7},{13,9},{15,11... | collective-permute-start | bytes 196616 | tf_op jit(solution)/shard_map/ppermute | solution.py:22
  47.1 0.0 collective-permute-done.10
  47.1 0.7 %collective-permute-start.15 = (bf16[256,128]{1,0:T(8,128)(2,1)S(1)}, bf16[256,128]{1,0:T(8,128)(2,1)S(1)}, u32[]{:S(2)}, u32[]{:S(2)}) collective-permute-start(bf16[256,128]{1,0:T(8,128)(2,1)S(1)} %get-tuple-element.100), channel_id=1, source_target_pairs={{14,2},{15,3},{30,18},{31,19}} | collective-permute-start | bytes 196616 | tf_op jit(solution)/shard_map/ppermute | solution.py:22
  47.8 1.4 %collective-permute-done.9 = bf16[512,128]{1,0:T(8,128)(2,1)S(1)} collective-permute-done((bf16[512,128]{1,0:T(8,128)(2,1)S(1)}, bf16[512,128]{1,0:T(8,128)(2,1)S(1)}, u32[]{:S(2)}, u32[]{:S(2)}) %collective-permute-start.9) | collective-permute-done | bytes 131104 | tf_op jit(solution)/shard_map/ppermute | solution.py:22
  49.2 0.1 select_add_fusion.1
  49.3 1.3 %collective-permute-start.16 = (bf16[512,128]{1,0:T(8,128)(2,1)S(1)}, bf16[512,128]{1,0:T(8,128)(2,1)S(1)}, u32[]{:S(2)}, u32[]{:S(2)}) collective-permute-start(bf16[512,128]{1,0:T(8,128)(2,1)S(1)} %get-tuple-element.98), channel_id=1, source_target_pairs={{2,0},{3,1},{18,16},{19,17}} | collective-permute-start | bytes 393224 | tf_op jit(solution)/shard_map/ppermute | solution.py:22
  50.6 0.0 collective-permute-done.13
  50.6 0.0 collective-permute-done.15
  50.6 0.0 collective-permute-done.17
  50.6 6.4 %collective-permute-done.16 = bf16[512,128]{1,0:T(8,128)(2,1)S(1)} collective-permute-done((bf16[512,128]{1,0:T(8,128)(2,1)S(1)}, bf16[512,128]{1,0:T(8,128)(2,1)S(1)}, u32[]{:S(2)}, u32[]{:S(2)}) %collective-permute-start.16) | collective-permute-done | bytes 131104 | tf_op jit(solution)/shard_map/ppermute | solution.py:22
  57.1 0.0 copy-start
  57.1 0.0 copy-start.1
  57.1 0.7 %copy-done = f32[512,128]{1,0:T(8,128)} copy-done((f32[512,128]{1,0:T(8,128)}, f32[512,128]{1,0:T(8,128)S(1)}, u32[]{:S(2)}) %copy-start) | copy-done | bytes 262168
  57.8 0.1 copy-done.1
  (11 shorter events, 0.3 us)
Async XLA Ops:
  0.6 10.1 %collective-permute-start = (bf16[512,128]{1,0:T(8,128)(2,1)}, bf16[512,128]{1,0:T(8,128)(2,1)S(1)}, u32[]{:S(2)}, u32[]{:S(2)}) collective-permute-start(bf16[512,128]{1,0:T(8,128)(2,1)} %bitcast.6), channel_id=1, source_target_pairs={{0,8},{1,9},{16,24},{17,25}} | collective-permute-start | bytes 393224 | tf_op jit(solution)/shard_map/ppermute | solution.py:22
  6.6 5.9 %collective-permute-start.2 = (bf16[512,128]{1,0:T(8,128)(2,1)}, bf16[512,128]{1,0:T(8,128)(2,1)S(1)}, u32[]{:S(2)}, u32[]{:S(2)}) collective-permute-start(bf16[512,128]{1,0:T(8,128)(2,1)} %bitcast.8), channel_id=1, source_target_pairs={{0,10},{1,11},{16,26},{17,27}} | collective-permute-start | bytes 393224 | tf_op jit(solution)/shard_map/ppermute | solution.py:22
  8.2 4.4 %collective-permute-start.1 = (bf16[512,128]{1,0:T(8,128)(2,1)}, bf16[512,128]{1,0:T(8,128)(2,1)S(1)}, u32[]{:S(2)}, u32[]{:S(2)}) collective-permute-start(bf16[512,128]{1,0:T(8,128)(2,1)} %bitcast.9), channel_id=1, source_target_pairs={{0,2},{1,3},{16,18},{17,19}} | collective-permute-start | bytes 393224 | tf_op jit(solution)/shard_map/ppermute | solution.py:22
  10.8 3.5 %collective-permute-start.4 = (bf16[256,128]{1,0:T(8,128)(2,1)S(1)}, bf16[256,128]{1,0:T(8,128)(2,1)S(1)}, u32[]{:S(2)}, u32[]{:S(2)}) collective-permute-start(bf16[256,128]{1,0:T(8,128)(2,1)S(1)} %get-tuple-element.70), channel_id=1, source_target_pairs={{2,10},{4,12},{6,14},{3,11},{5,13},{7,15},{18,26},{20,28},{22,30},... | collective-permute-start | bytes 196616 | tf_op jit(solution)/shard_map/ppermute | solution.py:22
  11.4 2.8 %collective-permute-start.3 = (bf16[256,128]{1,0:T(8,128)(2,1)S(1)}, bf16[256,128]{1,0:T(8,128)(2,1)S(1)}, u32[]{:S(2)}, u32[]{:S(2)}) collective-permute-start(bf16[256,128]{1,0:T(8,128)(2,1)S(1)} %get-tuple-element.70), channel_id=1, source_target_pairs={{2,14},{3,15},{18,30},{19,31}} | collective-permute-start | bytes 196616 | tf_op jit(solution)/shard_map/ppermute | solution.py:22
  14.3 7.2 %collective-permute-start.5 = (bf16[768,128]{1,0:T(8,128)(2,1)S(1)}, bf16[768,128]{1,0:T(8,128)(2,1)S(1)}, u32[]{:S(2)}, u32[]{:S(2)}) collective-permute-start(bf16[768,128]{1,0:T(8,128)(2,1)S(1)} %pad_maximum_fusion), channel_id=1, source_target_pairs={{0,4},{2,6},{4,8},{6,10},{8,12},{10,14},{1,5},{3,7},{5,9},{7,11},{... | collective-permute-start | bytes 589832 | tf_op jit(solution)/shard_map/ppermute | solution.py:22
  17.2 5.2 %collective-permute-start.6 = (bf16[512,128]{1,0:T(8,128)(2,1)S(1)}, bf16[512,128]{1,0:T(8,128)(2,1)S(1)}, u32[]{:S(2)}, u32[]{:S(2)}) collective-permute-start(bf16[512,128]{1,0:T(8,128)(2,1)S(1)} %maximum_select_fusion), channel_id=1, source_target_pairs={{0,2},{2,0},{4,6},{6,4},{8,10},{10,8},{12,14},{14,12},{1,3},{3,1},... | collective-permute-start | bytes 393224 | tf_op jit(solution)/shard_map/ppermute | solution.py:22
  22.4 5.7 %collective-permute-start.7 = (bf16[768,128]{1,0:T(8,128)(2,1)S(1)}, bf16[768,128]{1,0:T(8,128)(2,1)S(1)}, u32[]{:S(2)}, u32[]{:S(2)}) collective-permute-start(bf16[768,128]{1,0:T(8,128)(2,1)S(1)} %pad_maximum_fusion.1), channel_id=1, source_target_pairs={{0,2},{2,0},{4,6},{6,4},{8,10},{10,8},{12,14},{14,12},{1,3},{3,1},... | collective-permute-start | bytes 589832 | tf_op jit(solution)/shard_map/ppermute | solution.py:22
  30.7 5.3 %collective-permute-start.8 = (bf16[512,128]{1,0:T(8,128)(2,1)S(1)}, bf16[512,128]{1,0:T(8,128)(2,1)S(1)}, u32[]{:S(2)}, u32[]{:S(2)}) collective-permute-start(bf16[512,128]{1,0:T(8,128)(2,1)S(1)} %get-tuple-element.88), channel_id=1, source_target_pairs={{0,2},{2,0},{4,6},{6,4},{8,10},{10,8},{12,14},{14,12},{1,3},{3,1},... | collective-permute-start | bytes 393224 | tf_op jit(solution)/shard_map/ppermute | solution.py:22
  33.2 10.5 %collective-permute-start.12 = (bf16[768,128]{1,0:T(8,128)(2,1)S(1)}, bf16[768,128]{1,0:T(8,128)(2,1)S(1)}, u32[]{:S(2)}, u32[]{:S(2)}) collective-permute-start(bf16[768,128]{1,0:T(8,128)(2,1)S(1)} %get-tuple-element.93), channel_id=1, source_target_pairs={{0,2},{2,0},{4,6},{6,4},{8,10},{10,8},{12,14},{14,12},{1,3},{3,1},... | collective-permute-start | bytes 589832 | tf_op jit(solution)/shard_map/ppermute | solution.py:22
  36.1 14.6 %collective-permute-start.17 = (bf16[512,128]{1,0:T(8,128)(2,1)S(1)}, bf16[512,128]{1,0:T(8,128)(2,1)S(1)}, u32[]{:S(2)}, u32[]{:S(2)}) collective-permute-start(bf16[512,128]{1,0:T(8,128)(2,1)S(1)} %add_convert_fusion.1), channel_id=1, source_target_pairs={{14,0},{15,1},{30,16},{31,17}} | collective-permute-start | bytes 393224 | tf_op jit(solution)/shard_map/ppermute | solution.py:22
  37.4 9.1 %collective-permute-start.11 = (bf16[512,128]{1,0:T(8,128)(2,1)S(1)}, bf16[512,128]{1,0:T(8,128)(2,1)S(1)}, u32[]{:S(2)}, u32[]{:S(2)}) collective-permute-start(bf16[512,128]{1,0:T(8,128)(2,1)S(1)} %add_convert_fusion.1), channel_id=1, source_target_pairs={{12,0},{13,1},{28,16},{29,17}} | collective-permute-start | bytes 393224 | tf_op jit(solution)/shard_map/ppermute | solution.py:22
  38.7 8.4 %collective-permute-start.10 = (bf16[512,128]{1,0:T(8,128)(2,1)S(1)}, bf16[512,128]{1,0:T(8,128)(2,1)S(1)}, u32[]{:S(2)}, u32[]{:S(2)}) collective-permute-start(bf16[512,128]{1,0:T(8,128)(2,1)S(1)} %add_convert_fusion.1), channel_id=1, source_target_pairs={{4,0},{6,2},{5,1},{7,3},{20,16},{22,18},{21,17},{23,19}} | collective-permute-start | bytes 393224 | tf_op jit(solution)/shard_map/ppermute | solution.py:22
  40.0 9.2 %collective-permute-start.9 = (bf16[512,128]{1,0:T(8,128)(2,1)S(1)}, bf16[512,128]{1,0:T(8,128)(2,1)S(1)}, u32[]{:S(2)}, u32[]{:S(2)}) collective-permute-start(bf16[512,128]{1,0:T(8,128)(2,1)S(1)} %add_convert_fusion.1), channel_id=1, source_target_pairs={{8,0},{10,2},{9,1},{11,3},{24,16},{26,18},{25,17},{27,19}} | collective-permute-start | bytes 393224 | tf_op jit(solution)/shard_map/ppermute | solution.py:22
  43.7 6.9 %collective-permute-start.14 = (bf16[256,128]{1,0:T(8,128)(2,1)S(1)}, bf16[256,128]{1,0:T(8,128)(2,1)S(1)}, u32[]{:S(2)}, u32[]{:S(2)}) collective-permute-start(bf16[256,128]{1,0:T(8,128)(2,1)S(1)} %get-tuple-element.95), channel_id=1, source_target_pairs={{10,2},{12,4},{14,6},{11,3},{13,5},{15,7},{26,18},{28,20},{30,22},... | collective-permute-start | bytes 196616 | tf_op jit(solution)/shard_map/ppermute | solution.py:22
  46.4 4.2 %collective-permute-start.13 = (bf16[256,128]{1,0:T(8,128)(2,1)S(1)}, bf16[256,128]{1,0:T(8,128)(2,1)S(1)}, u32[]{:S(2)}, u32[]{:S(2)}) collective-permute-start(bf16[256,128]{1,0:T(8,128)(2,1)S(1)} %get-tuple-element.99), channel_id=1, source_target_pairs={{6,2},{8,4},{10,6},{12,8},{14,10},{7,3},{9,5},{11,7},{13,9},{15,11... | collective-permute-start | bytes 196616 | tf_op jit(solution)/shard_map/ppermute | solution.py:22
  47.1 3.5 %collective-permute-start.15 = (bf16[256,128]{1,0:T(8,128)(2,1)S(1)}, bf16[256,128]{1,0:T(8,128)(2,1)S(1)}, u32[]{:S(2)}, u32[]{:S(2)}) collective-permute-start(bf16[256,128]{1,0:T(8,128)(2,1)S(1)} %get-tuple-element.100), channel_id=1, source_target_pairs={{14,2},{15,3},{30,18},{31,19}} | collective-permute-start | bytes 196616 | tf_op jit(solution)/shard_map/ppermute | solution.py:22
  49.3 7.8 %collective-permute-start.16 = (bf16[512,128]{1,0:T(8,128)(2,1)S(1)}, bf16[512,128]{1,0:T(8,128)(2,1)S(1)}, u32[]{:S(2)}, u32[]{:S(2)}) collective-permute-start(bf16[512,128]{1,0:T(8,128)(2,1)S(1)} %get-tuple-element.98), channel_id=1, source_target_pairs={{2,0},{3,1},{18,16},{19,17}} | collective-permute-start | bytes 393224 | tf_op jit(solution)/shard_map/ppermute | solution.py:22
  57.1 0.7 %copy-start = (f32[512,128]{1,0:T(8,128)}, f32[512,128]{1,0:T(8,128)S(1)}, u32[]{:S(2)}) copy-start(f32[512,128]{1,0:T(8,128)S(1)} %get-tuple-element.105) | copy-start | bytes 786436
  57.1 0.8 %copy-start.1 = (f32[512,128]{1,0:T(8,128)}, f32[512,128]{1,0:T(8,128)S(1)}, u32[]{:S(2)}) copy-start(f32[512,128]{1,0:T(8,128)S(1)} %get-tuple-element.104) | copy-start | bytes 786436

commit v19 on v17

--- a/solution.py
+++ b/solution.py
@@ -436,7 +436,7 @@
         qh, gh = pack(queries, grad_out, keys.shape[0] // queries.shape[0])
         far = permuted(head, far_route)
         six = permuted(head, [(1, 7)])
-        held = after(added(held, values_next, values_far, keys_far).astype(BF16), six, far, qh)
+        held = after(added(held, values_next, values_far, keys_far).astype(BF16), six, far)
         second = permuted(jnp.concatenate([held, head]), near_route)
         crossed = jnp.where(even, jnp.concatenate([head, far]), jnp.concatenate([far, six]))
         crossed = permuted(crossed, neighbours)

time: 56.2 us -> 56.4 us (level)
  starting transfers between devices: 24.6 us -> 26.2 us
  waiting for transfers between devices: 18.3 us -> 16.9 us
    ppermute x17, starting transfers between devices: 24.6 us -> 26.2 us  [permuted(): return lax.ppermute(block, 'node', route)]
    ppermute x17, waiting for transfers between devices: 18.3 us -> 16.9 us  [permuted(): return lax.ppermute(block, 'node', route)]
  transfers between devices with their start and end apart: 17 -> 17, of which waited for: 11 -> 10; matrix products, arithmetic and copies ran while one was open for 1% -> 1% of each run, Pallas kernels for 15% -> 15%
where the time goes in v19:
time: 56.4 us; the launch traced here: 56.1 us
  starting transfers between devices  26.2 us (46%)
  waiting for transfers between devices  16.9 us (30%)
  Pallas kernels  10.8 us (19%)
  between operations  0.92 us (2%)
  local copies, waits for them, and re-layouts  0.78 us (1%)
    ppermute x17, starting transfers between devices, permuted(): return lax.ppermute(block, 'node', route)  26.2 us
    ppermute x17, waiting for transfers between devices, permuted(): return lax.ppermute(block, 'node', route)  16.9 us
    pallas_call x6, Pallas kernels, call(): pl.pallas_call(kernel, in_specs=[place] * len(operands), out_specs=[VMEM]...  10.8 us
  transfers between devices with their start and end apart: 17, of which 10 were waited for; matrix products, arithmetic and copies ran while one was open for 1% of the time, Pallas kernels for 15%

profile of v19, /device:TPU:0, one launch (start us, length us, event | category | flops | bytes accessed | tf_op | source)
XLA Modules:
  0.0 56.1 jit_solution(16592384738030082933)
XLA Ops:
  0.6 5.9 %collective-permute-start = (bf16[512,128]{1,0:T(8,128)(2,1)}, bf16[512,128]{1,0:T(8,128)(2,1)S(1)}, u32[]{:S(2)}, u32[]{:S(2)}) collective-permute-start(bf16[512,128]{1,0:T(8,128)(2,1)} %bitcast.6), channel_id=1, source_target_pairs={{0,8},{1,9},{16,24},{17,25}} | collective-permute-start | bytes 393224 | tf_op jit(solution)/shard_map/ppermute | solution.py:22
  6.6 1.6 %collective-permute-start.2 = (bf16[512,128]{1,0:T(8,128)(2,1)}, bf16[512,128]{1,0:T(8,128)(2,1)S(1)}, u32[]{:S(2)}, u32[]{:S(2)}) collective-permute-start(bf16[512,128]{1,0:T(8,128)(2,1)} %bitcast.8), channel_id=1, source_target_pairs={{0,10},{1,11},{16,26},{17,27}} | collective-permute-start | bytes 393224 | tf_op jit(solution)/shard_map/ppermute | solution.py:22
  8.2 1.3 %collective-permute-start.1 = (bf16[512,128]{1,0:T(8,128)(2,1)}, bf16[512,128]{1,0:T(8,128)(2,1)S(1)}, u32[]{:S(2)}, u32[]{:S(2)}) collective-permute-start(bf16[512,128]{1,0:T(8,128)(2,1)} %bitcast.9), channel_id=1, source_target_pairs={{0,2},{1,3},{16,18},{17,19}} | collective-permute-start | bytes 393224 | tf_op jit(solution)/shard_map/ppermute | solution.py:22
  9.5 1.2 %load.1 = (bf16[256,128]{1,0:T(8,128)(2,1)S(1)}, bf16[512,128]{1,0:T(8,128)(2,1)S(1)}, bf16[4,128,128]{2,1,0:T(8,128)(2,1)S(1)}, bf16[4,128,128]{2,1,0:T(8,128)(...) custom-call(s32[64]{0:T(128)} %refs_0_.1, s32[64]{0:T(128)} %refs_1_.1, bf16[512,128]{1,0:T(8,128)(2,1)} %bitcast.7, ...), custom_call_target="tpu_custom_call" | custom-call | flops 1048576 | bytes 983552 | tf_op jit(solution)/shard_map/load/pallas_call | solution.py:265
  10.7 0.1 collective-permute-done
  10.8 0.7 %collective-permute-start.4 = (bf16[256,128]{1,0:T(8,128)(2,1)S(1)}, bf16[256,128]{1,0:T(8,128)(2,1)S(1)}, u32[]{:S(2)}, u32[]{:S(2)}) collective-permute-start(bf16[256,128]{1,0:T(8,128)(2,1)S(1)} %get-tuple-element.70), channel_id=1, source_target_pairs={{2,10},{4,12},{6,14},{3,11},{5,13},{7,15},{18,26},{20,28},{22,30},... | collective-permute-start | bytes 196616 | tf_op jit(solution)/shard_map/ppermute | solution.py:22
  11.4 0.7 %collective-permute-start.3 = (bf16[256,128]{1,0:T(8,128)(2,1)S(1)}, bf16[256,128]{1,0:T(8,128)(2,1)S(1)}, u32[]{:S(2)}, u32[]{:S(2)}) collective-permute-start(bf16[256,128]{1,0:T(8,128)(2,1)S(1)} %get-tuple-element.70), channel_id=1, source_target_pairs={{2,14},{3,15},{18,30},{19,31}} | collective-permute-start | bytes 196616 | tf_op jit(solution)/shard_map/ppermute | solution.py:22
  12.1 0.4 collective-permute-done.2
  12.5 0.1 collective-permute-done.1
  12.5 0.1 add_convert_fusion.2
  12.6 0.0 collective-permute-done.4.refs_7_
  12.6 0.0 collective-permute-done.3.refs_8_
  12.7 4.5 %collective-permute-start.5 = (bf16[768,128]{1,0:T(8,128)(2,1)S(1)}, bf16[768,128]{1,0:T(8,128)(2,1)S(1)}, u32[]{:S(2)}, u32[]{:S(2)}) collective-permute-start(bf16[768,128]{1,0:T(8,128)(2,1)S(1)} %pad_maximum_fusion), channel_id=1, source_target_pairs={{0,4},{2,6},{4,8},{6,10},{8,12},{10,14},{1,5},{3,7},{5,9},{7,11},{... | collective-permute-start | bytes 589832 | tf_op jit(solution)/shard_map/ppermute | solution.py:22
  17.2 1.3 %collective-permute-start.6 = (bf16[512,128]{1,0:T(8,128)(2,1)S(1)}, bf16[512,128]{1,0:T(8,128)(2,1)S(1)}, u32[]{:S(2)}, u32[]{:S(2)}) collective-permute-start(bf16[512,128]{1,0:T(8,128)(2,1)S(1)} %maximum_select_fusion), channel_id=1, source_target_pairs={{0,2},{2,0},{4,6},{6,4},{8,10},{10,8},{12,14},{14,12},{1,3},{3,1},... | collective-permute-start | bytes 393224 | tf_op jit(solution)/shard_map/ppermute | solution.py:22
  18.4 3.0 %collective-permute-done.5.refs_5_ = bf16[768,128]{1,0:T(8,128)(2,1)S(1)} collective-permute-done((bf16[768,128]{1,0:T(8,128)(2,1)S(1)}, bf16[768,128]{1,0:T(8,128)(2,1)S(1)}, u32[]{:S(2)}, u32[]{:S(2)}) %collective-permute-start.5) | collective-permute-done | bytes 196640 | tf_op jit(solution)/shard_map/ppermute | solution.py:22
  21.5 0.9 %collective-permute-done.6.refs_6_ = bf16[512,128]{1,0:T(8,128)(2,1)S(1)} collective-permute-done((bf16[512,128]{1,0:T(8,128)(2,1)S(1)}, bf16[512,128]{1,0:T(8,128)(2,1)S(1)}, u32[]{:S(2)}, u32[]{:S(2)}) %collective-permute-start.6) | collective-permute-done | bytes 131104 | tf_op jit(solution)/shard_map/ppermute | solution.py:22
  22.4 1.0 %collective-permute-start.7 = (bf16[768,128]{1,0:T(8,128)(2,1)S(1)}, bf16[768,128]{1,0:T(8,128)(2,1)S(1)}, u32[]{:S(2)}, u32[]{:S(2)}) collective-permute-start(bf16[768,128]{1,0:T(8,128)(2,1)S(1)} %pad_maximum_fusion.1), channel_id=1, source_target_pairs={{0,2},{2,0},{4,6},{6,4},{8,10},{10,8},{12,14},{14,12},{1,3},{3,1},... | collective-permute-start | bytes 589832 | tf_op jit(solution)/shard_map/ppermute | solution.py:22
  23.4 1.6 %pack.1 = (bf16[4,1024,128]{2,1,0:T(8,128)(2,1)S(1)}, bf16[4,1024,128]{2,1,0:T(8,128)(2,1)S(1)}) custom-call(bf16[128,32,128]{2,1,0:T(8,128)(2,1)} %q_ref, bf16[128,32,128]{2,1,0:T(8,128)(2,1)} %g_ref.1), custom_call_target="tpu_custom_call" | custom-call | flops 1048576 | bytes 4194304 | tf_op jit(solution)/shard_map/pack/pallas_call | solution.py:265
  25.1 1.6 %early.1 = (bf16[4,288,128]{2,1,0:T(8,128)(2,1)S(1)}, f32[4,288,1024]{2,1,0:T(8,128)S(1)}, f32[4,288,1024]{2,1,0:T(8,128)S(1)}, f32[4,8,1024]{2,1,0:T(8,128)S(1)}) custom-call(bf16[4,128,128]{2,1,0:T(8,128)(2,1)S(1)} %get-tuple-element.75.refs_0_, bf16[4,128,128]{2,1,0:T(8,128)(2,1)S(1)} %get-tuple-element.76.refs_1_, ...), custom_call_target="tpu_custom_call" | custom-call | flops 603979776 | bytes 12910592 | tf_op jit(solution)/shard_map/early/pallas_call | solution.py:265
  26.7 1.4 %collective-permute-done.7.refs_7_ = bf16[768,128]{1,0:T(8,128)(2,1)S(1)} collective-permute-done((bf16[768,128]{1,0:T(8,128)(2,1)S(1)}, bf16[768,128]{1,0:T(8,128)(2,1)S(1)}, u32[]{:S(2)}, u32[]{:S(2)}) %collective-permute-start.7) | collective-permute-done | bytes 196640 | tf_op jit(solution)/shard_map/ppermute | solution.py:22
  28.1 2.6 %probs.1 = (bf16[512,128]{1,0:T(8,128)(2,1)S(1)}, bf16[512,128]{1,0:T(8,128)(2,1)S(1)}, bf16[4,160,128]{2,1,0:T(8,128)(2,1)S(1)}, bf16[4,160,1024]{2,1,0:T(8,128...) custom-call(bf16[512,128]{1,0:T(8,128)(2,1)S(1)} %get-tuple-element.103.refs_0_, ...), custom_call_target="tpu_custom_call" | custom-call | flops 671088640 | bytes 5079040 | tf_op jit(solution)/shard_map/probs/pallas_call | solution.py:265
  30.7 1.1 %collective-permute-start.8 = (bf16[512,128]{1,0:T(8,128)(2,1)S(1)}, bf16[512,128]{1,0:T(8,128)(2,1)S(1)}, u32[]{:S(2)}, u32[]{:S(2)}) collective-permute-start(bf16[512,128]{1,0:T(8,128)(2,1)S(1)} %get-tuple-element.88), channel_id=1, source_target_pairs={{0,2},{2,0},{4,6},{6,4},{8,10},{10,8},{12,14},{14,12},{1,3},{3,1},... | collective-permute-start | bytes 393224 | tf_op jit(solution)/shard_map/ppermute | solution.py:22
  31.8 1.4 %windows.1 = (bf16[768,128]{1,0:T(8,128)(2,1)S(1)}, bf16[768,128]{1,0:T(8,128)(2,1)S(1)}, bf16[4,288,1024]{2,1,0:T(8,128)(2,1)S(1)}, bf16[4,128,1024]{2,1,0:T(8,128)(2,1)S(1)}) custom-call(bf16[4,1024,128]{2,1,0:T(8,128)(2,1)S(1)} %get-tuple-element.65.refs_2_.refs_0_, bf16[4,1024,128]{2,1,0:T(8,128)(2,1)S(1)} %get-tuple-element.66.refs_3_.refs_1_, ...), custom_call_target="tpu_custom_call" | custom-call | flops 402653184 | bytes 17039360 | tf_op jit(solution)/shard_map/windows/pallas_call | solution.py:265
  33.2 1.1 %collective-permute-start.12 = (bf16[768,128]{1,0:T(8,128)(2,1)S(1)}, bf16[768,128]{1,0:T(8,128)(2,1)S(1)}, u32[]{:S(2)}, u32[]{:S(2)}) collective-permute-start(bf16[768,128]{1,0:T(8,128)(2,1)S(1)} %get-tuple-element.93), channel_id=1, source_target_pairs={{0,2},{2,0},{4,6},{6,4},{8,10},{10,8},{12,14},{14,12},{1,3},{3,1},... | collective-permute-start | bytes 589832 | tf_op jit(solution)/shard_map/ppermute | solution.py:22
  34.2 2.0 %collective-permute-done.8 = bf16[512,128]{1,0:T(8,128)(2,1)S(1)} collective-permute-done((bf16[512,128]{1,0:T(8,128)(2,1)S(1)}, bf16[512,128]{1,0:T(8,128)(2,1)S(1)}, u32[]{:S(2)}, u32[]{:S(2)}) %collective-permute-start.8) | collective-permute-done | bytes 131104 | tf_op jit(solution)/shard_map/ppermute | solution.py:22
  36.3 1.3 %collective-permute-start.11 = (bf16[512,128]{1,0:T(8,128)(2,1)S(1)}, bf16[512,128]{1,0:T(8,128)(2,1)S(1)}, u32[]{:S(2)}, u32[]{:S(2)}) collective-permute-start(bf16[512,128]{1,0:T(8,128)(2,1)S(1)} %add_convert_fusion.1), channel_id=1, source_target_pairs={{4,0},{6,2},{5,1},{7,3},{20,16},{22,18},{21,17},{23,19}} | collective-permute-start | bytes 393224 | tf_op jit(solution)/shard_map/ppermute | solution.py:22
  37.6 1.3 %collective-permute-start.10 = (bf16[512,128]{1,0:T(8,128)(2,1)S(1)}, bf16[512,128]{1,0:T(8,128)(2,1)S(1)}, u32[]{:S(2)}, u32[]{:S(2)}) collective-permute-start(bf16[512,128]{1,0:T(8,128)(2,1)S(1)} %add_convert_fusion.1), channel_id=1, source_target_pairs={{8,0},{10,2},{9,1},{11,3},{24,16},{26,18},{25,17},{27,19}} | collective-permute-start | bytes 393224 | tf_op jit(solution)/shard_map/ppermute | solution.py:22
  38.9 1.3 %collective-permute-start.9 = (bf16[512,128]{1,0:T(8,128)(2,1)S(1)}, bf16[512,128]{1,0:T(8,128)(2,1)S(1)}, u32[]{:S(2)}, u32[]{:S(2)}) collective-permute-start(bf16[512,128]{1,0:T(8,128)(2,1)S(1)} %add_convert_fusion.1), channel_id=1, source_target_pairs={{12,0},{14,2},{13,1},{15,3},{28,16},{30,18},{29,17},{31,19}} | collective-permute-start | bytes 393224 | tf_op jit(solution)/shard_map/ppermute | solution.py:22
  40.2 2.4 %grads.1 = (bf16[128,32,128]{2,1,0:T(8,128)(2,1)}, f32[512,128]{1,0:T(8,128)S(1)}, f32[512,128]{1,0:T(8,128)S(1)}) custom-call(bf16[4,1024,128]{2,1,0:T(8,128)(2,1)S(1)} %get-tuple-element.65.refs_2_.refs_0_, bf16[4,1024,128]{2,1,0:T(8,128)(2,1)S(1)} %get-tuple-element.66.refs_3_.refs_1_, bf16[4,160,128]{2,1,0:T(8,128)(2,1)S(1)} %get-tuple-element.78.refs_2_, ...), custom_call_target="tpu_custom_call" | custom-call | flops 469762048 | bytes 8847360 | tf_op jit(solution)/shard_map/grads/pallas_call | solution.py:265
  42.6 0.0 collective-permute-done.12
  42.6 0.1 add_convert_fusion.5
  42.6 0.7 %collective-permute-start.14 = (bf16[256,128]{1,0:T(8,128)(2,1)S(1)}, bf16[256,128]{1,0:T(8,128)(2,1)S(1)}, u32[]{:S(2)}, u32[]{:S(2)}) collective-permute-start(bf16[256,128]{1,0:T(8,128)(2,1)S(1)} %get-tuple-element.95), channel_id=1, source_target_pairs={{10,2},{12,4},{14,6},{11,3},{13,5},{15,7},{26,18},{28,20},{30,22},... | collective-permute-start | bytes 196616 | tf_op jit(solution)/shard_map/ppermute | solution.py:22
  43.3 0.7 %collective-permute-start.13 = (bf16[256,128]{1,0:T(8,128)(2,1)S(1)}, bf16[256,128]{1,0:T(8,128)(2,1)S(1)}, u32[]{:S(2)}, u32[]{:S(2)}) collective-permute-start(bf16[256,128]{1,0:T(8,128)(2,1)S(1)} %get-tuple-element.99), channel_id=1, source_target_pairs={{6,2},{8,4},{10,6},{12,8},{14,10},{7,3},{9,5},{11,7},{13,9},{15,11... | collective-permute-start | bytes 196616 | tf_op jit(solution)/shard_map/ppermute | solution.py:22
  44.0 0.0 collective-permute-done.11
  44.0 0.7 %collective-permute-start.15 = (bf16[256,128]{1,0:T(8,128)(2,1)S(1)}, bf16[256,128]{1,0:T(8,128)(2,1)S(1)}, u32[]{:S(2)}, u32[]{:S(2)}) collective-permute-start(bf16[256,128]{1,0:T(8,128)(2,1)S(1)} %get-tuple-element.100), channel_id=1, source_target_pairs={{14,2},{15,3},{30,18},{31,19}} | collective-permute-start | bytes 196616 | tf_op jit(solution)/shard_map/ppermute | solution.py:22
  44.7 2.0 %collective-permute-done.10 = bf16[512,128]{1,0:T(8,128)(2,1)S(1)} collective-permute-done((bf16[512,128]{1,0:T(8,128)(2,1)S(1)}, bf16[512,128]{1,0:T(8,128)(2,1)S(1)}, u32[]{:S(2)}, u32[]{:S(2)}) %collective-permute-start.10) | collective-permute-done | bytes 131104 | tf_op jit(solution)/shard_map/ppermute | solution.py:22
  46.6 1.6 %collective-permute-done.9 = bf16[512,128]{1,0:T(8,128)(2,1)S(1)} collective-permute-done((bf16[512,128]{1,0:T(8,128)(2,1)S(1)}, bf16[512,128]{1,0:T(8,128)(2,1)S(1)}, u32[]{:S(2)}, u32[]{:S(2)}) %collective-permute-start.9) | collective-permute-done | bytes 131104 | tf_op jit(solution)/shard_map/ppermute | solution.py:22
  48.3 0.1 select_add_fusion.1
  48.3 1.3 %collective-permute-start.16 = (bf16[512,128]{1,0:T(8,128)(2,1)S(1)}, bf16[512,128]{1,0:T(8,128)(2,1)S(1)}, u32[]{:S(2)}, u32[]{:S(2)}) collective-permute-start(bf16[512,128]{1,0:T(8,128)(2,1)S(1)} %get-tuple-element.98), channel_id=1, source_target_pairs={{2,0},{3,1},{18,16},{19,17}} | collective-permute-start | bytes 393224 | tf_op jit(solution)/shard_map/ppermute | solution.py:22
  49.6 0.0 collective-permute-done.14
  49.7 0.0 collective-permute-done.13
  49.7 0.0 collective-permute-done.15
  49.7 5.5 %collective-permute-done.16 = bf16[512,128]{1,0:T(8,128)(2,1)S(1)} collective-permute-done((bf16[512,128]{1,0:T(8,128)(2,1)S(1)}, bf16[512,128]{1,0:T(8,128)(2,1)S(1)}, u32[]{:S(2)}, u32[]{:S(2)}) %collective-permute-start.16) | collective-permute-done | bytes 131104 | tf_op jit(solution)/shard_map/ppermute | solution.py:22
  55.3 0.0 copy-start
  55.3 0.0 copy-start.1
  55.3 0.7 %copy-done = f32[512,128]{1,0:T(8,128)} copy-done((f32[512,128]{1,0:T(8,128)}, f32[512,128]{1,0:T(8,128)S(1)}, u32[]{:S(2)}) %copy-start) | copy-done | bytes 262168
  56.0 0.1 copy-done.1
  (10 shorter events, 0.2 us)
Async XLA Ops:
  0.6 10.1 %collective-permute-start = (bf16[512,128]{1,0:T(8,128)(2,1)}, bf16[512,128]{1,0:T(8,128)(2,1)S(1)}, u32[]{:S(2)}, u32[]{:S(2)}) collective-permute-start(bf16[512,128]{1,0:T(8,128)(2,1)} %bitcast.6), channel_id=1, source_target_pairs={{0,8},{1,9},{16,24},{17,25}} | collective-permute-start | bytes 393224 | tf_op jit(solution)/shard_map/ppermute | solution.py:22
  6.6 5.9 %collective-permute-start.2 = (bf16[512,128]{1,0:T(8,128)(2,1)}, bf16[512,128]{1,0:T(8,128)(2,1)S(1)}, u32[]{:S(2)}, u32[]{:S(2)}) collective-permute-start(bf16[512,128]{1,0:T(8,128)(2,1)} %bitcast.8), channel_id=1, source_target_pairs={{0,10},{1,11},{16,26},{17,27}} | collective-permute-start | bytes 393224 | tf_op jit(solution)/shard_map/ppermute | solution.py:22
  8.2 4.4 %collective-permute-start.1 = (bf16[512,128]{1,0:T(8,128)(2,1)}, bf16[512,128]{1,0:T(8,128)(2,1)S(1)}, u32[]{:S(2)}, u32[]{:S(2)}) collective-permute-start(bf16[512,128]{1,0:T(8,128)(2,1)} %bitcast.9), channel_id=1, source_target_pairs={{0,2},{1,3},{16,18},{17,19}} | collective-permute-start | bytes 393224 | tf_op jit(solution)/shard_map/ppermute | solution.py:22
  10.8 1.8 %collective-permute-start.4 = (bf16[256,128]{1,0:T(8,128)(2,1)S(1)}, bf16[256,128]{1,0:T(8,128)(2,1)S(1)}, u32[]{:S(2)}, u32[]{:S(2)}) collective-permute-start(bf16[256,128]{1,0:T(8,128)(2,1)S(1)} %get-tuple-element.70), channel_id=1, source_target_pairs={{2,10},{4,12},{6,14},{3,11},{5,13},{7,15},{18,26},{20,28},{22,30},... | collective-permute-start | bytes 196616 | tf_op jit(solution)/shard_map/ppermute | solution.py:22
  11.4 1.2 %collective-permute-start.3 = (bf16[256,128]{1,0:T(8,128)(2,1)S(1)}, bf16[256,128]{1,0:T(8,128)(2,1)S(1)}, u32[]{:S(2)}, u32[]{:S(2)}) collective-permute-start(bf16[256,128]{1,0:T(8,128)(2,1)S(1)} %get-tuple-element.70), channel_id=1, source_target_pairs={{2,14},{3,15},{18,30},{19,31}} | collective-permute-start | bytes 196616 | tf_op jit(solution)/shard_map/ppermute | solution.py:22
  12.7 8.8 %collective-permute-start.5 = (bf16[768,128]{1,0:T(8,128)(2,1)S(1)}, bf16[768,128]{1,0:T(8,128)(2,1)S(1)}, u32[]{:S(2)}, u32[]{:S(2)}) collective-permute-start(bf16[768,128]{1,0:T(8,128)(2,1)S(1)} %pad_maximum_fusion), channel_id=1, source_target_pairs={{0,4},{2,6},{4,8},{6,10},{8,12},{10,14},{1,5},{3,7},{5,9},{7,11},{... | collective-permute-start | bytes 589832 | tf_op jit(solution)/shard_map/ppermute | solution.py:22
  17.2 5.2 %collective-permute-start.6 = (bf16[512,128]{1,0:T(8,128)(2,1)S(1)}, bf16[512,128]{1,0:T(8,128)(2,1)S(1)}, u32[]{:S(2)}, u32[]{:S(2)}) collective-permute-start(bf16[512,128]{1,0:T(8,128)(2,1)S(1)} %maximum_select_fusion), channel_id=1, source_target_pairs={{0,2},{2,0},{4,6},{6,4},{8,10},{10,8},{12,14},{14,12},{1,3},{3,1},... | collective-permute-start | bytes 393224 | tf_op jit(solution)/shard_map/ppermute | solution.py:22
  22.4 5.7 %collective-permute-start.7 = (bf16[768,128]{1,0:T(8,128)(2,1)S(1)}, bf16[768,128]{1,0:T(8,128)(2,1)S(1)}, u32[]{:S(2)}, u32[]{:S(2)}) collective-permute-start(bf16[768,128]{1,0:T(8,128)(2,1)S(1)} %pad_maximum_fusion.1), channel_id=1, source_target_pairs={{0,2},{2,0},{4,6},{6,4},{8,10},{10,8},{12,14},{14,12},{1,3},{3,1},... | collective-permute-start | bytes 589832 | tf_op jit(solution)/shard_map/ppermute | solution.py:22
  30.7 5.6 %collective-permute-start.8 = (bf16[512,128]{1,0:T(8,128)(2,1)S(1)}, bf16[512,128]{1,0:T(8,128)(2,1)S(1)}, u32[]{:S(2)}, u32[]{:S(2)}) collective-permute-start(bf16[512,128]{1,0:T(8,128)(2,1)S(1)} %get-tuple-element.88), channel_id=1, source_target_pairs={{0,2},{2,0},{4,6},{6,4},{8,10},{10,8},{12,14},{14,12},{1,3},{3,1},... | collective-permute-start | bytes 393224 | tf_op jit(solution)/shard_map/ppermute | solution.py:22
  33.2 9.4 %collective-permute-start.12 = (bf16[768,128]{1,0:T(8,128)(2,1)S(1)}, bf16[768,128]{1,0:T(8,128)(2,1)S(1)}, u32[]{:S(2)}, u32[]{:S(2)}) collective-permute-start(bf16[768,128]{1,0:T(8,128)(2,1)S(1)} %get-tuple-element.93), channel_id=1, source_target_pairs={{0,2},{2,0},{4,6},{6,4},{8,10},{10,8},{12,14},{14,12},{1,3},{3,1},... | collective-permute-start | bytes 589832 | tf_op jit(solution)/shard_map/ppermute | solution.py:22
  36.3 7.7 %collective-permute-start.11 = (bf16[512,128]{1,0:T(8,128)(2,1)S(1)}, bf16[512,128]{1,0:T(8,128)(2,1)S(1)}, u32[]{:S(2)}, u32[]{:S(2)}) collective-permute-start(bf16[512,128]{1,0:T(8,128)(2,1)S(1)} %add_convert_fusion.1), channel_id=1, source_target_pairs={{4,0},{6,2},{5,1},{7,3},{20,16},{22,18},{21,17},{23,19}} | collective-permute-start | bytes 393224 | tf_op jit(solution)/shard_map/ppermute | solution.py:22
  37.6 9.0 %collective-permute-start.10 = (bf16[512,128]{1,0:T(8,128)(2,1)S(1)}, bf16[512,128]{1,0:T(8,128)(2,1)S(1)}, u32[]{:S(2)}, u32[]{:S(2)}) collective-permute-start(bf16[512,128]{1,0:T(8,128)(2,1)S(1)} %add_convert_fusion.1), channel_id=1, source_target_pairs={{8,0},{10,2},{9,1},{11,3},{24,16},{26,18},{25,17},{27,19}} | collective-permute-start | bytes 393224 | tf_op jit(solution)/shard_map/ppermute | solution.py:22
  38.9 9.4 %collective-permute-start.9 = (bf16[512,128]{1,0:T(8,128)(2,1)S(1)}, bf16[512,128]{1,0:T(8,128)(2,1)S(1)}, u32[]{:S(2)}, u32[]{:S(2)}) collective-permute-start(bf16[512,128]{1,0:T(8,128)(2,1)S(1)} %add_convert_fusion.1), channel_id=1, source_target_pairs={{12,0},{14,2},{13,1},{15,3},{28,16},{30,18},{29,17},{31,19}} | collective-permute-start | bytes 393224 | tf_op jit(solution)/shard_map/ppermute | solution.py:22
  42.6 7.0 %collective-permute-start.14 = (bf16[256,128]{1,0:T(8,128)(2,1)S(1)}, bf16[256,128]{1,0:T(8,128)(2,1)S(1)}, u32[]{:S(2)}, u32[]{:S(2)}) collective-permute-start(bf16[256,128]{1,0:T(8,128)(2,1)S(1)} %get-tuple-element.95), channel_id=1, source_target_pairs={{10,2},{12,4},{14,6},{11,3},{13,5},{15,7},{26,18},{28,20},{30,22},... | collective-permute-start | bytes 196616 | tf_op jit(solution)/shard_map/ppermute | solution.py:22
  43.3 6.3 %collective-permute-start.13 = (bf16[256,128]{1,0:T(8,128)(2,1)S(1)}, bf16[256,128]{1,0:T(8,128)(2,1)S(1)}, u32[]{:S(2)}, u32[]{:S(2)}) collective-permute-start(bf16[256,128]{1,0:T(8,128)(2,1)S(1)} %get-tuple-element.99), channel_id=1, source_target_pairs={{6,2},{8,4},{10,6},{12,8},{14,10},{7,3},{9,5},{11,7},{13,9},{15,11... | collective-permute-start | bytes 196616 | tf_op jit(solution)/shard_map/ppermute | solution.py:22
  44.0 5.7 %collective-permute-start.15 = (bf16[256,128]{1,0:T(8,128)(2,1)S(1)}, bf16[256,128]{1,0:T(8,128)(2,1)S(1)}, u32[]{:S(2)}, u32[]{:S(2)}) collective-permute-start(bf16[256,128]{1,0:T(8,128)(2,1)S(1)} %get-tuple-element.100), channel_id=1, source_target_pairs={{14,2},{15,3},{30,18},{31,19}} | collective-permute-start | bytes 196616 | tf_op jit(solution)/shard_map/ppermute | solution.py:22
  48.3 6.9 %collective-permute-start.16 = (bf16[512,128]{1,0:T(8,128)(2,1)S(1)}, bf16[512,128]{1,0:T(8,128)(2,1)S(1)}, u32[]{:S(2)}, u32[]{:S(2)}) collective-permute-start(bf16[512,128]{1,0:T(8,128)(2,1)S(1)} %get-tuple-element.98), channel_id=1, source_target_pairs={{2,0},{3,1},{18,16},{19,17}} | collective-permute-start | bytes 393224 | tf_op jit(solution)/shard_map/ppermute | solution.py:22
  55.3 0.7 %copy-start = (f32[512,128]{1,0:T(8,128)}, f32[512,128]{1,0:T(8,128)S(1)}, u32[]{:S(2)}) copy-start(f32[512,128]{1,0:T(8,128)S(1)} %get-tuple-element.104) | copy-start | bytes 786436
  55.3 0.8 %copy-start.1 = (f32[512,128]{1,0:T(8,128)}, f32[512,128]{1,0:T(8,128)S(1)}, u32[]{:S(2)}) copy-start(f32[512,128]{1,0:T(8,128)S(1)} %get-tuple-element.105) | copy-start | bytes 786436

commit v20 on v17

--- a/solution.py
+++ b/solution.py
@@ -481,7 +481,7 @@
         four = permuted(four, far_route)
         six = permuted(added(six, jnp.where(even, none, last)).astype(BF16), [(7, 1)])
         total = added(total, *parts).astype(BF16)
-        mine = added(jnp.where(even, first, none), two, four, six)
+        mine = added(jnp.where(even, first, none), six, four, two)
         return finished, total, permuted(total, [(1, 0)]).astype(F32), mine
     strides = [2**i for i in range(2, size.bit_length()) if 2**i < size]
     top = strides[-1]

time: 56.2 us -> 55.9 us (level)
  no operation moved by 1% of the time
where the time goes in v20:
time: 55.9 us; the launch traced here: 55.5 us
  starting transfers between devices  24.6 us (44%)
  waiting for transfers between devices  18 us (32%)
  Pallas kernels  10.8 us (19%)
  between operations  0.92 us (2%)
  local copies, waits for them, and re-layouts  0.78 us (1%)
    ppermute x17, starting transfers between devices, permuted(): return lax.ppermute(block, 'node', route)  24.6 us
    ppermute x17, waiting for transfers between devices, permuted(): return lax.ppermute(block, 'node', route)  18 us
    pallas_call x6, Pallas kernels, call(): pl.pallas_call(kernel, in_specs=[place] * len(operands), out_specs=[VMEM]...  10.8 us
  transfers between devices with their start and end apart: 17, of which 11 were waited for; matrix products, arithmetic and copies ran while one was open for 1% of the time, Pallas kernels for 15%

profile of v20, /device:TPU:0, one launch (start us, length us, event | category | flops | bytes accessed | tf_op | source)
XLA Modules:
  0.0 55.5 jit_solution(4839673186087385393)
XLA Ops:
  0.6 5.9 %collective-permute-start = (bf16[512,128]{1,0:T(8,128)(2,1)}, bf16[512,128]{1,0:T(8,128)(2,1)S(1)}, u32[]{:S(2)}, u32[]{:S(2)}) collective-permute-start(bf16[512,128]{1,0:T(8,128)(2,1)} %bitcast.6), channel_id=1, source_target_pairs={{0,8},{1,9},{16,24},{17,25}} | collective-permute-start | bytes 393224 | tf_op jit(solution)/shard_map/ppermute | solution.py:22
  6.6 1.6 %collective-permute-start.2 = (bf16[512,128]{1,0:T(8,128)(2,1)}, bf16[512,128]{1,0:T(8,128)(2,1)S(1)}, u32[]{:S(2)}, u32[]{:S(2)}) collective-permute-start(bf16[512,128]{1,0:T(8,128)(2,1)} %bitcast.8), channel_id=1, source_target_pairs={{0,10},{1,11},{16,26},{17,27}} | collective-permute-start | bytes 393224 | tf_op jit(solution)/shard_map/ppermute | solution.py:22
  8.2 1.3 %collective-permute-start.1 = (bf16[512,128]{1,0:T(8,128)(2,1)}, bf16[512,128]{1,0:T(8,128)(2,1)S(1)}, u32[]{:S(2)}, u32[]{:S(2)}) collective-permute-start(bf16[512,128]{1,0:T(8,128)(2,1)} %bitcast.9), channel_id=1, source_target_pairs={{0,2},{1,3},{16,18},{17,19}} | collective-permute-start | bytes 393224 | tf_op jit(solution)/shard_map/ppermute | solution.py:22
  9.5 1.2 %load.1 = (bf16[256,128]{1,0:T(8,128)(2,1)S(1)}, bf16[512,128]{1,0:T(8,128)(2,1)S(1)}, bf16[4,128,128]{2,1,0:T(8,128)(2,1)S(1)}, bf16[4,128,128]{2,1,0:T(8,128)(...) custom-call(s32[64]{0:T(128)} %refs_0_.1, s32[64]{0:T(128)} %refs_1_.1, bf16[512,128]{1,0:T(8,128)(2,1)} %bitcast.7, ...), custom_call_target="tpu_custom_call" | custom-call | flops 1048576 | bytes 983552 | tf_op jit(solution)/shard_map/load/pallas_call | solution.py:265
  10.7 0.1 collective-permute-done
  10.8 0.7 %collective-permute-start.4 = (bf16[256,128]{1,0:T(8,128)(2,1)S(1)}, bf16[256,128]{1,0:T(8,128)(2,1)S(1)}, u32[]{:S(2)}, u32[]{:S(2)}) collective-permute-start(bf16[256,128]{1,0:T(8,128)(2,1)S(1)} %get-tuple-element.70), channel_id=1, source_target_pairs={{2,10},{4,12},{6,14},{3,11},{5,13},{7,15},{18,26},{20,28},{22,30},... | collective-permute-start | bytes 196616 | tf_op jit(solution)/shard_map/ppermute | solution.py:22
  11.4 0.7 %collective-permute-start.3 = (bf16[256,128]{1,0:T(8,128)(2,1)S(1)}, bf16[256,128]{1,0:T(8,128)(2,1)S(1)}, u32[]{:S(2)}, u32[]{:S(2)}) collective-permute-start(bf16[256,128]{1,0:T(8,128)(2,1)S(1)} %get-tuple-element.70), channel_id=1, source_target_pairs={{2,14},{3,15},{18,30},{19,31}} | collective-permute-start | bytes 196616 | tf_op jit(solution)/shard_map/ppermute | solution.py:22
  12.1 0.4 collective-permute-done.2
  12.5 0.1 collective-permute-done.1
  12.5 0.1 add_convert_fusion.2
  12.6 1.6 %pack.1 = (bf16[4,1024,128]{2,1,0:T(8,128)(2,1)S(1)}, bf16[4,1024,128]{2,1,0:T(8,128)(2,1)S(1)}) custom-call(bf16[128,32,128]{2,1,0:T(8,128)(2,1)} %q_ref, bf16[128,32,128]{2,1,0:T(8,128)(2,1)} %g_ref.1), custom_call_target="tpu_custom_call" | custom-call | flops 1048576 | bytes 4194304 | tf_op jit(solution)/shard_map/pack/pallas_call | solution.py:265
  14.3 0.0 collective-permute-done.4.refs_7_
  14.3 0.0 collective-permute-done.3.refs_8_
  14.3 2.8 %collective-permute-start.5 = (bf16[768,128]{1,0:T(8,128)(2,1)S(1)}, bf16[768,128]{1,0:T(8,128)(2,1)S(1)}, u32[]{:S(2)}, u32[]{:S(2)}) collective-permute-start(bf16[768,128]{1,0:T(8,128)(2,1)S(1)} %pad_maximum_fusion), channel_id=1, source_target_pairs={{0,4},{2,6},{4,8},{6,10},{8,12},{10,14},{1,5},{3,7},{5,9},{7,11},{... | collective-permute-start | bytes 589832 | tf_op jit(solution)/shard_map/ppermute | solution.py:22
  17.2 1.3 %collective-permute-start.6 = (bf16[512,128]{1,0:T(8,128)(2,1)S(1)}, bf16[512,128]{1,0:T(8,128)(2,1)S(1)}, u32[]{:S(2)}, u32[]{:S(2)}) collective-permute-start(bf16[512,128]{1,0:T(8,128)(2,1)S(1)} %maximum_select_fusion), channel_id=1, source_target_pairs={{0,2},{2,0},{4,6},{6,4},{8,10},{10,8},{12,14},{14,12},{1,3},{3,1},... | collective-permute-start | bytes 393224 | tf_op jit(solution)/shard_map/ppermute | solution.py:22
  18.4 3.0 %collective-permute-done.5.refs_5_ = bf16[768,128]{1,0:T(8,128)(2,1)S(1)} collective-permute-done((bf16[768,128]{1,0:T(8,128)(2,1)S(1)}, bf16[768,128]{1,0:T(8,128)(2,1)S(1)}, u32[]{:S(2)}, u32[]{:S(2)}) %collective-permute-start.5) | collective-permute-done | bytes 196640 | tf_op jit(solution)/shard_map/ppermute | solution.py:22
  21.5 0.9 %collective-permute-done.6.refs_6_ = bf16[512,128]{1,0:T(8,128)(2,1)S(1)} collective-permute-done((bf16[512,128]{1,0:T(8,128)(2,1)S(1)}, bf16[512,128]{1,0:T(8,128)(2,1)S(1)}, u32[]{:S(2)}, u32[]{:S(2)}) %collective-permute-start.6) | collective-permute-done | bytes 131104 | tf_op jit(solution)/shard_map/ppermute | solution.py:22
  22.4 1.0 %collective-permute-start.7 = (bf16[768,128]{1,0:T(8,128)(2,1)S(1)}, bf16[768,128]{1,0:T(8,128)(2,1)S(1)}, u32[]{:S(2)}, u32[]{:S(2)}) collective-permute-start(bf16[768,128]{1,0:T(8,128)(2,1)S(1)} %pad_maximum_fusion.1), channel_id=1, source_target_pairs={{0,2},{2,0},{4,6},{6,4},{8,10},{10,8},{12,14},{14,12},{1,3},{3,1},... | collective-permute-start | bytes 589832 | tf_op jit(solution)/shard_map/ppermute | solution.py:22
  23.4 1.6 %early.1 = (bf16[4,288,128]{2,1,0:T(8,128)(2,1)S(1)}, f32[4,288,1024]{2,1,0:T(8,128)S(1)}, f32[4,288,1024]{2,1,0:T(8,128)S(1)}, f32[4,8,1024]{2,1,0:T(8,128)S(1)}) custom-call(bf16[4,128,128]{2,1,0:T(8,128)(2,1)S(1)} %get-tuple-element.75.refs_0_, bf16[4,128,128]{2,1,0:T(8,128)(2,1)S(1)} %get-tuple-element.76.refs_1_, ...), custom_call_target="tpu_custom_call" | custom-call | flops 603979776 | bytes 12910592 | tf_op jit(solution)/shard_map/early/pallas_call | solution.py:265
  25.0 3.0 %collective-permute-done.7.refs_7_ = bf16[768,128]{1,0:T(8,128)(2,1)S(1)} collective-permute-done((bf16[768,128]{1,0:T(8,128)(2,1)S(1)}, bf16[768,128]{1,0:T(8,128)(2,1)S(1)}, u32[]{:S(2)}, u32[]{:S(2)}) %collective-permute-start.7) | collective-permute-done | bytes 196640 | tf_op jit(solution)/shard_map/ppermute | solution.py:22
  28.1 2.6 %probs.1 = (bf16[512,128]{1,0:T(8,128)(2,1)S(1)}, bf16[512,128]{1,0:T(8,128)(2,1)S(1)}, bf16[4,160,128]{2,1,0:T(8,128)(2,1)S(1)}, bf16[4,160,1024]{2,1,0:T(8,128...) custom-call(bf16[512,128]{1,0:T(8,128)(2,1)S(1)} %get-tuple-element.103.refs_0_, ...), custom_call_target="tpu_custom_call" | custom-call | flops 671088640 | bytes 5079040 | tf_op jit(solution)/shard_map/probs/pallas_call | solution.py:265
  30.7 1.1 %collective-permute-start.8 = (bf16[512,128]{1,0:T(8,128)(2,1)S(1)}, bf16[512,128]{1,0:T(8,128)(2,1)S(1)}, u32[]{:S(2)}, u32[]{:S(2)}) collective-permute-start(bf16[512,128]{1,0:T(8,128)(2,1)S(1)} %get-tuple-element.88), channel_id=1, source_target_pairs={{0,2},{2,0},{4,6},{6,4},{8,10},{10,8},{12,14},{14,12},{1,3},{3,1},... | collective-permute-start | bytes 393224 | tf_op jit(solution)/shard_map/ppermute | solution.py:22
  31.8 1.4 %windows.1 = (bf16[768,128]{1,0:T(8,128)(2,1)S(1)}, bf16[768,128]{1,0:T(8,128)(2,1)S(1)}, bf16[4,288,1024]{2,1,0:T(8,128)(2,1)S(1)}, bf16[4,128,1024]{2,1,0:T(8,128)(2,1)S(1)}) custom-call(bf16[4,1024,128]{2,1,0:T(8,128)(2,1)S(1)} %get-tuple-element.65.refs_2_.refs_0_, bf16[4,1024,128]{2,1,0:T(8,128)(2,1)S(1)} %get-tuple-element.66.refs_3_.refs_1_, ...), custom_call_target="tpu_custom_call" | custom-call | flops 402653184 | bytes 17039360 | tf_op jit(solution)/shard_map/windows/pallas_call | solution.py:265
  33.2 1.1 %collective-permute-start.12 = (bf16[768,128]{1,0:T(8,128)(2,1)S(1)}, bf16[768,128]{1,0:T(8,128)(2,1)S(1)}, u32[]{:S(2)}, u32[]{:S(2)}) collective-permute-start(bf16[768,128]{1,0:T(8,128)(2,1)S(1)} %get-tuple-element.93), channel_id=1, source_target_pairs={{0,2},{2,0},{4,6},{6,4},{8,10},{10,8},{12,14},{14,12},{1,3},{3,1},... | collective-permute-start | bytes 589832 | tf_op jit(solution)/shard_map/ppermute | solution.py:22
  34.2 1.8 %collective-permute-done.8 = bf16[512,128]{1,0:T(8,128)(2,1)S(1)} collective-permute-done((bf16[512,128]{1,0:T(8,128)(2,1)S(1)}, bf16[512,128]{1,0:T(8,128)(2,1)S(1)}, u32[]{:S(2)}, u32[]{:S(2)}) %collective-permute-start.8) | collective-permute-done | bytes 131104 | tf_op jit(solution)/shard_map/ppermute | solution.py:22
  36.1 1.3 %collective-permute-start.11 = (bf16[512,128]{1,0:T(8,128)(2,1)S(1)}, bf16[512,128]{1,0:T(8,128)(2,1)S(1)}, u32[]{:S(2)}, u32[]{:S(2)}) collective-permute-start(bf16[512,128]{1,0:T(8,128)(2,1)S(1)} %add_convert_fusion.1), channel_id=1, source_target_pairs={{4,0},{6,2},{5,1},{7,3},{20,16},{22,18},{21,17},{23,19}} | collective-permute-start | bytes 393224 | tf_op jit(solution)/shard_map/ppermute | solution.py:22
  37.4 1.3 %collective-permute-start.10 = (bf16[512,128]{1,0:T(8,128)(2,1)S(1)}, bf16[512,128]{1,0:T(8,128)(2,1)S(1)}, u32[]{:S(2)}, u32[]{:S(2)}) collective-permute-start(bf16[512,128]{1,0:T(8,128)(2,1)S(1)} %add_convert_fusion.1), channel_id=1, source_target_pairs={{8,0},{10,2},{9,1},{11,3},{24,16},{26,18},{25,17},{27,19}} | collective-permute-start | bytes 393224 | tf_op jit(solution)/shard_map/ppermute | solution.py:22
  38.7 1.3 %collective-permute-start.9 = (bf16[512,128]{1,0:T(8,128)(2,1)S(1)}, bf16[512,128]{1,0:T(8,128)(2,1)S(1)}, u32[]{:S(2)}, u32[]{:S(2)}) collective-permute-start(bf16[512,128]{1,0:T(8,128)(2,1)S(1)} %add_convert_fusion.1), channel_id=1, source_target_pairs={{12,0},{14,2},{13,1},{15,3},{28,16},{30,18},{29,17},{31,19}} | collective-permute-start | bytes 393224 | tf_op jit(solution)/shard_map/ppermute | solution.py:22
  40.0 2.4 %grads.1 = (bf16[128,32,128]{2,1,0:T(8,128)(2,1)}, f32[512,128]{1,0:T(8,128)S(1)}, f32[512,128]{1,0:T(8,128)S(1)}) custom-call(bf16[4,1024,128]{2,1,0:T(8,128)(2,1)S(1)} %get-tuple-element.65.refs_2_.refs_0_, bf16[4,1024,128]{2,1,0:T(8,128)(2,1)S(1)} %get-tuple-element.66.refs_3_.refs_1_, bf16[4,160,128]{2,1,0:T(8,128)(2,1)S(1)} %get-tuple-element.78.refs_2_, ...), custom_call_target="tpu_custom_call" | custom-call | flops 469762048 | bytes 8847360 | tf_op jit(solution)/shard_map/grads/pallas_call | solution.py:265
  42.3 0.0 collective-permute-done.12
  42.3 0.1 add_convert_fusion.5
  42.4 0.7 %collective-permute-start.14 = (bf16[256,128]{1,0:T(8,128)(2,1)S(1)}, bf16[256,128]{1,0:T(8,128)(2,1)S(1)}, u32[]{:S(2)}, u32[]{:S(2)}) collective-permute-start(bf16[256,128]{1,0:T(8,128)(2,1)S(1)} %get-tuple-element.95), channel_id=1, source_target_pairs={{10,2},{12,4},{14,6},{11,3},{13,5},{15,7},{26,18},{28,20},{30,22},... | collective-permute-start | bytes 196616 | tf_op jit(solution)/shard_map/ppermute | solution.py:22
  43.1 0.7 %collective-permute-start.13 = (bf16[256,128]{1,0:T(8,128)(2,1)S(1)}, bf16[256,128]{1,0:T(8,128)(2,1)S(1)}, u32[]{:S(2)}, u32[]{:S(2)}) collective-permute-start(bf16[256,128]{1,0:T(8,128)(2,1)S(1)} %get-tuple-element.99), channel_id=1, source_target_pairs={{14,2},{15,3},{30,18},{31,19}} | collective-permute-start | bytes 196616 | tf_op jit(solution)/shard_map/ppermute | solution.py:22
  43.7 1.5 %collective-permute-done.11 = bf16[512,128]{1,0:T(8,128)(2,1)S(1)} collective-permute-done((bf16[512,128]{1,0:T(8,128)(2,1)S(1)}, bf16[512,128]{1,0:T(8,128)(2,1)S(1)}, u32[]{:S(2)}, u32[]{:S(2)}) %collective-permute-start.11) | collective-permute-done | bytes 131104 | tf_op jit(solution)/shard_map/ppermute | solution.py:22
  45.3 0.7 %collective-permute-start.15 = (bf16[256,128]{1,0:T(8,128)(2,1)S(1)}, bf16[256,128]{1,0:T(8,128)(2,1)S(1)}, u32[]{:S(2)}, u32[]{:S(2)}) collective-permute-start(bf16[256,128]{1,0:T(8,128)(2,1)S(1)} %get-tuple-element.100), channel_id=1, source_target_pairs={{6,2},{8,4},{10,6},{12,8},{14,10},{7,3},{9,5},{11,7},{13,9},{15,11... | collective-permute-start | bytes 196616 | tf_op jit(solution)/shard_map/ppermute | solution.py:22
  45.9 1.0 %collective-permute-done.10 = bf16[512,128]{1,0:T(8,128)(2,1)S(1)} collective-permute-done((bf16[512,128]{1,0:T(8,128)(2,1)S(1)}, bf16[512,128]{1,0:T(8,128)(2,1)S(1)}, u32[]{:S(2)}, u32[]{:S(2)}) %collective-permute-start.10) | collective-permute-done | bytes 131104 | tf_op jit(solution)/shard_map/ppermute | solution.py:22
  46.9 0.8 %collective-permute-done.9 = bf16[512,128]{1,0:T(8,128)(2,1)S(1)} collective-permute-done((bf16[512,128]{1,0:T(8,128)(2,1)S(1)}, bf16[512,128]{1,0:T(8,128)(2,1)S(1)}, u32[]{:S(2)}, u32[]{:S(2)}) %collective-permute-start.9) | collective-permute-done | bytes 131104 | tf_op jit(solution)/shard_map/ppermute | solution.py:22
  47.7 0.1 select_add_fusion.1
  47.8 1.3 %collective-permute-start.16 = (bf16[512,128]{1,0:T(8,128)(2,1)S(1)}, bf16[512,128]{1,0:T(8,128)(2,1)S(1)}, u32[]{:S(2)}, u32[]{:S(2)}) collective-permute-start(bf16[512,128]{1,0:T(8,128)(2,1)S(1)} %get-tuple-element.98), channel_id=1, source_target_pairs={{2,0},{3,1},{18,16},{19,17}} | collective-permute-start | bytes 393224 | tf_op jit(solution)/shard_map/ppermute | solution.py:22
  49.1 0.0 collective-permute-done.14
  49.1 0.0 collective-permute-done.13
  49.1 0.0 collective-permute-done.15
  49.2 5.5 %collective-permute-done.16 = bf16[512,128]{1,0:T(8,128)(2,1)S(1)} collective-permute-done((bf16[512,128]{1,0:T(8,128)(2,1)S(1)}, bf16[512,128]{1,0:T(8,128)(2,1)S(1)}, u32[]{:S(2)}, u32[]{:S(2)}) %collective-permute-start.16) | collective-permute-done | bytes 131104 | tf_op jit(solution)/shard_map/ppermute | solution.py:22
  54.7 0.0 copy-start
  54.7 0.0 copy-start.1
  54.7 0.7 %copy-done = f32[512,128]{1,0:T(8,128)} copy-done((f32[512,128]{1,0:T(8,128)}, f32[512,128]{1,0:T(8,128)S(1)}, u32[]{:S(2)}) %copy-start) | copy-done | bytes 262168
  55.4 0.1 copy-done.1
  (10 shorter events, 0.2 us)
Async XLA Ops:
  0.6 10.1 %collective-permute-start = (bf16[512,128]{1,0:T(8,128)(2,1)}, bf16[512,128]{1,0:T(8,128)(2,1)S(1)}, u32[]{:S(2)}, u32[]{:S(2)}) collective-permute-start(bf16[512,128]{1,0:T(8,128)(2,1)} %bitcast.6), channel_id=1, source_target_pairs={{0,8},{1,9},{16,24},{17,25}} | collective-permute-start | bytes 393224 | tf_op jit(solution)/shard_map/ppermute | solution.py:22
  6.6 5.9 %collective-permute-start.2 = (bf16[512,128]{1,0:T(8,128)(2,1)}, bf16[512,128]{1,0:T(8,128)(2,1)S(1)}, u32[]{:S(2)}, u32[]{:S(2)}) collective-permute-start(bf16[512,128]{1,0:T(8,128)(2,1)} %bitcast.8), channel_id=1, source_target_pairs={{0,10},{1,11},{16,26},{17,27}} | collective-permute-start | bytes 393224 | tf_op jit(solution)/shard_map/ppermute | solution.py:22
  8.2 4.4 %collective-permute-start.1 = (bf16[512,128]{1,0:T(8,128)(2,1)}, bf16[512,128]{1,0:T(8,128)(2,1)S(1)}, u32[]{:S(2)}, u32[]{:S(2)}) collective-permute-start(bf16[512,128]{1,0:T(8,128)(2,1)} %bitcast.9), channel_id=1, source_target_pairs={{0,2},{1,3},{16,18},{17,19}} | collective-permute-start | bytes 393224 | tf_op jit(solution)/shard_map/ppermute | solution.py:22
  10.8 3.5 %collective-permute-start.4 = (bf16[256,128]{1,0:T(8,128)(2,1)S(1)}, bf16[256,128]{1,0:T(8,128)(2,1)S(1)}, u32[]{:S(2)}, u32[]{:S(2)}) collective-permute-start(bf16[256,128]{1,0:T(8,128)(2,1)S(1)} %get-tuple-element.70), channel_id=1, source_target_pairs={{2,10},{4,12},{6,14},{3,11},{5,13},{7,15},{18,26},{20,28},{22,30},... | collective-permute-start | bytes 196616 | tf_op jit(solution)/shard_map/ppermute | solution.py:22
  11.4 2.8 %collective-permute-start.3 = (bf16[256,128]{1,0:T(8,128)(2,1)S(1)}, bf16[256,128]{1,0:T(8,128)(2,1)S(1)}, u32[]{:S(2)}, u32[]{:S(2)}) collective-permute-start(bf16[256,128]{1,0:T(8,128)(2,1)S(1)} %get-tuple-element.70), channel_id=1, source_target_pairs={{2,14},{3,15},{18,30},{19,31}} | collective-permute-start | bytes 196616 | tf_op jit(solution)/shard_map/ppermute | solution.py:22
  14.3 7.2 %collective-permute-start.5 = (bf16[768,128]{1,0:T(8,128)(2,1)S(1)}, bf16[768,128]{1,0:T(8,128)(2,1)S(1)}, u32[]{:S(2)}, u32[]{:S(2)}) collective-permute-start(bf16[768,128]{1,0:T(8,128)(2,1)S(1)} %pad_maximum_fusion), channel_id=1, source_target_pairs={{0,4},{2,6},{4,8},{6,10},{8,12},{10,14},{1,5},{3,7},{5,9},{7,11},{... | collective-permute-start | bytes 589832 | tf_op jit(solution)/shard_map/ppermute | solution.py:22
  17.2 5.2 %collective-permute-start.6 = (bf16[512,128]{1,0:T(8,128)(2,1)S(1)}, bf16[512,128]{1,0:T(8,128)(2,1)S(1)}, u32[]{:S(2)}, u32[]{:S(2)}) collective-permute-start(bf16[512,128]{1,0:T(8,128)(2,1)S(1)} %maximum_select_fusion), channel_id=1, source_target_pairs={{0,2},{2,0},{4,6},{6,4},{8,10},{10,8},{12,14},{14,12},{1,3},{3,1},... | collective-permute-start | bytes 393224 | tf_op jit(solution)/shard_map/ppermute | solution.py:22
  22.4 5.7 %collective-permute-start.7 = (bf16[768,128]{1,0:T(8,128)(2,1)S(1)}, bf16[768,128]{1,0:T(8,128)(2,1)S(1)}, u32[]{:S(2)}, u32[]{:S(2)}) collective-permute-start(bf16[768,128]{1,0:T(8,128)(2,1)S(1)} %pad_maximum_fusion.1), channel_id=1, source_target_pairs={{0,2},{2,0},{4,6},{6,4},{8,10},{10,8},{12,14},{14,12},{1,3},{3,1},... | collective-permute-start | bytes 589832 | tf_op jit(solution)/shard_map/ppermute | solution.py:22
  30.7 5.3 %collective-permute-start.8 = (bf16[512,128]{1,0:T(8,128)(2,1)S(1)}, bf16[512,128]{1,0:T(8,128)(2,1)S(1)}, u32[]{:S(2)}, u32[]{:S(2)}) collective-permute-start(bf16[512,128]{1,0:T(8,128)(2,1)S(1)} %get-tuple-element.88), channel_id=1, source_target_pairs={{0,2},{2,0},{4,6},{6,4},{8,10},{10,8},{12,14},{14,12},{1,3},{3,1},... | collective-permute-start | bytes 393224 | tf_op jit(solution)/shard_map/ppermute | solution.py:22
  33.2 9.2 %collective-permute-start.12 = (bf16[768,128]{1,0:T(8,128)(2,1)S(1)}, bf16[768,128]{1,0:T(8,128)(2,1)S(1)}, u32[]{:S(2)}, u32[]{:S(2)}) collective-permute-start(bf16[768,128]{1,0:T(8,128)(2,1)S(1)} %get-tuple-element.93), channel_id=1, source_target_pairs={{0,2},{2,0},{4,6},{6,4},{8,10},{10,8},{12,14},{14,12},{1,3},{3,1},... | collective-permute-start | bytes 589832 | tf_op jit(solution)/shard_map/ppermute | solution.py:22
  36.1 9.2 %collective-permute-start.11 = (bf16[512,128]{1,0:T(8,128)(2,1)S(1)}, bf16[512,128]{1,0:T(8,128)(2,1)S(1)}, u32[]{:S(2)}, u32[]{:S(2)}) collective-permute-start(bf16[512,128]{1,0:T(8,128)(2,1)S(1)} %add_convert_fusion.1), channel_id=1, source_target_pairs={{4,0},{6,2},{5,1},{7,3},{20,16},{22,18},{21,17},{23,19}} | collective-permute-start | bytes 393224 | tf_op jit(solution)/shard_map/ppermute | solution.py:22
  37.4 9.6 %collective-permute-start.10 = (bf16[512,128]{1,0:T(8,128)(2,1)S(1)}, bf16[512,128]{1,0:T(8,128)(2,1)S(1)}, u32[]{:S(2)}, u32[]{:S(2)}) collective-permute-start(bf16[512,128]{1,0:T(8,128)(2,1)S(1)} %add_convert_fusion.1), channel_id=1, source_target_pairs={{8,0},{10,2},{9,1},{11,3},{24,16},{26,18},{25,17},{27,19}} | collective-permute-start | bytes 393224 | tf_op jit(solution)/shard_map/ppermute | solution.py:22
  38.7 9.0 %collective-permute-start.9 = (bf16[512,128]{1,0:T(8,128)(2,1)S(1)}, bf16[512,128]{1,0:T(8,128)(2,1)S(1)}, u32[]{:S(2)}, u32[]{:S(2)}) collective-permute-start(bf16[512,128]{1,0:T(8,128)(2,1)S(1)} %add_convert_fusion.1), channel_id=1, source_target_pairs={{12,0},{14,2},{13,1},{15,3},{28,16},{30,18},{29,17},{31,19}} | collective-permute-start | bytes 393224 | tf_op jit(solution)/shard_map/ppermute | solution.py:22
  42.4 6.7 %collective-permute-start.14 = (bf16[256,128]{1,0:T(8,128)(2,1)S(1)}, bf16[256,128]{1,0:T(8,128)(2,1)S(1)}, u32[]{:S(2)}, u32[]{:S(2)}) collective-permute-start(bf16[256,128]{1,0:T(8,128)(2,1)S(1)} %get-tuple-element.95), channel_id=1, source_target_pairs={{10,2},{12,4},{14,6},{11,3},{13,5},{15,7},{26,18},{28,20},{30,22},... | collective-permute-start | bytes 196616 | tf_op jit(solution)/shard_map/ppermute | solution.py:22
  43.1 6.0 %collective-permute-start.13 = (bf16[256,128]{1,0:T(8,128)(2,1)S(1)}, bf16[256,128]{1,0:T(8,128)(2,1)S(1)}, u32[]{:S(2)}, u32[]{:S(2)}) collective-permute-start(bf16[256,128]{1,0:T(8,128)(2,1)S(1)} %get-tuple-element.99), channel_id=1, source_target_pairs={{14,2},{15,3},{30,18},{31,19}} | collective-permute-start | bytes 196616 | tf_op jit(solution)/shard_map/ppermute | solution.py:22
  45.3 3.8 %collective-permute-start.15 = (bf16[256,128]{1,0:T(8,128)(2,1)S(1)}, bf16[256,128]{1,0:T(8,128)(2,1)S(1)}, u32[]{:S(2)}, u32[]{:S(2)}) collective-permute-start(bf16[256,128]{1,0:T(8,128)(2,1)S(1)} %get-tuple-element.100), channel_id=1, source_target_pairs={{6,2},{8,4},{10,6},{12,8},{14,10},{7,3},{9,5},{11,7},{13,9},{15,11... | collective-permute-start | bytes 196616 | tf_op jit(solution)/shard_map/ppermute | solution.py:22
  47.8 6.9 %collective-permute-start.16 = (bf16[512,128]{1,0:T(8,128)(2,1)S(1)}, bf16[512,128]{1,0:T(8,128)(2,1)S(1)}, u32[]{:S(2)}, u32[]{:S(2)}) collective-permute-start(bf16[512,128]{1,0:T(8,128)(2,1)S(1)} %get-tuple-element.98), channel_id=1, source_target_pairs={{2,0},{3,1},{18,16},{19,17}} | collective-permute-start | bytes 393224 | tf_op jit(solution)/shard_map/ppermute | solution.py:22
  54.7 0.7 %copy-start = (f32[512,128]{1,0:T(8,128)}, f32[512,128]{1,0:T(8,128)S(1)}, u32[]{:S(2)}) copy-start(f32[512,128]{1,0:T(8,128)S(1)} %get-tuple-element.104) | copy-start | bytes 786436
  54.7 0.8 %copy-start.1 = (f32[512,128]{1,0:T(8,128)}, f32[512,128]{1,0:T(8,128)S(1)}, u32[]{:S(2)}) copy-start(f32[512,128]{1,0:T(8,128)S(1)} %get-tuple-element.105) | copy-start | bytes 786436

commit v21 on v20

--- a/solution.py
+++ b/solution.py
@@ -145,7 +145,7 @@
     send_ref, keep_ref, kh, ds_ref, p_behind, terms, vh, p_ref, grads, wide = refs[8:]
     tokens = TD * TILE
     front = CAP * TILE
-    columns = CHUNK * 8
+    columns = 2 * CHUNK * 8
     rate = scale * math.log2(math.e)
     device = lax.axis_index("node")
 
@@ -156,7 +156,7 @@
             split_heads(block_ref[at : at + front * heads_kv], heads_ref, tokens + k * front, front, heads_kv, wide)
 
     for head in range(heads_kv):
-        for c in range(tokens // CHUNK):
+        for c in range(tokens * 8 // columns):
             span = slice(c * columns, (c + 1) * columns)
             s = outer_product(kh[head], qh[head, span])
             dp = outer_product(vh[head], gh[head, span])

time: 55.9 us -> 56.2 us (level)
  no operation moved by 1% of the time
where the time goes in v21:
time: 56.2 us; the launch traced here: 55.8 us
  starting transfers between devices  24.6 us (44%)
  waiting for transfers between devices  18 us (32%)
  Pallas kernels  11.1 us (20%)
  between operations  0.92 us (2%)
  local copies, waits for them, and re-layouts  0.78 us (1%)
    ppermute x17, starting transfers between devices, permuted(): return lax.ppermute(block, 'node', route)  24.6 us
    ppermute x17, waiting for transfers between devices, permuted(): return lax.ppermute(block, 'node', route)  18 us
    pallas_call x6, Pallas kernels, call(): pl.pallas_call(kernel, in_specs=[place] * len(operands), out_specs=[VMEM]...  11.1 us
  transfers between devices with their start and end apart: 17, of which 11 were waited for; matrix products, arithmetic and copies ran while one was open for 1% of the time, Pallas kernels for 15%

profile of v21, /device:TPU:0, one launch (start us, length us, event | category | flops | bytes accessed | tf_op | source)
XLA Modules:
  0.0 55.8 jit_solution(9508230893610682973)
XLA Ops:
  0.6 5.9 %collective-permute-start = (bf16[512,128]{1,0:T(8,128)(2,1)}, bf16[512,128]{1,0:T(8,128)(2,1)S(1)}, u32[]{:S(2)}, u32[]{:S(2)}) collective-permute-start(bf16[512,128]{1,0:T(8,128)(2,1)} %bitcast.6), channel_id=1, source_target_pairs={{0,8},{1,9},{16,24},{17,25}} | collective-permute-start | bytes 393224 | tf_op jit(solution)/shard_map/ppermute | solution.py:22
  6.6 1.6 %collective-permute-start.2 = (bf16[512,128]{1,0:T(8,128)(2,1)}, bf16[512,128]{1,0:T(8,128)(2,1)S(1)}, u32[]{:S(2)}, u32[]{:S(2)}) collective-permute-start(bf16[512,128]{1,0:T(8,128)(2,1)} %bitcast.8), channel_id=1, source_target_pairs={{0,10},{1,11},{16,26},{17,27}} | collective-permute-start | bytes 393224 | tf_op jit(solution)/shard_map/ppermute | solution.py:22
  8.2 1.3 %collective-permute-start.1 = (bf16[512,128]{1,0:T(8,128)(2,1)}, bf16[512,128]{1,0:T(8,128)(2,1)S(1)}, u32[]{:S(2)}, u32[]{:S(2)}) collective-permute-start(bf16[512,128]{1,0:T(8,128)(2,1)} %bitcast.9), channel_id=1, source_target_pairs={{0,2},{1,3},{16,18},{17,19}} | collective-permute-start | bytes 393224 | tf_op jit(solution)/shard_map/ppermute | solution.py:22
  9.5 1.2 %load.1 = (bf16[256,128]{1,0:T(8,128)(2,1)S(1)}, bf16[512,128]{1,0:T(8,128)(2,1)S(1)}, bf16[4,128,128]{2,1,0:T(8,128)(2,1)S(1)}, bf16[4,128,128]{2,1,0:T(8,128)(...) custom-call(s32[64]{0:T(128)} %refs_0_.1, s32[64]{0:T(128)} %refs_1_.1, bf16[512,128]{1,0:T(8,128)(2,1)} %bitcast.7, ...), custom_call_target="tpu_custom_call" | custom-call | flops 1048576 | bytes 983552 | tf_op jit(solution)/shard_map/load/pallas_call | solution.py:265
  10.7 0.1 collective-permute-done
  10.8 0.7 %collective-permute-start.4 = (bf16[256,128]{1,0:T(8,128)(2,1)S(1)}, bf16[256,128]{1,0:T(8,128)(2,1)S(1)}, u32[]{:S(2)}, u32[]{:S(2)}) collective-permute-start(bf16[256,128]{1,0:T(8,128)(2,1)S(1)} %get-tuple-element.70), channel_id=1, source_target_pairs={{2,10},{4,12},{6,14},{3,11},{5,13},{7,15},{18,26},{20,28},{22,30},... | collective-permute-start | bytes 196616 | tf_op jit(solution)/shard_map/ppermute | solution.py:22
  11.4 0.7 %collective-permute-start.3 = (bf16[256,128]{1,0:T(8,128)(2,1)S(1)}, bf16[256,128]{1,0:T(8,128)(2,1)S(1)}, u32[]{:S(2)}, u32[]{:S(2)}) collective-permute-start(bf16[256,128]{1,0:T(8,128)(2,1)S(1)} %get-tuple-element.70), channel_id=1, source_target_pairs={{2,14},{3,15},{18,30},{19,31}} | collective-permute-start | bytes 196616 | tf_op jit(solution)/shard_map/ppermute | solution.py:22
  12.1 0.4 collective-permute-done.2
  12.5 0.1 collective-permute-done.1
  12.5 0.1 add_convert_fusion.2
  12.6 1.6 %pack.1 = (bf16[4,1024,128]{2,1,0:T(8,128)(2,1)S(1)}, bf16[4,1024,128]{2,1,0:T(8,128)(2,1)S(1)}) custom-call(bf16[128,32,128]{2,1,0:T(8,128)(2,1)} %q_ref, bf16[128,32,128]{2,1,0:T(8,128)(2,1)} %g_ref.1), custom_call_target="tpu_custom_call" | custom-call | flops 1048576 | bytes 4194304 | tf_op jit(solution)/shard_map/pack/pallas_call | solution.py:265
  14.3 0.0 collective-permute-done.4.refs_7_
  14.3 0.0 collective-permute-done.3.refs_8_
  14.3 2.8 %collective-permute-start.5 = (bf16[768,128]{1,0:T(8,128)(2,1)S(1)}, bf16[768,128]{1,0:T(8,128)(2,1)S(1)}, u32[]{:S(2)}, u32[]{:S(2)}) collective-permute-start(bf16[768,128]{1,0:T(8,128)(2,1)S(1)} %pad_maximum_fusion), channel_id=1, source_target_pairs={{0,4},{2,6},{4,8},{6,10},{8,12},{10,14},{1,5},{3,7},{5,9},{7,11},{... | collective-permute-start | bytes 589832 | tf_op jit(solution)/shard_map/ppermute | solution.py:22
  17.2 1.3 %collective-permute-start.6 = (bf16[512,128]{1,0:T(8,128)(2,1)S(1)}, bf16[512,128]{1,0:T(8,128)(2,1)S(1)}, u32[]{:S(2)}, u32[]{:S(2)}) collective-permute-start(bf16[512,128]{1,0:T(8,128)(2,1)S(1)} %maximum_select_fusion), channel_id=1, source_target_pairs={{0,2},{2,0},{4,6},{6,4},{8,10},{10,8},{12,14},{14,12},{1,3},{3,1},... | collective-permute-start | bytes 393224 | tf_op jit(solution)/shard_map/ppermute | solution.py:22
  18.4 3.0 %collective-permute-done.5.refs_5_ = bf16[768,128]{1,0:T(8,128)(2,1)S(1)} collective-permute-done((bf16[768,128]{1,0:T(8,128)(2,1)S(1)}, bf16[768,128]{1,0:T(8,128)(2,1)S(1)}, u32[]{:S(2)}, u32[]{:S(2)}) %collective-permute-start.5) | collective-permute-done | bytes 196640 | tf_op jit(solution)/shard_map/ppermute | solution.py:22
  21.5 0.9 %collective-permute-done.6.refs_6_ = bf16[512,128]{1,0:T(8,128)(2,1)S(1)} collective-permute-done((bf16[512,128]{1,0:T(8,128)(2,1)S(1)}, bf16[512,128]{1,0:T(8,128)(2,1)S(1)}, u32[]{:S(2)}, u32[]{:S(2)}) %collective-permute-start.6) | collective-permute-done | bytes 131104 | tf_op jit(solution)/shard_map/ppermute | solution.py:22
  22.4 1.0 %collective-permute-start.7 = (bf16[768,128]{1,0:T(8,128)(2,1)S(1)}, bf16[768,128]{1,0:T(8,128)(2,1)S(1)}, u32[]{:S(2)}, u32[]{:S(2)}) collective-permute-start(bf16[768,128]{1,0:T(8,128)(2,1)S(1)} %pad_maximum_fusion.1), channel_id=1, source_target_pairs={{0,2},{2,0},{4,6},{6,4},{8,10},{10,8},{12,14},{14,12},{1,3},{3,1},... | collective-permute-start | bytes 589832 | tf_op jit(solution)/shard_map/ppermute | solution.py:22
  23.4 1.6 %early.1 = (bf16[4,288,128]{2,1,0:T(8,128)(2,1)S(1)}, f32[4,288,1024]{2,1,0:T(8,128)S(1)}, f32[4,288,1024]{2,1,0:T(8,128)S(1)}, f32[4,8,1024]{2,1,0:T(8,128)S(1)}) custom-call(bf16[4,128,128]{2,1,0:T(8,128)(2,1)S(1)} %get-tuple-element.75.refs_0_, bf16[4,128,128]{2,1,0:T(8,128)(2,1)S(1)} %get-tuple-element.76.refs_1_, ...), custom_call_target="tpu_custom_call" | custom-call | flops 603979776 | bytes 12910592 | tf_op jit(solution)/shard_map/early/pallas_call | solution.py:265
  25.0 3.0 %collective-permute-done.7.refs_7_ = bf16[768,128]{1,0:T(8,128)(2,1)S(1)} collective-permute-done((bf16[768,128]{1,0:T(8,128)(2,1)S(1)}, bf16[768,128]{1,0:T(8,128)(2,1)S(1)}, u32[]{:S(2)}, u32[]{:S(2)}) %collective-permute-start.7) | collective-permute-done | bytes 196640 | tf_op jit(solution)/shard_map/ppermute | solution.py:22
  28.1 2.9 %probs.1 = (bf16[512,128]{1,0:T(8,128)(2,1)S(1)}, bf16[512,128]{1,0:T(8,128)(2,1)S(1)}, bf16[4,160,128]{2,1,0:T(8,128)(2,1)S(1)}, bf16[4,160,1024]{2,1,0:T(8,128...) custom-call(bf16[512,128]{1,0:T(8,128)(2,1)S(1)} %get-tuple-element.103.refs_0_, ...), custom_call_target="tpu_custom_call" | custom-call | flops 671088640 | bytes 5079040 | tf_op jit(solution)/shard_map/probs/pallas_call | solution.py:265
  31.0 1.1 %collective-permute-start.8 = (bf16[512,128]{1,0:T(8,128)(2,1)S(1)}, bf16[512,128]{1,0:T(8,128)(2,1)S(1)}, u32[]{:S(2)}, u32[]{:S(2)}) collective-permute-start(bf16[512,128]{1,0:T(8,128)(2,1)S(1)} %get-tuple-element.88), channel_id=1, source_target_pairs={{0,2},{2,0},{4,6},{6,4},{8,10},{10,8},{12,14},{14,12},{1,3},{3,1},... | collective-permute-start | bytes 393224 | tf_op jit(solution)/shard_map/ppermute | solution.py:22
  32.1 1.4 %windows.1 = (bf16[768,128]{1,0:T(8,128)(2,1)S(1)}, bf16[768,128]{1,0:T(8,128)(2,1)S(1)}, bf16[4,288,1024]{2,1,0:T(8,128)(2,1)S(1)}, bf16[4,128,1024]{2,1,0:T(8,128)(2,1)S(1)}) custom-call(bf16[4,1024,128]{2,1,0:T(8,128)(2,1)S(1)} %get-tuple-element.65.refs_2_.refs_0_, bf16[4,1024,128]{2,1,0:T(8,128)(2,1)S(1)} %get-tuple-element.66.refs_3_.refs_1_, ...), custom_call_target="tpu_custom_call" | custom-call | flops 402653184 | bytes 17039360 | tf_op jit(solution)/shard_map/windows/pallas_call | solution.py:265
  33.5 1.1 %collective-permute-start.12 = (bf16[768,128]{1,0:T(8,128)(2,1)S(1)}, bf16[768,128]{1,0:T(8,128)(2,1)S(1)}, u32[]{:S(2)}, u32[]{:S(2)}) collective-permute-start(bf16[768,128]{1,0:T(8,128)(2,1)S(1)} %get-tuple-element.93), channel_id=1, source_target_pairs={{0,2},{2,0},{4,6},{6,4},{8,10},{10,8},{12,14},{14,12},{1,3},{3,1},... | collective-permute-start | bytes 589832 | tf_op jit(solution)/shard_map/ppermute | solution.py:22
  34.5 1.8 %collective-permute-done.8 = bf16[512,128]{1,0:T(8,128)(2,1)S(1)} collective-permute-done((bf16[512,128]{1,0:T(8,128)(2,1)S(1)}, bf16[512,128]{1,0:T(8,128)(2,1)S(1)}, u32[]{:S(2)}, u32[]{:S(2)}) %collective-permute-start.8) | collective-permute-done | bytes 131104 | tf_op jit(solution)/shard_map/ppermute | solution.py:22
  36.4 1.3 %collective-permute-start.11 = (bf16[512,128]{1,0:T(8,128)(2,1)S(1)}, bf16[512,128]{1,0:T(8,128)(2,1)S(1)}, u32[]{:S(2)}, u32[]{:S(2)}) collective-permute-start(bf16[512,128]{1,0:T(8,128)(2,1)S(1)} %add_convert_fusion.1), channel_id=1, source_target_pairs={{4,0},{6,2},{5,1},{7,3},{20,16},{22,18},{21,17},{23,19}} | collective-permute-start | bytes 393224 | tf_op jit(solution)/shard_map/ppermute | solution.py:22
  37.7 1.3 %collective-permute-start.10 = (bf16[512,128]{1,0:T(8,128)(2,1)S(1)}, bf16[512,128]{1,0:T(8,128)(2,1)S(1)}, u32[]{:S(2)}, u32[]{:S(2)}) collective-permute-start(bf16[512,128]{1,0:T(8,128)(2,1)S(1)} %add_convert_fusion.1), channel_id=1, source_target_pairs={{8,0},{10,2},{9,1},{11,3},{24,16},{26,18},{25,17},{27,19}} | collective-permute-start | bytes 393224 | tf_op jit(solution)/shard_map/ppermute | solution.py:22
  39.0 1.3 %collective-permute-start.9 = (bf16[512,128]{1,0:T(8,128)(2,1)S(1)}, bf16[512,128]{1,0:T(8,128)(2,1)S(1)}, u32[]{:S(2)}, u32[]{:S(2)}) collective-permute-start(bf16[512,128]{1,0:T(8,128)(2,1)S(1)} %add_convert_fusion.1), channel_id=1, source_target_pairs={{12,0},{14,2},{13,1},{15,3},{28,16},{30,18},{29,17},{31,19}} | collective-permute-start | bytes 393224 | tf_op jit(solution)/shard_map/ppermute | solution.py:22
  40.3 2.4 %grads.1 = (bf16[128,32,128]{2,1,0:T(8,128)(2,1)}, f32[512,128]{1,0:T(8,128)S(1)}, f32[512,128]{1,0:T(8,128)S(1)}) custom-call(bf16[4,1024,128]{2,1,0:T(8,128)(2,1)S(1)} %get-tuple-element.65.refs_2_.refs_0_, bf16[4,1024,128]{2,1,0:T(8,128)(2,1)S(1)} %get-tuple-element.66.refs_3_.refs_1_, bf16[4,160,128]{2,1,0:T(8,128)(2,1)S(1)} %get-tuple-element.78.refs_2_, ...), custom_call_target="tpu_custom_call" | custom-call | flops 469762048 | bytes 8847360 | tf_op jit(solution)/shard_map/grads/pallas_call | solution.py:265
  42.6 0.0 collective-permute-done.12
  42.7 0.1 add_convert_fusion.5
  42.7 0.7 %collective-permute-start.14 = (bf16[256,128]{1,0:T(8,128)(2,1)S(1)}, bf16[256,128]{1,0:T(8,128)(2,1)S(1)}, u32[]{:S(2)}, u32[]{:S(2)}) collective-permute-start(bf16[256,128]{1,0:T(8,128)(2,1)S(1)} %get-tuple-element.95), channel_id=1, source_target_pairs={{10,2},{12,4},{14,6},{11,3},{13,5},{15,7},{26,18},{28,20},{30,22},... | collective-permute-start | bytes 196616 | tf_op jit(solution)/shard_map/ppermute | solution.py:22
  43.4 0.7 %collective-permute-start.13 = (bf16[256,128]{1,0:T(8,128)(2,1)S(1)}, bf16[256,128]{1,0:T(8,128)(2,1)S(1)}, u32[]{:S(2)}, u32[]{:S(2)}) collective-permute-start(bf16[256,128]{1,0:T(8,128)(2,1)S(1)} %get-tuple-element.99), channel_id=1, source_target_pairs={{14,2},{15,3},{30,18},{31,19}} | collective-permute-start | bytes 196616 | tf_op jit(solution)/shard_map/ppermute | solution.py:22
  44.1 1.5 %collective-permute-done.11 = bf16[512,128]{1,0:T(8,128)(2,1)S(1)} collective-permute-done((bf16[512,128]{1,0:T(8,128)(2,1)S(1)}, bf16[512,128]{1,0:T(8,128)(2,1)S(1)}, u32[]{:S(2)}, u32[]{:S(2)}) %collective-permute-start.11) | collective-permute-done | bytes 131104 | tf_op jit(solution)/shard_map/ppermute | solution.py:22
  45.6 0.7 %collective-permute-start.15 = (bf16[256,128]{1,0:T(8,128)(2,1)S(1)}, bf16[256,128]{1,0:T(8,128)(2,1)S(1)}, u32[]{:S(2)}, u32[]{:S(2)}) collective-permute-start(bf16[256,128]{1,0:T(8,128)(2,1)S(1)} %get-tuple-element.100), channel_id=1, source_target_pairs={{6,2},{8,4},{10,6},{12,8},{14,10},{7,3},{9,5},{11,7},{13,9},{15,11... | collective-permute-start | bytes 196616 | tf_op jit(solution)/shard_map/ppermute | solution.py:22
  46.3 1.0 %collective-permute-done.10 = bf16[512,128]{1,0:T(8,128)(2,1)S(1)} collective-permute-done((bf16[512,128]{1,0:T(8,128)(2,1)S(1)}, bf16[512,128]{1,0:T(8,128)(2,1)S(1)}, u32[]{:S(2)}, u32[]{:S(2)}) %collective-permute-start.10) | collective-permute-done | bytes 131104 | tf_op jit(solution)/shard_map/ppermute | solution.py:22
  47.3 0.8 %collective-permute-done.9 = bf16[512,128]{1,0:T(8,128)(2,1)S(1)} collective-permute-done((bf16[512,128]{1,0:T(8,128)(2,1)S(1)}, bf16[512,128]{1,0:T(8,128)(2,1)S(1)}, u32[]{:S(2)}, u32[]{:S(2)}) %collective-permute-start.9) | collective-permute-done | bytes 131104 | tf_op jit(solution)/shard_map/ppermute | solution.py:22
  48.0 0.1 select_add_fusion.1
  48.1 1.3 %collective-permute-start.16 = (bf16[512,128]{1,0:T(8,128)(2,1)S(1)}, bf16[512,128]{1,0:T(8,128)(2,1)S(1)}, u32[]{:S(2)}, u32[]{:S(2)}) collective-permute-start(bf16[512,128]{1,0:T(8,128)(2,1)S(1)} %get-tuple-element.98), channel_id=1, source_target_pairs={{2,0},{3,1},{18,16},{19,17}} | collective-permute-start | bytes 393224 | tf_op jit(solution)/shard_map/ppermute | solution.py:22
  49.4 0.0 collective-permute-done.14
  49.4 0.0 collective-permute-done.13
  49.4 0.0 collective-permute-done.15
  49.5 5.5 %collective-permute-done.16 = bf16[512,128]{1,0:T(8,128)(2,1)S(1)} collective-permute-done((bf16[512,128]{1,0:T(8,128)(2,1)S(1)}, bf16[512,128]{1,0:T(8,128)(2,1)S(1)}, u32[]{:S(2)}, u32[]{:S(2)}) %collective-permute-start.16) | collective-permute-done | bytes 131104 | tf_op jit(solution)/shard_map/ppermute | solution.py:22
  55.1 0.0 copy-start
  55.1 0.0 copy-start.1
  55.1 0.7 %copy-done = f32[512,128]{1,0:T(8,128)} copy-done((f32[512,128]{1,0:T(8,128)}, f32[512,128]{1,0:T(8,128)S(1)}, u32[]{:S(2)}) %copy-start) | copy-done | bytes 262168
  55.8 0.1 copy-done.1
  (10 shorter events, 0.2 us)
Async XLA Ops:
  0.6 10.1 %collective-permute-start = (bf16[512,128]{1,0:T(8,128)(2,1)}, bf16[512,128]{1,0:T(8,128)(2,1)S(1)}, u32[]{:S(2)}, u32[]{:S(2)}) collective-permute-start(bf16[512,128]{1,0:T(8,128)(2,1)} %bitcast.6), channel_id=1, source_target_pairs={{0,8},{1,9},{16,24},{17,25}} | collective-permute-start | bytes 393224 | tf_op jit(solution)/shard_map/ppermute | solution.py:22
  6.6 5.9 %collective-permute-start.2 = (bf16[512,128]{1,0:T(8,128)(2,1)}, bf16[512,128]{1,0:T(8,128)(2,1)S(1)}, u32[]{:S(2)}, u32[]{:S(2)}) collective-permute-start(bf16[512,128]{1,0:T(8,128)(2,1)} %bitcast.8), channel_id=1, source_target_pairs={{0,10},{1,11},{16,26},{17,27}} | collective-permute-start | bytes 393224 | tf_op jit(solution)/shard_map/ppermute | solution.py:22
  8.2 4.4 %collective-permute-start.1 = (bf16[512,128]{1,0:T(8,128)(2,1)}, bf16[512,128]{1,0:T(8,128)(2,1)S(1)}, u32[]{:S(2)}, u32[]{:S(2)}) collective-permute-start(bf16[512,128]{1,0:T(8,128)(2,1)} %bitcast.9), channel_id=1, source_target_pairs={{0,2},{1,3},{16,18},{17,19}} | collective-permute-start | bytes 393224 | tf_op jit(solution)/shard_map/ppermute | solution.py:22
  10.8 3.5 %collective-permute-start.4 = (bf16[256,128]{1,0:T(8,128)(2,1)S(1)}, bf16[256,128]{1,0:T(8,128)(2,1)S(1)}, u32[]{:S(2)}, u32[]{:S(2)}) collective-permute-start(bf16[256,128]{1,0:T(8,128)(2,1)S(1)} %get-tuple-element.70), channel_id=1, source_target_pairs={{2,10},{4,12},{6,14},{3,11},{5,13},{7,15},{18,26},{20,28},{22,30},... | collective-permute-start | bytes 196616 | tf_op jit(solution)/shard_map/ppermute | solution.py:22
  11.4 2.8 %collective-permute-start.3 = (bf16[256,128]{1,0:T(8,128)(2,1)S(1)}, bf16[256,128]{1,0:T(8,128)(2,1)S(1)}, u32[]{:S(2)}, u32[]{:S(2)}) collective-permute-start(bf16[256,128]{1,0:T(8,128)(2,1)S(1)} %get-tuple-element.70), channel_id=1, source_target_pairs={{2,14},{3,15},{18,30},{19,31}} | collective-permute-start | bytes 196616 | tf_op jit(solution)/shard_map/ppermute | solution.py:22
  14.3 7.2 %collective-permute-start.5 = (bf16[768,128]{1,0:T(8,128)(2,1)S(1)}, bf16[768,128]{1,0:T(8,128)(2,1)S(1)}, u32[]{:S(2)}, u32[]{:S(2)}) collective-permute-start(bf16[768,128]{1,0:T(8,128)(2,1)S(1)} %pad_maximum_fusion), channel_id=1, source_target_pairs={{0,4},{2,6},{4,8},{6,10},{8,12},{10,14},{1,5},{3,7},{5,9},{7,11},{... | collective-permute-start | bytes 589832 | tf_op jit(solution)/shard_map/ppermute | solution.py:22
  17.2 5.2 %collective-permute-start.6 = (bf16[512,128]{1,0:T(8,128)(2,1)S(1)}, bf16[512,128]{1,0:T(8,128)(2,1)S(1)}, u32[]{:S(2)}, u32[]{:S(2)}) collective-permute-start(bf16[512,128]{1,0:T(8,128)(2,1)S(1)} %maximum_select_fusion), channel_id=1, source_target_pairs={{0,2},{2,0},{4,6},{6,4},{8,10},{10,8},{12,14},{14,12},{1,3},{3,1},... | collective-permute-start | bytes 393224 | tf_op jit(solution)/shard_map/ppermute | solution.py:22
  22.4 5.7 %collective-permute-start.7 = (bf16[768,128]{1,0:T(8,128)(2,1)S(1)}, bf16[768,128]{1,0:T(8,128)(2,1)S(1)}, u32[]{:S(2)}, u32[]{:S(2)}) collective-permute-start(bf16[768,128]{1,0:T(8,128)(2,1)S(1)} %pad_maximum_fusion.1), channel_id=1, source_target_pairs={{0,2},{2,0},{4,6},{6,4},{8,10},{10,8},{12,14},{14,12},{1,3},{3,1},... | collective-permute-start | bytes 589832 | tf_op jit(solution)/shard_map/ppermute | solution.py:22
  31.0 5.3 %collective-permute-start.8 = (bf16[512,128]{1,0:T(8,128)(2,1)S(1)}, bf16[512,128]{1,0:T(8,128)(2,1)S(1)}, u32[]{:S(2)}, u32[]{:S(2)}) collective-permute-start(bf16[512,128]{1,0:T(8,128)(2,1)S(1)} %get-tuple-element.88), channel_id=1, source_target_pairs={{0,2},{2,0},{4,6},{6,4},{8,10},{10,8},{12,14},{14,12},{1,3},{3,1},... | collective-permute-start | bytes 393224 | tf_op jit(solution)/shard_map/ppermute | solution.py:22
  33.5 9.2 %collective-permute-start.12 = (bf16[768,128]{1,0:T(8,128)(2,1)S(1)}, bf16[768,128]{1,0:T(8,128)(2,1)S(1)}, u32[]{:S(2)}, u32[]{:S(2)}) collective-permute-start(bf16[768,128]{1,0:T(8,128)(2,1)S(1)} %get-tuple-element.93), channel_id=1, source_target_pairs={{0,2},{2,0},{4,6},{6,4},{8,10},{10,8},{12,14},{14,12},{1,3},{3,1},... | collective-permute-start | bytes 589832 | tf_op jit(solution)/shard_map/ppermute | solution.py:22
  36.4 9.2 %collective-permute-start.11 = (bf16[512,128]{1,0:T(8,128)(2,1)S(1)}, bf16[512,128]{1,0:T(8,128)(2,1)S(1)}, u32[]{:S(2)}, u32[]{:S(2)}) collective-permute-start(bf16[512,128]{1,0:T(8,128)(2,1)S(1)} %add_convert_fusion.1), channel_id=1, source_target_pairs={{4,0},{6,2},{5,1},{7,3},{20,16},{22,18},{21,17},{23,19}} | collective-permute-start | bytes 393224 | tf_op jit(solution)/shard_map/ppermute | solution.py:22
  37.7 9.6 %collective-permute-start.10 = (bf16[512,128]{1,0:T(8,128)(2,1)S(1)}, bf16[512,128]{1,0:T(8,128)(2,1)S(1)}, u32[]{:S(2)}, u32[]{:S(2)}) collective-permute-start(bf16[512,128]{1,0:T(8,128)(2,1)S(1)} %add_convert_fusion.1), channel_id=1, source_target_pairs={{8,0},{10,2},{9,1},{11,3},{24,16},{26,18},{25,17},{27,19}} | collective-permute-start | bytes 393224 | tf_op jit(solution)/shard_map/ppermute | solution.py:22
  39.0 9.1 %collective-permute-start.9 = (bf16[512,128]{1,0:T(8,128)(2,1)S(1)}, bf16[512,128]{1,0:T(8,128)(2,1)S(1)}, u32[]{:S(2)}, u32[]{:S(2)}) collective-permute-start(bf16[512,128]{1,0:T(8,128)(2,1)S(1)} %add_convert_fusion.1), channel_id=1, source_target_pairs={{12,0},{14,2},{13,1},{15,3},{28,16},{30,18},{29,17},{31,19}} | collective-permute-start | bytes 393224 | tf_op jit(solution)/shard_map/ppermute | solution.py:22
  42.7 6.7 %collective-permute-start.14 = (bf16[256,128]{1,0:T(8,128)(2,1)S(1)}, bf16[256,128]{1,0:T(8,128)(2,1)S(1)}, u32[]{:S(2)}, u32[]{:S(2)}) collective-permute-start(bf16[256,128]{1,0:T(8,128)(2,1)S(1)} %get-tuple-element.95), channel_id=1, source_target_pairs={{10,2},{12,4},{14,6},{11,3},{13,5},{15,7},{26,18},{28,20},{30,22},... | collective-permute-start | bytes 196616 | tf_op jit(solution)/shard_map/ppermute | solution.py:22
  43.4 6.0 %collective-permute-start.13 = (bf16[256,128]{1,0:T(8,128)(2,1)S(1)}, bf16[256,128]{1,0:T(8,128)(2,1)S(1)}, u32[]{:S(2)}, u32[]{:S(2)}) collective-permute-start(bf16[256,128]{1,0:T(8,128)(2,1)S(1)} %get-tuple-element.99), channel_id=1, source_target_pairs={{14,2},{15,3},{30,18},{31,19}} | collective-permute-start | bytes 196616 | tf_op jit(solution)/shard_map/ppermute | solution.py:22
  45.6 3.9 %collective-permute-start.15 = (bf16[256,128]{1,0:T(8,128)(2,1)S(1)}, bf16[256,128]{1,0:T(8,128)(2,1)S(1)}, u32[]{:S(2)}, u32[]{:S(2)}) collective-permute-start(bf16[256,128]{1,0:T(8,128)(2,1)S(1)} %get-tuple-element.100), channel_id=1, source_target_pairs={{6,2},{8,4},{10,6},{12,8},{14,10},{7,3},{9,5},{11,7},{13,9},{15,11... | collective-permute-start | bytes 196616 | tf_op jit(solution)/shard_map/ppermute | solution.py:22
  48.1 6.9 %collective-permute-start.16 = (bf16[512,128]{1,0:T(8,128)(2,1)S(1)}, bf16[512,128]{1,0:T(8,128)(2,1)S(1)}, u32[]{:S(2)}, u32[]{:S(2)}) collective-permute-start(bf16[512,128]{1,0:T(8,128)(2,1)S(1)} %get-tuple-element.98), channel_id=1, source_target_pairs={{2,0},{3,1},{18,16},{19,17}} | collective-permute-start | bytes 393224 | tf_op jit(solution)/shard_map/ppermute | solution.py:22
  55.1 0.7 %copy-start = (f32[512,128]{1,0:T(8,128)}, f32[512,128]{1,0:T(8,128)S(1)}, u32[]{:S(2)}) copy-start(f32[512,128]{1,0:T(8,128)S(1)} %get-tuple-element.104) | copy-start | bytes 786436
  55.1 0.8 %copy-start.1 = (f32[512,128]{1,0:T(8,128)}, f32[512,128]{1,0:T(8,128)S(1)}, u32[]{:S(2)}) copy-start(f32[512,128]{1,0:T(8,128)S(1)} %get-tuple-element.105) | copy-start | bytes 786436

commit v22 on v21

--- a/solution.py
+++ b/solution.py
@@ -145,7 +145,7 @@
     send_ref, keep_ref, kh, ds_ref, p_behind, terms, vh, p_ref, grads, wide = refs[8:]
     tokens = TD * TILE
     front = CAP * TILE
-    columns = 2 * CHUNK * 8
+    columns = TILE * 8
     rate = scale * math.log2(math.e)
     device = lax.axis_index("node")
 
@@ -156,7 +156,7 @@
             split_heads(block_ref[at : at + front * heads_kv], heads_ref, tokens + k * front, front, heads_kv, wide)
 
     for head in range(heads_kv):
-        for c in range(tokens * 8 // columns):
+        for c in range(tokens // TILE):
             span = slice(c * columns, (c + 1) * columns)
             s = outer_product(kh[head], qh[head, span])
             dp = outer_product(vh[head], gh[head, span])

time: 56.2 us -> 56.5 us (level)
  no operation moved by 1% of the time
where the time goes in v22:
time: 56.5 us; the launch traced here: 56.2 us
  starting transfers between devices  24.6 us (44%)
  waiting for transfers between devices  18 us (32%)
  Pallas kernels  11.5 us (20%)
  between operations  0.92 us (2%)
  local copies, waits for them, and re-layouts  0.78 us (1%)
    ppermute x17, starting transfers between devices, permuted(): return lax.ppermute(block, 'node', route)  24.6 us
    ppermute x17, waiting for transfers between devices, permuted(): return lax.ppermute(block, 'node', route)  18 us
    pallas_call x6, Pallas kernels, call(): pl.pallas_call(kernel, in_specs=[place] * len(operands), out_specs=[VMEM]...  11.5 us
  transfers between devices with their start and end apart: 17, of which 11 were waited for; matrix products, arithmetic and copies ran while one was open for 1% of the time, Pallas kernels for 15%

profile of v22, /device:TPU:0, one launch (start us, length us, event | category | flops | bytes accessed | tf_op | source)
XLA Modules:
  0.0 56.2 jit_solution(2281136854959297489)
XLA Ops:
  0.6 5.9 %collective-permute-start = (bf16[512,128]{1,0:T(8,128)(2,1)}, bf16[512,128]{1,0:T(8,128)(2,1)S(1)}, u32[]{:S(2)}, u32[]{:S(2)}) collective-permute-start(bf16[512,128]{1,0:T(8,128)(2,1)} %bitcast.6), channel_id=1, source_target_pairs={{0,8},{1,9},{16,24},{17,25}} | collective-permute-start | bytes 393224 | tf_op jit(solution)/shard_map/ppermute | solution.py:22
  6.6 1.6 %collective-permute-start.2 = (bf16[512,128]{1,0:T(8,128)(2,1)}, bf16[512,128]{1,0:T(8,128)(2,1)S(1)}, u32[]{:S(2)}, u32[]{:S(2)}) collective-permute-start(bf16[512,128]{1,0:T(8,128)(2,1)} %bitcast.8), channel_id=1, source_target_pairs={{0,10},{1,11},{16,26},{17,27}} | collective-permute-start | bytes 393224 | tf_op jit(solution)/shard_map/ppermute | solution.py:22
  8.2 1.3 %collective-permute-start.1 = (bf16[512,128]{1,0:T(8,128)(2,1)}, bf16[512,128]{1,0:T(8,128)(2,1)S(1)}, u32[]{:S(2)}, u32[]{:S(2)}) collective-permute-start(bf16[512,128]{1,0:T(8,128)(2,1)} %bitcast.9), channel_id=1, source_target_pairs={{0,2},{1,3},{16,18},{17,19}} | collective-permute-start | bytes 393224 | tf_op jit(solution)/shard_map/ppermute | solution.py:22
  9.5 1.2 %load.1 = (bf16[256,128]{1,0:T(8,128)(2,1)S(1)}, bf16[512,128]{1,0:T(8,128)(2,1)S(1)}, bf16[4,128,128]{2,1,0:T(8,128)(2,1)S(1)}, bf16[4,128,128]{2,1,0:T(8,128)(...) custom-call(s32[64]{0:T(128)} %refs_0_.1, s32[64]{0:T(128)} %refs_1_.1, bf16[512,128]{1,0:T(8,128)(2,1)} %bitcast.7, ...), custom_call_target="tpu_custom_call" | custom-call | flops 1048576 | bytes 983552 | tf_op jit(solution)/shard_map/load/pallas_call | solution.py:265
  10.7 0.1 collective-permute-done
  10.8 0.7 %collective-permute-start.4 = (bf16[256,128]{1,0:T(8,128)(2,1)S(1)}, bf16[256,128]{1,0:T(8,128)(2,1)S(1)}, u32[]{:S(2)}, u32[]{:S(2)}) collective-permute-start(bf16[256,128]{1,0:T(8,128)(2,1)S(1)} %get-tuple-element.70), channel_id=1, source_target_pairs={{2,10},{4,12},{6,14},{3,11},{5,13},{7,15},{18,26},{20,28},{22,30},... | collective-permute-start | bytes 196616 | tf_op jit(solution)/shard_map/ppermute | solution.py:22
  11.4 0.7 %collective-permute-start.3 = (bf16[256,128]{1,0:T(8,128)(2,1)S(1)}, bf16[256,128]{1,0:T(8,128)(2,1)S(1)}, u32[]{:S(2)}, u32[]{:S(2)}) collective-permute-start(bf16[256,128]{1,0:T(8,128)(2,1)S(1)} %get-tuple-element.70), channel_id=1, source_target_pairs={{2,14},{3,15},{18,30},{19,31}} | collective-permute-start | bytes 196616 | tf_op jit(solution)/shard_map/ppermute | solution.py:22
  12.1 0.4 collective-permute-done.2
  12.5 0.1 collective-permute-done.1
  12.5 0.1 add_convert_fusion.2
  12.6 1.6 %pack.1 = (bf16[4,1024,128]{2,1,0:T(8,128)(2,1)S(1)}, bf16[4,1024,128]{2,1,0:T(8,128)(2,1)S(1)}) custom-call(bf16[128,32,128]{2,1,0:T(8,128)(2,1)} %q_ref, bf16[128,32,128]{2,1,0:T(8,128)(2,1)} %g_ref.1), custom_call_target="tpu_custom_call" | custom-call | flops 1048576 | bytes 4194304 | tf_op jit(solution)/shard_map/pack/pallas_call | solution.py:265
  14.3 0.0 collective-permute-done.4.refs_7_
  14.3 0.0 collective-permute-done.3.refs_8_
  14.3 2.8 %collective-permute-start.5 = (bf16[768,128]{1,0:T(8,128)(2,1)S(1)}, bf16[768,128]{1,0:T(8,128)(2,1)S(1)}, u32[]{:S(2)}, u32[]{:S(2)}) collective-permute-start(bf16[768,128]{1,0:T(8,128)(2,1)S(1)} %pad_maximum_fusion), channel_id=1, source_target_pairs={{0,4},{2,6},{4,8},{6,10},{8,12},{10,14},{1,5},{3,7},{5,9},{7,11},{... | collective-permute-start | bytes 589832 | tf_op jit(solution)/shard_map/ppermute | solution.py:22
  17.2 1.3 %collective-permute-start.6 = (bf16[512,128]{1,0:T(8,128)(2,1)S(1)}, bf16[512,128]{1,0:T(8,128)(2,1)S(1)}, u32[]{:S(2)}, u32[]{:S(2)}) collective-permute-start(bf16[512,128]{1,0:T(8,128)(2,1)S(1)} %maximum_select_fusion), channel_id=1, source_target_pairs={{0,2},{2,0},{4,6},{6,4},{8,10},{10,8},{12,14},{14,12},{1,3},{3,1},... | collective-permute-start | bytes 393224 | tf_op jit(solution)/shard_map/ppermute | solution.py:22
  18.4 3.0 %collective-permute-done.5.refs_5_ = bf16[768,128]{1,0:T(8,128)(2,1)S(1)} collective-permute-done((bf16[768,128]{1,0:T(8,128)(2,1)S(1)}, bf16[768,128]{1,0:T(8,128)(2,1)S(1)}, u32[]{:S(2)}, u32[]{:S(2)}) %collective-permute-start.5) | collective-permute-done | bytes 196640 | tf_op jit(solution)/shard_map/ppermute | solution.py:22
  21.5 0.9 %collective-permute-done.6.refs_6_ = bf16[512,128]{1,0:T(8,128)(2,1)S(1)} collective-permute-done((bf16[512,128]{1,0:T(8,128)(2,1)S(1)}, bf16[512,128]{1,0:T(8,128)(2,1)S(1)}, u32[]{:S(2)}, u32[]{:S(2)}) %collective-permute-start.6) | collective-permute-done | bytes 131104 | tf_op jit(solution)/shard_map/ppermute | solution.py:22
  22.4 1.0 %collective-permute-start.7 = (bf16[768,128]{1,0:T(8,128)(2,1)S(1)}, bf16[768,128]{1,0:T(8,128)(2,1)S(1)}, u32[]{:S(2)}, u32[]{:S(2)}) collective-permute-start(bf16[768,128]{1,0:T(8,128)(2,1)S(1)} %pad_maximum_fusion.1), channel_id=1, source_target_pairs={{0,2},{2,0},{4,6},{6,4},{8,10},{10,8},{12,14},{14,12},{1,3},{3,1},... | collective-permute-start | bytes 589832 | tf_op jit(solution)/shard_map/ppermute | solution.py:22
  23.4 1.6 %early.1 = (bf16[4,288,128]{2,1,0:T(8,128)(2,1)S(1)}, f32[4,288,1024]{2,1,0:T(8,128)S(1)}, f32[4,288,1024]{2,1,0:T(8,128)S(1)}, f32[4,8,1024]{2,1,0:T(8,128)S(1)}) custom-call(bf16[4,128,128]{2,1,0:T(8,128)(2,1)S(1)} %get-tuple-element.75.refs_0_, bf16[4,128,128]{2,1,0:T(8,128)(2,1)S(1)} %get-tuple-element.76.refs_1_, ...), custom_call_target="tpu_custom_call" | custom-call | flops 603979776 | bytes 12910592 | tf_op jit(solution)/shard_map/early/pallas_call | solution.py:265
  25.0 3.0 %collective-permute-done.7.refs_7_ = bf16[768,128]{1,0:T(8,128)(2,1)S(1)} collective-permute-done((bf16[768,128]{1,0:T(8,128)(2,1)S(1)}, bf16[768,128]{1,0:T(8,128)(2,1)S(1)}, u32[]{:S(2)}, u32[]{:S(2)}) %collective-permute-start.7) | collective-permute-done | bytes 196640 | tf_op jit(solution)/shard_map/ppermute | solution.py:22
  28.1 3.2 %probs.1 = (bf16[512,128]{1,0:T(8,128)(2,1)S(1)}, bf16[512,128]{1,0:T(8,128)(2,1)S(1)}, bf16[4,160,128]{2,1,0:T(8,128)(2,1)S(1)}, bf16[4,160,1024]{2,1,0:T(8,128...) custom-call(bf16[512,128]{1,0:T(8,128)(2,1)S(1)} %get-tuple-element.103.refs_0_, ...), custom_call_target="tpu_custom_call" | custom-call | flops 671088640 | bytes 5079040 | tf_op jit(solution)/shard_map/probs/pallas_call | solution.py:265
  31.3 1.1 %collective-permute-start.8 = (bf16[512,128]{1,0:T(8,128)(2,1)S(1)}, bf16[512,128]{1,0:T(8,128)(2,1)S(1)}, u32[]{:S(2)}, u32[]{:S(2)}) collective-permute-start(bf16[512,128]{1,0:T(8,128)(2,1)S(1)} %get-tuple-element.88), channel_id=1, source_target_pairs={{0,2},{2,0},{4,6},{6,4},{8,10},{10,8},{12,14},{14,12},{1,3},{3,1},... | collective-permute-start | bytes 393224 | tf_op jit(solution)/shard_map/ppermute | solution.py:22
  32.4 1.4 %windows.1 = (bf16[768,128]{1,0:T(8,128)(2,1)S(1)}, bf16[768,128]{1,0:T(8,128)(2,1)S(1)}, bf16[4,288,1024]{2,1,0:T(8,128)(2,1)S(1)}, bf16[4,128,1024]{2,1,0:T(8,128)(2,1)S(1)}) custom-call(bf16[4,1024,128]{2,1,0:T(8,128)(2,1)S(1)} %get-tuple-element.65.refs_2_.refs_0_, bf16[4,1024,128]{2,1,0:T(8,128)(2,1)S(1)} %get-tuple-element.66.refs_3_.refs_1_, ...), custom_call_target="tpu_custom_call" | custom-call | flops 402653184 | bytes 17039360 | tf_op jit(solution)/shard_map/windows/pallas_call | solution.py:265
  33.8 1.1 %collective-permute-start.12 = (bf16[768,128]{1,0:T(8,128)(2,1)S(1)}, bf16[768,128]{1,0:T(8,128)(2,1)S(1)}, u32[]{:S(2)}, u32[]{:S(2)}) collective-permute-start(bf16[768,128]{1,0:T(8,128)(2,1)S(1)} %get-tuple-element.93), channel_id=1, source_target_pairs={{0,2},{2,0},{4,6},{6,4},{8,10},{10,8},{12,14},{14,12},{1,3},{3,1},... | collective-permute-start | bytes 589832 | tf_op jit(solution)/shard_map/ppermute | solution.py:22
  34.9 1.8 %collective-permute-done.8 = bf16[512,128]{1,0:T(8,128)(2,1)S(1)} collective-permute-done((bf16[512,128]{1,0:T(8,128)(2,1)S(1)}, bf16[512,128]{1,0:T(8,128)(2,1)S(1)}, u32[]{:S(2)}, u32[]{:S(2)}) %collective-permute-start.8) | collective-permute-done | bytes 131104 | tf_op jit(solution)/shard_map/ppermute | solution.py:22
  36.7 1.3 %collective-permute-start.11 = (bf16[512,128]{1,0:T(8,128)(2,1)S(1)}, bf16[512,128]{1,0:T(8,128)(2,1)S(1)}, u32[]{:S(2)}, u32[]{:S(2)}) collective-permute-start(bf16[512,128]{1,0:T(8,128)(2,1)S(1)} %add_convert_fusion.1), channel_id=1, source_target_pairs={{4,0},{6,2},{5,1},{7,3},{20,16},{22,18},{21,17},{23,19}} | collective-permute-start | bytes 393224 | tf_op jit(solution)/shard_map/ppermute | solution.py:22
  38.0 1.3 %collective-permute-start.10 = (bf16[512,128]{1,0:T(8,128)(2,1)S(1)}, bf16[512,128]{1,0:T(8,128)(2,1)S(1)}, u32[]{:S(2)}, u32[]{:S(2)}) collective-permute-start(bf16[512,128]{1,0:T(8,128)(2,1)S(1)} %add_convert_fusion.1), channel_id=1, source_target_pairs={{8,0},{10,2},{9,1},{11,3},{24,16},{26,18},{25,17},{27,19}} | collective-permute-start | bytes 393224 | tf_op jit(solution)/shard_map/ppermute | solution.py:22
  39.3 1.3 %collective-permute-start.9 = (bf16[512,128]{1,0:T(8,128)(2,1)S(1)}, bf16[512,128]{1,0:T(8,128)(2,1)S(1)}, u32[]{:S(2)}, u32[]{:S(2)}) collective-permute-start(bf16[512,128]{1,0:T(8,128)(2,1)S(1)} %add_convert_fusion.1), channel_id=1, source_target_pairs={{12,0},{14,2},{13,1},{15,3},{28,16},{30,18},{29,17},{31,19}} | collective-permute-start | bytes 393224 | tf_op jit(solution)/shard_map/ppermute | solution.py:22
  40.6 2.4 %grads.1 = (bf16[128,32,128]{2,1,0:T(8,128)(2,1)}, f32[512,128]{1,0:T(8,128)S(1)}, f32[512,128]{1,0:T(8,128)S(1)}) custom-call(bf16[4,1024,128]{2,1,0:T(8,128)(2,1)S(1)} %get-tuple-element.65.refs_2_.refs_0_, bf16[4,1024,128]{2,1,0:T(8,128)(2,1)S(1)} %get-tuple-element.66.refs_3_.refs_1_, bf16[4,160,128]{2,1,0:T(8,128)(2,1)S(1)} %get-tuple-element.78.refs_2_, ...), custom_call_target="tpu_custom_call" | custom-call | flops 469762048 | bytes 8847360 | tf_op jit(solution)/shard_map/grads/pallas_call | solution.py:265
  43.0 0.0 collective-permute-done.12
  43.0 0.1 add_convert_fusion.5
  43.1 0.7 %collective-permute-start.14 = (bf16[256,128]{1,0:T(8,128)(2,1)S(1)}, bf16[256,128]{1,0:T(8,128)(2,1)S(1)}, u32[]{:S(2)}, u32[]{:S(2)}) collective-permute-start(bf16[256,128]{1,0:T(8,128)(2,1)S(1)} %get-tuple-element.95), channel_id=1, source_target_pairs={{10,2},{12,4},{14,6},{11,3},{13,5},{15,7},{26,18},{28,20},{30,22},... | collective-permute-start | bytes 196616 | tf_op jit(solution)/shard_map/ppermute | solution.py:22
  43.7 0.7 %collective-permute-start.13 = (bf16[256,128]{1,0:T(8,128)(2,1)S(1)}, bf16[256,128]{1,0:T(8,128)(2,1)S(1)}, u32[]{:S(2)}, u32[]{:S(2)}) collective-permute-start(bf16[256,128]{1,0:T(8,128)(2,1)S(1)} %get-tuple-element.99), channel_id=1, source_target_pairs={{14,2},{15,3},{30,18},{31,19}} | collective-permute-start | bytes 196616 | tf_op jit(solution)/shard_map/ppermute | solution.py:22
  44.4 1.5 %collective-permute-done.11 = bf16[512,128]{1,0:T(8,128)(2,1)S(1)} collective-permute-done((bf16[512,128]{1,0:T(8,128)(2,1)S(1)}, bf16[512,128]{1,0:T(8,128)(2,1)S(1)}, u32[]{:S(2)}, u32[]{:S(2)}) %collective-permute-start.11) | collective-permute-done | bytes 131104 | tf_op jit(solution)/shard_map/ppermute | solution.py:22
  45.9 0.7 %collective-permute-start.15 = (bf16[256,128]{1,0:T(8,128)(2,1)S(1)}, bf16[256,128]{1,0:T(8,128)(2,1)S(1)}, u32[]{:S(2)}, u32[]{:S(2)}) collective-permute-start(bf16[256,128]{1,0:T(8,128)(2,1)S(1)} %get-tuple-element.100), channel_id=1, source_target_pairs={{6,2},{8,4},{10,6},{12,8},{14,10},{7,3},{9,5},{11,7},{13,9},{15,11... | collective-permute-start | bytes 196616 | tf_op jit(solution)/shard_map/ppermute | solution.py:22
  46.6 1.0 %collective-permute-done.10 = bf16[512,128]{1,0:T(8,128)(2,1)S(1)} collective-permute-done((bf16[512,128]{1,0:T(8,128)(2,1)S(1)}, bf16[512,128]{1,0:T(8,128)(2,1)S(1)}, u32[]{:S(2)}, u32[]{:S(2)}) %collective-permute-start.10) | collective-permute-done | bytes 131104 | tf_op jit(solution)/shard_map/ppermute | solution.py:22
  47.6 0.8 %collective-permute-done.9 = bf16[512,128]{1,0:T(8,128)(2,1)S(1)} collective-permute-done((bf16[512,128]{1,0:T(8,128)(2,1)S(1)}, bf16[512,128]{1,0:T(8,128)(2,1)S(1)}, u32[]{:S(2)}, u32[]{:S(2)}) %collective-permute-start.9) | collective-permute-done | bytes 131104 | tf_op jit(solution)/shard_map/ppermute | solution.py:22
  48.4 0.1 select_add_fusion.1
  48.4 1.3 %collective-permute-start.16 = (bf16[512,128]{1,0:T(8,128)(2,1)S(1)}, bf16[512,128]{1,0:T(8,128)(2,1)S(1)}, u32[]{:S(2)}, u32[]{:S(2)}) collective-permute-start(bf16[512,128]{1,0:T(8,128)(2,1)S(1)} %get-tuple-element.98), channel_id=1, source_target_pairs={{2,0},{3,1},{18,16},{19,17}} | collective-permute-start | bytes 393224 | tf_op jit(solution)/shard_map/ppermute | solution.py:22
  49.7 0.0 collective-permute-done.14
  49.8 0.0 collective-permute-done.13
  49.8 0.0 collective-permute-done.15
  49.8 5.5 %collective-permute-done.16 = bf16[512,128]{1,0:T(8,128)(2,1)S(1)} collective-permute-done((bf16[512,128]{1,0:T(8,128)(2,1)S(1)}, bf16[512,128]{1,0:T(8,128)(2,1)S(1)}, u32[]{:S(2)}, u32[]{:S(2)}) %collective-permute-start.16) | collective-permute-done | bytes 131104 | tf_op jit(solution)/shard_map/ppermute | solution.py:22
  55.4 0.0 copy-start
  55.4 0.0 copy-start.1
  55.4 0.7 %copy-done = f32[512,128]{1,0:T(8,128)} copy-done((f32[512,128]{1,0:T(8,128)}, f32[512,128]{1,0:T(8,128)S(1)}, u32[]{:S(2)}) %copy-start) | copy-done | bytes 262168
  56.1 0.1 copy-done.1
  (10 shorter events, 0.2 us)
Async XLA Ops:
  0.6 10.1 %collective-permute-start = (bf16[512,128]{1,0:T(8,128)(2,1)}, bf16[512,128]{1,0:T(8,128)(2,1)S(1)}, u32[]{:S(2)}, u32[]{:S(2)}) collective-permute-start(bf16[512,128]{1,0:T(8,128)(2,1)} %bitcast.6), channel_id=1, source_target_pairs={{0,8},{1,9},{16,24},{17,25}} | collective-permute-start | bytes 393224 | tf_op jit(solution)/shard_map/ppermute | solution.py:22
  6.6 5.9 %collective-permute-start.2 = (bf16[512,128]{1,0:T(8,128)(2,1)}, bf16[512,128]{1,0:T(8,128)(2,1)S(1)}, u32[]{:S(2)}, u32[]{:S(2)}) collective-permute-start(bf16[512,128]{1,0:T(8,128)(2,1)} %bitcast.8), channel_id=1, source_target_pairs={{0,10},{1,11},{16,26},{17,27}} | collective-permute-start | bytes 393224 | tf_op jit(solution)/shard_map/ppermute | solution.py:22
  8.2 4.4 %collective-permute-start.1 = (bf16[512,128]{1,0:T(8,128)(2,1)}, bf16[512,128]{1,0:T(8,128)(2,1)S(1)}, u32[]{:S(2)}, u32[]{:S(2)}) collective-permute-start(bf16[512,128]{1,0:T(8,128)(2,1)} %bitcast.9), channel_id=1, source_target_pairs={{0,2},{1,3},{16,18},{17,19}} | collective-permute-start | bytes 393224 | tf_op jit(solution)/shard_map/ppermute | solution.py:22
  10.8 3.5 %collective-permute-start.4 = (bf16[256,128]{1,0:T(8,128)(2,1)S(1)}, bf16[256,128]{1,0:T(8,128)(2,1)S(1)}, u32[]{:S(2)}, u32[]{:S(2)}) collective-permute-start(bf16[256,128]{1,0:T(8,128)(2,1)S(1)} %get-tuple-element.70), channel_id=1, source_target_pairs={{2,10},{4,12},{6,14},{3,11},{5,13},{7,15},{18,26},{20,28},{22,30},... | collective-permute-start | bytes 196616 | tf_op jit(solution)/shard_map/ppermute | solution.py:22
  11.4 2.8 %collective-permute-start.3 = (bf16[256,128]{1,0:T(8,128)(2,1)S(1)}, bf16[256,128]{1,0:T(8,128)(2,1)S(1)}, u32[]{:S(2)}, u32[]{:S(2)}) collective-permute-start(bf16[256,128]{1,0:T(8,128)(2,1)S(1)} %get-tuple-element.70), channel_id=1, source_target_pairs={{2,14},{3,15},{18,30},{19,31}} | collective-permute-start | bytes 196616 | tf_op jit(solution)/shard_map/ppermute | solution.py:22
  14.3 7.2 %collective-permute-start.5 = (bf16[768,128]{1,0:T(8,128)(2,1)S(1)}, bf16[768,128]{1,0:T(8,128)(2,1)S(1)}, u32[]{:S(2)}, u32[]{:S(2)}) collective-permute-start(bf16[768,128]{1,0:T(8,128)(2,1)S(1)} %pad_maximum_fusion), channel_id=1, source_target_pairs={{0,4},{2,6},{4,8},{6,10},{8,12},{10,14},{1,5},{3,7},{5,9},{7,11},{... | collective-permute-start | bytes 589832 | tf_op jit(solution)/shard_map/ppermute | solution.py:22
  17.2 5.2 %collective-permute-start.6 = (bf16[512,128]{1,0:T(8,128)(2,1)S(1)}, bf16[512,128]{1,0:T(8,128)(2,1)S(1)}, u32[]{:S(2)}, u32[]{:S(2)}) collective-permute-start(bf16[512,128]{1,0:T(8,128)(2,1)S(1)} %maximum_select_fusion), channel_id=1, source_target_pairs={{0,2},{2,0},{4,6},{6,4},{8,10},{10,8},{12,14},{14,12},{1,3},{3,1},... | collective-permute-start | bytes 393224 | tf_op jit(solution)/shard_map/ppermute | solution.py:22
  22.4 5.7 %collective-permute-start.7 = (bf16[768,128]{1,0:T(8,128)(2,1)S(1)}, bf16[768,128]{1,0:T(8,128)(2,1)S(1)}, u32[]{:S(2)}, u32[]{:S(2)}) collective-permute-start(bf16[768,128]{1,0:T(8,128)(2,1)S(1)} %pad_maximum_fusion.1), channel_id=1, source_target_pairs={{0,2},{2,0},{4,6},{6,4},{8,10},{10,8},{12,14},{14,12},{1,3},{3,1},... | collective-permute-start | bytes 589832 | tf_op jit(solution)/shard_map/ppermute | solution.py:22
  31.3 5.3 %collective-permute-start.8 = (bf16[512,128]{1,0:T(8,128)(2,1)S(1)}, bf16[512,128]{1,0:T(8,128)(2,1)S(1)}, u32[]{:S(2)}, u32[]{:S(2)}) collective-permute-start(bf16[512,128]{1,0:T(8,128)(2,1)S(1)} %get-tuple-element.88), channel_id=1, source_target_pairs={{0,2},{2,0},{4,6},{6,4},{8,10},{10,8},{12,14},{14,12},{1,3},{3,1},... | collective-permute-start | bytes 393224 | tf_op jit(solution)/shard_map/ppermute | solution.py:22
  33.8 9.2 %collective-permute-start.12 = (bf16[768,128]{1,0:T(8,128)(2,1)S(1)}, bf16[768,128]{1,0:T(8,128)(2,1)S(1)}, u32[]{:S(2)}, u32[]{:S(2)}) collective-permute-start(bf16[768,128]{1,0:T(8,128)(2,1)S(1)} %get-tuple-element.93), channel_id=1, source_target_pairs={{0,2},{2,0},{4,6},{6,4},{8,10},{10,8},{12,14},{14,12},{1,3},{3,1},... | collective-permute-start | bytes 589832 | tf_op jit(solution)/shard_map/ppermute | solution.py:22
  36.7 9.2 %collective-permute-start.11 = (bf16[512,128]{1,0:T(8,128)(2,1)S(1)}, bf16[512,128]{1,0:T(8,128)(2,1)S(1)}, u32[]{:S(2)}, u32[]{:S(2)}) collective-permute-start(bf16[512,128]{1,0:T(8,128)(2,1)S(1)} %add_convert_fusion.1), channel_id=1, source_target_pairs={{4,0},{6,2},{5,1},{7,3},{20,16},{22,18},{21,17},{23,19}} | collective-permute-start | bytes 393224 | tf_op jit(solution)/shard_map/ppermute | solution.py:22
  38.0 9.6 %collective-permute-start.10 = (bf16[512,128]{1,0:T(8,128)(2,1)S(1)}, bf16[512,128]{1,0:T(8,128)(2,1)S(1)}, u32[]{:S(2)}, u32[]{:S(2)}) collective-permute-start(bf16[512,128]{1,0:T(8,128)(2,1)S(1)} %add_convert_fusion.1), channel_id=1, source_target_pairs={{8,0},{10,2},{9,1},{11,3},{24,16},{26,18},{25,17},{27,19}} | collective-permute-start | bytes 393224 | tf_op jit(solution)/shard_map/ppermute | solution.py:22
  39.3 9.1 %collective-permute-start.9 = (bf16[512,128]{1,0:T(8,128)(2,1)S(1)}, bf16[512,128]{1,0:T(8,128)(2,1)S(1)}, u32[]{:S(2)}, u32[]{:S(2)}) collective-permute-start(bf16[512,128]{1,0:T(8,128)(2,1)S(1)} %add_convert_fusion.1), channel_id=1, source_target_pairs={{12,0},{14,2},{13,1},{15,3},{28,16},{30,18},{29,17},{31,19}} | collective-permute-start | bytes 393224 | tf_op jit(solution)/shard_map/ppermute | solution.py:22
  43.1 6.7 %collective-permute-start.14 = (bf16[256,128]{1,0:T(8,128)(2,1)S(1)}, bf16[256,128]{1,0:T(8,128)(2,1)S(1)}, u32[]{:S(2)}, u32[]{:S(2)}) collective-permute-start(bf16[256,128]{1,0:T(8,128)(2,1)S(1)} %get-tuple-element.95), channel_id=1, source_target_pairs={{10,2},{12,4},{14,6},{11,3},{13,5},{15,7},{26,18},{28,20},{30,22},... | collective-permute-start | bytes 196616 | tf_op jit(solution)/shard_map/ppermute | solution.py:22
  43.7 6.0 %collective-permute-start.13 = (bf16[256,128]{1,0:T(8,128)(2,1)S(1)}, bf16[256,128]{1,0:T(8,128)(2,1)S(1)}, u32[]{:S(2)}, u32[]{:S(2)}) collective-permute-start(bf16[256,128]{1,0:T(8,128)(2,1)S(1)} %get-tuple-element.99), channel_id=1, source_target_pairs={{14,2},{15,3},{30,18},{31,19}} | collective-permute-start | bytes 196616 | tf_op jit(solution)/shard_map/ppermute | solution.py:22
  45.9 3.8 %collective-permute-start.15 = (bf16[256,128]{1,0:T(8,128)(2,1)S(1)}, bf16[256,128]{1,0:T(8,128)(2,1)S(1)}, u32[]{:S(2)}, u32[]{:S(2)}) collective-permute-start(bf16[256,128]{1,0:T(8,128)(2,1)S(1)} %get-tuple-element.100), channel_id=1, source_target_pairs={{6,2},{8,4},{10,6},{12,8},{14,10},{7,3},{9,5},{11,7},{13,9},{15,11... | collective-permute-start | bytes 196616 | tf_op jit(solution)/shard_map/ppermute | solution.py:22
  48.4 6.9 %collective-permute-start.16 = (bf16[512,128]{1,0:T(8,128)(2,1)S(1)}, bf16[512,128]{1,0:T(8,128)(2,1)S(1)}, u32[]{:S(2)}, u32[]{:S(2)}) collective-permute-start(bf16[512,128]{1,0:T(8,128)(2,1)S(1)} %get-tuple-element.98), channel_id=1, source_target_pairs={{2,0},{3,1},{18,16},{19,17}} | collective-permute-start | bytes 393224 | tf_op jit(solution)/shard_map/ppermute | solution.py:22
  55.4 0.7 %copy-start = (f32[512,128]{1,0:T(8,128)}, f32[512,128]{1,0:T(8,128)S(1)}, u32[]{:S(2)}) copy-start(f32[512,128]{1,0:T(8,128)S(1)} %get-tuple-element.104) | copy-start | bytes 786436
  55.4 0.8 %copy-start.1 = (f32[512,128]{1,0:T(8,128)}, f32[512,128]{1,0:T(8,128)S(1)}, u32[]{:S(2)}) copy-start(f32[512,128]{1,0:T(8,128)S(1)} %get-tuple-element.105) | copy-start | bytes 786436
